TPU v7x, 32 devices: a whole 2x2x4 slice. The times are simulated.
32 devices in a mesh: pipe: 2 (over x), expert: 16 (over z, y, core).
Axes of the slice: x: 2, y: 2, z: 4, core: 2. Of those that a mesh axis runs over, the one named last changes fastest.
Arguments:
- state: bfloat16 [16, 2, 128, 2048], P('expert', 'pipe'), may hold values from -24 to 24
- query: bfloat16 [16, 2, 128, 2048], P('expert', 'pipe'), may hold values from -8 to 8
- enc_kv: bfloat16 [16, 64, 2, 2048], P('expert', 'pipe'), may hold values from -4 to 4
- gain: float32 [2048], replicated, may hold values from 0.1 to 1.9
- w_in: bfloat16 [2048, 6144], P(None, 'expert'), may hold values from -0.125 to 0.125
- w_out: bfloat16 [6144, 2048], P('expert'), may hold values from -0.109375 to 0.109375
- expert_id: int32 [16, 2, 128], P('expert', 'pipe'), may hold values from 0 to 1
- slot: int32 [16, 2, 128], P('expert', 'pipe'), may hold values from -1 to 95, as said below
- gate: float32 [16, 2, 128], P('expert', 'pipe'), may hold values from 0.3 to 1
Outputs:
- output: bfloat16 [16, 2, 128, 2048], P('expert', 'pipe')
Inputs may be any that keep to these rules, and one draw needn't show every extreme that they name: Within the 128 tokens of one source and sample, the tokens sent to one expert take slots 0, 1, 2, ... in token order until 96 are taken; later ones have slot -1. In every draw some expert is given 96 slotted tokens by every source and sample.
All inputs are finite; a program needn't handle non-finite values.
Results may differ from a plain program's by a relative error of at most 0.0055.
Values may be sent and summed in bfloat16 or wider, within the bound.
No kernel may reach another device: no remote copies, remote signals or barrier semaphores. Data moves between devices by JAX's collectives and lax.ppermute only.
A program may use at most 128 MiB of HBM per device.

v0:
```python
import math

import jax
import jax.numpy as jnp
from jax import lax
from jax.sharding import PartitionSpec as P

HEADS = 16
HD = 128
WSPLIT = 8


def expert_ffn(slot_rows, w_in, w_out):
    senders, slots_here, width = slot_rows.shape
    flat_rows = slot_rows.reshape(senders * slots_here, width)
    activation = jnp.maximum(
        jnp.dot(flat_rows, w_in, preferred_element_type=jnp.float32), 0.0
    ).astype(jnp.bfloat16)
    partial_value = jnp.dot(activation, w_out, preferred_element_type=jnp.float32).astype(
        jnp.bfloat16
    )
    return partial_value.reshape(senders, slots_here, width)


def body(state, query, enc_kv, gain, w_in, w_out, expert_id, slot, gate):
    tokens = state.shape[2]
    width = state.shape[3]
    queries = query.reshape(tokens, HEADS, HD)
    scale = 1.0 / math.sqrt(HD)
    kv_piece = lax.all_gather(enc_kv, "pipe", axis=1, tiled=True)
    best_score = jnp.full((HEADS, tokens), -jnp.inf, jnp.float32)
    denominator = jnp.zeros((HEADS, tokens), jnp.float32)
    accumulated = jnp.zeros((HEADS, tokens, HD), jnp.float32)
    key_rows = kv_piece[0, :, 0].reshape(-1, HEADS, HD)
    value_rows = kv_piece[0, :, 1].reshape(-1, HEADS, HD)
    scores = (
        jnp.einsum("thd,lhd->htl", queries, key_rows, preferred_element_type=jnp.float32) * scale
    )
    new_best = jnp.max(scores, axis=2)
    factor = jnp.exp(best_score - new_best)
    raised = jnp.exp(scores - new_best[:, :, None])
    denominator = denominator * factor + jnp.sum(raised, axis=2)
    update = jnp.einsum(
        "htl,lhd->htd", raised.astype(jnp.bfloat16), value_rows, preferred_element_type=jnp.float32
    )
    best_score, denominator, accumulated = (
        new_best,
        denominator,
        accumulated * factor[:, :, None] + update,
    )
    attended = jnp.transpose(accumulated / denominator[:, :, None], (1, 0, 2)).reshape(
        tokens, width
    )
    hidden_state = state[0, 0].astype(jnp.float32) + attended
    mean_square = jnp.mean(hidden_state * hidden_state, axis=-1, keepdims=True)
    normed = (hidden_state * lax.rsqrt(mean_square + 1e-06) * gain).astype(jnp.bfloat16)
    experts = lax.axis_size("expert") // WSPLIT
    capacity = 3 * tokens // (2 * experts)
    flat_slot = jnp.where(slot[0, 0] >= 0, expert_id[0, 0] * capacity + slot[0, 0], -1)
    slot_ids = jnp.arange(experts * capacity, dtype=jnp.int32)
    selector = (slot_ids[:, None] == flat_slot[None, :]).astype(jnp.bfloat16)
    packed = jnp.dot(selector, normed, preferred_element_type=jnp.float32).astype(jnp.bfloat16)
    copies = jnp.broadcast_to(
        packed.reshape(experts, 1, capacity, width), (experts, WSPLIT, capacity, width)
    )
    copies = copies.reshape(experts * WSPLIT, capacity, width)
    partial_value = expert_ffn(
        lax.all_to_all(copies, "expert", split_axis=0, concat_axis=0, tiled=True), w_in, w_out
    )
    returned = lax.all_to_all(partial_value, "expert", split_axis=0, concat_axis=0, tiled=True)
    summed = jnp.sum(returned.reshape(experts, WSPLIT, capacity, width), axis=1, dtype=jnp.float32)
    summed = summed.reshape(experts * capacity, width)
    picked = jnp.take(summed, jnp.maximum(flat_slot, 0), axis=0)
    contribution = jnp.where((flat_slot >= 0)[:, None], gate[0, 0][:, None] * picked, 0.0)
    output = (hidden_state + contribution).astype(jnp.bfloat16)
    return output.reshape(1, 1, tokens, width)


def solution(mesh):
    return jax.shard_map(
        body,
        mesh=mesh,
        in_specs=(
            P("expert", "pipe", None, None),
            P("expert", "pipe", None, None),
            P("expert", "pipe", None, None),
            P(),
            P(None, "expert"),
            P("expert", None),
            P("expert", "pipe", None),
            P("expert", "pipe", None),
            P("expert", "pipe", None),
        ),
        out_specs=P("expert", "pipe", None, None),
        check_vma=False,
    )
```

profile of v0, /device:TPU:13, one launch (start us, length us, event | category | flops | bytes accessed | tf_op | source)
XLA Modules:
  0.0 326.2 jit_solution(18248029078372797048)
XLA Ops:
  0.0 0.0 copy-start
  0.0 0.0 copy-start.3
  0.0 8.2 %all_gather.3 = bf16[1,64,2,2048]{3,2,0,1:T(2,128)(2,1)S(1)} all-gather(bf16[1,32,2,2048]{3,2,0,1:T(2,128)(2,1)} %bitcast.84), channel_id=1, replica_groups=mesh['pipe'=2,'expert'=16] {'pipe'}, dimensions={1}, use_global_device_ids=true | all-gather | bytes 786432 | tf_op jit(solution)/shard_map/all_gather | solution.py:30
  8.2 0.0 copy-start.1
  8.2 2.2 slice_reduce_fusion
  10.4 0.0 copy-done.3
  10.4 0.1 copy.29
  10.5 0.5 fusion.25
  11.0 0.0 copy-start.2
  11.0 0.8 copy-done.2
  11.8 0.1 fusion.15
  11.9 0.0 copy-done.1
  11.9 1.2 copy.26
  13.1 0.0 copy-start.6
  13.1 0.0 copy-start.7
  13.1 0.0 copy-start.4
  13.1 1.9 multiply_reduce_fusion
  15.0 1.3 copy.25
  16.3 0.0 copy-done.6
  16.4 0.0 copy-done.7
  16.4 0.0 copy-done.4
  16.4 1.7 convolution_convert_fusion.1
  18.1 0.8 broadcast_in_dim.54
  18.9 144.5 %all_to_all.10 = bf16[16,96,2048]{2,1,0:T(8,128)(2,1)} all-to-all(bf16[16,96,2048]{2,1,0:T(8,128)(2,1)S(1)} %bitcast.75), channel_id=1, replica_groups=mesh['pipe'=2,'expert'=16] {'expert'}, dimensions={0} | all-to-all | bytes 12582912 | tf_op jit(solution)/shard_map/all_to_all | solution.py:68
  163.4 0.0 copy-done
  163.4 10.9 %convolution_convert_fusion = bf16[1536,2048]{1,0:T(8,128)(2,1)} fusion(bf16[384,2048]{1,0:T(8,128)(2,1)S(1)} %copy-done, bf16[1536,2048]{1,0:T(8,128)(2,1)} %bitcast.77, bf16[2048,384]{1,0:T(8,128)(2,1)} %param.13), kind=kOutput, calls=%fused_computation.2 | convolution fusion | flops 4836163584 | bytes 15728640 | tf_op jit(solution)/shard_map/dot_general | solution.py:19
  174.3 5.5 %all-to-all-start.1 = ((bf16[16,96,2048]{2,1,0:T(8,128)(2,1)}), bf16[16,96,2048]{2,1,0:T(8,128)(2,1)}, u32[]{:S(2)}, u32[]{:S(2)}) async-start(bf16[16,96,2048]{2,1,0:T(8,128)(2,1)} %bitcast.76), calls=%async_computation.1 | async-start | bytes 12582912 | tf_op jit(solution)/shard_map/all_to_all | solution.py:70
  179.8 1.4 copy.24
  181.2 136.0 %all-to-all-done.1 = bf16[16,96,2048]{2,1,0:T(8,128)(2,1)} async-done(((bf16[16,96,2048]{2,1,0:T(8,128)(2,1)}), bf16[16,96,2048]{2,1,0:T(8,128)(2,1)}, u32[]{:S(2)}, u32[]{:S(2)}) %all-to-all-start.1) | async-done | bytes 6291488 | tf_op jit(solution)/shard_map/all_to_all | solution.py:70
  317.2 4.1 %convert_reduce_fusion = f32[2,96,2048]{2,1,0:T(8,128)S(1)} fusion(bf16[16,96,2048]{2,1,0:T(8,128)(2,1)} %all-to-all-done.1), kind=kLoop, calls=%fused_computation.1 | loop fusion | flops 5898240 | bytes 7864320 | tf_op jit(solution)/shard_map/reduce_sum | solution.py:71
  321.3 0.0 copy-start.5
  321.3 1.9 gather_fusion
  323.2 0.0 copy-done.5
  323.2 2.9 fusion.6
  (7 shorter events, 0.1 us)
Async XLA Ops:
  0.0 163.4 %copy-start = (bf16[384,2048]{1,0:T(8,128)(2,1)S(1)}, bf16[384,2048]{1,0:T(8,128)(2,1)}, u32[]{:S(2)}) copy-start(bf16[384,2048]{1,0:T(8,128)(2,1)} %param.14) | copy-start | bytes 4718596
  0.0 10.4 %copy-start.3 = (bf16[1,1,128,2048]{3,2,1,0:T(8,128)(2,1)S(1)}, bf16[1,1,128,2048]{3,2,1,0:T(8,128)(2,1)}, u32[]{:S(2)}) copy-start(bf16[1,1,128,2048]{3,2,1,0:T(8,128)(2,1)} %param.10) | copy-start | bytes 1572868
  8.2 3.7 %copy-start.1 = (bf16[1,1,128,2048]{3,2,1,0:T(8,128)(2,1)S(1)}, bf16[1,1,128,2048]{3,2,1,0:T(8,128)(2,1)}, u32[]{:S(2)}) copy-start(bf16[1,1,128,2048]{3,2,1,0:T(8,128)(2,1)} %param.9) | copy-start | bytes 1572868
  11.0 0.8 copy-start.2
  13.1 3.3 copy-start.6
  13.1 3.3 copy-start.7
  13.1 3.3 %copy-start.4 = (f32[2048]{0:T(1024)S(1)}, f32[2048]{0:T(1024)}, u32[]{:S(2)}) copy-start(f32[2048]{0:T(1024)} %param.12) | copy-start | bytes 24580
  174.3 142.9 %all-to-all-start.1 = ((bf16[16,96,2048]{2,1,0:T(8,128)(2,1)}), bf16[16,96,2048]{2,1,0:T(8,128)(2,1)}, u32[]{:S(2)}, u32[]{:S(2)}) async-start(bf16[16,96,2048]{2,1,0:T(8,128)(2,1)} %bitcast.76), calls=%async_computation.1 | async-start | bytes 12582912 | tf_op jit(solution)/shard_map/all_to_all | solution.py:70
  321.3 2.0 copy-start.5
where the time goes:
time: 327 us; the launch traced here: 326 us
  blocking collectives  153 us (47%)
  waiting for transfers between devices  136 us (42%)
  matrix products  15 us (5%)
  local copies, waits for them, and re-layouts  9.72 us (3%)
  other arithmetic  7.17 us (2%)
  starting transfers between devices  5.51 us (2%)
    all_to_all x1, blocking collectives, body(): lax.all_to_all(copies, 'expert', split_axis=0, concat_axis=0, tiled=True)  145 us
    all_to_all x1, waiting for transfers between devices, body(): lax.all_to_all(partial_value, 'expert', split_axis=0, concat_axis=0, tile...  136 us
    dot_general x1, matrix products, expert_ffn(): jnp.dot(activation, w_out, preferred_element_type=jnp.float32)  10.9 us
    all_gather x1, blocking collectives, body(): kv_piece = lax.all_gather(enc_kv, 'pipe', axis=1, tiled=True)  8.18 us
  transfers between devices with their start and end apart: 1, of which 1 were waited for; matrix products, arithmetic and copies ran while one was open for 0% of the time, Pallas kernels for 0%

commit v1 on v0

v1 whole, which is shorter than its diff:
```python
import functools
import math

import jax
import jax.numpy as jnp
from jax import lax
from jax.experimental import pallas as pl
from jax.experimental.pallas import tpu as pltpu
from jax.sharding import PartitionSpec as P

HEADS = 16
HD = 128
WSPLIT = 8
EPS = 1e-06
VMEM_LIMIT = 48 * 1024 * 1024

VMEM = pl.BlockSpec(memory_space=pltpu.VMEM)
ANY = pl.BlockSpec(memory_space=pl.ANY)


def params():
    return pltpu.CompilerParams(vmem_limit_bytes=VMEM_LIMIT)


def attend_kernel(pieces, groups, cap, *refs):
    state_ref, query_ref, gain_ref, flat_ref = refs[:4]
    kv_refs = refs[4 : 4 + pieces]
    hidden_ref = refs[4 + pieces]
    packed_refs = refs[5 + pieces :]
    tokens, width = state_ref.shape
    half = width // 2
    local = kv_refs[0].shape[0] // 2
    scale = 1.0 / math.sqrt(HD)
    squares = jnp.zeros((tokens, HD), jnp.float32)
    for head in range(HEADS):
        cols = slice(head * HD, (head + 1) * HD)
        keys = jnp.concatenate([r[:local, cols] for r in kv_refs], axis=0)
        values = jnp.concatenate([r[local:, cols] for r in kv_refs], axis=0)
        scores = (
            lax.dot_general(
                query_ref[:, cols],
                keys,
                (((1,), (1,)), ((), ())),
                preferred_element_type=jnp.float32,
            )
            * scale
        )
        raised = jnp.exp(scores - jnp.max(scores, axis=1, keepdims=True))
        total = jnp.sum(raised, axis=1, keepdims=True)
        mixed = jnp.dot(raised.astype(jnp.bfloat16), values, preferred_element_type=jnp.float32)
        hidden = state_ref[:, cols].astype(jnp.float32) + mixed / total
        hidden_ref[:, cols] = hidden
        squares = squares + hidden * hidden
    mean_square = jnp.sum(squares, axis=1, keepdims=True) * (1.0 / width)
    inverse = lax.rsqrt(mean_square + EPS)
    rows = lax.broadcasted_iota(jnp.int32, (groups * cap, tokens), 0)
    selector = (rows == flat_ref[...]).astype(jnp.float32).astype(jnp.bfloat16)
    step = 512
    for at in range(0, width, step):
        cols = slice(at, at + step)
        normed = (hidden_ref[:, cols] * inverse * gain_ref[:, cols]).astype(jnp.bfloat16)
        packed = jnp.dot(selector, normed, preferred_element_type=jnp.float32).astype(jnp.bfloat16)
        side, inner = divmod(at, half)
        for group in range(groups):
            packed_refs[2 * group + side][:, inner : inner + step] = packed[
                group * cap : (group + 1) * cap
            ]


def attend(state, query, gain, flat, kv_pieces, groups, cap):
    tokens, width = state.shape
    half = width // 2
    outs = [jax.ShapeDtypeStruct((tokens, width), jnp.float32)]
    outs += [jax.ShapeDtypeStruct((cap, half), jnp.bfloat16)] * (2 * groups)
    pieces = len(kv_pieces)
    return pl.pallas_call(
        functools.partial(attend_kernel, pieces, groups, cap),
        out_shape=outs,
        in_specs=[VMEM] * (4 + pieces),
        out_specs=[VMEM] * len(outs),
        compiler_params=params(),
        cost_estimate=pl.CostEstimate(
            flops=4 * tokens * pieces * kv_pieces[0].shape[0] * width,
            bytes_accessed=12 * tokens * width,
            transcendentals=tokens * 64 * HEADS,
        ),
        name="attend",
    )(state, query, gain, flat, *kv_pieces)


def ffn_kernel(*refs):
    blocks = refs[:8]
    weights = refs[8:12]
    own_ref, z0_ref, y1_ref, y0_ref, z1_ref = refs[12:17]
    held = refs[17:21]
    sems = refs[21]
    copies = [
        pltpu.make_async_copy(source, target, sems.at[i])
        for i, (source, target) in enumerate(zip(weights, held))
    ]
    for copy in copies:
        copy.start()
    rows, half = blocks[0].shape
    left = jnp.concatenate([blocks[2 * i][...] for i in range(4)], axis=0)
    right = jnp.concatenate([blocks[2 * i + 1][...] for i in range(4)], axis=0)
    entries = jnp.concatenate([left, right], axis=1)
    activations = []
    for i in range(2):
        copies[i].wait()
        raw = jnp.dot(entries, held[i][...], preferred_element_type=jnp.float32)
        activations.append(jnp.maximum(raw, 0.0).astype(jnp.bfloat16))
    copies[2].wait()
    copies[3].wait()
    step = 512
    for at in range(0, 2 * half, step):
        cols = slice(at, at + step)
        part = jnp.dot(activations[0], held[2][:, cols], preferred_element_type=jnp.float32)
        part = part + jnp.dot(activations[1], held[3][:, cols], preferred_element_type=jnp.float32)
        part = part.astype(jnp.bfloat16)
        own_ref[:, cols] = part[:rows]
        y_part, z_part, d_part = (part[i * rows : (i + 1) * rows] for i in (1, 2, 3))
        side, inner = divmod(at, half)
        cols = slice(inner, inner + step)
        if side == 0:
            y0_ref[:, cols] = y_part
            z0_ref[0, :, cols] = z_part
            z0_ref[1, :, cols] = d_part
        else:
            z1_ref[:, cols] = z_part
            y1_ref[0, :, cols] = y_part
            y1_ref[1, :, cols] = d_part


def ffn(blocks, weights):
    rows, half = blocks[0].shape
    width = 2 * half
    units = weights[0].shape[1]
    one = jax.ShapeDtypeStruct((rows, half), jnp.bfloat16)
    two = jax.ShapeDtypeStruct((2, rows, half), jnp.bfloat16)
    return pl.pallas_call(
        ffn_kernel,
        out_shape=[jax.ShapeDtypeStruct((rows, width), jnp.bfloat16), two, two, one, one],
        in_specs=[VMEM] * 8 + [ANY] * 4,
        out_specs=[VMEM] * 5,
        scratch_shapes=[pltpu.VMEM(w.shape, w.dtype) for w in weights]
        + [pltpu.SemaphoreType.DMA((4,))],
        compiler_params=params(),
        cost_estimate=pl.CostEstimate(
            flops=4 * 4 * rows * width * units * 2,
            bytes_accessed=8 * units * width + 16 * rows * width,
            transcendentals=0,
        ),
        name="expert_ffn",
    )(*blocks, *weights)


def finish_kernel(groups, cap, *refs):
    hidden_ref, gate_ref, flat_ref, own_ref, az_ref, ay_ref, by_ref, bz_ref = refs[:8]
    back_refs = refs[8:-1]
    out_ref = refs[-1]
    tokens, width = hidden_ref.shape
    half = width // 2
    flat = flat_ref[...]

    def picker(group):
        slots = lax.broadcasted_iota(jnp.int32, (tokens, cap), 1) + group * cap
        return (slots == flat).astype(jnp.float32).astype(jnp.bfloat16)

    pickers = [picker(group) for group in range(groups)]
    step = 512
    for at in range(0, width, step):
        side, inner = divmod(at, half)
        whole = slice(at, at + step)
        part = slice(inner, inner + step)
        first, second = (az_ref, by_ref) if side == 0 else (ay_ref, bz_ref)
        added = (
            own_ref[:, whole].astype(jnp.float32)
            + first[0, :, part].astype(jnp.float32)
            + second[:, part].astype(jnp.float32)
        )
        coarse = added.astype(jnp.bfloat16)
        fine = (added - coarse.astype(jnp.float32)).astype(jnp.bfloat16)
        picked = jnp.dot(pickers[0], coarse, preferred_element_type=jnp.float32)
        picked = picked + jnp.dot(pickers[0], fine, preferred_element_type=jnp.float32)
        for group in range(1, groups):
            picked = picked + jnp.dot(
                pickers[group], back_refs[group - 1][:, whole], preferred_element_type=jnp.float32
            )
        out_ref[:, whole] = (hidden_ref[:, whole] + gate_ref[...] * picked).astype(jnp.bfloat16)


def finish(hidden, gate, flat, own, pieces, backs, groups, cap):
    tokens, width = hidden.shape
    operands = [hidden, gate, flat, own, *pieces, *backs]
    return pl.pallas_call(
        functools.partial(finish_kernel, groups, cap),
        out_shape=jax.ShapeDtypeStruct((tokens, width), jnp.bfloat16),
        in_specs=[VMEM] * len(operands),
        out_specs=VMEM,
        compiler_params=params(),
        cost_estimate=pl.CostEstimate(
            flops=4 * tokens * cap * (groups + 1) * width,
            bytes_accessed=16 * tokens * width,
            transcendentals=0,
        ),
        name="finish",
    )(*operands)


def body(state, query, enc_kv, gain, w_in, w_out, expert_id, slot, gate):
    tokens, width = state.shape[2:]
    devices = lax.axis_size("expert")
    pipes = lax.axis_size("pipe")
    groups = devices // WSPLIT
    cap = 3 * tokens // (2 * groups)
    half = width // 2

    def across(value, bit):
        return lax.ppermute(value, "expert", [(i, i ^ bit) for i in range(devices)])

    def groups_on(value, count):
        shift = count * WSPLIT
        return lax.ppermute(value, "expert", [(i, (i + shift) % devices) for i in range(devices)])

    kv = jnp.transpose(enc_kv[0], (1, 0, 2)).reshape(-1, width)
    kv_pieces = [kv]
    for shift in range(1, pipes):
        perm = [(i, (i + shift) % pipes) for i in range(pipes)]
        kv_pieces.append(lax.ppermute(kv, "pipe", perm))
    weights = [w_in, across(w_in, 1), w_out, across(w_out, 1)]

    group = lax.axis_index("expert") // WSPLIT
    offset = (expert_id[0, 0] - group) % groups
    flat = jnp.where(slot[0, 0] >= 0, offset * cap + slot[0, 0], -1)

    hidden, *packed = attend(
        state[0, 0],
        query[0, 0],
        gain.reshape(1, width),
        flat.reshape(1, tokens),
        kv_pieces,
        groups,
        cap,
    )
    near = packed[:2]
    far = [[], []]
    for count in range(1, groups):
        for side in range(2):
            far[side].append(groups_on(packed[2 * count + side], count))
    far = [jnp.concatenate(side, axis=0) if len(side) > 1 else side[0] for side in far]

    def spread(zero, one):
        y0, z0 = across(zero, 2), across(zero, 4)
        y1, z1 = across(one, 2), across(one, 4)
        d0, d1 = across(y0, 4), across(z1, 2)
        return [zero, one, y0, y1, z0, z1, d0, d1]

    def gather_sums(own, z0, y1, y0, z1):
        from_z, from_y = across(z0, 4), across(y1, 2)
        on_y = (y0.astype(jnp.float32) + from_z[1].astype(jnp.float32)).astype(jnp.bfloat16)
        on_z = (z1.astype(jnp.float32) + from_y[1].astype(jnp.float32)).astype(jnp.bfloat16)
        return own, from_z, from_y, across(on_y, 2), across(on_z, 4)

    near_sums = gather_sums(*ffn(spread(*near), weights))
    own, from_z, from_y, last_y, last_z = gather_sums(*ffn(spread(*far), weights))
    own = own.astype(jnp.float32)
    far_sum = jnp.concatenate(
        [
            own[:, :half] + from_z[0].astype(jnp.float32) + last_y.astype(jnp.float32),
            own[:, half:] + from_y[0].astype(jnp.float32) + last_z.astype(jnp.float32),
        ],
        axis=1,
    ).astype(jnp.bfloat16)
    backs = [
        groups_on(far_sum[(count - 1) * cap : count * cap], groups - count)
        for count in range(1, groups)
    ]
    output = finish(
        hidden,
        gate[0, 0].reshape(tokens, 1),
        flat.reshape(tokens, 1),
        near_sums[0],
        near_sums[1:],
        backs,
        groups,
        cap,
    )
    return output.reshape(1, 1, tokens, width)


def solution(mesh):
    return jax.shard_map(
        body,
        mesh=mesh,
        in_specs=(
            P("expert", "pipe", None, None),
            P("expert", "pipe", None, None),
            P("expert", "pipe", None, None),
            P(),
            P(None, "expert"),
            P("expert", None),
            P("expert", "pipe", None),
            P("expert", "pipe", None),
            P("expert", "pipe", None),
        ),
        out_specs=P("expert", "pipe", None, None),
        check_vma=False,
    )
```

time: 327 us -> 106 us (0.32)
  the two profiles are of different devices: /device:TPU:13 before, /device:TPU:0 now
where the time goes in v1:
time: 106 us
  waiting for transfers between devices  50.7 us (48%)
  starting transfers between devices  31.9 us (30%)
  Pallas kernels  14.4 us (14%)
  local copies, waits for them, and re-layouts  5.55 us (5%)
  other arithmetic  3.02 us (3%)
    ppermute x22, waiting for transfers between devices, across(): return lax.ppermute(value, 'expert', [(i, i ^ bit) for i in range(devices)])  23.8 us
    ppermute x22, starting transfers between devices, across(): return lax.ppermute(value, 'expert', [(i, i ^ bit) for i in range(devices)])  21.5 us
    ppermute x3, waiting for transfers between devices, groups_on(): lax.ppermute(value, 'expert', [(i, (i + shift) % devices) for i in range(...  21.2 us
    pallas_call x2, Pallas kernels, ffn(): pl.pallas_call(ffn_kernel, out_shape=[jax.ShapeDtypeStruct((rows, width),...  10.8 us
    ppermute x3, starting transfers between devices, groups_on(): lax.ppermute(value, 'expert', [(i, (i + shift) % devices) for i in range(...  7.43 us
    ppermute x1, waiting for transfers between devices, body(): kv_pieces.append(lax.ppermute(kv, 'pipe', perm))  5.79 us
    unnamed x18, local copies, waits for them, and re-layouts  3.56 us
    ppermute x1, starting transfers between devices, body(): kv_pieces.append(lax.ppermute(kv, 'pipe', perm))  3 us
  transfers between devices with their start and end apart: 26, of which 13 were waited for; matrix products, arithmetic and copies ran while one was open for 5% of the time, Pallas kernels for 12%

profile of v1, /device:TPU:0, one launch (start us, length us, event | category | flops | bytes accessed | tf_op | source)
XLA Modules:
  0.0 105.7 jit_solution(1273195958425141028)
XLA Ops:
  0.0 0.5 collective-permute-start.7
  0.5 1.0 copy.10
  1.5 3.0 %collective-permute-start = (bf16[64,2048]{1,0:T(8,128)(2,1)S(1)}, bf16[64,2048]{1,0:T(8,128)(2,1)S(1)}, u32[]{:S(2)}, u32[]{:S(2)}) collective-permute-start(bf16[64,2048]{1,0:T(8,128)(2,1)S(1)} %bitcast.46), channel_id=1, source_target_pairs={{0,16},{16,0},{1,17},{17,1},{2,18},{18,2},{3,19},{19,3},{4,20},{20... | collective-permute-start | bytes 786440 | tf_op jit(solution)/shard_map/ppermute | solution.py:229
  4.5 0.7 compare_select_fusion.2.refs_3_
  5.2 5.8 %collective-permute-done.refs_5_ = bf16[64,2048]{1,0:T(8,128)(2,1)S(1)} collective-permute-done((bf16[64,2048]{1,0:T(8,128)(2,1)S(1)}, bf16[64,2048]{1,0:T(8,128)(2,1)S(1)}, u32[]{:S(2)}, u32[]{:S(2)}) %collective-permute-start) | collective-permute-done | bytes 262176 | tf_op jit(solution)/shard_map/ppermute | solution.py:229
  11.0 1.0 copy-done
  12.1 1.0 copy-done.1
  13.1 0.7 copy-done.2
  13.8 2.1 %attend.1 = (f32[128,2048]{1,0:T(8,128)S(1)}, bf16[96,1024]{1,0:T(8,128)(2,1)}, bf16[96,1024]{1,0:T(8,128)(2,1)}, bf16[96,1024]{1,0:T(8,128)(2,1)S(1)}, bf16[96,1024]{1,0:T(8,128)(2,1)S(1)}) custom-call(bf16[128,2048]{1,0:T(8,128)(2,1)S(1)} %bitcast.48, bf16[128,2048]{1,0:T(8,128)(2,1)S(1)} %bitcast.49, f32[1,2048]{1,0:T(1,128)S(1)} %bitcast.50, ...), custom_call_target="tpu_custom_call" | custom-call | flops 134217728 | bytes 3145728 | tf_op jit(solution)/shard_map/attend/pallas_call | solution.py:76
  15.9 2.8 %collective-permute-start.13 = (bf16[96,1024]{1,0:T(8,128)(2,1)S(1)}, bf16[96,1024]{1,0:T(8,128)(2,1)S(1)}, u32[]{:S(2)}, u32[]{:S(2)}) collective-permute-start(bf16[96,1024]{1,0:T(8,128)(2,1)S(1)} %get-tuple-element.28), channel_id=1, source_target_pairs={{0,8},{1,9},{2,10},{3,11},{4,12},{5,13},{6,14},{7,15},{8,0},{9,1},... | collective-permute-start | bytes 589832 | tf_op jit(solution)/shard_map/ppermute | solution.py:223
  18.8 1.8 %collective-permute-start.1 = (bf16[96,1024]{1,0:T(8,128)(2,1)}, bf16[96,1024]{1,0:T(8,128)(2,1)}, u32[]{:S(2)}, u32[]{:S(2)}) collective-permute-start(bf16[96,1024]{1,0:T(8,128)(2,1)} %get-tuple-element.21.refs_0_), channel_id=1, source_target_pairs={{0,2},{1,3},{2,0},{3,1},{4,6},{5,7},{6,4},{7,5},{8,10},{9,11},{10,... | collective-permute-start | bytes 589832 | tf_op jit(solution)/shard_map/ppermute | solution.py:219
  20.6 12.0 %collective-permute-done.13.refs_0_ = bf16[96,1024]{1,0:T(8,128)(2,1)S(1)} collective-permute-done((bf16[96,1024]{1,0:T(8,128)(2,1)S(1)}, bf16[96,1024]{1,0:T(8,128)(2,1)S(1)}, u32[]{:S(2)}, u32[]{:S(2)}) %collective-permute-start.13) | collective-permute-done | bytes 196640 | tf_op jit(solution)/shard_map/ppermute | solution.py:223
  32.6 3.2 %collective-permute-done.14.refs_1_ = bf16[96,1024]{1,0:T(8,128)(2,1)S(1)} collective-permute-done((bf16[96,1024]{1,0:T(8,128)(2,1)S(1)}, bf16[96,1024]{1,0:T(8,128)(2,1)S(1)}, u32[]{:S(2)}, u32[]{:S(2)}) %collective-permute-start.14) | collective-permute-done | bytes 196640 | tf_op jit(solution)/shard_map/ppermute | solution.py:223
  35.8 1.5 %collective-permute-start.15 = (bf16[96,1024]{1,0:T(8,128)(2,1)S(1)}, bf16[96,1024]{1,0:T(8,128)(2,1)S(1)}, u32[]{:S(2)}, u32[]{:S(2)}) collective-permute-start(bf16[96,1024]{1,0:T(8,128)(2,1)S(1)} %collective-permute-done.13.refs_0_), channel_id=1, source_target_pairs={{0,2},{1,3},{2,0},{3,1},{4,6},{5,7},{6,4},{7,5},{8,10},{9,11},{10,... | collective-permute-start | bytes 589832 | tf_op jit(solution)/shard_map/ppermute | solution.py:219
  37.3 0.6 collective-permute-start.18
  37.8 2.9 %collective-permute-done.4.refs_5_ = bf16[96,1024]{1,0:T(8,128)(2,1)} collective-permute-done((bf16[96,1024]{1,0:T(8,128)(2,1)}, bf16[96,1024]{1,0:T(8,128)(2,1)}, u32[]{:S(2)}, u32[]{:S(2)}) %collective-permute-start.4) | collective-permute-done | bytes 196640 | tf_op jit(solution)/shard_map/ppermute | solution.py:219
  40.8 1.5 %collective-permute-start.16 = (bf16[96,1024]{1,0:T(8,128)(2,1)S(1)}, bf16[96,1024]{1,0:T(8,128)(2,1)S(1)}, u32[]{:S(2)}, u32[]{:S(2)}) collective-permute-start(bf16[96,1024]{1,0:T(8,128)(2,1)S(1)} %collective-permute-done.14.refs_1_), channel_id=1, source_target_pairs={{0,2},{1,3},{2,0},{3,1},{4,6},{5,7},{6,4},{7,5},{8,10},{9,11},{10,... | collective-permute-start | bytes 589832 | tf_op jit(solution)/shard_map/ppermute | solution.py:219
  42.3 1.8 %collective-permute-start.17 = (bf16[96,1024]{1,0:T(8,128)(2,1)S(1)}, bf16[96,1024]{1,0:T(8,128)(2,1)S(1)}, u32[]{:S(2)}, u32[]{:S(2)}) collective-permute-start(bf16[96,1024]{1,0:T(8,128)(2,1)S(1)} %collective-permute-done.13.refs_0_), channel_id=1, source_target_pairs={{0,4},{1,5},{2,6},{3,7},{4,0},{5,1},{6,2},{7,3},{8,12},{9,13},{10,... | collective-permute-start | bytes 589832 | tf_op jit(solution)/shard_map/ppermute | solution.py:219
  44.1 1.0 collective-permute-done.18.refs_5_
  45.1 1.3 %collective-permute-done.16.refs_3_ = bf16[96,1024]{1,0:T(8,128)(2,1)S(1)} collective-permute-done((bf16[96,1024]{1,0:T(8,128)(2,1)S(1)}, bf16[96,1024]{1,0:T(8,128)(2,1)S(1)}, u32[]{:S(2)}, u32[]{:S(2)}) %collective-permute-start.16) | collective-permute-done | bytes 196640 | tf_op jit(solution)/shard_map/ppermute | solution.py:219
  46.4 1.5 %collective-permute-start.20 = (bf16[96,1024]{1,0:T(8,128)(2,1)S(1)}, bf16[96,1024]{1,0:T(8,128)(2,1)S(1)}, u32[]{:S(2)}, u32[]{:S(2)}) collective-permute-start(bf16[96,1024]{1,0:T(8,128)(2,1)S(1)} %collective-permute-done.18.refs_5_), channel_id=1, source_target_pairs={{0,2},{1,3},{2,0},{3,1},{4,6},{5,7},{6,4},{7,5},{8,10},{9,11},{10,... | collective-permute-start | bytes 589832 | tf_op jit(solution)/shard_map/ppermute | solution.py:219
  47.9 2.2 %collective-permute-done.17.refs_4_ = bf16[96,1024]{1,0:T(8,128)(2,1)S(1)} collective-permute-done((bf16[96,1024]{1,0:T(8,128)(2,1)S(1)}, bf16[96,1024]{1,0:T(8,128)(2,1)S(1)}, u32[]{:S(2)}, u32[]{:S(2)}) %collective-permute-start.17) | collective-permute-done | bytes 196640 | tf_op jit(solution)/shard_map/ppermute | solution.py:219
  50.1 1.3 %collective-permute-start.2 = (bf16[96,1024]{1,0:T(8,128)(2,1)}, bf16[96,1024]{1,0:T(8,128)(2,1)}, u32[]{:S(2)}, u32[]{:S(2)}) collective-permute-start(bf16[96,1024]{1,0:T(8,128)(2,1)} %get-tuple-element.22.refs_1_), channel_id=1, source_target_pairs={{0,2},{1,3},{2,0},{3,1},{4,6},{5,7},{6,4},{7,5},{8,10},{9,11},{10,... | collective-permute-start | bytes 589832 | tf_op jit(solution)/shard_map/ppermute | solution.py:219
  51.4 1.2 %collective-permute-done.19.refs_6_ = bf16[96,1024]{1,0:T(8,128)(2,1)S(1)} collective-permute-done((bf16[96,1024]{1,0:T(8,128)(2,1)S(1)}, bf16[96,1024]{1,0:T(8,128)(2,1)S(1)}, u32[]{:S(2)}, u32[]{:S(2)}) %collective-permute-start.19) | collective-permute-done | bytes 196640 | tf_op jit(solution)/shard_map/ppermute | solution.py:219
  52.6 0.8 collective-permute-start.3
  53.3 0.4 collective-permute-done.20.refs_7_
  53.7 1.5 %collective-permute-start.5 = (bf16[96,1024]{1,0:T(8,128)(2,1)}, bf16[96,1024]{1,0:T(8,128)(2,1)}, u32[]{:S(2)}, u32[]{:S(2)}) collective-permute-start(bf16[96,1024]{1,0:T(8,128)(2,1)} %collective-permute-done.1.refs_2_), channel_id=1, source_target_pairs={{0,4},{1,5},{2,6},{3,7},{4,0},{5,1},{6,2},{7,3},{8,12},{9,13},{10,... | collective-permute-start | bytes 589832 | tf_op jit(solution)/shard_map/ppermute | solution.py:219
  55.2 1.5 %collective-permute-start.6 = (bf16[96,1024]{1,0:T(8,128)(2,1)}, bf16[96,1024]{1,0:T(8,128)(2,1)}, u32[]{:S(2)}, u32[]{:S(2)}) collective-permute-start(bf16[96,1024]{1,0:T(8,128)(2,1)} %collective-permute-done.4.refs_5_), channel_id=1, source_target_pairs={{0,2},{1,3},{2,0},{3,1},{4,6},{5,7},{6,4},{7,5},{8,10},{9,11},{10,... | collective-permute-start | bytes 589832 | tf_op jit(solution)/shard_map/ppermute | solution.py:219
  56.7 5.1 %expert_ffn.3 = (bf16[96,2048]{1,0:T(8,128)(2,1)S(1)}, bf16[2,96,1024]{2,1,0:T(8,128)(2,1)S(1)}, bf16[2,96,1024]{2,1,0:T(8,128)(2,1)}, bf16[96,1024]{1,0:T(8,128)(2,1)S(1)}, bf16[96,1024]{1,0:T(8,128)(2,1)S(1)}) custom-call(bf16[96,1024]{1,0:T(8,128)(2,1)S(1)} %collective-permute-done.13.refs_0_, bf16[96,1024]{1,0:T(8,128)(2,1)S(1)} %collective-permute-done.14.refs_1_, ...), custom_call_target="tpu_custom_call" | custom-call | flops 2415919104 | bytes 9437184 | tf_op jit(solution)/shard_map/expert_ffn/pallas_call | solution.py:140
  61.8 0.8 copy-done.4
  62.6 0.5 collective-permute-start.23
  63.2 0.7 copy.11
  64.1 0.6 collective-permute-start.21
  64.7 5.8 %expert_ffn.2 = (bf16[96,2048]{1,0:T(8,128)(2,1)S(1)}, bf16[2,96,1024]{2,1,0:T(8,128)(2,1)S(1)}, bf16[2,96,1024]{2,1,0:T(8,128)(2,1)S(1)}, bf16[96,1024]{1,0:T(8,128)(2,1)S(1)}, bf16[96,1024]{1,0:T(8,128)(2,1)S(1)}) custom-call(bf16[96,1024]{1,0:T(8,128)(2,1)} %get-tuple-element.21.refs_0_, bf16[96,1024]{1,0:T(8,128)(2,1)} %get-tuple-element.22.refs_1_, ...), custom_call_target="tpu_custom_call" | custom-call | flops 2415919104 | bytes 9437184 | tf_op jit(solution)/shard_map/expert_ffn/pallas_call | solution.py:140
  70.5 1.7 %collective-permute-start.10 = (bf16[2,96,1024]{2,1,0:T(8,128)(2,1)S(1)}, bf16[2,96,1024]{2,1,0:T(8,128)(2,1)S(1)}, u32[]{:S(2)}, u32[]{:S(2)}) collective-permute-start(bf16[2,96,1024]{2,1,0:T(8,128)(2,1)S(1)} %get-tuple-element.25), channel_id=1, source_target_pairs={{0,2},{1,3},{2,0},{3,1},{4,6},{5,7},{6,4},{7,5},{8,10},{9,11},{10,... | collective-permute-start | bytes 1179656 | tf_op jit(solution)/shard_map/ppermute | solution.py:219
  72.2 1.4 %collective-permute-start.9 = (bf16[2,96,1024]{2,1,0:T(8,128)(2,1)S(1)}, bf16[2,96,1024]{2,1,0:T(8,128)(2,1)S(1)}, u32[]{:S(2)}, u32[]{:S(2)}) collective-permute-start(bf16[2,96,1024]{2,1,0:T(8,128)(2,1)S(1)} %get-tuple-element.24), channel_id=1, source_target_pairs={{0,4},{1,5},{2,6},{3,7},{4,0},{5,1},{6,2},{7,3},{8,12},{9,13},{10,... | collective-permute-start | bytes 1179656 | tf_op jit(solution)/shard_map/ppermute | solution.py:219
  73.6 1.0 fusion.4
  74.6 0.7 collective-permute-start.24
  75.3 1.0 collective-permute-start.22
  76.3 5.0 %collective-permute-done.10.refs_5_ = bf16[2,96,1024]{2,1,0:T(8,128)(2,1)S(1)} collective-permute-done((bf16[2,96,1024]{2,1,0:T(8,128)(2,1)S(1)}, bf16[2,96,1024]{2,1,0:T(8,128)(2,1)S(1)}, u32[]{:S(2)}, u32[]{:S(2)}) %collective-permute-start.10) | collective-permute-done | bytes 393248 | tf_op jit(solution)/shard_map/ppermute | solution.py:219
  81.4 0.5 collective-permute-start.12
  81.8 5.1 %collective-permute-done.24 = bf16[96,1024]{1,0:T(8,128)(2,1)S(1)} collective-permute-done((bf16[96,1024]{1,0:T(8,128)(2,1)S(1)}, bf16[96,1024]{1,0:T(8,128)(2,1)S(1)}, u32[]{:S(2)}, u32[]{:S(2)}) %collective-permute-start.24) | collective-permute-done | bytes 196640 | tf_op jit(solution)/shard_map/ppermute | solution.py:219
  86.9 1.1 %fusion.3 = (bf16[96,1024]{1,0:T(8,128)(2,1)S(1)}, bf16[96,1024]{1,0:T(8,128)(2,1)S(1)}) fusion(f32[96,2048]{1,0:T(8,128)S(1)} %convert_element_type.78, bf16[96,1024]{1,0:T(8,128)(2,1)S(1)} %collective-permute-done.22, bf16[2,96,1024]{2,1,0:T(8,128)(2,1)S(1)} %collective-permute-done.21, bf16[96,1024]{1,0:T(8,128)(2,1)S(1)} %collective-permute-done.24, ...), kind=kLoop, calls=%fused_computation.5 | loop fusion | flops 983040 | bytes 1966080 | tf_op jit(solution)/shard_map/convert.6
  88.0 4.5 %collective-permute-start.25 = (bf16[96,2048]{1,0:T(8,128)(2,1)S(1)}, bf16[96,2048]{1,0:T(8,128)(2,1)S(1)}, u32[]{:S(2)}, u32[]{:S(2)}) collective-permute-start(bf16[96,2048]{1,0:T(8,128)(2,1)S(1)} %pad_maximum_fusion), channel_id=1, source_target_pairs={{0,8},{1,9},{2,10},{3,11},{4,12},{5,13},{6,14},{7,15},{8,0},{9,1},... | collective-permute-start | bytes 1179656 | tf_op jit(solution)/shard_map/ppermute | solution.py:223
  92.6 0.9 collective-permute-start.11
  93.6 4.7 %collective-permute-done.11.refs_6_ = bf16[96,1024]{1,0:T(8,128)(2,1)S(1)} collective-permute-done((bf16[96,1024]{1,0:T(8,128)(2,1)S(1)}, bf16[96,1024]{1,0:T(8,128)(2,1)S(1)}, u32[]{:S(2)}, u32[]{:S(2)}) %collective-permute-start.11) | collective-permute-done | bytes 196640 | tf_op jit(solution)/shard_map/ppermute | solution.py:219
  98.3 5.9 %collective-permute-done.25.refs_8_ = bf16[96,2048]{1,0:T(8,128)(2,1)S(1)} collective-permute-done((bf16[96,2048]{1,0:T(8,128)(2,1)S(1)}, bf16[96,2048]{1,0:T(8,128)(2,1)S(1)}, u32[]{:S(2)}, u32[]{:S(2)}) %collective-permute-start.25) | collective-permute-done | bytes 393248 | tf_op jit(solution)/shard_map/ppermute | solution.py:223
  104.3 1.4 %finish.1 = bf16[128,2048]{1,0:T(8,128)(2,1)} custom-call(f32[128,2048]{1,0:T(8,128)S(1)} %get-tuple-element.20.refs_0_, f32[128,1]{1,0:T(8,128)S(1)} %copy.16.refs_1_, s32[128,1]{1,0:T(8,128)S(1)} %fusion.11.refs_2_, bf16[96,2048]{1,0:T(8,128)(2,1)S(1)} %get-tuple-element.23.refs_3_, bf16[2,96,1024]{2,1,0:T(8,128)(2,1)S(1)} %collective-permute-done.9.refs_4_, ...), custom_call_target="tpu_custom_call" | custom-call | flops 301989888 | bytes 4194304 | tf_op jit(solution)/shard_map/finish/pallas_call | solution.py:195
  (40 shorter events, 0.7 us)
Async XLA Ops:
  0.0 55.2 %collective-permute-start.7 = (bf16[2048,384]{1,0:T(8,128)(2,1)}, bf16[2048,384]{1,0:T(8,128)(2,1)}, u32[]{:S(2)}, u32[]{:S(2)}) collective-permute-start(bf16[2048,384]{1,0:T(8,128)(2,1)} %refs_8_.3), channel_id=1, source_target_pairs={{0,1},{1,0},{2,3},{3,2},{4,5},{5,4},{6,7},{7,6},{8,9},{9,8},{10,11... | collective-permute-start | bytes 4718600 | tf_op jit(solution)/shard_map/ppermute | solution.py:219
  0.5 56.3 %collective-permute-start.8 = (bf16[384,2048]{1,0:T(8,128)(2,1)}, bf16[384,2048]{1,0:T(8,128)(2,1)}, u32[]{:S(2)}, u32[]{:S(2)}) collective-permute-start(bf16[384,2048]{1,0:T(8,128)(2,1)} %refs_10_.3), channel_id=1, source_target_pairs={{0,1},{1,0},{2,3},{3,2},{4,5},{5,4},{6,7},{7,6},{8,9},{9,8},{10,11... | collective-permute-start | bytes 4718600 | tf_op jit(solution)/shard_map/ppermute | solution.py:219
  1.5 9.5 %collective-permute-start = (bf16[64,2048]{1,0:T(8,128)(2,1)S(1)}, bf16[64,2048]{1,0:T(8,128)(2,1)S(1)}, u32[]{:S(2)}, u32[]{:S(2)}) collective-permute-start(bf16[64,2048]{1,0:T(8,128)(2,1)S(1)} %bitcast.46), channel_id=1, source_target_pairs={{0,16},{16,0},{1,17},{17,1},{2,18},{18,2},{3,19},{19,3},{4,20},{20... | collective-permute-start | bytes 786440 | tf_op jit(solution)/shard_map/ppermute | solution.py:229
  11.0 1.0 copy-start
  12.1 1.0 copy-start.1
  13.1 0.7 copy-start.2
  13.8 42.9 %copy-start.3 = (bf16[2048,384]{1,0:T(8,128)(2,1)S(1)}, bf16[2048,384]{1,0:T(8,128)(2,1)}, u32[]{:S(2)}) copy-start(bf16[2048,384]{1,0:T(8,128)(2,1)} %refs_8_.3) | copy-start | bytes 4718596
  15.9 16.7 %collective-permute-start.13 = (bf16[96,1024]{1,0:T(8,128)(2,1)S(1)}, bf16[96,1024]{1,0:T(8,128)(2,1)S(1)}, u32[]{:S(2)}, u32[]{:S(2)}) collective-permute-start(bf16[96,1024]{1,0:T(8,128)(2,1)S(1)} %get-tuple-element.28), channel_id=1, source_target_pairs={{0,8},{1,9},{2,10},{3,11},{4,12},{5,13},{6,14},{7,15},{8,0},{9,1},... | collective-permute-start | bytes 589832 | tf_op jit(solution)/shard_map/ppermute | solution.py:223
  18.7 17.1 %collective-permute-start.14 = (bf16[96,1024]{1,0:T(8,128)(2,1)S(1)}, bf16[96,1024]{1,0:T(8,128)(2,1)S(1)}, u32[]{:S(2)}, u32[]{:S(2)}) collective-permute-start(bf16[96,1024]{1,0:T(8,128)(2,1)S(1)} %get-tuple-element.29), channel_id=1, source_target_pairs={{0,8},{1,9},{2,10},{3,11},{4,12},{5,13},{6,14},{7,15},{8,0},{9,1},... | collective-permute-start | bytes 589832 | tf_op jit(solution)/shard_map/ppermute | solution.py:223
  18.8 18.5 %collective-permute-start.1 = (bf16[96,1024]{1,0:T(8,128)(2,1)}, bf16[96,1024]{1,0:T(8,128)(2,1)}, u32[]{:S(2)}, u32[]{:S(2)}) collective-permute-start(bf16[96,1024]{1,0:T(8,128)(2,1)} %get-tuple-element.21.refs_0_), channel_id=1, source_target_pairs={{0,2},{1,3},{2,0},{3,1},{4,6},{5,7},{6,4},{7,5},{8,10},{9,11},{10,... | collective-permute-start | bytes 589832 | tf_op jit(solution)/shard_map/ppermute | solution.py:219
  32.6 30.5 %copy-start.8 = (s32[1,1,128]{2,1,0:T(1,128)S(1)}, s32[1,1,128]{2,1,0:T(1,128)}, u32[]{:S(2)}) copy-start(s32[1,1,128]{2,1,0:T(1,128)} %param.15) | copy-start | bytes 1540
  32.6 30.6 %copy-start.6 = (s32[1,1,128]{2,1,0:T(1,128)S(1)}, s32[1,1,128]{2,1,0:T(1,128)}, u32[]{:S(2)}) copy-start(s32[1,1,128]{2,1,0:T(1,128)} %param.16) | copy-start | bytes 1540
  32.6 31.3 %copy-start.7 = (f32[1,1,128]{2,1,0:T(1,128)S(1)}, f32[1,1,128]{2,1,0:T(1,128)}, u32[]{:S(2)}) copy-start(f32[1,1,128]{2,1,0:T(1,128)} %param.17) | copy-start | bytes 1540
  32.6 8.2 %collective-permute-start.4 = (bf16[96,1024]{1,0:T(8,128)(2,1)}, bf16[96,1024]{1,0:T(8,128)(2,1)}, u32[]{:S(2)}, u32[]{:S(2)}) collective-permute-start(bf16[96,1024]{1,0:T(8,128)(2,1)} %get-tuple-element.22.refs_1_), channel_id=1, source_target_pairs={{0,4},{1,5},{2,6},{3,7},{4,0},{5,1},{6,2},{7,3},{8,12},{9,13},{10,... | collective-permute-start | bytes 589832 | tf_op jit(solution)/shard_map/ppermute | solution.py:219
  35.8 6.5 %collective-permute-start.15 = (bf16[96,1024]{1,0:T(8,128)(2,1)S(1)}, bf16[96,1024]{1,0:T(8,128)(2,1)S(1)}, u32[]{:S(2)}, u32[]{:S(2)}) collective-permute-start(bf16[96,1024]{1,0:T(8,128)(2,1)S(1)} %collective-permute-done.13.refs_0_), channel_id=1, source_target_pairs={{0,2},{1,3},{2,0},{3,1},{4,6},{5,7},{6,4},{7,5},{8,10},{9,11},{10,... | collective-permute-start | bytes 589832 | tf_op jit(solution)/shard_map/ppermute | solution.py:219
  37.3 7.8 %collective-permute-start.18 = (bf16[96,1024]{1,0:T(8,128)(2,1)S(1)}, bf16[96,1024]{1,0:T(8,128)(2,1)S(1)}, u32[]{:S(2)}, u32[]{:S(2)}) collective-permute-start(bf16[96,1024]{1,0:T(8,128)(2,1)S(1)} %collective-permute-done.14.refs_1_), channel_id=1, source_target_pairs={{0,4},{1,5},{2,6},{3,7},{4,0},{5,1},{6,2},{7,3},{8,12},{9,13},{10,... | collective-permute-start | bytes 589832 | tf_op jit(solution)/shard_map/ppermute | solution.py:219
  40.8 5.7 %collective-permute-start.16 = (bf16[96,1024]{1,0:T(8,128)(2,1)S(1)}, bf16[96,1024]{1,0:T(8,128)(2,1)S(1)}, u32[]{:S(2)}, u32[]{:S(2)}) collective-permute-start(bf16[96,1024]{1,0:T(8,128)(2,1)S(1)} %collective-permute-done.14.refs_1_), channel_id=1, source_target_pairs={{0,2},{1,3},{2,0},{3,1},{4,6},{5,7},{6,4},{7,5},{8,10},{9,11},{10,... | collective-permute-start | bytes 589832 | tf_op jit(solution)/shard_map/ppermute | solution.py:219
  42.3 7.8 %collective-permute-start.17 = (bf16[96,1024]{1,0:T(8,128)(2,1)S(1)}, bf16[96,1024]{1,0:T(8,128)(2,1)S(1)}, u32[]{:S(2)}, u32[]{:S(2)}) collective-permute-start(bf16[96,1024]{1,0:T(8,128)(2,1)S(1)} %collective-permute-done.13.refs_0_), channel_id=1, source_target_pairs={{0,4},{1,5},{2,6},{3,7},{4,0},{5,1},{6,2},{7,3},{8,12},{9,13},{10,... | collective-permute-start | bytes 589832 | tf_op jit(solution)/shard_map/ppermute | solution.py:219
  45.1 7.5 %collective-permute-start.19 = (bf16[96,1024]{1,0:T(8,128)(2,1)S(1)}, bf16[96,1024]{1,0:T(8,128)(2,1)S(1)}, u32[]{:S(2)}, u32[]{:S(2)}) collective-permute-start(bf16[96,1024]{1,0:T(8,128)(2,1)S(1)} %collective-permute-done.15.refs_2_), channel_id=1, source_target_pairs={{0,4},{1,5},{2,6},{3,7},{4,0},{5,1},{6,2},{7,3},{8,12},{9,13},{10,... | collective-permute-start | bytes 589832 | tf_op jit(solution)/shard_map/ppermute | solution.py:219
  46.4 7.3 %collective-permute-start.20 = (bf16[96,1024]{1,0:T(8,128)(2,1)S(1)}, bf16[96,1024]{1,0:T(8,128)(2,1)S(1)}, u32[]{:S(2)}, u32[]{:S(2)}) collective-permute-start(bf16[96,1024]{1,0:T(8,128)(2,1)S(1)} %collective-permute-done.18.refs_5_), channel_id=1, source_target_pairs={{0,2},{1,3},{2,0},{3,1},{4,6},{5,7},{6,4},{7,5},{8,10},{9,11},{10,... | collective-permute-start | bytes 589832 | tf_op jit(solution)/shard_map/ppermute | solution.py:219
  50.1 14.0 %collective-permute-start.2 = (bf16[96,1024]{1,0:T(8,128)(2,1)}, bf16[96,1024]{1,0:T(8,128)(2,1)}, u32[]{:S(2)}, u32[]{:S(2)}) collective-permute-start(bf16[96,1024]{1,0:T(8,128)(2,1)} %get-tuple-element.22.refs_1_), channel_id=1, source_target_pairs={{0,2},{1,3},{2,0},{3,1},{4,6},{5,7},{6,4},{7,5},{8,10},{9,11},{10,... | collective-permute-start | bytes 589832 | tf_op jit(solution)/shard_map/ppermute | solution.py:219
  52.6 12.2 %collective-permute-start.3 = (bf16[96,1024]{1,0:T(8,128)(2,1)}, bf16[96,1024]{1,0:T(8,128)(2,1)}, u32[]{:S(2)}, u32[]{:S(2)}) collective-permute-start(bf16[96,1024]{1,0:T(8,128)(2,1)} %get-tuple-element.21.refs_0_), channel_id=1, source_target_pairs={{0,4},{1,5},{2,6},{3,7},{4,0},{5,1},{6,2},{7,3},{8,12},{9,13},{10,... | collective-permute-start | bytes 589832 | tf_op jit(solution)/shard_map/ppermute | solution.py:219
  53.7 11.0 %collective-permute-start.5 = (bf16[96,1024]{1,0:T(8,128)(2,1)}, bf16[96,1024]{1,0:T(8,128)(2,1)}, u32[]{:S(2)}, u32[]{:S(2)}) collective-permute-start(bf16[96,1024]{1,0:T(8,128)(2,1)} %collective-permute-done.1.refs_2_), channel_id=1, source_target_pairs={{0,4},{1,5},{2,6},{3,7},{4,0},{5,1},{6,2},{7,3},{8,12},{9,13},{10,... | collective-permute-start | bytes 589832 | tf_op jit(solution)/shard_map/ppermute | solution.py:219
  55.2 9.5 %collective-permute-start.6 = (bf16[96,1024]{1,0:T(8,128)(2,1)}, bf16[96,1024]{1,0:T(8,128)(2,1)}, u32[]{:S(2)}, u32[]{:S(2)}) collective-permute-start(bf16[96,1024]{1,0:T(8,128)(2,1)} %collective-permute-done.4.refs_5_), channel_id=1, source_target_pairs={{0,2},{1,3},{2,0},{3,1},{4,6},{5,7},{6,4},{7,5},{8,10},{9,11},{10,... | collective-permute-start | bytes 589832 | tf_op jit(solution)/shard_map/ppermute | solution.py:219
  61.8 0.8 copy-start.4
  62.6 11.0 %collective-permute-start.23 = (bf16[2,96,1024]{2,1,0:T(8,128)(2,1)}, bf16[2,96,1024]{2,1,0:T(8,128)(2,1)}, u32[]{:S(2)}, u32[]{:S(2)}) collective-permute-start(bf16[2,96,1024]{2,1,0:T(8,128)(2,1)} %get-tuple-element.33), channel_id=1, source_target_pairs={{0,2},{1,3},{2,0},{3,1},{4,6},{5,7},{6,4},{7,5},{8,10},{9,11},{10,... | collective-permute-start | bytes 1179656 | tf_op jit(solution)/shard_map/ppermute | solution.py:219
  64.1 11.2 %collective-permute-start.21 = (bf16[2,96,1024]{2,1,0:T(8,128)(2,1)}, bf16[2,96,1024]{2,1,0:T(8,128)(2,1)S(1)}, u32[]{:S(2)}, u32[]{:S(2)}) collective-permute-start(bf16[2,96,1024]{2,1,0:T(8,128)(2,1)} %copy-done.4), channel_id=1, source_target_pairs={{0,4},{1,5},{2,6},{3,7},{4,0},{5,1},{6,2},{7,3},{8,12},{9,13},{10,... | collective-permute-start | bytes 1179656 | tf_op jit(solution)/shard_map/ppermute | solution.py:219
  70.5 10.8 %collective-permute-start.10 = (bf16[2,96,1024]{2,1,0:T(8,128)(2,1)S(1)}, bf16[2,96,1024]{2,1,0:T(8,128)(2,1)S(1)}, u32[]{:S(2)}, u32[]{:S(2)}) collective-permute-start(bf16[2,96,1024]{2,1,0:T(8,128)(2,1)S(1)} %get-tuple-element.25), channel_id=1, source_target_pairs={{0,2},{1,3},{2,0},{3,1},{4,6},{5,7},{6,4},{7,5},{8,10},{9,11},{10,... | collective-permute-start | bytes 1179656 | tf_op jit(solution)/shard_map/ppermute | solution.py:219
  72.2 20.3 %collective-permute-start.9 = (bf16[2,96,1024]{2,1,0:T(8,128)(2,1)S(1)}, bf16[2,96,1024]{2,1,0:T(8,128)(2,1)S(1)}, u32[]{:S(2)}, u32[]{:S(2)}) collective-permute-start(bf16[2,96,1024]{2,1,0:T(8,128)(2,1)S(1)} %get-tuple-element.24), channel_id=1, source_target_pairs={{0,4},{1,5},{2,6},{3,7},{4,0},{5,1},{6,2},{7,3},{8,12},{9,13},{10,... | collective-permute-start | bytes 1179656 | tf_op jit(solution)/shard_map/ppermute | solution.py:219
  74.6 12.3 %collective-permute-start.24 = (bf16[96,1024]{1,0:T(8,128)(2,1)S(1)}, bf16[96,1024]{1,0:T(8,128)(2,1)S(1)}, u32[]{:S(2)}, u32[]{:S(2)}) collective-permute-start(bf16[96,1024]{1,0:T(8,128)(2,1)S(1)} %fusion.4), channel_id=1, source_target_pairs={{0,4},{1,5},{2,6},{3,7},{4,0},{5,1},{6,2},{7,3},{8,12},{9,13},{10,... | collective-permute-start | bytes 589832 | tf_op jit(solution)/shard_map/ppermute | solution.py:219
  75.3 11.6 %collective-permute-start.22 = (bf16[96,1024]{1,0:T(8,128)(2,1)S(1)}, bf16[96,1024]{1,0:T(8,128)(2,1)S(1)}, u32[]{:S(2)}, u32[]{:S(2)}) collective-permute-start(bf16[96,1024]{1,0:T(8,128)(2,1)S(1)} %fusion.5), channel_id=1, source_target_pairs={{0,2},{1,3},{2,0},{3,1},{4,6},{5,7},{6,4},{7,5},{8,10},{9,11},{10,... | collective-permute-start | bytes 589832 | tf_op jit(solution)/shard_map/ppermute | solution.py:219
  81.4 12.2 %copy-start.5 = (s32[128,1]{1,0:T(8,128)S(1)}, s32[128,1]{1,0:T(8,128)}, u32[]{:S(2)}) copy-start(s32[128,1]{1,0:T(8,128)} %copy.11) | copy-start | bytes 1540
  81.4 12.2 %collective-permute-start.12 = (bf16[96,1024]{1,0:T(8,128)(2,1)S(1)}, bf16[96,1024]{1,0:T(8,128)(2,1)S(1)}, u32[]{:S(2)}, u32[]{:S(2)}) collective-permute-start(bf16[96,1024]{1,0:T(8,128)(2,1)S(1)} %fusion.6), channel_id=1, source_target_pairs={{0,4},{1,5},{2,6},{3,7},{4,0},{5,1},{6,2},{7,3},{8,12},{9,13},{10,... | collective-permute-start | bytes 589832 | tf_op jit(solution)/shard_map/ppermute | solution.py:219
  88.0 16.2 %collective-permute-start.25 = (bf16[96,2048]{1,0:T(8,128)(2,1)S(1)}, bf16[96,2048]{1,0:T(8,128)(2,1)S(1)}, u32[]{:S(2)}, u32[]{:S(2)}) collective-permute-start(bf16[96,2048]{1,0:T(8,128)(2,1)S(1)} %pad_maximum_fusion), channel_id=1, source_target_pairs={{0,8},{1,9},{2,10},{3,11},{4,12},{5,13},{6,14},{7,15},{8,0},{9,1},... | collective-permute-start | bytes 1179656 | tf_op jit(solution)/shard_map/ppermute | solution.py:223
  92.6 5.7 %collective-permute-start.11 = (bf16[96,1024]{1,0:T(8,128)(2,1)S(1)}, bf16[96,1024]{1,0:T(8,128)(2,1)S(1)}, u32[]{:S(2)}, u32[]{:S(2)}) collective-permute-start(bf16[96,1024]{1,0:T(8,128)(2,1)S(1)} %fusion.7), channel_id=1, source_target_pairs={{0,2},{1,3},{2,0},{3,1},{4,6},{5,7},{6,4},{7,5},{8,10},{9,11},{10,... | collective-permute-start | bytes 589832 | tf_op jit(solution)/shard_map/ppermute | solution.py:219

commit v2 on v1

v2 whole, which is shorter than its diff:
```python
import functools
import math

import jax
import jax.numpy as jnp
from jax import lax
from jax.experimental import pallas as pl
from jax.experimental.pallas import tpu as pltpu
from jax.sharding import PartitionSpec as P

HEADS = 16
HD = 128
WSPLIT = 8
EPS = 1e-06
VMEM_LIMIT = 32 * 1024 * 1024

VMEM = pl.BlockSpec(memory_space=pltpu.VMEM)
SMEM = pl.BlockSpec(memory_space=pltpu.SMEM)
ANY = pl.BlockSpec(memory_space=pl.ANY)


def struct(shape, dtype=jnp.bfloat16):
    return jax.ShapeDtypeStruct(shape, dtype)


def call(
    kernel, outs, in_specs, name, flops, moved, out_specs=None, aliases=None
):
    return pl.pallas_call(
        kernel,
        out_shape=outs,
        in_specs=in_specs,
        out_specs=out_specs or jax.tree.map(lambda _: VMEM, outs),
        input_output_aliases=aliases or {},
        compiler_params=pltpu.CompilerParams(vmem_limit_bytes=VMEM_LIMIT),
        cost_estimate=pl.CostEstimate(flops=flops, bytes_accessed=moved, transcendentals=0),
        name=name,
    )


def as_column(row):
    count = row.shape[1]
    down = lax.broadcasted_iota(jnp.int32, (count, count), 0)
    along = lax.broadcasted_iota(jnp.int32, (count, count), 1)
    return jnp.sum(jnp.where(down == along, row, jnp.zeros_like(row)), axis=1, keepdims=True)


def stage_kernel(groups, cap, *refs):
    group_ref, state_in, query_in, gain_in, expert_ref, slot_ref, gate_ref = refs[:7]
    state_out, query_out, gain_out, flat_row, flat_column, gate_column = refs[7:]
    state_out[...] = state_in[...]
    query_out[...] = query_in[...]
    gain_out[...] = gain_in[...]
    offset = expert_ref[...] - group_ref[0]
    offset = jnp.where(offset < 0, offset + groups, offset)
    slot = slot_ref[...]
    flat = jnp.where(slot >= 0, offset * cap + slot, -1)
    flat_row[...] = flat
    flat_column[...] = as_column(flat)
    gate_column[...] = as_column(gate_ref[...])


def stage(group, state, query, gain, expert_id, slot, gate, groups, cap):
    tokens, width = state.shape
    outs = [
        struct((tokens, width)),
        struct((tokens, width)),
        struct((1, width), jnp.float32),
        struct((1, tokens), jnp.int32),
        struct((tokens, 1), jnp.int32),
        struct((tokens, 1), jnp.float32),
    ]
    return call(
        functools.partial(stage_kernel, groups, cap),
        outs,
        [SMEM] + [VMEM] * 6,
        "stage",
        tokens * tokens,
        8 * tokens * width,
    )(group, state, query, gain, expert_id, slot, gate)


def gate_kernel(*refs):
    pass


def after_all(value, others):
    return call(
        gate_kernel,
        struct(value.shape),
        [ANY] * (1 + len(others)),
        "hand_on",
        1,
        1,
        out_specs=ANY,
        aliases={0: 0},
    )(value, *others)


def attend_kernel(pieces, groups, cap, *refs):
    state_ref, query_ref, gain_ref, flat_ref = refs[:4]
    kv_refs = refs[4 : 4 + pieces]
    hidden_ref = refs[-1 - groups]
    packed_refs = refs[-groups:]
    tokens, width = state_ref.shape
    local = kv_refs[0].shape[0] // 2
    scale = 1.0 / math.sqrt(HD)
    squares = jnp.zeros((tokens, HD), jnp.float32)
    for head in range(HEADS):
        cols = slice(head * HD, (head + 1) * HD)
        keys = jnp.concatenate([r[:local, cols] for r in kv_refs], axis=0)
        values = jnp.concatenate([r[local:, cols] for r in kv_refs], axis=0)
        scores = (
            lax.dot_general(
                query_ref[:, cols],
                keys,
                (((1,), (1,)), ((), ())),
                preferred_element_type=jnp.float32,
            )
            * scale
        )
        raised = jnp.exp(scores - jnp.max(scores, axis=1, keepdims=True))
        total = jnp.sum(raised, axis=1, keepdims=True)
        mixed = jnp.dot(raised.astype(jnp.bfloat16), values, preferred_element_type=jnp.float32)
        hidden = state_ref[:, cols].astype(jnp.float32) + mixed / total
        hidden_ref[:, cols] = hidden
        squares = squares + hidden * hidden
    mean_square = jnp.sum(squares, axis=1, keepdims=True) * (1.0 / width)
    inverse = lax.rsqrt(mean_square + EPS)
    rows = lax.broadcasted_iota(jnp.int32, (groups * cap, tokens), 0)
    selector = (rows == flat_ref[...]).astype(jnp.float32).astype(jnp.bfloat16)
    step = 512
    for at in range(0, width, step):
        cols = slice(at, at + step)
        normed = (hidden_ref[:, cols] * inverse * gain_ref[:, cols]).astype(jnp.bfloat16)
        packed = jnp.dot(selector, normed, preferred_element_type=jnp.float32).astype(jnp.bfloat16)
        for group in range(groups):
            packed_refs[group][:, cols] = packed[group * cap : (group + 1) * cap]


def attend(state, query, gain, flat, kv_pieces, groups, cap, after):
    tokens, width = state.shape
    outs = [struct((tokens, width), jnp.float32)] + [struct((cap, width))] * groups
    pieces = len(kv_pieces)
    return call(
        functools.partial(attend_kernel, pieces, groups, cap),
        outs,
        [VMEM] * (4 + pieces) + [ANY] * len(after),
        "attend",
        4 * tokens * pieces * kv_pieces[0].shape[0] * width,
        12 * tokens * width,
    )(state, query, gain, flat, *kv_pieces, *after)


def ffn_kernel(parts, cut, *refs):
    own_in, y_in, z_in = refs[:3]
    d_in = refs[3 : 3 + parts]
    in_a, in_b, out_a, out_b = refs[3 + parts : 7 + parts]
    own_ref, z0_ref, y1_ref, y0_ref, z1_ref = refs[-5:]
    rows, width = own_in.shape
    diagonal = jnp.concatenate([r[...] for r in d_in], axis=1)
    entries = jnp.concatenate([own_in[...], y_in[...], z_in[...], diagonal], axis=0)
    w_in = jnp.concatenate([in_a[...], in_b[...]], axis=1)
    raw = jnp.dot(entries, w_in, preferred_element_type=jnp.float32)
    activation = jnp.maximum(raw, 0.0).astype(jnp.bfloat16)
    step = 512
    for at in range(0, width, step):
        cols = slice(at, at + step)
        w_out = jnp.concatenate([out_a[:, cols], out_b[:, cols]], axis=0)
        part = jnp.dot(activation, w_out, preferred_element_type=jnp.float32)
        part = part.astype(jnp.bfloat16)
        own_ref[:, cols] = part[:rows]
        y_part, z_part, d_part = (part[i * rows : (i + 1) * rows] for i in (1, 2, 3))
        if at < cut:
            y0_ref[:, cols] = y_part
            z0_ref[0, :, cols] = z_part
            z0_ref[1, :, cols] = d_part
        else:
            cols = slice(at - cut, at - cut + step)
            z1_ref[:, cols] = z_part
            y1_ref[0, :, cols] = y_part
            y1_ref[1, :, cols] = d_part


def ffn(blocks, weights, cut, after=()):
    rows, width = blocks[0].shape
    units = weights[0].shape[1]
    rest = width - cut
    outs = [
        struct((rows, width)),
        struct((2, rows, cut)),
        struct((2, rows, rest)),
        struct((rows, cut)),
        struct((rows, rest)),
    ]
    return call(
        functools.partial(ffn_kernel, len(blocks) - 3, cut),
        outs,
        [VMEM] * (len(blocks) + 4) + [ANY] * len(after),
        "expert_ffn",
        4 * 4 * rows * width * units * 2,
        8 * units * width + 16 * rows * width,
    )(*blocks, *weights, *after)


def first_kernel(y0_ref, az_ref, z1_ref, ay_ref, *refs):
    y_ref, z_ref = refs[-2:]
    for own, other, out in ((y0_ref, az_ref, y_ref), (z1_ref, ay_ref, z_ref)):
        out[...] = (own[...].astype(jnp.float32) + other[1].astype(jnp.float32)).astype(jnp.bfloat16)


def first_step(y0, from_z, z1, from_y, after=()):
    return call(
        first_kernel,
        [struct(y0.shape), struct(z1.shape)],
        [VMEM] * 4 + [ANY] * len(after),
        "first_step",
        y0.size + z1.size,
        6 * (y0.size + z1.size),
    )(y0, from_z, z1, from_y, *after)


def total_kernel(cut, *refs):
    own_ref, az_ref, ay_ref, by_ref, bz_ref = refs[:5]
    out_ref = refs[7]
    for first, second, cols in (
        (az_ref, by_ref, slice(0, cut)),
        (ay_ref, bz_ref, slice(cut, out_ref.shape[1])),
    ):
        out_ref[:, cols] = (
            own_ref[:, cols].astype(jnp.float32)
            + first[0].astype(jnp.float32)
            + second[...].astype(jnp.float32)
        ).astype(jnp.bfloat16)


def total(sums, cut, held):
    rows, width = sums[0].shape
    outs = [struct((rows, width))] + [struct(value.shape) for value in held]
    return call(
        functools.partial(total_kernel, cut),
        outs,
        [VMEM] * 5 + [ANY] * len(held),
        "far_total",
        3 * rows * width,
        8 * rows * width,
        out_specs=[VMEM] + [ANY] * len(held),
        aliases={5 + i: 1 + i for i in range(len(held))},
    )(*sums, *held)


def finish_kernel(groups, cap, cut, *refs):
    hidden_ref, gate_ref, flat_ref, own_ref, az_ref, ay_ref, by_ref, bz_ref = refs[:8]
    back_refs = refs[8:-1]
    out_ref = refs[-1]
    tokens, width = hidden_ref.shape
    flat = flat_ref[...]

    def picker(group):
        slots = lax.broadcasted_iota(jnp.int32, (tokens, cap), 1) + group * cap
        return (slots == flat).astype(jnp.float32).astype(jnp.bfloat16)

    pickers = [picker(group) for group in range(groups)]
    step = 512
    for at in range(0, width, step):
        whole = slice(at, at + step)
        inner = at if at < cut else at - cut
        part = slice(inner, inner + step)
        first, second = (az_ref, by_ref) if at < cut else (ay_ref, bz_ref)
        added = (
            own_ref[:, whole].astype(jnp.float32)
            + first[0, :, part].astype(jnp.float32)
            + second[:, part].astype(jnp.float32)
        )
        coarse = added.astype(jnp.bfloat16)
        fine = (added - coarse.astype(jnp.float32)).astype(jnp.bfloat16)
        picked = jnp.dot(pickers[0], coarse, preferred_element_type=jnp.float32)
        picked = picked + jnp.dot(pickers[0], fine, preferred_element_type=jnp.float32)
        for group in range(1, groups):
            picked = picked + jnp.dot(
                pickers[group], back_refs[group - 1][:, whole], preferred_element_type=jnp.float32
            )
        out_ref[:, whole] = (hidden_ref[:, whole] + gate_ref[...] * picked).astype(jnp.bfloat16)


def finish(hidden, gate, flat, sums, backs, groups, cap, cut):
    tokens, width = hidden.shape
    operands = [hidden, gate, flat, *sums, *backs]
    return call(
        functools.partial(finish_kernel, groups, cap, cut),
        struct((tokens, width)),
        [VMEM] * len(operands),
        "finish",
        4 * tokens * cap * (groups + 1) * width,
        16 * tokens * width,
    )(*operands)


def body(state, query, enc_kv, gain, w_in, w_out, expert_id, slot, gate):
    tokens, width = state.shape[2:]
    devices = lax.axis_size("expert")
    pipes = lax.axis_size("pipe")
    groups = devices // WSPLIT
    cap = 3 * tokens // (2 * groups)
    far_cut, near_cut = width // 2, width // 4

    def across(value, bit):
        return lax.ppermute(value, "expert", [(i, i ^ bit) for i in range(devices)])

    def groups_on(value, count):
        shift = count * WSPLIT
        return lax.ppermute(value, "expert", [(i, (i + shift) % devices) for i in range(devices)])

    kv = jnp.transpose(enc_kv[0], (1, 0, 2)).reshape(-1, width)
    kv_pieces = [kv]
    for shift in range(1, pipes):
        perm = [(i, (i + shift) % pipes) for i in range(pipes)]
        kv_pieces.append(lax.ppermute(kv, "pipe", perm))
    weights = [w_in, across(w_in, 1), w_out, across(w_out, 1)]

    group = (lax.axis_index("expert") // WSPLIT).astype(jnp.int32).reshape(1)
    staged = stage(
        group,
        state[0, 0],
        query[0, 0],
        gain.reshape(1, width),
        expert_id[0],
        slot[0],
        gate[0],
        groups,
        cap,
    )
    flat, gates = staged[4:]
    hidden, near, *packed = attend(
        *staged[:4], kv_pieces, groups, cap, after=[weights[1], weights[3]]
    )
    far = [groups_on(block, count) for count, block in enumerate(packed, 1)]
    far = jnp.concatenate(far, axis=0) if len(far) > 1 else far[0]

    near_y, near_z = across(near, 2), across(near, 4)
    near_blocks = [near, near_y, near_z, across(near_z, 2)]
    far = after_all(far, [near_y, near_z])
    far_y, far_z = across(far, 2), across(far, 4)
    far_blocks = [
        far,
        far_y,
        far_z,
        across(far_y[:, :far_cut], 4),
        across(far_z[:, far_cut:], 2),
    ]

    def first_sums(own, z0, y1, y0, z1, after=()):
        from_z, from_y = across(z0, 4), across(y1, 2)
        return own, from_z, from_y, *first_step(y0, from_z, z1, from_y, after)

    def last_sums(own, from_z, from_y, on_y, on_z):
        return own, from_z, from_y, across(on_y, 2), across(on_z, 4)

    far_parts = ffn(far_blocks, weights, far_cut)
    near_parts = ffn(near_blocks, weights, near_cut, after=far_parts[3:])
    far_sum, *held = total(
        last_sums(*first_sums(*far_parts, after=near_parts[3:])), far_cut, near_parts[1:3]
    )
    backs = [
        groups_on(far_sum[(count - 1) * cap : count * cap], groups - count)
        for count in range(1, groups)
    ]
    near_sums = last_sums(*first_sums(near_parts[0], *held, *near_parts[3:]))
    output = finish(hidden, gates, flat, near_sums, backs, groups, cap, near_cut)
    return output.reshape(1, 1, tokens, width)


def solution(mesh):
    return jax.shard_map(
        body,
        mesh=mesh,
        in_specs=(
            P("expert", "pipe", None, None),
            P("expert", "pipe", None, None),
            P("expert", "pipe", None, None),
            P(),
            P(None, "expert"),
            P("expert", None),
            P("expert", "pipe", None),
            P("expert", "pipe", None),
            P("expert", "pipe", None),
        ),
        out_specs=P("expert", "pipe", None, None),
        check_vma=False,
    )
```

time: 106 us -> 98.4 us (0.928)
  Pallas kernels: 14.4 us -> 10.5 us
  starting transfers between devices: 31.9 us -> 28.5 us
  other arithmetic: 3.02 us -> 0 us
  waiting for transfers between devices: 50.7 us -> 53.2 us
    ppermute x22 -> x17, waiting for transfers between devices: 23.8 us -> 31.6 us  [across(): return lax.ppermute(value, 'expert', [(i, i ^ bit) for i in range(devices)])]
    ppermute x1, waiting for transfers between devices: 5.79 us -> 1.7 us  [body(): kv_pieces.append(lax.ppermute(kv, 'pipe', perm))]
    pallas_call x4 -> x9, Pallas kernels: 14.4 us -> 10.5 us  [the longest x2 6.07 us: ffn(): call(functools.partial(ffn_kernel, len(blocks) - 3, cut), outs, [VMEM] *...]
    ppermute x22 -> x17, starting transfers between devices: 21.5 us -> 18.9 us  [across(): return lax.ppermute(value, 'expert', [(i, i ^ bit) for i in range(devices)])]
    ppermute x3 -> x2, waiting for transfers between devices: 21.2 us -> 19.9 us  [groups_on(): lax.ppermute(value, 'expert', [(i, (i + shift) % devices) for i in range(...]
    unnamed x18 -> x16, local copies, waits for them, and re-layouts: 3.56 us -> 4.75 us
    convert_element_type x5 -> x0, other arithmetic: 1.18 us -> none  [the longest x2 1.02 us: gather_sums(): (z1.astype(jnp.float32) + from_y[1].astype(jnp.float32)).astype(jnp.bfloa...]
    another operation x1 -> x0, other arithmetic: 1.09 us -> none
  transfers between devices with their start and end apart: 26 -> 20, of which waited for: 13 -> 14; matrix products, arithmetic and copies ran while one was open for 5% -> 1% of each run, Pallas kernels for 12% -> 6%
where the time goes in v2:
time: 98.4 us; the launch traced here: 98.1 us
  waiting for transfers between devices  53.2 us (54%)
  starting transfers between devices  28.5 us (29%)
  Pallas kernels  10.5 us (11%)
  local copies, waits for them, and re-layouts  5.81 us (6%)
    ppermute x17, waiting for transfers between devices, across(): return lax.ppermute(value, 'expert', [(i, i ^ bit) for i in range(devices)])  31.6 us
    ppermute x2, waiting for transfers between devices, groups_on(): lax.ppermute(value, 'expert', [(i, (i + shift) % devices) for i in range(...  19.9 us
    ppermute x17, starting transfers between devices, across(): return lax.ppermute(value, 'expert', [(i, i ^ bit) for i in range(devices)])  18.9 us
    ppermute x2, starting transfers between devices, groups_on(): lax.ppermute(value, 'expert', [(i, (i + shift) % devices) for i in range(...  6.58 us
    pallas_call x2, Pallas kernels, ffn(): call(functools.partial(ffn_kernel, len(blocks) - 3, cut), outs, [VMEM] *...  6.07 us
    unnamed x16, local copies, waits for them, and re-layouts  4.75 us
    ppermute x1, starting transfers between devices, body(): kv_pieces.append(lax.ppermute(kv, 'pipe', perm))  3 us
    pallas_call x1, Pallas kernels, attend(): call(functools.partial(attend_kernel, pieces, groups, cap), outs, [VMEM]...  2.5 us
  transfers between devices with their start and end apart: 20, of which 14 were waited for; matrix products, arithmetic and copies ran while one was open for 1% of the time, Pallas kernels for 6%

profile of v2, /device:TPU:0, one launch (start us, length us, event | category | flops | bytes accessed | tf_op | source)
XLA Modules:
  0.0 98.1 jit_solution(5696478450463232153)
XLA Ops:
  0.0 0.5 collective-permute-start.1
  0.5 1.0 %copy.13 = bf16[2,32,2048]{2,1,0:T(8,128)(2,1)S(1)} copy(bf16[2,32,2048]{2,0,1:T(2,128)(2,1)} %bitcast.20) | data formatting | bytes 524288 | tf_op jit(solution)/shard_map/transpose | solution.py:314
  1.5 3.0 %collective-permute-start = (bf16[64,2048]{1,0:T(8,128)(2,1)S(1)}, bf16[64,2048]{1,0:T(8,128)(2,1)}, u32[]{:S(2)}, u32[]{:S(2)}) collective-permute-start(bf16[64,2048]{1,0:T(8,128)(2,1)S(1)} %bitcast.12), channel_id=1, source_target_pairs={{0,16},{16,0},{1,17},{17,1},{2,18},{18,2},{3,19},{19,3},{4,20},{20... | collective-permute-start | bytes 786440 | tf_op jit(solution)/shard_map/ppermute | solution.py:318
  4.6 1.0 %copy-done = bf16[1,1,128,2048]{3,2,1,0:T(8,128)(2,1)S(1)} copy-done((bf16[1,1,128,2048]{3,2,1,0:T(8,128)(2,1)S(1)}, bf16[1,1,128,2048]{3,2,1,0:T(8,128)(2,1)}, u32[]{:S(2)}) %copy-start) | copy-done | bytes 524312
  5.6 1.0 %copy-done.1 = bf16[1,1,128,2048]{3,2,1,0:T(8,128)(2,1)S(1)} copy-done((bf16[1,1,128,2048]{3,2,1,0:T(8,128)(2,1)S(1)}, bf16[1,1,128,2048]{3,2,1,0:T(8,128)(2,1)}, u32[]{:S(2)}) %copy-start.1) | copy-done | bytes 524312
  6.6 0.7 copy-done.2
  7.3 0.7 copy-done.3
  8.0 0.7 copy-done.4
  8.6 0.7 copy-done.5
  9.3 0.1 stage.1
  9.4 1.7 %collective-permute-done.refs_5_ = bf16[64,2048]{1,0:T(8,128)(2,1)} collective-permute-done((bf16[64,2048]{1,0:T(8,128)(2,1)S(1)}, bf16[64,2048]{1,0:T(8,128)(2,1)}, u32[]{:S(2)}, u32[]{:S(2)}) %collective-permute-start) | collective-permute-done | bytes 262176 | tf_op jit(solution)/shard_map/ppermute | solution.py:318
  11.1 2.5 %attend.1 = (f32[128,2048]{1,0:T(8,128)S(1)}, bf16[96,2048]{1,0:T(8,128)(2,1)S(1)}, bf16[96,2048]{1,0:T(8,128)(2,1)S(1)}) custom-call(bf16[128,2048]{1,0:T(8,128)(2,1)S(1)} %get-tuple-element.31.refs_0_, bf16[128,2048]{1,0:T(8,128)(2,1)S(1)} %get-tuple-element.32.refs_1_, f32[1,2048]{1,0:T(1,128)S(1)} %get-tuple-element.33.refs_2_, ...), custom_call_target="tpu_custom_call" | custom-call | flops 134217728 | bytes 3145728 | tf_op jit(solution)/shard_map/attend/pallas_call | solution.py:145
  13.7 2.9 %collective-permute-start.6 = (bf16[96,2048]{1,0:T(8,128)(2,1)S(1)}, bf16[96,2048]{1,0:T(8,128)(2,1)S(1)}, u32[]{:S(2)}, u32[]{:S(2)}) collective-permute-start(bf16[96,2048]{1,0:T(8,128)(2,1)S(1)} %get-tuple-element.39), channel_id=1, source_target_pairs={{0,8},{1,9},{2,10},{3,11},{4,12},{5,13},{6,14},{7,15},{8,0},{9,1},... | collective-permute-start | bytes 1179656 | tf_op jit(solution)/shard_map/ppermute | solution.py:312
  16.6 1.6 %collective-permute-start.4 = (bf16[96,2048]{1,0:T(8,128)(2,1)S(1)}, bf16[96,2048]{1,0:T(8,128)(2,1)S(1)}, u32[]{:S(2)}, u32[]{:S(2)}) collective-permute-start(bf16[96,2048]{1,0:T(8,128)(2,1)S(1)} %get-tuple-element.38.refs_0_), channel_id=1, source_target_pairs={{0,4},{1,5},{2,6},{3,7},{4,0},{5,1},{6,2},{7,3},{8,12},{9,13},{10,... | collective-permute-start | bytes 1179656 | tf_op jit(solution)/shard_map/ppermute | solution.py:308
  18.1 1.5 %collective-permute-start.3 = (bf16[96,2048]{1,0:T(8,128)(2,1)S(1)}, bf16[96,2048]{1,0:T(8,128)(2,1)S(1)}, u32[]{:S(2)}, u32[]{:S(2)}) collective-permute-start(bf16[96,2048]{1,0:T(8,128)(2,1)S(1)} %get-tuple-element.38.refs_0_), channel_id=1, source_target_pairs={{0,2},{1,3},{2,0},{3,1},{4,6},{5,7},{6,4},{7,5},{8,10},{9,11},{10,... | collective-permute-start | bytes 1179656 | tf_op jit(solution)/shard_map/ppermute | solution.py:308
  19.7 14.0 %collective-permute-done.6.refs_0_ = bf16[96,2048]{1,0:T(8,128)(2,1)S(1)} collective-permute-done((bf16[96,2048]{1,0:T(8,128)(2,1)S(1)}, bf16[96,2048]{1,0:T(8,128)(2,1)S(1)}, u32[]{:S(2)}, u32[]{:S(2)}) %collective-permute-start.6) | collective-permute-done | bytes 393248 | tf_op jit(solution)/shard_map/ppermute | solution.py:312
  33.6 0.2 collective-permute-done.4.refs_2_
  33.8 1.4 %collective-permute-start.8 = (bf16[96,2048]{1,0:T(8,128)(2,1)S(1)}, bf16[96,2048]{1,0:T(8,128)(2,1)S(1)}, u32[]{:S(2)}, u32[]{:S(2)}) collective-permute-start(bf16[96,2048]{1,0:T(8,128)(2,1)S(1)} %hand_on.1.refs_0_), channel_id=1, source_target_pairs={{0,4},{1,5},{2,6},{3,7},{4,0},{5,1},{6,2},{7,3},{8,12},{9,13},{10,... | collective-permute-start | bytes 1179656 | tf_op jit(solution)/shard_map/ppermute | solution.py:308
  35.2 1.5 %collective-permute-start.7 = (bf16[96,2048]{1,0:T(8,128)(2,1)S(1)}, bf16[96,2048]{1,0:T(8,128)(2,1)S(1)}, u32[]{:S(2)}, u32[]{:S(2)}) collective-permute-start(bf16[96,2048]{1,0:T(8,128)(2,1)S(1)} %hand_on.1.refs_0_), channel_id=1, source_target_pairs={{0,2},{1,3},{2,0},{3,1},{4,6},{5,7},{6,4},{7,5},{8,10},{9,11},{10,... | collective-permute-start | bytes 1179656 | tf_op jit(solution)/shard_map/ppermute | solution.py:308
  36.7 6.9 %collective-permute-done.8.refs_2_ = bf16[96,2048]{1,0:T(8,128)(2,1)S(1)} collective-permute-done((bf16[96,2048]{1,0:T(8,128)(2,1)S(1)}, bf16[96,2048]{1,0:T(8,128)(2,1)S(1)}, u32[]{:S(2)}, u32[]{:S(2)}) %collective-permute-start.8) | collective-permute-done | bytes 393248 | tf_op jit(solution)/shard_map/ppermute | solution.py:308
  43.7 1.4 %collective-permute-start.10 = (bf16[96,1024]{1,0:T(8,128)(2,1)S(1)}, bf16[96,1024]{1,0:T(8,128)(2,1)S(1)}, u32[]{:S(2)}, u32[]{:S(2)}) collective-permute-start(bf16[96,1024]{1,0:T(8,128)(2,1)S(1)} %slice.9), channel_id=1, source_target_pairs={{0,2},{1,3},{2,0},{3,1},{4,6},{5,7},{6,4},{7,5},{8,10},{9,11},{10,... | collective-permute-start | bytes 589832 | tf_op jit(solution)/shard_map/ppermute | solution.py:308
  45.1 0.4 collective-permute-done.7.refs_1_
  45.5 1.4 %collective-permute-start.9 = (bf16[96,1024]{1,0:T(8,128)(2,1)S(1)}, bf16[96,1024]{1,0:T(8,128)(2,1)S(1)}, u32[]{:S(2)}, u32[]{:S(2)}) collective-permute-start(bf16[96,1024]{1,0:T(8,128)(2,1)S(1)} %slice.8), channel_id=1, source_target_pairs={{0,4},{1,5},{2,6},{3,7},{4,0},{5,1},{6,2},{7,3},{8,12},{9,13},{10,... | collective-permute-start | bytes 589832 | tf_op jit(solution)/shard_map/ppermute | solution.py:308
  46.9 0.5 collective-permute-start.5
  47.4 4.2 %collective-permute-done.10.refs_4_ = bf16[96,1024]{1,0:T(8,128)(2,1)S(1)} collective-permute-done((bf16[96,1024]{1,0:T(8,128)(2,1)S(1)}, bf16[96,1024]{1,0:T(8,128)(2,1)S(1)}, u32[]{:S(2)}, u32[]{:S(2)}) %collective-permute-start.10) | collective-permute-done | bytes 196640 | tf_op jit(solution)/shard_map/ppermute | solution.py:308
  51.6 3.0 %expert_ffn.2 = (bf16[96,2048]{1,0:T(8,128)(2,1)S(1)}, bf16[2,96,1024]{2,1,0:T(8,128)(2,1)S(1)}, bf16[2,96,1024]{2,1,0:T(8,128)(2,1)S(1)}, bf16[96,1024]{1,0:T(8,128)(2,1)S(1)}, bf16[96,1024]{1,0:T(8,128)(2,1)S(1)}) custom-call(bf16[96,2048]{1,0:T(8,128)(2,1)S(1)} %hand_on.1.refs_0_, bf16[96,2048]{1,0:T(8,128)(2,1)S(1)} %collective-permute-done.7.refs_1_, ...), custom_call_target="tpu_custom_call" | custom-call | flops 2415919104 | bytes 9437184 | tf_op jit(solution)/shard_map/expert_ffn/pallas_call | solution.py:196
  54.6 1.6 %collective-permute-start.11 = (bf16[2,96,1024]{2,1,0:T(8,128)(2,1)S(1)}, bf16[2,96,1024]{2,1,0:T(8,128)(2,1)S(1)}, u32[]{:S(2)}, u32[]{:S(2)}) collective-permute-start(bf16[2,96,1024]{2,1,0:T(8,128)(2,1)S(1)} %get-tuple-element.44), channel_id=1, source_target_pairs={{0,4},{1,5},{2,6},{3,7},{4,0},{5,1},{6,2},{7,3},{8,12},{9,13},{10,... | collective-permute-start | bytes 1179656 | tf_op jit(solution)/shard_map/ppermute | solution.py:308
  56.2 1.5 %collective-permute-start.12 = (bf16[2,96,1024]{2,1,0:T(8,128)(2,1)S(1)}, bf16[2,96,1024]{2,1,0:T(8,128)(2,1)S(1)}, u32[]{:S(2)}, u32[]{:S(2)}) collective-permute-start(bf16[2,96,1024]{2,1,0:T(8,128)(2,1)S(1)} %get-tuple-element.45), channel_id=1, source_target_pairs={{0,2},{1,3},{2,0},{3,1},{4,6},{5,7},{6,4},{7,5},{8,10},{9,11},{10,... | collective-permute-start | bytes 1179656 | tf_op jit(solution)/shard_map/ppermute | solution.py:308
  57.7 2.3 %collective-permute-done.5.refs_3_ = bf16[96,2048]{1,0:T(8,128)(2,1)S(1)} collective-permute-done((bf16[96,2048]{1,0:T(8,128)(2,1)S(1)}, bf16[96,2048]{1,0:T(8,128)(2,1)S(1)}, u32[]{:S(2)}, u32[]{:S(2)}) %collective-permute-start.5) | collective-permute-done | bytes 393248 | tf_op jit(solution)/shard_map/ppermute | solution.py:308
  60.0 3.0 %expert_ffn.3 = (bf16[96,2048]{1,0:T(8,128)(2,1)S(1)}, bf16[2,96,512]{2,1,0:T(8,128)(2,1)S(1)}, bf16[2,96,1536]{2,1,0:T(8,128)(2,1)S(1)}, bf16[96,512]{1,0:T(8,128)(2,1)S(1)}, bf16[96,1536]{1,0:T(8,128)(2,1)S(1)}) custom-call(bf16[96,2048]{1,0:T(8,128)(2,1)S(1)} %get-tuple-element.38.refs_0_, bf16[96,2048]{1,0:T(8,128)(2,1)S(1)} %collective-permute-done.3.refs_1_, ...), custom_call_target="tpu_custom_call" | custom-call | flops 2415919104 | bytes 9437184 | tf_op jit(solution)/shard_map/expert_ffn/pallas_call | solution.py:196
  63.1 2.9 %collective-permute-done.12.ay_ref.refs_2_ = bf16[2,96,1024]{2,1,0:T(8,128)(2,1)S(1)} collective-permute-done((bf16[2,96,1024]{2,1,0:T(8,128)(2,1)S(1)}, bf16[2,96,1024]{2,1,0:T(8,128)(2,1)S(1)}, u32[]{:S(2)}, u32[]{:S(2)}) %collective-permute-start.12) | collective-permute-done | bytes 393248 | tf_op jit(solution)/shard_map/ppermute | solution.py:308
  66.0 0.1 first_step.2
  66.1 1.6 %collective-permute-start.13 = (bf16[96,1024]{1,0:T(8,128)(2,1)S(1)}, bf16[96,1024]{1,0:T(8,128)(2,1)S(1)}, u32[]{:S(2)}, u32[]{:S(2)}) collective-permute-start(bf16[96,1024]{1,0:T(8,128)(2,1)S(1)} %get-tuple-element.48), channel_id=1, source_target_pairs={{0,2},{1,3},{2,0},{3,1},{4,6},{5,7},{6,4},{7,5},{8,10},{9,11},{10,... | collective-permute-start | bytes 589832 | tf_op jit(solution)/shard_map/ppermute | solution.py:308
  67.7 1.1 %collective-permute-start.14 = (bf16[96,1024]{1,0:T(8,128)(2,1)S(1)}, bf16[96,1024]{1,0:T(8,128)(2,1)S(1)}, u32[]{:S(2)}, u32[]{:S(2)}) collective-permute-start(bf16[96,1024]{1,0:T(8,128)(2,1)S(1)} %get-tuple-element.49), channel_id=1, source_target_pairs={{0,4},{1,5},{2,6},{3,7},{4,0},{5,1},{6,2},{7,3},{8,12},{9,13},{10,... | collective-permute-start | bytes 589832 | tf_op jit(solution)/shard_map/ppermute | solution.py:308
  68.7 3.1 %collective-permute-done.13.refs_3_ = bf16[96,1024]{1,0:T(8,128)(2,1)S(1)} collective-permute-done((bf16[96,1024]{1,0:T(8,128)(2,1)S(1)}, bf16[96,1024]{1,0:T(8,128)(2,1)S(1)}, u32[]{:S(2)}, u32[]{:S(2)}) %collective-permute-start.13) | collective-permute-done | bytes 196640 | tf_op jit(solution)/shard_map/ppermute | solution.py:308
  71.8 1.9 %collective-permute-done.14.refs_4_ = bf16[96,1024]{1,0:T(8,128)(2,1)S(1)} collective-permute-done((bf16[96,1024]{1,0:T(8,128)(2,1)S(1)}, bf16[96,1024]{1,0:T(8,128)(2,1)S(1)}, u32[]{:S(2)}, u32[]{:S(2)}) %collective-permute-start.14) | collective-permute-done | bytes 196640 | tf_op jit(solution)/shard_map/ppermute | solution.py:308
  73.7 0.1 far_total.1
  73.9 0.2 collective-permute-start.16
  74.0 1.9 %collective-permute-start.15 = (bf16[2,96,512]{2,1,0:T(8,128)(2,1)S(1)}, bf16[2,96,512]{2,1,0:T(8,128)(2,1)S(1)}, u32[]{:S(2)}, u32[]{:S(2)}) collective-permute-start(bf16[2,96,512]{2,1,0:T(8,128)(2,1)S(1)} %get-tuple-element.52), channel_id=1, source_target_pairs={{0,4},{1,5},{2,6},{3,7},{4,0},{5,1},{6,2},{7,3},{8,12},{9,13},{10,... | collective-permute-start | bytes 589832 | tf_op jit(solution)/shard_map/ppermute | solution.py:308
  75.9 3.7 %collective-permute-start.19 = (bf16[96,2048]{1,0:T(8,128)(2,1)S(1)}, bf16[96,2048]{1,0:T(8,128)(2,1)S(1)}, u32[]{:S(2)}, u32[]{:S(2)}) collective-permute-start(bf16[96,2048]{1,0:T(8,128)(2,1)S(1)} %get-tuple-element.56), channel_id=1, source_target_pairs={{0,8},{1,9},{2,10},{3,11},{4,12},{5,13},{6,14},{7,15},{8,0},{9,1},... | collective-permute-start | bytes 1179656 | tf_op jit(solution)/shard_map/ppermute | solution.py:312
  79.6 2.1 %collective-permute-done.15.az_ref.refs_4_ = bf16[2,96,512]{2,1,0:T(8,128)(2,1)S(1)} collective-permute-done((bf16[2,96,512]{2,1,0:T(8,128)(2,1)S(1)}, bf16[2,96,512]{2,1,0:T(8,128)(2,1)S(1)}, u32[]{:S(2)}, u32[]{:S(2)}) %collective-permute-start.15) | collective-permute-done | bytes 196640 | tf_op jit(solution)/shard_map/ppermute | solution.py:308
  81.7 4.8 %collective-permute-done.16.ay_ref.refs_5_ = bf16[2,96,1536]{2,1,0:T(8,128)(2,1)S(1)} collective-permute-done((bf16[2,96,1536]{2,1,0:T(8,128)(2,1)S(1)}, bf16[2,96,1536]{2,1,0:T(8,128)(2,1)S(1)}, u32[]{:S(2)}, u32[]{:S(2)}) %collective-permute-start.16) | collective-permute-done | bytes 589856 | tf_op jit(solution)/shard_map/ppermute | solution.py:308
  86.5 0.1 first_step.3
  86.6 0.1 collective-permute-start.18
  86.6 1.3 %collective-permute-start.17 = (bf16[96,512]{1,0:T(8,128)(2,1)S(1)}, bf16[96,512]{1,0:T(8,128)(2,1)S(1)}, u32[]{:S(2)}, u32[]{:S(2)}) collective-permute-start(bf16[96,512]{1,0:T(8,128)(2,1)S(1)} %get-tuple-element.54), channel_id=1, source_target_pairs={{0,2},{1,3},{2,0},{3,1},{4,6},{5,7},{6,4},{7,5},{8,10},{9,11},{10,... | collective-permute-start | bytes 294920 | tf_op jit(solution)/shard_map/ppermute | solution.py:308
  87.9 6.0 %collective-permute-done.19.refs_8_ = bf16[96,2048]{1,0:T(8,128)(2,1)S(1)} collective-permute-done((bf16[96,2048]{1,0:T(8,128)(2,1)S(1)}, bf16[96,2048]{1,0:T(8,128)(2,1)S(1)}, u32[]{:S(2)}, u32[]{:S(2)}) %collective-permute-start.19) | collective-permute-done | bytes 393248 | tf_op jit(solution)/shard_map/ppermute | solution.py:312
  93.8 2.8 %collective-permute-done.18.refs_7_ = bf16[96,1536]{1,0:T(8,128)(2,1)S(1)} collective-permute-done((bf16[96,1536]{1,0:T(8,128)(2,1)S(1)}, bf16[96,1536]{1,0:T(8,128)(2,1)S(1)}, u32[]{:S(2)}, u32[]{:S(2)}) %collective-permute-start.18) | collective-permute-done | bytes 294944 | tf_op jit(solution)/shard_map/ppermute | solution.py:308
  96.6 1.4 %finish.1 = bf16[128,2048]{1,0:T(8,128)(2,1)} custom-call(f32[128,2048]{1,0:T(8,128)S(1)} %get-tuple-element.35.refs_0_, f32[128,1]{1,0:T(8,128)S(1)} %get-tuple-element.36.refs_1_, s32[128,1]{1,0:T(8,128)S(1)} %get-tuple-element.37.refs_2_, bf16[96,2048]{1,0:T(8,128)(2,1)S(1)} %get-tuple-element.42.refs_3_, ...), custom_call_target="tpu_custom_call" | custom-call | flops 301989888 | bytes 4194304 | tf_op jit(solution)/shard_map/finish/pallas_call | solution.py:289
  (20 shorter events, 0.1 us)
Async XLA Ops:
  0.0 11.1 %collective-permute-start.1 = (bf16[2048,384]{1,0:T(8,128)(2,1)}, bf16[2048,384]{1,0:T(8,128)(2,1)S(1)}, u32[]{:S(2)}, u32[]{:S(2)}) collective-permute-start(bf16[2048,384]{1,0:T(8,128)(2,1)} %refs_4_.1), channel_id=1, source_target_pairs={{0,1},{1,0},{2,3},{3,2},{4,5},{5,4},{6,7},{7,6},{8,9},{9,8},{10,11... | collective-permute-start | bytes 4718600 | tf_op jit(solution)/shard_map/ppermute | solution.py:308
  0.5 10.7 %collective-permute-start.2 = (bf16[384,2048]{1,0:T(8,128)(2,1)}, bf16[384,2048]{1,0:T(8,128)(2,1)S(1)}, u32[]{:S(2)}, u32[]{:S(2)}) collective-permute-start(bf16[384,2048]{1,0:T(8,128)(2,1)} %refs_6_.1), channel_id=1, source_target_pairs={{0,1},{1,0},{2,3},{3,2},{4,5},{5,4},{6,7},{7,6},{8,9},{9,8},{10,11... | collective-permute-start | bytes 4718600 | tf_op jit(solution)/shard_map/ppermute | solution.py:308
  1.5 9.6 %collective-permute-start = (bf16[64,2048]{1,0:T(8,128)(2,1)S(1)}, bf16[64,2048]{1,0:T(8,128)(2,1)}, u32[]{:S(2)}, u32[]{:S(2)}) collective-permute-start(bf16[64,2048]{1,0:T(8,128)(2,1)S(1)} %bitcast.12), channel_id=1, source_target_pairs={{0,16},{16,0},{1,17},{17,1},{2,18},{18,2},{3,19},{19,3},{4,20},{20... | collective-permute-start | bytes 786440 | tf_op jit(solution)/shard_map/ppermute | solution.py:318
  4.5 1.0 %copy-start = (bf16[1,1,128,2048]{3,2,1,0:T(8,128)(2,1)S(1)}, bf16[1,1,128,2048]{3,2,1,0:T(8,128)(2,1)}, u32[]{:S(2)}) copy-start(bf16[1,1,128,2048]{3,2,1,0:T(8,128)(2,1)} %param.9) | copy-start | bytes 1572868
  5.6 1.0 %copy-start.1 = (bf16[1,1,128,2048]{3,2,1,0:T(8,128)(2,1)S(1)}, bf16[1,1,128,2048]{3,2,1,0:T(8,128)(2,1)}, u32[]{:S(2)}) copy-start(bf16[1,1,128,2048]{3,2,1,0:T(8,128)(2,1)} %param.10) | copy-start | bytes 1572868
  6.6 0.7 copy-start.2
  7.3 0.7 copy-start.3
  8.0 0.7 copy-start.4
  8.6 0.7 copy-start.5
  11.1 40.5 %copy-start.7 = (bf16[384,2048]{1,0:T(8,128)(2,1)S(1)}, bf16[384,2048]{1,0:T(8,128)(2,1)}, u32[]{:S(2)}) copy-start(bf16[384,2048]{1,0:T(8,128)(2,1)} %refs_6_.1) | copy-start | bytes 4718596
  13.6 38.0 %copy-start.6 = (bf16[2048,384]{1,0:T(8,128)(2,1)S(1)}, bf16[2048,384]{1,0:T(8,128)(2,1)}, u32[]{:S(2)}) copy-start(bf16[2048,384]{1,0:T(8,128)(2,1)} %refs_4_.1) | copy-start | bytes 4718596
  13.7 20.0 %collective-permute-start.6 = (bf16[96,2048]{1,0:T(8,128)(2,1)S(1)}, bf16[96,2048]{1,0:T(8,128)(2,1)S(1)}, u32[]{:S(2)}, u32[]{:S(2)}) collective-permute-start(bf16[96,2048]{1,0:T(8,128)(2,1)S(1)} %get-tuple-element.39), channel_id=1, source_target_pairs={{0,8},{1,9},{2,10},{3,11},{4,12},{5,13},{6,14},{7,15},{8,0},{9,1},... | collective-permute-start | bytes 1179656 | tf_op jit(solution)/shard_map/ppermute | solution.py:312
  16.6 17.3 %collective-permute-start.4 = (bf16[96,2048]{1,0:T(8,128)(2,1)S(1)}, bf16[96,2048]{1,0:T(8,128)(2,1)S(1)}, u32[]{:S(2)}, u32[]{:S(2)}) collective-permute-start(bf16[96,2048]{1,0:T(8,128)(2,1)S(1)} %get-tuple-element.38.refs_0_), channel_id=1, source_target_pairs={{0,4},{1,5},{2,6},{3,7},{4,0},{5,1},{6,2},{7,3},{8,12},{9,13},{10,... | collective-permute-start | bytes 1179656 | tf_op jit(solution)/shard_map/ppermute | solution.py:308
  18.1 15.7 %collective-permute-start.3 = (bf16[96,2048]{1,0:T(8,128)(2,1)S(1)}, bf16[96,2048]{1,0:T(8,128)(2,1)S(1)}, u32[]{:S(2)}, u32[]{:S(2)}) collective-permute-start(bf16[96,2048]{1,0:T(8,128)(2,1)S(1)} %get-tuple-element.38.refs_0_), channel_id=1, source_target_pairs={{0,2},{1,3},{2,0},{3,1},{4,6},{5,7},{6,4},{7,5},{8,10},{9,11},{10,... | collective-permute-start | bytes 1179656 | tf_op jit(solution)/shard_map/ppermute | solution.py:308
  33.8 9.8 %collective-permute-start.8 = (bf16[96,2048]{1,0:T(8,128)(2,1)S(1)}, bf16[96,2048]{1,0:T(8,128)(2,1)S(1)}, u32[]{:S(2)}, u32[]{:S(2)}) collective-permute-start(bf16[96,2048]{1,0:T(8,128)(2,1)S(1)} %hand_on.1.refs_0_), channel_id=1, source_target_pairs={{0,4},{1,5},{2,6},{3,7},{4,0},{5,1},{6,2},{7,3},{8,12},{9,13},{10,... | collective-permute-start | bytes 1179656 | tf_op jit(solution)/shard_map/ppermute | solution.py:308
  35.2 10.3 %collective-permute-start.7 = (bf16[96,2048]{1,0:T(8,128)(2,1)S(1)}, bf16[96,2048]{1,0:T(8,128)(2,1)S(1)}, u32[]{:S(2)}, u32[]{:S(2)}) collective-permute-start(bf16[96,2048]{1,0:T(8,128)(2,1)S(1)} %hand_on.1.refs_0_), channel_id=1, source_target_pairs={{0,2},{1,3},{2,0},{3,1},{4,6},{5,7},{6,4},{7,5},{8,10},{9,11},{10,... | collective-permute-start | bytes 1179656 | tf_op jit(solution)/shard_map/ppermute | solution.py:308
  43.7 7.9 %collective-permute-start.10 = (bf16[96,1024]{1,0:T(8,128)(2,1)S(1)}, bf16[96,1024]{1,0:T(8,128)(2,1)S(1)}, u32[]{:S(2)}, u32[]{:S(2)}) collective-permute-start(bf16[96,1024]{1,0:T(8,128)(2,1)S(1)} %slice.9), channel_id=1, source_target_pairs={{0,2},{1,3},{2,0},{3,1},{4,6},{5,7},{6,4},{7,5},{8,10},{9,11},{10,... | collective-permute-start | bytes 589832 | tf_op jit(solution)/shard_map/ppermute | solution.py:308
  45.5 6.1 %collective-permute-start.9 = (bf16[96,1024]{1,0:T(8,128)(2,1)S(1)}, bf16[96,1024]{1,0:T(8,128)(2,1)S(1)}, u32[]{:S(2)}, u32[]{:S(2)}) collective-permute-start(bf16[96,1024]{1,0:T(8,128)(2,1)S(1)} %slice.8), channel_id=1, source_target_pairs={{0,4},{1,5},{2,6},{3,7},{4,0},{5,1},{6,2},{7,3},{8,12},{9,13},{10,... | collective-permute-start | bytes 589832 | tf_op jit(solution)/shard_map/ppermute | solution.py:308
  46.9 13.1 %collective-permute-start.5 = (bf16[96,2048]{1,0:T(8,128)(2,1)S(1)}, bf16[96,2048]{1,0:T(8,128)(2,1)S(1)}, u32[]{:S(2)}, u32[]{:S(2)}) collective-permute-start(bf16[96,2048]{1,0:T(8,128)(2,1)S(1)} %collective-permute-done.4.refs_2_), channel_id=1, source_target_pairs={{0,2},{1,3},{2,0},{3,1},{4,6},{5,7},{6,4},{7,5},{8,10},{9,11},{10,... | collective-permute-start | bytes 1179656 | tf_op jit(solution)/shard_map/ppermute | solution.py:308
  54.6 8.4 %collective-permute-start.11 = (bf16[2,96,1024]{2,1,0:T(8,128)(2,1)S(1)}, bf16[2,96,1024]{2,1,0:T(8,128)(2,1)S(1)}, u32[]{:S(2)}, u32[]{:S(2)}) collective-permute-start(bf16[2,96,1024]{2,1,0:T(8,128)(2,1)S(1)} %get-tuple-element.44), channel_id=1, source_target_pairs={{0,4},{1,5},{2,6},{3,7},{4,0},{5,1},{6,2},{7,3},{8,12},{9,13},{10,... | collective-permute-start | bytes 1179656 | tf_op jit(solution)/shard_map/ppermute | solution.py:308
  56.2 9.7 %collective-permute-start.12 = (bf16[2,96,1024]{2,1,0:T(8,128)(2,1)S(1)}, bf16[2,96,1024]{2,1,0:T(8,128)(2,1)S(1)}, u32[]{:S(2)}, u32[]{:S(2)}) collective-permute-start(bf16[2,96,1024]{2,1,0:T(8,128)(2,1)S(1)} %get-tuple-element.45), channel_id=1, source_target_pairs={{0,2},{1,3},{2,0},{3,1},{4,6},{5,7},{6,4},{7,5},{8,10},{9,11},{10,... | collective-permute-start | bytes 1179656 | tf_op jit(solution)/shard_map/ppermute | solution.py:308
  66.1 5.7 %collective-permute-start.13 = (bf16[96,1024]{1,0:T(8,128)(2,1)S(1)}, bf16[96,1024]{1,0:T(8,128)(2,1)S(1)}, u32[]{:S(2)}, u32[]{:S(2)}) collective-permute-start(bf16[96,1024]{1,0:T(8,128)(2,1)S(1)} %get-tuple-element.48), channel_id=1, source_target_pairs={{0,2},{1,3},{2,0},{3,1},{4,6},{5,7},{6,4},{7,5},{8,10},{9,11},{10,... | collective-permute-start | bytes 589832 | tf_op jit(solution)/shard_map/ppermute | solution.py:308
  67.7 6.1 %collective-permute-start.14 = (bf16[96,1024]{1,0:T(8,128)(2,1)S(1)}, bf16[96,1024]{1,0:T(8,128)(2,1)S(1)}, u32[]{:S(2)}, u32[]{:S(2)}) collective-permute-start(bf16[96,1024]{1,0:T(8,128)(2,1)S(1)} %get-tuple-element.49), channel_id=1, source_target_pairs={{0,4},{1,5},{2,6},{3,7},{4,0},{5,1},{6,2},{7,3},{8,12},{9,13},{10,... | collective-permute-start | bytes 589832 | tf_op jit(solution)/shard_map/ppermute | solution.py:308
  73.9 12.6 %collective-permute-start.16 = (bf16[2,96,1536]{2,1,0:T(8,128)(2,1)S(1)}, bf16[2,96,1536]{2,1,0:T(8,128)(2,1)S(1)}, u32[]{:S(2)}, u32[]{:S(2)}) collective-permute-start(bf16[2,96,1536]{2,1,0:T(8,128)(2,1)S(1)} %get-tuple-element.53), channel_id=1, source_target_pairs={{0,2},{1,3},{2,0},{3,1},{4,6},{5,7},{6,4},{7,5},{8,10},{9,11},{10,... | collective-permute-start | bytes 1769480 | tf_op jit(solution)/shard_map/ppermute | solution.py:308
  74.0 7.6 %collective-permute-start.15 = (bf16[2,96,512]{2,1,0:T(8,128)(2,1)S(1)}, bf16[2,96,512]{2,1,0:T(8,128)(2,1)S(1)}, u32[]{:S(2)}, u32[]{:S(2)}) collective-permute-start(bf16[2,96,512]{2,1,0:T(8,128)(2,1)S(1)} %get-tuple-element.52), channel_id=1, source_target_pairs={{0,4},{1,5},{2,6},{3,7},{4,0},{5,1},{6,2},{7,3},{8,12},{9,13},{10,... | collective-permute-start | bytes 589832 | tf_op jit(solution)/shard_map/ppermute | solution.py:308
  75.9 17.9 %collective-permute-start.19 = (bf16[96,2048]{1,0:T(8,128)(2,1)S(1)}, bf16[96,2048]{1,0:T(8,128)(2,1)S(1)}, u32[]{:S(2)}, u32[]{:S(2)}) collective-permute-start(bf16[96,2048]{1,0:T(8,128)(2,1)S(1)} %get-tuple-element.56), channel_id=1, source_target_pairs={{0,8},{1,9},{2,10},{3,11},{4,12},{5,13},{6,14},{7,15},{8,0},{9,1},... | collective-permute-start | bytes 1179656 | tf_op jit(solution)/shard_map/ppermute | solution.py:312
  86.6 10.1 %collective-permute-start.18 = (bf16[96,1536]{1,0:T(8,128)(2,1)S(1)}, bf16[96,1536]{1,0:T(8,128)(2,1)S(1)}, u32[]{:S(2)}, u32[]{:S(2)}) collective-permute-start(bf16[96,1536]{1,0:T(8,128)(2,1)S(1)} %get-tuple-element.55), channel_id=1, source_target_pairs={{0,4},{1,5},{2,6},{3,7},{4,0},{5,1},{6,2},{7,3},{8,12},{9,13},{10,... | collective-permute-start | bytes 884744 | tf_op jit(solution)/shard_map/ppermute | solution.py:308
  86.6 7.2 %collective-permute-start.17 = (bf16[96,512]{1,0:T(8,128)(2,1)S(1)}, bf16[96,512]{1,0:T(8,128)(2,1)S(1)}, u32[]{:S(2)}, u32[]{:S(2)}) collective-permute-start(bf16[96,512]{1,0:T(8,128)(2,1)S(1)} %get-tuple-element.54), channel_id=1, source_target_pairs={{0,2},{1,3},{2,0},{3,1},{4,6},{5,7},{6,4},{7,5},{8,10},{9,11},{10,... | collective-permute-start | bytes 294920 | tf_op jit(solution)/shard_map/ppermute | solution.py:308

commit v3 on v2

--- a/solution.py
+++ b/solution.py
@@ -84,35 +84,39 @@
     pass
 
 
-def after_all(value, others):
+def after_all(values, others):
     return call(
         gate_kernel,
-        struct(value.shape),
-        [ANY] * (1 + len(others)),
+        [struct(value.shape) for value in values],
+        [ANY] * (len(values) + len(others)),
         "hand_on",
         1,
         1,
-        out_specs=ANY,
-        aliases={0: 0},
-    )(value, *others)
-
-
-def attend_kernel(pieces, groups, cap, *refs):
+        out_specs=[ANY] * len(values),
+        aliases={i: i for i in range(len(values))},
+    )(*values, *others)
+
+
+def attend_kernel(pieces, groups, cap, first, *refs):
     state_ref, query_ref, gain_ref, flat_ref = refs[:4]
     kv_refs = refs[4 : 4 + pieces]
-    hidden_ref = refs[-1 - groups]
+    hidden_ref, squares_ref = refs[-2 - groups : -groups]
     packed_refs = refs[-groups:]
-    tokens, width = state_ref.shape
+    tokens, width = hidden_ref.shape
     local = kv_refs[0].shape[0] // 2
     scale = 1.0 / math.sqrt(HD)
     squares = jnp.zeros((tokens, HD), jnp.float32)
-    for head in range(HEADS):
-        cols = slice(head * HD, (head + 1) * HD)
+    rows = lax.broadcasted_iota(jnp.int32, (groups * cap, tokens), 0)
+    selector = (rows == flat_ref[...]).astype(jnp.float32).astype(jnp.bfloat16)
+    step = 256
+    for at in range(0, width, HD):
+        cols = slice(at, at + HD)
+        whole = slice(first + at, first + at + HD)
         keys = jnp.concatenate([r[:local, cols] for r in kv_refs], axis=0)
         values = jnp.concatenate([r[local:, cols] for r in kv_refs], axis=0)
         scores = (
             lax.dot_general(
-                query_ref[:, cols],
+                query_ref[:, whole],
                 keys,
                 (((1,), (1,)), ((), ())),
                 preferred_element_type=jnp.float32,
@@ -122,28 +126,29 @@
         raised = jnp.exp(scores - jnp.max(scores, axis=1, keepdims=True))
         total = jnp.sum(raised, axis=1, keepdims=True)
         mixed = jnp.dot(raised.astype(jnp.bfloat16), values, preferred_element_type=jnp.float32)
-        hidden = state_ref[:, cols].astype(jnp.float32) + mixed / total
+        hidden = state_ref[:, whole].astype(jnp.float32) + mixed / total
         hidden_ref[:, cols] = hidden
         squares = squares + hidden * hidden
-    mean_square = jnp.sum(squares, axis=1, keepdims=True) * (1.0 / width)
-    inverse = lax.rsqrt(mean_square + EPS)
-    rows = lax.broadcasted_iota(jnp.int32, (groups * cap, tokens), 0)
-    selector = (rows == flat_ref[...]).astype(jnp.float32).astype(jnp.bfloat16)
-    step = 512
-    for at in range(0, width, step):
-        cols = slice(at, at + step)
-        normed = (hidden_ref[:, cols] * inverse * gain_ref[:, cols]).astype(jnp.bfloat16)
-        packed = jnp.dot(selector, normed, preferred_element_type=jnp.float32).astype(jnp.bfloat16)
-        for group in range(groups):
-            packed_refs[group][:, cols] = packed[group * cap : (group + 1) * cap]
-
-
-def attend(state, query, gain, flat, kv_pieces, groups, cap, after):
-    tokens, width = state.shape
-    outs = [struct((tokens, width), jnp.float32)] + [struct((cap, width))] * groups
+        done = at + HD
+        if done % step == 0:
+            cols = slice(done - step, done)
+            gained = hidden_ref[:, cols] * gain_ref[:, first + done - step : first + done]
+            packed = jnp.dot(
+                selector, gained.astype(jnp.bfloat16), preferred_element_type=jnp.float32
+            ).astype(jnp.bfloat16)
+            for group in range(groups):
+                packed_refs[group][:, cols] = packed[group * cap : (group + 1) * cap]
+    squares_ref[...] = squares
+
+
+def attend(state, query, gain, flat, kv_pieces, groups, cap, first, after=()):
+    tokens = state.shape[0]
+    width = kv_pieces[0].shape[1]
+    outs = [struct((tokens, width), jnp.float32), struct((tokens, HD), jnp.float32)]
+    outs += [struct((cap, width))] * groups
     pieces = len(kv_pieces)
     return call(
-        functools.partial(attend_kernel, pieces, groups, cap),
+        functools.partial(attend_kernel, pieces, groups, cap, first),
         outs,
         [VMEM] * (4 + pieces) + [ANY] * len(after),
         "attend",
@@ -152,15 +157,15 @@
     )(state, query, gain, flat, *kv_pieces, *after)
 
 
-def ffn_kernel(parts, cut, *refs):
-    own_in, y_in, z_in = refs[:3]
-    d_in = refs[3 : 3 + parts]
-    in_a, in_b, out_a, out_b = refs[3 + parts : 7 + parts]
+def ffn_kernel(cut, *refs):
+    in_a, in_b, out_a, out_b = refs[8:12]
     own_ref, z0_ref, y1_ref, y0_ref, z1_ref = refs[-5:]
-    rows, width = own_in.shape
-    diagonal = jnp.concatenate([r[...] for r in d_in], axis=1)
-    entries = jnp.concatenate([own_in[...], y_in[...], z_in[...], diagonal], axis=0)
+    rows, half = refs[0].shape
+    width = 2 * half
     w_in = jnp.concatenate([in_a[...], in_b[...]], axis=1)
+    left = jnp.concatenate([r[...] for r in refs[:4]], axis=0)
+    right = jnp.concatenate([r[...] for r in refs[4:8]], axis=0)
+    entries = jnp.concatenate([left, right], axis=1)
     raw = jnp.dot(entries, w_in, preferred_element_type=jnp.float32)
     activation = jnp.maximum(raw, 0.0).astype(jnp.bfloat16)
     step = 512
@@ -182,8 +187,9 @@
             y1_ref[1, :, cols] = d_part
 
 
-def ffn(blocks, weights, cut, after=()):
-    rows, width = blocks[0].shape
+def ffn(left, right, weights, cut, after=()):
+    rows, half = left[0].shape
+    width = 2 * half
     units = weights[0].shape[1]
     rest = width - cut
     outs = [
@@ -194,13 +200,13 @@
         struct((rows, rest)),
     ]
     return call(
-        functools.partial(ffn_kernel, len(blocks) - 3, cut),
+        functools.partial(ffn_kernel, cut),
         outs,
-        [VMEM] * (len(blocks) + 4) + [ANY] * len(after),
+        [VMEM] * 12 + [ANY] * len(after),
         "expert_ffn",
         4 * 4 * rows * width * units * 2,
         8 * units * width + 16 * rows * width,
-    )(*blocks, *weights, *after)
+    )(*left, *right, *weights, *after)
 
 
 def first_kernel(y0_ref, az_ref, z1_ref, ay_ref, *refs):
@@ -250,11 +256,16 @@
 
 
 def finish_kernel(groups, cap, cut, *refs):
-    hidden_ref, gate_ref, flat_ref, own_ref, az_ref, ay_ref, by_ref, bz_ref = refs[:8]
-    back_refs = refs[8:-1]
+    hidden_refs = refs[:2]
+    square_refs = refs[2:4]
+    gate_ref, flat_ref, own_ref, az_ref, ay_ref, by_ref, bz_ref = refs[4:11]
+    back_refs = refs[11:-1]
     out_ref = refs[-1]
-    tokens, width = hidden_ref.shape
+    tokens, width = out_ref.shape
+    half = width // 2
     flat = flat_ref[...]
+    squares = jnp.sum(square_refs[0][...] + square_refs[1][...], axis=1, keepdims=True)
+    factor = gate_ref[...] * lax.rsqrt(squares * (1.0 / width) + EPS)
 
     def picker(group):
         slots = lax.broadcasted_iota(jnp.int32, (tokens, cap), 1) + group * cap
@@ -280,12 +291,15 @@
             picked = picked + jnp.dot(
                 pickers[group], back_refs[group - 1][:, whole], preferred_element_type=jnp.float32
             )
-        out_ref[:, whole] = (hidden_ref[:, whole] + gate_ref[...] * picked).astype(jnp.bfloat16)
-
-
-def finish(hidden, gate, flat, sums, backs, groups, cap, cut):
-    tokens, width = hidden.shape
-    operands = [hidden, gate, flat, *sums, *backs]
+        side, inner = divmod(at, half)
+        hidden = hidden_refs[side][:, inner : inner + step]
+        out_ref[:, whole] = (hidden + factor * picked).astype(jnp.bfloat16)
+
+
+def finish(hidden, squares, gate, flat, sums, backs, groups, cap, cut):
+    tokens = hidden[0].shape[0]
+    width = 2 * hidden[0].shape[1]
+    operands = [*hidden, *squares, gate, flat, *sums, *backs]
     return call(
         functools.partial(finish_kernel, groups, cap, cut),
         struct((tokens, width)),
@@ -302,6 +316,7 @@
     pipes = lax.axis_size("pipe")
     groups = devices // WSPLIT
     cap = 3 * tokens // (2 * groups)
+    half = width // 2
     far_cut, near_cut = width // 2, width // 4
 
     def across(value, bit):
@@ -311,13 +326,21 @@
         shift = count * WSPLIT
         return lax.ppermute(value, "expert", [(i, (i + shift) % devices) for i in range(devices)])
 
-    kv = jnp.transpose(enc_kv[0], (1, 0, 2)).reshape(-1, width)
-    kv_pieces = [kv]
-    for shift in range(1, pipes):
-        perm = [(i, (i + shift) % pipes) for i in range(pipes)]
-        kv_pieces.append(lax.ppermute(kv, "pipe", perm))
+    def cross(blocks):
+        return [groups_on(block, count) for count, block in enumerate(blocks, 1)]
+
+    def join(blocks):
+        return jnp.concatenate(blocks, axis=0) if len(blocks) > 1 else blocks[0]
+
+    def share(value):
+        perms = [[(i, (i + shift) % pipes) for i in range(pipes)] for shift in range(1, pipes)]
+        return [value] + [lax.ppermute(value, "pipe", perm) for perm in perms]
+
+    def split(value):
+        return jnp.transpose(value, (1, 0, 2)).reshape(-1, half)
+
     weights = [w_in, across(w_in, 1), w_out, across(w_out, 1)]
-
+    kv_a = share(split(enc_kv[0, :, :, :half]))
     group = (lax.axis_index("expert") // WSPLIT).astype(jnp.int32).reshape(1)
     staged = stage(
         group,
@@ -330,24 +353,24 @@
         groups,
         cap,
     )
+    kv_b = share(*after_all([split(enc_kv[0, :, :, half:])], [*kv_a[1:], staged[3]]))
     flat, gates = staged[4:]
-    hidden, near, *packed = attend(
-        *staged[:4], kv_pieces, groups, cap, after=[weights[1], weights[3]]
+    hidden_a, squares_a, near_a, *far_a = attend(*staged[:4], kv_a, groups, cap, 0)
+    hidden_b, squares_b, near_b, *far_b = attend(
+        *staged[:4], kv_b, groups, cap, half, after=[weights[1], weights[3]]
     )
-    far = [groups_on(block, count) for count, block in enumerate(packed, 1)]
-    far = jnp.concatenate(far, axis=0) if len(far) > 1 else far[0]
-
-    near_y, near_z = across(near, 2), across(near, 4)
-    near_blocks = [near, near_y, near_z, across(near_z, 2)]
-    far = after_all(far, [near_y, near_z])
-    far_y, far_z = across(far, 2), across(far, 4)
-    far_blocks = [
-        far,
-        far_y,
-        far_z,
-        across(far_y[:, :far_cut], 4),
-        across(far_z[:, far_cut:], 2),
-    ]
+
+    near_ya, near_za, far_a = across(near_a, 2), across(near_a, 4), cross(far_a)
+    far_b = cross(after_all(far_b, [*far_a, near_ya, near_za]))
+    (far_a,) = after_all([join(far_a)], [squares_b])
+    near_yb, near_zb = across(near_b, 2), across(near_b, 4)
+    far_ya, far_za = across(far_a, 2), across(far_a, 4)
+    (far_b,) = after_all([join(far_b)], [far_ya, far_za, near_yb, near_zb])
+    far_yb, far_zb = across(far_b, 2), across(far_b, 4)
+    near_left = [near_a, near_ya, near_za, across(near_za, 2)]
+    near_right = [near_b, near_yb, near_zb, across(near_zb, 2)]
+    far_left = [far_a, far_ya, far_za, across(far_ya, 4)]
+    far_right = [far_b, far_yb, far_zb, across(far_zb, 2)]
 
     def first_sums(own, z0, y1, y0, z1, after=()):
         from_z, from_y = across(z0, 4), across(y1, 2)
@@ -356,8 +379,8 @@
     def last_sums(own, from_z, from_y, on_y, on_z):
         return own, from_z, from_y, across(on_y, 2), across(on_z, 4)
 
-    far_parts = ffn(far_blocks, weights, far_cut)
-    near_parts = ffn(near_blocks, weights, near_cut, after=far_parts[3:])
+    far_parts = ffn(far_left, far_right, weights, far_cut)
+    near_parts = ffn(near_left, near_right, weights, near_cut, after=far_parts[3:])
     far_sum, *held = total(
         last_sums(*first_sums(*far_parts, after=near_parts[3:])), far_cut, near_parts[1:3]
     )
@@ -366,7 +389,7 @@
         for count in range(1, groups)
     ]
     near_sums = last_sums(*first_sums(near_parts[0], *held, *near_parts[3:]))
-    output = finish(hidden, gates, flat, near_sums, backs, groups, cap, near_cut)
+    output = finish([hidden_a, hidden_b], [squares_a, squares_b], gates, flat, near_sums, backs, groups, cap, near_cut)
     return output.reshape(1, 1, tokens, width)
 
 

time: 98.4 us -> 102 us (1.037)
  starting transfers between devices: 28.5 us -> 33.4 us
  waiting for transfers between devices: 53.2 us -> 49.8 us
  Pallas kernels: 10.5 us -> 12.4 us
    ppermute x2 -> x3, waiting for transfers between devices: 19.9 us -> 11.3 us  [groups_on(): lax.ppermute(value, 'expert', [(i, (i + shift) % devices) for i in range(...]
    ppermute x17 -> x22, waiting for transfers between devices: 31.6 us -> 38.5 us  [across(): return lax.ppermute(value, 'expert', [(i, i ^ bit) for i in range(devices)])]
    ppermute x17 -> x22, starting transfers between devices: 18.9 us -> 22.4 us  [across(): return lax.ppermute(value, 'expert', [(i, i ^ bit) for i in range(devices)])]
    pallas_call x4 -> x8, Pallas kernels: 8.57 us -> 10.5 us  [the longest x2 6.07 us: ffn(): call(functools.partial(ffn_kernel, cut), outs, [VMEM] * 12 + [ANY] * len(...]
    ppermute x1 -> x2, waiting for transfers between devices: 1.7 us -> 0.01 us  [share(): return [value] + [lax.ppermute(value, 'pipe', perm) for perm in perms]]
    ppermute x2 -> x3, starting transfers between devices: 6.58 us -> 7.53 us  [groups_on(): lax.ppermute(value, 'expert', [(i, (i + shift) % devices) for i in range(...]
    ppermute x1 -> x2, starting transfers between devices: 3 us -> 3.48 us  [share(): return [value] + [lax.ppermute(value, 'pipe', perm) for perm in perms]]
  transfers between devices with their start and end apart: 20 -> 27, of which waited for: 14 -> 14; matrix products, arithmetic and copies ran while one was open for 1% -> 1% of each run, Pallas kernels for 6% -> 11%
where the time goes in v3:
time: 102 us
  waiting for transfers between devices  49.8 us (49%)
  starting transfers between devices  33.4 us (33%)
  Pallas kernels  12.4 us (12%)
  local copies, waits for them, and re-layouts  5.95 us (6%)
    ppermute x22, waiting for transfers between devices, across(): return lax.ppermute(value, 'expert', [(i, i ^ bit) for i in range(devices)])  38.5 us
    ppermute x22, starting transfers between devices, across(): return lax.ppermute(value, 'expert', [(i, i ^ bit) for i in range(devices)])  22.4 us
    ppermute x3, waiting for transfers between devices, groups_on(): lax.ppermute(value, 'expert', [(i, (i + shift) % devices) for i in range(...  11.3 us
    ppermute x3, starting transfers between devices, groups_on(): lax.ppermute(value, 'expert', [(i, (i + shift) % devices) for i in range(...  7.53 us
    pallas_call x2, Pallas kernels, ffn(): call(functools.partial(ffn_kernel, cut), outs, [VMEM] * 12 + [ANY] * len(...  6.07 us
    unnamed x16, local copies, waits for them, and re-layouts  4.75 us
    pallas_call x2, Pallas kernels, attend(): call(functools.partial(attend_kernel, pieces, groups, cap, first), outs,...  4.44 us
    ppermute x2, starting transfers between devices, share(): return [value] + [lax.ppermute(value, 'pipe', perm) for perm in perms]  3.48 us
  transfers between devices with their start and end apart: 27, of which 14 were waited for; matrix products, arithmetic and copies ran while one was open for 1% of the time, Pallas kernels for 11%

profile of v3, /device:TPU:0, one launch (start us, length us, event | category | flops | bytes accessed | tf_op | source)
XLA Modules:
  0.0 101.7 jit_solution(16567824508883315746)
XLA Ops:
  0.0 0.5 collective-permute-start.2
  0.5 1.1 %slice_bitcast_fusion = (bf16[2,32,1024]{2,0,1:T(2,128)(2,1)S(1)}, bf16[2,32,1024]{2,0,1:T(2,128)(2,1)S(1)}) fusion(bf16[1,32,2,2048]{3,2,1,0:T(2,128)(2,1)} %param.11), kind=kLoop, calls=%fused_computation | loop fusion | bytes 524288 | tf_op jit(solution)/shard_map/transpose | solution.py:340
  1.7 3.0 %collective-permute-start = (bf16[64,1024]{1,0:T(8,128)(2,1)S(1)}, bf16[64,1024]{1,0:T(8,128)(2,1)S(1)}, u32[]{:S(2)}, u32[]{:S(2)}) collective-permute-start(bf16[64,1024]{1,0:T(8,128)(2,1)S(1)} %bitcast.19), channel_id=1, source_target_pairs={{0,16},{16,0},{1,17},{17,1},{2,18},{18,2},{3,19},{19,3},{4,20},{20... | collective-permute-start | bytes 393224 | tf_op jit(solution)/shard_map/ppermute | solution.py:337
  4.7 1.0 %copy-done = bf16[1,1,128,2048]{3,2,1,0:T(8,128)(2,1)S(1)} copy-done((bf16[1,1,128,2048]{3,2,1,0:T(8,128)(2,1)S(1)}, bf16[1,1,128,2048]{3,2,1,0:T(8,128)(2,1)}, u32[]{:S(2)}) %copy-start) | copy-done | bytes 524312
  5.7 1.0 %copy-done.1 = bf16[1,1,128,2048]{3,2,1,0:T(8,128)(2,1)S(1)} copy-done((bf16[1,1,128,2048]{3,2,1,0:T(8,128)(2,1)S(1)}, bf16[1,1,128,2048]{3,2,1,0:T(8,128)(2,1)}, u32[]{:S(2)}) %copy-start.1) | copy-done | bytes 524312
  6.8 0.7 copy-done.2
  7.5 0.7 copy-done.3
  8.1 0.7 copy-done.4
  8.8 0.7 copy-done.5
  9.4 0.1 stage.1
  9.6 0.5 collective-permute-start.1
  10.1 2.2 %attend.2 = (f32[128,1024]{1,0:T(8,128)S(1)}, f32[128,128]{1,0:T(8,128)S(1)}, bf16[96,1024]{1,0:T(8,128)(2,1)S(1)}, bf16[96,1024]{1,0:T(8,128)(2,1)S(1)}) custom-call(bf16[128,2048]{1,0:T(8,128)(2,1)S(1)} %get-tuple-element.36.refs_0_, bf16[128,2048]{1,0:T(8,128)(2,1)S(1)} %get-tuple-element.37.refs_1_, f32[1,2048]{1,0:T(1,128)S(1)} %get-tuple-element.38.refs_2_, ...), custom_call_target="tpu_custom_call" | custom-call | flops 67108864 | bytes 1572864 | tf_op jit(solution)/shard_map/attend/pallas_call | solution.py:150
  12.3 2.8 %collective-permute-start.10 = (bf16[96,1024]{1,0:T(8,128)(2,1)S(1)}, bf16[96,1024]{1,0:T(8,128)(2,1)S(1)}, u32[]{:S(2)}, u32[]{:S(2)}) collective-permute-start(bf16[96,1024]{1,0:T(8,128)(2,1)S(1)} %get-tuple-element.48), channel_id=1, source_target_pairs={{0,8},{1,9},{2,10},{3,11},{4,12},{5,13},{6,14},{7,15},{8,0},{9,1},... | collective-permute-start | bytes 589832 | tf_op jit(solution)/shard_map/ppermute | solution.py:327
  15.1 1.6 %collective-permute-start.5 = (bf16[96,1024]{1,0:T(8,128)(2,1)S(1)}, bf16[96,1024]{1,0:T(8,128)(2,1)S(1)}, u32[]{:S(2)}, u32[]{:S(2)}) collective-permute-start(bf16[96,1024]{1,0:T(8,128)(2,1)S(1)} %get-tuple-element.46.refs_0_), channel_id=1, source_target_pairs={{0,4},{1,5},{2,6},{3,7},{4,0},{5,1},{6,2},{7,3},{8,12},{9,13},{10,... | collective-permute-start | bytes 589832 | tf_op jit(solution)/shard_map/ppermute | solution.py:323
  16.7 1.5 %collective-permute-start.4 = (bf16[96,1024]{1,0:T(8,128)(2,1)S(1)}, bf16[96,1024]{1,0:T(8,128)(2,1)S(1)}, u32[]{:S(2)}, u32[]{:S(2)}) collective-permute-start(bf16[96,1024]{1,0:T(8,128)(2,1)S(1)} %get-tuple-element.46.refs_0_), channel_id=1, source_target_pairs={{0,2},{1,3},{2,0},{3,1},{4,6},{5,7},{6,4},{7,5},{8,10},{9,11},{10,... | collective-permute-start | bytes 589832 | tf_op jit(solution)/shard_map/ppermute | solution.py:323
  18.2 2.2 %attend.3 = (f32[128,1024]{1,0:T(8,128)S(1)}, f32[128,128]{1,0:T(8,128)S(1)}, bf16[96,1024]{1,0:T(8,128)(2,1)S(1)}, bf16[96,1024]{1,0:T(8,128)(2,1)S(1)}) custom-call(bf16[128,2048]{1,0:T(8,128)(2,1)S(1)} %get-tuple-element.36.refs_0_, bf16[128,2048]{1,0:T(8,128)(2,1)S(1)} %get-tuple-element.37.refs_1_, f32[1,2048]{1,0:T(1,128)S(1)} %get-tuple-element.38.refs_2_, ...), custom_call_target="tpu_custom_call" | custom-call | flops 67108864 | bytes 1572864 | tf_op jit(solution)/shard_map/attend/pallas_call | solution.py:150
  20.5 3.5 %collective-permute-done.10.refs_0_.refs_1_ = bf16[96,1024]{1,0:T(8,128)(2,1)S(1)} collective-permute-done((bf16[96,1024]{1,0:T(8,128)(2,1)S(1)}, bf16[96,1024]{1,0:T(8,128)(2,1)S(1)}, u32[]{:S(2)}, u32[]{:S(2)}) %collective-permute-start.10) | collective-permute-done | bytes 196640 | tf_op jit(solution)/shard_map/ppermute | solution.py:327
  23.9 0.2 collective-permute-done.5.refs_3_.refs_2_
  24.1 1.5 %collective-permute-start.12 = (bf16[96,1024]{1,0:T(8,128)(2,1)S(1)}, bf16[96,1024]{1,0:T(8,128)(2,1)S(1)}, u32[]{:S(2)}, u32[]{:S(2)}) collective-permute-start(bf16[96,1024]{1,0:T(8,128)(2,1)S(1)} %hand_on.5.refs_0_), channel_id=1, source_target_pairs={{0,4},{1,5},{2,6},{3,7},{4,0},{5,1},{6,2},{7,3},{8,12},{9,13},{10,... | collective-permute-start | bytes 589832 | tf_op jit(solution)/shard_map/ppermute | solution.py:323
  25.6 1.5 %collective-permute-start.11 = (bf16[96,1024]{1,0:T(8,128)(2,1)S(1)}, bf16[96,1024]{1,0:T(8,128)(2,1)S(1)}, u32[]{:S(2)}, u32[]{:S(2)}) collective-permute-start(bf16[96,1024]{1,0:T(8,128)(2,1)S(1)} %hand_on.5.refs_0_), channel_id=1, source_target_pairs={{0,2},{1,3},{2,0},{3,1},{4,6},{5,7},{6,4},{7,5},{8,10},{9,11},{10,... | collective-permute-start | bytes 589832 | tf_op jit(solution)/shard_map/ppermute | solution.py:323
  27.2 2.4 %collective-permute-start.14 = (bf16[96,1024]{1,0:T(8,128)(2,1)S(1)}, bf16[96,1024]{1,0:T(8,128)(2,1)S(1)}, u32[]{:S(2)}, u32[]{:S(2)}) collective-permute-start(bf16[96,1024]{1,0:T(8,128)(2,1)S(1)} %hand_on.6), channel_id=1, source_target_pairs={{0,8},{1,9},{2,10},{3,11},{4,12},{5,13},{6,14},{7,15},{8,0},{9,1},... | collective-permute-start | bytes 589832 | tf_op jit(solution)/shard_map/ppermute | solution.py:327
  29.6 0.5 collective-permute-start.7
  30.1 1.2 %collective-permute-done.11.refs_1_ = bf16[96,1024]{1,0:T(8,128)(2,1)S(1)} collective-permute-done((bf16[96,1024]{1,0:T(8,128)(2,1)S(1)}, bf16[96,1024]{1,0:T(8,128)(2,1)S(1)}, u32[]{:S(2)}, u32[]{:S(2)}) %collective-permute-start.11) | collective-permute-done | bytes 196640 | tf_op jit(solution)/shard_map/ppermute | solution.py:323
  31.3 7.0 %collective-permute-done.14.refs_0_ = bf16[96,1024]{1,0:T(8,128)(2,1)S(1)} collective-permute-done((bf16[96,1024]{1,0:T(8,128)(2,1)S(1)}, bf16[96,1024]{1,0:T(8,128)(2,1)S(1)}, u32[]{:S(2)}, u32[]{:S(2)}) %collective-permute-start.14) | collective-permute-done | bytes 196640 | tf_op jit(solution)/shard_map/ppermute | solution.py:327
  38.3 1.8 %collective-permute-start.16 = (bf16[96,1024]{1,0:T(8,128)(2,1)S(1)}, bf16[96,1024]{1,0:T(8,128)(2,1)S(1)}, u32[]{:S(2)}, u32[]{:S(2)}) collective-permute-start(bf16[96,1024]{1,0:T(8,128)(2,1)S(1)} %hand_on.7.refs_4_), channel_id=1, source_target_pairs={{0,4},{1,5},{2,6},{3,7},{4,0},{5,1},{6,2},{7,3},{8,12},{9,13},{10,... | collective-permute-start | bytes 589832 | tf_op jit(solution)/shard_map/ppermute | solution.py:323
  40.1 1.4 %collective-permute-start.15 = (bf16[96,1024]{1,0:T(8,128)(2,1)S(1)}, bf16[96,1024]{1,0:T(8,128)(2,1)S(1)}, u32[]{:S(2)}, u32[]{:S(2)}) collective-permute-start(bf16[96,1024]{1,0:T(8,128)(2,1)S(1)} %hand_on.7.refs_4_), channel_id=1, source_target_pairs={{0,2},{1,3},{2,0},{3,1},{4,6},{5,7},{6,4},{7,5},{8,10},{9,11},{10,... | collective-permute-start | bytes 589832 | tf_op jit(solution)/shard_map/ppermute | solution.py:323
  41.5 0.4 collective-permute-start.13
  41.8 3.4 %collective-permute-done.16.refs_6_ = bf16[96,1024]{1,0:T(8,128)(2,1)S(1)} collective-permute-done((bf16[96,1024]{1,0:T(8,128)(2,1)S(1)}, bf16[96,1024]{1,0:T(8,128)(2,1)S(1)}, u32[]{:S(2)}, u32[]{:S(2)}) %collective-permute-start.16) | collective-permute-done | bytes 196640 | tf_op jit(solution)/shard_map/ppermute | solution.py:323
  45.3 2.4 %collective-permute-start.17 = (bf16[96,1024]{1,0:T(8,128)(2,1)S(1)}, bf16[96,1024]{1,0:T(8,128)(2,1)S(1)}, u32[]{:S(2)}, u32[]{:S(2)}) collective-permute-start(bf16[96,1024]{1,0:T(8,128)(2,1)S(1)} %collective-permute-done.16.refs_6_), channel_id=1, source_target_pairs={{0,2},{1,3},{2,0},{3,1},{4,6},{5,7},{6,4},{7,5},{8,10},{9,11},{10,... | collective-permute-start | bytes 589832 | tf_op jit(solution)/shard_map/ppermute | solution.py:323
  47.7 2.0 %collective-permute-start.9 = (bf16[96,1024]{1,0:T(8,128)(2,1)S(1)}, bf16[96,1024]{1,0:T(8,128)(2,1)S(1)}, u32[]{:S(2)}, u32[]{:S(2)}) collective-permute-start(bf16[96,1024]{1,0:T(8,128)(2,1)S(1)} %collective-permute-done.8.refs_4_.refs_6_), channel_id=1, source_target_pairs={{0,2},{1,3},{2,0},{3,1},{4,6},{5,7},{6,4},{7,5},{8,10},{9,11},{10,... | collective-permute-start | bytes 589832 | tf_op jit(solution)/shard_map/ppermute | solution.py:323
  49.7 3.8 %collective-permute-done.17.refs_7_ = bf16[96,1024]{1,0:T(8,128)(2,1)S(1)} collective-permute-done((bf16[96,1024]{1,0:T(8,128)(2,1)S(1)}, bf16[96,1024]{1,0:T(8,128)(2,1)S(1)}, u32[]{:S(2)}, u32[]{:S(2)}) %collective-permute-start.17) | collective-permute-done | bytes 196640 | tf_op jit(solution)/shard_map/ppermute | solution.py:323
  53.5 3.0 %expert_ffn.2 = (bf16[96,2048]{1,0:T(8,128)(2,1)S(1)}, bf16[2,96,1024]{2,1,0:T(8,128)(2,1)S(1)}, bf16[2,96,1024]{2,1,0:T(8,128)(2,1)S(1)}, bf16[96,1024]{1,0:T(8,128)(2,1)S(1)}, bf16[96,1024]{1,0:T(8,128)(2,1)S(1)}) custom-call(bf16[96,1024]{1,0:T(8,128)(2,1)S(1)} %hand_on.5.refs_0_, bf16[96,1024]{1,0:T(8,128)(2,1)S(1)} %collective-permute-done.11.refs_1_, ...), custom_call_target="tpu_custom_call" | custom-call | flops 2415919104 | bytes 9437184 | tf_op jit(solution)/shard_map/expert_ffn/pallas_call | solution.py:202
  56.5 1.8 %collective-permute-start.18 = (bf16[2,96,1024]{2,1,0:T(8,128)(2,1)S(1)}, bf16[2,96,1024]{2,1,0:T(8,128)(2,1)S(1)}, u32[]{:S(2)}, u32[]{:S(2)}) collective-permute-start(bf16[2,96,1024]{2,1,0:T(8,128)(2,1)S(1)} %get-tuple-element.54), channel_id=1, source_target_pairs={{0,4},{1,5},{2,6},{3,7},{4,0},{5,1},{6,2},{7,3},{8,12},{9,13},{10,... | collective-permute-start | bytes 1179656 | tf_op jit(solution)/shard_map/ppermute | solution.py:323
  58.3 1.7 %collective-permute-start.19 = (bf16[2,96,1024]{2,1,0:T(8,128)(2,1)S(1)}, bf16[2,96,1024]{2,1,0:T(8,128)(2,1)S(1)}, u32[]{:S(2)}, u32[]{:S(2)}) collective-permute-start(bf16[2,96,1024]{2,1,0:T(8,128)(2,1)S(1)} %get-tuple-element.55), channel_id=1, source_target_pairs={{0,2},{1,3},{2,0},{3,1},{4,6},{5,7},{6,4},{7,5},{8,10},{9,11},{10,... | collective-permute-start | bytes 1179656 | tf_op jit(solution)/shard_map/ppermute | solution.py:323
  60.0 1.9 %collective-permute-done.9.refs_7_ = bf16[96,1024]{1,0:T(8,128)(2,1)S(1)} collective-permute-done((bf16[96,1024]{1,0:T(8,128)(2,1)S(1)}, bf16[96,1024]{1,0:T(8,128)(2,1)S(1)}, u32[]{:S(2)}, u32[]{:S(2)}) %collective-permute-start.9) | collective-permute-done | bytes 196640 | tf_op jit(solution)/shard_map/ppermute | solution.py:323
  61.9 3.0 %expert_ffn.3 = (bf16[96,2048]{1,0:T(8,128)(2,1)S(1)}, bf16[2,96,512]{2,1,0:T(8,128)(2,1)S(1)}, bf16[2,96,1536]{2,1,0:T(8,128)(2,1)S(1)}, bf16[96,512]{1,0:T(8,128)(2,1)S(1)}, bf16[96,1536]{1,0:T(8,128)(2,1)S(1)}) custom-call(bf16[96,1024]{1,0:T(8,128)(2,1)S(1)} %get-tuple-element.46.refs_0_, bf16[96,1024]{1,0:T(8,128)(2,1)S(1)} %collective-permute-done.4.refs_2_.refs_1_, ...), custom_call_target="tpu_custom_call" | custom-call | flops 2415919104 | bytes 9437184 | tf_op jit(solution)/shard_map/expert_ffn/pallas_call | solution.py:202
  65.0 2.4 %collective-permute-done.19.ay_ref.refs_2_ = bf16[2,96,1024]{2,1,0:T(8,128)(2,1)S(1)} collective-permute-done((bf16[2,96,1024]{2,1,0:T(8,128)(2,1)S(1)}, bf16[2,96,1024]{2,1,0:T(8,128)(2,1)S(1)}, u32[]{:S(2)}, u32[]{:S(2)}) %collective-permute-start.19) | collective-permute-done | bytes 393248 | tf_op jit(solution)/shard_map/ppermute | solution.py:323
  67.5 1.8 %collective-permute-start.20 = (bf16[96,1024]{1,0:T(8,128)(2,1)S(1)}, bf16[96,1024]{1,0:T(8,128)(2,1)S(1)}, u32[]{:S(2)}, u32[]{:S(2)}) collective-permute-start(bf16[96,1024]{1,0:T(8,128)(2,1)S(1)} %get-tuple-element.58), channel_id=1, source_target_pairs={{0,2},{1,3},{2,0},{3,1},{4,6},{5,7},{6,4},{7,5},{8,10},{9,11},{10,... | collective-permute-start | bytes 589832 | tf_op jit(solution)/shard_map/ppermute | solution.py:323
  69.3 1.6 %collective-permute-start.21 = (bf16[96,1024]{1,0:T(8,128)(2,1)S(1)}, bf16[96,1024]{1,0:T(8,128)(2,1)S(1)}, u32[]{:S(2)}, u32[]{:S(2)}) collective-permute-start(bf16[96,1024]{1,0:T(8,128)(2,1)S(1)} %get-tuple-element.59), channel_id=1, source_target_pairs={{0,4},{1,5},{2,6},{3,7},{4,0},{5,1},{6,2},{7,3},{8,12},{9,13},{10,... | collective-permute-start | bytes 589832 | tf_op jit(solution)/shard_map/ppermute | solution.py:323
  70.9 3.7 %collective-permute-done.20.refs_3_ = bf16[96,1024]{1,0:T(8,128)(2,1)S(1)} collective-permute-done((bf16[96,1024]{1,0:T(8,128)(2,1)S(1)}, bf16[96,1024]{1,0:T(8,128)(2,1)S(1)}, u32[]{:S(2)}, u32[]{:S(2)}) %collective-permute-start.20) | collective-permute-done | bytes 196640 | tf_op jit(solution)/shard_map/ppermute | solution.py:323
  74.6 6.6 %collective-permute-done.21.refs_4_ = bf16[96,1024]{1,0:T(8,128)(2,1)S(1)} collective-permute-done((bf16[96,1024]{1,0:T(8,128)(2,1)S(1)}, bf16[96,1024]{1,0:T(8,128)(2,1)S(1)}, u32[]{:S(2)}, u32[]{:S(2)}) %collective-permute-start.21) | collective-permute-done | bytes 196640 | tf_op jit(solution)/shard_map/ppermute | solution.py:323
  81.2 0.1 far_total.1
  81.5 2.4 %collective-permute-start.26 = (bf16[96,2048]{1,0:T(8,128)(2,1)S(1)}, bf16[96,2048]{1,0:T(8,128)(2,1)S(1)}, u32[]{:S(2)}, u32[]{:S(2)}) collective-permute-start(bf16[96,2048]{1,0:T(8,128)(2,1)S(1)} %get-tuple-element.66), channel_id=1, source_target_pairs={{0,8},{1,9},{2,10},{3,11},{4,12},{5,13},{6,14},{7,15},{8,0},{9,1},... | collective-permute-start | bytes 1179656 | tf_op jit(solution)/shard_map/ppermute | solution.py:327
  83.9 9.5 %collective-permute-done.22.az_ref.refs_7_ = bf16[2,96,512]{2,1,0:T(8,128)(2,1)S(1)} collective-permute-done((bf16[2,96,512]{2,1,0:T(8,128)(2,1)S(1)}, bf16[2,96,512]{2,1,0:T(8,128)(2,1)S(1)}, u32[]{:S(2)}, u32[]{:S(2)}) %collective-permute-start.22) | collective-permute-done | bytes 196640 | tf_op jit(solution)/shard_map/ppermute | solution.py:323
  93.6 0.9 collective-permute-done.26.refs_11_
  94.5 3.7 %collective-permute-done.24.refs_9_ = bf16[96,512]{1,0:T(8,128)(2,1)S(1)} collective-permute-done((bf16[96,512]{1,0:T(8,128)(2,1)S(1)}, bf16[96,512]{1,0:T(8,128)(2,1)S(1)}, u32[]{:S(2)}, u32[]{:S(2)}) %collective-permute-start.24) | collective-permute-done | bytes 98336 | tf_op jit(solution)/shard_map/ppermute | solution.py:323
  98.2 2.0 %collective-permute-done.25.refs_10_ = bf16[96,1536]{1,0:T(8,128)(2,1)S(1)} collective-permute-done((bf16[96,1536]{1,0:T(8,128)(2,1)S(1)}, bf16[96,1536]{1,0:T(8,128)(2,1)S(1)}, u32[]{:S(2)}, u32[]{:S(2)}) %collective-permute-start.25) | collective-permute-done | bytes 294944 | tf_op jit(solution)/shard_map/ppermute | solution.py:323
  100.3 1.4 %finish.1 = bf16[128,2048]{1,0:T(8,128)(2,1)} custom-call(f32[128,1024]{1,0:T(8,128)S(1)} %get-tuple-element.40.refs_0_, f32[128,1024]{1,0:T(8,128)S(1)} %get-tuple-element.41.refs_1_, f32[128,128]{1,0:T(8,128)S(1)} %get-tuple-element.42.refs_2_, f32[128,128]{1,0:T(8,128)S(1)} %get-tuple-element.43.refs_1_.refs_3_, f32[128,1]{1,0:T(8,128)S(1)} %get-tuple-element.44.refs_4_, ...), custom_call_target="tpu_custom_call" | custom-call | flops 301989888 | bytes 4194304 | tf_op jit(solution)/shard_map/finish/pallas_call | solution.py:303
  (38 shorter events, 0.7 us)
Async XLA Ops:
  0.0 18.2 %collective-permute-start.2 = (bf16[2048,384]{1,0:T(8,128)(2,1)}, bf16[2048,384]{1,0:T(8,128)(2,1)S(1)}, u32[]{:S(2)}, u32[]{:S(2)}) collective-permute-start(bf16[2048,384]{1,0:T(8,128)(2,1)} %refs_8_.3), channel_id=1, source_target_pairs={{0,1},{1,0},{2,3},{3,2},{4,5},{5,4},{6,7},{7,6},{8,9},{9,8},{10,11... | collective-permute-start | bytes 4718600 | tf_op jit(solution)/shard_map/ppermute | solution.py:323
  0.5 17.8 %collective-permute-start.3 = (bf16[384,2048]{1,0:T(8,128)(2,1)}, bf16[384,2048]{1,0:T(8,128)(2,1)S(1)}, u32[]{:S(2)}, u32[]{:S(2)}) collective-permute-start(bf16[384,2048]{1,0:T(8,128)(2,1)} %refs_10_.3), channel_id=1, source_target_pairs={{0,1},{1,0},{2,3},{3,2},{4,5},{5,4},{6,7},{7,6},{8,9},{9,8},{10,11... | collective-permute-start | bytes 4718600 | tf_op jit(solution)/shard_map/ppermute | solution.py:323
  1.7 7.9 %collective-permute-start = (bf16[64,1024]{1,0:T(8,128)(2,1)S(1)}, bf16[64,1024]{1,0:T(8,128)(2,1)S(1)}, u32[]{:S(2)}, u32[]{:S(2)}) collective-permute-start(bf16[64,1024]{1,0:T(8,128)(2,1)S(1)} %bitcast.19), channel_id=1, source_target_pairs={{0,16},{16,0},{1,17},{17,1},{2,18},{18,2},{3,19},{19,3},{4,20},{20... | collective-permute-start | bytes 393224 | tf_op jit(solution)/shard_map/ppermute | solution.py:337
  4.7 1.0 %copy-start = (bf16[1,1,128,2048]{3,2,1,0:T(8,128)(2,1)S(1)}, bf16[1,1,128,2048]{3,2,1,0:T(8,128)(2,1)}, u32[]{:S(2)}) copy-start(bf16[1,1,128,2048]{3,2,1,0:T(8,128)(2,1)} %param.9) | copy-start | bytes 1572868
  5.7 1.0 %copy-start.1 = (bf16[1,1,128,2048]{3,2,1,0:T(8,128)(2,1)S(1)}, bf16[1,1,128,2048]{3,2,1,0:T(8,128)(2,1)}, u32[]{:S(2)}) copy-start(bf16[1,1,128,2048]{3,2,1,0:T(8,128)(2,1)} %param.10) | copy-start | bytes 1572868
  6.8 0.7 copy-start.2
  7.5 0.7 copy-start.3
  8.1 0.7 copy-start.4
  8.8 0.7 copy-start.5
  9.6 7.1 %collective-permute-start.1 = (bf16[64,1024]{1,0:T(8,128)(2,1)S(1)}, bf16[64,1024]{1,0:T(8,128)(2,1)S(1)}, u32[]{:S(2)}, u32[]{:S(2)}) collective-permute-start(bf16[64,1024]{1,0:T(8,128)(2,1)S(1)} %hand_on.4.refs_4_), channel_id=1, source_target_pairs={{0,16},{16,0},{1,17},{17,1},{2,18},{18,2},{3,19},{19,3},{4,20},{20... | collective-permute-start | bytes 393224 | tf_op jit(solution)/shard_map/ppermute | solution.py:337
  12.3 11.6 %collective-permute-start.10 = (bf16[96,1024]{1,0:T(8,128)(2,1)S(1)}, bf16[96,1024]{1,0:T(8,128)(2,1)S(1)}, u32[]{:S(2)}, u32[]{:S(2)}) collective-permute-start(bf16[96,1024]{1,0:T(8,128)(2,1)S(1)} %get-tuple-element.48), channel_id=1, source_target_pairs={{0,8},{1,9},{2,10},{3,11},{4,12},{5,13},{6,14},{7,15},{8,0},{9,1},... | collective-permute-start | bytes 589832 | tf_op jit(solution)/shard_map/ppermute | solution.py:327
  15.1 9.0 %collective-permute-start.5 = (bf16[96,1024]{1,0:T(8,128)(2,1)S(1)}, bf16[96,1024]{1,0:T(8,128)(2,1)S(1)}, u32[]{:S(2)}, u32[]{:S(2)}) collective-permute-start(bf16[96,1024]{1,0:T(8,128)(2,1)S(1)} %get-tuple-element.46.refs_0_), channel_id=1, source_target_pairs={{0,4},{1,5},{2,6},{3,7},{4,0},{5,1},{6,2},{7,3},{8,12},{9,13},{10,... | collective-permute-start | bytes 589832 | tf_op jit(solution)/shard_map/ppermute | solution.py:323
  16.7 7.4 %collective-permute-start.4 = (bf16[96,1024]{1,0:T(8,128)(2,1)S(1)}, bf16[96,1024]{1,0:T(8,128)(2,1)S(1)}, u32[]{:S(2)}, u32[]{:S(2)}) collective-permute-start(bf16[96,1024]{1,0:T(8,128)(2,1)S(1)} %get-tuple-element.46.refs_0_), channel_id=1, source_target_pairs={{0,2},{1,3},{2,0},{3,1},{4,6},{5,7},{6,4},{7,5},{8,10},{9,11},{10,... | collective-permute-start | bytes 589832 | tf_op jit(solution)/shard_map/ppermute | solution.py:323
  18.2 35.3 %copy-start.7 = (bf16[384,2048]{1,0:T(8,128)(2,1)S(1)}, bf16[384,2048]{1,0:T(8,128)(2,1)}, u32[]{:S(2)}) copy-start(bf16[384,2048]{1,0:T(8,128)(2,1)} %refs_10_.3) | copy-start | bytes 4718596
  20.5 33.0 %copy-start.6 = (bf16[2048,384]{1,0:T(8,128)(2,1)S(1)}, bf16[2048,384]{1,0:T(8,128)(2,1)}, u32[]{:S(2)}) copy-start(bf16[2048,384]{1,0:T(8,128)(2,1)} %refs_8_.3) | copy-start | bytes 4718596
  24.1 6.0 %collective-permute-start.12 = (bf16[96,1024]{1,0:T(8,128)(2,1)S(1)}, bf16[96,1024]{1,0:T(8,128)(2,1)S(1)}, u32[]{:S(2)}, u32[]{:S(2)}) collective-permute-start(bf16[96,1024]{1,0:T(8,128)(2,1)S(1)} %hand_on.5.refs_0_), channel_id=1, source_target_pairs={{0,4},{1,5},{2,6},{3,7},{4,0},{5,1},{6,2},{7,3},{8,12},{9,13},{10,... | collective-permute-start | bytes 589832 | tf_op jit(solution)/shard_map/ppermute | solution.py:323
  25.6 5.7 %collective-permute-start.11 = (bf16[96,1024]{1,0:T(8,128)(2,1)S(1)}, bf16[96,1024]{1,0:T(8,128)(2,1)S(1)}, u32[]{:S(2)}, u32[]{:S(2)}) collective-permute-start(bf16[96,1024]{1,0:T(8,128)(2,1)S(1)} %hand_on.5.refs_0_), channel_id=1, source_target_pairs={{0,2},{1,3},{2,0},{3,1},{4,6},{5,7},{6,4},{7,5},{8,10},{9,11},{10,... | collective-permute-start | bytes 589832 | tf_op jit(solution)/shard_map/ppermute | solution.py:323
  27.2 11.1 %collective-permute-start.14 = (bf16[96,1024]{1,0:T(8,128)(2,1)S(1)}, bf16[96,1024]{1,0:T(8,128)(2,1)S(1)}, u32[]{:S(2)}, u32[]{:S(2)}) collective-permute-start(bf16[96,1024]{1,0:T(8,128)(2,1)S(1)} %hand_on.6), channel_id=1, source_target_pairs={{0,8},{1,9},{2,10},{3,11},{4,12},{5,13},{6,14},{7,15},{8,0},{9,1},... | collective-permute-start | bytes 589832 | tf_op jit(solution)/shard_map/ppermute | solution.py:327
  29.5 8.7 %collective-permute-start.8 = (bf16[96,1024]{1,0:T(8,128)(2,1)S(1)}, bf16[96,1024]{1,0:T(8,128)(2,1)S(1)}, u32[]{:S(2)}, u32[]{:S(2)}) collective-permute-start(bf16[96,1024]{1,0:T(8,128)(2,1)S(1)} %get-tuple-element.47.refs_4_), channel_id=1, source_target_pairs={{0,4},{1,5},{2,6},{3,7},{4,0},{5,1},{6,2},{7,3},{8,12},{9,13},{10,... | collective-permute-start | bytes 589832 | tf_op jit(solution)/shard_map/ppermute | solution.py:323
  29.6 8.7 %collective-permute-start.7 = (bf16[96,1024]{1,0:T(8,128)(2,1)S(1)}, bf16[96,1024]{1,0:T(8,128)(2,1)S(1)}, u32[]{:S(2)}, u32[]{:S(2)}) collective-permute-start(bf16[96,1024]{1,0:T(8,128)(2,1)S(1)} %get-tuple-element.47.refs_4_), channel_id=1, source_target_pairs={{0,2},{1,3},{2,0},{3,1},{4,6},{5,7},{6,4},{7,5},{8,10},{9,11},{10,... | collective-permute-start | bytes 589832 | tf_op jit(solution)/shard_map/ppermute | solution.py:323
  38.3 7.0 %collective-permute-start.16 = (bf16[96,1024]{1,0:T(8,128)(2,1)S(1)}, bf16[96,1024]{1,0:T(8,128)(2,1)S(1)}, u32[]{:S(2)}, u32[]{:S(2)}) collective-permute-start(bf16[96,1024]{1,0:T(8,128)(2,1)S(1)} %hand_on.7.refs_4_), channel_id=1, source_target_pairs={{0,4},{1,5},{2,6},{3,7},{4,0},{5,1},{6,2},{7,3},{8,12},{9,13},{10,... | collective-permute-start | bytes 589832 | tf_op jit(solution)/shard_map/ppermute | solution.py:323
  40.1 9.6 %collective-permute-start.15 = (bf16[96,1024]{1,0:T(8,128)(2,1)S(1)}, bf16[96,1024]{1,0:T(8,128)(2,1)S(1)}, u32[]{:S(2)}, u32[]{:S(2)}) collective-permute-start(bf16[96,1024]{1,0:T(8,128)(2,1)S(1)} %hand_on.7.refs_4_), channel_id=1, source_target_pairs={{0,2},{1,3},{2,0},{3,1},{4,6},{5,7},{6,4},{7,5},{8,10},{9,11},{10,... | collective-permute-start | bytes 589832 | tf_op jit(solution)/shard_map/ppermute | solution.py:323
  41.5 8.2 %collective-permute-start.13 = (bf16[96,1024]{1,0:T(8,128)(2,1)S(1)}, bf16[96,1024]{1,0:T(8,128)(2,1)S(1)}, u32[]{:S(2)}, u32[]{:S(2)}) collective-permute-start(bf16[96,1024]{1,0:T(8,128)(2,1)S(1)} %collective-permute-done.11.refs_1_), channel_id=1, source_target_pairs={{0,4},{1,5},{2,6},{3,7},{4,0},{5,1},{6,2},{7,3},{8,12},{9,13},{10,... | collective-permute-start | bytes 589832 | tf_op jit(solution)/shard_map/ppermute | solution.py:323
  45.3 8.2 %collective-permute-start.17 = (bf16[96,1024]{1,0:T(8,128)(2,1)S(1)}, bf16[96,1024]{1,0:T(8,128)(2,1)S(1)}, u32[]{:S(2)}, u32[]{:S(2)}) collective-permute-start(bf16[96,1024]{1,0:T(8,128)(2,1)S(1)} %collective-permute-done.16.refs_6_), channel_id=1, source_target_pairs={{0,2},{1,3},{2,0},{3,1},{4,6},{5,7},{6,4},{7,5},{8,10},{9,11},{10,... | collective-permute-start | bytes 589832 | tf_op jit(solution)/shard_map/ppermute | solution.py:323
  47.7 12.4 %collective-permute-start.6 = (bf16[96,1024]{1,0:T(8,128)(2,1)S(1)}, bf16[96,1024]{1,0:T(8,128)(2,1)S(1)}, u32[]{:S(2)}, u32[]{:S(2)}) collective-permute-start(bf16[96,1024]{1,0:T(8,128)(2,1)S(1)} %collective-permute-done.5.refs_3_.refs_2_), channel_id=1, source_target_pairs={{0,2},{1,3},{2,0},{3,1},{4,6},{5,7},{6,4},{7,5},{8,10},{9,11},{10,... | collective-permute-start | bytes 589832 | tf_op jit(solution)/shard_map/ppermute | solution.py:323
  47.7 14.2 %collective-permute-start.9 = (bf16[96,1024]{1,0:T(8,128)(2,1)S(1)}, bf16[96,1024]{1,0:T(8,128)(2,1)S(1)}, u32[]{:S(2)}, u32[]{:S(2)}) collective-permute-start(bf16[96,1024]{1,0:T(8,128)(2,1)S(1)} %collective-permute-done.8.refs_4_.refs_6_), channel_id=1, source_target_pairs={{0,2},{1,3},{2,0},{3,1},{4,6},{5,7},{6,4},{7,5},{8,10},{9,11},{10,... | collective-permute-start | bytes 589832 | tf_op jit(solution)/shard_map/ppermute | solution.py:323
  56.5 8.4 %collective-permute-start.18 = (bf16[2,96,1024]{2,1,0:T(8,128)(2,1)S(1)}, bf16[2,96,1024]{2,1,0:T(8,128)(2,1)S(1)}, u32[]{:S(2)}, u32[]{:S(2)}) collective-permute-start(bf16[2,96,1024]{2,1,0:T(8,128)(2,1)S(1)} %get-tuple-element.54), channel_id=1, source_target_pairs={{0,4},{1,5},{2,6},{3,7},{4,0},{5,1},{6,2},{7,3},{8,12},{9,13},{10,... | collective-permute-start | bytes 1179656 | tf_op jit(solution)/shard_map/ppermute | solution.py:323
  58.3 9.1 %collective-permute-start.19 = (bf16[2,96,1024]{2,1,0:T(8,128)(2,1)S(1)}, bf16[2,96,1024]{2,1,0:T(8,128)(2,1)S(1)}, u32[]{:S(2)}, u32[]{:S(2)}) collective-permute-start(bf16[2,96,1024]{2,1,0:T(8,128)(2,1)S(1)} %get-tuple-element.55), channel_id=1, source_target_pairs={{0,2},{1,3},{2,0},{3,1},{4,6},{5,7},{6,4},{7,5},{8,10},{9,11},{10,... | collective-permute-start | bytes 1179656 | tf_op jit(solution)/shard_map/ppermute | solution.py:323
  67.5 7.1 %collective-permute-start.20 = (bf16[96,1024]{1,0:T(8,128)(2,1)S(1)}, bf16[96,1024]{1,0:T(8,128)(2,1)S(1)}, u32[]{:S(2)}, u32[]{:S(2)}) collective-permute-start(bf16[96,1024]{1,0:T(8,128)(2,1)S(1)} %get-tuple-element.58), channel_id=1, source_target_pairs={{0,2},{1,3},{2,0},{3,1},{4,6},{5,7},{6,4},{7,5},{8,10},{9,11},{10,... | collective-permute-start | bytes 589832 | tf_op jit(solution)/shard_map/ppermute | solution.py:323
  69.3 11.9 %collective-permute-start.21 = (bf16[96,1024]{1,0:T(8,128)(2,1)S(1)}, bf16[96,1024]{1,0:T(8,128)(2,1)S(1)}, u32[]{:S(2)}, u32[]{:S(2)}) collective-permute-start(bf16[96,1024]{1,0:T(8,128)(2,1)S(1)} %get-tuple-element.59), channel_id=1, source_target_pairs={{0,4},{1,5},{2,6},{3,7},{4,0},{5,1},{6,2},{7,3},{8,12},{9,13},{10,... | collective-permute-start | bytes 589832 | tf_op jit(solution)/shard_map/ppermute | solution.py:323
  81.4 12.0 %collective-permute-start.23 = (bf16[2,96,1536]{2,1,0:T(8,128)(2,1)S(1)}, bf16[2,96,1536]{2,1,0:T(8,128)(2,1)S(1)}, u32[]{:S(2)}, u32[]{:S(2)}) collective-permute-start(bf16[2,96,1536]{2,1,0:T(8,128)(2,1)S(1)} %get-tuple-element.63), channel_id=1, source_target_pairs={{0,2},{1,3},{2,0},{3,1},{4,6},{5,7},{6,4},{7,5},{8,10},{9,11},{10,... | collective-permute-start | bytes 1769480 | tf_op jit(solution)/shard_map/ppermute | solution.py:323
  81.4 11.9 %collective-permute-start.22 = (bf16[2,96,512]{2,1,0:T(8,128)(2,1)S(1)}, bf16[2,96,512]{2,1,0:T(8,128)(2,1)S(1)}, u32[]{:S(2)}, u32[]{:S(2)}) collective-permute-start(bf16[2,96,512]{2,1,0:T(8,128)(2,1)S(1)} %get-tuple-element.62), channel_id=1, source_target_pairs={{0,4},{1,5},{2,6},{3,7},{4,0},{5,1},{6,2},{7,3},{8,12},{9,13},{10,... | collective-permute-start | bytes 589832 | tf_op jit(solution)/shard_map/ppermute | solution.py:323
  81.5 13.0 %collective-permute-start.26 = (bf16[96,2048]{1,0:T(8,128)(2,1)S(1)}, bf16[96,2048]{1,0:T(8,128)(2,1)S(1)}, u32[]{:S(2)}, u32[]{:S(2)}) collective-permute-start(bf16[96,2048]{1,0:T(8,128)(2,1)S(1)} %get-tuple-element.66), channel_id=1, source_target_pairs={{0,8},{1,9},{2,10},{3,11},{4,12},{5,13},{6,14},{7,15},{8,0},{9,1},... | collective-permute-start | bytes 1179656 | tf_op jit(solution)/shard_map/ppermute | solution.py:327
  93.5 6.8 %collective-permute-start.25 = (bf16[96,1536]{1,0:T(8,128)(2,1)S(1)}, bf16[96,1536]{1,0:T(8,128)(2,1)S(1)}, u32[]{:S(2)}, u32[]{:S(2)}) collective-permute-start(bf16[96,1536]{1,0:T(8,128)(2,1)S(1)} %get-tuple-element.65), channel_id=1, source_target_pairs={{0,4},{1,5},{2,6},{3,7},{4,0},{5,1},{6,2},{7,3},{8,12},{9,13},{10,... | collective-permute-start | bytes 884744 | tf_op jit(solution)/shard_map/ppermute | solution.py:323
  93.6 4.7 %collective-permute-start.24 = (bf16[96,512]{1,0:T(8,128)(2,1)S(1)}, bf16[96,512]{1,0:T(8,128)(2,1)S(1)}, u32[]{:S(2)}, u32[]{:S(2)}) collective-permute-start(bf16[96,512]{1,0:T(8,128)(2,1)S(1)} %get-tuple-element.64), channel_id=1, source_target_pairs={{0,2},{1,3},{2,0},{3,1},{4,6},{5,7},{6,4},{7,5},{8,10},{9,11},{10,... | collective-permute-start | bytes 294920 | tf_op jit(solution)/shard_map/ppermute | solution.py:323

commit v4 on v2

v4 whole, which is shorter than its diff:
```python
import functools
import math

import jax
import jax.numpy as jnp
from jax import lax
from jax.experimental import pallas as pl
from jax.experimental.pallas import tpu as pltpu
from jax.sharding import PartitionSpec as P

HEADS = 16
HD = 128
WSPLIT = 8
EPS = 1e-06
VMEM_LIMIT = 32 * 1024 * 1024

VMEM = pl.BlockSpec(memory_space=pltpu.VMEM)
SMEM = pl.BlockSpec(memory_space=pltpu.SMEM)
ANY = pl.BlockSpec(memory_space=pl.ANY)


def struct(shape, dtype=jnp.bfloat16):
    return jax.ShapeDtypeStruct(shape, dtype)


def call(
    kernel, outs, in_specs, name, flops, moved, out_specs=None, aliases=None
):
    return pl.pallas_call(
        kernel,
        out_shape=outs,
        in_specs=in_specs,
        out_specs=out_specs or jax.tree.map(lambda _: VMEM, outs),
        input_output_aliases=aliases or {},
        compiler_params=pltpu.CompilerParams(vmem_limit_bytes=VMEM_LIMIT),
        cost_estimate=pl.CostEstimate(flops=flops, bytes_accessed=moved, transcendentals=0),
        name=name,
    )


def as_column(row):
    count = row.shape[1]
    down = lax.broadcasted_iota(jnp.int32, (count, count), 0)
    along = lax.broadcasted_iota(jnp.int32, (count, count), 1)
    return jnp.sum(jnp.where(down == along, row, jnp.zeros_like(row)), axis=1, keepdims=True)


def stage_kernel(groups, cap, *refs):
    group_ref, state_in, query_in, gain_in, expert_ref, slot_ref, gate_ref = refs[:7]
    state_out, query_out, gain_out, flat_row, flat_column, gate_column = refs[7:]
    state_out[...] = state_in[...]
    query_out[...] = query_in[...]
    gain_out[...] = gain_in[...]
    offset = expert_ref[...] - group_ref[0]
    offset = jnp.where(offset < 0, offset + groups, offset)
    slot = slot_ref[...]
    flat = jnp.where(slot >= 0, offset * cap + slot, -1)
    flat_row[...] = flat
    flat_column[...] = as_column(flat)
    gate_column[...] = as_column(gate_ref[...])


def stage(group, state, query, gain, expert_id, slot, gate, groups, cap):
    tokens, width = state.shape
    outs = [
        struct((tokens, width)),
        struct((tokens, width)),
        struct((1, width), jnp.float32),
        struct((1, tokens), jnp.int32),
        struct((tokens, 1), jnp.int32),
        struct((tokens, 1), jnp.float32),
    ]
    return call(
        functools.partial(stage_kernel, groups, cap),
        outs,
        [SMEM] + [VMEM] * 6,
        "stage",
        tokens * tokens,
        8 * tokens * width,
    )(group, state, query, gain, expert_id, slot, gate)


def gate_kernel(*refs):
    pass


def after_all(values, others):
    return call(
        gate_kernel,
        [struct(value.shape) for value in values],
        [ANY] * (len(values) + len(others)),
        "hand_on",
        1,
        1,
        out_specs=[ANY] * len(values),
        aliases={i: i for i in range(len(values))},
    )(*values, *others)


def attend_kernel(pieces, groups, cap, *refs):
    state_ref, query_ref, gain_ref, flat_ref = refs[:4]
    kv_refs = refs[4 : 4 + pieces]
    hidden_ref = refs[-1 - groups]
    packed_refs = refs[-groups:]
    tokens, width = state_ref.shape
    local = kv_refs[0].shape[0] // 2
    scale = 1.0 / math.sqrt(HD)
    squares = jnp.zeros((tokens, HD), jnp.float32)
    for head in range(HEADS):
        cols = slice(head * HD, (head + 1) * HD)
        keys = jnp.concatenate([r[:local, cols] for r in kv_refs], axis=0)
        values = jnp.concatenate([r[local:, cols] for r in kv_refs], axis=0)
        scores = (
            lax.dot_general(
                query_ref[:, cols],
                keys,
                (((1,), (1,)), ((), ())),
                preferred_element_type=jnp.float32,
            )
            * scale
        )
        raised = jnp.exp(scores - jnp.max(scores, axis=1, keepdims=True))
        total = jnp.sum(raised, axis=1, keepdims=True)
        mixed = jnp.dot(raised.astype(jnp.bfloat16), values, preferred_element_type=jnp.float32)
        hidden = state_ref[:, cols].astype(jnp.float32) + mixed / total
        hidden_ref[:, cols] = hidden
        squares = squares + hidden * hidden
    mean_square = jnp.sum(squares, axis=1, keepdims=True) * (1.0 / width)
    inverse = lax.rsqrt(mean_square + EPS)
    rows = lax.broadcasted_iota(jnp.int32, (groups * cap, tokens), 0)
    selector = (rows == flat_ref[...]).astype(jnp.float32).astype(jnp.bfloat16)
    step = 512
    for at in range(0, width, step):
        cols = slice(at, at + step)
        normed = (hidden_ref[:, cols] * inverse * gain_ref[:, cols]).astype(jnp.bfloat16)
        packed = jnp.dot(selector, normed, preferred_element_type=jnp.float32).astype(jnp.bfloat16)
        for group in range(groups):
            packed_refs[group][:, cols] = packed[group * cap : (group + 1) * cap]


def attend(state, query, gain, flat, kv_pieces, groups, cap, after):
    tokens, width = state.shape
    outs = [struct((tokens, width), jnp.float32)] + [struct((cap, width))] * groups
    pieces = len(kv_pieces)
    return call(
        functools.partial(attend_kernel, pieces, groups, cap),
        outs,
        [VMEM] * (4 + pieces) + [ANY] * len(after),
        "attend",
        4 * tokens * pieces * kv_pieces[0].shape[0] * width,
        12 * tokens * width,
    )(state, query, gain, flat, *kv_pieces, *after)


def ffn_kernel(rows_ref, in_a, in_b, out_a, out_b, out_ref):
    w_in = jnp.concatenate([in_a[...], in_b[...]], axis=1)
    raw = jnp.dot(rows_ref[...], w_in, preferred_element_type=jnp.float32)
    activation = jnp.maximum(raw, 0.0).astype(jnp.bfloat16)
    step = 512
    for at in range(0, out_ref.shape[1], step):
        cols = slice(at, at + step)
        w_out = jnp.concatenate([out_a[:, cols], out_b[:, cols]], axis=0)
        part = jnp.dot(activation, w_out, preferred_element_type=jnp.float32)
        out_ref[:, cols] = part.astype(jnp.bfloat16)


def ffn(rows, weights):
    count, width = rows.shape
    units = weights[0].shape[1]
    return call(
        ffn_kernel,
        struct((count, width)),
        [VMEM] * 5,
        "expert_ffn",
        4 * count * width * units * 2,
        8 * units * width + 4 * count * width,
    )(rows, *weights)


def finish_kernel(groups, cap, *refs):
    hidden_ref, gate_ref, flat_ref = refs[:3]
    sum_refs = refs[3:-1]
    out_ref = refs[-1]
    tokens, width = hidden_ref.shape
    flat = flat_ref[...]
    step = 512
    for at in range(0, width, step):
        cols = slice(at, at + step)
        picked = jnp.zeros((tokens, step), jnp.float32)
        for group in range(groups):
            slots = lax.broadcasted_iota(jnp.int32, (tokens, cap), 1) + group * cap
            picker = (slots == flat).astype(jnp.float32).astype(jnp.bfloat16)
            picked = picked + jnp.dot(
                picker, sum_refs[group][:, cols], preferred_element_type=jnp.float32
            )
        out_ref[:, cols] = (hidden_ref[:, cols] + gate_ref[...] * picked).astype(jnp.bfloat16)


def finish(hidden, gate, flat, sums, groups, cap):
    tokens, width = hidden.shape
    operands = [hidden, gate, flat, *sums]
    return call(
        functools.partial(finish_kernel, groups, cap),
        struct((tokens, width)),
        [VMEM] * len(operands),
        "finish",
        4 * tokens * cap * groups * width,
        16 * tokens * width,
    )(*operands)


def body(state, query, enc_kv, gain, w_in, w_out, expert_id, slot, gate):
    tokens, width = state.shape[2:]
    devices = lax.axis_size("expert")
    pipes = lax.axis_size("pipe")
    groups = devices // WSPLIT
    cap = 3 * tokens // (2 * groups)

    def across(value, bit):
        return lax.ppermute(value, "expert", [(i, i ^ bit) for i in range(devices)])

    def groups_on(value, count):
        shift = count * WSPLIT
        return lax.ppermute(value, "expert", [(i, (i + shift) % devices) for i in range(devices)])

    kv = jnp.transpose(enc_kv[0], (1, 0, 2)).reshape(-1, width)
    kv_pieces = [kv]
    for shift in range(1, pipes):
        perm = [(i, (i + shift) % pipes) for i in range(pipes)]
        kv_pieces.append(lax.ppermute(kv, "pipe", perm))
    weights = [w_in, across(w_in, 1), w_out, across(w_out, 1)]

    group = (lax.axis_index("expert") // WSPLIT).astype(jnp.int32).reshape(1)
    staged = stage(
        group,
        state[0, 0],
        query[0, 0],
        gain.reshape(1, width),
        expert_id[0],
        slot[0],
        gate[0],
        groups,
        cap,
    )
    flat, gates = staged[4:]
    hidden, near, *packed = attend(
        *staged[:4], kv_pieces, groups, cap, after=[weights[1], weights[3]]
    )
    far = [groups_on(block, count) for count, block in enumerate(packed, 1)]
    far = jnp.concatenate(far, axis=0) if len(far) > 1 else far[0]

    squares = [
        [base + core + 2 * chip for chip in range(WSPLIT // 2)]
        for base in range(0, devices, WSPLIT)
        for core in range(2)
    ]

    def spread(rows):
        return lax.all_gather(rows, "expert", axis_index_groups=squares, axis=0, tiled=True)

    def experts(spread):
        partial_value = ffn(spread, weights)
        return lax.psum_scatter(
            partial_value,
            "expert",
            scatter_dimension=0,
            axis_index_groups=squares,
            tiled=True,
        )

    near = spread(near)
    far = spread(*after_all([far], [near]))
    near_sum, far_sum = experts(near), experts(far)
    backs = [
        groups_on(far_sum[(count - 1) * cap : count * cap], groups - count)
        for count in range(1, groups)
    ]
    output = finish(hidden, gates, flat, [near_sum, *backs], groups, cap)
    return output.reshape(1, 1, tokens, width)


def solution(mesh):
    return jax.shard_map(
        body,
        mesh=mesh,
        in_specs=(
            P("expert", "pipe", None, None),
            P("expert", "pipe", None, None),
            P("expert", "pipe", None, None),
            P(),
            P(None, "expert"),
            P("expert", None),
            P("expert", "pipe", None),
            P("expert", "pipe", None),
            P("expert", "pipe", None),
        ),
        out_specs=P("expert", "pipe", None, None),
        check_vma=False,
    )
```

time: 98.4 us -> 191 us (1.94)
  waiting for transfers between devices: 53.2 us -> 137 us
  starting transfers between devices: 28.5 us -> 8.92 us
  local copies, waits for them, and re-layouts: 5.81 us -> 21.4 us
  between operations: 0.1 us -> 13.2 us
    reduce_scatter x0 -> x2, waiting for transfers between devices: none -> 62 us  [experts(): lax.psum_scatter(partial_value, 'expert', scatter_dimension=0, axis_index...]
    all_gather x0 -> x2, waiting for transfers between devices: none -> 55.6 us  [spread(): lax.all_gather(rows, 'expert', axis_index_groups=squares, axis=0, tiled=T...]
    ppermute x17 -> x2, waiting for transfers between devices: 31.6 us -> 0.01 us  [across(): return lax.ppermute(value, 'expert', [(i, i ^ bit) for i in range(devices)])]
    ppermute x17 -> x2, starting transfers between devices: 18.9 us -> 0.51 us  [across(): return lax.ppermute(value, 'expert', [(i, i ^ bit) for i in range(devices)])]
    unnamed x16 -> x40, local copies, waits for them, and re-layouts: 4.75 us -> 20.4 us
    ppermute x2, waiting for transfers between devices: 19.9 us -> 17.4 us  [groups_on(): lax.ppermute(value, 'expert', [(i, (i + shift) % devices) for i in range(...]
    pallas_call x7 -> x4, Pallas kernels: 7.82 us -> 7.33 us  [the longest x2 6.06 us: ffn(): call(ffn_kernel, struct((count, width)), [VMEM] * 5, 'expert_ffn', 4 * co...]
  transfers between devices with their start and end apart: 20 -> 9, of which waited for: 14 -> 6; matrix products, arithmetic and copies ran while one was open for 1% -> 1% of each run, Pallas kernels for 6% -> 2%
where the time goes in v4:
time: 191 us; the launch traced here: 190 us
  waiting for transfers between devices  137 us (72%)
  local copies, waits for them, and re-layouts  21.4 us (11%)
  between operations  13.2 us (7%)
  Pallas kernels  9.84 us (5%)
  starting transfers between devices  8.92 us (5%)
    reduce_scatter x2, waiting for transfers between devices, experts(): lax.psum_scatter(partial_value, 'expert', scatter_dimension=0, axis_index...  62 us
    all_gather x2, waiting for transfers between devices, spread(): lax.all_gather(rows, 'expert', axis_index_groups=squares, axis=0, tiled=T...  55.6 us
    unnamed x40, local copies, waits for them, and re-layouts  20.4 us
    ppermute x2, waiting for transfers between devices, groups_on(): lax.ppermute(value, 'expert', [(i, (i + shift) % devices) for i in range(...  17.4 us
    pallas_call x2, Pallas kernels, ffn(): call(ffn_kernel, struct((count, width)), [VMEM] * 5, 'expert_ffn', 4 * co...  6.06 us
    ppermute x2, starting transfers between devices, groups_on(): lax.ppermute(value, 'expert', [(i, (i + shift) % devices) for i in range(...  5.28 us
  transfers between devices with their start and end apart: 9, of which 6 were waited for; matrix products, arithmetic and copies ran while one was open for 1% of the time, Pallas kernels for 2%

profile of v4, /device:TPU:0, one launch (start us, length us, event | category | flops | bytes accessed | tf_op | source)
XLA Modules:
  0.0 190.2 jit_solution(10710298662977958404)
XLA Ops:
  6.5 0.0 all-gather.3.cloned.1.call-start
  6.5 0.5 collective-permute-start.1
  7.0 0.1 collective-permute-start.2
  7.0 1.0 copy.11
  8.1 3.0 %collective-permute-start = (bf16[64,2048]{1,0:T(8,128)(2,1)S(1)}, bf16[64,2048]{1,0:T(8,128)(2,1)}, u32[]{:S(2)}, u32[]{:S(2)}) collective-permute-start(bf16[64,2048]{1,0:T(8,128)(2,1)S(1)} %bitcast.12), channel_id=1, source_target_pairs={{0,16},{16,0},{1,17},{17,1},{2,18},{18,2},{3,19},{19,3},{4,20},{20... | collective-permute-start | bytes 786440 | tf_op jit(solution)/shard_map/ppermute | solution.py:230
  11.1 1.0 copy-done.11
  12.1 1.0 copy-done.12
  13.2 0.7 copy-done.15
  13.9 0.7 copy-done.16
  14.5 0.7 copy-done.17
  15.2 0.7 copy-done.18
  15.8 0.1 stage.1
  16.0 1.7 collective-permute-done.refs_5_
  17.7 0.0 collective-permute-done.1.refs_6_.in_b
  17.7 0.0 collective-permute-done.2.refs_7_.out_b
  17.7 2.4 %attend.1 = (f32[128,2048]{1,0:T(8,128)S(1)}, bf16[96,2048]{1,0:T(8,128)(2,1)S(1)}, bf16[96,2048]{1,0:T(8,128)(2,1)S(1)}) custom-call(bf16[128,2048]{1,0:T(8,128)(2,1)S(1)} %get-tuple-element.14.refs_0_, bf16[128,2048]{1,0:T(8,128)(2,1)S(1)} %get-tuple-element.15.refs_1_, f32[1,2048]{1,0:T(1,128)S(1)} %get-tuple-element.16.refs_2_, ...), custom_call_target="tpu_custom_call" | custom-call | flops 134217728 | bytes 3145728 | tf_op jit(solution)/shard_map/attend/pallas_call | solution.py:145
  20.1 1.0 copy-done.9
  21.0 0.7 copy-done.14
  21.8 0.7 copy-done.19
  22.5 0.0 all-gather.3.cloned.1.call-update
  22.5 0.0 all-gather.5.cloned.1.call-start
  22.6 2.9 %collective-permute-start.3 = (bf16[96,2048]{1,0:T(8,128)(2,1)}, bf16[96,2048]{1,0:T(8,128)(2,1)}, u32[]{:S(2)}, u32[]{:S(2)}) collective-permute-start(bf16[96,2048]{1,0:T(8,128)(2,1)} %copy-done.19), channel_id=1, source_target_pairs={{0,8},{1,9},{2,10},{3,11},{4,12},{5,13},{6,14},{7,15},{8,0},{9,1},... | collective-permute-start | bytes 1179656 | tf_op jit(solution)/shard_map/ppermute | solution.py:224
  25.5 17.4 %collective-permute-done.3.refs_0_ = bf16[96,2048]{1,0:T(8,128)(2,1)} collective-permute-done((bf16[96,2048]{1,0:T(8,128)(2,1)}, bf16[96,2048]{1,0:T(8,128)(2,1)}, u32[]{:S(2)}, u32[]{:S(2)}) %collective-permute-start.3) | collective-permute-done | bytes 393248 | tf_op jit(solution)/shard_map/ppermute | solution.py:224
  42.9 20.2 %all-gather.3.cloned.1.call-done.rows_ref.refs_1_ = bf16[384,2048]{1,0:T(8,128)(2,1)} async-done(((bf16[96,2048]{1,0:T(8,128)(2,1)}), bf16[384,2048]{1,0:T(8,128)(2,1)}) %all-gather.3.cloned.1.call-update) | async-done | bytes 1572880 | tf_op jit(solution)/shard_map/all_gather | solution.py:259
  63.1 1.4 copy-done.4
  64.5 0.0 all-gather.5.cloned.1.call-update
  64.6 0.0 reduce-scatter.5.cloned.1.call-start
  64.6 35.4 %all-gather.5.cloned.1.call-done.rows_ref = bf16[384,2048]{1,0:T(8,128)(2,1)} async-done(((bf16[96,2048]{1,0:T(8,128)(2,1)}), bf16[384,2048]{1,0:T(8,128)(2,1)}) %all-gather.5.cloned.1.call-update) | async-done | bytes 1572880 | tf_op jit(solution)/shard_map/all_gather | solution.py:259
  100.0 1.4 copy-done
  101.4 1.4 copy-done.2
  102.8 1.4 copy-done.8
  104.2 3.0 %expert_ffn.3 = bf16[384,2048]{1,0:T(8,128)(2,1)S(1)} custom-call(bf16[384,2048]{1,0:T(8,128)(2,1)S(1)} %copy-done.8, bf16[2048,384]{1,0:T(8,128)(2,1)S(1)} %copy-done, bf16[2048,384]{1,0:T(8,128)(2,1)S(1)} %collective-permute-done.1.refs_6_.in_b, bf16[384,2048]{1,0:T(8,128)(2,1)S(1)} %copy-done.2, bf16[384,2048]{1,0:T(8,128)(2,1)S(1)} %collective-permute-done.2.refs_7_.out_b), custom_call_target="tpu_custom_call" | custom-call | flops 2415919104 | bytes 9437184 | tf_op jit(solution)/shard_map/expert_ffn/pallas_call | solution.py:170
  107.3 1.1 copy-done.6
  108.4 0.0 reduce-scatter.5.cloned.1.call-update
  108.4 0.0 reduce-scatter.3.cloned.1.call-start
  108.5 0.0 copy-start.1
  108.5 1.4 copy-done.1
  109.9 1.4 copy-done.3
  111.3 1.4 copy-done.5
  112.7 3.0 %expert_ffn.2 = bf16[384,2048]{1,0:T(8,128)(2,1)S(1)} custom-call(bf16[384,2048]{1,0:T(8,128)(2,1)S(1)} %copy-done.5, bf16[2048,384]{1,0:T(8,128)(2,1)S(1)} %copy-done.1, bf16[2048,384]{1,0:T(8,128)(2,1)S(1)} %collective-permute-done.1.refs_6_.in_b, bf16[384,2048]{1,0:T(8,128)(2,1)S(1)} %copy-done.3, bf16[384,2048]{1,0:T(8,128)(2,1)S(1)} %collective-permute-done.2.refs_7_.out_b), custom_call_target="tpu_custom_call" | custom-call | flops 2415919104 | bytes 9437184 | tf_op jit(solution)/shard_map/expert_ffn/pallas_call | solution.py:170
  115.8 1.2 copy-done.7
  116.9 0.0 reduce-scatter.3.cloned.1.call-update
  117.0 25.8 %reduce-scatter.5.cloned.1.call-done = bf16[96,2048]{1,0:T(8,128)(2,1)} async-done(((bf16[384,2048]{1,0:T(8,128)(2,1)}), bf16[96,2048]{1,0:T(8,128)(2,1)}) %reduce-scatter.5.cloned.1.call-update) | async-done | bytes 393232 | tf_op jit(solution)/shard_map/reduce_scatter | solution.py:263
  142.7 2.4 %collective-permute-start.4 = (bf16[96,2048]{1,0:T(8,128)(2,1)}, bf16[96,2048]{1,0:T(8,128)(2,1)S(1)}, u32[]{:S(2)}, u32[]{:S(2)}) collective-permute-start(bf16[96,2048]{1,0:T(8,128)(2,1)} %reduce-scatter.5.cloned.1.call-done), channel_id=1, source_target_pairs={{0,8},{1,9},{2,10},{3,11},{4,12},{5,13},{6,14},{7,15},{8,0},{9,1},... | collective-permute-start | bytes 1179656 | tf_op jit(solution)/shard_map/ppermute | solution.py:224
  145.1 36.3 %reduce-scatter.3.cloned.1.call-done.refs_3_ = bf16[96,2048]{1,0:T(8,128)(2,1)} async-done(((bf16[384,2048]{1,0:T(8,128)(2,1)}), bf16[96,2048]{1,0:T(8,128)(2,1)}) %reduce-scatter.3.cloned.1.call-update) | async-done | bytes 393232 | tf_op jit(solution)/shard_map/reduce_scatter | solution.py:263
  181.4 0.0 collective-permute-done.4.refs_4_
  181.4 1.0 copy-done.13
  182.4 1.3 finish.1
  (21 shorter events, 0.0 us)
Async XLA Ops:
  6.5 56.6 %all-gather.3.cloned.1.call-start = ((), (), s32[]{:S(2)}) async-start(), calls=%async_computation.2 | async-start | bytes 1966080 | tf_op jit(solution)/shard_map/all_gather | solution.py:259
  6.5 11.1 %collective-permute-start.1 = (bf16[2048,384]{1,0:T(8,128)(2,1)}, bf16[2048,384]{1,0:T(8,128)(2,1)S(1)}, u32[]{:S(2)}, u32[]{:S(2)}) collective-permute-start(bf16[2048,384]{1,0:T(8,128)(2,1)} %in_a.3), channel_id=1, source_target_pairs={{0,1},{1,0},{2,3},{3,2},{4,5},{5,4},{6,7},{7,6},{8,9},{9,8},{10,11... | collective-permute-start | bytes 4718600 | tf_op jit(solution)/shard_map/ppermute | solution.py:220
  7.0 10.7 %collective-permute-start.2 = (bf16[384,2048]{1,0:T(8,128)(2,1)}, bf16[384,2048]{1,0:T(8,128)(2,1)S(1)}, u32[]{:S(2)}, u32[]{:S(2)}) collective-permute-start(bf16[384,2048]{1,0:T(8,128)(2,1)} %out_a.3), channel_id=1, source_target_pairs={{0,1},{1,0},{2,3},{3,2},{4,5},{5,4},{6,7},{7,6},{8,9},{9,8},{10,11... | collective-permute-start | bytes 4718600 | tf_op jit(solution)/shard_map/ppermute | solution.py:220
  8.1 9.6 %collective-permute-start = (bf16[64,2048]{1,0:T(8,128)(2,1)S(1)}, bf16[64,2048]{1,0:T(8,128)(2,1)}, u32[]{:S(2)}, u32[]{:S(2)}) collective-permute-start(bf16[64,2048]{1,0:T(8,128)(2,1)S(1)} %bitcast.12), channel_id=1, source_target_pairs={{0,16},{16,0},{1,17},{17,1},{2,18},{18,2},{3,19},{19,3},{4,20},{20... | collective-permute-start | bytes 786440 | tf_op jit(solution)/shard_map/ppermute | solution.py:230
  11.1 1.0 copy-start.11
  12.1 1.0 copy-start.12
  13.2 0.7 copy-start.15
  13.9 0.7 copy-start.16
  14.5 0.7 copy-start.17
  15.2 0.7 copy-start.18
  20.1 1.0 copy-start.9
  21.0 0.7 copy-start.14
  21.8 0.8 copy-start.19
  22.5 77.5 %all-gather.5.cloned.1.call-start = ((), (), s32[]{:S(2)}) async-start(), calls=%async_computation.4 | async-start | bytes 1966080 | tf_op jit(solution)/shard_map/all_gather | solution.py:259
  22.6 20.3 %collective-permute-start.3 = (bf16[96,2048]{1,0:T(8,128)(2,1)}, bf16[96,2048]{1,0:T(8,128)(2,1)}, u32[]{:S(2)}, u32[]{:S(2)}) collective-permute-start(bf16[96,2048]{1,0:T(8,128)(2,1)} %copy-done.19), channel_id=1, source_target_pairs={{0,8},{1,9},{2,10},{3,11},{4,12},{5,13},{6,14},{7,15},{8,0},{9,1},... | collective-permute-start | bytes 1179656 | tf_op jit(solution)/shard_map/ppermute | solution.py:224
  63.1 1.4 copy-start.4
  64.6 78.2 %reduce-scatter.5.cloned.1.call-start = ((), (), s32[]{:S(2)}) async-start(), calls=%async_computation.5 | async-start | bytes 1966080 | tf_op jit(solution)/shard_map/reduce_scatter | solution.py:263
  100.0 1.4 copy-start
  101.4 1.4 copy-start.2
  102.8 1.4 copy-start.8
  107.3 1.1 copy-start.6
  108.4 73.0 %reduce-scatter.3.cloned.1.call-start = ((), (), s32[]{:S(2)}) async-start(), calls=%async_computation.3 | async-start | bytes 1966080 | tf_op jit(solution)/shard_map/reduce_scatter | solution.py:263
  108.5 1.4 copy-start.1
  109.9 1.4 copy-start.3
  111.3 1.4 copy-start.5
  115.8 1.2 copy-start.7
  116.9 64.5 %copy-start.10 = (f32[128,2048]{1,0:T(8,128)S(1)}, f32[128,2048]{1,0:T(8,128)}, u32[]{:S(2)}) copy-start(f32[128,2048]{1,0:T(8,128)} %copy-done.9) | copy-start | bytes 3145732
  142.7 38.7 %collective-permute-start.4 = (bf16[96,2048]{1,0:T(8,128)(2,1)}, bf16[96,2048]{1,0:T(8,128)(2,1)S(1)}, u32[]{:S(2)}, u32[]{:S(2)}) collective-permute-start(bf16[96,2048]{1,0:T(8,128)(2,1)} %reduce-scatter.5.cloned.1.call-done), channel_id=1, source_target_pairs={{0,8},{1,9},{2,10},{3,11},{4,12},{5,13},{6,14},{7,15},{8,0},{9,1},... | collective-permute-start | bytes 1179656 | tf_op jit(solution)/shard_map/ppermute | solution.py:224
  181.4 1.0 copy-start.13
Sparse Core Ops, SparseCore 0:
  22.7 40.4 all-gather.2
  64.7 35.2 all-gather.4
  108.6 34.1 reduce-scatter.4
  144.9 36.4 reduce-scatter.2

commit v5 on v2

--- a/solution.py
+++ b/solution.py
@@ -12,6 +12,7 @@
 HD = 128
 WSPLIT = 8
 EPS = 1e-06
+RETURN_WEIGHT = 40_000_000_000
 VMEM_LIMIT = 32 * 1024 * 1024
 
 VMEM = pl.BlockSpec(memory_space=pltpu.VMEM)
@@ -84,17 +85,17 @@
     pass
 
 
-def after_all(value, others):
+def after_all(values, others=(), weight=1):
     return call(
         gate_kernel,
-        struct(value.shape),
-        [ANY] * (1 + len(others)),
+        [struct(value.shape) for value in values],
+        [ANY] * (len(values) + len(others)),
         "hand_on",
+        weight,
         1,
-        1,
-        out_specs=ANY,
-        aliases={0: 0},
-    )(value, *others)
+        out_specs=[ANY] * len(values),
+        aliases={i: i for i in range(len(values))},
+    )(*values, *others)
 
 
 def attend_kernel(pieces, groups, cap, *refs):
@@ -152,13 +153,12 @@
     )(state, query, gain, flat, *kv_pieces, *after)
 
 
-def ffn_kernel(parts, cut, *refs):
-    own_in, y_in, z_in = refs[:3]
-    d_in = refs[3 : 3 + parts]
-    in_a, in_b, out_a, out_b = refs[3 + parts : 7 + parts]
-    own_ref, z0_ref, y1_ref, y0_ref, z1_ref = refs[-5:]
+def ffn_kernel(cut, *refs):
+    own_in, y_in, z_in, d_left, d_right = refs[:5]
+    in_a, in_b, out_a, out_b = refs[5:9]
+    own_ref, z0_ref, y1y_ref, y1d_ref, y0_ref, z1_ref = refs[-6:]
     rows, width = own_in.shape
-    diagonal = jnp.concatenate([r[...] for r in d_in], axis=1)
+    diagonal = jnp.concatenate([d_left[...], d_right[...]], axis=1)
     entries = jnp.concatenate([own_in[...], y_in[...], z_in[...], diagonal], axis=0)
     w_in = jnp.concatenate([in_a[...], in_b[...]], axis=1)
     raw = jnp.dot(entries, w_in, preferred_element_type=jnp.float32)
@@ -178,35 +178,32 @@
         else:
             cols = slice(at - cut, at - cut + step)
             z1_ref[:, cols] = z_part
-            y1_ref[0, :, cols] = y_part
-            y1_ref[1, :, cols] = d_part
+            y1y_ref[:, cols] = y_part
+            y1d_ref[:, cols] = d_part
 
 
 def ffn(blocks, weights, cut, after=()):
     rows, width = blocks[0].shape
     units = weights[0].shape[1]
     rest = width - cut
-    outs = [
-        struct((rows, width)),
-        struct((2, rows, cut)),
-        struct((2, rows, rest)),
-        struct((rows, cut)),
-        struct((rows, rest)),
-    ]
-    return call(
-        functools.partial(ffn_kernel, len(blocks) - 3, cut),
+    outs = [struct((rows, width)), struct((2, rows, cut))]
+    outs += [struct((rows, size)) for size in (rest, rest, cut, rest)]
+    return call(
+        functools.partial(ffn_kernel, cut),
         outs,
-        [VMEM] * (len(blocks) + 4) + [ANY] * len(after),
+        [VMEM] * 9 + [ANY] * len(after),
         "expert_ffn",
         4 * 4 * rows * width * units * 2,
         8 * units * width + 16 * rows * width,
     )(*blocks, *weights, *after)
 
 
-def first_kernel(y0_ref, az_ref, z1_ref, ay_ref, *refs):
+def first_kernel(y0_ref, az_ref, z1_ref, ayd_ref, *refs):
     y_ref, z_ref = refs[-2:]
-    for own, other, out in ((y0_ref, az_ref, y_ref), (z1_ref, ay_ref, z_ref)):
-        out[...] = (own[...].astype(jnp.float32) + other[1].astype(jnp.float32)).astype(jnp.bfloat16)
+    for own, other, out in ((y0_ref, az_ref.at[1], y_ref), (z1_ref, ayd_ref, z_ref)):
+        out[...] = (own[...].astype(jnp.float32) + other[...].astype(jnp.float32)).astype(
+            jnp.bfloat16
+        )
 
 
 def first_step(y0, from_z, z1, from_y, after=()):
@@ -220,25 +217,26 @@
     )(y0, from_z, z1, from_y, *after)
 
 
-def total_kernel(cut, *refs):
-    own_ref, az_ref, ay_ref, by_ref, bz_ref = refs[:5]
-    out_ref = refs[7]
+def total_kernel(cut, held, *refs):
+    own_ref, az_ref, ayy_ref, by_ref, bz_ref = refs[:5]
+    out_ref = refs[5 + held]
     for first, second, cols in (
-        (az_ref, by_ref, slice(0, cut)),
-        (ay_ref, bz_ref, slice(cut, out_ref.shape[1])),
+        (az_ref.at[0], by_ref, slice(0, cut)),
+        (ayy_ref, bz_ref, slice(cut, out_ref.shape[1])),
     ):
         out_ref[:, cols] = (
             own_ref[:, cols].astype(jnp.float32)
-            + first[0].astype(jnp.float32)
+            + first[...].astype(jnp.float32)
             + second[...].astype(jnp.float32)
         ).astype(jnp.bfloat16)
 
 
 def total(sums, cut, held):
+    held = list(held)
     rows, width = sums[0].shape
     outs = [struct((rows, width))] + [struct(value.shape) for value in held]
     return call(
-        functools.partial(total_kernel, cut),
+        functools.partial(total_kernel, cut, len(held)),
         outs,
         [VMEM] * 5 + [ANY] * len(held),
         "far_total",
@@ -250,7 +248,7 @@
 
 
 def finish_kernel(groups, cap, cut, *refs):
-    hidden_ref, gate_ref, flat_ref, own_ref, az_ref, ay_ref, by_ref, bz_ref = refs[:8]
+    hidden_ref, gate_ref, flat_ref, own_ref, az_ref, ayy_ref, by_ref, bz_ref = refs[:8]
     back_refs = refs[8:-1]
     out_ref = refs[-1]
     tokens, width = hidden_ref.shape
@@ -266,10 +264,10 @@
         whole = slice(at, at + step)
         inner = at if at < cut else at - cut
         part = slice(inner, inner + step)
-        first, second = (az_ref, by_ref) if at < cut else (ay_ref, bz_ref)
+        first, second = (az_ref.at[0], by_ref) if at < cut else (ayy_ref, bz_ref)
         added = (
             own_ref[:, whole].astype(jnp.float32)
-            + first[0, :, part].astype(jnp.float32)
+            + first[:, part].astype(jnp.float32)
             + second[:, part].astype(jnp.float32)
         )
         coarse = added.astype(jnp.bfloat16)
@@ -302,6 +300,7 @@
     pipes = lax.axis_size("pipe")
     groups = devices // WSPLIT
     cap = 3 * tokens // (2 * groups)
+    half = width // 2
     far_cut, near_cut = width // 2, width // 4
 
     def across(value, bit):
@@ -338,34 +337,30 @@
     far = jnp.concatenate(far, axis=0) if len(far) > 1 else far[0]
 
     near_y, near_z = across(near, 2), across(near, 4)
-    near_blocks = [near, near_y, near_z, across(near_z, 2)]
-    far = after_all(far, [near_y, near_z])
+    (far,) = after_all([far], [near_y, near_z])
     far_y, far_z = across(far, 2), across(far, 4)
-    far_blocks = [
-        far,
-        far_y,
-        far_z,
-        across(far_y[:, :far_cut], 4),
-        across(far_z[:, far_cut:], 2),
-    ]
-
-    def first_sums(own, z0, y1, y0, z1, after=()):
-        from_z, from_y = across(z0, 4), across(y1, 2)
-        return own, from_z, from_y, *first_step(y0, from_z, z1, from_y, after)
+
+    def blocks(own, y, z):
+        return [own, y, z, across(y[:, :half], 4), across(z[:, half:], 2)]
+
+    def first_sums(own, z0, y1y, y1d, y0, z1, after=()):
+        from_z, from_yy, from_yd = across(z0, 4), across(y1y, 2), across(y1d, 2)
+        return own, from_z, from_yy, *first_step(y0, from_z, z1, from_yd, after)
 
     def last_sums(own, from_z, from_y, on_y, on_z):
         return own, from_z, from_y, across(on_y, 2), across(on_z, 4)
 
-    far_parts = ffn(far_blocks, weights, far_cut)
-    near_parts = ffn(near_blocks, weights, near_cut, after=far_parts[3:])
+    far_parts = ffn(blocks(far, far_y, far_z), weights, far_cut)
+    near_parts = ffn(blocks(near, near_y, near_z), weights, near_cut, after=far_parts[4:])
     far_sum, *held = total(
-        last_sums(*first_sums(*far_parts, after=near_parts[3:])), far_cut, near_parts[1:3]
+        last_sums(*first_sums(*far_parts, after=near_parts[4:])), far_cut, near_parts[1:4]
     )
     backs = [
         groups_on(far_sum[(count - 1) * cap : count * cap], groups - count)
         for count in range(1, groups)
     ]
-    near_sums = last_sums(*first_sums(near_parts[0], *held, *near_parts[3:]))
+    backs = after_all(backs, weight=RETURN_WEIGHT)
+    near_sums = last_sums(*first_sums(near_parts[0], *held, *near_parts[4:]))
     output = finish(hidden, gates, flat, near_sums, backs, groups, cap, near_cut)
     return output.reshape(1, 1, tokens, width)
 

time: 98.4 us -> 102 us (1.037)
  starting transfers between devices: 28.5 us -> 34.3 us
  waiting for transfers between devices: 53.2 us -> 50.6 us
    ppermute x2, waiting for transfers between devices: 19.9 us -> 14 us  [groups_on(): lax.ppermute(value, 'expert', [(i, (i + shift) % devices) for i in range(...]
    ppermute x17 -> x20, waiting for transfers between devices: 31.6 us -> 34.9 us  [across(): return lax.ppermute(value, 'expert', [(i, i ^ bit) for i in range(devices)])]
    ppermute x2, starting transfers between devices: 6.58 us -> 9.58 us  [groups_on(): lax.ppermute(value, 'expert', [(i, (i + shift) % devices) for i in range(...]
    ppermute x17 -> x20, starting transfers between devices: 18.9 us -> 21.8 us  [across(): return lax.ppermute(value, 'expert', [(i, i ^ bit) for i in range(devices)])]
    pallas_call x4 -> x5, Pallas kernels: 6.21 us -> 6.22 us  [the longest x2 6.07 us: ffn(): call(functools.partial(ffn_kernel, cut), outs, [VMEM] * 9 + [ANY] * len(a...]
  transfers between devices with their start and end apart: 20 -> 23, of which waited for: 14 -> 13; matrix products, arithmetic and copies ran while one was open for 1% -> 1% of each run, Pallas kernels for 6% -> 6%
where the time goes in v5:
time: 102 us; the launch traced here: 101 us
  waiting for transfers between devices  50.6 us (50%)
  starting transfers between devices  34.3 us (34%)
  Pallas kernels  10.3 us (10%)
  local copies, waits for them, and re-layouts  5.84 us (6%)
    ppermute x20, waiting for transfers between devices, across(): return lax.ppermute(value, 'expert', [(i, i ^ bit) for i in range(devices)])  34.9 us
    ppermute x20, starting transfers between devices, across(): return lax.ppermute(value, 'expert', [(i, i ^ bit) for i in range(devices)])  21.8 us
    ppermute x2, waiting for transfers between devices, groups_on(): lax.ppermute(value, 'expert', [(i, (i + shift) % devices) for i in range(...  14 us
    ppermute x2, starting transfers between devices, groups_on(): lax.ppermute(value, 'expert', [(i, (i + shift) % devices) for i in range(...  9.58 us
    pallas_call x2, Pallas kernels, ffn(): call(functools.partial(ffn_kernel, cut), outs, [VMEM] * 9 + [ANY] * len(a...  6.07 us
    unnamed x16, local copies, waits for them, and re-layouts  4.75 us
    ppermute x1, starting transfers between devices, body(): kv_pieces.append(lax.ppermute(kv, 'pipe', perm))  3 us
    pallas_call x1, Pallas kernels, attend(): call(functools.partial(attend_kernel, pieces, groups, cap), outs, [VMEM]...  2.38 us
  transfers between devices with their start and end apart: 23, of which 13 were waited for; matrix products, arithmetic and copies ran while one was open for 1% of the time, Pallas kernels for 6%

profile of v5, /device:TPU:0, one launch (start us, length us, event | category | flops | bytes accessed | tf_op | source)
XLA Modules:
  0.0 101.2 jit_solution(3091559301072313633)
XLA Ops:
  0.0 0.5 collective-permute-start.1
  0.5 1.0 %copy.15 = bf16[2,32,2048]{2,1,0:T(8,128)(2,1)S(1)} copy(bf16[2,32,2048]{2,0,1:T(2,128)(2,1)} %bitcast.20) | data formatting | bytes 524288 | tf_op jit(solution)/shard_map/transpose | solution.py:313
  1.5 3.0 %collective-permute-start = (bf16[64,2048]{1,0:T(8,128)(2,1)S(1)}, bf16[64,2048]{1,0:T(8,128)(2,1)}, u32[]{:S(2)}, u32[]{:S(2)}) collective-permute-start(bf16[64,2048]{1,0:T(8,128)(2,1)S(1)} %bitcast.12), channel_id=1, source_target_pairs={{0,16},{16,0},{1,17},{17,1},{2,18},{18,2},{3,19},{19,3},{4,20},{20... | collective-permute-start | bytes 786440 | tf_op jit(solution)/shard_map/ppermute | solution.py:317
  4.6 1.0 %copy-done = bf16[1,1,128,2048]{3,2,1,0:T(8,128)(2,1)S(1)} copy-done((bf16[1,1,128,2048]{3,2,1,0:T(8,128)(2,1)S(1)}, bf16[1,1,128,2048]{3,2,1,0:T(8,128)(2,1)}, u32[]{:S(2)}) %copy-start) | copy-done | bytes 524312
  5.6 1.0 %copy-done.1 = bf16[1,1,128,2048]{3,2,1,0:T(8,128)(2,1)S(1)} copy-done((bf16[1,1,128,2048]{3,2,1,0:T(8,128)(2,1)S(1)}, bf16[1,1,128,2048]{3,2,1,0:T(8,128)(2,1)}, u32[]{:S(2)}) %copy-start.1) | copy-done | bytes 524312
  6.6 0.7 copy-done.2
  7.3 0.7 copy-done.3
  8.0 0.7 copy-done.4
  8.6 0.7 copy-done.5
  9.3 0.1 stage.1
  9.4 1.7 %collective-permute-done.refs_5_ = bf16[64,2048]{1,0:T(8,128)(2,1)} collective-permute-done((bf16[64,2048]{1,0:T(8,128)(2,1)S(1)}, bf16[64,2048]{1,0:T(8,128)(2,1)}, u32[]{:S(2)}, u32[]{:S(2)}) %collective-permute-start) | collective-permute-done | bytes 262176 | tf_op jit(solution)/shard_map/ppermute | solution.py:317
  11.1 2.4 %attend.1 = (f32[128,2048]{1,0:T(8,128)S(1)}, bf16[96,2048]{1,0:T(8,128)(2,1)S(1)}, bf16[96,2048]{1,0:T(8,128)(2,1)S(1)}) custom-call(bf16[128,2048]{1,0:T(8,128)(2,1)S(1)} %get-tuple-element.34.refs_0_, bf16[128,2048]{1,0:T(8,128)(2,1)S(1)} %get-tuple-element.35.refs_1_, f32[1,2048]{1,0:T(1,128)S(1)} %get-tuple-element.36.refs_2_, ...), custom_call_target="tpu_custom_call" | custom-call | flops 134217728 | bytes 3145728 | tf_op jit(solution)/shard_map/attend/pallas_call | solution.py:146
  13.5 2.9 %collective-permute-start.7 = (bf16[96,2048]{1,0:T(8,128)(2,1)S(1)}, bf16[96,2048]{1,0:T(8,128)(2,1)S(1)}, u32[]{:S(2)}, u32[]{:S(2)}) collective-permute-start(bf16[96,2048]{1,0:T(8,128)(2,1)S(1)} %get-tuple-element.42), channel_id=1, source_target_pairs={{0,8},{1,9},{2,10},{3,11},{4,12},{5,13},{6,14},{7,15},{8,0},{9,1},... | collective-permute-start | bytes 1179656 | tf_op jit(solution)/shard_map/ppermute | solution.py:311
  16.4 1.6 %collective-permute-start.4 = (bf16[96,2048]{1,0:T(8,128)(2,1)S(1)}, bf16[96,2048]{1,0:T(8,128)(2,1)S(1)}, u32[]{:S(2)}, u32[]{:S(2)}) collective-permute-start(bf16[96,2048]{1,0:T(8,128)(2,1)S(1)} %get-tuple-element.41.refs_0_), channel_id=1, source_target_pairs={{0,4},{1,5},{2,6},{3,7},{4,0},{5,1},{6,2},{7,3},{8,12},{9,13},{10,... | collective-permute-start | bytes 1179656 | tf_op jit(solution)/shard_map/ppermute | solution.py:307
  18.0 1.5 %collective-permute-start.3 = (bf16[96,2048]{1,0:T(8,128)(2,1)S(1)}, bf16[96,2048]{1,0:T(8,128)(2,1)S(1)}, u32[]{:S(2)}, u32[]{:S(2)}) collective-permute-start(bf16[96,2048]{1,0:T(8,128)(2,1)S(1)} %get-tuple-element.41.refs_0_), channel_id=1, source_target_pairs={{0,2},{1,3},{2,0},{3,1},{4,6},{5,7},{6,4},{7,5},{8,10},{9,11},{10,... | collective-permute-start | bytes 1179656 | tf_op jit(solution)/shard_map/ppermute | solution.py:307
  19.5 14.0 %collective-permute-done.7.refs_0_ = bf16[96,2048]{1,0:T(8,128)(2,1)S(1)} collective-permute-done((bf16[96,2048]{1,0:T(8,128)(2,1)S(1)}, bf16[96,2048]{1,0:T(8,128)(2,1)S(1)}, u32[]{:S(2)}, u32[]{:S(2)}) %collective-permute-start.7) | collective-permute-done | bytes 393248 | tf_op jit(solution)/shard_map/ppermute | solution.py:311
  33.5 0.2 collective-permute-done.4.refs_2_
  33.7 1.4 %collective-permute-start.9 = (bf16[96,2048]{1,0:T(8,128)(2,1)S(1)}, bf16[96,2048]{1,0:T(8,128)(2,1)S(1)}, u32[]{:S(2)}, u32[]{:S(2)}) collective-permute-start(bf16[96,2048]{1,0:T(8,128)(2,1)S(1)} %hand_on.2.refs_0_), channel_id=1, source_target_pairs={{0,4},{1,5},{2,6},{3,7},{4,0},{5,1},{6,2},{7,3},{8,12},{9,13},{10,... | collective-permute-start | bytes 1179656 | tf_op jit(solution)/shard_map/ppermute | solution.py:307
  35.1 1.5 %collective-permute-start.8 = (bf16[96,2048]{1,0:T(8,128)(2,1)S(1)}, bf16[96,2048]{1,0:T(8,128)(2,1)S(1)}, u32[]{:S(2)}, u32[]{:S(2)}) collective-permute-start(bf16[96,2048]{1,0:T(8,128)(2,1)S(1)} %hand_on.2.refs_0_), channel_id=1, source_target_pairs={{0,2},{1,3},{2,0},{3,1},{4,6},{5,7},{6,4},{7,5},{8,10},{9,11},{10,... | collective-permute-start | bytes 1179656 | tf_op jit(solution)/shard_map/ppermute | solution.py:307
  36.6 7.0 %collective-permute-done.9.refs_2_ = bf16[96,2048]{1,0:T(8,128)(2,1)S(1)} collective-permute-done((bf16[96,2048]{1,0:T(8,128)(2,1)S(1)}, bf16[96,2048]{1,0:T(8,128)(2,1)S(1)}, u32[]{:S(2)}, u32[]{:S(2)}) %collective-permute-start.9) | collective-permute-done | bytes 393248 | tf_op jit(solution)/shard_map/ppermute | solution.py:307
  43.6 1.4 %collective-permute-start.11 = (bf16[96,1024]{1,0:T(8,128)(2,1)S(1)}, bf16[96,1024]{1,0:T(8,128)(2,1)S(1)}, u32[]{:S(2)}, u32[]{:S(2)}) collective-permute-start(bf16[96,1024]{1,0:T(8,128)(2,1)S(1)} %slice.19), channel_id=1, source_target_pairs={{0,2},{1,3},{2,0},{3,1},{4,6},{5,7},{6,4},{7,5},{8,10},{9,11},{10,... | collective-permute-start | bytes 589832 | tf_op jit(solution)/shard_map/ppermute | solution.py:307
  45.0 0.3 collective-permute-done.8.refs_1_
  45.4 1.4 %collective-permute-start.10 = (bf16[96,1024]{1,0:T(8,128)(2,1)S(1)}, bf16[96,1024]{1,0:T(8,128)(2,1)S(1)}, u32[]{:S(2)}, u32[]{:S(2)}) collective-permute-start(bf16[96,1024]{1,0:T(8,128)(2,1)S(1)} %slice.18), channel_id=1, source_target_pairs={{0,4},{1,5},{2,6},{3,7},{4,0},{5,1},{6,2},{7,3},{8,12},{9,13},{10,... | collective-permute-start | bytes 589832 | tf_op jit(solution)/shard_map/ppermute | solution.py:307
  46.8 0.6 collective-permute-start.6
  47.3 2.0 %collective-permute-start.5 = (bf16[96,1024]{1,0:T(8,128)(2,1)S(1)}, bf16[96,1024]{1,0:T(8,128)(2,1)S(1)}, u32[]{:S(2)}, u32[]{:S(2)}) collective-permute-start(bf16[96,1024]{1,0:T(8,128)(2,1)S(1)} %slice.16), channel_id=1, source_target_pairs={{0,4},{1,5},{2,6},{3,7},{4,0},{5,1},{6,2},{7,3},{8,12},{9,13},{10,... | collective-permute-start | bytes 589832 | tf_op jit(solution)/shard_map/ppermute | solution.py:307
  49.4 1.7 %collective-permute-done.11.refs_4_ = bf16[96,1024]{1,0:T(8,128)(2,1)S(1)} collective-permute-done((bf16[96,1024]{1,0:T(8,128)(2,1)S(1)}, bf16[96,1024]{1,0:T(8,128)(2,1)S(1)}, u32[]{:S(2)}, u32[]{:S(2)}) %collective-permute-start.11) | collective-permute-done | bytes 196640 | tf_op jit(solution)/shard_map/ppermute | solution.py:307
  51.1 0.6 collective-permute-done.10.refs_3_
  51.7 3.0 %expert_ffn.2 = (bf16[96,2048]{1,0:T(8,128)(2,1)S(1)}, bf16[2,96,1024]{2,1,0:T(8,128)(2,1)S(1)}, bf16[96,1024]{1,0:T(8,128)(2,1)S(1)}, bf16[96,1024]{1,0:T(8,128...) custom-call(bf16[96,2048]{1,0:T(8,128)(2,1)S(1)} %hand_on.2.refs_0_, ...), custom_call_target="tpu_custom_call" | custom-call | flops 2415919104 | bytes 9437184 | tf_op jit(solution)/shard_map/expert_ffn/pallas_call | solution.py:191
  54.7 1.8 %collective-permute-start.12 = (bf16[2,96,1024]{2,1,0:T(8,128)(2,1)S(1)}, bf16[2,96,1024]{2,1,0:T(8,128)(2,1)S(1)}, u32[]{:S(2)}, u32[]{:S(2)}) collective-permute-start(bf16[2,96,1024]{2,1,0:T(8,128)(2,1)S(1)} %get-tuple-element.47), channel_id=1, source_target_pairs={{0,4},{1,5},{2,6},{3,7},{4,0},{5,1},{6,2},{7,3},{8,12},{9,13},{10,... | collective-permute-start | bytes 1179656 | tf_op jit(solution)/shard_map/ppermute | solution.py:307
  56.5 0.5 collective-permute-start.13
  57.0 1.5 %collective-permute-start.14 = (bf16[96,1024]{1,0:T(8,128)(2,1)S(1)}, bf16[96,1024]{1,0:T(8,128)(2,1)S(1)}, u32[]{:S(2)}, u32[]{:S(2)}) collective-permute-start(bf16[96,1024]{1,0:T(8,128)(2,1)S(1)} %get-tuple-element.49), channel_id=1, source_target_pairs={{0,2},{1,3},{2,0},{3,1},{4,6},{5,7},{6,4},{7,5},{8,10},{9,11},{10,... | collective-permute-start | bytes 589832 | tf_op jit(solution)/shard_map/ppermute | solution.py:307
  58.6 3.0 %expert_ffn.3 = (bf16[96,2048]{1,0:T(8,128)(2,1)S(1)}, bf16[2,96,512]{2,1,0:T(8,128)(2,1)S(1)}, bf16[96,1536]{1,0:T(8,128)(2,1)S(1)}, bf16[96,1536]{1,0:T(8,128)...) custom-call(bf16[96,2048]{1,0:T(8,128)(2,1)S(1)} %get-tuple-element.41.refs_0_, ...), custom_call_target="tpu_custom_call" | custom-call | flops 2415919104 | bytes 9437184 | tf_op jit(solution)/shard_map/expert_ffn/pallas_call | solution.py:191
  61.6 4.8 %collective-permute-done.14.ayd_ref = bf16[96,1024]{1,0:T(8,128)(2,1)S(1)} collective-permute-done((bf16[96,1024]{1,0:T(8,128)(2,1)S(1)}, bf16[96,1024]{1,0:T(8,128)(2,1)S(1)}, u32[]{:S(2)}, u32[]{:S(2)}) %collective-permute-start.14) | collective-permute-done | bytes 196640 | tf_op jit(solution)/shard_map/ppermute | solution.py:307
  66.5 0.6 collective-permute-start.15
  67.1 1.2 %collective-permute-start.16 = (bf16[96,1024]{1,0:T(8,128)(2,1)S(1)}, bf16[96,1024]{1,0:T(8,128)(2,1)S(1)}, u32[]{:S(2)}, u32[]{:S(2)}) collective-permute-start(bf16[96,1024]{1,0:T(8,128)(2,1)S(1)} %get-tuple-element.53), channel_id=1, source_target_pairs={{0,4},{1,5},{2,6},{3,7},{4,0},{5,1},{6,2},{7,3},{8,12},{9,13},{10,... | collective-permute-start | bytes 589832 | tf_op jit(solution)/shard_map/ppermute | solution.py:307
  68.2 4.0 %collective-permute-done.15.refs_3_ = bf16[96,1024]{1,0:T(8,128)(2,1)S(1)} collective-permute-done((bf16[96,1024]{1,0:T(8,128)(2,1)S(1)}, bf16[96,1024]{1,0:T(8,128)(2,1)S(1)}, u32[]{:S(2)}, u32[]{:S(2)}) %collective-permute-start.15) | collective-permute-done | bytes 196640 | tf_op jit(solution)/shard_map/ppermute | solution.py:307
  72.2 0.6 collective-permute-done.16.refs_4_
  72.9 0.1 far_total.1
  73.0 6.7 %collective-permute-start.22 = (bf16[96,2048]{1,0:T(8,128)(2,1)S(1)}, bf16[96,2048]{1,0:T(8,128)(2,1)S(1)}, u32[]{:S(2)}, u32[]{:S(2)}) collective-permute-start(bf16[96,2048]{1,0:T(8,128)(2,1)S(1)} %get-tuple-element.62), channel_id=1, source_target_pairs={{0,8},{1,9},{2,10},{3,11},{4,12},{5,13},{6,14},{7,15},{8,0},{9,1},... | collective-permute-start | bytes 1179656 | tf_op jit(solution)/shard_map/ppermute | solution.py:311
  79.7 1.5 %collective-permute-start.19 = (bf16[96,1536]{1,0:T(8,128)(2,1)S(1)}, bf16[96,1536]{1,0:T(8,128)(2,1)S(1)}, u32[]{:S(2)}, u32[]{:S(2)}) collective-permute-start(bf16[96,1536]{1,0:T(8,128)(2,1)S(1)} %get-tuple-element.59), channel_id=1, source_target_pairs={{0,2},{1,3},{2,0},{3,1},{4,6},{5,7},{6,4},{7,5},{8,10},{9,11},{10,... | collective-permute-start | bytes 884744 | tf_op jit(solution)/shard_map/ppermute | solution.py:307
  81.2 0.2 collective-permute-start.17
  81.4 0.9 collective-permute-start.18
  82.3 10.1 %collective-permute-done.17.az_ref.refs_4_ = bf16[2,96,512]{2,1,0:T(8,128)(2,1)S(1)} collective-permute-done((bf16[2,96,512]{2,1,0:T(8,128)(2,1)S(1)}, bf16[2,96,512]{2,1,0:T(8,128)(2,1)S(1)}, u32[]{:S(2)}, u32[]{:S(2)}) %collective-permute-start.17) | collective-permute-done | bytes 196640 | tf_op jit(solution)/shard_map/ppermute | solution.py:307
  92.6 0.5 collective-permute-start.20
  93.1 1.2 %collective-permute-start.21 = (bf16[96,1536]{1,0:T(8,128)(2,1)S(1)}, bf16[96,1536]{1,0:T(8,128)(2,1)S(1)}, u32[]{:S(2)}, u32[]{:S(2)}) collective-permute-start(bf16[96,1536]{1,0:T(8,128)(2,1)S(1)} %get-tuple-element.61), channel_id=1, source_target_pairs={{0,4},{1,5},{2,6},{3,7},{4,0},{5,1},{6,2},{7,3},{8,12},{9,13},{10,... | collective-permute-start | bytes 884744 | tf_op jit(solution)/shard_map/ppermute | solution.py:307
  94.2 3.0 %collective-permute-done.20.refs_6_ = bf16[96,512]{1,0:T(8,128)(2,1)S(1)} collective-permute-done((bf16[96,512]{1,0:T(8,128)(2,1)S(1)}, bf16[96,512]{1,0:T(8,128)(2,1)S(1)}, u32[]{:S(2)}, u32[]{:S(2)}) %collective-permute-start.20) | collective-permute-done | bytes 98336 | tf_op jit(solution)/shard_map/ppermute | solution.py:307
  97.2 2.5 %collective-permute-done.21.refs_7_ = bf16[96,1536]{1,0:T(8,128)(2,1)S(1)} collective-permute-done((bf16[96,1536]{1,0:T(8,128)(2,1)S(1)}, bf16[96,1536]{1,0:T(8,128)(2,1)S(1)}, u32[]{:S(2)}, u32[]{:S(2)}) %collective-permute-start.21) | collective-permute-done | bytes 294944 | tf_op jit(solution)/shard_map/ppermute | solution.py:307
  99.8 1.4 %finish.1 = bf16[128,2048]{1,0:T(8,128)(2,1)} custom-call(f32[128,2048]{1,0:T(8,128)S(1)} %get-tuple-element.38.refs_0_, f32[128,1]{1,0:T(8,128)S(1)} %get-tuple-element.39.refs_1_, s32[128,1]{1,0:T(8,128)S(1)} %get-tuple-element.40.refs_2_, bf16[96,2048]{1,0:T(8,128)(2,1)S(1)} %get-tuple-element.45.refs_3_, ...), custom_call_target="tpu_custom_call" | custom-call | flops 301989888 | bytes 4194304 | tf_op jit(solution)/shard_map/finish/pallas_call | solution.py:287
  (29 shorter events, 0.3 us)
Async XLA Ops:
  0.0 11.1 %collective-permute-start.1 = (bf16[2048,384]{1,0:T(8,128)(2,1)}, bf16[2048,384]{1,0:T(8,128)(2,1)S(1)}, u32[]{:S(2)}, u32[]{:S(2)}) collective-permute-start(bf16[2048,384]{1,0:T(8,128)(2,1)} %refs_5_.3), channel_id=1, source_target_pairs={{0,1},{1,0},{2,3},{3,2},{4,5},{5,4},{6,7},{7,6},{8,9},{9,8},{10,11... | collective-permute-start | bytes 4718600 | tf_op jit(solution)/shard_map/ppermute | solution.py:307
  0.5 10.7 %collective-permute-start.2 = (bf16[384,2048]{1,0:T(8,128)(2,1)}, bf16[384,2048]{1,0:T(8,128)(2,1)S(1)}, u32[]{:S(2)}, u32[]{:S(2)}) collective-permute-start(bf16[384,2048]{1,0:T(8,128)(2,1)} %refs_7_.3), channel_id=1, source_target_pairs={{0,1},{1,0},{2,3},{3,2},{4,5},{5,4},{6,7},{7,6},{8,9},{9,8},{10,11... | collective-permute-start | bytes 4718600 | tf_op jit(solution)/shard_map/ppermute | solution.py:307
  1.5 9.6 %collective-permute-start = (bf16[64,2048]{1,0:T(8,128)(2,1)S(1)}, bf16[64,2048]{1,0:T(8,128)(2,1)}, u32[]{:S(2)}, u32[]{:S(2)}) collective-permute-start(bf16[64,2048]{1,0:T(8,128)(2,1)S(1)} %bitcast.12), channel_id=1, source_target_pairs={{0,16},{16,0},{1,17},{17,1},{2,18},{18,2},{3,19},{19,3},{4,20},{20... | collective-permute-start | bytes 786440 | tf_op jit(solution)/shard_map/ppermute | solution.py:317
  4.5 1.0 %copy-start = (bf16[1,1,128,2048]{3,2,1,0:T(8,128)(2,1)S(1)}, bf16[1,1,128,2048]{3,2,1,0:T(8,128)(2,1)}, u32[]{:S(2)}) copy-start(bf16[1,1,128,2048]{3,2,1,0:T(8,128)(2,1)} %param.9) | copy-start | bytes 1572868
  5.6 1.0 %copy-start.1 = (bf16[1,1,128,2048]{3,2,1,0:T(8,128)(2,1)S(1)}, bf16[1,1,128,2048]{3,2,1,0:T(8,128)(2,1)}, u32[]{:S(2)}) copy-start(bf16[1,1,128,2048]{3,2,1,0:T(8,128)(2,1)} %param.10) | copy-start | bytes 1572868
  6.6 0.7 copy-start.2
  7.3 0.7 copy-start.3
  8.0 0.7 copy-start.4
  8.6 0.7 copy-start.5
  13.5 20.0 %collective-permute-start.7 = (bf16[96,2048]{1,0:T(8,128)(2,1)S(1)}, bf16[96,2048]{1,0:T(8,128)(2,1)S(1)}, u32[]{:S(2)}, u32[]{:S(2)}) collective-permute-start(bf16[96,2048]{1,0:T(8,128)(2,1)S(1)} %get-tuple-element.42), channel_id=1, source_target_pairs={{0,8},{1,9},{2,10},{3,11},{4,12},{5,13},{6,14},{7,15},{8,0},{9,1},... | collective-permute-start | bytes 1179656 | tf_op jit(solution)/shard_map/ppermute | solution.py:311
  16.4 35.2 %copy-start.7 = (bf16[384,2048]{1,0:T(8,128)(2,1)S(1)}, bf16[384,2048]{1,0:T(8,128)(2,1)}, u32[]{:S(2)}) copy-start(bf16[384,2048]{1,0:T(8,128)(2,1)} %refs_7_.3) | copy-start | bytes 4718596
  16.4 35.2 %copy-start.6 = (bf16[2048,384]{1,0:T(8,128)(2,1)S(1)}, bf16[2048,384]{1,0:T(8,128)(2,1)}, u32[]{:S(2)}) copy-start(bf16[2048,384]{1,0:T(8,128)(2,1)} %refs_5_.3) | copy-start | bytes 4718596
  16.4 17.3 %collective-permute-start.4 = (bf16[96,2048]{1,0:T(8,128)(2,1)S(1)}, bf16[96,2048]{1,0:T(8,128)(2,1)S(1)}, u32[]{:S(2)}, u32[]{:S(2)}) collective-permute-start(bf16[96,2048]{1,0:T(8,128)(2,1)S(1)} %get-tuple-element.41.refs_0_), channel_id=1, source_target_pairs={{0,4},{1,5},{2,6},{3,7},{4,0},{5,1},{6,2},{7,3},{8,12},{9,13},{10,... | collective-permute-start | bytes 1179656 | tf_op jit(solution)/shard_map/ppermute | solution.py:307
  18.0 15.7 %collective-permute-start.3 = (bf16[96,2048]{1,0:T(8,128)(2,1)S(1)}, bf16[96,2048]{1,0:T(8,128)(2,1)S(1)}, u32[]{:S(2)}, u32[]{:S(2)}) collective-permute-start(bf16[96,2048]{1,0:T(8,128)(2,1)S(1)} %get-tuple-element.41.refs_0_), channel_id=1, source_target_pairs={{0,2},{1,3},{2,0},{3,1},{4,6},{5,7},{6,4},{7,5},{8,10},{9,11},{10,... | collective-permute-start | bytes 1179656 | tf_op jit(solution)/shard_map/ppermute | solution.py:307
  33.7 9.8 %collective-permute-start.9 = (bf16[96,2048]{1,0:T(8,128)(2,1)S(1)}, bf16[96,2048]{1,0:T(8,128)(2,1)S(1)}, u32[]{:S(2)}, u32[]{:S(2)}) collective-permute-start(bf16[96,2048]{1,0:T(8,128)(2,1)S(1)} %hand_on.2.refs_0_), channel_id=1, source_target_pairs={{0,4},{1,5},{2,6},{3,7},{4,0},{5,1},{6,2},{7,3},{8,12},{9,13},{10,... | collective-permute-start | bytes 1179656 | tf_op jit(solution)/shard_map/ppermute | solution.py:307
  35.1 10.3 %collective-permute-start.8 = (bf16[96,2048]{1,0:T(8,128)(2,1)S(1)}, bf16[96,2048]{1,0:T(8,128)(2,1)S(1)}, u32[]{:S(2)}, u32[]{:S(2)}) collective-permute-start(bf16[96,2048]{1,0:T(8,128)(2,1)S(1)} %hand_on.2.refs_0_), channel_id=1, source_target_pairs={{0,2},{1,3},{2,0},{3,1},{4,6},{5,7},{6,4},{7,5},{8,10},{9,11},{10,... | collective-permute-start | bytes 1179656 | tf_op jit(solution)/shard_map/ppermute | solution.py:307
  43.6 7.5 %collective-permute-start.11 = (bf16[96,1024]{1,0:T(8,128)(2,1)S(1)}, bf16[96,1024]{1,0:T(8,128)(2,1)S(1)}, u32[]{:S(2)}, u32[]{:S(2)}) collective-permute-start(bf16[96,1024]{1,0:T(8,128)(2,1)S(1)} %slice.19), channel_id=1, source_target_pairs={{0,2},{1,3},{2,0},{3,1},{4,6},{5,7},{6,4},{7,5},{8,10},{9,11},{10,... | collective-permute-start | bytes 589832 | tf_op jit(solution)/shard_map/ppermute | solution.py:307
  45.4 6.3 %collective-permute-start.10 = (bf16[96,1024]{1,0:T(8,128)(2,1)S(1)}, bf16[96,1024]{1,0:T(8,128)(2,1)S(1)}, u32[]{:S(2)}, u32[]{:S(2)}) collective-permute-start(bf16[96,1024]{1,0:T(8,128)(2,1)S(1)} %slice.18), channel_id=1, source_target_pairs={{0,4},{1,5},{2,6},{3,7},{4,0},{5,1},{6,2},{7,3},{8,12},{9,13},{10,... | collective-permute-start | bytes 589832 | tf_op jit(solution)/shard_map/ppermute | solution.py:307
  46.8 11.8 %collective-permute-start.6 = (bf16[96,1024]{1,0:T(8,128)(2,1)S(1)}, bf16[96,1024]{1,0:T(8,128)(2,1)S(1)}, u32[]{:S(2)}, u32[]{:S(2)}) collective-permute-start(bf16[96,1024]{1,0:T(8,128)(2,1)S(1)} %slice.17), channel_id=1, source_target_pairs={{0,2},{1,3},{2,0},{3,1},{4,6},{5,7},{6,4},{7,5},{8,10},{9,11},{10,... | collective-permute-start | bytes 589832 | tf_op jit(solution)/shard_map/ppermute | solution.py:307
  47.3 11.2 %collective-permute-start.5 = (bf16[96,1024]{1,0:T(8,128)(2,1)S(1)}, bf16[96,1024]{1,0:T(8,128)(2,1)S(1)}, u32[]{:S(2)}, u32[]{:S(2)}) collective-permute-start(bf16[96,1024]{1,0:T(8,128)(2,1)S(1)} %slice.16), channel_id=1, source_target_pairs={{0,4},{1,5},{2,6},{3,7},{4,0},{5,1},{6,2},{7,3},{8,12},{9,13},{10,... | collective-permute-start | bytes 589832 | tf_op jit(solution)/shard_map/ppermute | solution.py:307
  54.7 11.7 %collective-permute-start.12 = (bf16[2,96,1024]{2,1,0:T(8,128)(2,1)S(1)}, bf16[2,96,1024]{2,1,0:T(8,128)(2,1)S(1)}, u32[]{:S(2)}, u32[]{:S(2)}) collective-permute-start(bf16[2,96,1024]{2,1,0:T(8,128)(2,1)S(1)} %get-tuple-element.47), channel_id=1, source_target_pairs={{0,4},{1,5},{2,6},{3,7},{4,0},{5,1},{6,2},{7,3},{8,12},{9,13},{10,... | collective-permute-start | bytes 1179656 | tf_op jit(solution)/shard_map/ppermute | solution.py:307
  56.5 11.7 %collective-permute-start.13 = (bf16[96,1024]{1,0:T(8,128)(2,1)S(1)}, bf16[96,1024]{1,0:T(8,128)(2,1)S(1)}, u32[]{:S(2)}, u32[]{:S(2)}) collective-permute-start(bf16[96,1024]{1,0:T(8,128)(2,1)S(1)} %get-tuple-element.48), channel_id=1, source_target_pairs={{0,2},{1,3},{2,0},{3,1},{4,6},{5,7},{6,4},{7,5},{8,10},{9,11},{10,... | collective-permute-start | bytes 589832 | tf_op jit(solution)/shard_map/ppermute | solution.py:307
  57.0 9.4 %collective-permute-start.14 = (bf16[96,1024]{1,0:T(8,128)(2,1)S(1)}, bf16[96,1024]{1,0:T(8,128)(2,1)S(1)}, u32[]{:S(2)}, u32[]{:S(2)}) collective-permute-start(bf16[96,1024]{1,0:T(8,128)(2,1)S(1)} %get-tuple-element.49), channel_id=1, source_target_pairs={{0,2},{1,3},{2,0},{3,1},{4,6},{5,7},{6,4},{7,5},{8,10},{9,11},{10,... | collective-permute-start | bytes 589832 | tf_op jit(solution)/shard_map/ppermute | solution.py:307
  66.5 5.7 %collective-permute-start.15 = (bf16[96,1024]{1,0:T(8,128)(2,1)S(1)}, bf16[96,1024]{1,0:T(8,128)(2,1)S(1)}, u32[]{:S(2)}, u32[]{:S(2)}) collective-permute-start(bf16[96,1024]{1,0:T(8,128)(2,1)S(1)} %get-tuple-element.52), channel_id=1, source_target_pairs={{0,2},{1,3},{2,0},{3,1},{4,6},{5,7},{6,4},{7,5},{8,10},{9,11},{10,... | collective-permute-start | bytes 589832 | tf_op jit(solution)/shard_map/ppermute | solution.py:307
  67.1 5.8 %collective-permute-start.16 = (bf16[96,1024]{1,0:T(8,128)(2,1)S(1)}, bf16[96,1024]{1,0:T(8,128)(2,1)S(1)}, u32[]{:S(2)}, u32[]{:S(2)}) collective-permute-start(bf16[96,1024]{1,0:T(8,128)(2,1)S(1)} %get-tuple-element.53), channel_id=1, source_target_pairs={{0,4},{1,5},{2,6},{3,7},{4,0},{5,1},{6,2},{7,3},{8,12},{9,13},{10,... | collective-permute-start | bytes 589832 | tf_op jit(solution)/shard_map/ppermute | solution.py:307
  73.0 21.2 %collective-permute-start.22 = (bf16[96,2048]{1,0:T(8,128)(2,1)S(1)}, bf16[96,2048]{1,0:T(8,128)(2,1)S(1)}, u32[]{:S(2)}, u32[]{:S(2)}) collective-permute-start(bf16[96,2048]{1,0:T(8,128)(2,1)S(1)} %get-tuple-element.62), channel_id=1, source_target_pairs={{0,8},{1,9},{2,10},{3,11},{4,12},{5,13},{6,14},{7,15},{8,0},{9,1},... | collective-permute-start | bytes 1179656 | tf_op jit(solution)/shard_map/ppermute | solution.py:311
  79.7 12.8 %collective-permute-start.19 = (bf16[96,1536]{1,0:T(8,128)(2,1)S(1)}, bf16[96,1536]{1,0:T(8,128)(2,1)S(1)}, u32[]{:S(2)}, u32[]{:S(2)}) collective-permute-start(bf16[96,1536]{1,0:T(8,128)(2,1)S(1)} %get-tuple-element.59), channel_id=1, source_target_pairs={{0,2},{1,3},{2,0},{3,1},{4,6},{5,7},{6,4},{7,5},{8,10},{9,11},{10,... | collective-permute-start | bytes 884744 | tf_op jit(solution)/shard_map/ppermute | solution.py:307
  81.2 11.2 %collective-permute-start.17 = (bf16[2,96,512]{2,1,0:T(8,128)(2,1)S(1)}, bf16[2,96,512]{2,1,0:T(8,128)(2,1)S(1)}, u32[]{:S(2)}, u32[]{:S(2)}) collective-permute-start(bf16[2,96,512]{2,1,0:T(8,128)(2,1)S(1)} %get-tuple-element.57), channel_id=1, source_target_pairs={{0,4},{1,5},{2,6},{3,7},{4,0},{5,1},{6,2},{7,3},{8,12},{9,13},{10,... | collective-permute-start | bytes 589832 | tf_op jit(solution)/shard_map/ppermute | solution.py:307
  81.4 12.8 %collective-permute-start.18 = (bf16[96,1536]{1,0:T(8,128)(2,1)S(1)}, bf16[96,1536]{1,0:T(8,128)(2,1)S(1)}, u32[]{:S(2)}, u32[]{:S(2)}) collective-permute-start(bf16[96,1536]{1,0:T(8,128)(2,1)S(1)} %get-tuple-element.58), channel_id=1, source_target_pairs={{0,2},{1,3},{2,0},{3,1},{4,6},{5,7},{6,4},{7,5},{8,10},{9,11},{10,... | collective-permute-start | bytes 884744 | tf_op jit(solution)/shard_map/ppermute | solution.py:307
  92.6 4.7 %collective-permute-start.20 = (bf16[96,512]{1,0:T(8,128)(2,1)S(1)}, bf16[96,512]{1,0:T(8,128)(2,1)S(1)}, u32[]{:S(2)}, u32[]{:S(2)}) collective-permute-start(bf16[96,512]{1,0:T(8,128)(2,1)S(1)} %get-tuple-element.60), channel_id=1, source_target_pairs={{0,2},{1,3},{2,0},{3,1},{4,6},{5,7},{6,4},{7,5},{8,10},{9,11},{10,... | collective-permute-start | bytes 294920 | tf_op jit(solution)/shard_map/ppermute | solution.py:307
  93.1 6.7 %collective-permute-start.21 = (bf16[96,1536]{1,0:T(8,128)(2,1)S(1)}, bf16[96,1536]{1,0:T(8,128)(2,1)S(1)}, u32[]{:S(2)}, u32[]{:S(2)}) collective-permute-start(bf16[96,1536]{1,0:T(8,128)(2,1)S(1)} %get-tuple-element.61), channel_id=1, source_target_pairs={{0,4},{1,5},{2,6},{3,7},{4,0},{5,1},{6,2},{7,3},{8,12},{9,13},{10,... | collective-permute-start | bytes 884744 | tf_op jit(solution)/shard_map/ppermute | solution.py:307

commit v6 on v4

--- a/solution.py
+++ b/solution.py
@@ -39,10 +39,7 @@
 
 
 def as_column(row):
-    count = row.shape[1]
-    down = lax.broadcasted_iota(jnp.int32, (count, count), 0)
-    along = lax.broadcasted_iota(jnp.int32, (count, count), 1)
-    return jnp.sum(jnp.where(down == along, row, jnp.zeros_like(row)), axis=1, keepdims=True)
+    return jnp.transpose(jnp.broadcast_to(row, (8, row.shape[1])))[:, :1]
 
 
 def stage_kernel(groups, cap, *refs):
@@ -112,17 +109,22 @@
         values = jnp.concatenate([r[local:, cols] for r in kv_refs], axis=0)
         scores = (
             lax.dot_general(
+                keys,
                 query_ref[:, cols],
-                keys,
                 (((1,), (1,)), ((), ())),
                 preferred_element_type=jnp.float32,
             )
             * scale
         )
-        raised = jnp.exp(scores - jnp.max(scores, axis=1, keepdims=True))
-        total = jnp.sum(raised, axis=1, keepdims=True)
-        mixed = jnp.dot(raised.astype(jnp.bfloat16), values, preferred_element_type=jnp.float32)
-        hidden = state_ref[:, cols].astype(jnp.float32) + mixed / total
+        raised = jnp.exp(scores - jnp.max(scores, axis=0, keepdims=True))
+        total = jnp.sum(raised, axis=0, keepdims=True)
+        mixed = lax.dot_general(
+            raised.astype(jnp.bfloat16),
+            values,
+            (((0,), (0,)), ((), ())),
+            preferred_element_type=jnp.float32,
+        )
+        hidden = state_ref[:, cols].astype(jnp.float32) + mixed * as_column(1.0 / total)
         hidden_ref[:, cols] = hidden
         squares = squares + hidden * hidden
     mean_square = jnp.sum(squares, axis=1, keepdims=True) * (1.0 / width)
@@ -152,53 +154,126 @@
     )(state, query, gain, flat, *kv_pieces, *after)
 
 
-def ffn_kernel(rows_ref, in_a, in_b, out_a, out_b, out_ref):
+def ffn_kernel(counts, cut, *refs):
+    blocks = []
+    for count in counts:
+        parts, refs = refs[:count], refs[count:]
+        blocks.append(jnp.concatenate([r[...] for r in parts], axis=1))
+    in_a, in_b, out_a, out_b = refs[:4]
+    own_ref, zd_ref, yd_ref, zz_ref, yy_ref, y0_ref, z1_ref = refs[-7:]
+    rows, width = blocks[0].shape
+    entries = jnp.concatenate(blocks, axis=0)
     w_in = jnp.concatenate([in_a[...], in_b[...]], axis=1)
-    raw = jnp.dot(rows_ref[...], w_in, preferred_element_type=jnp.float32)
+    raw = jnp.dot(entries, w_in, preferred_element_type=jnp.float32)
     activation = jnp.maximum(raw, 0.0).astype(jnp.bfloat16)
     step = 512
-    for at in range(0, out_ref.shape[1], step):
+    for at in range(0, width, step):
         cols = slice(at, at + step)
         w_out = jnp.concatenate([out_a[:, cols], out_b[:, cols]], axis=0)
         part = jnp.dot(activation, w_out, preferred_element_type=jnp.float32)
-        out_ref[:, cols] = part.astype(jnp.bfloat16)
-
-
-def ffn(rows, weights):
-    count, width = rows.shape
-    units = weights[0].shape[1]
-    return call(
-        ffn_kernel,
-        struct((count, width)),
-        [VMEM] * 5,
+        part = part.astype(jnp.bfloat16)
+        own_ref[:, cols] = part[:rows]
+        y_part, z_part, d_part = (part[i * rows : (i + 1) * rows] for i in (1, 2, 3))
+        if at < cut:
+            y0_ref[:, cols] = y_part
+            zz_ref[:, cols] = z_part
+            zd_ref[:, cols] = d_part
+        else:
+            cols = slice(at - cut, at - cut + step)
+            z1_ref[:, cols] = z_part
+            yy_ref[:, cols] = y_part
+            yd_ref[:, cols] = d_part
+
+
+def ffn(blocks, weights, cut, after=()):
+    rows = blocks[0][0].shape[0]
+    width, units = weights[0].shape
+    rest = width - cut
+    outs = [struct((rows, size)) for size in (width, cut, rest, cut, rest, cut, rest)]
+    counts = [len(parts) for parts in blocks]
+    return call(
+        functools.partial(ffn_kernel, counts, cut),
+        outs,
+        [VMEM] * (sum(counts) + 4) + [ANY] * len(after),
         "expert_ffn",
-        4 * count * width * units * 2,
-        8 * units * width + 4 * count * width,
-    )(rows, *weights)
+        4 * 4 * rows * width * units * 2,
+        8 * units * width + 16 * rows * width,
+    )(*sum(blocks, []), *weights, *after)
+
+
+def first_kernel(y0_ref, zd_ref, z1_ref, yd_ref, y_ref, z_ref):
+    for own, other, out in ((y0_ref, zd_ref, y_ref), (z1_ref, yd_ref, z_ref)):
+        out[...] = (own[...].astype(jnp.float32) + other[...].astype(jnp.float32)).astype(
+            jnp.bfloat16
+        )
+
+
+def first_step(y0, from_zd, z1, from_yd):
+    return call(
+        first_kernel,
+        [struct(y0.shape), struct(z1.shape)],
+        [VMEM] * 4,
+        "first_step",
+        y0.size + z1.size,
+        6 * (y0.size + z1.size),
+    )(y0, from_zd, z1, from_yd)
+
+
+def add_up(own_ref, zz_ref, yy_ref, by_ref, bz_ref, cols):
+    cut = zz_ref.shape[1]
+    whole = slice(*cols)
+    if cols[0] < cut:
+        first, second, part = zz_ref, by_ref, whole
+    else:
+        first, second, part = yy_ref, bz_ref, slice(cols[0] - cut, cols[1] - cut)
+    return (
+        own_ref[:, whole].astype(jnp.float32)
+        + first[:, part].astype(jnp.float32)
+        + second[:, part].astype(jnp.float32)
+    ).astype(jnp.bfloat16)
+
+
+def total_kernel(held, *refs):
+    out_ref = refs[5 + held]
+    for at in range(0, out_ref.shape[1], 512):
+        out_ref[:, at : at + 512] = add_up(*refs[:5], (at, at + 512))
+
+
+def total(sums, held):
+    rows, width = sums[0].shape
+    outs = [struct((rows, width))] + [struct(value.shape) for value in held]
+    return call(
+        functools.partial(total_kernel, len(held)),
+        outs,
+        [VMEM] * 5 + [ANY] * len(held),
+        "far_total",
+        3 * rows * width,
+        8 * rows * width,
+        out_specs=[VMEM] + [ANY] * len(held),
+        aliases={5 + i: 1 + i for i in range(len(held))},
+    )(*sums, *held)
 
 
 def finish_kernel(groups, cap, *refs):
     hidden_ref, gate_ref, flat_ref = refs[:3]
-    sum_refs = refs[3:-1]
+    sums = refs[3:8]
+    back_refs = refs[8:-1]
     out_ref = refs[-1]
     tokens, width = hidden_ref.shape
-    flat = flat_ref[...]
+    slots = lax.broadcasted_iota(jnp.int32, (tokens, groups * cap), 1)
+    picker = (slots == flat_ref[...]).astype(jnp.float32).astype(jnp.bfloat16)
     step = 512
     for at in range(0, width, step):
         cols = slice(at, at + step)
-        picked = jnp.zeros((tokens, step), jnp.float32)
-        for group in range(groups):
-            slots = lax.broadcasted_iota(jnp.int32, (tokens, cap), 1) + group * cap
-            picker = (slots == flat).astype(jnp.float32).astype(jnp.bfloat16)
-            picked = picked + jnp.dot(
-                picker, sum_refs[group][:, cols], preferred_element_type=jnp.float32
-            )
+        near = add_up(*sums, (at, at + step))
+        found = jnp.concatenate([near] + [r[:, cols] for r in back_refs], axis=0)
+        picked = jnp.dot(picker, found, preferred_element_type=jnp.float32)
         out_ref[:, cols] = (hidden_ref[:, cols] + gate_ref[...] * picked).astype(jnp.bfloat16)
 
 
-def finish(hidden, gate, flat, sums, groups, cap):
+def finish(hidden, gate, flat, sums, backs, groups, cap):
     tokens, width = hidden.shape
-    operands = [hidden, gate, flat, *sums]
+    operands = [hidden, gate, flat, *sums, *backs]
     return call(
         functools.partial(finish_kernel, groups, cap),
         struct((tokens, width)),
@@ -215,6 +290,8 @@
     pipes = lax.axis_size("pipe")
     groups = devices // WSPLIT
     cap = 3 * tokens // (2 * groups)
+    half = width // 2
+    far_cut, near_cut = width // 2, width // 4
 
     def across(value, bit):
         return lax.ppermute(value, "expert", [(i, i ^ bit) for i in range(devices)])
@@ -249,33 +326,40 @@
     far = [groups_on(block, count) for count, block in enumerate(packed, 1)]
     far = jnp.concatenate(far, axis=0) if len(far) > 1 else far[0]
 
-    squares = [
-        [base + core + 2 * chip for chip in range(WSPLIT // 2)]
-        for base in range(0, devices, WSPLIT)
-        for core in range(2)
+    near_y, near_z = across(near, 2), across(near, 4)
+    near_blocks = [[near], [near_y], [near_z], [across(near_z, 2)]]
+    (far,) = after_all([far], [near_y, near_z])
+    left, right = far[:, :half], far[:, half:]
+    y_left, z_right = across(left, 2), across(right, 4)
+    y_right, z_left = across(right, 2), across(left, 4)
+    far_blocks = [
+        [far],
+        [y_left, y_right],
+        [z_left, z_right],
+        [across(y_left, 4), across(z_right, 2)],
     ]
 
-    def spread(rows):
-        return lax.all_gather(rows, "expert", axis_index_groups=squares, axis=0, tiled=True)
-
-    def experts(spread):
-        partial_value = ffn(spread, weights)
-        return lax.psum_scatter(
-            partial_value,
-            "expert",
-            scatter_dimension=0,
-            axis_index_groups=squares,
-            tiled=True,
-        )
-
-    near = spread(near)
-    far = spread(*after_all([far], [near]))
-    near_sum, far_sum = experts(near), experts(far)
+    far_own, far_zd, far_yd, far_zz, far_yy, far_y0, far_z1 = ffn(far_blocks, weights, far_cut)
+    near_own, *near_sent, near_y0, near_z1 = ffn(
+        near_blocks, weights, near_cut, after=[far_y0, far_z1]
+    )
+    from_zd, from_yd = across(far_zd, 4), across(far_yd, 2)
+    far_zz, far_yy = after_all([far_zz, far_yy], [near_y0])
+    from_zz, from_yy = across(far_zz, 4), across(far_yy, 2)
+    on_y, on_z = first_step(far_y0, from_zd, far_z1, from_yd)
+    far_sum, *near_sent = total(
+        [far_own, from_zz, from_yy, across(on_y, 2), across(on_z, 4)], near_sent
+    )
     backs = [
         groups_on(far_sum[(count - 1) * cap : count * cap], groups - count)
         for count in range(1, groups)
     ]
-    output = finish(hidden, gates, flat, [near_sum, *backs], groups, cap)
+    from_zd, from_yd, from_zz, from_yy = (
+        across(value, bit) for value, bit in zip(near_sent, (4, 2, 4, 2))
+    )
+    on_y, on_z = first_step(near_y0, from_zd, near_z1, from_yd)
+    near_sums = [near_own, from_zz, from_yy, across(on_y, 2), across(on_z, 4)]
+    output = finish(hidden, gates, flat, near_sums, backs, groups, cap)
     return output.reshape(1, 1, tokens, width)
 
 

time: 191 us -> 99.5 us (0.52)
  waiting for transfers between devices: 137 us -> 49 us
  starting transfers between devices: 8.92 us -> 31.1 us
  local copies, waits for them, and re-layouts: 21.4 us -> 5.81 us
  between operations: 13.2 us -> 0.11 us
  Pallas kernels: 9.84 us -> 13.2 us
    reduce_scatter x2 -> x0, waiting for transfers between devices: 62 us -> none  [experts(): lax.psum_scatter(partial_value, 'expert', scatter_dimension=0, axis_index...]
    all_gather x2 -> x0, waiting for transfers between devices: 55.6 us -> none  [spread(): lax.all_gather(rows, 'expert', axis_index_groups=squares, axis=0, tiled=T...]
    ppermute x2 -> x23, waiting for transfers between devices: 0.01 us -> 33.3 us  [across(): return lax.ppermute(value, 'expert', [(i, i ^ bit) for i in range(devices)])]
    ppermute x2 -> x23, starting transfers between devices: 0.51 us -> 24.7 us  [across(): return lax.ppermute(value, 'expert', [(i, i ^ bit) for i in range(devices)])]
    unnamed x40 -> x16, local copies, waits for them, and re-layouts: 20.4 us -> 4.75 us
    ppermute x2, waiting for transfers between devices: 17.4 us -> 14 us  [groups_on(): lax.ppermute(value, 'expert', [(i, (i + shift) % devices) for i in range(...]
    pallas_call x1, Pallas kernels: 2.38 us -> 5.51 us  [attend(): call(functools.partial(attend_kernel, pieces, groups, cap), outs, [VMEM]...]
    pallas_call x2 -> x5, Pallas kernels: 6.06 us -> 6.4 us  [the longest x2 6.07 us: ffn(): call(functools.partial(ffn_kernel, counts, cut), outs, [VMEM] * (sum(coun...]
  transfers between devices with their start and end apart: 9 -> 26, of which waited for: 6 -> 14; matrix products, arithmetic and copies ran while one was open for 1% -> 1% of each run, Pallas kernels for 2% -> 6%
where the time goes in v6:
time: 99.5 us; the launch traced here: 99.2 us
  waiting for transfers between devices  49 us (49%)
  starting transfers between devices  31.1 us (31%)
  Pallas kernels  13.2 us (13%)
  local copies, waits for them, and re-layouts  5.81 us (6%)
    ppermute x23, waiting for transfers between devices, across(): return lax.ppermute(value, 'expert', [(i, i ^ bit) for i in range(devices)])  33.3 us
    ppermute x23, starting transfers between devices, across(): return lax.ppermute(value, 'expert', [(i, i ^ bit) for i in range(devices)])  24.7 us
    ppermute x2, waiting for transfers between devices, groups_on(): lax.ppermute(value, 'expert', [(i, (i + shift) % devices) for i in range(...  14 us
    pallas_call x2, Pallas kernels, ffn(): call(functools.partial(ffn_kernel, counts, cut), outs, [VMEM] * (sum(coun...  6.07 us
    pallas_call x1, Pallas kernels, attend(): call(functools.partial(attend_kernel, pieces, groups, cap), outs, [VMEM]...  5.51 us
    unnamed x16, local copies, waits for them, and re-layouts  4.75 us
    ppermute x2, starting transfers between devices, groups_on(): lax.ppermute(value, 'expert', [(i, (i + shift) % devices) for i in range(...  3.38 us
    ppermute x1, starting transfers between devices, body(): kv_pieces.append(lax.ppermute(kv, 'pipe', perm))  3 us
  transfers between devices with their start and end apart: 26, of which 14 were waited for; matrix products, arithmetic and copies ran while one was open for 1% of the time, Pallas kernels for 6%

profile of v6, /device:TPU:0, one launch (start us, length us, event | category | flops | bytes accessed | tf_op | source)
XLA Modules:
  0.0 99.2 jit_solution(15588984675433039514)
XLA Ops:
  0.5 1.0 %copy.17 = bf16[2,32,2048]{2,1,0:T(8,128)(2,1)S(1)} copy(bf16[2,32,2048]{2,0,1:T(2,128)(2,1)} %bitcast.20) | data formatting | bytes 524288 | tf_op jit(solution)/shard_map/transpose | solution.py:303
  1.5 3.0 %collective-permute-start = (bf16[64,2048]{1,0:T(8,128)(2,1)S(1)}, bf16[64,2048]{1,0:T(8,128)(2,1)}, u32[]{:S(2)}, u32[]{:S(2)}) collective-permute-start(bf16[64,2048]{1,0:T(8,128)(2,1)S(1)} %bitcast.12), channel_id=1, source_target_pairs={{0,16},{16,0},{1,17},{17,1},{2,18},{18,2},{3,19},{19,3},{4,20},{20... | collective-permute-start | bytes 786440 | tf_op jit(solution)/shard_map/ppermute | solution.py:307
  4.6 1.0 %copy-done = bf16[1,1,128,2048]{3,2,1,0:T(8,128)(2,1)S(1)} copy-done((bf16[1,1,128,2048]{3,2,1,0:T(8,128)(2,1)S(1)}, bf16[1,1,128,2048]{3,2,1,0:T(8,128)(2,1)}, u32[]{:S(2)}) %copy-start) | copy-done | bytes 524312
  5.6 1.0 %copy-done.1 = bf16[1,1,128,2048]{3,2,1,0:T(8,128)(2,1)S(1)} copy-done((bf16[1,1,128,2048]{3,2,1,0:T(8,128)(2,1)S(1)}, bf16[1,1,128,2048]{3,2,1,0:T(8,128)(2,1)}, u32[]{:S(2)}) %copy-start.1) | copy-done | bytes 524312
  6.6 0.7 copy-done.2
  7.3 0.7 copy-done.3
  8.0 0.7 copy-done.4
  8.6 0.7 copy-done.5
  9.4 1.7 %collective-permute-done.refs_5_ = bf16[64,2048]{1,0:T(8,128)(2,1)} collective-permute-done((bf16[64,2048]{1,0:T(8,128)(2,1)S(1)}, bf16[64,2048]{1,0:T(8,128)(2,1)}, u32[]{:S(2)}, u32[]{:S(2)}) %collective-permute-start) | collective-permute-done | bytes 262176 | tf_op jit(solution)/shard_map/ppermute | solution.py:307
  11.1 5.5 %attend.1 = (f32[128,2048]{1,0:T(8,128)S(1)}, bf16[96,2048]{1,0:T(8,128)(2,1)S(1)}, bf16[96,2048]{1,0:T(8,128)(2,1)S(1)}) custom-call(bf16[128,2048]{1,0:T(8,128)(2,1)S(1)} %get-tuple-element.39.refs_0_, bf16[128,2048]{1,0:T(8,128)(2,1)S(1)} %get-tuple-element.40.refs_1_, f32[1,2048]{1,0:T(1,128)S(1)} %get-tuple-element.41.refs_2_, ...), custom_call_target="tpu_custom_call" | custom-call | flops 134217728 | bytes 3145728 | tf_op jit(solution)/shard_map/attend/pallas_call | solution.py:147
  16.7 2.9 %collective-permute-start.6 = (bf16[96,2048]{1,0:T(8,128)(2,1)S(1)}, bf16[96,2048]{1,0:T(8,128)(2,1)S(1)}, u32[]{:S(2)}, u32[]{:S(2)}) collective-permute-start(bf16[96,2048]{1,0:T(8,128)(2,1)S(1)} %get-tuple-element.47), channel_id=1, source_target_pairs={{0,8},{1,9},{2,10},{3,11},{4,12},{5,13},{6,14},{7,15},{8,0},{9,1},... | collective-permute-start | bytes 1179656 | tf_op jit(solution)/shard_map/ppermute | solution.py:301
  19.6 1.6 %collective-permute-start.4 = (bf16[96,2048]{1,0:T(8,128)(2,1)S(1)}, bf16[96,2048]{1,0:T(8,128)(2,1)S(1)}, u32[]{:S(2)}, u32[]{:S(2)}) collective-permute-start(bf16[96,2048]{1,0:T(8,128)(2,1)S(1)} %get-tuple-element.46.refs_0_), channel_id=1, source_target_pairs={{0,4},{1,5},{2,6},{3,7},{4,0},{5,1},{6,2},{7,3},{8,12},{9,13},{10,... | collective-permute-start | bytes 1179656 | tf_op jit(solution)/shard_map/ppermute | solution.py:297
  21.2 1.5 %collective-permute-start.3 = (bf16[96,2048]{1,0:T(8,128)(2,1)S(1)}, bf16[96,2048]{1,0:T(8,128)(2,1)S(1)}, u32[]{:S(2)}, u32[]{:S(2)}) collective-permute-start(bf16[96,2048]{1,0:T(8,128)(2,1)S(1)} %get-tuple-element.46.refs_0_), channel_id=1, source_target_pairs={{0,2},{1,3},{2,0},{3,1},{4,6},{5,7},{6,4},{7,5},{8,10},{9,11},{10,... | collective-permute-start | bytes 1179656 | tf_op jit(solution)/shard_map/ppermute | solution.py:297
  22.7 14.0 %collective-permute-done.6.refs_0_ = bf16[96,2048]{1,0:T(8,128)(2,1)S(1)} collective-permute-done((bf16[96,2048]{1,0:T(8,128)(2,1)S(1)}, bf16[96,2048]{1,0:T(8,128)(2,1)S(1)}, u32[]{:S(2)}, u32[]{:S(2)}) %collective-permute-start.6) | collective-permute-done | bytes 393248 | tf_op jit(solution)/shard_map/ppermute | solution.py:301
  36.9 1.4 %collective-permute-start.10 = (bf16[96,1024]{1,0:T(8,128)(2,1)S(1)}, bf16[96,1024]{1,0:T(8,128)(2,1)S(1)}, u32[]{:S(2)}, u32[]{:S(2)}) collective-permute-start(bf16[96,1024]{1,0:T(8,128)(2,1)S(1)} %get-tuple-element.73), channel_id=1, source_target_pairs={{0,4},{1,5},{2,6},{3,7},{4,0},{5,1},{6,2},{7,3},{8,12},{9,13},{10,... | collective-permute-start | bytes 589832 | tf_op jit(solution)/shard_map/ppermute | solution.py:297
  38.3 1.5 %collective-permute-start.7 = (bf16[96,1024]{1,0:T(8,128)(2,1)S(1)}, bf16[96,1024]{1,0:T(8,128)(2,1)S(1)}, u32[]{:S(2)}, u32[]{:S(2)}) collective-permute-start(bf16[96,1024]{1,0:T(8,128)(2,1)S(1)} %get-tuple-element.74), channel_id=1, source_target_pairs={{0,2},{1,3},{2,0},{3,1},{4,6},{5,7},{6,4},{7,5},{8,10},{9,11},{10,... | collective-permute-start | bytes 589832 | tf_op jit(solution)/shard_map/ppermute | solution.py:297
  39.8 0.5 collective-permute-start.8
  40.3 0.7 collective-permute-start.9
  41.0 3.2 %collective-permute-done.10.refs_4_ = bf16[96,1024]{1,0:T(8,128)(2,1)S(1)} collective-permute-done((bf16[96,1024]{1,0:T(8,128)(2,1)S(1)}, bf16[96,1024]{1,0:T(8,128)(2,1)S(1)}, u32[]{:S(2)}, u32[]{:S(2)}) %collective-permute-start.10) | collective-permute-done | bytes 196640 | tf_op jit(solution)/shard_map/ppermute | solution.py:297
  44.3 1.4 %collective-permute-start.12 = (bf16[96,1024]{1,0:T(8,128)(2,1)S(1)}, bf16[96,1024]{1,0:T(8,128)(2,1)S(1)}, u32[]{:S(2)}, u32[]{:S(2)}) collective-permute-start(bf16[96,1024]{1,0:T(8,128)(2,1)S(1)} %collective-permute-done.10.refs_4_), channel_id=1, source_target_pairs={{0,2},{1,3},{2,0},{3,1},{4,6},{5,7},{6,4},{7,5},{8,10},{9,11},{10,... | collective-permute-start | bytes 589832 | tf_op jit(solution)/shard_map/ppermute | solution.py:297
  45.6 0.5 collective-permute-done.7.refs_1_
  46.2 1.5 %collective-permute-start.11 = (bf16[96,1024]{1,0:T(8,128)(2,1)S(1)}, bf16[96,1024]{1,0:T(8,128)(2,1)S(1)}, u32[]{:S(2)}, u32[]{:S(2)}) collective-permute-start(bf16[96,1024]{1,0:T(8,128)(2,1)S(1)} %collective-permute-done.7.refs_1_), channel_id=1, source_target_pairs={{0,4},{1,5},{2,6},{3,7},{4,0},{5,1},{6,2},{7,3},{8,12},{9,13},{10,... | collective-permute-start | bytes 589832 | tf_op jit(solution)/shard_map/ppermute | solution.py:297
  47.7 0.6 collective-permute-start.5
  48.3 2.1 %collective-permute-done.8.refs_2_ = bf16[96,1024]{1,0:T(8,128)(2,1)S(1)} collective-permute-done((bf16[96,1024]{1,0:T(8,128)(2,1)S(1)}, bf16[96,1024]{1,0:T(8,128)(2,1)S(1)}, u32[]{:S(2)}, u32[]{:S(2)}) %collective-permute-start.8) | collective-permute-done | bytes 196640 | tf_op jit(solution)/shard_map/ppermute | solution.py:297
  50.4 4.2 %collective-permute-done.12.refs_6_ = bf16[96,1024]{1,0:T(8,128)(2,1)S(1)} collective-permute-done((bf16[96,1024]{1,0:T(8,128)(2,1)S(1)}, bf16[96,1024]{1,0:T(8,128)(2,1)S(1)}, u32[]{:S(2)}, u32[]{:S(2)}) %collective-permute-start.12) | collective-permute-done | bytes 196640 | tf_op jit(solution)/shard_map/ppermute | solution.py:297
  54.6 3.0 %expert_ffn.2 = (bf16[96,2048]{1,0:T(8,128)(2,1)S(1)}, bf16[96,1024]{1,0:T(8,128)(2,1)S(1)}, bf16[96,1024]{1,0:T(8,128)(2,1)S(1)}, bf16[96,1024]{1,0:T(8,128)(2,...) custom-call(bf16[96,2048]{1,0:T(8,128)(2,1)S(1)} %hand_on.2.refs_0_, ...), custom_call_target="tpu_custom_call" | custom-call | flops 2415919104 | bytes 9437184 | tf_op jit(solution)/shard_map/expert_ffn/pallas_call | solution.py:194
  57.6 0.7 collective-permute-start.15
  58.4 1.4 %collective-permute-start.16 = (bf16[96,1024]{1,0:T(8,128)(2,1)S(1)}, bf16[96,1024]{1,0:T(8,128)(2,1)S(1)}, u32[]{:S(2)}, u32[]{:S(2)}) collective-permute-start(bf16[96,1024]{1,0:T(8,128)(2,1)S(1)} %get-tuple-element.58), channel_id=1, source_target_pairs={{0,2},{1,3},{2,0},{3,1},{4,6},{5,7},{6,4},{7,5},{8,10},{9,11},{10,... | collective-permute-start | bytes 589832 | tf_op jit(solution)/shard_map/ppermute | solution.py:297
  59.8 2.9 %collective-permute-done.5.refs_3_ = bf16[96,2048]{1,0:T(8,128)(2,1)S(1)} collective-permute-done((bf16[96,2048]{1,0:T(8,128)(2,1)S(1)}, bf16[96,2048]{1,0:T(8,128)(2,1)S(1)}, u32[]{:S(2)}, u32[]{:S(2)}) %collective-permute-start.5) | collective-permute-done | bytes 393248 | tf_op jit(solution)/shard_map/ppermute | solution.py:297
  62.8 3.0 %expert_ffn.3 = (bf16[96,2048]{1,0:T(8,128)(2,1)S(1)}, bf16[96,512]{1,0:T(8,128)(2,1)S(1)}, bf16[96,1536]{1,0:T(8,128)(2,1)S(1)}, bf16[96,512]{1,0:T(8,128)(2,1)...) custom-call(bf16[96,2048]{1,0:T(8,128)(2,1)S(1)} %get-tuple-element.46.refs_0_, ...), custom_call_target="tpu_custom_call" | custom-call | flops 2415919104 | bytes 9437184 | tf_op jit(solution)/shard_map/expert_ffn/pallas_call | solution.py:194
  65.8 0.5 collective-permute-start.13
  66.3 1.4 %collective-permute-start.14 = (bf16[96,1024]{1,0:T(8,128)(2,1)S(1)}, bf16[96,1024]{1,0:T(8,128)(2,1)S(1)}, u32[]{:S(2)}, u32[]{:S(2)}) collective-permute-start(bf16[96,1024]{1,0:T(8,128)(2,1)S(1)} %get-tuple-element.56), channel_id=1, source_target_pairs={{0,2},{1,3},{2,0},{3,1},{4,6},{5,7},{6,4},{7,5},{8,10},{9,11},{10,... | collective-permute-start | bytes 589832 | tf_op jit(solution)/shard_map/ppermute | solution.py:297
  67.9 0.7 collective-permute-start.17
  68.5 1.6 %collective-permute-start.18 = (bf16[96,1024]{1,0:T(8,128)(2,1)S(1)}, bf16[96,1024]{1,0:T(8,128)(2,1)S(1)}, u32[]{:S(2)}, u32[]{:S(2)}) collective-permute-start(bf16[96,1024]{1,0:T(8,128)(2,1)S(1)} %get-tuple-element.60), channel_id=1, source_target_pairs={{0,4},{1,5},{2,6},{3,7},{4,0},{5,1},{6,2},{7,3},{8,12},{9,13},{10,... | collective-permute-start | bytes 589832 | tf_op jit(solution)/shard_map/ppermute | solution.py:297
  70.1 1.4 %collective-permute-done.13.refs_1_ = bf16[96,1024]{1,0:T(8,128)(2,1)S(1)} collective-permute-done((bf16[96,1024]{1,0:T(8,128)(2,1)S(1)}, bf16[96,1024]{1,0:T(8,128)(2,1)S(1)}, u32[]{:S(2)}, u32[]{:S(2)}) %collective-permute-start.13) | collective-permute-done | bytes 196640 | tf_op jit(solution)/shard_map/ppermute | solution.py:297
  71.6 0.7 collective-permute-done.14.refs_2_
  72.3 4.2 %collective-permute-done.17.refs_3_ = bf16[96,1024]{1,0:T(8,128)(2,1)S(1)} collective-permute-done((bf16[96,1024]{1,0:T(8,128)(2,1)S(1)}, bf16[96,1024]{1,0:T(8,128)(2,1)S(1)}, u32[]{:S(2)}, u32[]{:S(2)}) %collective-permute-start.17) | collective-permute-done | bytes 196640 | tf_op jit(solution)/shard_map/ppermute | solution.py:297
  76.6 1.4 %collective-permute-start.22 = (bf16[96,1536]{1,0:T(8,128)(2,1)S(1)}, bf16[96,1536]{1,0:T(8,128)(2,1)S(1)}, u32[]{:S(2)}, u32[]{:S(2)}) collective-permute-start(bf16[96,1536]{1,0:T(8,128)(2,1)S(1)} %get-tuple-element.69), channel_id=1, source_target_pairs={{0,2},{1,3},{2,0},{3,1},{4,6},{5,7},{6,4},{7,5},{8,10},{9,11},{10,... | collective-permute-start | bytes 884744 | tf_op jit(solution)/shard_map/ppermute | solution.py:297
  78.0 2.0 %collective-permute-start.21 = (bf16[96,512]{1,0:T(8,128)(2,1)S(1)}, bf16[96,512]{1,0:T(8,128)(2,1)S(1)}, u32[]{:S(2)}, u32[]{:S(2)}) collective-permute-start(bf16[96,512]{1,0:T(8,128)(2,1)S(1)} %get-tuple-element.67), channel_id=1, source_target_pairs={{0,4},{1,5},{2,6},{3,7},{4,0},{5,1},{6,2},{7,3},{8,12},{9,13},{10,... | collective-permute-start | bytes 294920 | tf_op jit(solution)/shard_map/ppermute | solution.py:297
  80.0 0.5 collective-permute-start.25
  80.5 0.5 collective-permute-start.20
  81.0 4.1 %collective-permute-done.21.zd_ref = bf16[96,512]{1,0:T(8,128)(2,1)S(1)} collective-permute-done((bf16[96,512]{1,0:T(8,128)(2,1)S(1)}, bf16[96,512]{1,0:T(8,128)(2,1)S(1)}, u32[]{:S(2)}, u32[]{:S(2)}) %collective-permute-start.21) | collective-permute-done | bytes 98336 | tf_op jit(solution)/shard_map/ppermute | solution.py:297
  85.2 1.3 %collective-permute-done.22.yd_ref = bf16[96,1536]{1,0:T(8,128)(2,1)S(1)} collective-permute-done((bf16[96,1536]{1,0:T(8,128)(2,1)S(1)}, bf16[96,1536]{1,0:T(8,128)(2,1)S(1)}, u32[]{:S(2)}, u32[]{:S(2)}) %collective-permute-start.22) | collective-permute-done | bytes 294944 | tf_op jit(solution)/shard_map/ppermute | solution.py:297
  86.6 1.0 collective-permute-start.24
  87.6 1.1 %collective-permute-start.19 = (bf16[96,512]{1,0:T(8,128)(2,1)S(1)}, bf16[96,512]{1,0:T(8,128)(2,1)S(1)}, u32[]{:S(2)}, u32[]{:S(2)}) collective-permute-start(bf16[96,512]{1,0:T(8,128)(2,1)S(1)} %get-tuple-element.65), channel_id=1, source_target_pairs={{0,4},{1,5},{2,6},{3,7},{4,0},{5,1},{6,2},{7,3},{8,12},{9,13},{10,... | collective-permute-start | bytes 294920 | tf_op jit(solution)/shard_map/ppermute | solution.py:297
  88.7 1.1 %collective-permute-start.23 = (bf16[96,512]{1,0:T(8,128)(2,1)S(1)}, bf16[96,512]{1,0:T(8,128)(2,1)S(1)}, u32[]{:S(2)}, u32[]{:S(2)}) collective-permute-start(bf16[96,512]{1,0:T(8,128)(2,1)S(1)} %get-tuple-element.70), channel_id=1, source_target_pairs={{0,2},{1,3},{2,0},{3,1},{4,6},{5,7},{6,4},{7,5},{8,10},{9,11},{10,... | collective-permute-start | bytes 294920 | tf_op jit(solution)/shard_map/ppermute | solution.py:297
  89.8 8.2 %collective-permute-done.19.refs_4_ = bf16[96,512]{1,0:T(8,128)(2,1)S(1)} collective-permute-done((bf16[96,512]{1,0:T(8,128)(2,1)S(1)}, bf16[96,512]{1,0:T(8,128)(2,1)S(1)}, u32[]{:S(2)}, u32[]{:S(2)}) %collective-permute-start.19) | collective-permute-done | bytes 98336 | tf_op jit(solution)/shard_map/ppermute | solution.py:297
  98.0 1.1 %finish.1 = bf16[128,2048]{1,0:T(8,128)(2,1)} custom-call(f32[128,2048]{1,0:T(8,128)S(1)} %get-tuple-element.43.refs_0_, f32[128,1]{1,0:T(8,128)S(1)} %get-tuple-element.44.refs_1_, s32[128,1]{1,0:T(8,128)S(1)} %get-tuple-element.45.refs_2_, bf16[96,2048]{1,0:T(8,128)(2,1)S(1)} %get-tuple-element.50.refs_3_, ...), custom_call_target="tpu_custom_call" | custom-call | flops 201326592 | bytes 4194304 | tf_op jit(solution)/shard_map/finish/pallas_call | solution.py:277
  (32 shorter events, 1.2 us)
Async XLA Ops:
  0.0 11.1 %collective-permute-start.1 = (bf16[2048,384]{1,0:T(8,128)(2,1)}, bf16[2048,384]{1,0:T(8,128)(2,1)S(1)}, u32[]{:S(2)}, u32[]{:S(2)}) collective-permute-start(bf16[2048,384]{1,0:T(8,128)(2,1)} %refs_4_.1), channel_id=1, source_target_pairs={{0,1},{1,0},{2,3},{3,2},{4,5},{5,4},{6,7},{7,6},{8,9},{9,8},{10,11... | collective-permute-start | bytes 4718600 | tf_op jit(solution)/shard_map/ppermute | solution.py:297
  0.5 10.7 %collective-permute-start.2 = (bf16[384,2048]{1,0:T(8,128)(2,1)}, bf16[384,2048]{1,0:T(8,128)(2,1)S(1)}, u32[]{:S(2)}, u32[]{:S(2)}) collective-permute-start(bf16[384,2048]{1,0:T(8,128)(2,1)} %refs_6_.1), channel_id=1, source_target_pairs={{0,1},{1,0},{2,3},{3,2},{4,5},{5,4},{6,7},{7,6},{8,9},{9,8},{10,11... | collective-permute-start | bytes 4718600 | tf_op jit(solution)/shard_map/ppermute | solution.py:297
  1.5 9.6 %collective-permute-start = (bf16[64,2048]{1,0:T(8,128)(2,1)S(1)}, bf16[64,2048]{1,0:T(8,128)(2,1)}, u32[]{:S(2)}, u32[]{:S(2)}) collective-permute-start(bf16[64,2048]{1,0:T(8,128)(2,1)S(1)} %bitcast.12), channel_id=1, source_target_pairs={{0,16},{16,0},{1,17},{17,1},{2,18},{18,2},{3,19},{19,3},{4,20},{20... | collective-permute-start | bytes 786440 | tf_op jit(solution)/shard_map/ppermute | solution.py:307
  4.5 1.0 %copy-start = (bf16[1,1,128,2048]{3,2,1,0:T(8,128)(2,1)S(1)}, bf16[1,1,128,2048]{3,2,1,0:T(8,128)(2,1)}, u32[]{:S(2)}) copy-start(bf16[1,1,128,2048]{3,2,1,0:T(8,128)(2,1)} %param.9) | copy-start | bytes 1572868
  5.6 1.0 %copy-start.1 = (bf16[1,1,128,2048]{3,2,1,0:T(8,128)(2,1)S(1)}, bf16[1,1,128,2048]{3,2,1,0:T(8,128)(2,1)}, u32[]{:S(2)}) copy-start(bf16[1,1,128,2048]{3,2,1,0:T(8,128)(2,1)} %param.10) | copy-start | bytes 1572868
  6.6 0.7 copy-start.2
  7.3 0.7 copy-start.3
  8.0 0.7 copy-start.4
  8.6 0.7 copy-start.5
  11.1 43.5 %copy-start.7 = (bf16[384,2048]{1,0:T(8,128)(2,1)S(1)}, bf16[384,2048]{1,0:T(8,128)(2,1)}, u32[]{:S(2)}) copy-start(bf16[384,2048]{1,0:T(8,128)(2,1)} %refs_6_.1) | copy-start | bytes 4718596
  16.7 37.9 %copy-start.6 = (bf16[2048,384]{1,0:T(8,128)(2,1)S(1)}, bf16[2048,384]{1,0:T(8,128)(2,1)}, u32[]{:S(2)}) copy-start(bf16[2048,384]{1,0:T(8,128)(2,1)} %refs_4_.1) | copy-start | bytes 4718596
  16.7 20.0 %collective-permute-start.6 = (bf16[96,2048]{1,0:T(8,128)(2,1)S(1)}, bf16[96,2048]{1,0:T(8,128)(2,1)S(1)}, u32[]{:S(2)}, u32[]{:S(2)}) collective-permute-start(bf16[96,2048]{1,0:T(8,128)(2,1)S(1)} %get-tuple-element.47), channel_id=1, source_target_pairs={{0,8},{1,9},{2,10},{3,11},{4,12},{5,13},{6,14},{7,15},{8,0},{9,1},... | collective-permute-start | bytes 1179656 | tf_op jit(solution)/shard_map/ppermute | solution.py:301
  19.6 17.3 %collective-permute-start.4 = (bf16[96,2048]{1,0:T(8,128)(2,1)S(1)}, bf16[96,2048]{1,0:T(8,128)(2,1)S(1)}, u32[]{:S(2)}, u32[]{:S(2)}) collective-permute-start(bf16[96,2048]{1,0:T(8,128)(2,1)S(1)} %get-tuple-element.46.refs_0_), channel_id=1, source_target_pairs={{0,4},{1,5},{2,6},{3,7},{4,0},{5,1},{6,2},{7,3},{8,12},{9,13},{10,... | collective-permute-start | bytes 1179656 | tf_op jit(solution)/shard_map/ppermute | solution.py:297
  21.2 15.7 %collective-permute-start.3 = (bf16[96,2048]{1,0:T(8,128)(2,1)S(1)}, bf16[96,2048]{1,0:T(8,128)(2,1)S(1)}, u32[]{:S(2)}, u32[]{:S(2)}) collective-permute-start(bf16[96,2048]{1,0:T(8,128)(2,1)S(1)} %get-tuple-element.46.refs_0_), channel_id=1, source_target_pairs={{0,2},{1,3},{2,0},{3,1},{4,6},{5,7},{6,4},{7,5},{8,10},{9,11},{10,... | collective-permute-start | bytes 1179656 | tf_op jit(solution)/shard_map/ppermute | solution.py:297
  36.9 7.4 %collective-permute-start.10 = (bf16[96,1024]{1,0:T(8,128)(2,1)S(1)}, bf16[96,1024]{1,0:T(8,128)(2,1)S(1)}, u32[]{:S(2)}, u32[]{:S(2)}) collective-permute-start(bf16[96,1024]{1,0:T(8,128)(2,1)S(1)} %get-tuple-element.73), channel_id=1, source_target_pairs={{0,4},{1,5},{2,6},{3,7},{4,0},{5,1},{6,2},{7,3},{8,12},{9,13},{10,... | collective-permute-start | bytes 589832 | tf_op jit(solution)/shard_map/ppermute | solution.py:297
  38.3 7.8 %collective-permute-start.7 = (bf16[96,1024]{1,0:T(8,128)(2,1)S(1)}, bf16[96,1024]{1,0:T(8,128)(2,1)S(1)}, u32[]{:S(2)}, u32[]{:S(2)}) collective-permute-start(bf16[96,1024]{1,0:T(8,128)(2,1)S(1)} %get-tuple-element.74), channel_id=1, source_target_pairs={{0,2},{1,3},{2,0},{3,1},{4,6},{5,7},{6,4},{7,5},{8,10},{9,11},{10,... | collective-permute-start | bytes 589832 | tf_op jit(solution)/shard_map/ppermute | solution.py:297
  39.8 10.5 %collective-permute-start.8 = (bf16[96,1024]{1,0:T(8,128)(2,1)S(1)}, bf16[96,1024]{1,0:T(8,128)(2,1)S(1)}, u32[]{:S(2)}, u32[]{:S(2)}) collective-permute-start(bf16[96,1024]{1,0:T(8,128)(2,1)S(1)} %get-tuple-element.73), channel_id=1, source_target_pairs={{0,2},{1,3},{2,0},{3,1},{4,6},{5,7},{6,4},{7,5},{8,10},{9,11},{10,... | collective-permute-start | bytes 589832 | tf_op jit(solution)/shard_map/ppermute | solution.py:297
  40.3 10.0 %collective-permute-start.9 = (bf16[96,1024]{1,0:T(8,128)(2,1)S(1)}, bf16[96,1024]{1,0:T(8,128)(2,1)S(1)}, u32[]{:S(2)}, u32[]{:S(2)}) collective-permute-start(bf16[96,1024]{1,0:T(8,128)(2,1)S(1)} %get-tuple-element.74), channel_id=1, source_target_pairs={{0,4},{1,5},{2,6},{3,7},{4,0},{5,1},{6,2},{7,3},{8,12},{9,13},{10,... | collective-permute-start | bytes 589832 | tf_op jit(solution)/shard_map/ppermute | solution.py:297
  44.3 10.3 %collective-permute-start.12 = (bf16[96,1024]{1,0:T(8,128)(2,1)S(1)}, bf16[96,1024]{1,0:T(8,128)(2,1)S(1)}, u32[]{:S(2)}, u32[]{:S(2)}) collective-permute-start(bf16[96,1024]{1,0:T(8,128)(2,1)S(1)} %collective-permute-done.10.refs_4_), channel_id=1, source_target_pairs={{0,2},{1,3},{2,0},{3,1},{4,6},{5,7},{6,4},{7,5},{8,10},{9,11},{10,... | collective-permute-start | bytes 589832 | tf_op jit(solution)/shard_map/ppermute | solution.py:297
  46.2 8.4 %collective-permute-start.11 = (bf16[96,1024]{1,0:T(8,128)(2,1)S(1)}, bf16[96,1024]{1,0:T(8,128)(2,1)S(1)}, u32[]{:S(2)}, u32[]{:S(2)}) collective-permute-start(bf16[96,1024]{1,0:T(8,128)(2,1)S(1)} %collective-permute-done.7.refs_1_), channel_id=1, source_target_pairs={{0,4},{1,5},{2,6},{3,7},{4,0},{5,1},{6,2},{7,3},{8,12},{9,13},{10,... | collective-permute-start | bytes 589832 | tf_op jit(solution)/shard_map/ppermute | solution.py:297
  47.7 15.1 %collective-permute-start.5 = (bf16[96,2048]{1,0:T(8,128)(2,1)S(1)}, bf16[96,2048]{1,0:T(8,128)(2,1)S(1)}, u32[]{:S(2)}, u32[]{:S(2)}) collective-permute-start(bf16[96,2048]{1,0:T(8,128)(2,1)S(1)} %collective-permute-done.4.refs_2_), channel_id=1, source_target_pairs={{0,2},{1,3},{2,0},{3,1},{4,6},{5,7},{6,4},{7,5},{8,10},{9,11},{10,... | collective-permute-start | bytes 1179656 | tf_op jit(solution)/shard_map/ppermute | solution.py:297
  57.6 10.1 %collective-permute-start.15 = (bf16[96,1024]{1,0:T(8,128)(2,1)S(1)}, bf16[96,1024]{1,0:T(8,128)(2,1)S(1)}, u32[]{:S(2)}, u32[]{:S(2)}) collective-permute-start(bf16[96,1024]{1,0:T(8,128)(2,1)S(1)} %get-tuple-element.57), channel_id=1, source_target_pairs={{0,4},{1,5},{2,6},{3,7},{4,0},{5,1},{6,2},{7,3},{8,12},{9,13},{10,... | collective-permute-start | bytes 589832 | tf_op jit(solution)/shard_map/ppermute | solution.py:297
  58.4 9.4 %collective-permute-start.16 = (bf16[96,1024]{1,0:T(8,128)(2,1)S(1)}, bf16[96,1024]{1,0:T(8,128)(2,1)S(1)}, u32[]{:S(2)}, u32[]{:S(2)}) collective-permute-start(bf16[96,1024]{1,0:T(8,128)(2,1)S(1)} %get-tuple-element.58), channel_id=1, source_target_pairs={{0,2},{1,3},{2,0},{3,1},{4,6},{5,7},{6,4},{7,5},{8,10},{9,11},{10,... | collective-permute-start | bytes 589832 | tf_op jit(solution)/shard_map/ppermute | solution.py:297
  65.8 5.7 %collective-permute-start.13 = (bf16[96,1024]{1,0:T(8,128)(2,1)S(1)}, bf16[96,1024]{1,0:T(8,128)(2,1)S(1)}, u32[]{:S(2)}, u32[]{:S(2)}) collective-permute-start(bf16[96,1024]{1,0:T(8,128)(2,1)S(1)} %get-tuple-element.55), channel_id=1, source_target_pairs={{0,4},{1,5},{2,6},{3,7},{4,0},{5,1},{6,2},{7,3},{8,12},{9,13},{10,... | collective-permute-start | bytes 589832 | tf_op jit(solution)/shard_map/ppermute | solution.py:297
  66.3 5.9 %collective-permute-start.14 = (bf16[96,1024]{1,0:T(8,128)(2,1)S(1)}, bf16[96,1024]{1,0:T(8,128)(2,1)S(1)}, u32[]{:S(2)}, u32[]{:S(2)}) collective-permute-start(bf16[96,1024]{1,0:T(8,128)(2,1)S(1)} %get-tuple-element.56), channel_id=1, source_target_pairs={{0,2},{1,3},{2,0},{3,1},{4,6},{5,7},{6,4},{7,5},{8,10},{9,11},{10,... | collective-permute-start | bytes 589832 | tf_op jit(solution)/shard_map/ppermute | solution.py:297
  67.9 8.6 %collective-permute-start.17 = (bf16[96,1024]{1,0:T(8,128)(2,1)S(1)}, bf16[96,1024]{1,0:T(8,128)(2,1)S(1)}, u32[]{:S(2)}, u32[]{:S(2)}) collective-permute-start(bf16[96,1024]{1,0:T(8,128)(2,1)S(1)} %get-tuple-element.59), channel_id=1, source_target_pairs={{0,2},{1,3},{2,0},{3,1},{4,6},{5,7},{6,4},{7,5},{8,10},{9,11},{10,... | collective-permute-start | bytes 589832 | tf_op jit(solution)/shard_map/ppermute | solution.py:297
  68.5 7.9 %collective-permute-start.18 = (bf16[96,1024]{1,0:T(8,128)(2,1)S(1)}, bf16[96,1024]{1,0:T(8,128)(2,1)S(1)}, u32[]{:S(2)}, u32[]{:S(2)}) collective-permute-start(bf16[96,1024]{1,0:T(8,128)(2,1)S(1)} %get-tuple-element.60), channel_id=1, source_target_pairs={{0,4},{1,5},{2,6},{3,7},{4,0},{5,1},{6,2},{7,3},{8,12},{9,13},{10,... | collective-permute-start | bytes 589832 | tf_op jit(solution)/shard_map/ppermute | solution.py:297
  76.6 9.9 %collective-permute-start.22 = (bf16[96,1536]{1,0:T(8,128)(2,1)S(1)}, bf16[96,1536]{1,0:T(8,128)(2,1)S(1)}, u32[]{:S(2)}, u32[]{:S(2)}) collective-permute-start(bf16[96,1536]{1,0:T(8,128)(2,1)S(1)} %get-tuple-element.69), channel_id=1, source_target_pairs={{0,2},{1,3},{2,0},{3,1},{4,6},{5,7},{6,4},{7,5},{8,10},{9,11},{10,... | collective-permute-start | bytes 884744 | tf_op jit(solution)/shard_map/ppermute | solution.py:297
  78.0 7.2 %collective-permute-start.21 = (bf16[96,512]{1,0:T(8,128)(2,1)S(1)}, bf16[96,512]{1,0:T(8,128)(2,1)S(1)}, u32[]{:S(2)}, u32[]{:S(2)}) collective-permute-start(bf16[96,512]{1,0:T(8,128)(2,1)S(1)} %get-tuple-element.67), channel_id=1, source_target_pairs={{0,4},{1,5},{2,6},{3,7},{4,0},{5,1},{6,2},{7,3},{8,12},{9,13},{10,... | collective-permute-start | bytes 294920 | tf_op jit(solution)/shard_map/ppermute | solution.py:297
  80.0 18.0 %collective-permute-start.25 = (bf16[96,2048]{1,0:T(8,128)(2,1)S(1)}, bf16[96,2048]{1,0:T(8,128)(2,1)S(1)}, u32[]{:S(2)}, u32[]{:S(2)}) collective-permute-start(bf16[96,2048]{1,0:T(8,128)(2,1)S(1)} %get-tuple-element.72), channel_id=1, source_target_pairs={{0,8},{1,9},{2,10},{3,11},{4,12},{5,13},{6,14},{7,15},{8,0},{9,1},... | collective-permute-start | bytes 1179656 | tf_op jit(solution)/shard_map/ppermute | solution.py:301
  80.5 17.5 %collective-permute-start.20 = (bf16[96,1536]{1,0:T(8,128)(2,1)S(1)}, bf16[96,1536]{1,0:T(8,128)(2,1)S(1)}, u32[]{:S(2)}, u32[]{:S(2)}) collective-permute-start(bf16[96,1536]{1,0:T(8,128)(2,1)S(1)} %get-tuple-element.66), channel_id=1, source_target_pairs={{0,2},{1,3},{2,0},{3,1},{4,6},{5,7},{6,4},{7,5},{8,10},{9,11},{10,... | collective-permute-start | bytes 884744 | tf_op jit(solution)/shard_map/ppermute | solution.py:297
  86.6 11.4 %collective-permute-start.24 = (bf16[96,1536]{1,0:T(8,128)(2,1)S(1)}, bf16[96,1536]{1,0:T(8,128)(2,1)S(1)}, u32[]{:S(2)}, u32[]{:S(2)}) collective-permute-start(bf16[96,1536]{1,0:T(8,128)(2,1)S(1)} %get-tuple-element.71), channel_id=1, source_target_pairs={{0,4},{1,5},{2,6},{3,7},{4,0},{5,1},{6,2},{7,3},{8,12},{9,13},{10,... | collective-permute-start | bytes 884744 | tf_op jit(solution)/shard_map/ppermute | solution.py:297
  87.6 10.4 %collective-permute-start.19 = (bf16[96,512]{1,0:T(8,128)(2,1)S(1)}, bf16[96,512]{1,0:T(8,128)(2,1)S(1)}, u32[]{:S(2)}, u32[]{:S(2)}) collective-permute-start(bf16[96,512]{1,0:T(8,128)(2,1)S(1)} %get-tuple-element.65), channel_id=1, source_target_pairs={{0,4},{1,5},{2,6},{3,7},{4,0},{5,1},{6,2},{7,3},{8,12},{9,13},{10,... | collective-permute-start | bytes 294920 | tf_op jit(solution)/shard_map/ppermute | solution.py:297
  88.7 9.3 %collective-permute-start.23 = (bf16[96,512]{1,0:T(8,128)(2,1)S(1)}, bf16[96,512]{1,0:T(8,128)(2,1)S(1)}, u32[]{:S(2)}, u32[]{:S(2)}) collective-permute-start(bf16[96,512]{1,0:T(8,128)(2,1)S(1)} %get-tuple-element.70), channel_id=1, source_target_pairs={{0,2},{1,3},{2,0},{3,1},{4,6},{5,7},{6,4},{7,5},{8,10},{9,11},{10,... | collective-permute-start | bytes 294920 | tf_op jit(solution)/shard_map/ppermute | solution.py:297

commit v7 on v6

--- a/solution.py
+++ b/solution.py
@@ -39,7 +39,10 @@
 
 
 def as_column(row):
-    return jnp.transpose(jnp.broadcast_to(row, (8, row.shape[1])))[:, :1]
+    count = row.shape[1]
+    down = lax.broadcasted_iota(jnp.int32, (count, count), 0)
+    along = lax.broadcasted_iota(jnp.int32, (count, count), 1)
+    return jnp.sum(jnp.where(down == along, row, jnp.zeros_like(row)), axis=1, keepdims=True)
 
 
 def stage_kernel(groups, cap, *refs):
@@ -109,22 +112,17 @@
         values = jnp.concatenate([r[local:, cols] for r in kv_refs], axis=0)
         scores = (
             lax.dot_general(
+                query_ref[:, cols],
                 keys,
-                query_ref[:, cols],
                 (((1,), (1,)), ((), ())),
                 preferred_element_type=jnp.float32,
             )
             * scale
         )
-        raised = jnp.exp(scores - jnp.max(scores, axis=0, keepdims=True))
-        total = jnp.sum(raised, axis=0, keepdims=True)
-        mixed = lax.dot_general(
-            raised.astype(jnp.bfloat16),
-            values,
-            (((0,), (0,)), ((), ())),
-            preferred_element_type=jnp.float32,
-        )
-        hidden = state_ref[:, cols].astype(jnp.float32) + mixed * as_column(1.0 / total)
+        raised = jnp.exp(scores - jnp.max(scores, axis=1, keepdims=True))
+        total = jnp.sum(raised, axis=1, keepdims=True)
+        mixed = jnp.dot(raised.astype(jnp.bfloat16), values, preferred_element_type=jnp.float32)
+        hidden = state_ref[:, cols].astype(jnp.float32) + mixed / total
         hidden_ref[:, cols] = hidden
         squares = squares + hidden * hidden
     mean_square = jnp.sum(squares, axis=1, keepdims=True) * (1.0 / width)

time: 99.5 us -> 96.5 us (0.970)
  Pallas kernels: 13.2 us -> 10.2 us
    pallas_call x1, Pallas kernels: 5.51 us -> 2.5 us  [attend(): call(functools.partial(attend_kernel, pieces, groups, cap), outs, [VMEM]...]
  transfers between devices with their start and end apart: 26 -> 26, of which waited for: 14 -> 14; matrix products, arithmetic and copies ran while one was open for 1% -> 1% of each run, Pallas kernels for 6% -> 7%
where the time goes in v7:
time: 96.5 us; the launch traced here: 96.2 us
  waiting for transfers between devices  48.9 us (51%)
  starting transfers between devices  31.1 us (32%)
  Pallas kernels  10.2 us (11%)
  local copies, waits for them, and re-layouts  5.81 us (6%)
    ppermute x23, waiting for transfers between devices, across(): return lax.ppermute(value, 'expert', [(i, i ^ bit) for i in range(devices)])  33.2 us
    ppermute x23, starting transfers between devices, across(): return lax.ppermute(value, 'expert', [(i, i ^ bit) for i in range(devices)])  24.7 us
    ppermute x2, waiting for transfers between devices, groups_on(): lax.ppermute(value, 'expert', [(i, (i + shift) % devices) for i in range(...  14 us
    pallas_call x2, Pallas kernels, ffn(): call(functools.partial(ffn_kernel, counts, cut), outs, [VMEM] * (sum(coun...  6.07 us
    unnamed x16, local copies, waits for them, and re-layouts  4.75 us
    ppermute x2, starting transfers between devices, groups_on(): lax.ppermute(value, 'expert', [(i, (i + shift) % devices) for i in range(...  3.38 us
    ppermute x1, starting transfers between devices, body(): kv_pieces.append(lax.ppermute(kv, 'pipe', perm))  3 us
    pallas_call x1, Pallas kernels, attend(): call(functools.partial(attend_kernel, pieces, groups, cap), outs, [VMEM]...  2.5 us
  transfers between devices with their start and end apart: 26, of which 14 were waited for; matrix products, arithmetic and copies ran while one was open for 1% of the time, Pallas kernels for 7%

profile of v7, /device:TPU:0, one launch (start us, length us, event | category | flops | bytes accessed | tf_op | source)
XLA Modules:
  0.0 96.2 jit_solution(17317954342088427336)
XLA Ops:
  0.5 1.0 %copy.17 = bf16[2,32,2048]{2,1,0:T(8,128)(2,1)S(1)} copy(bf16[2,32,2048]{2,0,1:T(2,128)(2,1)} %bitcast.20) | data formatting | bytes 524288 | tf_op jit(solution)/shard_map/transpose | solution.py:301
  1.5 3.0 %collective-permute-start = (bf16[64,2048]{1,0:T(8,128)(2,1)S(1)}, bf16[64,2048]{1,0:T(8,128)(2,1)}, u32[]{:S(2)}, u32[]{:S(2)}) collective-permute-start(bf16[64,2048]{1,0:T(8,128)(2,1)S(1)} %bitcast.12), channel_id=1, source_target_pairs={{0,16},{16,0},{1,17},{17,1},{2,18},{18,2},{3,19},{19,3},{4,20},{20... | collective-permute-start | bytes 786440 | tf_op jit(solution)/shard_map/ppermute | solution.py:305
  4.6 1.0 %copy-done = bf16[1,1,128,2048]{3,2,1,0:T(8,128)(2,1)S(1)} copy-done((bf16[1,1,128,2048]{3,2,1,0:T(8,128)(2,1)S(1)}, bf16[1,1,128,2048]{3,2,1,0:T(8,128)(2,1)}, u32[]{:S(2)}) %copy-start) | copy-done | bytes 524312
  5.6 1.0 %copy-done.1 = bf16[1,1,128,2048]{3,2,1,0:T(8,128)(2,1)S(1)} copy-done((bf16[1,1,128,2048]{3,2,1,0:T(8,128)(2,1)S(1)}, bf16[1,1,128,2048]{3,2,1,0:T(8,128)(2,1)}, u32[]{:S(2)}) %copy-start.1) | copy-done | bytes 524312
  6.6 0.7 copy-done.2
  7.3 0.7 copy-done.3
  8.0 0.7 copy-done.4
  8.6 0.7 copy-done.5
  9.4 1.7 %collective-permute-done.refs_5_ = bf16[64,2048]{1,0:T(8,128)(2,1)} collective-permute-done((bf16[64,2048]{1,0:T(8,128)(2,1)S(1)}, bf16[64,2048]{1,0:T(8,128)(2,1)}, u32[]{:S(2)}, u32[]{:S(2)}) %collective-permute-start) | collective-permute-done | bytes 262176 | tf_op jit(solution)/shard_map/ppermute | solution.py:305
  11.1 2.5 %attend.1 = (f32[128,2048]{1,0:T(8,128)S(1)}, bf16[96,2048]{1,0:T(8,128)(2,1)S(1)}, bf16[96,2048]{1,0:T(8,128)(2,1)S(1)}) custom-call(bf16[128,2048]{1,0:T(8,128)(2,1)S(1)} %get-tuple-element.39.refs_0_, bf16[128,2048]{1,0:T(8,128)(2,1)S(1)} %get-tuple-element.40.refs_1_, f32[1,2048]{1,0:T(1,128)S(1)} %get-tuple-element.41.refs_2_, ...), custom_call_target="tpu_custom_call" | custom-call | flops 134217728 | bytes 3145728 | tf_op jit(solution)/shard_map/attend/pallas_call | solution.py:145
  13.7 2.9 %collective-permute-start.6 = (bf16[96,2048]{1,0:T(8,128)(2,1)S(1)}, bf16[96,2048]{1,0:T(8,128)(2,1)S(1)}, u32[]{:S(2)}, u32[]{:S(2)}) collective-permute-start(bf16[96,2048]{1,0:T(8,128)(2,1)S(1)} %get-tuple-element.47), channel_id=1, source_target_pairs={{0,8},{1,9},{2,10},{3,11},{4,12},{5,13},{6,14},{7,15},{8,0},{9,1},... | collective-permute-start | bytes 1179656 | tf_op jit(solution)/shard_map/ppermute | solution.py:299
  16.6 1.6 %collective-permute-start.4 = (bf16[96,2048]{1,0:T(8,128)(2,1)S(1)}, bf16[96,2048]{1,0:T(8,128)(2,1)S(1)}, u32[]{:S(2)}, u32[]{:S(2)}) collective-permute-start(bf16[96,2048]{1,0:T(8,128)(2,1)S(1)} %get-tuple-element.46.refs_0_), channel_id=1, source_target_pairs={{0,4},{1,5},{2,6},{3,7},{4,0},{5,1},{6,2},{7,3},{8,12},{9,13},{10,... | collective-permute-start | bytes 1179656 | tf_op jit(solution)/shard_map/ppermute | solution.py:295
  18.1 1.5 %collective-permute-start.3 = (bf16[96,2048]{1,0:T(8,128)(2,1)S(1)}, bf16[96,2048]{1,0:T(8,128)(2,1)S(1)}, u32[]{:S(2)}, u32[]{:S(2)}) collective-permute-start(bf16[96,2048]{1,0:T(8,128)(2,1)S(1)} %get-tuple-element.46.refs_0_), channel_id=1, source_target_pairs={{0,2},{1,3},{2,0},{3,1},{4,6},{5,7},{6,4},{7,5},{8,10},{9,11},{10,... | collective-permute-start | bytes 1179656 | tf_op jit(solution)/shard_map/ppermute | solution.py:295
  19.7 14.0 %collective-permute-done.6.refs_0_ = bf16[96,2048]{1,0:T(8,128)(2,1)S(1)} collective-permute-done((bf16[96,2048]{1,0:T(8,128)(2,1)S(1)}, bf16[96,2048]{1,0:T(8,128)(2,1)S(1)}, u32[]{:S(2)}, u32[]{:S(2)}) %collective-permute-start.6) | collective-permute-done | bytes 393248 | tf_op jit(solution)/shard_map/ppermute | solution.py:299
  33.9 1.4 %collective-permute-start.10 = (bf16[96,1024]{1,0:T(8,128)(2,1)S(1)}, bf16[96,1024]{1,0:T(8,128)(2,1)S(1)}, u32[]{:S(2)}, u32[]{:S(2)}) collective-permute-start(bf16[96,1024]{1,0:T(8,128)(2,1)S(1)} %get-tuple-element.73), channel_id=1, source_target_pairs={{0,4},{1,5},{2,6},{3,7},{4,0},{5,1},{6,2},{7,3},{8,12},{9,13},{10,... | collective-permute-start | bytes 589832 | tf_op jit(solution)/shard_map/ppermute | solution.py:295
  35.3 1.5 %collective-permute-start.7 = (bf16[96,1024]{1,0:T(8,128)(2,1)S(1)}, bf16[96,1024]{1,0:T(8,128)(2,1)S(1)}, u32[]{:S(2)}, u32[]{:S(2)}) collective-permute-start(bf16[96,1024]{1,0:T(8,128)(2,1)S(1)} %get-tuple-element.74), channel_id=1, source_target_pairs={{0,2},{1,3},{2,0},{3,1},{4,6},{5,7},{6,4},{7,5},{8,10},{9,11},{10,... | collective-permute-start | bytes 589832 | tf_op jit(solution)/shard_map/ppermute | solution.py:295
  36.8 0.5 collective-permute-start.8
  37.3 0.7 collective-permute-start.9
  38.0 3.2 %collective-permute-done.10.refs_4_ = bf16[96,1024]{1,0:T(8,128)(2,1)S(1)} collective-permute-done((bf16[96,1024]{1,0:T(8,128)(2,1)S(1)}, bf16[96,1024]{1,0:T(8,128)(2,1)S(1)}, u32[]{:S(2)}, u32[]{:S(2)}) %collective-permute-start.10) | collective-permute-done | bytes 196640 | tf_op jit(solution)/shard_map/ppermute | solution.py:295
  41.2 1.4 %collective-permute-start.12 = (bf16[96,1024]{1,0:T(8,128)(2,1)S(1)}, bf16[96,1024]{1,0:T(8,128)(2,1)S(1)}, u32[]{:S(2)}, u32[]{:S(2)}) collective-permute-start(bf16[96,1024]{1,0:T(8,128)(2,1)S(1)} %collective-permute-done.10.refs_4_), channel_id=1, source_target_pairs={{0,2},{1,3},{2,0},{3,1},{4,6},{5,7},{6,4},{7,5},{8,10},{9,11},{10,... | collective-permute-start | bytes 589832 | tf_op jit(solution)/shard_map/ppermute | solution.py:295
  42.6 0.5 collective-permute-done.7.refs_1_
  43.1 1.5 %collective-permute-start.11 = (bf16[96,1024]{1,0:T(8,128)(2,1)S(1)}, bf16[96,1024]{1,0:T(8,128)(2,1)S(1)}, u32[]{:S(2)}, u32[]{:S(2)}) collective-permute-start(bf16[96,1024]{1,0:T(8,128)(2,1)S(1)} %collective-permute-done.7.refs_1_), channel_id=1, source_target_pairs={{0,4},{1,5},{2,6},{3,7},{4,0},{5,1},{6,2},{7,3},{8,12},{9,13},{10,... | collective-permute-start | bytes 589832 | tf_op jit(solution)/shard_map/ppermute | solution.py:295
  44.7 0.6 collective-permute-start.5
  45.3 2.1 %collective-permute-done.8.refs_2_ = bf16[96,1024]{1,0:T(8,128)(2,1)S(1)} collective-permute-done((bf16[96,1024]{1,0:T(8,128)(2,1)S(1)}, bf16[96,1024]{1,0:T(8,128)(2,1)S(1)}, u32[]{:S(2)}, u32[]{:S(2)}) %collective-permute-start.8) | collective-permute-done | bytes 196640 | tf_op jit(solution)/shard_map/ppermute | solution.py:295
  47.4 4.2 %collective-permute-done.12.refs_6_ = bf16[96,1024]{1,0:T(8,128)(2,1)S(1)} collective-permute-done((bf16[96,1024]{1,0:T(8,128)(2,1)S(1)}, bf16[96,1024]{1,0:T(8,128)(2,1)S(1)}, u32[]{:S(2)}, u32[]{:S(2)}) %collective-permute-start.12) | collective-permute-done | bytes 196640 | tf_op jit(solution)/shard_map/ppermute | solution.py:295
  51.6 3.0 %expert_ffn.2 = (bf16[96,2048]{1,0:T(8,128)(2,1)S(1)}, bf16[96,1024]{1,0:T(8,128)(2,1)S(1)}, bf16[96,1024]{1,0:T(8,128)(2,1)S(1)}, bf16[96,1024]{1,0:T(8,128)(2,...) custom-call(bf16[96,2048]{1,0:T(8,128)(2,1)S(1)} %hand_on.2.refs_0_, ...), custom_call_target="tpu_custom_call" | custom-call | flops 2415919104 | bytes 9437184 | tf_op jit(solution)/shard_map/expert_ffn/pallas_call | solution.py:192
  54.6 0.7 collective-permute-start.15
  55.4 1.4 %collective-permute-start.16 = (bf16[96,1024]{1,0:T(8,128)(2,1)S(1)}, bf16[96,1024]{1,0:T(8,128)(2,1)S(1)}, u32[]{:S(2)}, u32[]{:S(2)}) collective-permute-start(bf16[96,1024]{1,0:T(8,128)(2,1)S(1)} %get-tuple-element.58), channel_id=1, source_target_pairs={{0,2},{1,3},{2,0},{3,1},{4,6},{5,7},{6,4},{7,5},{8,10},{9,11},{10,... | collective-permute-start | bytes 589832 | tf_op jit(solution)/shard_map/ppermute | solution.py:295
  56.8 3.0 %collective-permute-done.5.refs_3_ = bf16[96,2048]{1,0:T(8,128)(2,1)S(1)} collective-permute-done((bf16[96,2048]{1,0:T(8,128)(2,1)S(1)}, bf16[96,2048]{1,0:T(8,128)(2,1)S(1)}, u32[]{:S(2)}, u32[]{:S(2)}) %collective-permute-start.5) | collective-permute-done | bytes 393248 | tf_op jit(solution)/shard_map/ppermute | solution.py:295
  59.8 3.0 %expert_ffn.3 = (bf16[96,2048]{1,0:T(8,128)(2,1)S(1)}, bf16[96,512]{1,0:T(8,128)(2,1)S(1)}, bf16[96,1536]{1,0:T(8,128)(2,1)S(1)}, bf16[96,512]{1,0:T(8,128)(2,1)...) custom-call(bf16[96,2048]{1,0:T(8,128)(2,1)S(1)} %get-tuple-element.46.refs_0_, ...), custom_call_target="tpu_custom_call" | custom-call | flops 2415919104 | bytes 9437184 | tf_op jit(solution)/shard_map/expert_ffn/pallas_call | solution.py:192
  62.8 0.5 collective-permute-start.13
  63.3 1.4 %collective-permute-start.14 = (bf16[96,1024]{1,0:T(8,128)(2,1)S(1)}, bf16[96,1024]{1,0:T(8,128)(2,1)S(1)}, u32[]{:S(2)}, u32[]{:S(2)}) collective-permute-start(bf16[96,1024]{1,0:T(8,128)(2,1)S(1)} %get-tuple-element.56), channel_id=1, source_target_pairs={{0,2},{1,3},{2,0},{3,1},{4,6},{5,7},{6,4},{7,5},{8,10},{9,11},{10,... | collective-permute-start | bytes 589832 | tf_op jit(solution)/shard_map/ppermute | solution.py:295
  64.8 0.7 collective-permute-start.17
  65.5 1.6 %collective-permute-start.18 = (bf16[96,1024]{1,0:T(8,128)(2,1)S(1)}, bf16[96,1024]{1,0:T(8,128)(2,1)S(1)}, u32[]{:S(2)}, u32[]{:S(2)}) collective-permute-start(bf16[96,1024]{1,0:T(8,128)(2,1)S(1)} %get-tuple-element.60), channel_id=1, source_target_pairs={{0,4},{1,5},{2,6},{3,7},{4,0},{5,1},{6,2},{7,3},{8,12},{9,13},{10,... | collective-permute-start | bytes 589832 | tf_op jit(solution)/shard_map/ppermute | solution.py:295
  67.1 1.4 %collective-permute-done.13.refs_1_ = bf16[96,1024]{1,0:T(8,128)(2,1)S(1)} collective-permute-done((bf16[96,1024]{1,0:T(8,128)(2,1)S(1)}, bf16[96,1024]{1,0:T(8,128)(2,1)S(1)}, u32[]{:S(2)}, u32[]{:S(2)}) %collective-permute-start.13) | collective-permute-done | bytes 196640 | tf_op jit(solution)/shard_map/ppermute | solution.py:295
  68.5 0.7 collective-permute-done.14.refs_2_
  69.2 4.2 %collective-permute-done.17.refs_3_ = bf16[96,1024]{1,0:T(8,128)(2,1)S(1)} collective-permute-done((bf16[96,1024]{1,0:T(8,128)(2,1)S(1)}, bf16[96,1024]{1,0:T(8,128)(2,1)S(1)}, u32[]{:S(2)}, u32[]{:S(2)}) %collective-permute-start.17) | collective-permute-done | bytes 196640 | tf_op jit(solution)/shard_map/ppermute | solution.py:295
  73.6 1.4 %collective-permute-start.22 = (bf16[96,1536]{1,0:T(8,128)(2,1)S(1)}, bf16[96,1536]{1,0:T(8,128)(2,1)S(1)}, u32[]{:S(2)}, u32[]{:S(2)}) collective-permute-start(bf16[96,1536]{1,0:T(8,128)(2,1)S(1)} %get-tuple-element.69), channel_id=1, source_target_pairs={{0,2},{1,3},{2,0},{3,1},{4,6},{5,7},{6,4},{7,5},{8,10},{9,11},{10,... | collective-permute-start | bytes 884744 | tf_op jit(solution)/shard_map/ppermute | solution.py:295
  75.0 2.0 %collective-permute-start.21 = (bf16[96,512]{1,0:T(8,128)(2,1)S(1)}, bf16[96,512]{1,0:T(8,128)(2,1)S(1)}, u32[]{:S(2)}, u32[]{:S(2)}) collective-permute-start(bf16[96,512]{1,0:T(8,128)(2,1)S(1)} %get-tuple-element.67), channel_id=1, source_target_pairs={{0,4},{1,5},{2,6},{3,7},{4,0},{5,1},{6,2},{7,3},{8,12},{9,13},{10,... | collective-permute-start | bytes 294920 | tf_op jit(solution)/shard_map/ppermute | solution.py:295
  77.0 0.5 collective-permute-start.25
  77.5 0.5 collective-permute-start.20
  78.0 4.1 %collective-permute-done.21.zd_ref = bf16[96,512]{1,0:T(8,128)(2,1)S(1)} collective-permute-done((bf16[96,512]{1,0:T(8,128)(2,1)S(1)}, bf16[96,512]{1,0:T(8,128)(2,1)S(1)}, u32[]{:S(2)}, u32[]{:S(2)}) %collective-permute-start.21) | collective-permute-done | bytes 98336 | tf_op jit(solution)/shard_map/ppermute | solution.py:295
  82.1 1.3 %collective-permute-done.22.yd_ref = bf16[96,1536]{1,0:T(8,128)(2,1)S(1)} collective-permute-done((bf16[96,1536]{1,0:T(8,128)(2,1)S(1)}, bf16[96,1536]{1,0:T(8,128)(2,1)S(1)}, u32[]{:S(2)}, u32[]{:S(2)}) %collective-permute-start.22) | collective-permute-done | bytes 294944 | tf_op jit(solution)/shard_map/ppermute | solution.py:295
  83.6 1.0 %collective-permute-start.24 = (bf16[96,1536]{1,0:T(8,128)(2,1)S(1)}, bf16[96,1536]{1,0:T(8,128)(2,1)S(1)}, u32[]{:S(2)}, u32[]{:S(2)}) collective-permute-start(bf16[96,1536]{1,0:T(8,128)(2,1)S(1)} %get-tuple-element.71), channel_id=1, source_target_pairs={{0,4},{1,5},{2,6},{3,7},{4,0},{5,1},{6,2},{7,3},{8,12},{9,13},{10,... | collective-permute-start | bytes 884744 | tf_op jit(solution)/shard_map/ppermute | solution.py:295
  84.6 1.1 %collective-permute-start.19 = (bf16[96,512]{1,0:T(8,128)(2,1)S(1)}, bf16[96,512]{1,0:T(8,128)(2,1)S(1)}, u32[]{:S(2)}, u32[]{:S(2)}) collective-permute-start(bf16[96,512]{1,0:T(8,128)(2,1)S(1)} %get-tuple-element.65), channel_id=1, source_target_pairs={{0,4},{1,5},{2,6},{3,7},{4,0},{5,1},{6,2},{7,3},{8,12},{9,13},{10,... | collective-permute-start | bytes 294920 | tf_op jit(solution)/shard_map/ppermute | solution.py:295
  85.6 1.2 %collective-permute-start.23 = (bf16[96,512]{1,0:T(8,128)(2,1)S(1)}, bf16[96,512]{1,0:T(8,128)(2,1)S(1)}, u32[]{:S(2)}, u32[]{:S(2)}) collective-permute-start(bf16[96,512]{1,0:T(8,128)(2,1)S(1)} %get-tuple-element.70), channel_id=1, source_target_pairs={{0,2},{1,3},{2,0},{3,1},{4,6},{5,7},{6,4},{7,5},{8,10},{9,11},{10,... | collective-permute-start | bytes 294920 | tf_op jit(solution)/shard_map/ppermute | solution.py:295
  86.8 8.2 %collective-permute-done.19.refs_4_ = bf16[96,512]{1,0:T(8,128)(2,1)S(1)} collective-permute-done((bf16[96,512]{1,0:T(8,128)(2,1)S(1)}, bf16[96,512]{1,0:T(8,128)(2,1)S(1)}, u32[]{:S(2)}, u32[]{:S(2)}) %collective-permute-start.19) | collective-permute-done | bytes 98336 | tf_op jit(solution)/shard_map/ppermute | solution.py:295
  95.0 1.1 %finish.1 = bf16[128,2048]{1,0:T(8,128)(2,1)} custom-call(f32[128,2048]{1,0:T(8,128)S(1)} %get-tuple-element.43.refs_0_, f32[128,1]{1,0:T(8,128)S(1)} %get-tuple-element.44.refs_1_, s32[128,1]{1,0:T(8,128)S(1)} %get-tuple-element.45.refs_2_, bf16[96,2048]{1,0:T(8,128)(2,1)S(1)} %get-tuple-element.50.refs_3_, ...), custom_call_target="tpu_custom_call" | custom-call | flops 201326592 | bytes 4194304 | tf_op jit(solution)/shard_map/finish/pallas_call | solution.py:275
  (32 shorter events, 1.2 us)
Async XLA Ops:
  0.0 11.1 %collective-permute-start.1 = (bf16[2048,384]{1,0:T(8,128)(2,1)}, bf16[2048,384]{1,0:T(8,128)(2,1)S(1)}, u32[]{:S(2)}, u32[]{:S(2)}) collective-permute-start(bf16[2048,384]{1,0:T(8,128)(2,1)} %refs_4_.1), channel_id=1, source_target_pairs={{0,1},{1,0},{2,3},{3,2},{4,5},{5,4},{6,7},{7,6},{8,9},{9,8},{10,11... | collective-permute-start | bytes 4718600 | tf_op jit(solution)/shard_map/ppermute | solution.py:295
  0.5 10.7 %collective-permute-start.2 = (bf16[384,2048]{1,0:T(8,128)(2,1)}, bf16[384,2048]{1,0:T(8,128)(2,1)S(1)}, u32[]{:S(2)}, u32[]{:S(2)}) collective-permute-start(bf16[384,2048]{1,0:T(8,128)(2,1)} %refs_6_.1), channel_id=1, source_target_pairs={{0,1},{1,0},{2,3},{3,2},{4,5},{5,4},{6,7},{7,6},{8,9},{9,8},{10,11... | collective-permute-start | bytes 4718600 | tf_op jit(solution)/shard_map/ppermute | solution.py:295
  1.5 9.6 %collective-permute-start = (bf16[64,2048]{1,0:T(8,128)(2,1)S(1)}, bf16[64,2048]{1,0:T(8,128)(2,1)}, u32[]{:S(2)}, u32[]{:S(2)}) collective-permute-start(bf16[64,2048]{1,0:T(8,128)(2,1)S(1)} %bitcast.12), channel_id=1, source_target_pairs={{0,16},{16,0},{1,17},{17,1},{2,18},{18,2},{3,19},{19,3},{4,20},{20... | collective-permute-start | bytes 786440 | tf_op jit(solution)/shard_map/ppermute | solution.py:305
  4.5 1.0 %copy-start = (bf16[1,1,128,2048]{3,2,1,0:T(8,128)(2,1)S(1)}, bf16[1,1,128,2048]{3,2,1,0:T(8,128)(2,1)}, u32[]{:S(2)}) copy-start(bf16[1,1,128,2048]{3,2,1,0:T(8,128)(2,1)} %param.9) | copy-start | bytes 1572868
  5.6 1.0 %copy-start.1 = (bf16[1,1,128,2048]{3,2,1,0:T(8,128)(2,1)S(1)}, bf16[1,1,128,2048]{3,2,1,0:T(8,128)(2,1)}, u32[]{:S(2)}) copy-start(bf16[1,1,128,2048]{3,2,1,0:T(8,128)(2,1)} %param.10) | copy-start | bytes 1572868
  6.6 0.7 copy-start.2
  7.3 0.7 copy-start.3
  8.0 0.7 copy-start.4
  8.6 0.7 copy-start.5
  11.1 40.4 %copy-start.7 = (bf16[384,2048]{1,0:T(8,128)(2,1)S(1)}, bf16[384,2048]{1,0:T(8,128)(2,1)}, u32[]{:S(2)}) copy-start(bf16[384,2048]{1,0:T(8,128)(2,1)} %refs_6_.1) | copy-start | bytes 4718596
  13.6 37.9 %copy-start.6 = (bf16[2048,384]{1,0:T(8,128)(2,1)S(1)}, bf16[2048,384]{1,0:T(8,128)(2,1)}, u32[]{:S(2)}) copy-start(bf16[2048,384]{1,0:T(8,128)(2,1)} %refs_4_.1) | copy-start | bytes 4718596
  13.7 20.0 %collective-permute-start.6 = (bf16[96,2048]{1,0:T(8,128)(2,1)S(1)}, bf16[96,2048]{1,0:T(8,128)(2,1)S(1)}, u32[]{:S(2)}, u32[]{:S(2)}) collective-permute-start(bf16[96,2048]{1,0:T(8,128)(2,1)S(1)} %get-tuple-element.47), channel_id=1, source_target_pairs={{0,8},{1,9},{2,10},{3,11},{4,12},{5,13},{6,14},{7,15},{8,0},{9,1},... | collective-permute-start | bytes 1179656 | tf_op jit(solution)/shard_map/ppermute | solution.py:299
  16.6 17.3 %collective-permute-start.4 = (bf16[96,2048]{1,0:T(8,128)(2,1)S(1)}, bf16[96,2048]{1,0:T(8,128)(2,1)S(1)}, u32[]{:S(2)}, u32[]{:S(2)}) collective-permute-start(bf16[96,2048]{1,0:T(8,128)(2,1)S(1)} %get-tuple-element.46.refs_0_), channel_id=1, source_target_pairs={{0,4},{1,5},{2,6},{3,7},{4,0},{5,1},{6,2},{7,3},{8,12},{9,13},{10,... | collective-permute-start | bytes 1179656 | tf_op jit(solution)/shard_map/ppermute | solution.py:295
  18.1 15.7 %collective-permute-start.3 = (bf16[96,2048]{1,0:T(8,128)(2,1)S(1)}, bf16[96,2048]{1,0:T(8,128)(2,1)S(1)}, u32[]{:S(2)}, u32[]{:S(2)}) collective-permute-start(bf16[96,2048]{1,0:T(8,128)(2,1)S(1)} %get-tuple-element.46.refs_0_), channel_id=1, source_target_pairs={{0,2},{1,3},{2,0},{3,1},{4,6},{5,7},{6,4},{7,5},{8,10},{9,11},{10,... | collective-permute-start | bytes 1179656 | tf_op jit(solution)/shard_map/ppermute | solution.py:295
  33.9 7.4 %collective-permute-start.10 = (bf16[96,1024]{1,0:T(8,128)(2,1)S(1)}, bf16[96,1024]{1,0:T(8,128)(2,1)S(1)}, u32[]{:S(2)}, u32[]{:S(2)}) collective-permute-start(bf16[96,1024]{1,0:T(8,128)(2,1)S(1)} %get-tuple-element.73), channel_id=1, source_target_pairs={{0,4},{1,5},{2,6},{3,7},{4,0},{5,1},{6,2},{7,3},{8,12},{9,13},{10,... | collective-permute-start | bytes 589832 | tf_op jit(solution)/shard_map/ppermute | solution.py:295
  35.3 7.8 %collective-permute-start.7 = (bf16[96,1024]{1,0:T(8,128)(2,1)S(1)}, bf16[96,1024]{1,0:T(8,128)(2,1)S(1)}, u32[]{:S(2)}, u32[]{:S(2)}) collective-permute-start(bf16[96,1024]{1,0:T(8,128)(2,1)S(1)} %get-tuple-element.74), channel_id=1, source_target_pairs={{0,2},{1,3},{2,0},{3,1},{4,6},{5,7},{6,4},{7,5},{8,10},{9,11},{10,... | collective-permute-start | bytes 589832 | tf_op jit(solution)/shard_map/ppermute | solution.py:295
  36.8 10.5 %collective-permute-start.8 = (bf16[96,1024]{1,0:T(8,128)(2,1)S(1)}, bf16[96,1024]{1,0:T(8,128)(2,1)S(1)}, u32[]{:S(2)}, u32[]{:S(2)}) collective-permute-start(bf16[96,1024]{1,0:T(8,128)(2,1)S(1)} %get-tuple-element.73), channel_id=1, source_target_pairs={{0,2},{1,3},{2,0},{3,1},{4,6},{5,7},{6,4},{7,5},{8,10},{9,11},{10,... | collective-permute-start | bytes 589832 | tf_op jit(solution)/shard_map/ppermute | solution.py:295
  37.3 10.0 %collective-permute-start.9 = (bf16[96,1024]{1,0:T(8,128)(2,1)S(1)}, bf16[96,1024]{1,0:T(8,128)(2,1)S(1)}, u32[]{:S(2)}, u32[]{:S(2)}) collective-permute-start(bf16[96,1024]{1,0:T(8,128)(2,1)S(1)} %get-tuple-element.74), channel_id=1, source_target_pairs={{0,4},{1,5},{2,6},{3,7},{4,0},{5,1},{6,2},{7,3},{8,12},{9,13},{10,... | collective-permute-start | bytes 589832 | tf_op jit(solution)/shard_map/ppermute | solution.py:295
  41.2 10.3 %collective-permute-start.12 = (bf16[96,1024]{1,0:T(8,128)(2,1)S(1)}, bf16[96,1024]{1,0:T(8,128)(2,1)S(1)}, u32[]{:S(2)}, u32[]{:S(2)}) collective-permute-start(bf16[96,1024]{1,0:T(8,128)(2,1)S(1)} %collective-permute-done.10.refs_4_), channel_id=1, source_target_pairs={{0,2},{1,3},{2,0},{3,1},{4,6},{5,7},{6,4},{7,5},{8,10},{9,11},{10,... | collective-permute-start | bytes 589832 | tf_op jit(solution)/shard_map/ppermute | solution.py:295
  43.1 8.4 %collective-permute-start.11 = (bf16[96,1024]{1,0:T(8,128)(2,1)S(1)}, bf16[96,1024]{1,0:T(8,128)(2,1)S(1)}, u32[]{:S(2)}, u32[]{:S(2)}) collective-permute-start(bf16[96,1024]{1,0:T(8,128)(2,1)S(1)} %collective-permute-done.7.refs_1_), channel_id=1, source_target_pairs={{0,4},{1,5},{2,6},{3,7},{4,0},{5,1},{6,2},{7,3},{8,12},{9,13},{10,... | collective-permute-start | bytes 589832 | tf_op jit(solution)/shard_map/ppermute | solution.py:295
  44.7 15.1 %collective-permute-start.5 = (bf16[96,2048]{1,0:T(8,128)(2,1)S(1)}, bf16[96,2048]{1,0:T(8,128)(2,1)S(1)}, u32[]{:S(2)}, u32[]{:S(2)}) collective-permute-start(bf16[96,2048]{1,0:T(8,128)(2,1)S(1)} %collective-permute-done.4.refs_2_), channel_id=1, source_target_pairs={{0,2},{1,3},{2,0},{3,1},{4,6},{5,7},{6,4},{7,5},{8,10},{9,11},{10,... | collective-permute-start | bytes 1179656 | tf_op jit(solution)/shard_map/ppermute | solution.py:295
  54.6 10.1 %collective-permute-start.15 = (bf16[96,1024]{1,0:T(8,128)(2,1)S(1)}, bf16[96,1024]{1,0:T(8,128)(2,1)S(1)}, u32[]{:S(2)}, u32[]{:S(2)}) collective-permute-start(bf16[96,1024]{1,0:T(8,128)(2,1)S(1)} %get-tuple-element.57), channel_id=1, source_target_pairs={{0,4},{1,5},{2,6},{3,7},{4,0},{5,1},{6,2},{7,3},{8,12},{9,13},{10,... | collective-permute-start | bytes 589832 | tf_op jit(solution)/shard_map/ppermute | solution.py:295
  55.4 9.4 %collective-permute-start.16 = (bf16[96,1024]{1,0:T(8,128)(2,1)S(1)}, bf16[96,1024]{1,0:T(8,128)(2,1)S(1)}, u32[]{:S(2)}, u32[]{:S(2)}) collective-permute-start(bf16[96,1024]{1,0:T(8,128)(2,1)S(1)} %get-tuple-element.58), channel_id=1, source_target_pairs={{0,2},{1,3},{2,0},{3,1},{4,6},{5,7},{6,4},{7,5},{8,10},{9,11},{10,... | collective-permute-start | bytes 589832 | tf_op jit(solution)/shard_map/ppermute | solution.py:295
  62.8 5.7 %collective-permute-start.13 = (bf16[96,1024]{1,0:T(8,128)(2,1)S(1)}, bf16[96,1024]{1,0:T(8,128)(2,1)S(1)}, u32[]{:S(2)}, u32[]{:S(2)}) collective-permute-start(bf16[96,1024]{1,0:T(8,128)(2,1)S(1)} %get-tuple-element.55), channel_id=1, source_target_pairs={{0,4},{1,5},{2,6},{3,7},{4,0},{5,1},{6,2},{7,3},{8,12},{9,13},{10,... | collective-permute-start | bytes 589832 | tf_op jit(solution)/shard_map/ppermute | solution.py:295
  63.3 5.9 %collective-permute-start.14 = (bf16[96,1024]{1,0:T(8,128)(2,1)S(1)}, bf16[96,1024]{1,0:T(8,128)(2,1)S(1)}, u32[]{:S(2)}, u32[]{:S(2)}) collective-permute-start(bf16[96,1024]{1,0:T(8,128)(2,1)S(1)} %get-tuple-element.56), channel_id=1, source_target_pairs={{0,2},{1,3},{2,0},{3,1},{4,6},{5,7},{6,4},{7,5},{8,10},{9,11},{10,... | collective-permute-start | bytes 589832 | tf_op jit(solution)/shard_map/ppermute | solution.py:295
  64.8 8.6 %collective-permute-start.17 = (bf16[96,1024]{1,0:T(8,128)(2,1)S(1)}, bf16[96,1024]{1,0:T(8,128)(2,1)S(1)}, u32[]{:S(2)}, u32[]{:S(2)}) collective-permute-start(bf16[96,1024]{1,0:T(8,128)(2,1)S(1)} %get-tuple-element.59), channel_id=1, source_target_pairs={{0,2},{1,3},{2,0},{3,1},{4,6},{5,7},{6,4},{7,5},{8,10},{9,11},{10,... | collective-permute-start | bytes 589832 | tf_op jit(solution)/shard_map/ppermute | solution.py:295
  65.5 7.9 %collective-permute-start.18 = (bf16[96,1024]{1,0:T(8,128)(2,1)S(1)}, bf16[96,1024]{1,0:T(8,128)(2,1)S(1)}, u32[]{:S(2)}, u32[]{:S(2)}) collective-permute-start(bf16[96,1024]{1,0:T(8,128)(2,1)S(1)} %get-tuple-element.60), channel_id=1, source_target_pairs={{0,4},{1,5},{2,6},{3,7},{4,0},{5,1},{6,2},{7,3},{8,12},{9,13},{10,... | collective-permute-start | bytes 589832 | tf_op jit(solution)/shard_map/ppermute | solution.py:295
  73.6 9.9 %collective-permute-start.22 = (bf16[96,1536]{1,0:T(8,128)(2,1)S(1)}, bf16[96,1536]{1,0:T(8,128)(2,1)S(1)}, u32[]{:S(2)}, u32[]{:S(2)}) collective-permute-start(bf16[96,1536]{1,0:T(8,128)(2,1)S(1)} %get-tuple-element.69), channel_id=1, source_target_pairs={{0,2},{1,3},{2,0},{3,1},{4,6},{5,7},{6,4},{7,5},{8,10},{9,11},{10,... | collective-permute-start | bytes 884744 | tf_op jit(solution)/shard_map/ppermute | solution.py:295
  75.0 7.2 %collective-permute-start.21 = (bf16[96,512]{1,0:T(8,128)(2,1)S(1)}, bf16[96,512]{1,0:T(8,128)(2,1)S(1)}, u32[]{:S(2)}, u32[]{:S(2)}) collective-permute-start(bf16[96,512]{1,0:T(8,128)(2,1)S(1)} %get-tuple-element.67), channel_id=1, source_target_pairs={{0,4},{1,5},{2,6},{3,7},{4,0},{5,1},{6,2},{7,3},{8,12},{9,13},{10,... | collective-permute-start | bytes 294920 | tf_op jit(solution)/shard_map/ppermute | solution.py:295
  77.0 18.0 %collective-permute-start.25 = (bf16[96,2048]{1,0:T(8,128)(2,1)S(1)}, bf16[96,2048]{1,0:T(8,128)(2,1)S(1)}, u32[]{:S(2)}, u32[]{:S(2)}) collective-permute-start(bf16[96,2048]{1,0:T(8,128)(2,1)S(1)} %get-tuple-element.72), channel_id=1, source_target_pairs={{0,8},{1,9},{2,10},{3,11},{4,12},{5,13},{6,14},{7,15},{8,0},{9,1},... | collective-permute-start | bytes 1179656 | tf_op jit(solution)/shard_map/ppermute | solution.py:299
  77.5 17.5 %collective-permute-start.20 = (bf16[96,1536]{1,0:T(8,128)(2,1)S(1)}, bf16[96,1536]{1,0:T(8,128)(2,1)S(1)}, u32[]{:S(2)}, u32[]{:S(2)}) collective-permute-start(bf16[96,1536]{1,0:T(8,128)(2,1)S(1)} %get-tuple-element.66), channel_id=1, source_target_pairs={{0,2},{1,3},{2,0},{3,1},{4,6},{5,7},{6,4},{7,5},{8,10},{9,11},{10,... | collective-permute-start | bytes 884744 | tf_op jit(solution)/shard_map/ppermute | solution.py:295
  83.6 11.5 %collective-permute-start.24 = (bf16[96,1536]{1,0:T(8,128)(2,1)S(1)}, bf16[96,1536]{1,0:T(8,128)(2,1)S(1)}, u32[]{:S(2)}, u32[]{:S(2)}) collective-permute-start(bf16[96,1536]{1,0:T(8,128)(2,1)S(1)} %get-tuple-element.71), channel_id=1, source_target_pairs={{0,4},{1,5},{2,6},{3,7},{4,0},{5,1},{6,2},{7,3},{8,12},{9,13},{10,... | collective-permute-start | bytes 884744 | tf_op jit(solution)/shard_map/ppermute | solution.py:295
  84.6 10.4 %collective-permute-start.19 = (bf16[96,512]{1,0:T(8,128)(2,1)S(1)}, bf16[96,512]{1,0:T(8,128)(2,1)S(1)}, u32[]{:S(2)}, u32[]{:S(2)}) collective-permute-start(bf16[96,512]{1,0:T(8,128)(2,1)S(1)} %get-tuple-element.65), channel_id=1, source_target_pairs={{0,4},{1,5},{2,6},{3,7},{4,0},{5,1},{6,2},{7,3},{8,12},{9,13},{10,... | collective-permute-start | bytes 294920 | tf_op jit(solution)/shard_map/ppermute | solution.py:295
  85.6 9.4 %collective-permute-start.23 = (bf16[96,512]{1,0:T(8,128)(2,1)S(1)}, bf16[96,512]{1,0:T(8,128)(2,1)S(1)}, u32[]{:S(2)}, u32[]{:S(2)}) collective-permute-start(bf16[96,512]{1,0:T(8,128)(2,1)S(1)} %get-tuple-element.70), channel_id=1, source_target_pairs={{0,2},{1,3},{2,0},{3,1},{4,6},{5,7},{6,4},{7,5},{8,10},{9,11},{10,... | collective-permute-start | bytes 294920 | tf_op jit(solution)/shard_map/ppermute | solution.py:295

commit v8 on v4

--- a/solution.py
+++ b/solution.py
@@ -12,6 +12,9 @@
 HD = 128
 WSPLIT = 8
 EPS = 1e-06
+FAR_WEIGHT = 3_000_000_000
+FAR_STEPS = 4
+CROSS_WEIGHT = 1
 VMEM_LIMIT = 32 * 1024 * 1024
 
 VMEM = pl.BlockSpec(memory_space=pltpu.VMEM)
@@ -24,13 +27,14 @@
 
 
 def call(
-    kernel, outs, in_specs, name, flops, moved, out_specs=None, aliases=None
+    kernel, outs, in_specs, name, flops, moved, scratch=(), out_specs=None, aliases=None
 ):
     return pl.pallas_call(
         kernel,
         out_shape=outs,
         in_specs=in_specs,
         out_specs=out_specs or jax.tree.map(lambda _: VMEM, outs),
+        scratch_shapes=list(scratch),
         input_output_aliases=aliases or {},
         compiler_params=pltpu.CompilerParams(vmem_limit_bytes=VMEM_LIMIT),
         cost_estimate=pl.CostEstimate(flops=flops, bytes_accessed=moved, transcendentals=0),
@@ -84,13 +88,13 @@
     pass
 
 
-def after_all(values, others):
+def after_all(values, others, weight=1):
     return call(
         gate_kernel,
         [struct(value.shape) for value in values],
         [ANY] * (len(values) + len(others)),
         "hand_on",
-        1,
+        weight,
         1,
         out_specs=[ANY] * len(values),
         aliases={i: i for i in range(len(values))},
@@ -152,53 +156,132 @@
     )(state, query, gain, flat, *kv_pieces, *after)
 
 
-def ffn_kernel(rows_ref, in_a, in_b, out_a, out_b, out_ref):
-    w_in = jnp.concatenate([in_a[...], in_b[...]], axis=1)
-    raw = jnp.dot(rows_ref[...], w_in, preferred_element_type=jnp.float32)
-    activation = jnp.maximum(raw, 0.0).astype(jnp.bfloat16)
-    step = 512
-    for at in range(0, out_ref.shape[1], step):
-        cols = slice(at, at + step)
-        w_out = jnp.concatenate([out_a[:, cols], out_b[:, cols]], axis=0)
-        part = jnp.dot(activation, w_out, preferred_element_type=jnp.float32)
-        out_ref[:, cols] = part.astype(jnp.bfloat16)
-
-
-def ffn(rows, weights):
-    count, width = rows.shape
-    units = weights[0].shape[1]
-    return call(
-        ffn_kernel,
-        struct((count, width)),
-        [VMEM] * 5,
-        "expert_ffn",
-        4 * count * width * units * 2,
-        8 * units * width + 4 * count * width,
-    )(rows, *weights)
-
-
-def finish_kernel(groups, cap, *refs):
-    hidden_ref, gate_ref, flat_ref = refs[:3]
-    sum_refs = refs[3:-1]
-    out_ref = refs[-1]
-    tokens, width = hidden_ref.shape
-    flat = flat_ref[...]
+def place(pipes, shift, pipe, size):
+    at = pipe - shift
+    at = jnp.where(at < 0, at + pipes, at)
+    return pl.multiple_of(at * size, size)
+
+
+def up_kernel(pipes, *refs):
+    pipe = refs[0][0]
+    own_in, z_in, w_own, w_pair = refs[1:5]
+    y_parts = refs[5 : 5 + pipes]
+    pair_parts = refs[5 + pipes : 5 + 2 * pipes]
+    out_ref, entries = refs[-2:]
+    rows, width = own_in.shape
+    units = w_own.shape[1]
+    entries[:rows] = own_in[...]
+    entries[rows:] = z_in[...]
+    weights = jnp.concatenate([w_own[...], w_pair[...]], axis=1)
+    raw = jnp.dot(entries[...], weights, preferred_element_type=jnp.float32)
+    out_ref[:, : 2 * units] = jnp.maximum(raw, 0.0).astype(jnp.bfloat16)
+    depth = width // pipes
+    raw = jnp.zeros_like(raw)
+    for shift in range(pipes):
+        part = entries[:, pl.ds(place(pipes, shift, pipe, depth), depth)]
+        weights = jnp.concatenate([y_parts[shift][...], pair_parts[shift][...]], axis=1)
+        raw = raw + jnp.dot(part, weights, preferred_element_type=jnp.float32)
+    out_ref[:, 2 * units :] = jnp.maximum(raw, 0.0).astype(jnp.bfloat16)
+
+
+def up(pipe, own, z, w_in, y_parts, pair_parts, after=()):
+    rows, width = own.shape
+    units = w_in[0].shape[1]
+    pipes = len(y_parts)
+    return call(
+        functools.partial(up_kernel, pipes),
+        struct((2 * rows, 4 * units)),
+        [SMEM] + [VMEM] * (4 + 2 * pipes) + [ANY] * len(after),
+        "expert_up",
+        16 * rows * width * units,
+        8 * units * width,
+        scratch=[pltpu.VMEM((2 * rows, width), jnp.bfloat16)],
+    )(pipe, own, z, *w_in, *y_parts, *pair_parts, *after)
+
+
+def down_kernel(pipes, *refs):
+    pipe = refs[0][0]
+    act_ref, w_own, w_pair = refs[1:4]
+    y_parts, refs = refs[4 : 4 + pipes], refs[4 + pipes :]
+    pair_parts, refs = refs[:pipes], refs[pipes:]
+    y_rest, pair_rest = refs[:2]
+    own_ref, z_ref, held = refs[-3:]
+    rows, width = own_ref.shape
+    units = w_own.shape[0]
+    size = y_parts[0].shape[0]
+    for shift in range(pipes):
+        at = place(pipes, shift, pipe, size)
+        held[pl.ds(at, size)] = y_parts[shift][...]
+        held[pl.ds(pl.multiple_of(units + at, size), size)] = pair_parts[shift][...]
+    held[pipes * size : units] = y_rest[...]
+    held[units + pipes * size :] = pair_rest[...]
     step = 512
     for at in range(0, width, step):
         cols = slice(at, at + step)
-        picked = jnp.zeros((tokens, step), jnp.float32)
-        for group in range(groups):
-            slots = lax.broadcasted_iota(jnp.int32, (tokens, cap), 1) + group * cap
-            picker = (slots == flat).astype(jnp.float32).astype(jnp.bfloat16)
-            picked = picked + jnp.dot(
-                picker, sum_refs[group][:, cols], preferred_element_type=jnp.float32
-            )
+        weights = jnp.concatenate([w_own[:, cols], w_pair[:, cols], held[:, cols]], axis=0)
+        part = jnp.dot(act_ref[...], weights, preferred_element_type=jnp.float32)
+        part = part.astype(jnp.bfloat16)
+        own_ref[:, cols] = part[:rows]
+        z_ref[:, cols] = part[rows:]
+
+
+def down(pipe, act, w_out, y_parts, pair_parts, rests, after=()):
+    rows = act.shape[0] // 2
+    units, width = w_out[0].shape
+    pipes = len(y_parts)
+    return call(
+        functools.partial(down_kernel, pipes),
+        [struct((rows, width))] * 2,
+        [SMEM] + [VMEM] * (5 + 2 * pipes) + [ANY] * len(after),
+        "expert_down",
+        16 * rows * width * units,
+        8 * units * width,
+        scratch=[pltpu.VMEM((2 * units, width), jnp.bfloat16)],
+    )(pipe, act, *w_out, *y_parts, *pair_parts, *rests, *after)
+
+
+def total_kernel(held, own_ref, z_ref, *refs):
+    refs[held][...] = (own_ref[...].astype(jnp.float32) + z_ref[...].astype(jnp.float32)).astype(
+        jnp.bfloat16
+    )
+
+
+def total(own, z, held):
+    outs = [struct(own.shape)] + [struct(value.shape) for value in held]
+    return call(
+        functools.partial(total_kernel, len(held)),
+        outs,
+        [VMEM] * 2 + [ANY] * len(held),
+        "far_total",
+        own.size,
+        6 * own.size,
+        out_specs=[VMEM] + [ANY] * len(held),
+        aliases={2 + i: 1 + i for i in range(len(held))},
+    )(own, z, *held)
+
+
+def finish_kernel(groups, cap, *refs):
+    hidden_ref, gate_ref, flat_ref = refs[:3]
+    own_ref, z_ref = refs[3:5]
+    back_refs = refs[5:-1]
+    out_ref = refs[-1]
+    tokens, width = hidden_ref.shape
+    slots = lax.broadcasted_iota(jnp.int32, (tokens, groups * cap), 1)
+    picker = (slots == flat_ref[...]).astype(jnp.float32).astype(jnp.bfloat16)
+    step = 512
+    for at in range(0, width, step):
+        cols = slice(at, at + step)
+        near = (own_ref[:, cols].astype(jnp.float32) + z_ref[:, cols].astype(jnp.float32)).astype(
+            jnp.bfloat16
+        )
+        found = jnp.concatenate([near] + [r[:, cols] for r in back_refs], axis=0)
+        picked = jnp.dot(picker, found, preferred_element_type=jnp.float32)
         out_ref[:, cols] = (hidden_ref[:, cols] + gate_ref[...] * picked).astype(jnp.bfloat16)
 
 
-def finish(hidden, gate, flat, sums, groups, cap):
+def finish(hidden, gate, flat, sums, backs, groups, cap):
     tokens, width = hidden.shape
-    operands = [hidden, gate, flat, *sums]
+    operands = [hidden, gate, flat, *sums, *backs]
     return call(
         functools.partial(finish_kernel, groups, cap),
         struct((tokens, width)),
@@ -228,7 +311,22 @@
     for shift in range(1, pipes):
         perm = [(i, (i + shift) % pipes) for i in range(pipes)]
         kv_pieces.append(lax.ppermute(kv, "pipe", perm))
-    weights = [w_in, across(w_in, 1), w_out, across(w_out, 1)]
+    def along(value):
+        perms = [[(i, (i + shift) % pipes) for i in range(pipes)] for shift in range(1, pipes)]
+        return [value] + [lax.ppermute(value, "pipe", perm) for perm in perms]
+
+    def paired(parts):
+        return [across(value, 1) for value in parts]
+
+    pipe = lax.axis_index("pipe").astype(jnp.int32)
+    w_in_pair, w_out_pair = across(w_in, 1), across(w_out, 1)
+    units = w_in.shape[1]
+    depth, size = width // pipes, units // 2 // pipes // 16 * 16
+    in_part = lax.dynamic_slice_in_dim(w_in, pipe * depth, depth, 0)
+    out_part = lax.dynamic_slice_in_dim(w_out, pipe * size, size, 0)
+    out_rest = w_out[pipes * size :]
+    pipe = pipe.reshape(1)
+    in_y = across(in_part, 2)
 
     group = (lax.axis_index("expert") // WSPLIT).astype(jnp.int32).reshape(1)
     staged = stage(
@@ -244,38 +342,42 @@
     )
     flat, gates = staged[4:]
     hidden, near, *packed = attend(
-        *staged[:4], kv_pieces, groups, cap, after=[weights[1], weights[3]]
+        *staged[:4], kv_pieces, groups, cap, after=[w_in_pair, w_out_pair]
     )
     far = [groups_on(block, count) for count, block in enumerate(packed, 1)]
     far = jnp.concatenate(far, axis=0) if len(far) > 1 else far[0]
 
-    squares = [
-        [base + core + 2 * chip for chip in range(WSPLIT // 2)]
-        for base in range(0, devices, WSPLIT)
-        for core in range(2)
-    ]
-
-    def spread(rows):
-        return lax.all_gather(rows, "expert", axis_index_groups=squares, axis=0, tiled=True)
-
-    def experts(spread):
-        partial_value = ffn(spread, weights)
-        return lax.psum_scatter(
-            partial_value,
-            "expert",
-            scatter_dimension=0,
-            axis_index_groups=squares,
-            tiled=True,
-        )
-
-    near = spread(near)
-    far = spread(*after_all([far], [near]))
-    near_sum, far_sum = experts(near), experts(far)
+    (in_y,) = after_all([in_y], [near])
+    out_part, out_rest = after_all([out_part, out_rest], [in_y])
+    in_y = after_all(along(in_y), [])
+    in_pair = paired(in_y)
+    out_y = across(out_part, 2)
+    out_y = after_all(along(out_y), [])
+    out_pair = paired(out_y)
+    rest_y = across(out_rest, 2)
+    rests = [rest_y, across(rest_y, 1)]
+
+    near_z = across(near, 4)
+    (far,) = after_all([far], [near_z], CROSS_WEIGHT)
+    far_z = across(far, 4)
+    for _ in range(FAR_STEPS):
+        (far_z,) = after_all([far_z], [], FAR_WEIGHT)
+
+    def experts_up(own, z, after=()):
+        return up(pipe, own, z, [w_in, w_in_pair], in_y, in_pair, after)
+
+    def experts_down(act, after=()):
+        return down(pipe, act, [w_out, w_out_pair], out_y, out_pair, rests, after)
+
+    far_own, far_sent = experts_down(experts_up(far, far_z))
+    near_own, near_sent = experts_down(experts_up(near, near_z, [far_own]))
+    far_sum, near_sent = total(far_own, across(far_sent, 4), [near_sent])
     backs = [
         groups_on(far_sum[(count - 1) * cap : count * cap], groups - count)
         for count in range(1, groups)
     ]
-    output = finish(hidden, gates, flat, [near_sum, *backs], groups, cap)
+    near_sums = [near_own, across(near_sent, 4)]
+    output = finish(hidden, gates, flat, near_sums, backs, groups, cap)
     return output.reshape(1, 1, tokens, width)
 
 

time: 191 us -> 97.6 us (0.51)
  waiting for transfers between devices: 137 us -> 51.2 us
  starting transfers between devices: 8.92 us -> 24.1 us
  between operations: 13.2 us -> 0.15 us
  local copies, waits for them, and re-layouts: 21.4 us -> 9.14 us
  Pallas kernels: 9.84 us -> 12.5 us
    reduce_scatter x2 -> x0, waiting for transfers between devices: 62 us -> none  [experts(): lax.psum_scatter(partial_value, 'expert', scatter_dimension=0, axis_index...]
    all_gather x2 -> x0, waiting for transfers between devices: 55.6 us -> none  [spread(): lax.all_gather(rows, 'expert', axis_index_groups=squares, axis=0, tiled=T...]
    ppermute x2 -> x14, waiting for transfers between devices: 0.01 us -> 33.1 us  [across(): return lax.ppermute(value, 'expert', [(i, i ^ bit) for i in range(devices)])]
    unnamed x40 -> x26, local copies, waits for them, and re-layouts: 20.4 us -> 4.72 us
    ppermute x2 -> x14, starting transfers between devices: 0.51 us -> 13.4 us  [across(): return lax.ppermute(value, 'expert', [(i, i ^ bit) for i in range(devices)])]
    ppermute x2, waiting for transfers between devices: 17.4 us -> 11.9 us  [groups_on(): lax.ppermute(value, 'expert', [(i, (i + shift) % devices) for i in range(...]
    ppermute x0 -> x2, waiting for transfers between devices: none -> 4.58 us  [along(): return [value] + [lax.ppermute(value, 'pipe', perm) for perm in perms]]
    ppermute x0 -> x2, starting transfers between devices: none -> 3.22 us  [along(): return [value] + [lax.ppermute(value, 'pipe', perm) for perm in perms]]
  transfers between devices with their start and end apart: 9 -> 19, of which waited for: 6 -> 11; matrix products, arithmetic and copies ran while one was open for 1% -> 5% of each run, Pallas kernels for 2% -> 10%
where the time goes in v8:
time: 97.6 us; the launch traced here: 97.2 us
  waiting for transfers between devices  51.2 us (52%)
  starting transfers between devices  24.1 us (25%)
  Pallas kernels  12.5 us (13%)
  local copies, waits for them, and re-layouts  9.14 us (9%)
    ppermute x14, waiting for transfers between devices, across(): return lax.ppermute(value, 'expert', [(i, i ^ bit) for i in range(devices)])  33.1 us
    ppermute x14, starting transfers between devices, across(): return lax.ppermute(value, 'expert', [(i, i ^ bit) for i in range(devices)])  13.4 us
    ppermute x2, waiting for transfers between devices, groups_on(): lax.ppermute(value, 'expert', [(i, (i + shift) % devices) for i in range(...  11.9 us
    ppermute x2, starting transfers between devices, groups_on(): lax.ppermute(value, 'expert', [(i, (i + shift) % devices) for i in range(...  5.97 us
    pallas_call x2, Pallas kernels, up(): call(functools.partial(up_kernel, pipes), struct((2 * rows, 4 * units)),...  5.82 us
    unnamed x26, local copies, waits for them, and re-layouts  4.72 us
    ppermute x2, waiting for transfers between devices, along(): return [value] + [lax.ppermute(value, 'pipe', perm) for perm in perms]  4.58 us
    ppermute x2, starting transfers between devices, along(): return [value] + [lax.ppermute(value, 'pipe', perm) for perm in perms]  3.22 us
  transfers between devices with their start and end apart: 19, of which 11 were waited for; matrix products, arithmetic and copies ran while one was open for 5% of the time, Pallas kernels for 10%

profile of v8, /device:TPU:0, one launch (start us, length us, event | category | flops | bytes accessed | tf_op | source)
XLA Modules:
  0.0 97.2 jit_solution(7436384441286761763)
XLA Ops:
  0.0 0.5 collective-permute-start.1
  0.5 0.1 collective-permute-start.2
  0.6 2.1 %constant_dynamic-slice_fusion.1 = bf16[1024,384]{1,0:T(8,128)(2,1)} fusion(bf16[2048,384]{1,0:T(8,128)(2,1)} %refs_3_.3, s32[]{:T(128)S(6)} %select_n.12), kind=kLoop, calls=%fused_computation.1 | loop fusion | bytes 1572868 | tf_op jit(solution)/shard_map/dynamic_slice | solution.py:325
  2.8 2.9 %collective-permute-start.4 = (bf16[1024,384]{1,0:T(8,128)(2,1)}, bf16[1024,384]{1,0:T(8,128)(2,1)S(1)}, u32[]{:S(2)}, u32[]{:S(2)}) collective-permute-start(bf16[1024,384]{1,0:T(8,128)(2,1)} %constant_dynamic-slice_fusion.1), channel_id=1, source_target_pairs={{0,2},{1,3},{2,0},{3,1},{4,6},{5,7},{6,4},{7,5},{8,10},{9,11},{10,... | collective-permute-start | bytes 2359304 | tf_op jit(solution)/shard_map/ppermute | solution.py:303
  5.7 0.1 copy.23
  5.8 1.6 %collective-permute-start = (bf16[64,2048]{1,0:T(8,128)(2,1)S(1)}, bf16[64,2048]{1,0:T(8,128)(2,1)}, u32[]{:S(2)}, u32[]{:S(2)}) collective-permute-start(bf16[64,2048]{1,0:T(8,128)(2,1)S(1)} %bitcast.13), channel_id=1, source_target_pairs={{0,16},{16,0},{1,17},{17,1},{2,18},{18,2},{3,19},{19,3},{4,20},{20... | collective-permute-start | bytes 786440 | tf_op jit(solution)/shard_map/ppermute | solution.py:313
  7.4 0.0 copy-start.7
  7.4 1.0 %copy-done.7 = bf16[1,1,128,2048]{3,2,1,0:T(8,128)(2,1)S(1)} copy-done((bf16[1,1,128,2048]{3,2,1,0:T(8,128)(2,1)S(1)}, bf16[1,1,128,2048]{3,2,1,0:T(8,128)(2,1)}, u32[]{:S(2)}) %copy-start.7) | copy-done | bytes 524312
  8.4 0.1 stage.1
  8.6 0.8 copy-done.2
  9.3 0.8 copy-done.4
  10.1 1.2 %slice.3.refs_1_ = bf16[192,2048]{1,0:T(8,128)(2,1)S(1)} slice(bf16[384,2048]{1,0:T(8,128)(2,1)} %refs_2_.3), slice={[192:384], [0:2048]} | slice | bytes 1572864 | tf_op jit(solution)/shard_map/slice | solution.py:327
  11.3 1.0 %constant_dynamic-slice_fusion.refs_0_ = bf16[96,2048]{1,0:T(8,128)(2,1)S(1)} fusion(bf16[384,2048]{1,0:T(8,128)(2,1)} %refs_2_.3, s32[]{:T(128)S(6)} %select_n.13), kind=kLoop, calls=%fused_computation | loop fusion | bytes 786436 | tf_op jit(solution)/shard_map/dynamic_slice | solution.py:326
  12.3 1.6 %collective-permute-done.refs_5_ = bf16[64,2048]{1,0:T(8,128)(2,1)} collective-permute-done((bf16[64,2048]{1,0:T(8,128)(2,1)S(1)}, bf16[64,2048]{1,0:T(8,128)(2,1)}, u32[]{:S(2)}, u32[]{:S(2)}) %collective-permute-start) | collective-permute-done | bytes 262176 | tf_op jit(solution)/shard_map/ppermute | solution.py:313
  14.0 0.0 collective-permute-done.1.refs_6_.refs_4_
  14.0 0.0 collective-permute-done.2.refs_7_.refs_3_
  14.0 1.0 %copy-done.3 = bf16[128,2048]{1,0:T(8,128)(2,1)S(1)} copy-done((bf16[128,2048]{1,0:T(8,128)(2,1)S(1)}, bf16[128,2048]{1,0:T(8,128)(2,1)}, u32[]{:S(2)}) %copy-start.3) | copy-done | bytes 524312
  15.0 1.0 %copy-done.5 = bf16[128,2048]{1,0:T(8,128)(2,1)S(1)} copy-done((bf16[128,2048]{1,0:T(8,128)(2,1)S(1)}, bf16[128,2048]{1,0:T(8,128)(2,1)}, u32[]{:S(2)}) %copy-start.5) | copy-done | bytes 524312
  16.1 2.4 %attend.1 = (f32[128,2048]{1,0:T(8,128)S(1)}, bf16[96,2048]{1,0:T(8,128)(2,1)S(1)}, bf16[96,2048]{1,0:T(8,128)(2,1)S(1)}) custom-call(bf16[128,2048]{1,0:T(8,128)(2,1)S(1)} %copy-done.3, bf16[128,2048]{1,0:T(8,128)(2,1)S(1)} %copy-done.5, f32[1,2048]{1,0:T(1,128)S(1)} %get-tuple-element.28.refs_2_, s32[1,128]{1,0:T(1,128)S(1)} %get-tuple-element.29.refs_3_, ...), custom_call_target="tpu_custom_call" | custom-call | flops 134217728 | bytes 3145728 | tf_op jit(solution)/shard_map/attend/pallas_call | solution.py:149
  18.4 5.3 %collective-permute-done.4.refs_0_ = bf16[1024,384]{1,0:T(8,128)(2,1)S(1)} collective-permute-done((bf16[1024,384]{1,0:T(8,128)(2,1)}, bf16[1024,384]{1,0:T(8,128)(2,1)S(1)}, u32[]{:S(2)}, u32[]{:S(2)}) %collective-permute-start.4) | collective-permute-done | bytes 786464 | tf_op jit(solution)/shard_map/ppermute | solution.py:303
  23.7 1.7 %collective-permute-start.10 = (bf16[96,2048]{1,0:T(8,128)(2,1)S(1)}, bf16[96,2048]{1,0:T(8,128)(2,1)S(1)}, u32[]{:S(2)}, u32[]{:S(2)}) collective-permute-start(bf16[96,2048]{1,0:T(8,128)(2,1)S(1)} %get-tuple-element.37), channel_id=1, source_target_pairs={{0,2},{1,3},{2,0},{3,1},{4,6},{5,7},{6,4},{7,5},{8,10},{9,11},{10,... | collective-permute-start | bytes 1179656 | tf_op jit(solution)/shard_map/ppermute | solution.py:303
  25.4 1.5 %collective-permute-start.5 = (bf16[1024,384]{1,0:T(8,128)(2,1)S(1)}, bf16[1024,384]{1,0:T(8,128)(2,1)S(1)}, u32[]{:S(2)}, u32[]{:S(2)}) collective-permute-start(bf16[1024,384]{1,0:T(8,128)(2,1)S(1)} %hand_on.9.refs_0_.refs_2_), channel_id=1, source_target_pairs={{0,16},{16,0},{1,17},{17,1},{2,18},{18,2},{3,19},{19,3},{4,20},{20... | collective-permute-start | bytes 2359304 | tf_op jit(solution)/shard_map/ppermute | solution.py:316
  26.9 2.6 %collective-permute-start.8 = (bf16[96,2048]{1,0:T(8,128)(2,1)S(1)}, bf16[96,2048]{1,0:T(8,128)(2,1)S(1)}, u32[]{:S(2)}, u32[]{:S(2)}) collective-permute-start(bf16[96,2048]{1,0:T(8,128)(2,1)S(1)} %get-tuple-element.36), channel_id=1, source_target_pairs={{0,8},{1,9},{2,10},{3,11},{4,12},{5,13},{6,14},{7,15},{8,0},{9,1},... | collective-permute-start | bytes 1179656 | tf_op jit(solution)/shard_map/ppermute | solution.py:307
  29.5 1.6 %collective-permute-start.3 = (bf16[96,2048]{1,0:T(8,128)(2,1)S(1)}, bf16[96,2048]{1,0:T(8,128)(2,1)S(1)}, u32[]{:S(2)}, u32[]{:S(2)}) collective-permute-start(bf16[96,2048]{1,0:T(8,128)(2,1)S(1)} %get-tuple-element.33.refs_1_), channel_id=1, source_target_pairs={{0,4},{1,5},{2,6},{3,7},{4,0},{5,1},{6,2},{7,3},{8,12},{9,13},{10,... | collective-permute-start | bytes 1179656 | tf_op jit(solution)/shard_map/ppermute | solution.py:303
  31.1 0.5 collective-permute-start.14
  31.6 4.1 %collective-permute-done.10.refs_0_ = bf16[96,2048]{1,0:T(8,128)(2,1)S(1)} collective-permute-done((bf16[96,2048]{1,0:T(8,128)(2,1)S(1)}, bf16[96,2048]{1,0:T(8,128)(2,1)S(1)}, u32[]{:S(2)}, u32[]{:S(2)}) %collective-permute-start.10) | collective-permute-done | bytes 393248 | tf_op jit(solution)/shard_map/ppermute | solution.py:303
  35.7 1.7 %collective-permute-start.11 = (bf16[96,2048]{1,0:T(8,128)(2,1)S(1)}, bf16[96,2048]{1,0:T(8,128)(2,1)S(1)}, u32[]{:S(2)}, u32[]{:S(2)}) collective-permute-start(bf16[96,2048]{1,0:T(8,128)(2,1)S(1)} %collective-permute-done.10.refs_0_), channel_id=1, source_target_pairs={{0,16},{16,0},{1,17},{17,1},{2,18},{18,2},{3,19},{19,3},{4,20},{20... | collective-permute-start | bytes 1179656 | tf_op jit(solution)/shard_map/ppermute | solution.py:316
  37.5 8.6 %collective-permute-done.8.refs_0_ = bf16[96,2048]{1,0:T(8,128)(2,1)S(1)} collective-permute-done((bf16[96,2048]{1,0:T(8,128)(2,1)S(1)}, bf16[96,2048]{1,0:T(8,128)(2,1)S(1)}, u32[]{:S(2)}, u32[]{:S(2)}) %collective-permute-start.8) | collective-permute-done | bytes 393248 | tf_op jit(solution)/shard_map/ppermute | solution.py:307
  46.1 0.2 collective-permute-done.3.refs_1_.refs_2_
  46.3 1.4 %collective-permute-start.9 = (bf16[96,2048]{1,0:T(8,128)(2,1)S(1)}, bf16[96,2048]{1,0:T(8,128)(2,1)S(1)}, u32[]{:S(2)}, u32[]{:S(2)}) collective-permute-start(bf16[96,2048]{1,0:T(8,128)(2,1)S(1)} %hand_on.11.refs_1_), channel_id=1, source_target_pairs={{0,4},{1,5},{2,6},{3,7},{4,0},{5,1},{6,2},{7,3},{8,12},{9,13},{10,... | collective-permute-start | bytes 1179656 | tf_op jit(solution)/shard_map/ppermute | solution.py:303
  47.7 4.6 %collective-permute-done.11.refs_1_ = bf16[96,2048]{1,0:T(8,128)(2,1)S(1)} collective-permute-done((bf16[96,2048]{1,0:T(8,128)(2,1)S(1)}, bf16[96,2048]{1,0:T(8,128)(2,1)S(1)}, u32[]{:S(2)}, u32[]{:S(2)}) %collective-permute-start.11) | collective-permute-done | bytes 393248 | tf_op jit(solution)/shard_map/ppermute | solution.py:316
  52.3 0.5 collective-permute-start.13
  52.8 0.0 collective-permute-start.6
  52.8 3.2 %collective-permute-done.9.refs_0_ = bf16[96,2048]{1,0:T(8,128)(2,1)S(1)} collective-permute-done((bf16[96,2048]{1,0:T(8,128)(2,1)S(1)}, bf16[96,2048]{1,0:T(8,128)(2,1)S(1)}, u32[]{:S(2)}, u32[]{:S(2)}) %collective-permute-start.9) | collective-permute-done | bytes 393248 | tf_op jit(solution)/shard_map/ppermute | solution.py:303
  56.0 0.5 collective-permute-start.15
  56.5 1.8 %collective-permute-done.7.refs_8_ = bf16[1024,384]{1,0:T(8,128)(2,1)S(1)} collective-permute-done((bf16[1024,384]{1,0:T(8,128)(2,1)S(1)}, bf16[1024,384]{1,0:T(8,128)(2,1)S(1)}, u32[]{:S(2)}, u32[]{:S(2)}) %collective-permute-start.7) | collective-permute-done | bytes 786464 | tf_op jit(solution)/shard_map/ppermute | solution.py:303
  58.3 3.0 %expert_up.2.refs_1_ = bf16[192,1536]{1,0:T(8,128)(2,1)S(1)} custom-call(s32[1]{0:T(128)} %bitcast.10.refs_0_, bf16[96,2048]{1,0:T(8,128)(2,1)S(1)} %hand_on.11.refs_1_, bf16[96,2048]{1,0:T(8,128)(2,1)S(1)} %hand_on.15.refs_2_, bf16[2048,384]{1,0:T(8,128)(2,1)S(1)} %copy-done.1, bf16[2048,384]{1,0:T(8,128)(2,1)} %collective-permute-done.1.refs_6_.refs_4_, ...), custom_call_target="tpu_custom_call" | custom-call | flops 1207959552 | bytes 6291456 | tf_op jit(solution)/shard_map/expert_up/pallas_call | solution.py:191
  61.3 1.5 %expert_down.2 = (bf16[96,2048]{1,0:T(8,128)(2,1)S(1)}, bf16[96,2048]{1,0:T(8,128)(2,1)S(1)}) custom-call(s32[1]{0:T(128)} %bitcast.10.refs_0_, bf16[192,1536]{1,0:T(8,128)(2,1)S(1)} %expert_up.2.refs_1_, bf16[384,2048]{1,0:T(8,128)(2,1)S(1)} %copy-done, bf16[384,2048]{1,0:T(8,128)(2,1)S(1)} %collective-permute-done.2.refs_7_.refs_3_, ...), custom_call_target="tpu_custom_call" | custom-call | flops 1207959552 | bytes 6291456 | tf_op jit(solution)/shard_map/expert_down/pallas_call | solution.py:232
  62.8 1.8 %collective-permute-start.16 = (bf16[96,2048]{1,0:T(8,128)(2,1)S(1)}, bf16[96,2048]{1,0:T(8,128)(2,1)S(1)}, u32[]{:S(2)}, u32[]{:S(2)}) collective-permute-start(bf16[96,2048]{1,0:T(8,128)(2,1)S(1)} %get-tuple-element.43), channel_id=1, source_target_pairs={{0,4},{1,5},{2,6},{3,7},{4,0},{5,1},{6,2},{7,3},{8,12},{9,13},{10,... | collective-permute-start | bytes 1179656 | tf_op jit(solution)/shard_map/ppermute | solution.py:303
  64.5 2.8 %expert_up.3.refs_1_ = bf16[192,1536]{1,0:T(8,128)(2,1)S(1)} custom-call(s32[1]{0:T(128)} %bitcast.10.refs_0_, bf16[96,2048]{1,0:T(8,128)(2,1)S(1)} %get-tuple-element.33.refs_1_, bf16[96,2048]{1,0:T(8,128)(2,1)S(1)} %collective-permute-done.3.refs_1_.refs_2_, bf16[2048,384]{1,0:T(8,128)(2,1)S(1)} %copy-done.1, ...), custom_call_target="tpu_custom_call" | custom-call | flops 1207959552 | bytes 6291456 | tf_op jit(solution)/shard_map/expert_up/pallas_call | solution.py:191
  67.4 1.5 %expert_down.3 = (bf16[96,2048]{1,0:T(8,128)(2,1)S(1)}, bf16[96,2048]{1,0:T(8,128)(2,1)S(1)}) custom-call(s32[1]{0:T(128)} %bitcast.10.refs_0_, bf16[192,1536]{1,0:T(8,128)(2,1)S(1)} %expert_up.3.refs_1_, bf16[384,2048]{1,0:T(8,128)(2,1)S(1)} %copy-done, bf16[384,2048]{1,0:T(8,128)(2,1)S(1)} %collective-permute-done.2.refs_7_.refs_3_, ...), custom_call_target="tpu_custom_call" | custom-call | flops 1207959552 | bytes 6291456 | tf_op jit(solution)/shard_map/expert_down/pallas_call | solution.py:232
  68.9 5.1 %collective-permute-done.16.z_ref = bf16[96,2048]{1,0:T(8,128)(2,1)S(1)} collective-permute-done((bf16[96,2048]{1,0:T(8,128)(2,1)S(1)}, bf16[96,2048]{1,0:T(8,128)(2,1)S(1)}, u32[]{:S(2)}, u32[]{:S(2)}) %collective-permute-start.16) | collective-permute-done | bytes 393248 | tf_op jit(solution)/shard_map/ppermute | solution.py:303
  74.0 0.1 far_total.1
  74.1 1.8 %collective-permute-start.17 = (bf16[96,2048]{1,0:T(8,128)(2,1)S(1)}, bf16[96,2048]{1,0:T(8,128)(2,1)S(1)}, u32[]{:S(2)}, u32[]{:S(2)}) collective-permute-start(bf16[96,2048]{1,0:T(8,128)(2,1)S(1)} %get-tuple-element.45), channel_id=1, source_target_pairs={{0,4},{1,5},{2,6},{3,7},{4,0},{5,1},{6,2},{7,3},{8,12},{9,13},{10,... | collective-permute-start | bytes 1179656 | tf_op jit(solution)/shard_map/ppermute | solution.py:303
  75.9 3.4 %collective-permute-start.18 = (bf16[96,2048]{1,0:T(8,128)(2,1)S(1)}, bf16[96,2048]{1,0:T(8,128)(2,1)S(1)}, u32[]{:S(2)}, u32[]{:S(2)}) collective-permute-start(bf16[96,2048]{1,0:T(8,128)(2,1)S(1)} %get-tuple-element.46), channel_id=1, source_target_pairs={{0,8},{1,9},{2,10},{3,11},{4,12},{5,13},{6,14},{7,15},{8,0},{9,1},... | collective-permute-start | bytes 1179656 | tf_op jit(solution)/shard_map/ppermute | solution.py:307
  79.2 13.4 %collective-permute-done.17.refs_4_ = bf16[96,2048]{1,0:T(8,128)(2,1)S(1)} collective-permute-done((bf16[96,2048]{1,0:T(8,128)(2,1)S(1)}, bf16[96,2048]{1,0:T(8,128)(2,1)S(1)}, u32[]{:S(2)}, u32[]{:S(2)}) %collective-permute-start.17) | collective-permute-done | bytes 393248 | tf_op jit(solution)/shard_map/ppermute | solution.py:303
  92.7 3.3 %collective-permute-done.18.refs_5_ = bf16[96,2048]{1,0:T(8,128)(2,1)S(1)} collective-permute-done((bf16[96,2048]{1,0:T(8,128)(2,1)S(1)}, bf16[96,2048]{1,0:T(8,128)(2,1)S(1)}, u32[]{:S(2)}, u32[]{:S(2)}) %collective-permute-start.18) | collective-permute-done | bytes 393248 | tf_op jit(solution)/shard_map/ppermute | solution.py:307
  96.0 1.2 %finish.1 = bf16[128,2048]{1,0:T(8,128)(2,1)} custom-call(f32[128,2048]{1,0:T(8,128)S(1)} %get-tuple-element.30.refs_0_, f32[128,1]{1,0:T(8,128)S(1)} %get-tuple-element.31.refs_1_, s32[128,1]{1,0:T(8,128)S(1)} %get-tuple-element.32.refs_2_, bf16[96,2048]{1,0:T(8,128)(2,1)S(1)} %get-tuple-element.42.refs_3_, ...), custom_call_target="tpu_custom_call" | custom-call | flops 201326592 | bytes 4194304 | tf_op jit(solution)/shard_map/finish/pallas_call | solution.py:285
  (37 shorter events, 0.1 us)
Async XLA Ops:
  0.0 7.3 %copy-start.11 = (f32[1,1,128]{2,1,0:T(1,128)S(1)}, f32[1,1,128]{2,1,0:T(1,128)}, u32[]{:S(2)}) copy-start(f32[1,1,128]{2,1,0:T(1,128)} %param.17) | copy-start | bytes 1540
  0.0 7.3 %copy-start.10 = (s32[1,1,128]{2,1,0:T(1,128)S(1)}, s32[1,1,128]{2,1,0:T(1,128)}, u32[]{:S(2)}) copy-start(s32[1,1,128]{2,1,0:T(1,128)} %param.16) | copy-start | bytes 1540
  0.0 7.3 %copy-start.9 = (s32[1,1,128]{2,1,0:T(1,128)S(1)}, s32[1,1,128]{2,1,0:T(1,128)}, u32[]{:S(2)}) copy-start(s32[1,1,128]{2,1,0:T(1,128)} %param.15) | copy-start | bytes 1540
  0.0 7.3 %copy-start.8 = (f32[2048]{0:T(1024)S(1)}, f32[2048]{0:T(1024)}, u32[]{:S(2)}) copy-start(f32[2048]{0:T(1024)} %param.12) | copy-start | bytes 24580
  0.0 7.4 %copy-start.6 = (bf16[1,1,128,2048]{3,2,1,0:T(8,128)(2,1)S(1)}, bf16[1,1,128,2048]{3,2,1,0:T(8,128)(2,1)}, u32[]{:S(2)}) copy-start(bf16[1,1,128,2048]{3,2,1,0:T(8,128)(2,1)} %param.9) | copy-start | bytes 1572868
  0.0 14.0 %collective-permute-start.1 = (bf16[2048,384]{1,0:T(8,128)(2,1)}, bf16[2048,384]{1,0:T(8,128)(2,1)}, u32[]{:S(2)}, u32[]{:S(2)}) collective-permute-start(bf16[2048,384]{1,0:T(8,128)(2,1)} %refs_3_.3), channel_id=1, source_target_pairs={{0,1},{1,0},{2,3},{3,2},{4,5},{5,4},{6,7},{7,6},{8,9},{9,8},{10,11... | collective-permute-start | bytes 4718600 | tf_op jit(solution)/shard_map/ppermute | solution.py:303
  0.5 13.4 %collective-permute-start.2 = (bf16[384,2048]{1,0:T(8,128)(2,1)}, bf16[384,2048]{1,0:T(8,128)(2,1)S(1)}, u32[]{:S(2)}, u32[]{:S(2)}) collective-permute-start(bf16[384,2048]{1,0:T(8,128)(2,1)} %refs_2_.3), channel_id=1, source_target_pairs={{0,1},{1,0},{2,3},{3,2},{4,5},{5,4},{6,7},{7,6},{8,9},{9,8},{10,11... | collective-permute-start | bytes 4718600 | tf_op jit(solution)/shard_map/ppermute | solution.py:303
  0.6 5.1 %copy-start.12 = (bf16[1,32,2,2048]{3,2,1,0:T(2,128)(2,1)S(1)}, bf16[1,32,2,2048]{3,2,1,0:T(2,128)(2,1)}, u32[]{:S(2)}) copy-start(bf16[1,32,2,2048]{3,2,1,0:T(2,128)(2,1)} %param.11) | copy-start | bytes 786436
  2.8 20.9 %collective-permute-start.4 = (bf16[1024,384]{1,0:T(8,128)(2,1)}, bf16[1024,384]{1,0:T(8,128)(2,1)S(1)}, u32[]{:S(2)}, u32[]{:S(2)}) collective-permute-start(bf16[1024,384]{1,0:T(8,128)(2,1)} %constant_dynamic-slice_fusion.1), channel_id=1, source_target_pairs={{0,2},{1,3},{2,0},{3,1},{4,6},{5,7},{6,4},{7,5},{8,10},{9,11},{10,... | collective-permute-start | bytes 2359304 | tf_op jit(solution)/shard_map/ppermute | solution.py:303
  5.8 8.2 %collective-permute-start = (bf16[64,2048]{1,0:T(8,128)(2,1)S(1)}, bf16[64,2048]{1,0:T(8,128)(2,1)}, u32[]{:S(2)}, u32[]{:S(2)}) collective-permute-start(bf16[64,2048]{1,0:T(8,128)(2,1)S(1)} %bitcast.13), channel_id=1, source_target_pairs={{0,16},{16,0},{1,17},{17,1},{2,18},{18,2},{3,19},{19,3},{4,20},{20... | collective-permute-start | bytes 786440 | tf_op jit(solution)/shard_map/ppermute | solution.py:313
  7.4 1.0 %copy-start.7 = (bf16[1,1,128,2048]{3,2,1,0:T(8,128)(2,1)S(1)}, bf16[1,1,128,2048]{3,2,1,0:T(8,128)(2,1)}, u32[]{:S(2)}) copy-start(bf16[1,1,128,2048]{3,2,1,0:T(8,128)(2,1)} %param.10) | copy-start | bytes 1572868
  8.5 0.8 copy-start.2
  9.3 0.8 copy-start.4
  14.0 1.0 %copy-start.3 = (bf16[128,2048]{1,0:T(8,128)(2,1)S(1)}, bf16[128,2048]{1,0:T(8,128)(2,1)}, u32[]{:S(2)}) copy-start(bf16[128,2048]{1,0:T(8,128)(2,1)} %copy-done.2) | copy-start | bytes 1572868
  15.0 1.0 %copy-start.5 = (bf16[128,2048]{1,0:T(8,128)(2,1)S(1)}, bf16[128,2048]{1,0:T(8,128)(2,1)}, u32[]{:S(2)}) copy-start(bf16[128,2048]{1,0:T(8,128)(2,1)} %copy-done.4) | copy-start | bytes 1572868
  23.7 12.0 %collective-permute-start.10 = (bf16[96,2048]{1,0:T(8,128)(2,1)S(1)}, bf16[96,2048]{1,0:T(8,128)(2,1)S(1)}, u32[]{:S(2)}, u32[]{:S(2)}) collective-permute-start(bf16[96,2048]{1,0:T(8,128)(2,1)S(1)} %get-tuple-element.37), channel_id=1, source_target_pairs={{0,2},{1,3},{2,0},{3,1},{4,6},{5,7},{6,4},{7,5},{8,10},{9,11},{10,... | collective-permute-start | bytes 1179656 | tf_op jit(solution)/shard_map/ppermute | solution.py:303
  25.4 27.4 %collective-permute-start.5 = (bf16[1024,384]{1,0:T(8,128)(2,1)S(1)}, bf16[1024,384]{1,0:T(8,128)(2,1)S(1)}, u32[]{:S(2)}, u32[]{:S(2)}) collective-permute-start(bf16[1024,384]{1,0:T(8,128)(2,1)S(1)} %hand_on.9.refs_0_.refs_2_), channel_id=1, source_target_pairs={{0,16},{16,0},{1,17},{17,1},{2,18},{18,2},{3,19},{19,3},{4,20},{20... | collective-permute-start | bytes 2359304 | tf_op jit(solution)/shard_map/ppermute | solution.py:316
  26.9 19.1 %collective-permute-start.8 = (bf16[96,2048]{1,0:T(8,128)(2,1)S(1)}, bf16[96,2048]{1,0:T(8,128)(2,1)S(1)}, u32[]{:S(2)}, u32[]{:S(2)}) collective-permute-start(bf16[96,2048]{1,0:T(8,128)(2,1)S(1)} %get-tuple-element.36), channel_id=1, source_target_pairs={{0,8},{1,9},{2,10},{3,11},{4,12},{5,13},{6,14},{7,15},{8,0},{9,1},... | collective-permute-start | bytes 1179656 | tf_op jit(solution)/shard_map/ppermute | solution.py:307
  29.5 16.7 %collective-permute-start.3 = (bf16[96,2048]{1,0:T(8,128)(2,1)S(1)}, bf16[96,2048]{1,0:T(8,128)(2,1)S(1)}, u32[]{:S(2)}, u32[]{:S(2)}) collective-permute-start(bf16[96,2048]{1,0:T(8,128)(2,1)S(1)} %get-tuple-element.33.refs_1_), channel_id=1, source_target_pairs={{0,4},{1,5},{2,6},{3,7},{4,0},{5,1},{6,2},{7,3},{8,12},{9,13},{10,... | collective-permute-start | bytes 1179656 | tf_op jit(solution)/shard_map/ppermute | solution.py:303
  31.1 24.9 %collective-permute-start.14 = (bf16[192,2048]{1,0:T(8,128)(2,1)S(1)}, bf16[192,2048]{1,0:T(8,128)(2,1)S(1)}, u32[]{:S(2)}, u32[]{:S(2)}) collective-permute-start(bf16[192,2048]{1,0:T(8,128)(2,1)S(1)} %get-tuple-element.40), channel_id=1, source_target_pairs={{0,2},{1,3},{2,0},{3,1},{4,6},{5,7},{6,4},{7,5},{8,10},{9,11},{10,... | collective-permute-start | bytes 2359304 | tf_op jit(solution)/shard_map/ppermute | solution.py:303
  35.7 16.5 %collective-permute-start.11 = (bf16[96,2048]{1,0:T(8,128)(2,1)S(1)}, bf16[96,2048]{1,0:T(8,128)(2,1)S(1)}, u32[]{:S(2)}, u32[]{:S(2)}) collective-permute-start(bf16[96,2048]{1,0:T(8,128)(2,1)S(1)} %collective-permute-done.10.refs_0_), channel_id=1, source_target_pairs={{0,16},{16,0},{1,17},{17,1},{2,18},{18,2},{3,19},{19,3},{4,20},{20... | collective-permute-start | bytes 1179656 | tf_op jit(solution)/shard_map/ppermute | solution.py:316
  46.3 9.7 %collective-permute-start.9 = (bf16[96,2048]{1,0:T(8,128)(2,1)S(1)}, bf16[96,2048]{1,0:T(8,128)(2,1)S(1)}, u32[]{:S(2)}, u32[]{:S(2)}) collective-permute-start(bf16[96,2048]{1,0:T(8,128)(2,1)S(1)} %hand_on.11.refs_1_), channel_id=1, source_target_pairs={{0,4},{1,5},{2,6},{3,7},{4,0},{5,1},{6,2},{7,3},{8,12},{9,13},{10,... | collective-permute-start | bytes 1179656 | tf_op jit(solution)/shard_map/ppermute | solution.py:303
  52.3 9.0 %collective-permute-start.12 = (bf16[96,2048]{1,0:T(8,128)(2,1)S(1)}, bf16[96,2048]{1,0:T(8,128)(2,1)S(1)}, u32[]{:S(2)}, u32[]{:S(2)}) collective-permute-start(bf16[96,2048]{1,0:T(8,128)(2,1)S(1)} %get-tuple-element.38.refs_4_), channel_id=1, source_target_pairs={{0,1},{1,0},{2,3},{3,2},{4,5},{5,4},{6,7},{7,6},{8,9},{9,8},{10,11... | collective-permute-start | bytes 1179656 | tf_op jit(solution)/shard_map/ppermute | solution.py:303
  52.3 9.0 %collective-permute-start.13 = (bf16[96,2048]{1,0:T(8,128)(2,1)S(1)}, bf16[96,2048]{1,0:T(8,128)(2,1)S(1)}, u32[]{:S(2)}, u32[]{:S(2)}) collective-permute-start(bf16[96,2048]{1,0:T(8,128)(2,1)S(1)} %get-tuple-element.39.refs_5_), channel_id=1, source_target_pairs={{0,1},{1,0},{2,3},{3,2},{4,5},{5,4},{6,7},{7,6},{8,9},{9,8},{10,11... | collective-permute-start | bytes 1179656 | tf_op jit(solution)/shard_map/ppermute | solution.py:303
  52.8 3.7 %collective-permute-start.6 = (bf16[1024,384]{1,0:T(8,128)(2,1)S(1)}, bf16[1024,384]{1,0:T(8,128)(2,1)S(1)}, u32[]{:S(2)}, u32[]{:S(2)}) collective-permute-start(bf16[1024,384]{1,0:T(8,128)(2,1)S(1)} %get-tuple-element.34.refs_5_), channel_id=1, source_target_pairs={{0,1},{1,0},{2,3},{3,2},{4,5},{5,4},{6,7},{7,6},{8,9},{9,8},{10,11... | collective-permute-start | bytes 2359304 | tf_op jit(solution)/shard_map/ppermute | solution.py:303
  56.0 2.3 %collective-permute-start.7 = (bf16[1024,384]{1,0:T(8,128)(2,1)S(1)}, bf16[1024,384]{1,0:T(8,128)(2,1)S(1)}, u32[]{:S(2)}, u32[]{:S(2)}) collective-permute-start(bf16[1024,384]{1,0:T(8,128)(2,1)S(1)} %get-tuple-element.35.refs_6_), channel_id=1, source_target_pairs={{0,1},{1,0},{2,3},{3,2},{4,5},{5,4},{6,7},{7,6},{8,9},{9,8},{10,11... | collective-permute-start | bytes 2359304 | tf_op jit(solution)/shard_map/ppermute | solution.py:303
  56.0 5.3 %collective-permute-start.15 = (bf16[192,2048]{1,0:T(8,128)(2,1)S(1)}, bf16[192,2048]{1,0:T(8,128)(2,1)S(1)}, u32[]{:S(2)}, u32[]{:S(2)}) collective-permute-start(bf16[192,2048]{1,0:T(8,128)(2,1)S(1)} %collective-permute-done.14.refs_8_), channel_id=1, source_target_pairs={{0,1},{1,0},{2,3},{3,2},{4,5},{5,4},{6,7},{7,6},{8,9},{9,8},{10,11... | collective-permute-start | bytes 2359304 | tf_op jit(solution)/shard_map/ppermute | solution.py:303
  56.5 1.8 %copy-start.1 = (bf16[2048,384]{1,0:T(8,128)(2,1)S(1)}, bf16[2048,384]{1,0:T(8,128)(2,1)}, u32[]{:S(2)}) copy-start(bf16[2048,384]{1,0:T(8,128)(2,1)} %refs_3_.3) | copy-start | bytes 4718596
  58.3 3.0 %copy-start = (bf16[384,2048]{1,0:T(8,128)(2,1)S(1)}, bf16[384,2048]{1,0:T(8,128)(2,1)}, u32[]{:S(2)}) copy-start(bf16[384,2048]{1,0:T(8,128)(2,1)} %refs_2_.3) | copy-start | bytes 4718596
  62.8 11.2 %collective-permute-start.16 = (bf16[96,2048]{1,0:T(8,128)(2,1)S(1)}, bf16[96,2048]{1,0:T(8,128)(2,1)S(1)}, u32[]{:S(2)}, u32[]{:S(2)}) collective-permute-start(bf16[96,2048]{1,0:T(8,128)(2,1)S(1)} %get-tuple-element.43), channel_id=1, source_target_pairs={{0,4},{1,5},{2,6},{3,7},{4,0},{5,1},{6,2},{7,3},{8,12},{9,13},{10,... | collective-permute-start | bytes 1179656 | tf_op jit(solution)/shard_map/ppermute | solution.py:303
  74.1 18.6 %collective-permute-start.17 = (bf16[96,2048]{1,0:T(8,128)(2,1)S(1)}, bf16[96,2048]{1,0:T(8,128)(2,1)S(1)}, u32[]{:S(2)}, u32[]{:S(2)}) collective-permute-start(bf16[96,2048]{1,0:T(8,128)(2,1)S(1)} %get-tuple-element.45), channel_id=1, source_target_pairs={{0,4},{1,5},{2,6},{3,7},{4,0},{5,1},{6,2},{7,3},{8,12},{9,13},{10,... | collective-permute-start | bytes 1179656 | tf_op jit(solution)/shard_map/ppermute | solution.py:303
  75.9 20.1 %collective-permute-start.18 = (bf16[96,2048]{1,0:T(8,128)(2,1)S(1)}, bf16[96,2048]{1,0:T(8,128)(2,1)S(1)}, u32[]{:S(2)}, u32[]{:S(2)}) collective-permute-start(bf16[96,2048]{1,0:T(8,128)(2,1)S(1)} %get-tuple-element.46), channel_id=1, source_target_pairs={{0,8},{1,9},{2,10},{3,11},{4,12},{5,13},{6,14},{7,15},{8,0},{9,1},... | collective-permute-start | bytes 1179656 | tf_op jit(solution)/shard_map/ppermute | solution.py:307

commit v9 on v8

--- a/solution.py
+++ b/solution.py
@@ -14,8 +14,11 @@
 EPS = 1e-06
 FAR_WEIGHT = 3_000_000_000
 FAR_STEPS = 4
-CROSS_WEIGHT = 1
+CROSS_STEPS = 1
+CROSS_WEIGHT = 3_000_000_000
+BACK_WEIGHT = 10_000_000_000
 VMEM_LIMIT = 32 * 1024 * 1024
+PART_LIMIT = 60 * 1024 * 1024
 
 VMEM = pl.BlockSpec(memory_space=pltpu.VMEM)
 SMEM = pl.BlockSpec(memory_space=pltpu.SMEM)
@@ -27,7 +30,7 @@
 
 
 def call(
-    kernel, outs, in_specs, name, flops, moved, scratch=(), out_specs=None, aliases=None
+    kernel, outs, in_specs, name, flops, moved, scratch=(), out_specs=None, aliases=None, limit=VMEM_LIMIT
 ):
     return pl.pallas_call(
         kernel,
@@ -36,7 +39,7 @@
         out_specs=out_specs or jax.tree.map(lambda _: VMEM, outs),
         scratch_shapes=list(scratch),
         input_output_aliases=aliases or {},
-        compiler_params=pltpu.CompilerParams(vmem_limit_bytes=VMEM_LIMIT),
+        compiler_params=pltpu.CompilerParams(vmem_limit_bytes=limit),
         cost_estimate=pl.CostEstimate(flops=flops, bytes_accessed=moved, transcendentals=0),
         name=name,
     )
@@ -162,47 +165,101 @@
     return pl.multiple_of(at * size, size)
 
 
-def up_kernel(pipes, *refs):
+def part_kernel(pipes, pipe_ref, w_in, w_out, in_part, out_part, out_rest, sems):
+    depth, size = in_part.shape[0], out_part.shape[0]
+    pipe = pipe_ref[0]
+    copies = [
+        pltpu.make_async_copy(source, target, sems.at[i])
+        for i, (source, target) in enumerate(
+            (
+                (w_in.at[pl.ds(pl.multiple_of(pipe * depth, depth), depth)], in_part),
+                (w_out.at[pl.ds(pl.multiple_of(pipe * size, size), size)], out_part),
+                (w_out.at[pipes * size :], out_rest),
+            )
+        )
+    ]
+    for copy in copies:
+        copy.start()
+    for copy in copies:
+        copy.wait()
+
+
+def parts(pipe, w_in, w_out, pipes):
+    width, units = w_in.shape
+    size = units // 2 // pipes // 16 * 16
+    return call(
+        functools.partial(part_kernel, pipes),
+        [
+            struct((width // pipes, units)),
+            struct((size, width)),
+            struct((units - pipes * size, width)),
+        ],
+        [SMEM, ANY, ANY],
+        "weight_parts",
+        1,
+        4 * units * width,
+        scratch=[pltpu.SemaphoreType.DMA((3,))],
+        limit=PART_LIMIT,
+    )(pipe, w_in, w_out)
+
+
+def up_kernel(own_in, z_in, w_own, w_pair, out_ref):
+    entries = jnp.concatenate([own_in[...], z_in[...]], axis=0)
+    weights = jnp.concatenate([w_own[...], w_pair[...]], axis=1)
+    raw = jnp.dot(entries, weights, preferred_element_type=jnp.float32)
+    out_ref[...] = jnp.maximum(raw, 0.0).astype(jnp.bfloat16)
+
+
+def up(own, z, w_in):
+    rows, width = own.shape
+    units = w_in[0].shape[1]
+    return call(
+        up_kernel,
+        struct((2 * rows, 2 * units)),
+        [VMEM] * 4,
+        "expert_up",
+        8 * rows * width * units,
+        4 * units * width,
+    )(own, z, *w_in)
+
+
+def up_y_kernel(pipes, *refs):
     pipe = refs[0][0]
-    own_in, z_in, w_own, w_pair = refs[1:5]
-    y_parts = refs[5 : 5 + pipes]
-    pair_parts = refs[5 + pipes : 5 + 2 * pipes]
+    own_in, z_in = refs[1:3]
+    y_parts = refs[3 : 3 + pipes]
+    pair_parts = refs[3 + pipes : 3 + 2 * pipes]
     out_ref, entries = refs[-2:]
     rows, width = own_in.shape
-    units = w_own.shape[1]
     entries[:rows] = own_in[...]
     entries[rows:] = z_in[...]
-    weights = jnp.concatenate([w_own[...], w_pair[...]], axis=1)
-    raw = jnp.dot(entries[...], weights, preferred_element_type=jnp.float32)
-    out_ref[:, : 2 * units] = jnp.maximum(raw, 0.0).astype(jnp.bfloat16)
     depth = width // pipes
-    raw = jnp.zeros_like(raw)
+    raw = jnp.zeros(out_ref.shape, jnp.float32)
     for shift in range(pipes):
         part = entries[:, pl.ds(place(pipes, shift, pipe, depth), depth)]
         weights = jnp.concatenate([y_parts[shift][...], pair_parts[shift][...]], axis=1)
         raw = raw + jnp.dot(part, weights, preferred_element_type=jnp.float32)
-    out_ref[:, 2 * units :] = jnp.maximum(raw, 0.0).astype(jnp.bfloat16)
-
-
-def up(pipe, own, z, w_in, y_parts, pair_parts, after=()):
+    out_ref[...] = jnp.maximum(raw, 0.0).astype(jnp.bfloat16)
+
+
+def up_y(pipe, own, z, y_parts, pair_parts, after=()):
     rows, width = own.shape
-    units = w_in[0].shape[1]
+    units = y_parts[0].shape[1]
     pipes = len(y_parts)
     return call(
-        functools.partial(up_kernel, pipes),
-        struct((2 * rows, 4 * units)),
-        [SMEM] + [VMEM] * (4 + 2 * pipes) + [ANY] * len(after),
-        "expert_up",
-        16 * rows * width * units,
-        8 * units * width,
+        functools.partial(up_y_kernel, pipes),
+        struct((2 * rows, 2 * units)),
+        [SMEM] + [VMEM] * (2 + 2 * pipes) + [ANY] * len(after),
+        "expert_up_y",
+        8 * rows * width * units,
+        4 * units * width,
         scratch=[pltpu.VMEM((2 * rows, width), jnp.bfloat16)],
-    )(pipe, own, z, *w_in, *y_parts, *pair_parts, *after)
+    )(pipe, own, z, *y_parts, *pair_parts, *after)
 
 
 def down_kernel(pipes, *refs):
     pipe = refs[0][0]
-    act_ref, w_own, w_pair = refs[1:4]
-    y_parts, refs = refs[4 : 4 + pipes], refs[4 + pipes :]
+    act_ref, act_y_ref, w_own, w_pair = refs[1:5]
+    y_parts, refs = refs[5 : 5 + pipes], refs[5 + pipes :]
     pair_parts, refs = refs[:pipes], refs[pipes:]
     y_rest, pair_rest = refs[:2]
     own_ref, z_ref, held = refs[-3:]
@@ -218,26 +275,27 @@
     step = 512
     for at in range(0, width, step):
         cols = slice(at, at + step)
-        weights = jnp.concatenate([w_own[:, cols], w_pair[:, cols], held[:, cols]], axis=0)
+        weights = jnp.concatenate([w_own[:, cols], w_pair[:, cols]], axis=0)
         part = jnp.dot(act_ref[...], weights, preferred_element_type=jnp.float32)
+        part = part + jnp.dot(act_y_ref[...], held[:, cols], preferred_element_type=jnp.float32)
         part = part.astype(jnp.bfloat16)
         own_ref[:, cols] = part[:rows]
         z_ref[:, cols] = part[rows:]
 
 
-def down(pipe, act, w_out, y_parts, pair_parts, rests, after=()):
-    rows = act.shape[0] // 2
+def down(pipe, acts, w_out, y_parts, pair_parts, rests):
+    rows = acts[0].shape[0] // 2
     units, width = w_out[0].shape
     pipes = len(y_parts)
     return call(
         functools.partial(down_kernel, pipes),
         [struct((rows, width))] * 2,
-        [SMEM] + [VMEM] * (5 + 2 * pipes) + [ANY] * len(after),
+        [SMEM] + [VMEM] * (6 + 2 * pipes),
         "expert_down",
         16 * rows * width * units,
         8 * units * width,
         scratch=[pltpu.VMEM((2 * units, width), jnp.bfloat16)],
-    )(pipe, act, *w_out, *y_parts, *pair_parts, *rests, *after)
+    )(pipe, *acts, *w_out, *y_parts, *pair_parts, *rests)
 
 
 def total_kernel(held, own_ref, z_ref, *refs):
@@ -320,12 +378,8 @@
 
     pipe = lax.axis_index("pipe").astype(jnp.int32)
     w_in_pair, w_out_pair = across(w_in, 1), across(w_out, 1)
-    units = w_in.shape[1]
-    depth, size = width // pipes, units // 2 // pipes // 16 * 16
-    in_part = lax.dynamic_slice_in_dim(w_in, pipe * depth, depth, 0)
-    out_part = lax.dynamic_slice_in_dim(w_out, pipe * size, size, 0)
-    out_rest = w_out[pipes * size :]
     pipe = pipe.reshape(1)
+    in_part, out_part, out_rest = parts(pipe, w_in, w_out, pipes)
     in_y = across(in_part, 2)
 
     group = (lax.axis_index("expert") // WSPLIT).astype(jnp.int32).reshape(1)
@@ -349,33 +403,37 @@
 
     (in_y,) = after_all([in_y], [near])
     out_part, out_rest = after_all([out_part, out_rest], [in_y])
+    out_y = across(out_part, 2)
+    rest_y = across(out_rest, 2)
     in_y = after_all(along(in_y), [])
     in_pair = paired(in_y)
-    out_y = across(out_part, 2)
+    (out_y,) = after_all([out_y], [in_y[-1]])
     out_y = after_all(along(out_y), [])
     out_pair = paired(out_y)
-    rest_y = across(out_rest, 2)
     rests = [rest_y, across(rest_y, 1)]
 
     near_z = across(near, 4)
-    (far,) = after_all([far], [near_z], CROSS_WEIGHT)
-    far_z = across(far, 4)
+    far = [far]
+    for step in range(CROSS_STEPS):
+        far = after_all(far, [] if step else [near_z], CROSS_WEIGHT)
+    (far,) = far
+    far_z = [across(far, 4)]
     for _ in range(FAR_STEPS):
-        (far_z,) = after_all([far_z], [], FAR_WEIGHT)
-
-    def experts_up(own, z, after=()):
-        return up(pipe, own, z, [w_in, w_in_pair], in_y, in_pair, after)
-
-    def experts_down(act, after=()):
-        return down(pipe, act, [w_out, w_out_pair], out_y, out_pair, rests, after)
-
-    far_own, far_sent = experts_down(experts_up(far, far_z))
-    near_own, near_sent = experts_down(experts_up(near, near_z, [far_own]))
+        far_z = after_all(far_z, [], FAR_WEIGHT)
+    (far_z,) = far_z
+
+    def experts(own, z, after=()):
+        acts = up(own, z, [w_in, w_in_pair]), up_y(pipe, own, z, in_y, in_pair, after)
+        return down(pipe, acts, [w_out, w_out_pair], out_y, out_pair, rests)
+
+    far_own, far_sent = experts(far, far_z)
+    near_own, near_sent = experts(near, near_z, [far_own])
     far_sum, near_sent = total(far_own, across(far_sent, 4), [near_sent])
     backs = [
         groups_on(far_sum[(count - 1) * cap : count * cap], groups - count)
         for count in range(1, groups)
     ]
+    backs = after_all(backs, [], BACK_WEIGHT)
     near_sums = [near_own, across(near_sent, 4)]
     output = finish(hidden, gates, flat, near_sums, backs, groups, cap)
     return output.reshape(1, 1, tokens, width)

time: 97.6 us -> 95 us (0.973)
  local copies, waits for them, and re-layouts: 9.14 us -> 2.54 us
  waiting for transfers between devices: 51.2 us -> 54.8 us
  Pallas kernels: 12.5 us -> 14.9 us
  starting transfers between devices: 24.1 us -> 22.3 us
    ppermute x14, waiting for transfers between devices: 33.1 us -> 17.9 us  [across(): return lax.ppermute(value, 'expert', [(i, i ^ bit) for i in range(devices)])]
    ppermute x2, waiting for transfers between devices: 11.9 us -> 23.3 us  [groups_on(): lax.ppermute(value, 'expert', [(i, (i + shift) % devices) for i in range(...]
    ppermute x2, waiting for transfers between devices: 4.58 us -> 8.29 us  [along(): return [value] + [lax.ppermute(value, 'pipe', perm) for perm in perms]]
    ppermute x1, waiting for transfers between devices: 1.62 us -> 5.24 us  [body(): kv_pieces.append(lax.ppermute(kv, 'pipe', perm))]
    dynamic_slice x2 -> x0, local copies, waits for them, and re-layouts: 3.15 us -> none  [the longest x1 2.13 us: body(): in_part = lax.dynamic_slice_in_dim(w_in, pipe * depth, depth, 0)]
    pallas_call x2, Pallas kernels: 2.97 us -> 5.89 us  [down(): call(functools.partial(down_kernel, pipes), [struct((rows, width))] * 2,...]
    unnamed x26 -> x22, local copies, waits for them, and re-layouts: 4.72 us -> 2.46 us
    slice x1 -> x0, local copies, waits for them, and re-layouts: 1.18 us -> none  [body(): out_rest = w_out[pipes * size:]]
  transfers between devices with their start and end apart: 19 -> 19, of which waited for: 11 -> 11; matrix products, arithmetic and copies ran while one was open for 5% -> 0% of each run, Pallas kernels for 10% -> 11%
where the time goes in v9:
time: 95 us; the launch traced here: 94.7 us
  waiting for transfers between devices  54.8 us (58%)
  starting transfers between devices  22.3 us (23%)
  Pallas kernels  14.9 us (16%)
  local copies, waits for them, and re-layouts  2.54 us (3%)
    ppermute x2, waiting for transfers between devices, groups_on(): lax.ppermute(value, 'expert', [(i, (i + shift) % devices) for i in range(...  23.3 us
    ppermute x14, waiting for transfers between devices, across(): return lax.ppermute(value, 'expert', [(i, i ^ bit) for i in range(devices)])  17.9 us
    ppermute x14, starting transfers between devices, across(): return lax.ppermute(value, 'expert', [(i, i ^ bit) for i in range(devices)])  12.4 us
    ppermute x2, waiting for transfers between devices, along(): return [value] + [lax.ppermute(value, 'pipe', perm) for perm in perms]  8.29 us
    pallas_call x2, Pallas kernels, down(): call(functools.partial(down_kernel, pipes), [struct((rows, width))] * 2,...  5.89 us
    ppermute x1, waiting for transfers between devices, body(): kv_pieces.append(lax.ppermute(kv, 'pipe', perm))  5.24 us
    ppermute x2, starting transfers between devices, groups_on(): lax.ppermute(value, 'expert', [(i, (i + shift) % devices) for i in range(...  5.22 us
    ppermute x2, starting transfers between devices, along(): return [value] + [lax.ppermute(value, 'pipe', perm) for perm in perms]  3.17 us
  transfers between devices with their start and end apart: 19, of which 11 were waited for; matrix products, arithmetic and copies ran while one was open for 0% of the time, Pallas kernels for 11%

profile of v9, /device:TPU:0, one launch (start us, length us, event | category | flops | bytes accessed | tf_op | source)
XLA Modules:
  0.0 94.7 jit_solution(8563173015032940339)
XLA Ops:
  0.0 0.5 collective-permute-start.1
  0.5 0.1 collective-permute-start.2
  0.5 2.9 %weight_parts.1 = (bf16[1024,384]{1,0:T(8,128)(2,1)}, bf16[96,2048]{1,0:T(8,128)(2,1)}, bf16[192,2048]{1,0:T(8,128)(2,1)}) custom-call(s32[1]{0:T(128)} %bitcast.10.pipe_ref.refs_0_, bf16[2048,384]{1,0:T(8,128)(2,1)} %w_own.3, bf16[384,2048]{1,0:T(8,128)(2,1)} %refs_3_.3), custom_call_target="tpu_custom_call" | custom-call | flops 1 | bytes 3145728 | tf_op jit(solution)/shard_map/weight_parts/pallas_call | solution.py:190
  3.4 3.0 %collective-permute-start.4 = (bf16[1024,384]{1,0:T(8,128)(2,1)}, bf16[1024,384]{1,0:T(8,128)(2,1)S(1)}, u32[]{:S(2)}, u32[]{:S(2)}) collective-permute-start(bf16[1024,384]{1,0:T(8,128)(2,1)} %get-tuple-element.37), channel_id=1, source_target_pairs={{0,2},{1,3},{2,0},{3,1},{4,6},{5,7},{6,4},{7,5},{8,10},{9,11},{10,... | collective-permute-start | bytes 2359304 | tf_op jit(solution)/shard_map/ppermute | solution.py:361
  6.4 0.1 copy.25
  6.5 1.6 %collective-permute-start = (bf16[64,2048]{1,0:T(8,128)(2,1)S(1)}, bf16[64,2048]{1,0:T(8,128)(2,1)S(1)}, u32[]{:S(2)}, u32[]{:S(2)}) collective-permute-start(bf16[64,2048]{1,0:T(8,128)(2,1)S(1)} %bitcast.13), channel_id=1, source_target_pairs={{0,16},{16,0},{1,17},{17,1},{2,18},{18,2},{3,19},{19,3},{4,20},{20... | collective-permute-start | bytes 786440 | tf_op jit(solution)/shard_map/ppermute | solution.py:371
  8.1 0.0 copy-start.4
  8.1 1.0 %copy-done.4 = bf16[1,1,128,2048]{3,2,1,0:T(8,128)(2,1)S(1)} copy-done((bf16[1,1,128,2048]{3,2,1,0:T(8,128)(2,1)S(1)}, bf16[1,1,128,2048]{3,2,1,0:T(8,128)(2,1)}, u32[]{:S(2)}) %copy-start.4) | copy-done | bytes 524312
  9.2 0.1 stage.1
  9.3 5.2 %collective-permute-done.refs_5_ = bf16[64,2048]{1,0:T(8,128)(2,1)S(1)} collective-permute-done((bf16[64,2048]{1,0:T(8,128)(2,1)S(1)}, bf16[64,2048]{1,0:T(8,128)(2,1)S(1)}, u32[]{:S(2)}, u32[]{:S(2)}) %collective-permute-start) | collective-permute-done | bytes 262176 | tf_op jit(solution)/shard_map/ppermute | solution.py:371
  14.5 0.0 collective-permute-done.1.refs_6_.w_pair
  14.5 0.0 collective-permute-done.2.refs_7_.refs_4_
  14.5 1.4 %attend.1 = (f32[128,2048]{1,0:T(8,128)S(1)}, bf16[96,2048]{1,0:T(8,128)(2,1)S(1)}, bf16[96,2048]{1,0:T(8,128)(2,1)S(1)}) custom-call(bf16[128,2048]{1,0:T(8,128)(2,1)S(1)} %get-tuple-element.29.refs_0_, bf16[128,2048]{1,0:T(8,128)(2,1)S(1)} %get-tuple-element.30.refs_1_, f32[1,2048]{1,0:T(1,128)S(1)} %get-tuple-element.31.refs_2_, ...), custom_call_target="tpu_custom_call" | custom-call | flops 134217728 | bytes 3145728 | tf_op jit(solution)/shard_map/attend/pallas_call | solution.py:152
  16.0 0.0 copy-start.5
  16.0 2.6 %collective-permute-start.8 = (bf16[96,2048]{1,0:T(8,128)(2,1)S(1)}, bf16[96,2048]{1,0:T(8,128)(2,1)S(1)}, u32[]{:S(2)}, u32[]{:S(2)}) collective-permute-start(bf16[96,2048]{1,0:T(8,128)(2,1)S(1)} %get-tuple-element.40), channel_id=1, source_target_pairs={{0,8},{1,9},{2,10},{3,11},{4,12},{5,13},{6,14},{7,15},{8,0},{9,1},... | collective-permute-start | bytes 1179656 | tf_op jit(solution)/shard_map/ppermute | solution.py:365
  18.7 1.6 %collective-permute-start.3 = (bf16[96,2048]{1,0:T(8,128)(2,1)S(1)}, bf16[96,2048]{1,0:T(8,128)(2,1)S(1)}, u32[]{:S(2)}, u32[]{:S(2)}) collective-permute-start(bf16[96,2048]{1,0:T(8,128)(2,1)S(1)} %get-tuple-element.36.own_in.refs_1_), channel_id=1, source_target_pairs={{0,4},{1,5},{2,6},{3,7},{4,0},{5,1},{6,2},{7,3},{8,12},{9,13},{10,... | collective-permute-start | bytes 1179656 | tf_op jit(solution)/shard_map/ppermute | solution.py:361
  20.2 4.1 %collective-permute-done.4.refs_0_ = bf16[1024,384]{1,0:T(8,128)(2,1)S(1)} collective-permute-done((bf16[1024,384]{1,0:T(8,128)(2,1)}, bf16[1024,384]{1,0:T(8,128)(2,1)S(1)}, u32[]{:S(2)}, u32[]{:S(2)}) %collective-permute-start.4) | collective-permute-done | bytes 786464 | tf_op jit(solution)/shard_map/ppermute | solution.py:361
  24.4 1.7 %collective-permute-start.5 = (bf16[1024,384]{1,0:T(8,128)(2,1)S(1)}, bf16[1024,384]{1,0:T(8,128)(2,1)S(1)}, u32[]{:S(2)}, u32[]{:S(2)}) collective-permute-start(bf16[1024,384]{1,0:T(8,128)(2,1)S(1)} %hand_on.11.refs_0_.refs_2_), channel_id=1, source_target_pairs={{0,16},{16,0},{1,17},{17,1},{2,18},{18,2},{3,19},{19,3},{4,20},{20... | collective-permute-start | bytes 2359304 | tf_op jit(solution)/shard_map/ppermute | solution.py:374
  26.1 1.5 %collective-permute-start.10 = (bf16[96,2048]{1,0:T(8,128)(2,1)S(1)}, bf16[96,2048]{1,0:T(8,128)(2,1)S(1)}, u32[]{:S(2)}, u32[]{:S(2)}) collective-permute-start(bf16[96,2048]{1,0:T(8,128)(2,1)S(1)} %get-tuple-element.43), channel_id=1, source_target_pairs={{0,2},{1,3},{2,0},{3,1},{4,6},{5,7},{6,4},{7,5},{8,10},{9,11},{10,... | collective-permute-start | bytes 1179656 | tf_op jit(solution)/shard_map/ppermute | solution.py:361
  27.6 0.5 collective-permute-start.14
  28.1 7.2 %collective-permute-done.8.refs_0_ = bf16[96,2048]{1,0:T(8,128)(2,1)S(1)} collective-permute-done((bf16[96,2048]{1,0:T(8,128)(2,1)S(1)}, bf16[96,2048]{1,0:T(8,128)(2,1)S(1)}, u32[]{:S(2)}, u32[]{:S(2)}) %collective-permute-start.8) | collective-permute-done | bytes 393248 | tf_op jit(solution)/shard_map/ppermute | solution.py:365
  35.4 0.2 collective-permute-done.3.z_in.refs_1_.refs_2_
  35.5 1.4 %collective-permute-start.9 = (bf16[96,2048]{1,0:T(8,128)(2,1)S(1)}, bf16[96,2048]{1,0:T(8,128)(2,1)S(1)}, u32[]{:S(2)}, u32[]{:S(2)}) collective-permute-start(bf16[96,2048]{1,0:T(8,128)(2,1)S(1)} %hand_on.13.own_in.refs_1_), channel_id=1, source_target_pairs={{0,4},{1,5},{2,6},{3,7},{4,0},{5,1},{6,2},{7,3},{8,12},{9,13},{10,... | collective-permute-start | bytes 1179656 | tf_op jit(solution)/shard_map/ppermute | solution.py:361
  37.0 6.3 %collective-permute-done.5.refs_1_ = bf16[1024,384]{1,0:T(8,128)(2,1)S(1)} collective-permute-done((bf16[1024,384]{1,0:T(8,128)(2,1)S(1)}, bf16[1024,384]{1,0:T(8,128)(2,1)S(1)}, u32[]{:S(2)}, u32[]{:S(2)}) %collective-permute-start.5) | collective-permute-done | bytes 786464 | tf_op jit(solution)/shard_map/ppermute | solution.py:374
  43.3 0.0 collective-permute-done.10.refs_0_
  43.3 1.5 %collective-permute-start.11 = (bf16[96,2048]{1,0:T(8,128)(2,1)S(1)}, bf16[96,2048]{1,0:T(8,128)(2,1)S(1)}, u32[]{:S(2)}, u32[]{:S(2)}) collective-permute-start(bf16[96,2048]{1,0:T(8,128)(2,1)S(1)} %hand_on.19.refs_0_), channel_id=1, source_target_pairs={{0,16},{16,0},{1,17},{17,1},{2,18},{18,2},{3,19},{19,3},{4,20},{20... | collective-permute-start | bytes 1179656 | tf_op jit(solution)/shard_map/ppermute | solution.py:374
  44.8 0.2 collective-permute-start.6
  44.9 0.3 collective-permute-done.9.refs_0_
  45.3 7.6 %collective-permute-done.14.refs_9_ = bf16[192,2048]{1,0:T(8,128)(2,1)S(1)} collective-permute-done((bf16[192,2048]{1,0:T(8,128)(2,1)S(1)}, bf16[192,2048]{1,0:T(8,128)(2,1)S(1)}, u32[]{:S(2)}, u32[]{:S(2)}) %collective-permute-start.14) | collective-permute-done | bytes 786464 | tf_op jit(solution)/shard_map/ppermute | solution.py:361
  52.8 2.0 %collective-permute-done.11.refs_1_ = bf16[96,2048]{1,0:T(8,128)(2,1)S(1)} collective-permute-done((bf16[96,2048]{1,0:T(8,128)(2,1)S(1)}, bf16[96,2048]{1,0:T(8,128)(2,1)S(1)}, u32[]{:S(2)}, u32[]{:S(2)}) %collective-permute-start.11) | collective-permute-done | bytes 393248 | tf_op jit(solution)/shard_map/ppermute | solution.py:374
  54.8 0.5 collective-permute-start.13
  55.4 0.9 copy-done
  56.2 0.8 expert_up.3.refs_1_
  57.1 0.0 copy-start.1
  57.1 0.9 expert_up_y.2.refs_2_
  58.0 0.5 copy-done.1
  58.5 3.0 %expert_down.2 = (bf16[96,2048]{1,0:T(8,128)(2,1)S(1)}, bf16[96,2048]{1,0:T(8,128)(2,1)S(1)}) custom-call(s32[1]{0:T(128)} %bitcast.10.pipe_ref.refs_0_, bf16[192,768]{1,0:T(8,128)(2,1)S(1)} %expert_up.3.refs_1_, bf16[192,768]{1,0:T(8,128)(2,1)S(1)} %expert_up_y.2.refs_2_, bf16[384,2048]{1,0:T(8,128)(2,1)S(1)} %copy-done.1, ...), custom_call_target="tpu_custom_call" | custom-call | flops 1207959552 | bytes 6291456 | tf_op jit(solution)/shard_map/expert_down/pallas_call | solution.py:290
  61.4 1.5 %collective-permute-start.16 = (bf16[96,2048]{1,0:T(8,128)(2,1)S(1)}, bf16[96,2048]{1,0:T(8,128)(2,1)S(1)}, u32[]{:S(2)}, u32[]{:S(2)}) collective-permute-start(bf16[96,2048]{1,0:T(8,128)(2,1)S(1)} %get-tuple-element.49), channel_id=1, source_target_pairs={{0,4},{1,5},{2,6},{3,7},{4,0},{5,1},{6,2},{7,3},{8,12},{9,13},{10,... | collective-permute-start | bytes 1179656 | tf_op jit(solution)/shard_map/ppermute | solution.py:361
  63.0 0.8 expert_up.2.refs_1_
  63.8 0.9 expert_up_y.3.refs_2_
  64.6 2.9 %expert_down.3 = (bf16[96,2048]{1,0:T(8,128)(2,1)S(1)}, bf16[96,2048]{1,0:T(8,128)(2,1)S(1)}) custom-call(s32[1]{0:T(128)} %bitcast.10.pipe_ref.refs_0_, bf16[192,768]{1,0:T(8,128)(2,1)S(1)} %expert_up.2.refs_1_, bf16[192,768]{1,0:T(8,128)(2,1)S(1)} %expert_up_y.3.refs_2_, bf16[384,2048]{1,0:T(8,128)(2,1)S(1)} %copy-done.1, ...), custom_call_target="tpu_custom_call" | custom-call | flops 1207959552 | bytes 6291456 | tf_op jit(solution)/shard_map/expert_down/pallas_call | solution.py:290
  67.6 5.4 %collective-permute-done.16.z_ref = bf16[96,2048]{1,0:T(8,128)(2,1)S(1)} collective-permute-done((bf16[96,2048]{1,0:T(8,128)(2,1)S(1)}, bf16[96,2048]{1,0:T(8,128)(2,1)S(1)}, u32[]{:S(2)}, u32[]{:S(2)}) %collective-permute-start.16) | collective-permute-done | bytes 393248 | tf_op jit(solution)/shard_map/ppermute | solution.py:361
  73.0 0.1 far_total.1
  73.1 2.6 %collective-permute-start.18 = (bf16[96,2048]{1,0:T(8,128)(2,1)S(1)}, bf16[96,2048]{1,0:T(8,128)(2,1)S(1)}, u32[]{:S(2)}, u32[]{:S(2)}) collective-permute-start(bf16[96,2048]{1,0:T(8,128)(2,1)S(1)} %get-tuple-element.52), channel_id=1, source_target_pairs={{0,8},{1,9},{2,10},{3,11},{4,12},{5,13},{6,14},{7,15},{8,0},{9,1},... | collective-permute-start | bytes 1179656 | tf_op jit(solution)/shard_map/ppermute | solution.py:365
  75.7 1.6 %collective-permute-start.17 = (bf16[96,2048]{1,0:T(8,128)(2,1)S(1)}, bf16[96,2048]{1,0:T(8,128)(2,1)S(1)}, u32[]{:S(2)}, u32[]{:S(2)}) collective-permute-start(bf16[96,2048]{1,0:T(8,128)(2,1)S(1)} %get-tuple-element.51), channel_id=1, source_target_pairs={{0,4},{1,5},{2,6},{3,7},{4,0},{5,1},{6,2},{7,3},{8,12},{9,13},{10,... | collective-permute-start | bytes 1179656 | tf_op jit(solution)/shard_map/ppermute | solution.py:361
  77.2 16.1 %collective-permute-done.18.refs_0_ = bf16[96,2048]{1,0:T(8,128)(2,1)S(1)} collective-permute-done((bf16[96,2048]{1,0:T(8,128)(2,1)S(1)}, bf16[96,2048]{1,0:T(8,128)(2,1)S(1)}, u32[]{:S(2)}, u32[]{:S(2)}) %collective-permute-start.18) | collective-permute-done | bytes 393248 | tf_op jit(solution)/shard_map/ppermute | solution.py:365
  93.3 0.2 collective-permute-done.17.refs_4_
  93.5 1.2 %finish.1 = bf16[128,2048]{1,0:T(8,128)(2,1)} custom-call(f32[128,2048]{1,0:T(8,128)S(1)} %get-tuple-element.33.refs_0_, f32[128,1]{1,0:T(8,128)S(1)} %get-tuple-element.34.refs_1_, s32[128,1]{1,0:T(8,128)S(1)} %get-tuple-element.35.refs_2_, bf16[96,2048]{1,0:T(8,128)(2,1)S(1)} %get-tuple-element.48.refs_3_, ...), custom_call_target="tpu_custom_call" | custom-call | flops 201326592 | bytes 4194304 | tf_op jit(solution)/shard_map/finish/pallas_call | solution.py:343
  (35 shorter events, 0.1 us)
Async XLA Ops:
  0.0 14.5 %collective-permute-start.1 = (bf16[2048,384]{1,0:T(8,128)(2,1)}, bf16[2048,384]{1,0:T(8,128)(2,1)S(1)}, u32[]{:S(2)}, u32[]{:S(2)}) collective-permute-start(bf16[2048,384]{1,0:T(8,128)(2,1)} %w_own.3), channel_id=1, source_target_pairs={{0,1},{1,0},{2,3},{3,2},{4,5},{5,4},{6,7},{7,6},{8,9},{9,8},{10,11... | collective-permute-start | bytes 4718600 | tf_op jit(solution)/shard_map/ppermute | solution.py:361
  0.5 14.1 %collective-permute-start.2 = (bf16[384,2048]{1,0:T(8,128)(2,1)}, bf16[384,2048]{1,0:T(8,128)(2,1)}, u32[]{:S(2)}, u32[]{:S(2)}) collective-permute-start(bf16[384,2048]{1,0:T(8,128)(2,1)} %refs_3_.3), channel_id=1, source_target_pairs={{0,1},{1,0},{2,3},{3,2},{4,5},{5,4},{6,7},{7,6},{8,9},{9,8},{10,11... | collective-permute-start | bytes 4718600 | tf_op jit(solution)/shard_map/ppermute | solution.py:361
  0.5 5.9 %copy-start.10 = (bf16[1,32,2,2048]{3,2,1,0:T(2,128)(2,1)S(1)}, bf16[1,32,2,2048]{3,2,1,0:T(2,128)(2,1)}, u32[]{:S(2)}) copy-start(bf16[1,32,2,2048]{3,2,1,0:T(2,128)(2,1)} %param.11) | copy-start | bytes 786436
  0.5 7.6 %copy-start.3 = (bf16[1,1,128,2048]{3,2,1,0:T(8,128)(2,1)S(1)}, bf16[1,1,128,2048]{3,2,1,0:T(8,128)(2,1)}, u32[]{:S(2)}) copy-start(bf16[1,1,128,2048]{3,2,1,0:T(8,128)(2,1)} %param.9) | copy-start | bytes 1572868
  0.5 7.6 %copy-start.6 = (f32[2048]{0:T(1024)S(1)}, f32[2048]{0:T(1024)}, u32[]{:S(2)}) copy-start(f32[2048]{0:T(1024)} %param.12) | copy-start | bytes 24580
  0.5 7.6 %copy-start.7 = (s32[1,1,128]{2,1,0:T(1,128)S(1)}, s32[1,1,128]{2,1,0:T(1,128)}, u32[]{:S(2)}) copy-start(s32[1,1,128]{2,1,0:T(1,128)} %param.15) | copy-start | bytes 1540
  0.5 7.6 %copy-start.8 = (s32[1,1,128]{2,1,0:T(1,128)S(1)}, s32[1,1,128]{2,1,0:T(1,128)}, u32[]{:S(2)}) copy-start(s32[1,1,128]{2,1,0:T(1,128)} %param.16) | copy-start | bytes 1540
  0.5 7.6 %copy-start.9 = (f32[1,1,128]{2,1,0:T(1,128)S(1)}, f32[1,1,128]{2,1,0:T(1,128)}, u32[]{:S(2)}) copy-start(f32[1,1,128]{2,1,0:T(1,128)} %param.17) | copy-start | bytes 1540
  3.4 21.0 %collective-permute-start.4 = (bf16[1024,384]{1,0:T(8,128)(2,1)}, bf16[1024,384]{1,0:T(8,128)(2,1)S(1)}, u32[]{:S(2)}, u32[]{:S(2)}) collective-permute-start(bf16[1024,384]{1,0:T(8,128)(2,1)} %get-tuple-element.37), channel_id=1, source_target_pairs={{0,2},{1,3},{2,0},{3,1},{4,6},{5,7},{6,4},{7,5},{8,10},{9,11},{10,... | collective-permute-start | bytes 2359304 | tf_op jit(solution)/shard_map/ppermute | solution.py:361
  6.5 8.0 %collective-permute-start = (bf16[64,2048]{1,0:T(8,128)(2,1)S(1)}, bf16[64,2048]{1,0:T(8,128)(2,1)S(1)}, u32[]{:S(2)}, u32[]{:S(2)}) collective-permute-start(bf16[64,2048]{1,0:T(8,128)(2,1)S(1)} %bitcast.13), channel_id=1, source_target_pairs={{0,16},{16,0},{1,17},{17,1},{2,18},{18,2},{3,19},{19,3},{4,20},{20... | collective-permute-start | bytes 786440 | tf_op jit(solution)/shard_map/ppermute | solution.py:371
  8.1 1.0 %copy-start.4 = (bf16[1,1,128,2048]{3,2,1,0:T(8,128)(2,1)S(1)}, bf16[1,1,128,2048]{3,2,1,0:T(8,128)(2,1)}, u32[]{:S(2)}) copy-start(bf16[1,1,128,2048]{3,2,1,0:T(8,128)(2,1)} %param.10) | copy-start | bytes 1572868
  16.0 10.1 %copy-start.2 = (bf16[192,2048]{1,0:T(8,128)(2,1)S(1)}, bf16[192,2048]{1,0:T(8,128)(2,1)}, u32[]{:S(2)}) copy-start(bf16[192,2048]{1,0:T(8,128)(2,1)} %get-tuple-element.42.refs_1_) | copy-start | bytes 2359300
  16.0 10.1 %copy-start.5 = (bf16[96,2048]{1,0:T(8,128)(2,1)S(1)}, bf16[96,2048]{1,0:T(8,128)(2,1)}, u32[]{:S(2)}) copy-start(bf16[96,2048]{1,0:T(8,128)(2,1)} %get-tuple-element.41.refs_0_) | copy-start | bytes 1179652
  16.0 19.4 %collective-permute-start.8 = (bf16[96,2048]{1,0:T(8,128)(2,1)S(1)}, bf16[96,2048]{1,0:T(8,128)(2,1)S(1)}, u32[]{:S(2)}, u32[]{:S(2)}) collective-permute-start(bf16[96,2048]{1,0:T(8,128)(2,1)S(1)} %get-tuple-element.40), channel_id=1, source_target_pairs={{0,8},{1,9},{2,10},{3,11},{4,12},{5,13},{6,14},{7,15},{8,0},{9,1},... | collective-permute-start | bytes 1179656 | tf_op jit(solution)/shard_map/ppermute | solution.py:365
  18.7 16.9 %collective-permute-start.3 = (bf16[96,2048]{1,0:T(8,128)(2,1)S(1)}, bf16[96,2048]{1,0:T(8,128)(2,1)S(1)}, u32[]{:S(2)}, u32[]{:S(2)}) collective-permute-start(bf16[96,2048]{1,0:T(8,128)(2,1)S(1)} %get-tuple-element.36.own_in.refs_1_), channel_id=1, source_target_pairs={{0,4},{1,5},{2,6},{3,7},{4,0},{5,1},{6,2},{7,3},{8,12},{9,13},{10,... | collective-permute-start | bytes 1179656 | tf_op jit(solution)/shard_map/ppermute | solution.py:361
  24.4 18.9 %collective-permute-start.5 = (bf16[1024,384]{1,0:T(8,128)(2,1)S(1)}, bf16[1024,384]{1,0:T(8,128)(2,1)S(1)}, u32[]{:S(2)}, u32[]{:S(2)}) collective-permute-start(bf16[1024,384]{1,0:T(8,128)(2,1)S(1)} %hand_on.11.refs_0_.refs_2_), channel_id=1, source_target_pairs={{0,16},{16,0},{1,17},{17,1},{2,18},{18,2},{3,19},{19,3},{4,20},{20... | collective-permute-start | bytes 2359304 | tf_op jit(solution)/shard_map/ppermute | solution.py:374
  26.1 17.2 %collective-permute-start.10 = (bf16[96,2048]{1,0:T(8,128)(2,1)S(1)}, bf16[96,2048]{1,0:T(8,128)(2,1)S(1)}, u32[]{:S(2)}, u32[]{:S(2)}) collective-permute-start(bf16[96,2048]{1,0:T(8,128)(2,1)S(1)} %get-tuple-element.43), channel_id=1, source_target_pairs={{0,2},{1,3},{2,0},{3,1},{4,6},{5,7},{6,4},{7,5},{8,10},{9,11},{10,... | collective-permute-start | bytes 1179656 | tf_op jit(solution)/shard_map/ppermute | solution.py:361
  27.6 25.2 %collective-permute-start.14 = (bf16[192,2048]{1,0:T(8,128)(2,1)S(1)}, bf16[192,2048]{1,0:T(8,128)(2,1)S(1)}, u32[]{:S(2)}, u32[]{:S(2)}) collective-permute-start(bf16[192,2048]{1,0:T(8,128)(2,1)S(1)} %get-tuple-element.46), channel_id=1, source_target_pairs={{0,2},{1,3},{2,0},{3,1},{4,6},{5,7},{6,4},{7,5},{8,10},{9,11},{10,... | collective-permute-start | bytes 2359304 | tf_op jit(solution)/shard_map/ppermute | solution.py:361
  35.5 9.7 %collective-permute-start.9 = (bf16[96,2048]{1,0:T(8,128)(2,1)S(1)}, bf16[96,2048]{1,0:T(8,128)(2,1)S(1)}, u32[]{:S(2)}, u32[]{:S(2)}) collective-permute-start(bf16[96,2048]{1,0:T(8,128)(2,1)S(1)} %hand_on.13.own_in.refs_1_), channel_id=1, source_target_pairs={{0,4},{1,5},{2,6},{3,7},{4,0},{5,1},{6,2},{7,3},{8,12},{9,13},{10,... | collective-permute-start | bytes 1179656 | tf_op jit(solution)/shard_map/ppermute | solution.py:361
  43.3 13.8 %collective-permute-start.7 = (bf16[1024,384]{1,0:T(8,128)(2,1)S(1)}, bf16[1024,384]{1,0:T(8,128)(2,1)S(1)}, u32[]{:S(2)}, u32[]{:S(2)}) collective-permute-start(bf16[1024,384]{1,0:T(8,128)(2,1)S(1)} %get-tuple-element.39.refs_4_.refs_1_), channel_id=1, source_target_pairs={{0,1},{1,0},{2,3},{3,2},{4,5},{5,4},{6,7},{7,6},{8,9},{9,8},{10,11... | collective-permute-start | bytes 2359304 | tf_op jit(solution)/shard_map/ppermute | solution.py:361
  43.3 11.5 %collective-permute-start.11 = (bf16[96,2048]{1,0:T(8,128)(2,1)S(1)}, bf16[96,2048]{1,0:T(8,128)(2,1)S(1)}, u32[]{:S(2)}, u32[]{:S(2)}) collective-permute-start(bf16[96,2048]{1,0:T(8,128)(2,1)S(1)} %hand_on.19.refs_0_), channel_id=1, source_target_pairs={{0,16},{16,0},{1,17},{17,1},{2,18},{18,2},{3,19},{19,3},{4,20},{20... | collective-permute-start | bytes 1179656 | tf_op jit(solution)/shard_map/ppermute | solution.py:374
  44.8 12.3 %collective-permute-start.6 = (bf16[1024,384]{1,0:T(8,128)(2,1)S(1)}, bf16[1024,384]{1,0:T(8,128)(2,1)S(1)}, u32[]{:S(2)}, u32[]{:S(2)}) collective-permute-start(bf16[1024,384]{1,0:T(8,128)(2,1)S(1)} %get-tuple-element.38.refs_3_), channel_id=1, source_target_pairs={{0,1},{1,0},{2,3},{3,2},{4,5},{5,4},{6,7},{7,6},{8,9},{9,8},{10,11... | collective-permute-start | bytes 2359304 | tf_op jit(solution)/shard_map/ppermute | solution.py:361
  52.8 5.1 %collective-permute-start.15 = (bf16[192,2048]{1,0:T(8,128)(2,1)S(1)}, bf16[192,2048]{1,0:T(8,128)(2,1)S(1)}, u32[]{:S(2)}, u32[]{:S(2)}) collective-permute-start(bf16[192,2048]{1,0:T(8,128)(2,1)S(1)} %collective-permute-done.14.refs_9_), channel_id=1, source_target_pairs={{0,1},{1,0},{2,3},{3,2},{4,5},{5,4},{6,7},{7,6},{8,9},{9,8},{10,11... | collective-permute-start | bytes 2359304 | tf_op jit(solution)/shard_map/ppermute | solution.py:361
  54.8 3.1 %collective-permute-start.12 = (bf16[96,2048]{1,0:T(8,128)(2,1)S(1)}, bf16[96,2048]{1,0:T(8,128)(2,1)S(1)}, u32[]{:S(2)}, u32[]{:S(2)}) collective-permute-start(bf16[96,2048]{1,0:T(8,128)(2,1)S(1)} %get-tuple-element.44.refs_5_), channel_id=1, source_target_pairs={{0,1},{1,0},{2,3},{3,2},{4,5},{5,4},{6,7},{7,6},{8,9},{9,8},{10,11... | collective-permute-start | bytes 1179656 | tf_op jit(solution)/shard_map/ppermute | solution.py:361
  54.8 1.4 %copy-start = (bf16[2048,384]{1,0:T(8,128)(2,1)S(1)}, bf16[2048,384]{1,0:T(8,128)(2,1)}, u32[]{:S(2)}) copy-start(bf16[2048,384]{1,0:T(8,128)(2,1)} %w_own.3) | copy-start | bytes 4718596
  54.8 3.1 %collective-permute-start.13 = (bf16[96,2048]{1,0:T(8,128)(2,1)S(1)}, bf16[96,2048]{1,0:T(8,128)(2,1)S(1)}, u32[]{:S(2)}, u32[]{:S(2)}) collective-permute-start(bf16[96,2048]{1,0:T(8,128)(2,1)S(1)} %get-tuple-element.45.refs_6_), channel_id=1, source_target_pairs={{0,1},{1,0},{2,3},{3,2},{4,5},{5,4},{6,7},{7,6},{8,9},{9,8},{10,11... | collective-permute-start | bytes 1179656 | tf_op jit(solution)/shard_map/ppermute | solution.py:361
  57.1 1.4 %copy-start.1 = (bf16[384,2048]{1,0:T(8,128)(2,1)S(1)}, bf16[384,2048]{1,0:T(8,128)(2,1)}, u32[]{:S(2)}) copy-start(bf16[384,2048]{1,0:T(8,128)(2,1)} %refs_3_.3) | copy-start | bytes 4718596
  61.4 11.6 %collective-permute-start.16 = (bf16[96,2048]{1,0:T(8,128)(2,1)S(1)}, bf16[96,2048]{1,0:T(8,128)(2,1)S(1)}, u32[]{:S(2)}, u32[]{:S(2)}) collective-permute-start(bf16[96,2048]{1,0:T(8,128)(2,1)S(1)} %get-tuple-element.49), channel_id=1, source_target_pairs={{0,4},{1,5},{2,6},{3,7},{4,0},{5,1},{6,2},{7,3},{8,12},{9,13},{10,... | collective-permute-start | bytes 1179656 | tf_op jit(solution)/shard_map/ppermute | solution.py:361
  73.1 20.2 %collective-permute-start.18 = (bf16[96,2048]{1,0:T(8,128)(2,1)S(1)}, bf16[96,2048]{1,0:T(8,128)(2,1)S(1)}, u32[]{:S(2)}, u32[]{:S(2)}) collective-permute-start(bf16[96,2048]{1,0:T(8,128)(2,1)S(1)} %get-tuple-element.52), channel_id=1, source_target_pairs={{0,8},{1,9},{2,10},{3,11},{4,12},{5,13},{6,14},{7,15},{8,0},{9,1},... | collective-permute-start | bytes 1179656 | tf_op jit(solution)/shard_map/ppermute | solution.py:365
  75.7 17.9 %collective-permute-start.17 = (bf16[96,2048]{1,0:T(8,128)(2,1)S(1)}, bf16[96,2048]{1,0:T(8,128)(2,1)S(1)}, u32[]{:S(2)}, u32[]{:S(2)}) collective-permute-start(bf16[96,2048]{1,0:T(8,128)(2,1)S(1)} %get-tuple-element.51), channel_id=1, source_target_pairs={{0,4},{1,5},{2,6},{3,7},{4,0},{5,1},{6,2},{7,3},{8,12},{9,13},{10,... | collective-permute-start | bytes 1179656 | tf_op jit(solution)/shard_map/ppermute | solution.py:361

commit v10 on v9

--- a/solution.py
+++ b/solution.py
@@ -165,15 +165,37 @@
     return pl.multiple_of(at * size, size)
 
 
-def part_kernel(pipes, pipe_ref, w_in, w_out, in_part, out_part, out_rest, sems):
-    depth, size = in_part.shape[0], out_part.shape[0]
-    pipe = pipe_ref[0]
+def part_kernel(pipe_ref, whole, part, sem):
+    size = part.shape[0]
+    at = pl.multiple_of(pipe_ref[0] * size, size)
+    copy = pltpu.make_async_copy(whole.at[pl.ds(at, size)], part, sem)
+    copy.start()
+    copy.wait()
+
+
+def cut_part(pipe, whole, size):
+    return call(
+        part_kernel,
+        struct((size, whole.shape[1])),
+        [SMEM, ANY],
+        "weight_part",
+        1,
+        4 * size * whole.shape[1],
+        scratch=[pltpu.SemaphoreType.DMA],
+        limit=PART_LIMIT,
+    )(pipe, whole)
+
+
+def hold_kernel(pipes, pipe_ref, w_in, w_out, in_held, out_held, out_part, out_rest, sems):
+    size = out_part.shape[0]
+    at = pl.multiple_of(pipe_ref[0] * size, size)
     copies = [
         pltpu.make_async_copy(source, target, sems.at[i])
         for i, (source, target) in enumerate(
             (
-                (w_in.at[pl.ds(pl.multiple_of(pipe * depth, depth), depth)], in_part),
-                (w_out.at[pl.ds(pl.multiple_of(pipe * size, size), size)], out_part),
+                (w_in, in_held),
+                (w_out, out_held),
+                (w_out.at[pl.ds(at, size)], out_part),
                 (w_out.at[pipes * size :], out_rest),
             )
         )
@@ -184,22 +206,22 @@
         copy.wait()
 
 
-def parts(pipe, w_in, w_out, pipes):
-    width, units = w_in.shape
+def hold(pipe, w_in, w_out, pipes):
+    units, width = w_out.shape
     size = units // 2 // pipes // 16 * 16
     return call(
-        functools.partial(part_kernel, pipes),
+        functools.partial(hold_kernel, pipes),
         [
-            struct((width // pipes, units)),
+            struct(w_in.shape),
+            struct(w_out.shape),
             struct((size, width)),
             struct((units - pipes * size, width)),
         ],
         [SMEM, ANY, ANY],
-        "weight_parts",
+        "hold_weights",
         1,
-        4 * units * width,
-        scratch=[pltpu.SemaphoreType.DMA((3,))],
-        limit=PART_LIMIT,
+        8 * units * width,
+        scratch=[pltpu.SemaphoreType.DMA((4,))],
     )(pipe, w_in, w_out)
 
 
@@ -272,12 +294,12 @@
         held[pl.ds(pl.multiple_of(units + at, size), size)] = pair_parts[shift][...]
     held[pipes * size : units] = y_rest[...]
     held[units + pipes * size :] = pair_rest[...]
+    activation = jnp.concatenate([act_ref[...], act_y_ref[...]], axis=1)
     step = 512
     for at in range(0, width, step):
         cols = slice(at, at + step)
-        weights = jnp.concatenate([w_own[:, cols], w_pair[:, cols]], axis=0)
-        part = jnp.dot(act_ref[...], weights, preferred_element_type=jnp.float32)
-        part = part + jnp.dot(act_y_ref[...], held[:, cols], preferred_element_type=jnp.float32)
+        weights = jnp.concatenate([w_own[:, cols], w_pair[:, cols], held[:, cols]], axis=0)
+        part = jnp.dot(activation, weights, preferred_element_type=jnp.float32)
         part = part.astype(jnp.bfloat16)
         own_ref[:, cols] = part[:rows]
         z_ref[:, cols] = part[rows:]
@@ -379,7 +401,8 @@
     pipe = lax.axis_index("pipe").astype(jnp.int32)
     w_in_pair, w_out_pair = across(w_in, 1), across(w_out, 1)
     pipe = pipe.reshape(1)
-    in_part, out_part, out_rest = parts(pipe, w_in, w_out, pipes)
+    in_part = cut_part(pipe, w_in, width // pipes)
+    w_in_held, w_out_held, out_part, out_rest = hold(pipe, w_in, w_out, pipes)
     in_y = across(in_part, 2)
 
     group = (lax.axis_index("expert") // WSPLIT).astype(jnp.int32).reshape(1)
@@ -396,7 +419,7 @@
     )
     flat, gates = staged[4:]
     hidden, near, *packed = attend(
-        *staged[:4], kv_pieces, groups, cap, after=[w_in_pair, w_out_pair]
+        *staged[:4], kv_pieces, groups, cap, after=[w_in_pair, w_out_pair, w_out_held]
     )
     far = [groups_on(block, count) for count, block in enumerate(packed, 1)]
     far = jnp.concatenate(far, axis=0) if len(far) > 1 else far[0]
@@ -407,10 +430,6 @@
     rest_y = across(out_rest, 2)
     in_y = after_all(along(in_y), [])
     in_pair = paired(in_y)
-    (out_y,) = after_all([out_y], [in_y[-1]])
-    out_y = after_all(along(out_y), [])
-    out_pair = paired(out_y)
-    rests = [rest_y, across(rest_y, 1)]
 
     near_z = across(near, 4)
     far = [far]
@@ -422,12 +441,21 @@
         far_z = after_all(far_z, [], FAR_WEIGHT)
     (far_z,) = far_z
 
-    def experts(own, z, after=()):
-        acts = up(own, z, [w_in, w_in_pair]), up_y(pipe, own, z, in_y, in_pair, after)
-        return down(pipe, acts, [w_out, w_out_pair], out_y, out_pair, rests)
-
-    far_own, far_sent = experts(far, far_z)
-    near_own, near_sent = experts(near, near_z, [far_own])
+    def experts_up(own, z, after=()):
+        own_act = up(own, z, [w_in_held, w_in_pair])
+        return own_act, up_y(pipe, own, z, in_y, in_pair, after)
+
+    far_acts = experts_up(far, far_z)
+    (out_y,) = after_all([out_y], [in_y[-1]])
+    out_y = after_all(along(out_y), [*far_acts])
+    out_pair = paired(out_y)
+    rests = [rest_y, across(rest_y, 1)]
+
+    def experts_down(acts):
+        return down(pipe, acts, [w_out_held, w_out_pair], out_y, out_pair, rests)
+
+    far_own, far_sent = experts_down(far_acts)
+    near_own, near_sent = experts_down(experts_up(near, near_z, [far_own]))
     far_sum, near_sent = total(far_own, across(far_sent, 4), [near_sent])
     backs = [
         groups_on(far_sum[(count - 1) * cap : count * cap], groups - count)

time: 95 us -> 94.1 us (level)
  waiting for transfers between devices: 54.8 us -> 44.8 us
  local copies, waits for them, and re-layouts: 2.54 us -> 10.9 us
    unnamed x22 -> x32, local copies, waits for them, and re-layouts: 2.46 us -> 10.8 us
    ppermute x2, waiting for transfers between devices: 8.29 us -> 1.22 us  [along(): return [value] + [lax.ppermute(value, 'pipe', perm) for perm in perms]]
    ppermute x1, waiting for transfers between devices: 5.24 us -> 0.01 us  [body(): kv_pieces.append(lax.ppermute(kv, 'pipe', perm))]
    ppermute x2, waiting for transfers between devices: 23.3 us -> 28.2 us  [groups_on(): lax.ppermute(value, 'expert', [(i, (i + shift) % devices) for i in range(...]
    ppermute x14, waiting for transfers between devices: 17.9 us -> 15.4 us  [across(): return lax.ppermute(value, 'expert', [(i, i ^ bit) for i in range(devices)])]
    pallas_call x1 -> x2, Pallas kernels: 2.86 us -> 2.56 us  [the longest x1 2.06 us: cut_part(): call(part_kernel, struct((size, whole.shape[1])), [SMEM, ANY], 'weight_pa...]
  transfers between devices with their start and end apart: 19 -> 19, of which waited for: 11 -> 10; matrix products, arithmetic and copies ran while one was open for 0% -> 0% of each run, Pallas kernels for 11% -> 12%
where the time goes in v10:
time: 94.1 us; the launch traced here: 93.6 us
  waiting for transfers between devices  44.8 us (48%)
  starting transfers between devices  22.3 us (24%)
  Pallas kernels  15.4 us (16%)
  local copies, waits for them, and re-layouts  10.9 us (12%)
    ppermute x2, waiting for transfers between devices, groups_on(): lax.ppermute(value, 'expert', [(i, (i + shift) % devices) for i in range(...  28.2 us
    ppermute x14, waiting for transfers between devices, across(): return lax.ppermute(value, 'expert', [(i, i ^ bit) for i in range(devices)])  15.4 us
    ppermute x14, starting transfers between devices, across(): return lax.ppermute(value, 'expert', [(i, i ^ bit) for i in range(devices)])  12.6 us
    unnamed x32, local copies, waits for them, and re-layouts  10.8 us
    pallas_call x2, Pallas kernels, down(): call(functools.partial(down_kernel, pipes), [struct((rows, width))] * 2,...  5.79 us
    ppermute x2, starting transfers between devices, groups_on(): lax.ppermute(value, 'expert', [(i, (i + shift) % devices) for i in range(...  5.32 us
    ppermute x2, starting transfers between devices, along(): return [value] + [lax.ppermute(value, 'pipe', perm) for perm in perms]  2.82 us
    pallas_call x1, Pallas kernels, attend(): call(functools.partial(attend_kernel, pieces, groups, cap), outs, [VMEM]...  2.38 us
  transfers between devices with their start and end apart: 19, of which 10 were waited for; matrix products, arithmetic and copies ran while one was open for 0% of the time, Pallas kernels for 12%

profile of v10, /device:TPU:0, one launch (start us, length us, event | category | flops | bytes accessed | tf_op | source)
XLA Modules:
  0.0 93.6 jit_solution(17513609213218843552)
XLA Ops:
  0.0 0.5 collective-permute-start.2
  0.5 2.1 %weight_part.1 = bf16[1024,384]{1,0:T(8,128)(2,1)} custom-call(s32[1]{0:T(128)} %bitcast.10.pipe_ref.refs_0_, bf16[2048,384]{1,0:T(8,128)(2,1)} %whole.1), custom_call_target="tpu_custom_call" | custom-call | flops 1 | bytes 1572864 | tf_op jit(solution)/shard_map/weight_part/pallas_call | solution.py:177
  2.6 3.0 %collective-permute-start.4 = (bf16[1024,384]{1,0:T(8,128)(2,1)}, bf16[1024,384]{1,0:T(8,128)(2,1)S(1)}, u32[]{:S(2)}, u32[]{:S(2)}) collective-permute-start(bf16[1024,384]{1,0:T(8,128)(2,1)} %weight_part.1), channel_id=1, source_target_pairs={{0,2},{1,3},{2,0},{3,1},{4,6},{5,7},{6,4},{7,5},{8,10},{9,11},{10,... | collective-permute-start | bytes 2359304 | tf_op jit(solution)/shard_map/ppermute | solution.py:383
  5.6 0.1 copy.25
  5.7 1.6 %collective-permute-start = (bf16[64,2048]{1,0:T(8,128)(2,1)S(1)}, bf16[64,2048]{1,0:T(8,128)(2,1)}, u32[]{:S(2)}, u32[]{:S(2)}) collective-permute-start(bf16[64,2048]{1,0:T(8,128)(2,1)S(1)} %bitcast.13), channel_id=1, source_target_pairs={{0,16},{16,0},{1,17},{17,1},{2,18},{18,2},{3,19},{19,3},{4,20},{20... | collective-permute-start | bytes 786440 | tf_op jit(solution)/shard_map/ppermute | solution.py:393
  7.3 1.4 %copy-done.5 = bf16[2048,384]{1,0:T(8,128)(2,1)S(1)} copy-done((bf16[2048,384]{1,0:T(8,128)(2,1)S(1)}, bf16[2048,384]{1,0:T(8,128)(2,1)}, u32[]{:S(2)}) %copy-start.5) | copy-done | bytes 1572888
  8.7 1.4 %copy-done.6 = bf16[384,2048]{1,0:T(8,128)(2,1)S(1)} copy-done((bf16[384,2048]{1,0:T(8,128)(2,1)S(1)}, bf16[384,2048]{1,0:T(8,128)(2,1)}, u32[]{:S(2)}) %copy-start.6) | copy-done | bytes 1572888
  10.1 0.5 hold_weights.1
  10.6 1.2 %copy-done = bf16[384,2048]{1,0:T(8,128)(2,1)} copy-done((bf16[384,2048]{1,0:T(8,128)(2,1)}, bf16[384,2048]{1,0:T(8,128)(2,1)S(1)}, u32[]{:S(2)}) %copy-start) | copy-done | bytes 1572888
  11.8 1.1 %copy-done.3 = bf16[2048,384]{1,0:T(8,128)(2,1)} copy-done((bf16[2048,384]{1,0:T(8,128)(2,1)}, bf16[2048,384]{1,0:T(8,128)(2,1)S(1)}, u32[]{:S(2)}) %copy-start.3) | copy-done | bytes 1572888
  12.9 0.7 copy-done.9
  13.7 1.0 %copy-done.7 = bf16[1,1,128,2048]{3,2,1,0:T(8,128)(2,1)S(1)} copy-done((bf16[1,1,128,2048]{3,2,1,0:T(8,128)(2,1)S(1)}, bf16[1,1,128,2048]{3,2,1,0:T(8,128)(2,1)}, u32[]{:S(2)}) %copy-start.7) | copy-done | bytes 524312
  14.7 1.0 %copy-done.8 = bf16[1,1,128,2048]{3,2,1,0:T(8,128)(2,1)S(1)} copy-done((bf16[1,1,128,2048]{3,2,1,0:T(8,128)(2,1)S(1)}, bf16[1,1,128,2048]{3,2,1,0:T(8,128)(2,1)}, u32[]{:S(2)}) %copy-start.8) | copy-done | bytes 524312
  15.7 0.1 stage.1
  15.9 1.4 %copy-done.1 = bf16[384,2048]{1,0:T(8,128)(2,1)S(1)} copy-done((bf16[384,2048]{1,0:T(8,128)(2,1)S(1)}, bf16[384,2048]{1,0:T(8,128)(2,1)}, u32[]{:S(2)}) %copy-start.1) | copy-done | bytes 1572888
  17.3 2.4 %attend.1 = (f32[128,2048]{1,0:T(8,128)S(1)}, bf16[96,2048]{1,0:T(8,128)(2,1)S(1)}, bf16[96,2048]{1,0:T(8,128)(2,1)S(1)}) custom-call(bf16[128,2048]{1,0:T(8,128)(2,1)S(1)} %get-tuple-element.30.refs_0_, bf16[128,2048]{1,0:T(8,128)(2,1)S(1)} %get-tuple-element.31.refs_1_, f32[1,2048]{1,0:T(1,128)S(1)} %get-tuple-element.32.refs_2_, ...), custom_call_target="tpu_custom_call" | custom-call | flops 134217728 | bytes 3145728 | tf_op jit(solution)/shard_map/attend/pallas_call | solution.py:152
  19.7 2.7 %collective-permute-start.8 = (bf16[96,2048]{1,0:T(8,128)(2,1)S(1)}, bf16[96,2048]{1,0:T(8,128)(2,1)S(1)}, u32[]{:S(2)}, u32[]{:S(2)}) collective-permute-start(bf16[96,2048]{1,0:T(8,128)(2,1)S(1)} %get-tuple-element.42), channel_id=1, source_target_pairs={{0,8},{1,9},{2,10},{3,11},{4,12},{5,13},{6,14},{7,15},{8,0},{9,1},... | collective-permute-start | bytes 1179656 | tf_op jit(solution)/shard_map/ppermute | solution.py:387
  22.4 1.6 %collective-permute-start.3 = (bf16[96,2048]{1,0:T(8,128)(2,1)S(1)}, bf16[96,2048]{1,0:T(8,128)(2,1)S(1)}, u32[]{:S(2)}, u32[]{:S(2)}) collective-permute-start(bf16[96,2048]{1,0:T(8,128)(2,1)S(1)} %get-tuple-element.38.own_in.refs_1_), channel_id=1, source_target_pairs={{0,4},{1,5},{2,6},{3,7},{4,0},{5,1},{6,2},{7,3},{8,12},{9,13},{10,... | collective-permute-start | bytes 1179656 | tf_op jit(solution)/shard_map/ppermute | solution.py:383
  24.0 1.4 %collective-permute-start.5 = (bf16[1024,384]{1,0:T(8,128)(2,1)S(1)}, bf16[1024,384]{1,0:T(8,128)(2,1)S(1)}, u32[]{:S(2)}, u32[]{:S(2)}) collective-permute-start(bf16[1024,384]{1,0:T(8,128)(2,1)S(1)} %hand_on.11.refs_0_.refs_2_), channel_id=1, source_target_pairs={{0,16},{16,0},{1,17},{17,1},{2,18},{18,2},{3,19},{19,3},{4,20},{20... | collective-permute-start | bytes 2359304 | tf_op jit(solution)/shard_map/ppermute | solution.py:396
  25.3 1.5 %collective-permute-start.10 = (bf16[96,2048]{1,0:T(8,128)(2,1)S(1)}, bf16[96,2048]{1,0:T(8,128)(2,1)S(1)}, u32[]{:S(2)}, u32[]{:S(2)}) collective-permute-start(bf16[96,2048]{1,0:T(8,128)(2,1)S(1)} %get-tuple-element.45), channel_id=1, source_target_pairs={{0,2},{1,3},{2,0},{3,1},{4,6},{5,7},{6,4},{7,5},{8,10},{9,11},{10,... | collective-permute-start | bytes 1179656 | tf_op jit(solution)/shard_map/ppermute | solution.py:383
  26.8 0.5 collective-permute-start.14
  27.3 12.4 %collective-permute-done.8.refs_0_ = bf16[96,2048]{1,0:T(8,128)(2,1)S(1)} collective-permute-done((bf16[96,2048]{1,0:T(8,128)(2,1)S(1)}, bf16[96,2048]{1,0:T(8,128)(2,1)S(1)}, u32[]{:S(2)}, u32[]{:S(2)}) %collective-permute-start.8) | collective-permute-done | bytes 393248 | tf_op jit(solution)/shard_map/ppermute | solution.py:387
  39.7 0.2 collective-permute-done.3.z_in.refs_1_.refs_2_
  39.9 1.4 %collective-permute-start.9 = (bf16[96,2048]{1,0:T(8,128)(2,1)S(1)}, bf16[96,2048]{1,0:T(8,128)(2,1)S(1)}, u32[]{:S(2)}, u32[]{:S(2)}) collective-permute-start(bf16[96,2048]{1,0:T(8,128)(2,1)S(1)} %hand_on.13.own_in.refs_1_), channel_id=1, source_target_pairs={{0,4},{1,5},{2,6},{3,7},{4,0},{5,1},{6,2},{7,3},{8,12},{9,13},{10,... | collective-permute-start | bytes 1179656 | tf_op jit(solution)/shard_map/ppermute | solution.py:383
  41.4 1.2 %collective-permute-done.5.refs_1_ = bf16[1024,384]{1,0:T(8,128)(2,1)S(1)} collective-permute-done((bf16[1024,384]{1,0:T(8,128)(2,1)S(1)}, bf16[1024,384]{1,0:T(8,128)(2,1)S(1)}, u32[]{:S(2)}, u32[]{:S(2)}) %collective-permute-start.5) | collective-permute-done | bytes 786464 | tf_op jit(solution)/shard_map/ppermute | solution.py:396
  42.6 1.5 %collective-permute-start.11 = (bf16[96,2048]{1,0:T(8,128)(2,1)S(1)}, bf16[96,2048]{1,0:T(8,128)(2,1)S(1)}, u32[]{:S(2)}, u32[]{:S(2)}) collective-permute-start(bf16[96,2048]{1,0:T(8,128)(2,1)S(1)} %hand_on.19.refs_0_), channel_id=1, source_target_pairs={{0,16},{16,0},{1,17},{17,1},{2,18},{18,2},{3,19},{19,3},{4,20},{20... | collective-permute-start | bytes 1179656 | tf_op jit(solution)/shard_map/ppermute | solution.py:396
  44.1 0.2 collective-permute-start.6
  44.2 5.4 %collective-permute-done.9.refs_0_ = bf16[96,2048]{1,0:T(8,128)(2,1)S(1)} collective-permute-done((bf16[96,2048]{1,0:T(8,128)(2,1)S(1)}, bf16[96,2048]{1,0:T(8,128)(2,1)S(1)}, u32[]{:S(2)}, u32[]{:S(2)}) %collective-permute-start.9) | collective-permute-done | bytes 393248 | tf_op jit(solution)/shard_map/ppermute | solution.py:383
  49.6 2.5 %collective-permute-done.14.refs_9_ = bf16[192,2048]{1,0:T(8,128)(2,1)S(1)} collective-permute-done((bf16[192,2048]{1,0:T(8,128)(2,1)S(1)}, bf16[192,2048]{1,0:T(8,128)(2,1)S(1)}, u32[]{:S(2)}, u32[]{:S(2)}) %collective-permute-start.14) | collective-permute-done | bytes 786464 | tf_op jit(solution)/shard_map/ppermute | solution.py:383
  52.1 1.4 %copy-done.4 = bf16[2048,384]{1,0:T(8,128)(2,1)S(1)} copy-done((bf16[2048,384]{1,0:T(8,128)(2,1)S(1)}, bf16[2048,384]{1,0:T(8,128)(2,1)}, u32[]{:S(2)}) %copy-start.4) | copy-done | bytes 1572888
  53.5 0.8 expert_up.3.refs_2_.refs_1_
  54.4 0.9 expert_up_y.2.refs_3_.refs_2_
  55.3 0.6 collective-permute-start.12
  55.8 0.1 collective-permute-start.13
  55.9 1.3 %collective-permute-done.12.refs_7_ = bf16[96,2048]{1,0:T(8,128)(2,1)S(1)} collective-permute-done((bf16[96,2048]{1,0:T(8,128)(2,1)S(1)}, bf16[96,2048]{1,0:T(8,128)(2,1)S(1)}, u32[]{:S(2)}, u32[]{:S(2)}) %collective-permute-start.12) | collective-permute-done | bytes 393248 | tf_op jit(solution)/shard_map/ppermute | solution.py:383
  57.2 0.6 collective-permute-done.13.refs_8_
  57.7 2.9 %expert_down.2 = (bf16[96,2048]{1,0:T(8,128)(2,1)S(1)}, bf16[96,2048]{1,0:T(8,128)(2,1)S(1)}) custom-call(s32[1]{0:T(128)} %bitcast.10.pipe_ref.refs_0_, bf16[192,768]{1,0:T(8,128)(2,1)S(1)} %expert_up.3.refs_2_.refs_1_, bf16[192,768]{1,0:T(8,128)(2,1)S(1)} %expert_up_y.2.refs_3_.refs_2_, bf16[384,2048]{1,0:T(8,128)(2,1)S(1)} %copy-done.2, ...), custom_call_target="tpu_custom_call" | custom-call | flops 1207959552 | bytes 6291456 | tf_op jit(solution)/shard_map/expert_down/pallas_call | solution.py:312
  60.6 1.7 %collective-permute-start.16 = (bf16[96,2048]{1,0:T(8,128)(2,1)S(1)}, bf16[96,2048]{1,0:T(8,128)(2,1)S(1)}, u32[]{:S(2)}, u32[]{:S(2)}) collective-permute-start(bf16[96,2048]{1,0:T(8,128)(2,1)S(1)} %get-tuple-element.51), channel_id=1, source_target_pairs={{0,4},{1,5},{2,6},{3,7},{4,0},{5,1},{6,2},{7,3},{8,12},{9,13},{10,... | collective-permute-start | bytes 1179656 | tf_op jit(solution)/shard_map/ppermute | solution.py:383
  62.3 0.8 expert_up.2.refs_1_
  63.1 0.9 expert_up_y.3.refs_2_
  64.0 2.9 %expert_down.3 = (bf16[96,2048]{1,0:T(8,128)(2,1)S(1)}, bf16[96,2048]{1,0:T(8,128)(2,1)S(1)}) custom-call(s32[1]{0:T(128)} %bitcast.10.pipe_ref.refs_0_, bf16[192,768]{1,0:T(8,128)(2,1)S(1)} %expert_up.2.refs_1_, bf16[192,768]{1,0:T(8,128)(2,1)S(1)} %expert_up_y.3.refs_2_, bf16[384,2048]{1,0:T(8,128)(2,1)S(1)} %copy-done.2, ...), custom_call_target="tpu_custom_call" | custom-call | flops 1207959552 | bytes 6291456 | tf_op jit(solution)/shard_map/expert_down/pallas_call | solution.py:312
  66.9 5.2 %collective-permute-done.16.z_ref = bf16[96,2048]{1,0:T(8,128)(2,1)S(1)} collective-permute-done((bf16[96,2048]{1,0:T(8,128)(2,1)S(1)}, bf16[96,2048]{1,0:T(8,128)(2,1)S(1)}, u32[]{:S(2)}, u32[]{:S(2)}) %collective-permute-start.16) | collective-permute-done | bytes 393248 | tf_op jit(solution)/shard_map/ppermute | solution.py:383
  72.1 0.1 far_total.1
  72.2 2.7 %collective-permute-start.18 = (bf16[96,2048]{1,0:T(8,128)(2,1)S(1)}, bf16[96,2048]{1,0:T(8,128)(2,1)S(1)}, u32[]{:S(2)}, u32[]{:S(2)}) collective-permute-start(bf16[96,2048]{1,0:T(8,128)(2,1)S(1)} %get-tuple-element.54), channel_id=1, source_target_pairs={{0,8},{1,9},{2,10},{3,11},{4,12},{5,13},{6,14},{7,15},{8,0},{9,1},... | collective-permute-start | bytes 1179656 | tf_op jit(solution)/shard_map/ppermute | solution.py:387
  74.9 1.6 %collective-permute-start.17 = (bf16[96,2048]{1,0:T(8,128)(2,1)S(1)}, bf16[96,2048]{1,0:T(8,128)(2,1)S(1)}, u32[]{:S(2)}, u32[]{:S(2)}) collective-permute-start(bf16[96,2048]{1,0:T(8,128)(2,1)S(1)} %get-tuple-element.53), channel_id=1, source_target_pairs={{0,4},{1,5},{2,6},{3,7},{4,0},{5,1},{6,2},{7,3},{8,12},{9,13},{10,... | collective-permute-start | bytes 1179656 | tf_op jit(solution)/shard_map/ppermute | solution.py:383
  76.4 15.8 %collective-permute-done.18.refs_0_ = bf16[96,2048]{1,0:T(8,128)(2,1)S(1)} collective-permute-done((bf16[96,2048]{1,0:T(8,128)(2,1)S(1)}, bf16[96,2048]{1,0:T(8,128)(2,1)S(1)}, u32[]{:S(2)}, u32[]{:S(2)}) %collective-permute-start.18) | collective-permute-done | bytes 393248 | tf_op jit(solution)/shard_map/ppermute | solution.py:387
  92.3 0.2 collective-permute-done.17.refs_4_
  92.5 1.2 %finish.1 = bf16[128,2048]{1,0:T(8,128)(2,1)} custom-call(f32[128,2048]{1,0:T(8,128)S(1)} %get-tuple-element.35.refs_0_, f32[128,1]{1,0:T(8,128)S(1)} %get-tuple-element.36.refs_1_, s32[128,1]{1,0:T(8,128)S(1)} %get-tuple-element.37.refs_2_, bf16[96,2048]{1,0:T(8,128)(2,1)S(1)} %get-tuple-element.50.refs_3_, ...), custom_call_target="tpu_custom_call" | custom-call | flops 201326592 | bytes 4194304 | tf_op jit(solution)/shard_map/finish/pallas_call | solution.py:365
  (46 shorter events, 0.1 us)
Async XLA Ops:
  0.0 5.6 %copy-start.15 = (bf16[1,32,2,2048]{3,2,1,0:T(2,128)(2,1)S(1)}, bf16[1,32,2,2048]{3,2,1,0:T(2,128)(2,1)}, u32[]{:S(2)}) copy-start(bf16[1,32,2,2048]{3,2,1,0:T(2,128)(2,1)} %param.11) | copy-start | bytes 786436
  0.0 15.9 %collective-permute-start.2 = (bf16[384,2048]{1,0:T(8,128)(2,1)}, bf16[384,2048]{1,0:T(8,128)(2,1)}, u32[]{:S(2)}, u32[]{:S(2)}) collective-permute-start(bf16[384,2048]{1,0:T(8,128)(2,1)} %w_out.1), channel_id=1, source_target_pairs={{0,1},{1,0},{2,3},{3,2},{4,5},{5,4},{6,7},{7,6},{8,9},{9,8},{10,11... | collective-permute-start | bytes 4718600 | tf_op jit(solution)/shard_map/ppermute | solution.py:383
  0.5 15.4 %collective-permute-start.1 = (bf16[2048,384]{1,0:T(8,128)(2,1)}, bf16[2048,384]{1,0:T(8,128)(2,1)S(1)}, u32[]{:S(2)}, u32[]{:S(2)}) collective-permute-start(bf16[2048,384]{1,0:T(8,128)(2,1)} %whole.1), channel_id=1, source_target_pairs={{0,1},{1,0},{2,3},{3,2},{4,5},{5,4},{6,7},{7,6},{8,9},{9,8},{10,11... | collective-permute-start | bytes 4718600 | tf_op jit(solution)/shard_map/ppermute | solution.py:383
  2.6 21.4 %collective-permute-start.4 = (bf16[1024,384]{1,0:T(8,128)(2,1)}, bf16[1024,384]{1,0:T(8,128)(2,1)S(1)}, u32[]{:S(2)}, u32[]{:S(2)}) collective-permute-start(bf16[1024,384]{1,0:T(8,128)(2,1)} %weight_part.1), channel_id=1, source_target_pairs={{0,2},{1,3},{2,0},{3,1},{4,6},{5,7},{6,4},{7,5},{8,10},{9,11},{10,... | collective-permute-start | bytes 2359304 | tf_op jit(solution)/shard_map/ppermute | solution.py:383
  5.7 10.2 %collective-permute-start = (bf16[64,2048]{1,0:T(8,128)(2,1)S(1)}, bf16[64,2048]{1,0:T(8,128)(2,1)}, u32[]{:S(2)}, u32[]{:S(2)}) collective-permute-start(bf16[64,2048]{1,0:T(8,128)(2,1)S(1)} %bitcast.13), channel_id=1, source_target_pairs={{0,16},{16,0},{1,17},{17,1},{2,18},{18,2},{3,19},{19,3},{4,20},{20... | collective-permute-start | bytes 786440 | tf_op jit(solution)/shard_map/ppermute | solution.py:393
  7.3 1.4 %copy-start.5 = (bf16[2048,384]{1,0:T(8,128)(2,1)S(1)}, bf16[2048,384]{1,0:T(8,128)(2,1)}, u32[]{:S(2)}) copy-start(bf16[2048,384]{1,0:T(8,128)(2,1)} %whole.1) | copy-start | bytes 4718596
  8.7 1.4 %copy-start.6 = (bf16[384,2048]{1,0:T(8,128)(2,1)S(1)}, bf16[384,2048]{1,0:T(8,128)(2,1)}, u32[]{:S(2)}) copy-start(bf16[384,2048]{1,0:T(8,128)(2,1)} %w_out.1) | copy-start | bytes 4718596
  10.1 3.6 %copy-start.11 = (f32[2048]{0:T(1024)S(1)}, f32[2048]{0:T(1024)}, u32[]{:S(2)}) copy-start(f32[2048]{0:T(1024)} %param.12) | copy-start | bytes 24580
  10.1 3.6 %copy-start.12 = (s32[1,1,128]{2,1,0:T(1,128)S(1)}, s32[1,1,128]{2,1,0:T(1,128)}, u32[]{:S(2)}) copy-start(s32[1,1,128]{2,1,0:T(1,128)} %param.15) | copy-start | bytes 1540
  10.1 3.6 %copy-start.13 = (s32[1,1,128]{2,1,0:T(1,128)S(1)}, s32[1,1,128]{2,1,0:T(1,128)}, u32[]{:S(2)}) copy-start(s32[1,1,128]{2,1,0:T(1,128)} %param.16) | copy-start | bytes 1540
  10.1 3.6 %copy-start.14 = (f32[1,1,128]{2,1,0:T(1,128)S(1)}, f32[1,1,128]{2,1,0:T(1,128)}, u32[]{:S(2)}) copy-start(f32[1,1,128]{2,1,0:T(1,128)} %param.17) | copy-start | bytes 1540
  10.6 1.2 %copy-start = (bf16[384,2048]{1,0:T(8,128)(2,1)}, bf16[384,2048]{1,0:T(8,128)(2,1)S(1)}, u32[]{:S(2)}) copy-start(bf16[384,2048]{1,0:T(8,128)(2,1)S(1)} %get-tuple-element.34.refs_8_.refs_3_) | copy-start | bytes 4718596
  11.8 1.1 %copy-start.3 = (bf16[2048,384]{1,0:T(8,128)(2,1)}, bf16[2048,384]{1,0:T(8,128)(2,1)S(1)}, u32[]{:S(2)}) copy-start(bf16[2048,384]{1,0:T(8,128)(2,1)S(1)} %get-tuple-element.39.w_own) | copy-start | bytes 4718596
  12.9 0.7 copy-start.9
  13.7 1.0 %copy-start.7 = (bf16[1,1,128,2048]{3,2,1,0:T(8,128)(2,1)S(1)}, bf16[1,1,128,2048]{3,2,1,0:T(8,128)(2,1)}, u32[]{:S(2)}) copy-start(bf16[1,1,128,2048]{3,2,1,0:T(8,128)(2,1)} %param.9) | copy-start | bytes 1572868
  14.7 1.0 %copy-start.8 = (bf16[1,1,128,2048]{3,2,1,0:T(8,128)(2,1)S(1)}, bf16[1,1,128,2048]{3,2,1,0:T(8,128)(2,1)}, u32[]{:S(2)}) copy-start(bf16[1,1,128,2048]{3,2,1,0:T(8,128)(2,1)} %param.10) | copy-start | bytes 1572868
  15.9 1.4 %copy-start.1 = (bf16[384,2048]{1,0:T(8,128)(2,1)S(1)}, bf16[384,2048]{1,0:T(8,128)(2,1)}, u32[]{:S(2)}) copy-start(bf16[384,2048]{1,0:T(8,128)(2,1)} %copy-done) | copy-start | bytes 4718596
  19.7 5.6 %copy-start.10 = (bf16[96,2048]{1,0:T(8,128)(2,1)S(1)}, bf16[96,2048]{1,0:T(8,128)(2,1)}, u32[]{:S(2)}) copy-start(bf16[96,2048]{1,0:T(8,128)(2,1)} %copy-done.9) | copy-start | bytes 1179652
  19.7 20.0 %collective-permute-start.8 = (bf16[96,2048]{1,0:T(8,128)(2,1)S(1)}, bf16[96,2048]{1,0:T(8,128)(2,1)S(1)}, u32[]{:S(2)}, u32[]{:S(2)}) collective-permute-start(bf16[96,2048]{1,0:T(8,128)(2,1)S(1)} %get-tuple-element.42), channel_id=1, source_target_pairs={{0,8},{1,9},{2,10},{3,11},{4,12},{5,13},{6,14},{7,15},{8,0},{9,1},... | collective-permute-start | bytes 1179656 | tf_op jit(solution)/shard_map/ppermute | solution.py:387
  22.4 17.6 %collective-permute-start.3 = (bf16[96,2048]{1,0:T(8,128)(2,1)S(1)}, bf16[96,2048]{1,0:T(8,128)(2,1)S(1)}, u32[]{:S(2)}, u32[]{:S(2)}) collective-permute-start(bf16[96,2048]{1,0:T(8,128)(2,1)S(1)} %get-tuple-element.38.own_in.refs_1_), channel_id=1, source_target_pairs={{0,4},{1,5},{2,6},{3,7},{4,0},{5,1},{6,2},{7,3},{8,12},{9,13},{10,... | collective-permute-start | bytes 1179656 | tf_op jit(solution)/shard_map/ppermute | solution.py:383
  24.0 18.6 %collective-permute-start.5 = (bf16[1024,384]{1,0:T(8,128)(2,1)S(1)}, bf16[1024,384]{1,0:T(8,128)(2,1)S(1)}, u32[]{:S(2)}, u32[]{:S(2)}) collective-permute-start(bf16[1024,384]{1,0:T(8,128)(2,1)S(1)} %hand_on.11.refs_0_.refs_2_), channel_id=1, source_target_pairs={{0,16},{16,0},{1,17},{17,1},{2,18},{18,2},{3,19},{19,3},{4,20},{20... | collective-permute-start | bytes 2359304 | tf_op jit(solution)/shard_map/ppermute | solution.py:396
  25.3 17.3 %collective-permute-start.10 = (bf16[96,2048]{1,0:T(8,128)(2,1)S(1)}, bf16[96,2048]{1,0:T(8,128)(2,1)S(1)}, u32[]{:S(2)}, u32[]{:S(2)}) collective-permute-start(bf16[96,2048]{1,0:T(8,128)(2,1)S(1)} %get-tuple-element.45), channel_id=1, source_target_pairs={{0,2},{1,3},{2,0},{3,1},{4,6},{5,7},{6,4},{7,5},{8,10},{9,11},{10,... | collective-permute-start | bytes 1179656 | tf_op jit(solution)/shard_map/ppermute | solution.py:383
  26.8 25.3 %collective-permute-start.14 = (bf16[192,2048]{1,0:T(8,128)(2,1)S(1)}, bf16[192,2048]{1,0:T(8,128)(2,1)S(1)}, u32[]{:S(2)}, u32[]{:S(2)}) collective-permute-start(bf16[192,2048]{1,0:T(8,128)(2,1)S(1)} %get-tuple-element.48), channel_id=1, source_target_pairs={{0,2},{1,3},{2,0},{3,1},{4,6},{5,7},{6,4},{7,5},{8,10},{9,11},{10,... | collective-permute-start | bytes 2359304 | tf_op jit(solution)/shard_map/ppermute | solution.py:383
  39.9 9.7 %collective-permute-start.9 = (bf16[96,2048]{1,0:T(8,128)(2,1)S(1)}, bf16[96,2048]{1,0:T(8,128)(2,1)S(1)}, u32[]{:S(2)}, u32[]{:S(2)}) collective-permute-start(bf16[96,2048]{1,0:T(8,128)(2,1)S(1)} %hand_on.13.own_in.refs_1_), channel_id=1, source_target_pairs={{0,4},{1,5},{2,6},{3,7},{4,0},{5,1},{6,2},{7,3},{8,12},{9,13},{10,... | collective-permute-start | bytes 1179656 | tf_op jit(solution)/shard_map/ppermute | solution.py:383
  42.6 11.8 %collective-permute-start.7 = (bf16[1024,384]{1,0:T(8,128)(2,1)S(1)}, bf16[1024,384]{1,0:T(8,128)(2,1)S(1)}, u32[]{:S(2)}, u32[]{:S(2)}) collective-permute-start(bf16[1024,384]{1,0:T(8,128)(2,1)S(1)} %get-tuple-element.41.refs_4_.refs_1_), channel_id=1, source_target_pairs={{0,1},{1,0},{2,3},{3,2},{4,5},{5,4},{6,7},{7,6},{8,9},{9,8},{10,11... | collective-permute-start | bytes 2359304 | tf_op jit(solution)/shard_map/ppermute | solution.py:383
  42.6 12.6 %collective-permute-start.11 = (bf16[96,2048]{1,0:T(8,128)(2,1)S(1)}, bf16[96,2048]{1,0:T(8,128)(2,1)S(1)}, u32[]{:S(2)}, u32[]{:S(2)}) collective-permute-start(bf16[96,2048]{1,0:T(8,128)(2,1)S(1)} %hand_on.19.refs_0_), channel_id=1, source_target_pairs={{0,16},{16,0},{1,17},{17,1},{2,18},{18,2},{3,19},{19,3},{4,20},{20... | collective-permute-start | bytes 1179656 | tf_op jit(solution)/shard_map/ppermute | solution.py:396
  44.1 10.3 %collective-permute-start.6 = (bf16[1024,384]{1,0:T(8,128)(2,1)S(1)}, bf16[1024,384]{1,0:T(8,128)(2,1)S(1)}, u32[]{:S(2)}, u32[]{:S(2)}) collective-permute-start(bf16[1024,384]{1,0:T(8,128)(2,1)S(1)} %get-tuple-element.40.refs_3_), channel_id=1, source_target_pairs={{0,1},{1,0},{2,3},{3,2},{4,5},{5,4},{6,7},{7,6},{8,9},{9,8},{10,11... | collective-permute-start | bytes 2359304 | tf_op jit(solution)/shard_map/ppermute | solution.py:383
  52.1 3.8 %collective-permute-start.15 = (bf16[192,2048]{1,0:T(8,128)(2,1)S(1)}, bf16[192,2048]{1,0:T(8,128)(2,1)S(1)}, u32[]{:S(2)}, u32[]{:S(2)}) collective-permute-start(bf16[192,2048]{1,0:T(8,128)(2,1)S(1)} %collective-permute-done.14.refs_9_), channel_id=1, source_target_pairs={{0,1},{1,0},{2,3},{3,2},{4,5},{5,4},{6,7},{7,6},{8,9},{9,8},{10,11... | collective-permute-start | bytes 2359304 | tf_op jit(solution)/shard_map/ppermute | solution.py:383
  52.1 1.4 %copy-start.4 = (bf16[2048,384]{1,0:T(8,128)(2,1)S(1)}, bf16[2048,384]{1,0:T(8,128)(2,1)}, u32[]{:S(2)}) copy-start(bf16[2048,384]{1,0:T(8,128)(2,1)} %copy-done.3) | copy-start | bytes 4718596
  54.4 3.4 %copy-start.2 = (bf16[384,2048]{1,0:T(8,128)(2,1)S(1)}, bf16[384,2048]{1,0:T(8,128)(2,1)}, u32[]{:S(2)}) copy-start(bf16[384,2048]{1,0:T(8,128)(2,1)} %copy-done) | copy-start | bytes 4718596
  55.3 1.9 %collective-permute-start.12 = (bf16[96,2048]{1,0:T(8,128)(2,1)S(1)}, bf16[96,2048]{1,0:T(8,128)(2,1)S(1)}, u32[]{:S(2)}, u32[]{:S(2)}) collective-permute-start(bf16[96,2048]{1,0:T(8,128)(2,1)S(1)} %get-tuple-element.46.refs_5_), channel_id=1, source_target_pairs={{0,1},{1,0},{2,3},{3,2},{4,5},{5,4},{6,7},{7,6},{8,9},{9,8},{10,11... | collective-permute-start | bytes 1179656 | tf_op jit(solution)/shard_map/ppermute | solution.py:383
  55.8 1.9 %collective-permute-start.13 = (bf16[96,2048]{1,0:T(8,128)(2,1)S(1)}, bf16[96,2048]{1,0:T(8,128)(2,1)S(1)}, u32[]{:S(2)}, u32[]{:S(2)}) collective-permute-start(bf16[96,2048]{1,0:T(8,128)(2,1)S(1)} %get-tuple-element.47.refs_6_), channel_id=1, source_target_pairs={{0,1},{1,0},{2,3},{3,2},{4,5},{5,4},{6,7},{7,6},{8,9},{9,8},{10,11... | collective-permute-start | bytes 1179656 | tf_op jit(solution)/shard_map/ppermute | solution.py:383
  60.6 11.5 %collective-permute-start.16 = (bf16[96,2048]{1,0:T(8,128)(2,1)S(1)}, bf16[96,2048]{1,0:T(8,128)(2,1)S(1)}, u32[]{:S(2)}, u32[]{:S(2)}) collective-permute-start(bf16[96,2048]{1,0:T(8,128)(2,1)S(1)} %get-tuple-element.51), channel_id=1, source_target_pairs={{0,4},{1,5},{2,6},{3,7},{4,0},{5,1},{6,2},{7,3},{8,12},{9,13},{10,... | collective-permute-start | bytes 1179656 | tf_op jit(solution)/shard_map/ppermute | solution.py:383
  72.2 20.1 %collective-permute-start.18 = (bf16[96,2048]{1,0:T(8,128)(2,1)S(1)}, bf16[96,2048]{1,0:T(8,128)(2,1)S(1)}, u32[]{:S(2)}, u32[]{:S(2)}) collective-permute-start(bf16[96,2048]{1,0:T(8,128)(2,1)S(1)} %get-tuple-element.54), channel_id=1, source_target_pairs={{0,8},{1,9},{2,10},{3,11},{4,12},{5,13},{6,14},{7,15},{8,0},{9,1},... | collective-permute-start | bytes 1179656 | tf_op jit(solution)/shard_map/ppermute | solution.py:387
  74.9 17.6 %collective-permute-start.17 = (bf16[96,2048]{1,0:T(8,128)(2,1)S(1)}, bf16[96,2048]{1,0:T(8,128)(2,1)S(1)}, u32[]{:S(2)}, u32[]{:S(2)}) collective-permute-start(bf16[96,2048]{1,0:T(8,128)(2,1)S(1)} %get-tuple-element.53), channel_id=1, source_target_pairs={{0,4},{1,5},{2,6},{3,7},{4,0},{5,1},{6,2},{7,3},{8,12},{9,13},{10,... | collective-permute-start | bytes 1179656 | tf_op jit(solution)/shard_map/ppermute | solution.py:383

commit v11 on v10

--- a/solution.py
+++ b/solution.py
@@ -112,9 +112,8 @@
     tokens, width = state_ref.shape
     local = kv_refs[0].shape[0] // 2
     scale = 1.0 / math.sqrt(HD)
-    squares = jnp.zeros((tokens, HD), jnp.float32)
-    for head in range(HEADS):
-        cols = slice(head * HD, (head + 1) * HD)
+    def one_head(head, squares):
+        cols = pl.ds(pl.multiple_of(head * HD, HD), HD)
         keys = jnp.concatenate([r[:local, cols] for r in kv_refs], axis=0)
         values = jnp.concatenate([r[local:, cols] for r in kv_refs], axis=0)
         scores = (
@@ -131,7 +130,11 @@
         mixed = jnp.dot(raised.astype(jnp.bfloat16), values, preferred_element_type=jnp.float32)
         hidden = state_ref[:, cols].astype(jnp.float32) + mixed / total
         hidden_ref[:, cols] = hidden
-        squares = squares + hidden * hidden
+        return squares + hidden * hidden
+
+    squares = lax.fori_loop(
+        0, HEADS, one_head, jnp.zeros((tokens, HD), jnp.float32), unroll=HEADS // 4
+    )
     mean_square = jnp.sum(squares, axis=1, keepdims=True) * (1.0 / width)
     inverse = lax.rsqrt(mean_square + EPS)
     rows = lax.broadcasted_iota(jnp.int32, (groups * cap, tokens), 0)
@@ -182,11 +185,13 @@
         1,
         4 * size * whole.shape[1],
         scratch=[pltpu.SemaphoreType.DMA],
+        out_specs=ANY,
         limit=PART_LIMIT,
     )(pipe, whole)
 
 
-def hold_kernel(pipes, pipe_ref, w_in, w_out, in_held, out_held, out_part, out_rest, sems):
+def hold_kernel(pipes, pipe_ref, w_in, w_out, *refs):
+    in_held, out_held, out_part, out_rest, sems = refs[-5:]
     size = out_part.shape[0]
     at = pl.multiple_of(pipe_ref[0] * size, size)
     copies = [
@@ -206,7 +211,7 @@
         copy.wait()
 
 
-def hold(pipe, w_in, w_out, pipes):
+def hold(pipe, w_in, w_out, pipes, after):
     units, width = w_out.shape
     size = units // 2 // pipes // 16 * 16
     return call(
@@ -217,12 +222,12 @@
             struct((size, width)),
             struct((units - pipes * size, width)),
         ],
-        [SMEM, ANY, ANY],
+        [SMEM, ANY, ANY] + [ANY] * len(after),
         "hold_weights",
         1,
         8 * units * width,
         scratch=[pltpu.SemaphoreType.DMA((4,))],
-    )(pipe, w_in, w_out)
+    )(pipe, w_in, w_out, *after)
 
 
 def up_kernel(own_in, z_in, w_own, w_pair, out_ref):
@@ -296,13 +301,17 @@
     held[units + pipes * size :] = pair_rest[...]
     activation = jnp.concatenate([act_ref[...], act_y_ref[...]], axis=1)
     step = 512
-    for at in range(0, width, step):
-        cols = slice(at, at + step)
+
+    def block(i, carry):
+        cols = pl.ds(pl.multiple_of(i * step, step), step)
         weights = jnp.concatenate([w_own[:, cols], w_pair[:, cols], held[:, cols]], axis=0)
         part = jnp.dot(activation, weights, preferred_element_type=jnp.float32)
         part = part.astype(jnp.bfloat16)
         own_ref[:, cols] = part[:rows]
         z_ref[:, cols] = part[rows:]
+        return carry
+
+    lax.fori_loop(0, width // step, block, 0)
 
 
 def down(pipe, acts, w_out, y_parts, pair_parts, rests):
@@ -402,7 +411,6 @@
     w_in_pair, w_out_pair = across(w_in, 1), across(w_out, 1)
     pipe = pipe.reshape(1)
     in_part = cut_part(pipe, w_in, width // pipes)
-    w_in_held, w_out_held, out_part, out_rest = hold(pipe, w_in, w_out, pipes)
     in_y = across(in_part, 2)
 
     group = (lax.axis_index("expert") // WSPLIT).astype(jnp.int32).reshape(1)
@@ -419,12 +427,13 @@
     )
     flat, gates = staged[4:]
     hidden, near, *packed = attend(
-        *staged[:4], kv_pieces, groups, cap, after=[w_in_pair, w_out_pair, w_out_held]
+        *staged[:4], kv_pieces, groups, cap, after=[w_in_pair, w_out_pair]
     )
     far = [groups_on(block, count) for count, block in enumerate(packed, 1)]
     far = jnp.concatenate(far, axis=0) if len(far) > 1 else far[0]
 
-    (in_y,) = after_all([in_y], [near])
+    w_in_held, w_out_held, out_part, out_rest = hold(pipe, w_in, w_out, pipes, [near])
+    (in_y,) = after_all([in_y], [out_part])
     out_part, out_rest = after_all([out_part, out_rest], [in_y])
     out_y = across(out_part, 2)
     rest_y = across(out_rest, 2)

time: 94.1 us -> 116 us (1.23)
  Pallas kernels: 15.4 us -> 40.2 us
  local copies, waits for them, and re-layouts: 10.9 us -> 1.15 us
  waiting for transfers between devices: 44.8 us -> 51.8 us
    pallas_call x1, Pallas kernels: 2.06 us -> 24.9 us  [cut_part(): call(part_kernel, struct((size, whole.shape[1])), [SMEM, ANY], 'weight_pa...]
    unnamed x32 -> x18, local copies, waits for them, and re-layouts: 10.8 us -> 1.07 us
    ppermute x1, waiting for transfers between devices: 0.01 us -> 5.32 us  [body(): kv_pieces.append(lax.ppermute(kv, 'pipe', perm))]
    ppermute x2, waiting for transfers between devices: 1.22 us -> 5.12 us  [along(): return [value] + [lax.ppermute(value, 'pipe', perm) for perm in perms]]
    ppermute x2, waiting for transfers between devices: 28.2 us -> 24.6 us  [groups_on(): lax.ppermute(value, 'expert', [(i, (i + shift) % devices) for i in range(...]
    pallas_call x2, Pallas kernels: 5.79 us -> 7.18 us  [down(): call(functools.partial(down_kernel, pipes), [struct((rows, width))] * 2,...]
    ppermute x14, waiting for transfers between devices: 15.4 us -> 16.7 us  [across(): return lax.ppermute(value, 'expert', [(i, i ^ bit) for i in range(devices)])]
  transfers between devices with their start and end apart: 19 -> 19, of which waited for: 10 -> 13; matrix products, arithmetic and copies ran while one was open for 0% -> 0% of each run, Pallas kernels for 12% -> 31%
where the time goes in v11:
time: 116 us
  waiting for transfers between devices  51.8 us (45%)
  Pallas kernels  40.2 us (35%)
  starting transfers between devices  22.5 us (19%)
    pallas_call x1, Pallas kernels, cut_part(): call(part_kernel, struct((size, whole.shape[1])), [SMEM, ANY], 'weight_pa...  24.9 us
    ppermute x2, waiting for transfers between devices, groups_on(): lax.ppermute(value, 'expert', [(i, (i + shift) % devices) for i in range(...  24.6 us
    ppermute x14, waiting for transfers between devices, across(): return lax.ppermute(value, 'expert', [(i, i ^ bit) for i in range(devices)])  16.7 us
    ppermute x14, starting transfers between devices, across(): return lax.ppermute(value, 'expert', [(i, i ^ bit) for i in range(devices)])  12.5 us
    pallas_call x2, Pallas kernels, down(): call(functools.partial(down_kernel, pipes), [struct((rows, width))] * 2,...  7.18 us
    ppermute x2, starting transfers between devices, groups_on(): lax.ppermute(value, 'expert', [(i, (i + shift) % devices) for i in range(...  5.32 us
    ppermute x1, waiting for transfers between devices, body(): kv_pieces.append(lax.ppermute(kv, 'pipe', perm))  5.32 us
    ppermute x2, waiting for transfers between devices, along(): return [value] + [lax.ppermute(value, 'pipe', perm) for perm in perms]  5.12 us
  transfers between devices with their start and end apart: 19, of which 13 were waited for; matrix products, arithmetic and copies ran while one was open for 0% of the time, Pallas kernels for 31%

profile of v11, /device:TPU:0, one launch (start us, length us, event | category | flops | bytes accessed | tf_op | source)
XLA Modules:
  0.0 115.8 jit_solution(17704420336195434190)
XLA Ops:
  0.0 0.5 collective-permute-start.2
  0.6 0.1 collective-permute-start.1
  0.6 24.9 %weight_part.1 = bf16[1024,384]{1,0:T(8,128)(2,1)} custom-call(s32[1]{0:T(128)} %bitcast.10.pipe_ref.refs_0_, bf16[2048,384]{1,0:T(8,128)(2,1)} %whole.1), custom_call_target="tpu_custom_call" | custom-call | flops 1 | bytes 1572864 | tf_op jit(solution)/shard_map/weight_part/pallas_call | solution.py:180
  25.6 3.0 %collective-permute-start.4 = (bf16[1024,384]{1,0:T(8,128)(2,1)}, bf16[1024,384]{1,0:T(8,128)(2,1)S(1)}, u32[]{:S(2)}, u32[]{:S(2)}) collective-permute-start(bf16[1024,384]{1,0:T(8,128)(2,1)} %weight_part.1), channel_id=1, source_target_pairs={{0,2},{1,3},{2,0},{3,1},{4,6},{5,7},{6,4},{7,5},{8,10},{9,11},{10,... | collective-permute-start | bytes 2359304 | tf_op jit(solution)/shard_map/ppermute | solution.py:392
  28.6 0.1 copy.25
  28.7 1.6 %collective-permute-start = (bf16[64,2048]{1,0:T(8,128)(2,1)S(1)}, bf16[64,2048]{1,0:T(8,128)(2,1)S(1)}, u32[]{:S(2)}, u32[]{:S(2)}) collective-permute-start(bf16[64,2048]{1,0:T(8,128)(2,1)S(1)} %bitcast.13), channel_id=1, source_target_pairs={{0,16},{16,0},{1,17},{17,1},{2,18},{18,2},{3,19},{19,3},{4,20},{20... | collective-permute-start | bytes 786440 | tf_op jit(solution)/shard_map/ppermute | solution.py:402
  30.3 0.0 copy-start.3
  30.3 1.0 copy-done.3
  31.3 0.1 stage.1
  31.4 5.3 %collective-permute-done.refs_5_ = bf16[64,2048]{1,0:T(8,128)(2,1)S(1)} collective-permute-done((bf16[64,2048]{1,0:T(8,128)(2,1)S(1)}, bf16[64,2048]{1,0:T(8,128)(2,1)S(1)}, u32[]{:S(2)}, u32[]{:S(2)}) %collective-permute-start) | collective-permute-done | bytes 262176 | tf_op jit(solution)/shard_map/ppermute | solution.py:402
  36.8 0.0 collective-permute-done.1.refs_6_.w_pair
  36.8 0.0 copy-start.1
  36.8 2.9 %attend.1 = (f32[128,2048]{1,0:T(8,128)S(1)}, bf16[96,2048]{1,0:T(8,128)(2,1)S(1)}, bf16[96,2048]{1,0:T(8,128)(2,1)S(1)}) custom-call(bf16[128,2048]{1,0:T(8,128)(2,1)S(1)} %get-tuple-element.30.refs_0_, bf16[128,2048]{1,0:T(8,128)(2,1)S(1)} %get-tuple-element.31.refs_1_, f32[1,2048]{1,0:T(1,128)S(1)} %get-tuple-element.32.refs_2_, ...), custom_call_target="tpu_custom_call" | custom-call | flops 134217728 | bytes 3145728 | tf_op jit(solution)/shard_map/attend/pallas_call | solution.py:155
  39.7 2.7 %collective-permute-start.8 = (bf16[96,2048]{1,0:T(8,128)(2,1)S(1)}, bf16[96,2048]{1,0:T(8,128)(2,1)S(1)}, u32[]{:S(2)}, u32[]{:S(2)}) collective-permute-start(bf16[96,2048]{1,0:T(8,128)(2,1)S(1)} %get-tuple-element.42), channel_id=1, source_target_pairs={{0,8},{1,9},{2,10},{3,11},{4,12},{5,13},{6,14},{7,15},{8,0},{9,1},... | collective-permute-start | bytes 1179656 | tf_op jit(solution)/shard_map/ppermute | solution.py:396
  42.3 1.6 %collective-permute-start.3 = (bf16[96,2048]{1,0:T(8,128)(2,1)S(1)}, bf16[96,2048]{1,0:T(8,128)(2,1)S(1)}, u32[]{:S(2)}, u32[]{:S(2)}) collective-permute-start(bf16[96,2048]{1,0:T(8,128)(2,1)S(1)} %get-tuple-element.37.refs_0_.own_in.refs_1_), channel_id=1, source_target_pairs={{0,4},{1,5},{2,6},{3,7},{4,0},{5,1},{6,2},{7,3},{8,12},{9,13},{10,... | collective-permute-start | bytes 1179656 | tf_op jit(solution)/shard_map/ppermute | solution.py:392
  43.9 0.5 hold_weights.1
  44.4 2.2 %collective-permute-done.4.refs_0_ = bf16[1024,384]{1,0:T(8,128)(2,1)S(1)} collective-permute-done((bf16[1024,384]{1,0:T(8,128)(2,1)}, bf16[1024,384]{1,0:T(8,128)(2,1)S(1)}, u32[]{:S(2)}, u32[]{:S(2)}) %collective-permute-start.4) | collective-permute-done | bytes 786464 | tf_op jit(solution)/shard_map/ppermute | solution.py:392
  46.6 1.7 %collective-permute-start.5 = (bf16[1024,384]{1,0:T(8,128)(2,1)S(1)}, bf16[1024,384]{1,0:T(8,128)(2,1)S(1)}, u32[]{:S(2)}, u32[]{:S(2)}) collective-permute-start(bf16[1024,384]{1,0:T(8,128)(2,1)S(1)} %hand_on.11.refs_0_.refs_2_), channel_id=1, source_target_pairs={{0,16},{16,0},{1,17},{17,1},{2,18},{18,2},{3,19},{19,3},{4,20},{20... | collective-permute-start | bytes 2359304 | tf_op jit(solution)/shard_map/ppermute | solution.py:405
  48.3 1.5 %collective-permute-start.10 = (bf16[96,2048]{1,0:T(8,128)(2,1)S(1)}, bf16[96,2048]{1,0:T(8,128)(2,1)S(1)}, u32[]{:S(2)}, u32[]{:S(2)}) collective-permute-start(bf16[96,2048]{1,0:T(8,128)(2,1)S(1)} %get-tuple-element.45), channel_id=1, source_target_pairs={{0,2},{1,3},{2,0},{3,1},{4,6},{5,7},{6,4},{7,5},{8,10},{9,11},{10,... | collective-permute-start | bytes 1179656 | tf_op jit(solution)/shard_map/ppermute | solution.py:392
  49.8 0.5 collective-permute-start.14
  50.3 8.8 %collective-permute-done.8.refs_0_ = bf16[96,2048]{1,0:T(8,128)(2,1)S(1)} collective-permute-done((bf16[96,2048]{1,0:T(8,128)(2,1)S(1)}, bf16[96,2048]{1,0:T(8,128)(2,1)S(1)}, u32[]{:S(2)}, u32[]{:S(2)}) %collective-permute-start.8) | collective-permute-done | bytes 393248 | tf_op jit(solution)/shard_map/ppermute | solution.py:396
  59.1 0.2 collective-permute-done.3.z_in.refs_1_.refs_2_
  59.3 1.4 %collective-permute-start.9 = (bf16[96,2048]{1,0:T(8,128)(2,1)S(1)}, bf16[96,2048]{1,0:T(8,128)(2,1)S(1)}, u32[]{:S(2)}, u32[]{:S(2)}) collective-permute-start(bf16[96,2048]{1,0:T(8,128)(2,1)S(1)} %hand_on.13.own_in.refs_1_), channel_id=1, source_target_pairs={{0,4},{1,5},{2,6},{3,7},{4,0},{5,1},{6,2},{7,3},{8,12},{9,13},{10,... | collective-permute-start | bytes 1179656 | tf_op jit(solution)/shard_map/ppermute | solution.py:392
  60.8 4.8 %collective-permute-done.5.refs_1_ = bf16[1024,384]{1,0:T(8,128)(2,1)S(1)} collective-permute-done((bf16[1024,384]{1,0:T(8,128)(2,1)S(1)}, bf16[1024,384]{1,0:T(8,128)(2,1)S(1)}, u32[]{:S(2)}, u32[]{:S(2)}) %collective-permute-start.5) | collective-permute-done | bytes 786464 | tf_op jit(solution)/shard_map/ppermute | solution.py:405
  65.6 0.0 collective-permute-start.7
  65.6 1.5 %collective-permute-start.11 = (bf16[96,2048]{1,0:T(8,128)(2,1)S(1)}, bf16[96,2048]{1,0:T(8,128)(2,1)S(1)}, u32[]{:S(2)}, u32[]{:S(2)}) collective-permute-start(bf16[96,2048]{1,0:T(8,128)(2,1)S(1)} %hand_on.19.refs_0_), channel_id=1, source_target_pairs={{0,16},{16,0},{1,17},{17,1},{2,18},{18,2},{3,19},{19,3},{4,20},{20... | collective-permute-start | bytes 1179656 | tf_op jit(solution)/shard_map/ppermute | solution.py:405
  67.1 0.2 collective-permute-start.6
  67.2 1.8 %collective-permute-done.9.refs_0_ = bf16[96,2048]{1,0:T(8,128)(2,1)S(1)} collective-permute-done((bf16[96,2048]{1,0:T(8,128)(2,1)S(1)}, bf16[96,2048]{1,0:T(8,128)(2,1)S(1)}, u32[]{:S(2)}, u32[]{:S(2)}) %collective-permute-start.9) | collective-permute-done | bytes 393248 | tf_op jit(solution)/shard_map/ppermute | solution.py:392
  69.0 6.1 %collective-permute-done.14.refs_9_ = bf16[192,2048]{1,0:T(8,128)(2,1)S(1)} collective-permute-done((bf16[192,2048]{1,0:T(8,128)(2,1)S(1)}, bf16[192,2048]{1,0:T(8,128)(2,1)S(1)}, u32[]{:S(2)}, u32[]{:S(2)}) %collective-permute-start.14) | collective-permute-done | bytes 786464 | tf_op jit(solution)/shard_map/ppermute | solution.py:392
  75.1 0.8 expert_up.3.refs_2_.refs_1_
  76.0 0.9 expert_up_y.2.refs_3_.refs_2_
  76.8 0.3 collective-permute-done.11.refs_1_
  77.1 0.3 collective-permute-start.12
  77.4 0.2 collective-permute-start.13
  77.6 1.2 %collective-permute-done.12.refs_7_ = bf16[96,2048]{1,0:T(8,128)(2,1)S(1)} collective-permute-done((bf16[96,2048]{1,0:T(8,128)(2,1)S(1)}, bf16[96,2048]{1,0:T(8,128)(2,1)S(1)}, u32[]{:S(2)}, u32[]{:S(2)}) %collective-permute-start.12) | collective-permute-done | bytes 393248 | tf_op jit(solution)/shard_map/ppermute | solution.py:392
  78.9 0.6 collective-permute-done.13.refs_8_
  79.4 3.6 %expert_down.2 = (bf16[96,2048]{1,0:T(8,128)(2,1)S(1)}, bf16[96,2048]{1,0:T(8,128)(2,1)S(1)}) custom-call(s32[1]{0:T(128)} %bitcast.10.pipe_ref.refs_0_, bf16[192,768]{1,0:T(8,128)(2,1)S(1)} %expert_up.3.refs_2_.refs_1_, bf16[192,768]{1,0:T(8,128)(2,1)S(1)} %expert_up_y.2.refs_3_.refs_2_, bf16[384,2048]{1,0:T(8,128)(2,1)S(1)} %get-tuple-element.43.refs_3_, ...), custom_call_target="tpu_custom_call" | custom-call | flops 1207959552 | bytes 6291456 | tf_op jit(solution)/shard_map/expert_down/pallas_call | solution.py:321
  83.0 1.6 %collective-permute-start.16 = (bf16[96,2048]{1,0:T(8,128)(2,1)S(1)}, bf16[96,2048]{1,0:T(8,128)(2,1)S(1)}, u32[]{:S(2)}, u32[]{:S(2)}) collective-permute-start(bf16[96,2048]{1,0:T(8,128)(2,1)S(1)} %get-tuple-element.51), channel_id=1, source_target_pairs={{0,4},{1,5},{2,6},{3,7},{4,0},{5,1},{6,2},{7,3},{8,12},{9,13},{10,... | collective-permute-start | bytes 1179656 | tf_op jit(solution)/shard_map/ppermute | solution.py:392
  84.6 0.8 expert_up.2.refs_1_
  85.4 0.8 expert_up_y.3.refs_2_
  86.3 3.6 %expert_down.3 = (bf16[96,2048]{1,0:T(8,128)(2,1)S(1)}, bf16[96,2048]{1,0:T(8,128)(2,1)S(1)}) custom-call(s32[1]{0:T(128)} %bitcast.10.pipe_ref.refs_0_, bf16[192,768]{1,0:T(8,128)(2,1)S(1)} %expert_up.2.refs_1_, bf16[192,768]{1,0:T(8,128)(2,1)S(1)} %expert_up_y.3.refs_2_, bf16[384,2048]{1,0:T(8,128)(2,1)S(1)} %get-tuple-element.43.refs_3_, ...), custom_call_target="tpu_custom_call" | custom-call | flops 1207959552 | bytes 6291456 | tf_op jit(solution)/shard_map/expert_down/pallas_call | solution.py:321
  89.9 4.5 %collective-permute-done.16.z_ref = bf16[96,2048]{1,0:T(8,128)(2,1)S(1)} collective-permute-done((bf16[96,2048]{1,0:T(8,128)(2,1)S(1)}, bf16[96,2048]{1,0:T(8,128)(2,1)S(1)}, u32[]{:S(2)}, u32[]{:S(2)}) %collective-permute-start.16) | collective-permute-done | bytes 393248 | tf_op jit(solution)/shard_map/ppermute | solution.py:392
  94.4 0.1 far_total.1
  94.5 2.7 %collective-permute-start.18 = (bf16[96,2048]{1,0:T(8,128)(2,1)S(1)}, bf16[96,2048]{1,0:T(8,128)(2,1)S(1)}, u32[]{:S(2)}, u32[]{:S(2)}) collective-permute-start(bf16[96,2048]{1,0:T(8,128)(2,1)S(1)} %get-tuple-element.54), channel_id=1, source_target_pairs={{0,8},{1,9},{2,10},{3,11},{4,12},{5,13},{6,14},{7,15},{8,0},{9,1},... | collective-permute-start | bytes 1179656 | tf_op jit(solution)/shard_map/ppermute | solution.py:396
  97.2 1.6 %collective-permute-start.17 = (bf16[96,2048]{1,0:T(8,128)(2,1)S(1)}, bf16[96,2048]{1,0:T(8,128)(2,1)S(1)}, u32[]{:S(2)}, u32[]{:S(2)}) collective-permute-start(bf16[96,2048]{1,0:T(8,128)(2,1)S(1)} %get-tuple-element.53), channel_id=1, source_target_pairs={{0,4},{1,5},{2,6},{3,7},{4,0},{5,1},{6,2},{7,3},{8,12},{9,13},{10,... | collective-permute-start | bytes 1179656 | tf_op jit(solution)/shard_map/ppermute | solution.py:392
  98.7 15.8 %collective-permute-done.18.refs_0_ = bf16[96,2048]{1,0:T(8,128)(2,1)S(1)} collective-permute-done((bf16[96,2048]{1,0:T(8,128)(2,1)S(1)}, bf16[96,2048]{1,0:T(8,128)(2,1)S(1)}, u32[]{:S(2)}, u32[]{:S(2)}) %collective-permute-start.18) | collective-permute-done | bytes 393248 | tf_op jit(solution)/shard_map/ppermute | solution.py:396
  114.5 0.2 collective-permute-done.17.refs_4_
  114.7 1.2 finish.1
  (32 shorter events, 0.1 us)
Async XLA Ops:
  0.0 28.6 %copy-start.8 = (bf16[1,32,2,2048]{3,2,1,0:T(2,128)(2,1)S(1)}, bf16[1,32,2,2048]{3,2,1,0:T(2,128)(2,1)}, u32[]{:S(2)}) copy-start(bf16[1,32,2,2048]{3,2,1,0:T(2,128)(2,1)} %param.11) | copy-start | bytes 786436
  0.0 30.2 %copy-start.7 = (f32[1,1,128]{2,1,0:T(1,128)S(1)}, f32[1,1,128]{2,1,0:T(1,128)}, u32[]{:S(2)}) copy-start(f32[1,1,128]{2,1,0:T(1,128)} %param.17) | copy-start | bytes 1540
  0.0 30.2 %copy-start.6 = (s32[1,1,128]{2,1,0:T(1,128)S(1)}, s32[1,1,128]{2,1,0:T(1,128)}, u32[]{:S(2)}) copy-start(s32[1,1,128]{2,1,0:T(1,128)} %param.16) | copy-start | bytes 1540
  0.0 30.2 %copy-start.5 = (s32[1,1,128]{2,1,0:T(1,128)S(1)}, s32[1,1,128]{2,1,0:T(1,128)}, u32[]{:S(2)}) copy-start(s32[1,1,128]{2,1,0:T(1,128)} %param.15) | copy-start | bytes 1540
  0.0 30.2 %copy-start.4 = (f32[2048]{0:T(1024)S(1)}, f32[2048]{0:T(1024)}, u32[]{:S(2)}) copy-start(f32[2048]{0:T(1024)} %param.12) | copy-start | bytes 24580
  0.0 30.2 %copy-start.2 = (bf16[1,1,128,2048]{3,2,1,0:T(8,128)(2,1)S(1)}, bf16[1,1,128,2048]{3,2,1,0:T(8,128)(2,1)}, u32[]{:S(2)}) copy-start(bf16[1,1,128,2048]{3,2,1,0:T(8,128)(2,1)} %param.9) | copy-start | bytes 1572868
  0.0 36.7 %collective-permute-start.2 = (bf16[384,2048]{1,0:T(8,128)(2,1)}, bf16[384,2048]{1,0:T(8,128)(2,1)}, u32[]{:S(2)}, u32[]{:S(2)}) collective-permute-start(bf16[384,2048]{1,0:T(8,128)(2,1)} %w_out.1), channel_id=1, source_target_pairs={{0,1},{1,0},{2,3},{3,2},{4,5},{5,4},{6,7},{7,6},{8,9},{9,8},{10,11... | collective-permute-start | bytes 4718600 | tf_op jit(solution)/shard_map/ppermute | solution.py:392
  0.6 36.2 %collective-permute-start.1 = (bf16[2048,384]{1,0:T(8,128)(2,1)}, bf16[2048,384]{1,0:T(8,128)(2,1)S(1)}, u32[]{:S(2)}, u32[]{:S(2)}) collective-permute-start(bf16[2048,384]{1,0:T(8,128)(2,1)} %whole.1), channel_id=1, source_target_pairs={{0,1},{1,0},{2,3},{3,2},{4,5},{5,4},{6,7},{7,6},{8,9},{9,8},{10,11... | collective-permute-start | bytes 4718600 | tf_op jit(solution)/shard_map/ppermute | solution.py:392
  25.6 21.0 %collective-permute-start.4 = (bf16[1024,384]{1,0:T(8,128)(2,1)}, bf16[1024,384]{1,0:T(8,128)(2,1)S(1)}, u32[]{:S(2)}, u32[]{:S(2)}) collective-permute-start(bf16[1024,384]{1,0:T(8,128)(2,1)} %weight_part.1), channel_id=1, source_target_pairs={{0,2},{1,3},{2,0},{3,1},{4,6},{5,7},{6,4},{7,5},{8,10},{9,11},{10,... | collective-permute-start | bytes 2359304 | tf_op jit(solution)/shard_map/ppermute | solution.py:392
  28.7 8.1 %collective-permute-start = (bf16[64,2048]{1,0:T(8,128)(2,1)S(1)}, bf16[64,2048]{1,0:T(8,128)(2,1)S(1)}, u32[]{:S(2)}, u32[]{:S(2)}) collective-permute-start(bf16[64,2048]{1,0:T(8,128)(2,1)S(1)} %bitcast.13), channel_id=1, source_target_pairs={{0,16},{16,0},{1,17},{17,1},{2,18},{18,2},{3,19},{19,3},{4,20},{20... | collective-permute-start | bytes 786440 | tf_op jit(solution)/shard_map/ppermute | solution.py:402
  30.3 1.0 copy-start.3
  36.8 7.2 %copy-start = (bf16[2048,384]{1,0:T(8,128)(2,1)S(1)}, bf16[2048,384]{1,0:T(8,128)(2,1)}, u32[]{:S(2)}) copy-start(bf16[2048,384]{1,0:T(8,128)(2,1)} %whole.1) | copy-start | bytes 4718596
  36.8 7.2 %copy-start.1 = (bf16[384,2048]{1,0:T(8,128)(2,1)S(1)}, bf16[384,2048]{1,0:T(8,128)(2,1)}, u32[]{:S(2)}) copy-start(bf16[384,2048]{1,0:T(8,128)(2,1)} %w_out.1) | copy-start | bytes 4718596
  39.7 19.4 %collective-permute-start.8 = (bf16[96,2048]{1,0:T(8,128)(2,1)S(1)}, bf16[96,2048]{1,0:T(8,128)(2,1)S(1)}, u32[]{:S(2)}, u32[]{:S(2)}) collective-permute-start(bf16[96,2048]{1,0:T(8,128)(2,1)S(1)} %get-tuple-element.42), channel_id=1, source_target_pairs={{0,8},{1,9},{2,10},{3,11},{4,12},{5,13},{6,14},{7,15},{8,0},{9,1},... | collective-permute-start | bytes 1179656 | tf_op jit(solution)/shard_map/ppermute | solution.py:396
  42.3 17.0 %collective-permute-start.3 = (bf16[96,2048]{1,0:T(8,128)(2,1)S(1)}, bf16[96,2048]{1,0:T(8,128)(2,1)S(1)}, u32[]{:S(2)}, u32[]{:S(2)}) collective-permute-start(bf16[96,2048]{1,0:T(8,128)(2,1)S(1)} %get-tuple-element.37.refs_0_.own_in.refs_1_), channel_id=1, source_target_pairs={{0,4},{1,5},{2,6},{3,7},{4,0},{5,1},{6,2},{7,3},{8,12},{9,13},{10,... | collective-permute-start | bytes 1179656 | tf_op jit(solution)/shard_map/ppermute | solution.py:392
  46.6 19.0 %collective-permute-start.5 = (bf16[1024,384]{1,0:T(8,128)(2,1)S(1)}, bf16[1024,384]{1,0:T(8,128)(2,1)S(1)}, u32[]{:S(2)}, u32[]{:S(2)}) collective-permute-start(bf16[1024,384]{1,0:T(8,128)(2,1)S(1)} %hand_on.11.refs_0_.refs_2_), channel_id=1, source_target_pairs={{0,16},{16,0},{1,17},{17,1},{2,18},{18,2},{3,19},{19,3},{4,20},{20... | collective-permute-start | bytes 2359304 | tf_op jit(solution)/shard_map/ppermute | solution.py:405
  48.3 17.3 %collective-permute-start.10 = (bf16[96,2048]{1,0:T(8,128)(2,1)S(1)}, bf16[96,2048]{1,0:T(8,128)(2,1)S(1)}, u32[]{:S(2)}, u32[]{:S(2)}) collective-permute-start(bf16[96,2048]{1,0:T(8,128)(2,1)S(1)} %get-tuple-element.45), channel_id=1, source_target_pairs={{0,2},{1,3},{2,0},{3,1},{4,6},{5,7},{6,4},{7,5},{8,10},{9,11},{10,... | collective-permute-start | bytes 1179656 | tf_op jit(solution)/shard_map/ppermute | solution.py:392
  49.8 25.3 %collective-permute-start.14 = (bf16[192,2048]{1,0:T(8,128)(2,1)S(1)}, bf16[192,2048]{1,0:T(8,128)(2,1)S(1)}, u32[]{:S(2)}, u32[]{:S(2)}) collective-permute-start(bf16[192,2048]{1,0:T(8,128)(2,1)S(1)} %get-tuple-element.48), channel_id=1, source_target_pairs={{0,2},{1,3},{2,0},{3,1},{4,6},{5,7},{6,4},{7,5},{8,10},{9,11},{10,... | collective-permute-start | bytes 2359304 | tf_op jit(solution)/shard_map/ppermute | solution.py:392
  59.3 9.7 %collective-permute-start.9 = (bf16[96,2048]{1,0:T(8,128)(2,1)S(1)}, bf16[96,2048]{1,0:T(8,128)(2,1)S(1)}, u32[]{:S(2)}, u32[]{:S(2)}) collective-permute-start(bf16[96,2048]{1,0:T(8,128)(2,1)S(1)} %hand_on.13.own_in.refs_1_), channel_id=1, source_target_pairs={{0,4},{1,5},{2,6},{3,7},{4,0},{5,1},{6,2},{7,3},{8,12},{9,13},{10,... | collective-permute-start | bytes 1179656 | tf_op jit(solution)/shard_map/ppermute | solution.py:392
  65.6 10.4 %collective-permute-start.7 = (bf16[1024,384]{1,0:T(8,128)(2,1)S(1)}, bf16[1024,384]{1,0:T(8,128)(2,1)S(1)}, u32[]{:S(2)}, u32[]{:S(2)}) collective-permute-start(bf16[1024,384]{1,0:T(8,128)(2,1)S(1)} %get-tuple-element.41.refs_4_.refs_1_), channel_id=1, source_target_pairs={{0,1},{1,0},{2,3},{3,2},{4,5},{5,4},{6,7},{7,6},{8,9},{9,8},{10,11... | collective-permute-start | bytes 2359304 | tf_op jit(solution)/shard_map/ppermute | solution.py:392
  65.6 11.5 %collective-permute-start.11 = (bf16[96,2048]{1,0:T(8,128)(2,1)S(1)}, bf16[96,2048]{1,0:T(8,128)(2,1)S(1)}, u32[]{:S(2)}, u32[]{:S(2)}) collective-permute-start(bf16[96,2048]{1,0:T(8,128)(2,1)S(1)} %hand_on.19.refs_0_), channel_id=1, source_target_pairs={{0,16},{16,0},{1,17},{17,1},{2,18},{18,2},{3,19},{19,3},{4,20},{20... | collective-permute-start | bytes 1179656 | tf_op jit(solution)/shard_map/ppermute | solution.py:405
  67.1 8.9 %collective-permute-start.6 = (bf16[1024,384]{1,0:T(8,128)(2,1)S(1)}, bf16[1024,384]{1,0:T(8,128)(2,1)S(1)}, u32[]{:S(2)}, u32[]{:S(2)}) collective-permute-start(bf16[1024,384]{1,0:T(8,128)(2,1)S(1)} %get-tuple-element.40.refs_3_), channel_id=1, source_target_pairs={{0,1},{1,0},{2,3},{3,2},{4,5},{5,4},{6,7},{7,6},{8,9},{9,8},{10,11... | collective-permute-start | bytes 2359304 | tf_op jit(solution)/shard_map/ppermute | solution.py:392
  75.1 2.5 %collective-permute-start.15 = (bf16[192,2048]{1,0:T(8,128)(2,1)S(1)}, bf16[192,2048]{1,0:T(8,128)(2,1)S(1)}, u32[]{:S(2)}, u32[]{:S(2)}) collective-permute-start(bf16[192,2048]{1,0:T(8,128)(2,1)S(1)} %collective-permute-done.14.refs_9_), channel_id=1, source_target_pairs={{0,1},{1,0},{2,3},{3,2},{4,5},{5,4},{6,7},{7,6},{8,9},{9,8},{10,11... | collective-permute-start | bytes 2359304 | tf_op jit(solution)/shard_map/ppermute | solution.py:392
  77.1 1.7 %collective-permute-start.12 = (bf16[96,2048]{1,0:T(8,128)(2,1)S(1)}, bf16[96,2048]{1,0:T(8,128)(2,1)S(1)}, u32[]{:S(2)}, u32[]{:S(2)}) collective-permute-start(bf16[96,2048]{1,0:T(8,128)(2,1)S(1)} %get-tuple-element.46.refs_5_), channel_id=1, source_target_pairs={{0,1},{1,0},{2,3},{3,2},{4,5},{5,4},{6,7},{7,6},{8,9},{9,8},{10,11... | collective-permute-start | bytes 1179656 | tf_op jit(solution)/shard_map/ppermute | solution.py:392
  77.4 2.0 %collective-permute-start.13 = (bf16[96,2048]{1,0:T(8,128)(2,1)S(1)}, bf16[96,2048]{1,0:T(8,128)(2,1)S(1)}, u32[]{:S(2)}, u32[]{:S(2)}) collective-permute-start(bf16[96,2048]{1,0:T(8,128)(2,1)S(1)} %get-tuple-element.47.refs_6_), channel_id=1, source_target_pairs={{0,1},{1,0},{2,3},{3,2},{4,5},{5,4},{6,7},{7,6},{8,9},{9,8},{10,11... | collective-permute-start | bytes 1179656 | tf_op jit(solution)/shard_map/ppermute | solution.py:392
  83.0 11.4 %collective-permute-start.16 = (bf16[96,2048]{1,0:T(8,128)(2,1)S(1)}, bf16[96,2048]{1,0:T(8,128)(2,1)S(1)}, u32[]{:S(2)}, u32[]{:S(2)}) collective-permute-start(bf16[96,2048]{1,0:T(8,128)(2,1)S(1)} %get-tuple-element.51), channel_id=1, source_target_pairs={{0,4},{1,5},{2,6},{3,7},{4,0},{5,1},{6,2},{7,3},{8,12},{9,13},{10,... | collective-permute-start | bytes 1179656 | tf_op jit(solution)/shard_map/ppermute | solution.py:392
  94.5 20.0 %collective-permute-start.18 = (bf16[96,2048]{1,0:T(8,128)(2,1)S(1)}, bf16[96,2048]{1,0:T(8,128)(2,1)S(1)}, u32[]{:S(2)}, u32[]{:S(2)}) collective-permute-start(bf16[96,2048]{1,0:T(8,128)(2,1)S(1)} %get-tuple-element.54), channel_id=1, source_target_pairs={{0,8},{1,9},{2,10},{3,11},{4,12},{5,13},{6,14},{7,15},{8,0},{9,1},... | collective-permute-start | bytes 1179656 | tf_op jit(solution)/shard_map/ppermute | solution.py:396
  97.2 17.5 %collective-permute-start.17 = (bf16[96,2048]{1,0:T(8,128)(2,1)S(1)}, bf16[96,2048]{1,0:T(8,128)(2,1)S(1)}, u32[]{:S(2)}, u32[]{:S(2)}) collective-permute-start(bf16[96,2048]{1,0:T(8,128)(2,1)S(1)} %get-tuple-element.53), channel_id=1, source_target_pairs={{0,4},{1,5},{2,6},{3,7},{4,0},{5,1},{6,2},{7,3},{8,12},{9,13},{10,... | collective-permute-start | bytes 1179656 | tf_op jit(solution)/shard_map/ppermute | solution.py:392

commit v12 on v10

--- a/solution.py
+++ b/solution.py
@@ -165,17 +165,17 @@
     return pl.multiple_of(at * size, size)
 
 
-def part_kernel(pipe_ref, whole, part, sem):
+def part_kernel(stride, first, pipe_ref, whole, part, sem):
     size = part.shape[0]
-    at = pl.multiple_of(pipe_ref[0] * size, size)
+    at = pl.multiple_of(pipe_ref[0] * stride + first, size)
     copy = pltpu.make_async_copy(whole.at[pl.ds(at, size)], part, sem)
     copy.start()
     copy.wait()
 
 
-def cut_part(pipe, whole, size):
-    return call(
-        part_kernel,
+def cut_part(pipe, whole, stride, first, size):
+    return call(
+        functools.partial(part_kernel, stride, first),
         struct((size, whole.shape[1])),
         [SMEM, ANY],
         "weight_part",
@@ -186,7 +186,8 @@
     )(pipe, whole)
 
 
-def hold_kernel(pipes, pipe_ref, w_in, w_out, in_held, out_held, out_part, out_rest, sems):
+def hold_kernel(pipes, pipe_ref, w_in, w_out, *refs):
+    in_held, out_held, out_part, out_rest, sems = refs[-5:]
     size = out_part.shape[0]
     at = pl.multiple_of(pipe_ref[0] * size, size)
     copies = [
@@ -206,9 +207,9 @@
         copy.wait()
 
 
-def hold(pipe, w_in, w_out, pipes):
+def hold(pipe, w_in, w_out, pipes, after):
     units, width = w_out.shape
-    size = units // 2 // pipes // 16 * 16
+    size = units * 7 // 12 // pipes // 16 * 16
     return call(
         functools.partial(hold_kernel, pipes),
         [
@@ -217,12 +218,12 @@
             struct((size, width)),
             struct((units - pipes * size, width)),
         ],
-        [SMEM, ANY, ANY],
+        [SMEM, ANY, ANY] + [ANY] * len(after),
         "hold_weights",
         1,
         8 * units * width,
         scratch=[pltpu.SemaphoreType.DMA((4,))],
-    )(pipe, w_in, w_out)
+    )(pipe, w_in, w_out, *after)
 
 
 def up_kernel(own_in, z_in, w_own, w_pair, out_ref):
@@ -245,43 +246,48 @@
     )(own, z, *w_in)
 
 
-def up_y_kernel(pipes, *refs):
+def up_y_kernel(pipes, halves, *refs):
     pipe = refs[0][0]
-    own_in, z_in = refs[1:3]
-    y_parts = refs[3 : 3 + pipes]
-    pair_parts = refs[3 + pipes : 3 + 2 * pipes]
+    act_ref, own_in, z_in = refs[1:4]
+    count = pipes * halves
+    y_parts = refs[4 : 4 + count]
+    pair_parts = refs[4 + count : 4 + 2 * count]
     out_ref, entries = refs[-2:]
     rows, width = own_in.shape
+    units = act_ref.shape[1]
     entries[:rows] = own_in[...]
     entries[rows:] = z_in[...]
-    depth = width // pipes
-    raw = jnp.zeros(out_ref.shape, jnp.float32)
-    for shift in range(pipes):
-        part = entries[:, pl.ds(place(pipes, shift, pipe, depth), depth)]
-        weights = jnp.concatenate([y_parts[shift][...], pair_parts[shift][...]], axis=1)
+    out_ref[:, :units] = act_ref[...]
+    depth = width // count
+    raw = jnp.zeros(act_ref.shape, jnp.float32)
+    for i in range(count):
+        half, shift = divmod(i, pipes)
+        at = place(pipes, shift, pipe, halves * depth) + half * depth
+        part = entries[:, pl.ds(pl.multiple_of(at, depth), depth)]
+        weights = jnp.concatenate([y_parts[i][...], pair_parts[i][...]], axis=1)
         raw = raw + jnp.dot(part, weights, preferred_element_type=jnp.float32)
-    out_ref[...] = jnp.maximum(raw, 0.0).astype(jnp.bfloat16)
-
-
-def up_y(pipe, own, z, y_parts, pair_parts, after=()):
+    out_ref[:, units:] = jnp.maximum(raw, 0.0).astype(jnp.bfloat16)
+
+
+def up_y(pipe, act, own, z, y_parts, pair_parts, pipes, after=()):
     rows, width = own.shape
     units = y_parts[0].shape[1]
-    pipes = len(y_parts)
-    return call(
-        functools.partial(up_y_kernel, pipes),
-        struct((2 * rows, 2 * units)),
-        [SMEM] + [VMEM] * (2 + 2 * pipes) + [ANY] * len(after),
+    count = len(y_parts)
+    return call(
+        functools.partial(up_y_kernel, pipes, count // pipes),
+        struct((2 * rows, 4 * units)),
+        [SMEM] + [VMEM] * (3 + 2 * count) + [ANY] * len(after),
         "expert_up_y",
         8 * rows * width * units,
         4 * units * width,
         scratch=[pltpu.VMEM((2 * rows, width), jnp.bfloat16)],
-    )(pipe, own, z, *y_parts, *pair_parts, *after)
+    )(pipe, act, own, z, *y_parts, *pair_parts, *after)
 
 
 def down_kernel(pipes, *refs):
     pipe = refs[0][0]
-    act_ref, act_y_ref, w_own, w_pair = refs[1:5]
-    y_parts, refs = refs[5 : 5 + pipes], refs[5 + pipes :]
+    act_ref, w_own, w_pair = refs[1:4]
+    y_parts, refs = refs[4 : 4 + pipes], refs[4 + pipes :]
     pair_parts, refs = refs[:pipes], refs[pipes:]
     y_rest, pair_rest = refs[:2]
     own_ref, z_ref, held = refs[-3:]
@@ -294,30 +300,29 @@
         held[pl.ds(pl.multiple_of(units + at, size), size)] = pair_parts[shift][...]
     held[pipes * size : units] = y_rest[...]
     held[units + pipes * size :] = pair_rest[...]
-    activation = jnp.concatenate([act_ref[...], act_y_ref[...]], axis=1)
     step = 512
     for at in range(0, width, step):
         cols = slice(at, at + step)
         weights = jnp.concatenate([w_own[:, cols], w_pair[:, cols], held[:, cols]], axis=0)
-        part = jnp.dot(activation, weights, preferred_element_type=jnp.float32)
+        part = jnp.dot(act_ref[...], weights, preferred_element_type=jnp.float32)
         part = part.astype(jnp.bfloat16)
         own_ref[:, cols] = part[:rows]
         z_ref[:, cols] = part[rows:]
 
 
-def down(pipe, acts, w_out, y_parts, pair_parts, rests):
-    rows = acts[0].shape[0] // 2
+def down(pipe, act, w_out, y_parts, pair_parts, rests, after=()):
+    rows = act.shape[0] // 2
     units, width = w_out[0].shape
     pipes = len(y_parts)
     return call(
         functools.partial(down_kernel, pipes),
         [struct((rows, width))] * 2,
-        [SMEM] + [VMEM] * (6 + 2 * pipes),
+        [SMEM] + [VMEM] * (5 + 2 * pipes) + [ANY] * len(after),
         "expert_down",
         16 * rows * width * units,
         8 * units * width,
         scratch=[pltpu.VMEM((2 * units, width), jnp.bfloat16)],
-    )(pipe, *acts, *w_out, *y_parts, *pair_parts, *rests)
+    )(pipe, act, *w_out, *y_parts, *pair_parts, *rests, *after)
 
 
 def total_kernel(held, own_ref, z_ref, *refs):
@@ -401,9 +406,10 @@
     pipe = lax.axis_index("pipe").astype(jnp.int32)
     w_in_pair, w_out_pair = across(w_in, 1), across(w_out, 1)
     pipe = pipe.reshape(1)
-    in_part = cut_part(pipe, w_in, width // pipes)
-    w_in_held, w_out_held, out_part, out_rest = hold(pipe, w_in, w_out, pipes)
-    in_y = across(in_part, 2)
+    depth = width // pipes
+    in_y, in_late = (cut_part(pipe, w_in, depth, at, depth // 2) for at in (0, depth // 2))
+    in_y = across(in_y, 2)
+    in_late = across(*after_all([in_late], kv_pieces[1:2]), 2)
 
     group = (lax.axis_index("expert") // WSPLIT).astype(jnp.int32).reshape(1)
     staged = stage(
@@ -419,17 +425,17 @@
     )
     flat, gates = staged[4:]
     hidden, near, *packed = attend(
-        *staged[:4], kv_pieces, groups, cap, after=[w_in_pair, w_out_pair, w_out_held]
+        *staged[:4], kv_pieces, groups, cap, after=[w_in_pair, w_out_pair]
     )
     far = [groups_on(block, count) for count, block in enumerate(packed, 1)]
     far = jnp.concatenate(far, axis=0) if len(far) > 1 else far[0]
 
-    (in_y,) = after_all([in_y], [near])
-    out_part, out_rest = after_all([out_part, out_rest], [in_y])
-    out_y = across(out_part, 2)
-    rest_y = across(out_rest, 2)
-    in_y = after_all(along(in_y), [])
-    in_pair = paired(in_y)
+    w_in_held, w_out_held, out_part, out_rest = hold(pipe, w_in, w_out, pipes, [near])
+    in_first = along(*after_all([in_y], [out_part]))
+    in_last = after_all([in_late], [in_first[0]])
+    out_part, out_rest = after_all([out_part, out_rest], in_last)
+    in_last = along(*in_last)
+    out_y, rest_y = across(out_part, 2), across(out_rest, 2)
 
     near_z = across(near, 4)
     far = [far]
@@ -437,24 +443,28 @@
         far = after_all(far, [] if step else [near_z], CROSS_WEIGHT)
     (far,) = far
     far_z = [across(far, 4)]
+    in_sent = in_last[-1]
+    in_parts = after_all([*in_first, *in_last], far_z)
     for _ in range(FAR_STEPS):
         far_z = after_all(far_z, [], FAR_WEIGHT)
     (far_z,) = far_z
 
+    in_pair = paired(in_parts)
+
     def experts_up(own, z, after=()):
-        own_act = up(own, z, [w_in_held, w_in_pair])
-        return own_act, up_y(pipe, own, z, in_y, in_pair, after)
-
-    far_acts = experts_up(far, far_z)
-    (out_y,) = after_all([out_y], [in_y[-1]])
-    out_y = after_all(along(out_y), [*far_acts])
-    out_pair = paired(out_y)
+        act = up(own, z, [w_in_held, w_in_pair])
+        return up_y(pipe, act, own, z, in_parts, in_pair, pipes, after)
+
+    far_act = experts_up(far, far_z)
+    out_parts = along(*after_all([out_y], [in_sent]))
+    *out_parts[1:], rest_y = after_all([*out_parts[1:], rest_y], [far_act])
+    out_pair = paired(out_parts)
     rests = [rest_y, across(rest_y, 1)]
 
-    def experts_down(acts):
-        return down(pipe, acts, [w_out_held, w_out_pair], out_y, out_pair, rests)
-
-    far_own, far_sent = experts_down(far_acts)
+    def experts_down(act, after=()):
+        return down(pipe, act, [w_out_held, w_out_pair], out_parts, out_pair, rests, after)
+
+    far_own, far_sent = experts_down(far_act)
     near_own, near_sent = experts_down(experts_up(near, near_z, [far_own]))
     far_sum, near_sent = total(far_own, across(far_sent, 4), [near_sent])
     backs = [

time: 94.1 us -> 92.7 us (0.985)
  local copies, waits for them, and re-layouts: 10.9 us -> 4.5 us
  waiting for transfers between devices: 44.8 us -> 50.2 us
    ppermute x14 -> x17, waiting for transfers between devices: 15.4 us -> 25.6 us  [across(): return lax.ppermute(value, 'expert', [(i, i ^ bit) for i in range(devices)])]
    unnamed x32 -> x16, local copies, waits for them, and re-layouts: 10.8 us -> 2.75 us
    ppermute x2, waiting for transfers between devices: 28.2 us -> 24.2 us  [groups_on(): lax.ppermute(value, 'expert', [(i, (i + shift) % devices) for i in range(...]
    pallas_call x2, Pallas kernels: 5.79 us -> 3.04 us  [down(): call(functools.partial(down_kernel, pipes), [struct((rows, width))] * 2,...]
    transpose x1, local copies, waits for them, and re-layouts: 0.08 us -> 1.75 us  [body(): kv = jnp.transpose(enc_kv[0], (1, 0, 2)).reshape(-1, width)]
    ppermute x14 -> x17, starting transfers between devices: 12.6 us -> 11 us  [across(): return lax.ppermute(value, 'expert', [(i, i ^ bit) for i in range(devices)])]
    pallas_call x3 -> x4, Pallas kernels: 3.77 us -> 5.27 us  [the longest x2 3.55 us: cut_part(): call(functools.partial(part_kernel, stride, first), struct((size, whole.s...]
    ppermute x1, starting transfers between devices: 1.56 us -> 2.94 us  [body(): kv_pieces.append(lax.ppermute(kv, 'pipe', perm))]
  transfers between devices with their start and end apart: 19 -> 23, of which waited for: 10 -> 14; matrix products, arithmetic and copies ran while one was open for 0% -> 2% of each run, Pallas kernels for 12% -> 13%
where the time goes in v12:
time: 92.7 us; the launch traced here: 92.4 us
  waiting for transfers between devices  50.2 us (54%)
  starting transfers between devices  22.9 us (25%)
  Pallas kernels  14.6 us (16%)
  local copies, waits for them, and re-layouts  4.5 us (5%)
    ppermute x17, waiting for transfers between devices, across(): return lax.ppermute(value, 'expert', [(i, i ^ bit) for i in range(devices)])  25.6 us
    ppermute x2, waiting for transfers between devices, groups_on(): lax.ppermute(value, 'expert', [(i, (i + shift) % devices) for i in range(...  24.2 us
    ppermute x17, starting transfers between devices, across(): return lax.ppermute(value, 'expert', [(i, i ^ bit) for i in range(devices)])  11 us
    ppermute x2, starting transfers between devices, groups_on(): lax.ppermute(value, 'expert', [(i, (i + shift) % devices) for i in range(...  6.12 us
    pallas_call x2, Pallas kernels, cut_part(): call(functools.partial(part_kernel, stride, first), struct((size, whole.s...  3.55 us
    pallas_call x2, Pallas kernels, down(): call(functools.partial(down_kernel, pipes), [struct((rows, width))] * 2,...  3.04 us
    ppermute x1, starting transfers between devices, body(): kv_pieces.append(lax.ppermute(kv, 'pipe', perm))  2.94 us
    ppermute x3, starting transfers between devices, along(): return [value] + [lax.ppermute(value, 'pipe', perm) for perm in perms]  2.86 us
  transfers between devices with their start and end apart: 23, of which 14 were waited for; matrix products, arithmetic and copies ran while one was open for 2% of the time, Pallas kernels for 13%

profile of v12, /device:TPU:0, one launch (start us, length us, event | category | flops | bytes accessed | tf_op | source)
XLA Modules:
  0.0 92.4 jit_solution(15890801122772876898)
XLA Ops:
  0.0 0.5 collective-permute-start.2
  0.5 1.7 %copy.29 = bf16[2,32,2048]{2,1,0:T(8,128)(2,1)} copy(bf16[2,32,2048]{2,0,1:T(2,128)(2,1)} %bitcast.19) | data formatting | bytes 524288 | tf_op jit(solution)/shard_map/transpose | solution.py:394
  2.3 2.9 %collective-permute-start = (bf16[64,2048]{1,0:T(8,128)(2,1)}, bf16[64,2048]{1,0:T(8,128)(2,1)}, u32[]{:S(2)}, u32[]{:S(2)}) collective-permute-start(bf16[64,2048]{1,0:T(8,128)(2,1)} %bitcast.9.refs_4_), channel_id=1, source_target_pairs={{0,16},{16,0},{1,17},{17,1},{2,18},{18,2},{3,19},{19,3},{4,20},{20... | collective-permute-start | bytes 786440 | tf_op jit(solution)/shard_map/ppermute | solution.py:398
  5.2 1.8 %weight_part.2 = bf16[512,384]{1,0:T(8,128)(2,1)} custom-call(s32[1]{0:T(128)} %bitcast.10.pipe_ref.refs_0_, bf16[2048,384]{1,0:T(8,128)(2,1)} %whole.3), custom_call_target="tpu_custom_call" | custom-call | flops 1 | bytes 786432 | tf_op jit(solution)/shard_map/weight_part/pallas_call | solution.py:177
  7.0 1.6 %collective-permute-start.4 = (bf16[512,384]{1,0:T(8,128)(2,1)}, bf16[512,384]{1,0:T(8,128)(2,1)S(1)}, u32[]{:S(2)}, u32[]{:S(2)}) collective-permute-start(bf16[512,384]{1,0:T(8,128)(2,1)} %weight_part.2), channel_id=1, source_target_pairs={{0,2},{1,3},{2,0},{3,1},{4,6},{5,7},{6,4},{7,5},{8,10},{9,11},{10,... | collective-permute-start | bytes 1179656 | tf_op jit(solution)/shard_map/ppermute | solution.py:388
  8.6 1.8 %weight_part.3.refs_0_ = bf16[512,384]{1,0:T(8,128)(2,1)} custom-call(s32[1]{0:T(128)} %bitcast.10.pipe_ref.refs_0_, bf16[2048,384]{1,0:T(8,128)(2,1)} %whole.3), custom_call_target="tpu_custom_call" | custom-call | flops 1 | bytes 786432 | tf_op jit(solution)/shard_map/weight_part/pallas_call | solution.py:177
  10.4 1.0 %copy-done.2 = bf16[1,1,128,2048]{3,2,1,0:T(8,128)(2,1)S(1)} copy-done((bf16[1,1,128,2048]{3,2,1,0:T(8,128)(2,1)S(1)}, bf16[1,1,128,2048]{3,2,1,0:T(8,128)(2,1)}, u32[]{:S(2)}) %copy-start.2) | copy-done | bytes 524312
  11.4 1.0 %copy-done.3 = bf16[1,1,128,2048]{3,2,1,0:T(8,128)(2,1)S(1)} copy-done((bf16[1,1,128,2048]{3,2,1,0:T(8,128)(2,1)S(1)}, bf16[1,1,128,2048]{3,2,1,0:T(8,128)(2,1)}, u32[]{:S(2)}) %copy-start.3) | copy-done | bytes 524312
  12.5 0.7 copy-done.7
  13.1 0.1 stage.1
  13.3 0.6 collective-permute-start.6
  13.9 2.6 %attend.1 = (f32[128,2048]{1,0:T(8,128)S(1)}, bf16[96,2048]{1,0:T(8,128)(2,1)S(1)}, bf16[96,2048]{1,0:T(8,128)(2,1)S(1)}) custom-call(bf16[128,2048]{1,0:T(8,128)(2,1)S(1)} %get-tuple-element.32.refs_0_, bf16[128,2048]{1,0:T(8,128)(2,1)S(1)} %get-tuple-element.33.refs_1_, f32[1,2048]{1,0:T(1,128)S(1)} %get-tuple-element.34.refs_2_, ...), custom_call_target="tpu_custom_call" | custom-call | flops 134217728 | bytes 3145728 | tf_op jit(solution)/shard_map/attend/pallas_call | solution.py:152
  16.5 2.7 %collective-permute-start.8 = (bf16[96,2048]{1,0:T(8,128)(2,1)S(1)}, bf16[96,2048]{1,0:T(8,128)(2,1)S(1)}, u32[]{:S(2)}, u32[]{:S(2)}) collective-permute-start(bf16[96,2048]{1,0:T(8,128)(2,1)S(1)} %get-tuple-element.42), channel_id=1, source_target_pairs={{0,8},{1,9},{2,10},{3,11},{4,12},{5,13},{6,14},{7,15},{8,0},{9,1},... | collective-permute-start | bytes 1179656 | tf_op jit(solution)/shard_map/ppermute | solution.py:392
  19.2 1.6 %collective-permute-start.3 = (bf16[96,2048]{1,0:T(8,128)(2,1)S(1)}, bf16[96,2048]{1,0:T(8,128)(2,1)S(1)}, u32[]{:S(2)}, u32[]{:S(2)}) collective-permute-start(bf16[96,2048]{1,0:T(8,128)(2,1)S(1)} %get-tuple-element.39.refs_0_.own_in.refs_2_), channel_id=1, source_target_pairs={{0,4},{1,5},{2,6},{3,7},{4,0},{5,1},{6,2},{7,3},{8,12},{9,13},{10,... | collective-permute-start | bytes 1179656 | tf_op jit(solution)/shard_map/ppermute | solution.py:388
  20.7 0.7 hold_weights.1
  21.5 1.5 %collective-permute-start.5 = (bf16[512,384]{1,0:T(8,128)(2,1)S(1)}, bf16[512,384]{1,0:T(8,128)(2,1)S(1)}, u32[]{:S(2)}, u32[]{:S(2)}) collective-permute-start(bf16[512,384]{1,0:T(8,128)(2,1)S(1)} %hand_on.13.refs_1_.refs_0_), channel_id=1, source_target_pairs={{0,16},{16,0},{1,17},{17,1},{2,18},{18,2},{3,19},{19,3},{4,20},{20... | collective-permute-start | bytes 1179656 | tf_op jit(solution)/shard_map/ppermute | solution.py:401
  23.0 3.5 %collective-permute-done.6.refs_0_ = bf16[512,384]{1,0:T(8,128)(2,1)S(1)} collective-permute-done((bf16[512,384]{1,0:T(8,128)(2,1)}, bf16[512,384]{1,0:T(8,128)(2,1)S(1)}, u32[]{:S(2)}, u32[]{:S(2)}) %collective-permute-start.6) | collective-permute-done | bytes 393248 | tf_op jit(solution)/shard_map/ppermute | solution.py:388
  26.5 0.3 collective-permute-start.7
  26.8 1.7 %collective-permute-start.14 = (bf16[112,2048]{1,0:T(8,128)(2,1)S(1)}, bf16[112,2048]{1,0:T(8,128)(2,1)S(1)}, u32[]{:S(2)}, u32[]{:S(2)}) collective-permute-start(bf16[112,2048]{1,0:T(8,128)(2,1)S(1)} %get-tuple-element.49), channel_id=1, source_target_pairs={{0,2},{1,3},{2,0},{3,1},{4,6},{5,7},{6,4},{7,5},{8,10},{9,11},{10,... | collective-permute-start | bytes 1376264 | tf_op jit(solution)/shard_map/ppermute | solution.py:388
  28.5 7.7 %collective-permute-done.8.refs_0_ = bf16[96,2048]{1,0:T(8,128)(2,1)S(1)} collective-permute-done((bf16[96,2048]{1,0:T(8,128)(2,1)S(1)}, bf16[96,2048]{1,0:T(8,128)(2,1)S(1)}, u32[]{:S(2)}, u32[]{:S(2)}) %collective-permute-start.8) | collective-permute-done | bytes 393248 | tf_op jit(solution)/shard_map/ppermute | solution.py:392
  36.2 0.2 collective-permute-done.3.z_in.refs_1_.refs_3_
  36.4 1.4 %collective-permute-start.9 = (bf16[96,2048]{1,0:T(8,128)(2,1)S(1)}, bf16[96,2048]{1,0:T(8,128)(2,1)S(1)}, u32[]{:S(2)}, u32[]{:S(2)}) collective-permute-start(bf16[96,2048]{1,0:T(8,128)(2,1)S(1)} %hand_on.16.own_in.refs_2_), channel_id=1, source_target_pairs={{0,4},{1,5},{2,6},{3,7},{4,0},{5,1},{6,2},{7,3},{8,12},{9,13},{10,... | collective-permute-start | bytes 1179656 | tf_op jit(solution)/shard_map/ppermute | solution.py:388
  37.8 1.5 %collective-permute-start.16 = (bf16[160,2048]{1,0:T(8,128)(2,1)S(1)}, bf16[160,2048]{1,0:T(8,128)(2,1)S(1)}, u32[]{:S(2)}, u32[]{:S(2)}) collective-permute-start(bf16[160,2048]{1,0:T(8,128)(2,1)S(1)} %get-tuple-element.50), channel_id=1, source_target_pairs={{0,2},{1,3},{2,0},{3,1},{4,6},{5,7},{6,4},{7,5},{8,10},{9,11},{10,... | collective-permute-start | bytes 1966088 | tf_op jit(solution)/shard_map/ppermute | solution.py:388
  39.3 0.3 collective-permute-done.7.refs_3_.refs_1_
  39.6 1.1 %collective-permute-start.15 = (bf16[112,2048]{1,0:T(8,128)(2,1)S(1)}, bf16[112,2048]{1,0:T(8,128)(2,1)S(1)}, u32[]{:S(2)}, u32[]{:S(2)}) collective-permute-start(bf16[112,2048]{1,0:T(8,128)(2,1)S(1)} %hand_on.23.refs_4_), channel_id=1, source_target_pairs={{0,16},{16,0},{1,17},{17,1},{2,18},{18,2},{3,19},{19,3},{4,20},{20... | collective-permute-start | bytes 1376264 | tf_op jit(solution)/shard_map/ppermute | solution.py:401
  40.7 5.4 %collective-permute-done.9.refs_4_.refs_0_ = bf16[96,2048]{1,0:T(8,128)(2,1)S(1)} collective-permute-done((bf16[96,2048]{1,0:T(8,128)(2,1)S(1)}, bf16[96,2048]{1,0:T(8,128)(2,1)S(1)}, u32[]{:S(2)}, u32[]{:S(2)}) %collective-permute-start.9) | collective-permute-done | bytes 393248 | tf_op jit(solution)/shard_map/ppermute | solution.py:388
  46.1 0.5 collective-permute-start.11
  46.6 1.2 %collective-permute-done.10.refs_8_ = bf16[512,384]{1,0:T(8,128)(2,1)S(1)} collective-permute-done((bf16[512,384]{1,0:T(8,128)(2,1)S(1)}, bf16[512,384]{1,0:T(8,128)(2,1)S(1)}, u32[]{:S(2)}, u32[]{:S(2)}) %collective-permute-start.10) | collective-permute-done | bytes 393248 | tf_op jit(solution)/shard_map/ppermute | solution.py:388
  47.8 0.1 collective-permute-start.13
  48.0 0.8 expert_up.3.refs_1_
  48.8 0.2 collective-permute-done.12.refs_10_
  48.9 0.6 collective-permute-done.13.refs_11_
  49.5 0.9 expert_up_y.2.refs_2_.refs_1_
  50.4 2.7 %collective-permute-done.16.refs_1_ = bf16[160,2048]{1,0:T(8,128)(2,1)S(1)} collective-permute-done((bf16[160,2048]{1,0:T(8,128)(2,1)S(1)}, bf16[160,2048]{1,0:T(8,128)(2,1)S(1)}, u32[]{:S(2)}, u32[]{:S(2)}) %collective-permute-start.16) | collective-permute-done | bytes 655392 | tf_op jit(solution)/shard_map/ppermute | solution.py:388
  53.1 0.5 collective-permute-start.17
  53.7 2.2 %collective-permute-done.17.refs_6_ = bf16[112,2048]{1,0:T(8,128)(2,1)S(1)} collective-permute-done((bf16[112,2048]{1,0:T(8,128)(2,1)S(1)}, bf16[112,2048]{1,0:T(8,128)(2,1)S(1)}, u32[]{:S(2)}, u32[]{:S(2)}) %collective-permute-start.17) | collective-permute-done | bytes 458784 | tf_op jit(solution)/shard_map/ppermute | solution.py:388
  55.9 0.7 collective-permute-done.18.refs_7_
  56.6 1.5 %expert_down.2 = (bf16[96,2048]{1,0:T(8,128)(2,1)S(1)}, bf16[96,2048]{1,0:T(8,128)(2,1)S(1)}) custom-call(s32[1]{0:T(128)} %bitcast.10.pipe_ref.refs_0_, bf16[192,1536]{1,0:T(8,128)(2,1)S(1)} %expert_up_y.2.refs_2_.refs_1_, bf16[384,2048]{1,0:T(8,128)(2,1)S(1)} %get-tuple-element.47.refs_2_, bf16[384,2048]{1,0:T(8,128)(2,1)S(1)} %collective-permute-done.2.refs_7_.refs_3_, ...), custom_call_target="tpu_custom_call" | custom-call | flops 1207959552 | bytes 6291456 | tf_op jit(solution)/shard_map/expert_down/pallas_call | solution.py:317
  58.1 0.5 collective-permute-start.20
  58.6 0.8 expert_up.2.refs_1_
  59.4 0.9 expert_up_y.3.refs_1_
  60.3 1.5 %expert_down.3 = (bf16[96,2048]{1,0:T(8,128)(2,1)S(1)}, bf16[96,2048]{1,0:T(8,128)(2,1)S(1)}) custom-call(s32[1]{0:T(128)} %bitcast.10.pipe_ref.refs_0_, bf16[192,1536]{1,0:T(8,128)(2,1)S(1)} %expert_up_y.3.refs_1_, bf16[384,2048]{1,0:T(8,128)(2,1)S(1)} %get-tuple-element.47.refs_2_, bf16[384,2048]{1,0:T(8,128)(2,1)S(1)} %collective-permute-done.2.refs_7_.refs_3_, ...), custom_call_target="tpu_custom_call" | custom-call | flops 1207959552 | bytes 6291456 | tf_op jit(solution)/shard_map/expert_down/pallas_call | solution.py:317
  61.8 7.5 %collective-permute-done.20.z_ref = bf16[96,2048]{1,0:T(8,128)(2,1)S(1)} collective-permute-done((bf16[96,2048]{1,0:T(8,128)(2,1)S(1)}, bf16[96,2048]{1,0:T(8,128)(2,1)S(1)}, u32[]{:S(2)}, u32[]{:S(2)}) %collective-permute-start.20) | collective-permute-done | bytes 393248 | tf_op jit(solution)/shard_map/ppermute | solution.py:388
  69.4 3.5 %collective-permute-start.22 = (bf16[96,2048]{1,0:T(8,128)(2,1)S(1)}, bf16[96,2048]{1,0:T(8,128)(2,1)S(1)}, u32[]{:S(2)}, u32[]{:S(2)}) collective-permute-start(bf16[96,2048]{1,0:T(8,128)(2,1)S(1)} %get-tuple-element.58), channel_id=1, source_target_pairs={{0,8},{1,9},{2,10},{3,11},{4,12},{5,13},{6,14},{7,15},{8,0},{9,1},... | collective-permute-start | bytes 1179656 | tf_op jit(solution)/shard_map/ppermute | solution.py:392
  72.9 0.3 collective-permute-start.21
  73.2 16.6 %collective-permute-done.22.refs_0_ = bf16[96,2048]{1,0:T(8,128)(2,1)S(1)} collective-permute-done((bf16[96,2048]{1,0:T(8,128)(2,1)S(1)}, bf16[96,2048]{1,0:T(8,128)(2,1)S(1)}, u32[]{:S(2)}, u32[]{:S(2)}) %collective-permute-start.22) | collective-permute-done | bytes 393248 | tf_op jit(solution)/shard_map/ppermute | solution.py:392
  89.7 1.5 %collective-permute-done.21.refs_4_ = bf16[96,2048]{1,0:T(8,128)(2,1)S(1)} collective-permute-done((bf16[96,2048]{1,0:T(8,128)(2,1)S(1)}, bf16[96,2048]{1,0:T(8,128)(2,1)S(1)}, u32[]{:S(2)}, u32[]{:S(2)}) %collective-permute-start.21) | collective-permute-done | bytes 393248 | tf_op jit(solution)/shard_map/ppermute | solution.py:388
  91.2 1.2 %finish.1 = bf16[128,2048]{1,0:T(8,128)(2,1)} custom-call(f32[128,2048]{1,0:T(8,128)S(1)} %get-tuple-element.36.refs_0_, f32[128,1]{1,0:T(8,128)S(1)} %get-tuple-element.37.refs_1_, s32[128,1]{1,0:T(8,128)S(1)} %get-tuple-element.38.refs_2_, bf16[96,2048]{1,0:T(8,128)(2,1)S(1)} %get-tuple-element.54.refs_3_, ...), custom_call_target="tpu_custom_call" | custom-call | flops 201326592 | bytes 4194304 | tf_op jit(solution)/shard_map/finish/pallas_call | solution.py:370
  (41 shorter events, 0.3 us)
Async XLA Ops:
  0.0 13.9 %collective-permute-start.2 = (bf16[384,2048]{1,0:T(8,128)(2,1)}, bf16[384,2048]{1,0:T(8,128)(2,1)S(1)}, u32[]{:S(2)}, u32[]{:S(2)}) collective-permute-start(bf16[384,2048]{1,0:T(8,128)(2,1)} %w_out.1), channel_id=1, source_target_pairs={{0,1},{1,0},{2,3},{3,2},{4,5},{5,4},{6,7},{7,6},{8,9},{9,8},{10,11... | collective-permute-start | bytes 4718600 | tf_op jit(solution)/shard_map/ppermute | solution.py:388
  0.5 13.4 %collective-permute-start.1 = (bf16[2048,384]{1,0:T(8,128)(2,1)}, bf16[2048,384]{1,0:T(8,128)(2,1)S(1)}, u32[]{:S(2)}, u32[]{:S(2)}) collective-permute-start(bf16[2048,384]{1,0:T(8,128)(2,1)} %whole.3), channel_id=1, source_target_pairs={{0,1},{1,0},{2,3},{3,2},{4,5},{5,4},{6,7},{7,6},{8,9},{9,8},{10,11... | collective-permute-start | bytes 4718600 | tf_op jit(solution)/shard_map/ppermute | solution.py:388
  2.3 11.0 %collective-permute-start = (bf16[64,2048]{1,0:T(8,128)(2,1)}, bf16[64,2048]{1,0:T(8,128)(2,1)}, u32[]{:S(2)}, u32[]{:S(2)}) collective-permute-start(bf16[64,2048]{1,0:T(8,128)(2,1)} %bitcast.9.refs_4_), channel_id=1, source_target_pairs={{0,16},{16,0},{1,17},{17,1},{2,18},{18,2},{3,19},{19,3},{4,20},{20... | collective-permute-start | bytes 786440 | tf_op jit(solution)/shard_map/ppermute | solution.py:398
  5.2 5.2 %copy-start.4 = (f32[2048]{0:T(1024)S(1)}, f32[2048]{0:T(1024)}, u32[]{:S(2)}) copy-start(f32[2048]{0:T(1024)} %param.12) | copy-start | bytes 24580
  5.2 5.2 %copy-start.5 = (s32[1,1,128]{2,1,0:T(1,128)S(1)}, s32[1,1,128]{2,1,0:T(1,128)}, u32[]{:S(2)}) copy-start(s32[1,1,128]{2,1,0:T(1,128)} %param.15) | copy-start | bytes 1540
  5.2 5.2 %copy-start.6 = (s32[1,1,128]{2,1,0:T(1,128)S(1)}, s32[1,1,128]{2,1,0:T(1,128)}, u32[]{:S(2)}) copy-start(s32[1,1,128]{2,1,0:T(1,128)} %param.16) | copy-start | bytes 1540
  7.0 14.5 %collective-permute-start.4 = (bf16[512,384]{1,0:T(8,128)(2,1)}, bf16[512,384]{1,0:T(8,128)(2,1)S(1)}, u32[]{:S(2)}, u32[]{:S(2)}) collective-permute-start(bf16[512,384]{1,0:T(8,128)(2,1)} %weight_part.2), channel_id=1, source_target_pairs={{0,2},{1,3},{2,0},{3,1},{4,6},{5,7},{6,4},{7,5},{8,10},{9,11},{10,... | collective-permute-start | bytes 1179656 | tf_op jit(solution)/shard_map/ppermute | solution.py:388
  10.4 1.0 %copy-start.2 = (bf16[1,1,128,2048]{3,2,1,0:T(8,128)(2,1)S(1)}, bf16[1,1,128,2048]{3,2,1,0:T(8,128)(2,1)}, u32[]{:S(2)}) copy-start(bf16[1,1,128,2048]{3,2,1,0:T(8,128)(2,1)} %param.9) | copy-start | bytes 1572868
  11.4 1.0 %copy-start.3 = (bf16[1,1,128,2048]{3,2,1,0:T(8,128)(2,1)S(1)}, bf16[1,1,128,2048]{3,2,1,0:T(8,128)(2,1)}, u32[]{:S(2)}) copy-start(bf16[1,1,128,2048]{3,2,1,0:T(8,128)(2,1)} %param.10) | copy-start | bytes 1572868
  12.5 0.7 copy-start.7
  13.3 13.2 %collective-permute-start.6 = (bf16[512,384]{1,0:T(8,128)(2,1)}, bf16[512,384]{1,0:T(8,128)(2,1)S(1)}, u32[]{:S(2)}, u32[]{:S(2)}) collective-permute-start(bf16[512,384]{1,0:T(8,128)(2,1)} %hand_on.14), channel_id=1, source_target_pairs={{0,2},{1,3},{2,0},{3,1},{4,6},{5,7},{6,4},{7,5},{8,10},{9,11},{10,... | collective-permute-start | bytes 1179656 | tf_op jit(solution)/shard_map/ppermute | solution.py:388
  13.9 6.9 %copy-start = (bf16[2048,384]{1,0:T(8,128)(2,1)S(1)}, bf16[2048,384]{1,0:T(8,128)(2,1)}, u32[]{:S(2)}) copy-start(bf16[2048,384]{1,0:T(8,128)(2,1)} %whole.3) | copy-start | bytes 4718596
  13.9 6.9 %copy-start.1 = (bf16[384,2048]{1,0:T(8,128)(2,1)S(1)}, bf16[384,2048]{1,0:T(8,128)(2,1)}, u32[]{:S(2)}) copy-start(bf16[384,2048]{1,0:T(8,128)(2,1)} %w_out.1) | copy-start | bytes 4718596
  16.5 19.7 %collective-permute-start.8 = (bf16[96,2048]{1,0:T(8,128)(2,1)S(1)}, bf16[96,2048]{1,0:T(8,128)(2,1)S(1)}, u32[]{:S(2)}, u32[]{:S(2)}) collective-permute-start(bf16[96,2048]{1,0:T(8,128)(2,1)S(1)} %get-tuple-element.42), channel_id=1, source_target_pairs={{0,8},{1,9},{2,10},{3,11},{4,12},{5,13},{6,14},{7,15},{8,0},{9,1},... | collective-permute-start | bytes 1179656 | tf_op jit(solution)/shard_map/ppermute | solution.py:392
  19.2 17.2 %collective-permute-start.3 = (bf16[96,2048]{1,0:T(8,128)(2,1)S(1)}, bf16[96,2048]{1,0:T(8,128)(2,1)S(1)}, u32[]{:S(2)}, u32[]{:S(2)}) collective-permute-start(bf16[96,2048]{1,0:T(8,128)(2,1)S(1)} %get-tuple-element.39.refs_0_.own_in.refs_2_), channel_id=1, source_target_pairs={{0,4},{1,5},{2,6},{3,7},{4,0},{5,1},{6,2},{7,3},{8,12},{9,13},{10,... | collective-permute-start | bytes 1179656 | tf_op jit(solution)/shard_map/ppermute | solution.py:388
  21.5 19.2 %collective-permute-start.5 = (bf16[512,384]{1,0:T(8,128)(2,1)S(1)}, bf16[512,384]{1,0:T(8,128)(2,1)S(1)}, u32[]{:S(2)}, u32[]{:S(2)}) collective-permute-start(bf16[512,384]{1,0:T(8,128)(2,1)S(1)} %hand_on.13.refs_1_.refs_0_), channel_id=1, source_target_pairs={{0,16},{16,0},{1,17},{17,1},{2,18},{18,2},{3,19},{19,3},{4,20},{20... | collective-permute-start | bytes 1179656 | tf_op jit(solution)/shard_map/ppermute | solution.py:401
  26.5 13.2 %collective-permute-start.7 = (bf16[512,384]{1,0:T(8,128)(2,1)S(1)}, bf16[512,384]{1,0:T(8,128)(2,1)S(1)}, u32[]{:S(2)}, u32[]{:S(2)}) collective-permute-start(bf16[512,384]{1,0:T(8,128)(2,1)S(1)} %hand_on.15.refs_2_), channel_id=1, source_target_pairs={{0,16},{16,0},{1,17},{17,1},{2,18},{18,2},{3,19},{19,3},{4,20},{20... | collective-permute-start | bytes 1179656 | tf_op jit(solution)/shard_map/ppermute | solution.py:401
  26.8 12.9 %collective-permute-start.14 = (bf16[112,2048]{1,0:T(8,128)(2,1)S(1)}, bf16[112,2048]{1,0:T(8,128)(2,1)S(1)}, u32[]{:S(2)}, u32[]{:S(2)}) collective-permute-start(bf16[112,2048]{1,0:T(8,128)(2,1)S(1)} %get-tuple-element.49), channel_id=1, source_target_pairs={{0,2},{1,3},{2,0},{3,1},{4,6},{5,7},{6,4},{7,5},{8,10},{9,11},{10,... | collective-permute-start | bytes 1376264 | tf_op jit(solution)/shard_map/ppermute | solution.py:388
  36.4 9.7 %collective-permute-start.9 = (bf16[96,2048]{1,0:T(8,128)(2,1)S(1)}, bf16[96,2048]{1,0:T(8,128)(2,1)S(1)}, u32[]{:S(2)}, u32[]{:S(2)}) collective-permute-start(bf16[96,2048]{1,0:T(8,128)(2,1)S(1)} %hand_on.16.own_in.refs_2_), channel_id=1, source_target_pairs={{0,4},{1,5},{2,6},{3,7},{4,0},{5,1},{6,2},{7,3},{8,12},{9,13},{10,... | collective-permute-start | bytes 1179656 | tf_op jit(solution)/shard_map/ppermute | solution.py:388
  37.8 15.3 %collective-permute-start.16 = (bf16[160,2048]{1,0:T(8,128)(2,1)S(1)}, bf16[160,2048]{1,0:T(8,128)(2,1)S(1)}, u32[]{:S(2)}, u32[]{:S(2)}) collective-permute-start(bf16[160,2048]{1,0:T(8,128)(2,1)S(1)} %get-tuple-element.50), channel_id=1, source_target_pairs={{0,2},{1,3},{2,0},{3,1},{4,6},{5,7},{6,4},{7,5},{8,10},{9,11},{10,... | collective-permute-start | bytes 1966088 | tf_op jit(solution)/shard_map/ppermute | solution.py:388
  39.6 13.5 %collective-permute-start.15 = (bf16[112,2048]{1,0:T(8,128)(2,1)S(1)}, bf16[112,2048]{1,0:T(8,128)(2,1)S(1)}, u32[]{:S(2)}, u32[]{:S(2)}) collective-permute-start(bf16[112,2048]{1,0:T(8,128)(2,1)S(1)} %hand_on.23.refs_4_), channel_id=1, source_target_pairs={{0,16},{16,0},{1,17},{17,1},{2,18},{18,2},{3,19},{19,3},{4,20},{20... | collective-permute-start | bytes 1376264 | tf_op jit(solution)/shard_map/ppermute | solution.py:401
  46.1 1.7 %collective-permute-start.10 = (bf16[512,384]{1,0:T(8,128)(2,1)S(1)}, bf16[512,384]{1,0:T(8,128)(2,1)S(1)}, u32[]{:S(2)}, u32[]{:S(2)}) collective-permute-start(bf16[512,384]{1,0:T(8,128)(2,1)S(1)} %get-tuple-element.43.refs_4_), channel_id=1, source_target_pairs={{0,1},{1,0},{2,3},{3,2},{4,5},{5,4},{6,7},{7,6},{8,9},{9,8},{10,11... | collective-permute-start | bytes 1179656 | tf_op jit(solution)/shard_map/ppermute | solution.py:388
  46.1 2.7 %collective-permute-start.11 = (bf16[512,384]{1,0:T(8,128)(2,1)S(1)}, bf16[512,384]{1,0:T(8,128)(2,1)S(1)}, u32[]{:S(2)}, u32[]{:S(2)}) collective-permute-start(bf16[512,384]{1,0:T(8,128)(2,1)S(1)} %get-tuple-element.44.refs_5_), channel_id=1, source_target_pairs={{0,1},{1,0},{2,3},{3,2},{4,5},{5,4},{6,7},{7,6},{8,9},{9,8},{10,11... | collective-permute-start | bytes 1179656 | tf_op jit(solution)/shard_map/ppermute | solution.py:388
  46.6 2.3 %collective-permute-start.12 = (bf16[512,384]{1,0:T(8,128)(2,1)S(1)}, bf16[512,384]{1,0:T(8,128)(2,1)S(1)}, u32[]{:S(2)}, u32[]{:S(2)}) collective-permute-start(bf16[512,384]{1,0:T(8,128)(2,1)S(1)} %get-tuple-element.45.refs_6_), channel_id=1, source_target_pairs={{0,1},{1,0},{2,3},{3,2},{4,5},{5,4},{6,7},{7,6},{8,9},{9,8},{10,11... | collective-permute-start | bytes 1179656 | tf_op jit(solution)/shard_map/ppermute | solution.py:388
  47.8 1.7 %collective-permute-start.13 = (bf16[512,384]{1,0:T(8,128)(2,1)S(1)}, bf16[512,384]{1,0:T(8,128)(2,1)S(1)}, u32[]{:S(2)}, u32[]{:S(2)}) collective-permute-start(bf16[512,384]{1,0:T(8,128)(2,1)S(1)} %get-tuple-element.46.refs_7_), channel_id=1, source_target_pairs={{0,1},{1,0},{2,3},{3,2},{4,5},{5,4},{6,7},{7,6},{8,9},{9,8},{10,11... | collective-permute-start | bytes 1179656 | tf_op jit(solution)/shard_map/ppermute | solution.py:388
  53.1 3.4 %collective-permute-start.19 = (bf16[160,2048]{1,0:T(8,128)(2,1)S(1)}, bf16[160,2048]{1,0:T(8,128)(2,1)S(1)}, u32[]{:S(2)}, u32[]{:S(2)}) collective-permute-start(bf16[160,2048]{1,0:T(8,128)(2,1)S(1)} %get-tuple-element.52.refs_8_), channel_id=1, source_target_pairs={{0,1},{1,0},{2,3},{3,2},{4,5},{5,4},{6,7},{7,6},{8,9},{9,8},{10,11... | collective-permute-start | bytes 1966088 | tf_op jit(solution)/shard_map/ppermute | solution.py:388
  53.1 2.8 %collective-permute-start.17 = (bf16[112,2048]{1,0:T(8,128)(2,1)S(1)}, bf16[112,2048]{1,0:T(8,128)(2,1)S(1)}, u32[]{:S(2)}, u32[]{:S(2)}) collective-permute-start(bf16[112,2048]{1,0:T(8,128)(2,1)S(1)} %hand_on.23.refs_4_), channel_id=1, source_target_pairs={{0,1},{1,0},{2,3},{3,2},{4,5},{5,4},{6,7},{7,6},{8,9},{9,8},{10,11... | collective-permute-start | bytes 1376264 | tf_op jit(solution)/shard_map/ppermute | solution.py:388
  53.7 2.9 %collective-permute-start.18 = (bf16[112,2048]{1,0:T(8,128)(2,1)S(1)}, bf16[112,2048]{1,0:T(8,128)(2,1)S(1)}, u32[]{:S(2)}, u32[]{:S(2)}) collective-permute-start(bf16[112,2048]{1,0:T(8,128)(2,1)S(1)} %get-tuple-element.51.refs_5_), channel_id=1, source_target_pairs={{0,1},{1,0},{2,3},{3,2},{4,5},{5,4},{6,7},{7,6},{8,9},{9,8},{10,11... | collective-permute-start | bytes 1376264 | tf_op jit(solution)/shard_map/ppermute | solution.py:388
  58.1 11.2 %collective-permute-start.20 = (bf16[96,2048]{1,0:T(8,128)(2,1)S(1)}, bf16[96,2048]{1,0:T(8,128)(2,1)S(1)}, u32[]{:S(2)}, u32[]{:S(2)}) collective-permute-start(bf16[96,2048]{1,0:T(8,128)(2,1)S(1)} %get-tuple-element.55), channel_id=1, source_target_pairs={{0,4},{1,5},{2,6},{3,7},{4,0},{5,1},{6,2},{7,3},{8,12},{9,13},{10,... | collective-permute-start | bytes 1179656 | tf_op jit(solution)/shard_map/ppermute | solution.py:388
  69.4 20.3 %collective-permute-start.22 = (bf16[96,2048]{1,0:T(8,128)(2,1)S(1)}, bf16[96,2048]{1,0:T(8,128)(2,1)S(1)}, u32[]{:S(2)}, u32[]{:S(2)}) collective-permute-start(bf16[96,2048]{1,0:T(8,128)(2,1)S(1)} %get-tuple-element.58), channel_id=1, source_target_pairs={{0,8},{1,9},{2,10},{3,11},{4,12},{5,13},{6,14},{7,15},{8,0},{9,1},... | collective-permute-start | bytes 1179656 | tf_op jit(solution)/shard_map/ppermute | solution.py:392
  72.9 18.4 %collective-permute-start.21 = (bf16[96,2048]{1,0:T(8,128)(2,1)S(1)}, bf16[96,2048]{1,0:T(8,128)(2,1)S(1)}, u32[]{:S(2)}, u32[]{:S(2)}) collective-permute-start(bf16[96,2048]{1,0:T(8,128)(2,1)S(1)} %get-tuple-element.57), channel_id=1, source_target_pairs={{0,4},{1,5},{2,6},{3,7},{4,0},{5,1},{6,2},{7,3},{8,12},{9,13},{10,... | collective-permute-start | bytes 1179656 | tf_op jit(solution)/shard_map/ppermute | solution.py:388

commit v13 on v12

--- a/solution.py
+++ b/solution.py
@@ -284,7 +284,7 @@
     )(pipe, act, own, z, *y_parts, *pair_parts, *after)
 
 
-def down_kernel(pipes, *refs):
+def down_kernel(pipes, first, *refs):
     pipe = refs[0][0]
     act_ref, w_own, w_pair = refs[1:4]
     y_parts, refs = refs[4 : 4 + pipes], refs[4 + pipes :]
@@ -292,30 +292,32 @@
     y_rest, pair_rest = refs[:2]
     own_ref, z_ref, held = refs[-3:]
     rows, width = own_ref.shape
+    whole = slice(first, first + width)
     units = w_own.shape[0]
     size = y_parts[0].shape[0]
     for shift in range(pipes):
         at = place(pipes, shift, pipe, size)
-        held[pl.ds(at, size)] = y_parts[shift][...]
-        held[pl.ds(pl.multiple_of(units + at, size), size)] = pair_parts[shift][...]
-    held[pipes * size : units] = y_rest[...]
-    held[units + pipes * size :] = pair_rest[...]
+        held[pl.ds(at, size)] = y_parts[shift][:, whole]
+        held[pl.ds(pl.multiple_of(units + at, size), size)] = pair_parts[shift][:, whole]
+    held[pipes * size : units] = y_rest[:, whole]
+    held[units + pipes * size :] = pair_rest[:, whole]
     step = 512
     for at in range(0, width, step):
         cols = slice(at, at + step)
-        weights = jnp.concatenate([w_own[:, cols], w_pair[:, cols], held[:, cols]], axis=0)
+        there = slice(first + at, first + at + step)
+        weights = jnp.concatenate([w_own[:, there], w_pair[:, there], held[:, cols]], axis=0)
         part = jnp.dot(act_ref[...], weights, preferred_element_type=jnp.float32)
         part = part.astype(jnp.bfloat16)
         own_ref[:, cols] = part[:rows]
         z_ref[:, cols] = part[rows:]
 
 
-def down(pipe, act, w_out, y_parts, pair_parts, rests, after=()):
+def down(pipe, act, w_out, y_parts, pair_parts, rests, first, width, after=()):
     rows = act.shape[0] // 2
-    units, width = w_out[0].shape
+    units = w_out[0].shape[0]
     pipes = len(y_parts)
     return call(
-        functools.partial(down_kernel, pipes),
+        functools.partial(down_kernel, pipes, first),
         [struct((rows, width))] * 2,
         [SMEM] + [VMEM] * (5 + 2 * pipes) + [ANY] * len(after),
         "expert_down",
@@ -359,7 +361,9 @@
         near = (own_ref[:, cols].astype(jnp.float32) + z_ref[:, cols].astype(jnp.float32)).astype(
             jnp.bfloat16
         )
-        found = jnp.concatenate([near] + [r[:, cols] for r in back_refs], axis=0)
+        side, inner = divmod(at, width // 2)
+        backs = [r[:, inner : inner + step] for r in back_refs[side::2]]
+        found = jnp.concatenate([near, *backs], axis=0)
         picked = jnp.dot(picker, found, preferred_element_type=jnp.float32)
         out_ref[:, cols] = (hidden_ref[:, cols] + gate_ref[...] * picked).astype(jnp.bfloat16)
 
@@ -391,11 +395,6 @@
         shift = count * WSPLIT
         return lax.ppermute(value, "expert", [(i, (i + shift) % devices) for i in range(devices)])
 
-    kv = jnp.transpose(enc_kv[0], (1, 0, 2)).reshape(-1, width)
-    kv_pieces = [kv]
-    for shift in range(1, pipes):
-        perm = [(i, (i + shift) % pipes) for i in range(pipes)]
-        kv_pieces.append(lax.ppermute(kv, "pipe", perm))
     def along(value):
         perms = [[(i, (i + shift) % pipes) for i in range(pipes)] for shift in range(1, pipes)]
         return [value] + [lax.ppermute(value, "pipe", perm) for perm in perms]
@@ -408,6 +407,12 @@
     pipe = pipe.reshape(1)
     depth = width // pipes
     in_y, in_late = (cut_part(pipe, w_in, depth, at, depth // 2) for at in (0, depth // 2))
+    kv = jnp.transpose(enc_kv[0], (1, 0, 2)).reshape(-1, width)
+    (kv,) = after_all([kv], [in_y])
+    kv_pieces = [kv]
+    for shift in range(1, pipes):
+        perm = [(i, (i + shift) % pipes) for i in range(pipes)]
+        kv_pieces.append(lax.ppermute(kv, "pipe", perm))
     in_y = across(in_y, 2)
     in_late = across(*after_all([in_late], kv_pieces[1:2]), 2)
 
@@ -457,19 +462,28 @@
 
     far_act = experts_up(far, far_z)
     out_parts = along(*after_all([out_y], [in_sent]))
-    *out_parts[1:], rest_y = after_all([*out_parts[1:], rest_y], [far_act])
-    out_pair = paired(out_parts)
+    out_pair = paired(out_parts[:1])
+    *out_parts[1:], rest_y = after_all([*out_parts[1:], rest_y], [far_act, *out_pair])
+    out_pair += paired(out_parts[1:])
     rests = [rest_y, across(rest_y, 1)]
 
-    def experts_down(act, after=()):
-        return down(pipe, act, [w_out_held, w_out_pair], out_parts, out_pair, rests, after)
-
-    far_own, far_sent = experts_down(far_act)
-    near_own, near_sent = experts_down(experts_up(near, near_z, [far_own]))
-    far_sum, near_sent = total(far_own, across(far_sent, 4), [near_sent])
+    def experts_down(act, first, size, after=()):
+        return down(
+            pipe, act, [w_out_held, w_out_pair], out_parts, out_pair, rests, first, size, after
+        )
+
+    half = width // 2
+    far_a, sent_a = experts_down(far_act, 0, half)
+    far_b, sent_b = experts_down(far_act, half, half, [far_a])
+    near_act = experts_up(near, near_z, [far_b])
+    (sent_b,) = after_all([sent_b], [near_act])
+    near_own, near_sent = experts_down(near_act, 0, width)
+    (sum_a,) = total(far_a, across(sent_a, 4), [])
+    sum_b, near_sent = total(far_b, across(sent_b, 4), [near_sent])
     backs = [
-        groups_on(far_sum[(count - 1) * cap : count * cap], groups - count)
+        groups_on(side[(count - 1) * cap : count * cap], groups - count)
         for count in range(1, groups)
+        for side in (sum_a, sum_b)
     ]
     backs = after_all(backs, [], BACK_WEIGHT)
     near_sums = [near_own, across(near_sent, 4)]

time: 92.7 us -> 90.3 us (0.974)
  waiting for transfers between devices: 50.2 us -> 44.5 us
  starting transfers between devices: 22.9 us -> 27 us
  local copies, waits for them, and re-layouts: 4.5 us -> 3.56 us
    ppermute x17 -> x18, waiting for transfers between devices: 25.6 us -> 21.9 us  [across(): return lax.ppermute(value, 'expert', [(i, i ^ bit) for i in range(devices)])]
    ppermute x2 -> x3, waiting for transfers between devices: 24.2 us -> 20.7 us  [groups_on(): lax.ppermute(value, 'expert', [(i, (i + shift) % devices) for i in range(...]
    ppermute x17 -> x18, starting transfers between devices: 11 us -> 13.2 us  [across(): return lax.ppermute(value, 'expert', [(i, i ^ bit) for i in range(devices)])]
    ppermute x2 -> x3, starting transfers between devices: 6.12 us -> 7.37 us  [groups_on(): lax.ppermute(value, 'expert', [(i, (i + shift) % devices) for i in range(...]
    ppermute x3, waiting for transfers between devices: 0.28 us -> 1.3 us  [along(): return [value] + [lax.ppermute(value, 'pipe', perm) for perm in perms]]
    transpose x1, local copies, waits for them, and re-layouts: 1.75 us -> 0.8 us  [body(): kv = jnp.transpose(enc_kv[0], (1, 0, 2)).reshape(-1, width)]
    pallas_call x2 -> x3, Pallas kernels: 3.04 us -> 3.2 us  [down(): call(functools.partial(down_kernel, pipes, first), [struct((rows, width))...]
    unnamed x16 -> x18, local copies, waits for them, and re-layouts: 2.75 us -> 2.76 us
  transfers between devices with their start and end apart: 23 -> 25, of which waited for: 14 -> 17; matrix products, arithmetic and copies ran while one was open for 2% -> 1% of each run, Pallas kernels for 13% -> 12%
where the time goes in v13:
time: 90.3 us; the launch traced here: 90.1 us
  waiting for transfers between devices  44.5 us (49%)
  starting transfers between devices  27 us (30%)
  Pallas kernels  14.8 us (16%)
  local copies, waits for them, and re-layouts  3.56 us (4%)
    ppermute x18, waiting for transfers between devices, across(): return lax.ppermute(value, 'expert', [(i, i ^ bit) for i in range(devices)])  21.9 us
    ppermute x3, waiting for transfers between devices, groups_on(): lax.ppermute(value, 'expert', [(i, (i + shift) % devices) for i in range(...  20.7 us
    ppermute x18, starting transfers between devices, across(): return lax.ppermute(value, 'expert', [(i, i ^ bit) for i in range(devices)])  13.2 us
    ppermute x3, starting transfers between devices, groups_on(): lax.ppermute(value, 'expert', [(i, (i + shift) % devices) for i in range(...  7.37 us
    pallas_call x2, Pallas kernels, cut_part(): call(functools.partial(part_kernel, stride, first), struct((size, whole.s...  3.49 us
    ppermute x3, starting transfers between devices, along(): return [value] + [lax.ppermute(value, 'pipe', perm) for perm in perms]  3.47 us
    pallas_call x3, Pallas kernels, down(): call(functools.partial(down_kernel, pipes, first), [struct((rows, width))...  3.2 us
    ppermute x1, starting transfers between devices, body(): kv_pieces.append(lax.ppermute(kv, 'pipe', perm))  2.93 us
  transfers between devices with their start and end apart: 25, of which 17 were waited for; matrix products, arithmetic and copies ran while one was open for 1% of the time, Pallas kernels for 12%

profile of v13, /device:TPU:0, one launch (start us, length us, event | category | flops | bytes accessed | tf_op | source)
XLA Modules:
  0.0 90.1 jit_solution(2020585075993699787)
XLA Ops:
  0.0 0.5 collective-permute-start.2
  0.5 1.7 %weight_part.2.refs_1_ = bf16[512,384]{1,0:T(8,128)(2,1)} custom-call(s32[1]{0:T(128)} %bitcast.10.pipe_ref.refs_0_, bf16[2048,384]{1,0:T(8,128)(2,1)} %whole.3), custom_call_target="tpu_custom_call" | custom-call | flops 1 | bytes 786432 | tf_op jit(solution)/shard_map/weight_part/pallas_call | solution.py:177
  2.3 0.8 copy.32
  3.1 2.9 %collective-permute-start = (bf16[64,2048]{1,0:T(8,128)(2,1)}, bf16[64,2048]{1,0:T(8,128)(2,1)}, u32[]{:S(2)}, u32[]{:S(2)}) collective-permute-start(bf16[64,2048]{1,0:T(8,128)(2,1)} %hand_on.15.refs_4_), channel_id=1, source_target_pairs={{0,16},{16,0},{1,17},{17,1},{2,18},{18,2},{3,19},{19,3},{4,20},{20... | collective-permute-start | bytes 786440 | tf_op jit(solution)/shard_map/ppermute | solution.py:415
  6.0 1.5 %collective-permute-start.4 = (bf16[512,384]{1,0:T(8,128)(2,1)}, bf16[512,384]{1,0:T(8,128)(2,1)S(1)}, u32[]{:S(2)}, u32[]{:S(2)}) collective-permute-start(bf16[512,384]{1,0:T(8,128)(2,1)} %weight_part.2.refs_1_), channel_id=1, source_target_pairs={{0,2},{1,3},{2,0},{3,1},{4,6},{5,7},{6,4},{7,5},{8,10},{9,11},{10,... | collective-permute-start | bytes 1179656 | tf_op jit(solution)/shard_map/ppermute | solution.py:392
  7.5 1.7 %weight_part.3.refs_0_ = bf16[512,384]{1,0:T(8,128)(2,1)} custom-call(s32[1]{0:T(128)} %bitcast.10.pipe_ref.refs_0_, bf16[2048,384]{1,0:T(8,128)(2,1)} %whole.3), custom_call_target="tpu_custom_call" | custom-call | flops 1 | bytes 786432 | tf_op jit(solution)/shard_map/weight_part/pallas_call | solution.py:177
  9.4 1.0 %copy-done.2 = bf16[1,1,128,2048]{3,2,1,0:T(8,128)(2,1)S(1)} copy-done((bf16[1,1,128,2048]{3,2,1,0:T(8,128)(2,1)S(1)}, bf16[1,1,128,2048]{3,2,1,0:T(8,128)(2,1)}, u32[]{:S(2)}) %copy-start.2) | copy-done | bytes 524312
  10.4 1.0 %copy-done.3 = bf16[1,1,128,2048]{3,2,1,0:T(8,128)(2,1)S(1)} copy-done((bf16[1,1,128,2048]{3,2,1,0:T(8,128)(2,1)S(1)}, bf16[1,1,128,2048]{3,2,1,0:T(8,128)(2,1)}, u32[]{:S(2)}) %copy-start.3) | copy-done | bytes 524312
  11.4 0.7 copy-done.7
  12.2 0.7 collective-permute-done.refs_5_.refs_1_
  12.9 1.8 %collective-permute-start.6 = (bf16[512,384]{1,0:T(8,128)(2,1)}, bf16[512,384]{1,0:T(8,128)(2,1)S(1)}, u32[]{:S(2)}, u32[]{:S(2)}) collective-permute-start(bf16[512,384]{1,0:T(8,128)(2,1)} %hand_on.17), channel_id=1, source_target_pairs={{0,2},{1,3},{2,0},{3,1},{4,6},{5,7},{6,4},{7,5},{8,10},{9,11},{10,... | collective-permute-start | bytes 1179656 | tf_op jit(solution)/shard_map/ppermute | solution.py:392
  14.7 2.6 %attend.1 = (f32[128,2048]{1,0:T(8,128)S(1)}, bf16[96,2048]{1,0:T(8,128)(2,1)S(1)}, bf16[96,2048]{1,0:T(8,128)(2,1)S(1)}) custom-call(bf16[128,2048]{1,0:T(8,128)(2,1)S(1)} %get-tuple-element.36.refs_0_, bf16[128,2048]{1,0:T(8,128)(2,1)S(1)} %get-tuple-element.37.refs_1_, f32[1,2048]{1,0:T(1,128)S(1)} %get-tuple-element.38.refs_2_, ...), custom_call_target="tpu_custom_call" | custom-call | flops 134217728 | bytes 3145728 | tf_op jit(solution)/shard_map/attend/pallas_call | solution.py:152
  17.3 2.7 %collective-permute-start.8 = (bf16[96,2048]{1,0:T(8,128)(2,1)S(1)}, bf16[96,2048]{1,0:T(8,128)(2,1)S(1)}, u32[]{:S(2)}, u32[]{:S(2)}) collective-permute-start(bf16[96,2048]{1,0:T(8,128)(2,1)S(1)} %get-tuple-element.46), channel_id=1, source_target_pairs={{0,8},{1,9},{2,10},{3,11},{4,12},{5,13},{6,14},{7,15},{8,0},{9,1},... | collective-permute-start | bytes 1179656 | tf_op jit(solution)/shard_map/ppermute | solution.py:396
  19.9 1.6 %collective-permute-start.3 = (bf16[96,2048]{1,0:T(8,128)(2,1)S(1)}, bf16[96,2048]{1,0:T(8,128)(2,1)S(1)}, u32[]{:S(2)}, u32[]{:S(2)}) collective-permute-start(bf16[96,2048]{1,0:T(8,128)(2,1)S(1)} %get-tuple-element.43.refs_0_.own_in.refs_2_), channel_id=1, source_target_pairs={{0,4},{1,5},{2,6},{3,7},{4,0},{5,1},{6,2},{7,3},{8,12},{9,13},{10,... | collective-permute-start | bytes 1179656 | tf_op jit(solution)/shard_map/ppermute | solution.py:392
  21.5 0.7 hold_weights.1
  22.3 1.6 %collective-permute-start.5 = (bf16[512,384]{1,0:T(8,128)(2,1)S(1)}, bf16[512,384]{1,0:T(8,128)(2,1)S(1)}, u32[]{:S(2)}, u32[]{:S(2)}) collective-permute-start(bf16[512,384]{1,0:T(8,128)(2,1)S(1)} %hand_on.16.refs_1_.refs_0_), channel_id=1, source_target_pairs={{0,16},{16,0},{1,17},{17,1},{2,18},{18,2},{3,19},{19,3},{4,20},{20... | collective-permute-start | bytes 1179656 | tf_op jit(solution)/shard_map/ppermute | solution.py:400
  23.8 1.6 %collective-permute-done.6.refs_0_ = bf16[512,384]{1,0:T(8,128)(2,1)S(1)} collective-permute-done((bf16[512,384]{1,0:T(8,128)(2,1)}, bf16[512,384]{1,0:T(8,128)(2,1)S(1)}, u32[]{:S(2)}, u32[]{:S(2)}) %collective-permute-start.6) | collective-permute-done | bytes 393248 | tf_op jit(solution)/shard_map/ppermute | solution.py:392
  25.8 1.7 %collective-permute-start.14 = (bf16[112,2048]{1,0:T(8,128)(2,1)S(1)}, bf16[112,2048]{1,0:T(8,128)(2,1)S(1)}, u32[]{:S(2)}, u32[]{:S(2)}) collective-permute-start(bf16[112,2048]{1,0:T(8,128)(2,1)S(1)} %get-tuple-element.53), channel_id=1, source_target_pairs={{0,2},{1,3},{2,0},{3,1},{4,6},{5,7},{6,4},{7,5},{8,10},{9,11},{10,... | collective-permute-start | bytes 1376264 | tf_op jit(solution)/shard_map/ppermute | solution.py:392
  27.5 9.2 %collective-permute-done.8.refs_0_ = bf16[96,2048]{1,0:T(8,128)(2,1)S(1)} collective-permute-done((bf16[96,2048]{1,0:T(8,128)(2,1)S(1)}, bf16[96,2048]{1,0:T(8,128)(2,1)S(1)}, u32[]{:S(2)}, u32[]{:S(2)}) %collective-permute-start.8) | collective-permute-done | bytes 393248 | tf_op jit(solution)/shard_map/ppermute | solution.py:396
  36.9 1.4 %collective-permute-start.9 = (bf16[96,2048]{1,0:T(8,128)(2,1)S(1)}, bf16[96,2048]{1,0:T(8,128)(2,1)S(1)}, u32[]{:S(2)}, u32[]{:S(2)}) collective-permute-start(bf16[96,2048]{1,0:T(8,128)(2,1)S(1)} %hand_on.19.own_in.refs_2_), channel_id=1, source_target_pairs={{0,4},{1,5},{2,6},{3,7},{4,0},{5,1},{6,2},{7,3},{8,12},{9,13},{10,... | collective-permute-start | bytes 1179656 | tf_op jit(solution)/shard_map/ppermute | solution.py:392
  38.4 0.5 collective-permute-start.16
  38.9 1.3 %collective-permute-done.7.refs_3_.refs_1_ = bf16[512,384]{1,0:T(8,128)(2,1)S(1)} collective-permute-done((bf16[512,384]{1,0:T(8,128)(2,1)S(1)}, bf16[512,384]{1,0:T(8,128)(2,1)S(1)}, u32[]{:S(2)}, u32[]{:S(2)}) %collective-permute-start.7) | collective-permute-done | bytes 393248 | tf_op jit(solution)/shard_map/ppermute | solution.py:400
  40.2 1.6 %collective-permute-start.15 = (bf16[112,2048]{1,0:T(8,128)(2,1)S(1)}, bf16[112,2048]{1,0:T(8,128)(2,1)S(1)}, u32[]{:S(2)}, u32[]{:S(2)}) collective-permute-start(bf16[112,2048]{1,0:T(8,128)(2,1)S(1)} %hand_on.26.refs_4_), channel_id=1, source_target_pairs={{0,16},{16,0},{1,17},{17,1},{2,18},{18,2},{3,19},{19,3},{4,20},{20... | collective-permute-start | bytes 1376264 | tf_op jit(solution)/shard_map/ppermute | solution.py:400
  41.7 4.9 %collective-permute-done.9.refs_4_.refs_0_ = bf16[96,2048]{1,0:T(8,128)(2,1)S(1)} collective-permute-done((bf16[96,2048]{1,0:T(8,128)(2,1)S(1)}, bf16[96,2048]{1,0:T(8,128)(2,1)S(1)}, u32[]{:S(2)}, u32[]{:S(2)}) %collective-permute-start.9) | collective-permute-done | bytes 393248 | tf_op jit(solution)/shard_map/ppermute | solution.py:392
  46.6 0.5 collective-permute-start.11
  47.2 1.2 %collective-permute-done.10.refs_8_ = bf16[512,384]{1,0:T(8,128)(2,1)S(1)} collective-permute-done((bf16[512,384]{1,0:T(8,128)(2,1)S(1)}, bf16[512,384]{1,0:T(8,128)(2,1)S(1)}, u32[]{:S(2)}, u32[]{:S(2)}) %collective-permute-start.10) | collective-permute-done | bytes 393248 | tf_op jit(solution)/shard_map/ppermute | solution.py:392
  48.5 0.4 collective-permute-done.11.refs_9_
  49.1 0.8 expert_up.3.refs_1_
  50.1 0.6 collective-permute-done.13.refs_11_
  50.7 0.9 expert_up_y.2.refs_2_.refs_1_
  51.5 2.2 %collective-permute-done.16.refs_1_ = bf16[160,2048]{1,0:T(8,128)(2,1)S(1)} collective-permute-done((bf16[160,2048]{1,0:T(8,128)(2,1)S(1)}, bf16[160,2048]{1,0:T(8,128)(2,1)S(1)}, u32[]{:S(2)}, u32[]{:S(2)}) %collective-permute-start.16) | collective-permute-done | bytes 655392 | tf_op jit(solution)/shard_map/ppermute | solution.py:392
  53.8 0.5 collective-permute-start.18
  54.3 0.8 expert_up.2.refs_1_
  55.1 1.4 %collective-permute-done.18.refs_7_ = bf16[112,2048]{1,0:T(8,128)(2,1)S(1)} collective-permute-done((bf16[112,2048]{1,0:T(8,128)(2,1)S(1)}, bf16[112,2048]{1,0:T(8,128)(2,1)S(1)}, u32[]{:S(2)}, u32[]{:S(2)}) %collective-permute-start.18) | collective-permute-done | bytes 458784 | tf_op jit(solution)/shard_map/ppermute | solution.py:392
  56.5 0.8 expert_down.3
  57.4 0.8 expert_down.4
  58.2 0.9 expert_up_y.3.refs_1_
  59.5 1.7 %collective-permute-start.22 = (bf16[96,1024]{1,0:T(8,128)(2,1)S(1)}, bf16[96,1024]{1,0:T(8,128)(2,1)S(1)}, u32[]{:S(2)}, u32[]{:S(2)}) collective-permute-start(bf16[96,1024]{1,0:T(8,128)(2,1)S(1)} %get-tuple-element.63), channel_id=1, source_target_pairs={{0,4},{1,5},{2,6},{3,7},{4,0},{5,1},{6,2},{7,3},{8,12},{9,13},{10,... | collective-permute-start | bytes 589832 | tf_op jit(solution)/shard_map/ppermute | solution.py:392
  61.2 1.5 %expert_down.5 = (bf16[96,2048]{1,0:T(8,128)(2,1)S(1)}, bf16[96,2048]{1,0:T(8,128)(2,1)S(1)}) custom-call(s32[1]{0:T(128)} %bitcast.10.pipe_ref.refs_0_, bf16[192,1536]{1,0:T(8,128)(2,1)S(1)} %expert_up_y.3.refs_1_, bf16[384,2048]{1,0:T(8,128)(2,1)S(1)} %get-tuple-element.51.refs_2_, bf16[384,2048]{1,0:T(8,128)(2,1)S(1)} %collective-permute-done.2.refs_7_.refs_3_, ...), custom_call_target="tpu_custom_call" | custom-call | flops 1207959552 | bytes 6291456 | tf_op jit(solution)/shard_map/expert_down/pallas_call | solution.py:319
  62.7 4.2 %collective-permute-done.20.z_ref = bf16[96,1024]{1,0:T(8,128)(2,1)S(1)} collective-permute-done((bf16[96,1024]{1,0:T(8,128)(2,1)S(1)}, bf16[96,1024]{1,0:T(8,128)(2,1)S(1)}, u32[]{:S(2)}, u32[]{:S(2)}) %collective-permute-start.20) | collective-permute-done | bytes 196640 | tf_op jit(solution)/shard_map/ppermute | solution.py:392
  67.0 3.4 %collective-permute-start.24 = (bf16[96,1024]{1,0:T(8,128)(2,1)S(1)}, bf16[96,1024]{1,0:T(8,128)(2,1)S(1)}, u32[]{:S(2)}, u32[]{:S(2)}) collective-permute-start(bf16[96,1024]{1,0:T(8,128)(2,1)S(1)} %get-tuple-element.64), channel_id=1, source_target_pairs={{0,8},{1,9},{2,10},{3,11},{4,12},{5,13},{6,14},{7,15},{8,0},{9,1},... | collective-permute-start | bytes 589832 | tf_op jit(solution)/shard_map/ppermute | solution.py:396
  70.4 2.9 %collective-permute-done.22.z_ref = bf16[96,1024]{1,0:T(8,128)(2,1)S(1)} collective-permute-done((bf16[96,1024]{1,0:T(8,128)(2,1)S(1)}, bf16[96,1024]{1,0:T(8,128)(2,1)S(1)}, u32[]{:S(2)}, u32[]{:S(2)}) %collective-permute-start.22) | collective-permute-done | bytes 196640 | tf_op jit(solution)/shard_map/ppermute | solution.py:392
  73.3 1.3 %collective-permute-start.23 = (bf16[96,1024]{1,0:T(8,128)(2,1)S(1)}, bf16[96,1024]{1,0:T(8,128)(2,1)S(1)}, u32[]{:S(2)}, u32[]{:S(2)}) collective-permute-start(bf16[96,1024]{1,0:T(8,128)(2,1)S(1)} %far_total.3), channel_id=1, source_target_pairs={{0,8},{1,9},{2,10},{3,11},{4,12},{5,13},{6,14},{7,15},{8,0},{9,1},... | collective-permute-start | bytes 589832 | tf_op jit(solution)/shard_map/ppermute | solution.py:396
  74.6 0.7 collective-permute-start.21
  75.3 8.0 %collective-permute-done.24.refs_1_ = bf16[96,1024]{1,0:T(8,128)(2,1)S(1)} collective-permute-done((bf16[96,1024]{1,0:T(8,128)(2,1)S(1)}, bf16[96,1024]{1,0:T(8,128)(2,1)S(1)}, u32[]{:S(2)}, u32[]{:S(2)}) %collective-permute-start.24) | collective-permute-done | bytes 196640 | tf_op jit(solution)/shard_map/ppermute | solution.py:396
  83.4 3.4 %collective-permute-done.23.refs_0_ = bf16[96,1024]{1,0:T(8,128)(2,1)S(1)} collective-permute-done((bf16[96,1024]{1,0:T(8,128)(2,1)S(1)}, bf16[96,1024]{1,0:T(8,128)(2,1)S(1)}, u32[]{:S(2)}, u32[]{:S(2)}) %collective-permute-start.23) | collective-permute-done | bytes 196640 | tf_op jit(solution)/shard_map/ppermute | solution.py:396
  86.8 2.1 %collective-permute-done.21.refs_4_ = bf16[96,2048]{1,0:T(8,128)(2,1)S(1)} collective-permute-done((bf16[96,2048]{1,0:T(8,128)(2,1)S(1)}, bf16[96,2048]{1,0:T(8,128)(2,1)S(1)}, u32[]{:S(2)}, u32[]{:S(2)}) %collective-permute-start.21) | collective-permute-done | bytes 393248 | tf_op jit(solution)/shard_map/ppermute | solution.py:392
  88.9 1.2 %finish.1 = bf16[128,2048]{1,0:T(8,128)(2,1)} custom-call(f32[128,2048]{1,0:T(8,128)S(1)} %get-tuple-element.40.refs_0_, f32[128,1]{1,0:T(8,128)S(1)} %get-tuple-element.41.refs_1_, s32[128,1]{1,0:T(8,128)S(1)} %get-tuple-element.42.refs_2_, bf16[96,2048]{1,0:T(8,128)(2,1)S(1)} %get-tuple-element.59.refs_3_, ...), custom_call_target="tpu_custom_call" | custom-call | flops 201326592 | bytes 4194304 | tf_op jit(solution)/shard_map/finish/pallas_call | solution.py:374
  (51 shorter events, 1.8 us)
Async XLA Ops:
  0.0 2.3 %copy-start.8 = (bf16[1,32,2,2048]{3,2,1,0:T(2,128)(2,1)S(1)}, bf16[1,32,2,2048]{3,2,1,0:T(2,128)(2,1)}, u32[]{:S(2)}) copy-start(bf16[1,32,2,2048]{3,2,1,0:T(2,128)(2,1)} %param.11) | copy-start | bytes 786436
  0.0 14.6 %collective-permute-start.2 = (bf16[384,2048]{1,0:T(8,128)(2,1)}, bf16[384,2048]{1,0:T(8,128)(2,1)S(1)}, u32[]{:S(2)}, u32[]{:S(2)}) collective-permute-start(bf16[384,2048]{1,0:T(8,128)(2,1)} %w_out.1), channel_id=1, source_target_pairs={{0,1},{1,0},{2,3},{3,2},{4,5},{5,4},{6,7},{7,6},{8,9},{9,8},{10,11... | collective-permute-start | bytes 4718600 | tf_op jit(solution)/shard_map/ppermute | solution.py:392
  0.5 14.2 %collective-permute-start.1 = (bf16[2048,384]{1,0:T(8,128)(2,1)}, bf16[2048,384]{1,0:T(8,128)(2,1)S(1)}, u32[]{:S(2)}, u32[]{:S(2)}) collective-permute-start(bf16[2048,384]{1,0:T(8,128)(2,1)} %whole.3), channel_id=1, source_target_pairs={{0,1},{1,0},{2,3},{3,2},{4,5},{5,4},{6,7},{7,6},{8,9},{9,8},{10,11... | collective-permute-start | bytes 4718600 | tf_op jit(solution)/shard_map/ppermute | solution.py:392
  3.1 6.2 %copy-start.4 = (f32[2048]{0:T(1024)S(1)}, f32[2048]{0:T(1024)}, u32[]{:S(2)}) copy-start(f32[2048]{0:T(1024)} %param.12) | copy-start | bytes 24580
  3.1 6.2 %copy-start.5 = (s32[1,1,128]{2,1,0:T(1,128)S(1)}, s32[1,1,128]{2,1,0:T(1,128)}, u32[]{:S(2)}) copy-start(s32[1,1,128]{2,1,0:T(1,128)} %param.15) | copy-start | bytes 1540
  3.1 6.2 %copy-start.6 = (s32[1,1,128]{2,1,0:T(1,128)S(1)}, s32[1,1,128]{2,1,0:T(1,128)}, u32[]{:S(2)}) copy-start(s32[1,1,128]{2,1,0:T(1,128)} %param.16) | copy-start | bytes 1540
  3.1 9.8 %collective-permute-start = (bf16[64,2048]{1,0:T(8,128)(2,1)}, bf16[64,2048]{1,0:T(8,128)(2,1)}, u32[]{:S(2)}, u32[]{:S(2)}) collective-permute-start(bf16[64,2048]{1,0:T(8,128)(2,1)} %hand_on.15.refs_4_), channel_id=1, source_target_pairs={{0,16},{16,0},{1,17},{17,1},{2,18},{18,2},{3,19},{19,3},{4,20},{20... | collective-permute-start | bytes 786440 | tf_op jit(solution)/shard_map/ppermute | solution.py:415
  6.0 16.2 %collective-permute-start.4 = (bf16[512,384]{1,0:T(8,128)(2,1)}, bf16[512,384]{1,0:T(8,128)(2,1)S(1)}, u32[]{:S(2)}, u32[]{:S(2)}) collective-permute-start(bf16[512,384]{1,0:T(8,128)(2,1)} %weight_part.2.refs_1_), channel_id=1, source_target_pairs={{0,2},{1,3},{2,0},{3,1},{4,6},{5,7},{6,4},{7,5},{8,10},{9,11},{10,... | collective-permute-start | bytes 1179656 | tf_op jit(solution)/shard_map/ppermute | solution.py:392
  9.3 1.0 %copy-start.2 = (bf16[1,1,128,2048]{3,2,1,0:T(8,128)(2,1)S(1)}, bf16[1,1,128,2048]{3,2,1,0:T(8,128)(2,1)}, u32[]{:S(2)}) copy-start(bf16[1,1,128,2048]{3,2,1,0:T(8,128)(2,1)} %param.9) | copy-start | bytes 1572868
  10.4 1.0 %copy-start.3 = (bf16[1,1,128,2048]{3,2,1,0:T(8,128)(2,1)S(1)}, bf16[1,1,128,2048]{3,2,1,0:T(8,128)(2,1)}, u32[]{:S(2)}) copy-start(bf16[1,1,128,2048]{3,2,1,0:T(8,128)(2,1)} %param.10) | copy-start | bytes 1572868
  11.4 0.7 copy-start.7
  12.9 12.6 %collective-permute-start.6 = (bf16[512,384]{1,0:T(8,128)(2,1)}, bf16[512,384]{1,0:T(8,128)(2,1)S(1)}, u32[]{:S(2)}, u32[]{:S(2)}) collective-permute-start(bf16[512,384]{1,0:T(8,128)(2,1)} %hand_on.17), channel_id=1, source_target_pairs={{0,2},{1,3},{2,0},{3,1},{4,6},{5,7},{6,4},{7,5},{8,10},{9,11},{10,... | collective-permute-start | bytes 1179656 | tf_op jit(solution)/shard_map/ppermute | solution.py:392
  14.7 6.9 %copy-start = (bf16[2048,384]{1,0:T(8,128)(2,1)S(1)}, bf16[2048,384]{1,0:T(8,128)(2,1)}, u32[]{:S(2)}) copy-start(bf16[2048,384]{1,0:T(8,128)(2,1)} %whole.3) | copy-start | bytes 4718596
  14.7 6.9 %copy-start.1 = (bf16[384,2048]{1,0:T(8,128)(2,1)S(1)}, bf16[384,2048]{1,0:T(8,128)(2,1)}, u32[]{:S(2)}) copy-start(bf16[384,2048]{1,0:T(8,128)(2,1)} %w_out.1) | copy-start | bytes 4718596
  17.3 19.5 %collective-permute-start.8 = (bf16[96,2048]{1,0:T(8,128)(2,1)S(1)}, bf16[96,2048]{1,0:T(8,128)(2,1)S(1)}, u32[]{:S(2)}, u32[]{:S(2)}) collective-permute-start(bf16[96,2048]{1,0:T(8,128)(2,1)S(1)} %get-tuple-element.46), channel_id=1, source_target_pairs={{0,8},{1,9},{2,10},{3,11},{4,12},{5,13},{6,14},{7,15},{8,0},{9,1},... | collective-permute-start | bytes 1179656 | tf_op jit(solution)/shard_map/ppermute | solution.py:396
  19.9 17.0 %collective-permute-start.3 = (bf16[96,2048]{1,0:T(8,128)(2,1)S(1)}, bf16[96,2048]{1,0:T(8,128)(2,1)S(1)}, u32[]{:S(2)}, u32[]{:S(2)}) collective-permute-start(bf16[96,2048]{1,0:T(8,128)(2,1)S(1)} %get-tuple-element.43.refs_0_.own_in.refs_2_), channel_id=1, source_target_pairs={{0,4},{1,5},{2,6},{3,7},{4,0},{5,1},{6,2},{7,3},{8,12},{9,13},{10,... | collective-permute-start | bytes 1179656 | tf_op jit(solution)/shard_map/ppermute | solution.py:392
  22.3 19.5 %collective-permute-start.5 = (bf16[512,384]{1,0:T(8,128)(2,1)S(1)}, bf16[512,384]{1,0:T(8,128)(2,1)S(1)}, u32[]{:S(2)}, u32[]{:S(2)}) collective-permute-start(bf16[512,384]{1,0:T(8,128)(2,1)S(1)} %hand_on.16.refs_1_.refs_0_), channel_id=1, source_target_pairs={{0,16},{16,0},{1,17},{17,1},{2,18},{18,2},{3,19},{19,3},{4,20},{20... | collective-permute-start | bytes 1179656 | tf_op jit(solution)/shard_map/ppermute | solution.py:400
  25.5 14.7 %collective-permute-start.7 = (bf16[512,384]{1,0:T(8,128)(2,1)S(1)}, bf16[512,384]{1,0:T(8,128)(2,1)S(1)}, u32[]{:S(2)}, u32[]{:S(2)}) collective-permute-start(bf16[512,384]{1,0:T(8,128)(2,1)S(1)} %hand_on.18.refs_2_), channel_id=1, source_target_pairs={{0,16},{16,0},{1,17},{17,1},{2,18},{18,2},{3,19},{19,3},{4,20},{20... | collective-permute-start | bytes 1179656 | tf_op jit(solution)/shard_map/ppermute | solution.py:400
  25.8 14.4 %collective-permute-start.14 = (bf16[112,2048]{1,0:T(8,128)(2,1)S(1)}, bf16[112,2048]{1,0:T(8,128)(2,1)S(1)}, u32[]{:S(2)}, u32[]{:S(2)}) collective-permute-start(bf16[112,2048]{1,0:T(8,128)(2,1)S(1)} %get-tuple-element.53), channel_id=1, source_target_pairs={{0,2},{1,3},{2,0},{3,1},{4,6},{5,7},{6,4},{7,5},{8,10},{9,11},{10,... | collective-permute-start | bytes 1376264 | tf_op jit(solution)/shard_map/ppermute | solution.py:392
  36.9 9.7 %collective-permute-start.9 = (bf16[96,2048]{1,0:T(8,128)(2,1)S(1)}, bf16[96,2048]{1,0:T(8,128)(2,1)S(1)}, u32[]{:S(2)}, u32[]{:S(2)}) collective-permute-start(bf16[96,2048]{1,0:T(8,128)(2,1)S(1)} %hand_on.19.own_in.refs_2_), channel_id=1, source_target_pairs={{0,4},{1,5},{2,6},{3,7},{4,0},{5,1},{6,2},{7,3},{8,12},{9,13},{10,... | collective-permute-start | bytes 1179656 | tf_op jit(solution)/shard_map/ppermute | solution.py:392
  38.4 15.3 %collective-permute-start.16 = (bf16[160,2048]{1,0:T(8,128)(2,1)S(1)}, bf16[160,2048]{1,0:T(8,128)(2,1)S(1)}, u32[]{:S(2)}, u32[]{:S(2)}) collective-permute-start(bf16[160,2048]{1,0:T(8,128)(2,1)S(1)} %get-tuple-element.54), channel_id=1, source_target_pairs={{0,2},{1,3},{2,0},{3,1},{4,6},{5,7},{6,4},{7,5},{8,10},{9,11},{10,... | collective-permute-start | bytes 1966088 | tf_op jit(solution)/shard_map/ppermute | solution.py:392
  40.2 13.5 %collective-permute-start.17 = (bf16[112,2048]{1,0:T(8,128)(2,1)S(1)}, bf16[112,2048]{1,0:T(8,128)(2,1)S(1)}, u32[]{:S(2)}, u32[]{:S(2)}) collective-permute-start(bf16[112,2048]{1,0:T(8,128)(2,1)S(1)} %hand_on.26.refs_4_), channel_id=1, source_target_pairs={{0,1},{1,0},{2,3},{3,2},{4,5},{5,4},{6,7},{7,6},{8,9},{9,8},{10,11... | collective-permute-start | bytes 1376264 | tf_op jit(solution)/shard_map/ppermute | solution.py:392
  40.2 13.5 %collective-permute-start.15 = (bf16[112,2048]{1,0:T(8,128)(2,1)S(1)}, bf16[112,2048]{1,0:T(8,128)(2,1)S(1)}, u32[]{:S(2)}, u32[]{:S(2)}) collective-permute-start(bf16[112,2048]{1,0:T(8,128)(2,1)S(1)} %hand_on.26.refs_4_), channel_id=1, source_target_pairs={{0,16},{16,0},{1,17},{17,1},{2,18},{18,2},{3,19},{19,3},{4,20},{20... | collective-permute-start | bytes 1376264 | tf_op jit(solution)/shard_map/ppermute | solution.py:400
  46.6 1.7 %collective-permute-start.10 = (bf16[512,384]{1,0:T(8,128)(2,1)S(1)}, bf16[512,384]{1,0:T(8,128)(2,1)S(1)}, u32[]{:S(2)}, u32[]{:S(2)}) collective-permute-start(bf16[512,384]{1,0:T(8,128)(2,1)S(1)} %get-tuple-element.47.refs_4_), channel_id=1, source_target_pairs={{0,1},{1,0},{2,3},{3,2},{4,5},{5,4},{6,7},{7,6},{8,9},{9,8},{10,11... | collective-permute-start | bytes 1179656 | tf_op jit(solution)/shard_map/ppermute | solution.py:392
  46.6 2.3 %collective-permute-start.11 = (bf16[512,384]{1,0:T(8,128)(2,1)S(1)}, bf16[512,384]{1,0:T(8,128)(2,1)S(1)}, u32[]{:S(2)}, u32[]{:S(2)}) collective-permute-start(bf16[512,384]{1,0:T(8,128)(2,1)S(1)} %get-tuple-element.48.refs_5_), channel_id=1, source_target_pairs={{0,1},{1,0},{2,3},{3,2},{4,5},{5,4},{6,7},{7,6},{8,9},{9,8},{10,11... | collective-permute-start | bytes 1179656 | tf_op jit(solution)/shard_map/ppermute | solution.py:392
  48.4 1.7 %collective-permute-start.12 = (bf16[512,384]{1,0:T(8,128)(2,1)S(1)}, bf16[512,384]{1,0:T(8,128)(2,1)S(1)}, u32[]{:S(2)}, u32[]{:S(2)}) collective-permute-start(bf16[512,384]{1,0:T(8,128)(2,1)S(1)} %get-tuple-element.49.refs_6_), channel_id=1, source_target_pairs={{0,1},{1,0},{2,3},{3,2},{4,5},{5,4},{6,7},{7,6},{8,9},{9,8},{10,11... | collective-permute-start | bytes 1179656 | tf_op jit(solution)/shard_map/ppermute | solution.py:392
  48.9 1.7 %collective-permute-start.13 = (bf16[512,384]{1,0:T(8,128)(2,1)S(1)}, bf16[512,384]{1,0:T(8,128)(2,1)S(1)}, u32[]{:S(2)}, u32[]{:S(2)}) collective-permute-start(bf16[512,384]{1,0:T(8,128)(2,1)S(1)} %get-tuple-element.50.refs_7_), channel_id=1, source_target_pairs={{0,1},{1,0},{2,3},{3,2},{4,5},{5,4},{6,7},{7,6},{8,9},{9,8},{10,11... | collective-permute-start | bytes 1179656 | tf_op jit(solution)/shard_map/ppermute | solution.py:392
  53.7 2.8 %collective-permute-start.19 = (bf16[160,2048]{1,0:T(8,128)(2,1)S(1)}, bf16[160,2048]{1,0:T(8,128)(2,1)S(1)}, u32[]{:S(2)}, u32[]{:S(2)}) collective-permute-start(bf16[160,2048]{1,0:T(8,128)(2,1)S(1)} %get-tuple-element.56.refs_8_), channel_id=1, source_target_pairs={{0,1},{1,0},{2,3},{3,2},{4,5},{5,4},{6,7},{7,6},{8,9},{9,8},{10,11... | collective-permute-start | bytes 1966088 | tf_op jit(solution)/shard_map/ppermute | solution.py:392
  53.8 2.7 %collective-permute-start.18 = (bf16[112,2048]{1,0:T(8,128)(2,1)S(1)}, bf16[112,2048]{1,0:T(8,128)(2,1)S(1)}, u32[]{:S(2)}, u32[]{:S(2)}) collective-permute-start(bf16[112,2048]{1,0:T(8,128)(2,1)S(1)} %get-tuple-element.55.refs_5_), channel_id=1, source_target_pairs={{0,1},{1,0},{2,3},{3,2},{4,5},{5,4},{6,7},{7,6},{8,9},{9,8},{10,11... | collective-permute-start | bytes 1376264 | tf_op jit(solution)/shard_map/ppermute | solution.py:392
  59.1 7.8 %collective-permute-start.20 = (bf16[96,1024]{1,0:T(8,128)(2,1)S(1)}, bf16[96,1024]{1,0:T(8,128)(2,1)S(1)}, u32[]{:S(2)}, u32[]{:S(2)}) collective-permute-start(bf16[96,1024]{1,0:T(8,128)(2,1)S(1)} %hand_on.28), channel_id=1, source_target_pairs={{0,4},{1,5},{2,6},{3,7},{4,0},{5,1},{6,2},{7,3},{8,12},{9,13},{10,... | collective-permute-start | bytes 589832 | tf_op jit(solution)/shard_map/ppermute | solution.py:392
  59.5 13.8 %collective-permute-start.22 = (bf16[96,1024]{1,0:T(8,128)(2,1)S(1)}, bf16[96,1024]{1,0:T(8,128)(2,1)S(1)}, u32[]{:S(2)}, u32[]{:S(2)}) collective-permute-start(bf16[96,1024]{1,0:T(8,128)(2,1)S(1)} %get-tuple-element.63), channel_id=1, source_target_pairs={{0,4},{1,5},{2,6},{3,7},{4,0},{5,1},{6,2},{7,3},{8,12},{9,13},{10,... | collective-permute-start | bytes 589832 | tf_op jit(solution)/shard_map/ppermute | solution.py:392
  67.0 16.4 %collective-permute-start.24 = (bf16[96,1024]{1,0:T(8,128)(2,1)S(1)}, bf16[96,1024]{1,0:T(8,128)(2,1)S(1)}, u32[]{:S(2)}, u32[]{:S(2)}) collective-permute-start(bf16[96,1024]{1,0:T(8,128)(2,1)S(1)} %get-tuple-element.64), channel_id=1, source_target_pairs={{0,8},{1,9},{2,10},{3,11},{4,12},{5,13},{6,14},{7,15},{8,0},{9,1},... | collective-permute-start | bytes 589832 | tf_op jit(solution)/shard_map/ppermute | solution.py:396
  73.3 13.5 %collective-permute-start.23 = (bf16[96,1024]{1,0:T(8,128)(2,1)S(1)}, bf16[96,1024]{1,0:T(8,128)(2,1)S(1)}, u32[]{:S(2)}, u32[]{:S(2)}) collective-permute-start(bf16[96,1024]{1,0:T(8,128)(2,1)S(1)} %far_total.3), channel_id=1, source_target_pairs={{0,8},{1,9},{2,10},{3,11},{4,12},{5,13},{6,14},{7,15},{8,0},{9,1},... | collective-permute-start | bytes 589832 | tf_op jit(solution)/shard_map/ppermute | solution.py:396
  74.6 14.3 %collective-permute-start.21 = (bf16[96,2048]{1,0:T(8,128)(2,1)S(1)}, bf16[96,2048]{1,0:T(8,128)(2,1)S(1)}, u32[]{:S(2)}, u32[]{:S(2)}) collective-permute-start(bf16[96,2048]{1,0:T(8,128)(2,1)S(1)} %get-tuple-element.62), channel_id=1, source_target_pairs={{0,4},{1,5},{2,6},{3,7},{4,0},{5,1},{6,2},{7,3},{8,12},{9,13},{10,... | collective-permute-start | bytes 1179656 | tf_op jit(solution)/shard_map/ppermute | solution.py:392

commit v14 on v13

--- a/solution.py
+++ b/solution.py
@@ -16,7 +16,8 @@
 FAR_STEPS = 4
 CROSS_STEPS = 1
 CROSS_WEIGHT = 3_000_000_000
-BACK_WEIGHT = 10_000_000_000
+SUM_WEIGHT = 1_000_000_000
+BACK_WEIGHT = 3_000_000_000
 VMEM_LIMIT = 32 * 1024 * 1024
 PART_LIMIT = 60 * 1024 * 1024
 
@@ -485,7 +486,8 @@
         for count in range(1, groups)
         for side in (sum_a, sum_b)
     ]
-    backs = after_all(backs, [], BACK_WEIGHT)
+    backs[::2] = after_all(backs[::2], [], SUM_WEIGHT)
+    backs[::2] = after_all(backs[::2], [], BACK_WEIGHT)
     near_sums = [near_own, across(near_sent, 4)]
     output = finish(hidden, gates, flat, near_sums, backs, groups, cap)
     return output.reshape(1, 1, tokens, width)

time: 90.3 us -> 87.3 us (0.967)
  waiting for transfers between devices: 44.5 us -> 41.3 us
    ppermute x18, waiting for transfers between devices: 21.9 us -> 19.6 us  [across(): return lax.ppermute(value, 'expert', [(i, i ^ bit) for i in range(devices)])]
  transfers between devices with their start and end apart: 25 -> 25, of which waited for: 17 -> 17; matrix products, arithmetic and copies ran while one was open for 1% -> 1% of each run, Pallas kernels for 12% -> 15%
where the time goes in v14:
time: 87.3 us; the launch traced here: 86.6 us
  waiting for transfers between devices  41.3 us (47%)
  starting transfers between devices  26.8 us (31%)
  Pallas kernels  14.7 us (17%)
  local copies, waits for them, and re-layouts  3.56 us (4%)
    ppermute x3, waiting for transfers between devices, groups_on(): lax.ppermute(value, 'expert', [(i, (i + shift) % devices) for i in range(...  19.8 us
    ppermute x18, waiting for transfers between devices, across(): return lax.ppermute(value, 'expert', [(i, i ^ bit) for i in range(devices)])  19.6 us
    ppermute x18, starting transfers between devices, across(): return lax.ppermute(value, 'expert', [(i, i ^ bit) for i in range(devices)])  12.6 us
    ppermute x3, starting transfers between devices, groups_on(): lax.ppermute(value, 'expert', [(i, (i + shift) % devices) for i in range(...  7.77 us
    pallas_call x2, Pallas kernels, cut_part(): call(functools.partial(part_kernel, stride, first), struct((size, whole.s...  3.49 us
    ppermute x3, starting transfers between devices, along(): return [value] + [lax.ppermute(value, 'pipe', perm) for perm in perms]  3.46 us
    pallas_call x3, Pallas kernels, down(): call(functools.partial(down_kernel, pipes, first), [struct((rows, width))...  3.19 us
    ppermute x1, starting transfers between devices, body(): kv_pieces.append(lax.ppermute(kv, 'pipe', perm))  2.93 us
  transfers between devices with their start and end apart: 25, of which 17 were waited for; matrix products, arithmetic and copies ran while one was open for 1% of the time, Pallas kernels for 15%

profile of v14, /device:TPU:0, one launch (start us, length us, event | category | flops | bytes accessed | tf_op | source)
XLA Modules:
  0.0 86.6 jit_solution(12824094342543805301)
XLA Ops:
  0.0 0.5 collective-permute-start.2
  0.5 1.7 %weight_part.2.refs_1_ = bf16[512,384]{1,0:T(8,128)(2,1)} custom-call(s32[1]{0:T(128)} %bitcast.10.pipe_ref.refs_0_, bf16[2048,384]{1,0:T(8,128)(2,1)} %whole.3), custom_call_target="tpu_custom_call" | custom-call | flops 1 | bytes 786432 | tf_op jit(solution)/shard_map/weight_part/pallas_call | solution.py:178
  2.3 0.8 copy.32
  3.1 2.9 %collective-permute-start = (bf16[64,2048]{1,0:T(8,128)(2,1)}, bf16[64,2048]{1,0:T(8,128)(2,1)}, u32[]{:S(2)}, u32[]{:S(2)}) collective-permute-start(bf16[64,2048]{1,0:T(8,128)(2,1)} %hand_on.16.refs_4_), channel_id=1, source_target_pairs={{0,16},{16,0},{1,17},{17,1},{2,18},{18,2},{3,19},{19,3},{4,20},{20... | collective-permute-start | bytes 786440 | tf_op jit(solution)/shard_map/ppermute | solution.py:416
  6.0 1.5 %collective-permute-start.4 = (bf16[512,384]{1,0:T(8,128)(2,1)}, bf16[512,384]{1,0:T(8,128)(2,1)S(1)}, u32[]{:S(2)}, u32[]{:S(2)}) collective-permute-start(bf16[512,384]{1,0:T(8,128)(2,1)} %weight_part.2.refs_1_), channel_id=1, source_target_pairs={{0,2},{1,3},{2,0},{3,1},{4,6},{5,7},{6,4},{7,5},{8,10},{9,11},{10,... | collective-permute-start | bytes 1179656 | tf_op jit(solution)/shard_map/ppermute | solution.py:393
  7.6 1.7 %weight_part.3.refs_0_ = bf16[512,384]{1,0:T(8,128)(2,1)} custom-call(s32[1]{0:T(128)} %bitcast.10.pipe_ref.refs_0_, bf16[2048,384]{1,0:T(8,128)(2,1)} %whole.3), custom_call_target="tpu_custom_call" | custom-call | flops 1 | bytes 786432 | tf_op jit(solution)/shard_map/weight_part/pallas_call | solution.py:178
  9.4 1.0 %copy-done.2 = bf16[1,1,128,2048]{3,2,1,0:T(8,128)(2,1)S(1)} copy-done((bf16[1,1,128,2048]{3,2,1,0:T(8,128)(2,1)S(1)}, bf16[1,1,128,2048]{3,2,1,0:T(8,128)(2,1)}, u32[]{:S(2)}) %copy-start.2) | copy-done | bytes 524312
  10.4 1.0 %copy-done.3 = bf16[1,1,128,2048]{3,2,1,0:T(8,128)(2,1)S(1)} copy-done((bf16[1,1,128,2048]{3,2,1,0:T(8,128)(2,1)S(1)}, bf16[1,1,128,2048]{3,2,1,0:T(8,128)(2,1)}, u32[]{:S(2)}) %copy-start.3) | copy-done | bytes 524312
  11.4 0.7 copy-done.7
  12.2 0.7 collective-permute-done.refs_5_.refs_1_
  12.9 1.8 %collective-permute-start.6 = (bf16[512,384]{1,0:T(8,128)(2,1)}, bf16[512,384]{1,0:T(8,128)(2,1)S(1)}, u32[]{:S(2)}, u32[]{:S(2)}) collective-permute-start(bf16[512,384]{1,0:T(8,128)(2,1)} %hand_on.18), channel_id=1, source_target_pairs={{0,2},{1,3},{2,0},{3,1},{4,6},{5,7},{6,4},{7,5},{8,10},{9,11},{10,... | collective-permute-start | bytes 1179656 | tf_op jit(solution)/shard_map/ppermute | solution.py:393
  14.7 2.6 %attend.1 = (f32[128,2048]{1,0:T(8,128)S(1)}, bf16[96,2048]{1,0:T(8,128)(2,1)S(1)}, bf16[96,2048]{1,0:T(8,128)(2,1)S(1)}) custom-call(bf16[128,2048]{1,0:T(8,128)(2,1)S(1)} %get-tuple-element.34.refs_0_, bf16[128,2048]{1,0:T(8,128)(2,1)S(1)} %get-tuple-element.35.refs_1_, f32[1,2048]{1,0:T(1,128)S(1)} %get-tuple-element.36.refs_2_, ...), custom_call_target="tpu_custom_call" | custom-call | flops 134217728 | bytes 3145728 | tf_op jit(solution)/shard_map/attend/pallas_call | solution.py:153
  17.3 2.7 %collective-permute-start.8 = (bf16[96,2048]{1,0:T(8,128)(2,1)S(1)}, bf16[96,2048]{1,0:T(8,128)(2,1)S(1)}, u32[]{:S(2)}, u32[]{:S(2)}) collective-permute-start(bf16[96,2048]{1,0:T(8,128)(2,1)S(1)} %get-tuple-element.44), channel_id=1, source_target_pairs={{0,8},{1,9},{2,10},{3,11},{4,12},{5,13},{6,14},{7,15},{8,0},{9,1},... | collective-permute-start | bytes 1179656 | tf_op jit(solution)/shard_map/ppermute | solution.py:397
  19.9 1.6 %collective-permute-start.3 = (bf16[96,2048]{1,0:T(8,128)(2,1)S(1)}, bf16[96,2048]{1,0:T(8,128)(2,1)S(1)}, u32[]{:S(2)}, u32[]{:S(2)}) collective-permute-start(bf16[96,2048]{1,0:T(8,128)(2,1)S(1)} %get-tuple-element.41.refs_0_.own_in.refs_2_), channel_id=1, source_target_pairs={{0,4},{1,5},{2,6},{3,7},{4,0},{5,1},{6,2},{7,3},{8,12},{9,13},{10,... | collective-permute-start | bytes 1179656 | tf_op jit(solution)/shard_map/ppermute | solution.py:393
  21.5 0.7 hold_weights.1
  22.3 1.6 %collective-permute-start.5 = (bf16[512,384]{1,0:T(8,128)(2,1)S(1)}, bf16[512,384]{1,0:T(8,128)(2,1)S(1)}, u32[]{:S(2)}, u32[]{:S(2)}) collective-permute-start(bf16[512,384]{1,0:T(8,128)(2,1)S(1)} %hand_on.17.refs_1_.refs_0_), channel_id=1, source_target_pairs={{0,16},{16,0},{1,17},{17,1},{2,18},{18,2},{3,19},{19,3},{4,20},{20... | collective-permute-start | bytes 1179656 | tf_op jit(solution)/shard_map/ppermute | solution.py:401
  23.8 1.6 %collective-permute-done.6.refs_0_ = bf16[512,384]{1,0:T(8,128)(2,1)S(1)} collective-permute-done((bf16[512,384]{1,0:T(8,128)(2,1)}, bf16[512,384]{1,0:T(8,128)(2,1)S(1)}, u32[]{:S(2)}, u32[]{:S(2)}) %collective-permute-start.6) | collective-permute-done | bytes 393248 | tf_op jit(solution)/shard_map/ppermute | solution.py:393
  25.8 1.7 %collective-permute-start.14 = (bf16[112,2048]{1,0:T(8,128)(2,1)S(1)}, bf16[112,2048]{1,0:T(8,128)(2,1)S(1)}, u32[]{:S(2)}, u32[]{:S(2)}) collective-permute-start(bf16[112,2048]{1,0:T(8,128)(2,1)S(1)} %get-tuple-element.51), channel_id=1, source_target_pairs={{0,2},{1,3},{2,0},{3,1},{4,6},{5,7},{6,4},{7,5},{8,10},{9,11},{10,... | collective-permute-start | bytes 1376264 | tf_op jit(solution)/shard_map/ppermute | solution.py:393
  27.5 9.2 %collective-permute-done.8.refs_0_ = bf16[96,2048]{1,0:T(8,128)(2,1)S(1)} collective-permute-done((bf16[96,2048]{1,0:T(8,128)(2,1)S(1)}, bf16[96,2048]{1,0:T(8,128)(2,1)S(1)}, u32[]{:S(2)}, u32[]{:S(2)}) %collective-permute-start.8) | collective-permute-done | bytes 393248 | tf_op jit(solution)/shard_map/ppermute | solution.py:397
  36.9 1.4 %collective-permute-start.9 = (bf16[96,2048]{1,0:T(8,128)(2,1)S(1)}, bf16[96,2048]{1,0:T(8,128)(2,1)S(1)}, u32[]{:S(2)}, u32[]{:S(2)}) collective-permute-start(bf16[96,2048]{1,0:T(8,128)(2,1)S(1)} %hand_on.20.own_in.refs_2_), channel_id=1, source_target_pairs={{0,4},{1,5},{2,6},{3,7},{4,0},{5,1},{6,2},{7,3},{8,12},{9,13},{10,... | collective-permute-start | bytes 1179656 | tf_op jit(solution)/shard_map/ppermute | solution.py:393
  38.4 0.5 collective-permute-start.16
  38.9 1.3 %collective-permute-done.7.refs_3_.refs_1_ = bf16[512,384]{1,0:T(8,128)(2,1)S(1)} collective-permute-done((bf16[512,384]{1,0:T(8,128)(2,1)S(1)}, bf16[512,384]{1,0:T(8,128)(2,1)S(1)}, u32[]{:S(2)}, u32[]{:S(2)}) %collective-permute-start.7) | collective-permute-done | bytes 393248 | tf_op jit(solution)/shard_map/ppermute | solution.py:401
  40.2 1.6 %collective-permute-start.15 = (bf16[112,2048]{1,0:T(8,128)(2,1)S(1)}, bf16[112,2048]{1,0:T(8,128)(2,1)S(1)}, u32[]{:S(2)}, u32[]{:S(2)}) collective-permute-start(bf16[112,2048]{1,0:T(8,128)(2,1)S(1)} %hand_on.27.refs_4_), channel_id=1, source_target_pairs={{0,16},{16,0},{1,17},{17,1},{2,18},{18,2},{3,19},{19,3},{4,20},{20... | collective-permute-start | bytes 1376264 | tf_op jit(solution)/shard_map/ppermute | solution.py:401
  41.7 4.9 %collective-permute-done.9.refs_4_.refs_0_ = bf16[96,2048]{1,0:T(8,128)(2,1)S(1)} collective-permute-done((bf16[96,2048]{1,0:T(8,128)(2,1)S(1)}, bf16[96,2048]{1,0:T(8,128)(2,1)S(1)}, u32[]{:S(2)}, u32[]{:S(2)}) %collective-permute-start.9) | collective-permute-done | bytes 393248 | tf_op jit(solution)/shard_map/ppermute | solution.py:393
  46.7 0.5 collective-permute-start.11
  47.2 1.2 %collective-permute-done.10.refs_8_ = bf16[512,384]{1,0:T(8,128)(2,1)S(1)} collective-permute-done((bf16[512,384]{1,0:T(8,128)(2,1)S(1)}, bf16[512,384]{1,0:T(8,128)(2,1)S(1)}, u32[]{:S(2)}, u32[]{:S(2)}) %collective-permute-start.10) | collective-permute-done | bytes 393248 | tf_op jit(solution)/shard_map/ppermute | solution.py:393
  48.5 0.4 collective-permute-done.11.refs_9_
  49.1 0.8 expert_up.3.refs_1_
  50.1 0.6 collective-permute-done.13.refs_11_
  50.7 0.9 expert_up_y.2.refs_2_.refs_1_
  51.5 2.2 %collective-permute-done.16.refs_1_ = bf16[160,2048]{1,0:T(8,128)(2,1)S(1)} collective-permute-done((bf16[160,2048]{1,0:T(8,128)(2,1)S(1)}, bf16[160,2048]{1,0:T(8,128)(2,1)S(1)}, u32[]{:S(2)}, u32[]{:S(2)}) %collective-permute-start.16) | collective-permute-done | bytes 655392 | tf_op jit(solution)/shard_map/ppermute | solution.py:393
  53.8 0.5 collective-permute-start.18
  54.3 2.2 %collective-permute-done.18.refs_7_ = bf16[112,2048]{1,0:T(8,128)(2,1)S(1)} collective-permute-done((bf16[112,2048]{1,0:T(8,128)(2,1)S(1)}, bf16[112,2048]{1,0:T(8,128)(2,1)S(1)}, u32[]{:S(2)}, u32[]{:S(2)}) %collective-permute-start.18) | collective-permute-done | bytes 458784 | tf_op jit(solution)/shard_map/ppermute | solution.py:393
  56.5 0.8 expert_down.3
  57.4 0.4 collective-permute-start.22
  57.7 0.8 expert_up.2.refs_1_
  58.6 0.8 expert_down.4
  59.4 0.9 %expert_up_y.3.refs_1_ = bf16[192,1536]{1,0:T(8,128)(2,1)S(1)} custom-call(s32[1]{0:T(128)} %bitcast.10.pipe_ref.refs_0_, bf16[192,768]{1,0:T(8,128)(2,1)S(1)} %expert_up.2.refs_1_, bf16[96,2048]{1,0:T(8,128)(2,1)S(1)} %get-tuple-element.41.refs_0_.own_in.refs_2_, bf16[96,2048]{1,0:T(8,128)(2,1)S(1)} %collective-permute-done.3.z_in.refs_1_.refs_3_, ...), custom_call_target="tpu_custom_call" | custom-call | flops 603979776 | bytes 3145728 | tf_op jit(solution)/shard_map/expert_up_y/pallas_call | solution.py:277
  60.3 1.8 %collective-permute-start.20 = (bf16[96,1024]{1,0:T(8,128)(2,1)S(1)}, bf16[96,1024]{1,0:T(8,128)(2,1)S(1)}, u32[]{:S(2)}, u32[]{:S(2)}) collective-permute-start(bf16[96,1024]{1,0:T(8,128)(2,1)S(1)} %hand_on.29), channel_id=1, source_target_pairs={{0,4},{1,5},{2,6},{3,7},{4,0},{5,1},{6,2},{7,3},{8,12},{9,13},{10,... | collective-permute-start | bytes 589832 | tf_op jit(solution)/shard_map/ppermute | solution.py:393
  62.1 3.1 %collective-permute-done.22.z_ref = bf16[96,1024]{1,0:T(8,128)(2,1)S(1)} collective-permute-done((bf16[96,1024]{1,0:T(8,128)(2,1)S(1)}, bf16[96,1024]{1,0:T(8,128)(2,1)S(1)}, u32[]{:S(2)}, u32[]{:S(2)}) %collective-permute-start.22) | collective-permute-done | bytes 196640 | tf_op jit(solution)/shard_map/ppermute | solution.py:393
  65.2 3.4 %collective-permute-start.23 = (bf16[96,1024]{1,0:T(8,128)(2,1)S(1)}, bf16[96,1024]{1,0:T(8,128)(2,1)S(1)}, u32[]{:S(2)}, u32[]{:S(2)}) collective-permute-start(bf16[96,1024]{1,0:T(8,128)(2,1)S(1)} %far_total.3), channel_id=1, source_target_pairs={{0,8},{1,9},{2,10},{3,11},{4,12},{5,13},{6,14},{7,15},{8,0},{9,1},... | collective-permute-start | bytes 589832 | tf_op jit(solution)/shard_map/ppermute | solution.py:397
  68.7 1.5 %expert_down.5 = (bf16[96,2048]{1,0:T(8,128)(2,1)S(1)}, bf16[96,2048]{1,0:T(8,128)(2,1)S(1)}) custom-call(s32[1]{0:T(128)} %bitcast.10.pipe_ref.refs_0_, bf16[192,1536]{1,0:T(8,128)(2,1)S(1)} %expert_up_y.3.refs_1_, bf16[384,2048]{1,0:T(8,128)(2,1)S(1)} %get-tuple-element.49.refs_2_, bf16[384,2048]{1,0:T(8,128)(2,1)S(1)} %collective-permute-done.2.refs_7_.refs_3_, ...), custom_call_target="tpu_custom_call" | custom-call | flops 1207959552 | bytes 6291456 | tf_op jit(solution)/shard_map/expert_down/pallas_call | solution.py:320
  70.2 1.6 %collective-permute-done.20.z_ref = bf16[96,1024]{1,0:T(8,128)(2,1)S(1)} collective-permute-done((bf16[96,1024]{1,0:T(8,128)(2,1)S(1)}, bf16[96,1024]{1,0:T(8,128)(2,1)S(1)}, u32[]{:S(2)}, u32[]{:S(2)}) %collective-permute-start.20) | collective-permute-done | bytes 196640 | tf_op jit(solution)/shard_map/ppermute | solution.py:393
  71.9 1.7 %collective-permute-start.24 = (bf16[96,1024]{1,0:T(8,128)(2,1)S(1)}, bf16[96,1024]{1,0:T(8,128)(2,1)S(1)}, u32[]{:S(2)}, u32[]{:S(2)}) collective-permute-start(bf16[96,1024]{1,0:T(8,128)(2,1)S(1)} %get-tuple-element.62), channel_id=1, source_target_pairs={{0,8},{1,9},{2,10},{3,11},{4,12},{5,13},{6,14},{7,15},{8,0},{9,1},... | collective-permute-start | bytes 589832 | tf_op jit(solution)/shard_map/ppermute | solution.py:397
  73.6 3.8 %collective-permute-done.23.refs_0_ = bf16[96,1024]{1,0:T(8,128)(2,1)S(1)} collective-permute-done((bf16[96,1024]{1,0:T(8,128)(2,1)S(1)}, bf16[96,1024]{1,0:T(8,128)(2,1)S(1)}, u32[]{:S(2)}, u32[]{:S(2)}) %collective-permute-start.23) | collective-permute-done | bytes 196640 | tf_op jit(solution)/shard_map/ppermute | solution.py:397
  77.4 6.8 %collective-permute-done.24.refs_6_ = bf16[96,1024]{1,0:T(8,128)(2,1)S(1)} collective-permute-done((bf16[96,1024]{1,0:T(8,128)(2,1)S(1)}, bf16[96,1024]{1,0:T(8,128)(2,1)S(1)}, u32[]{:S(2)}, u32[]{:S(2)}) %collective-permute-start.24) | collective-permute-done | bytes 196640 | tf_op jit(solution)/shard_map/ppermute | solution.py:397
  84.2 1.3 %collective-permute-done.21.refs_4_ = bf16[96,2048]{1,0:T(8,128)(2,1)S(1)} collective-permute-done((bf16[96,2048]{1,0:T(8,128)(2,1)S(1)}, bf16[96,2048]{1,0:T(8,128)(2,1)S(1)}, u32[]{:S(2)}, u32[]{:S(2)}) %collective-permute-start.21) | collective-permute-done | bytes 393248 | tf_op jit(solution)/shard_map/ppermute | solution.py:393
  85.4 1.2 %finish.1 = bf16[128,2048]{1,0:T(8,128)(2,1)} custom-call(f32[128,2048]{1,0:T(8,128)S(1)} %get-tuple-element.38.refs_0_, f32[128,1]{1,0:T(8,128)S(1)} %get-tuple-element.39.refs_1_, s32[128,1]{1,0:T(8,128)S(1)} %get-tuple-element.40.refs_2_, bf16[96,2048]{1,0:T(8,128)(2,1)S(1)} %get-tuple-element.57.refs_3_, ...), custom_call_target="tpu_custom_call" | custom-call | flops 201326592 | bytes 4194304 | tf_op jit(solution)/shard_map/finish/pallas_call | solution.py:375
  (52 shorter events, 1.5 us)
Async XLA Ops:
  0.0 2.3 %copy-start.8 = (bf16[1,32,2,2048]{3,2,1,0:T(2,128)(2,1)S(1)}, bf16[1,32,2,2048]{3,2,1,0:T(2,128)(2,1)}, u32[]{:S(2)}) copy-start(bf16[1,32,2,2048]{3,2,1,0:T(2,128)(2,1)} %param.11) | copy-start | bytes 786436
  0.0 14.7 %collective-permute-start.2 = (bf16[384,2048]{1,0:T(8,128)(2,1)}, bf16[384,2048]{1,0:T(8,128)(2,1)S(1)}, u32[]{:S(2)}, u32[]{:S(2)}) collective-permute-start(bf16[384,2048]{1,0:T(8,128)(2,1)} %w_out.1), channel_id=1, source_target_pairs={{0,1},{1,0},{2,3},{3,2},{4,5},{5,4},{6,7},{7,6},{8,9},{9,8},{10,11... | collective-permute-start | bytes 4718600 | tf_op jit(solution)/shard_map/ppermute | solution.py:393
  0.5 14.2 %collective-permute-start.1 = (bf16[2048,384]{1,0:T(8,128)(2,1)}, bf16[2048,384]{1,0:T(8,128)(2,1)S(1)}, u32[]{:S(2)}, u32[]{:S(2)}) collective-permute-start(bf16[2048,384]{1,0:T(8,128)(2,1)} %whole.3), channel_id=1, source_target_pairs={{0,1},{1,0},{2,3},{3,2},{4,5},{5,4},{6,7},{7,6},{8,9},{9,8},{10,11... | collective-permute-start | bytes 4718600 | tf_op jit(solution)/shard_map/ppermute | solution.py:393
  3.1 6.2 %copy-start.4 = (f32[2048]{0:T(1024)S(1)}, f32[2048]{0:T(1024)}, u32[]{:S(2)}) copy-start(f32[2048]{0:T(1024)} %param.12) | copy-start | bytes 24580
  3.1 6.2 %copy-start.5 = (s32[1,1,128]{2,1,0:T(1,128)S(1)}, s32[1,1,128]{2,1,0:T(1,128)}, u32[]{:S(2)}) copy-start(s32[1,1,128]{2,1,0:T(1,128)} %param.15) | copy-start | bytes 1540
  3.1 6.2 %copy-start.6 = (s32[1,1,128]{2,1,0:T(1,128)S(1)}, s32[1,1,128]{2,1,0:T(1,128)}, u32[]{:S(2)}) copy-start(s32[1,1,128]{2,1,0:T(1,128)} %param.16) | copy-start | bytes 1540
  3.1 9.8 %collective-permute-start = (bf16[64,2048]{1,0:T(8,128)(2,1)}, bf16[64,2048]{1,0:T(8,128)(2,1)}, u32[]{:S(2)}, u32[]{:S(2)}) collective-permute-start(bf16[64,2048]{1,0:T(8,128)(2,1)} %hand_on.16.refs_4_), channel_id=1, source_target_pairs={{0,16},{16,0},{1,17},{17,1},{2,18},{18,2},{3,19},{19,3},{4,20},{20... | collective-permute-start | bytes 786440 | tf_op jit(solution)/shard_map/ppermute | solution.py:416
  6.0 16.2 %collective-permute-start.4 = (bf16[512,384]{1,0:T(8,128)(2,1)}, bf16[512,384]{1,0:T(8,128)(2,1)S(1)}, u32[]{:S(2)}, u32[]{:S(2)}) collective-permute-start(bf16[512,384]{1,0:T(8,128)(2,1)} %weight_part.2.refs_1_), channel_id=1, source_target_pairs={{0,2},{1,3},{2,0},{3,1},{4,6},{5,7},{6,4},{7,5},{8,10},{9,11},{10,... | collective-permute-start | bytes 1179656 | tf_op jit(solution)/shard_map/ppermute | solution.py:393
  9.3 1.0 %copy-start.2 = (bf16[1,1,128,2048]{3,2,1,0:T(8,128)(2,1)S(1)}, bf16[1,1,128,2048]{3,2,1,0:T(8,128)(2,1)}, u32[]{:S(2)}) copy-start(bf16[1,1,128,2048]{3,2,1,0:T(8,128)(2,1)} %param.9) | copy-start | bytes 1572868
  10.4 1.0 %copy-start.3 = (bf16[1,1,128,2048]{3,2,1,0:T(8,128)(2,1)S(1)}, bf16[1,1,128,2048]{3,2,1,0:T(8,128)(2,1)}, u32[]{:S(2)}) copy-start(bf16[1,1,128,2048]{3,2,1,0:T(8,128)(2,1)} %param.10) | copy-start | bytes 1572868
  11.4 0.7 copy-start.7
  12.9 12.6 %collective-permute-start.6 = (bf16[512,384]{1,0:T(8,128)(2,1)}, bf16[512,384]{1,0:T(8,128)(2,1)S(1)}, u32[]{:S(2)}, u32[]{:S(2)}) collective-permute-start(bf16[512,384]{1,0:T(8,128)(2,1)} %hand_on.18), channel_id=1, source_target_pairs={{0,2},{1,3},{2,0},{3,1},{4,6},{5,7},{6,4},{7,5},{8,10},{9,11},{10,... | collective-permute-start | bytes 1179656 | tf_op jit(solution)/shard_map/ppermute | solution.py:393
  14.7 6.9 %copy-start = (bf16[2048,384]{1,0:T(8,128)(2,1)S(1)}, bf16[2048,384]{1,0:T(8,128)(2,1)}, u32[]{:S(2)}) copy-start(bf16[2048,384]{1,0:T(8,128)(2,1)} %whole.3) | copy-start | bytes 4718596
  14.7 6.9 %copy-start.1 = (bf16[384,2048]{1,0:T(8,128)(2,1)S(1)}, bf16[384,2048]{1,0:T(8,128)(2,1)}, u32[]{:S(2)}) copy-start(bf16[384,2048]{1,0:T(8,128)(2,1)} %w_out.1) | copy-start | bytes 4718596
  17.3 19.5 %collective-permute-start.8 = (bf16[96,2048]{1,0:T(8,128)(2,1)S(1)}, bf16[96,2048]{1,0:T(8,128)(2,1)S(1)}, u32[]{:S(2)}, u32[]{:S(2)}) collective-permute-start(bf16[96,2048]{1,0:T(8,128)(2,1)S(1)} %get-tuple-element.44), channel_id=1, source_target_pairs={{0,8},{1,9},{2,10},{3,11},{4,12},{5,13},{6,14},{7,15},{8,0},{9,1},... | collective-permute-start | bytes 1179656 | tf_op jit(solution)/shard_map/ppermute | solution.py:397
  19.9 17.0 %collective-permute-start.3 = (bf16[96,2048]{1,0:T(8,128)(2,1)S(1)}, bf16[96,2048]{1,0:T(8,128)(2,1)S(1)}, u32[]{:S(2)}, u32[]{:S(2)}) collective-permute-start(bf16[96,2048]{1,0:T(8,128)(2,1)S(1)} %get-tuple-element.41.refs_0_.own_in.refs_2_), channel_id=1, source_target_pairs={{0,4},{1,5},{2,6},{3,7},{4,0},{5,1},{6,2},{7,3},{8,12},{9,13},{10,... | collective-permute-start | bytes 1179656 | tf_op jit(solution)/shard_map/ppermute | solution.py:393
  22.3 19.5 %collective-permute-start.5 = (bf16[512,384]{1,0:T(8,128)(2,1)S(1)}, bf16[512,384]{1,0:T(8,128)(2,1)S(1)}, u32[]{:S(2)}, u32[]{:S(2)}) collective-permute-start(bf16[512,384]{1,0:T(8,128)(2,1)S(1)} %hand_on.17.refs_1_.refs_0_), channel_id=1, source_target_pairs={{0,16},{16,0},{1,17},{17,1},{2,18},{18,2},{3,19},{19,3},{4,20},{20... | collective-permute-start | bytes 1179656 | tf_op jit(solution)/shard_map/ppermute | solution.py:401
  25.5 14.7 %collective-permute-start.7 = (bf16[512,384]{1,0:T(8,128)(2,1)S(1)}, bf16[512,384]{1,0:T(8,128)(2,1)S(1)}, u32[]{:S(2)}, u32[]{:S(2)}) collective-permute-start(bf16[512,384]{1,0:T(8,128)(2,1)S(1)} %hand_on.19.refs_2_), channel_id=1, source_target_pairs={{0,16},{16,0},{1,17},{17,1},{2,18},{18,2},{3,19},{19,3},{4,20},{20... | collective-permute-start | bytes 1179656 | tf_op jit(solution)/shard_map/ppermute | solution.py:401
  25.8 14.4 %collective-permute-start.14 = (bf16[112,2048]{1,0:T(8,128)(2,1)S(1)}, bf16[112,2048]{1,0:T(8,128)(2,1)S(1)}, u32[]{:S(2)}, u32[]{:S(2)}) collective-permute-start(bf16[112,2048]{1,0:T(8,128)(2,1)S(1)} %get-tuple-element.51), channel_id=1, source_target_pairs={{0,2},{1,3},{2,0},{3,1},{4,6},{5,7},{6,4},{7,5},{8,10},{9,11},{10,... | collective-permute-start | bytes 1376264 | tf_op jit(solution)/shard_map/ppermute | solution.py:393
  36.9 9.7 %collective-permute-start.9 = (bf16[96,2048]{1,0:T(8,128)(2,1)S(1)}, bf16[96,2048]{1,0:T(8,128)(2,1)S(1)}, u32[]{:S(2)}, u32[]{:S(2)}) collective-permute-start(bf16[96,2048]{1,0:T(8,128)(2,1)S(1)} %hand_on.20.own_in.refs_2_), channel_id=1, source_target_pairs={{0,4},{1,5},{2,6},{3,7},{4,0},{5,1},{6,2},{7,3},{8,12},{9,13},{10,... | collective-permute-start | bytes 1179656 | tf_op jit(solution)/shard_map/ppermute | solution.py:393
  38.4 15.3 %collective-permute-start.16 = (bf16[160,2048]{1,0:T(8,128)(2,1)S(1)}, bf16[160,2048]{1,0:T(8,128)(2,1)S(1)}, u32[]{:S(2)}, u32[]{:S(2)}) collective-permute-start(bf16[160,2048]{1,0:T(8,128)(2,1)S(1)} %get-tuple-element.52), channel_id=1, source_target_pairs={{0,2},{1,3},{2,0},{3,1},{4,6},{5,7},{6,4},{7,5},{8,10},{9,11},{10,... | collective-permute-start | bytes 1966088 | tf_op jit(solution)/shard_map/ppermute | solution.py:393
  40.2 13.5 %collective-permute-start.17 = (bf16[112,2048]{1,0:T(8,128)(2,1)S(1)}, bf16[112,2048]{1,0:T(8,128)(2,1)S(1)}, u32[]{:S(2)}, u32[]{:S(2)}) collective-permute-start(bf16[112,2048]{1,0:T(8,128)(2,1)S(1)} %hand_on.27.refs_4_), channel_id=1, source_target_pairs={{0,1},{1,0},{2,3},{3,2},{4,5},{5,4},{6,7},{7,6},{8,9},{9,8},{10,11... | collective-permute-start | bytes 1376264 | tf_op jit(solution)/shard_map/ppermute | solution.py:393
  40.2 13.5 %collective-permute-start.15 = (bf16[112,2048]{1,0:T(8,128)(2,1)S(1)}, bf16[112,2048]{1,0:T(8,128)(2,1)S(1)}, u32[]{:S(2)}, u32[]{:S(2)}) collective-permute-start(bf16[112,2048]{1,0:T(8,128)(2,1)S(1)} %hand_on.27.refs_4_), channel_id=1, source_target_pairs={{0,16},{16,0},{1,17},{17,1},{2,18},{18,2},{3,19},{19,3},{4,20},{20... | collective-permute-start | bytes 1376264 | tf_op jit(solution)/shard_map/ppermute | solution.py:401
  46.7 1.7 %collective-permute-start.10 = (bf16[512,384]{1,0:T(8,128)(2,1)S(1)}, bf16[512,384]{1,0:T(8,128)(2,1)S(1)}, u32[]{:S(2)}, u32[]{:S(2)}) collective-permute-start(bf16[512,384]{1,0:T(8,128)(2,1)S(1)} %get-tuple-element.45.refs_4_), channel_id=1, source_target_pairs={{0,1},{1,0},{2,3},{3,2},{4,5},{5,4},{6,7},{7,6},{8,9},{9,8},{10,11... | collective-permute-start | bytes 1179656 | tf_op jit(solution)/shard_map/ppermute | solution.py:393
  46.7 2.3 %collective-permute-start.11 = (bf16[512,384]{1,0:T(8,128)(2,1)S(1)}, bf16[512,384]{1,0:T(8,128)(2,1)S(1)}, u32[]{:S(2)}, u32[]{:S(2)}) collective-permute-start(bf16[512,384]{1,0:T(8,128)(2,1)S(1)} %get-tuple-element.46.refs_5_), channel_id=1, source_target_pairs={{0,1},{1,0},{2,3},{3,2},{4,5},{5,4},{6,7},{7,6},{8,9},{9,8},{10,11... | collective-permute-start | bytes 1179656 | tf_op jit(solution)/shard_map/ppermute | solution.py:393
  48.4 1.7 %collective-permute-start.12 = (bf16[512,384]{1,0:T(8,128)(2,1)S(1)}, bf16[512,384]{1,0:T(8,128)(2,1)S(1)}, u32[]{:S(2)}, u32[]{:S(2)}) collective-permute-start(bf16[512,384]{1,0:T(8,128)(2,1)S(1)} %get-tuple-element.47.refs_6_), channel_id=1, source_target_pairs={{0,1},{1,0},{2,3},{3,2},{4,5},{5,4},{6,7},{7,6},{8,9},{9,8},{10,11... | collective-permute-start | bytes 1179656 | tf_op jit(solution)/shard_map/ppermute | solution.py:393
  48.9 1.7 %collective-permute-start.13 = (bf16[512,384]{1,0:T(8,128)(2,1)S(1)}, bf16[512,384]{1,0:T(8,128)(2,1)S(1)}, u32[]{:S(2)}, u32[]{:S(2)}) collective-permute-start(bf16[512,384]{1,0:T(8,128)(2,1)S(1)} %get-tuple-element.48.refs_7_), channel_id=1, source_target_pairs={{0,1},{1,0},{2,3},{3,2},{4,5},{5,4},{6,7},{7,6},{8,9},{9,8},{10,11... | collective-permute-start | bytes 1179656 | tf_op jit(solution)/shard_map/ppermute | solution.py:393
  53.7 2.8 %collective-permute-start.19 = (bf16[160,2048]{1,0:T(8,128)(2,1)S(1)}, bf16[160,2048]{1,0:T(8,128)(2,1)S(1)}, u32[]{:S(2)}, u32[]{:S(2)}) collective-permute-start(bf16[160,2048]{1,0:T(8,128)(2,1)S(1)} %get-tuple-element.54.refs_8_), channel_id=1, source_target_pairs={{0,1},{1,0},{2,3},{3,2},{4,5},{5,4},{6,7},{7,6},{8,9},{9,8},{10,11... | collective-permute-start | bytes 1966088 | tf_op jit(solution)/shard_map/ppermute | solution.py:393
  53.8 2.7 %collective-permute-start.18 = (bf16[112,2048]{1,0:T(8,128)(2,1)S(1)}, bf16[112,2048]{1,0:T(8,128)(2,1)S(1)}, u32[]{:S(2)}, u32[]{:S(2)}) collective-permute-start(bf16[112,2048]{1,0:T(8,128)(2,1)S(1)} %get-tuple-element.53.refs_5_), channel_id=1, source_target_pairs={{0,1},{1,0},{2,3},{3,2},{4,5},{5,4},{6,7},{7,6},{8,9},{9,8},{10,11... | collective-permute-start | bytes 1376264 | tf_op jit(solution)/shard_map/ppermute | solution.py:393
  57.4 7.8 %collective-permute-start.22 = (bf16[96,1024]{1,0:T(8,128)(2,1)S(1)}, bf16[96,1024]{1,0:T(8,128)(2,1)S(1)}, u32[]{:S(2)}, u32[]{:S(2)}) collective-permute-start(bf16[96,1024]{1,0:T(8,128)(2,1)S(1)} %get-tuple-element.61), channel_id=1, source_target_pairs={{0,4},{1,5},{2,6},{3,7},{4,0},{5,1},{6,2},{7,3},{8,12},{9,13},{10,... | collective-permute-start | bytes 589832 | tf_op jit(solution)/shard_map/ppermute | solution.py:393
  60.3 11.5 %collective-permute-start.20 = (bf16[96,1024]{1,0:T(8,128)(2,1)S(1)}, bf16[96,1024]{1,0:T(8,128)(2,1)S(1)}, u32[]{:S(2)}, u32[]{:S(2)}) collective-permute-start(bf16[96,1024]{1,0:T(8,128)(2,1)S(1)} %hand_on.29), channel_id=1, source_target_pairs={{0,4},{1,5},{2,6},{3,7},{4,0},{5,1},{6,2},{7,3},{8,12},{9,13},{10,... | collective-permute-start | bytes 589832 | tf_op jit(solution)/shard_map/ppermute | solution.py:393
  65.2 12.2 %collective-permute-start.23 = (bf16[96,1024]{1,0:T(8,128)(2,1)S(1)}, bf16[96,1024]{1,0:T(8,128)(2,1)S(1)}, u32[]{:S(2)}, u32[]{:S(2)}) collective-permute-start(bf16[96,1024]{1,0:T(8,128)(2,1)S(1)} %far_total.3), channel_id=1, source_target_pairs={{0,8},{1,9},{2,10},{3,11},{4,12},{5,13},{6,14},{7,15},{8,0},{9,1},... | collective-permute-start | bytes 589832 | tf_op jit(solution)/shard_map/ppermute | solution.py:397
  71.9 13.6 %collective-permute-start.21 = (bf16[96,2048]{1,0:T(8,128)(2,1)S(1)}, bf16[96,2048]{1,0:T(8,128)(2,1)S(1)}, u32[]{:S(2)}, u32[]{:S(2)}) collective-permute-start(bf16[96,2048]{1,0:T(8,128)(2,1)S(1)} %get-tuple-element.60), channel_id=1, source_target_pairs={{0,4},{1,5},{2,6},{3,7},{4,0},{5,1},{6,2},{7,3},{8,12},{9,13},{10,... | collective-permute-start | bytes 1179656 | tf_op jit(solution)/shard_map/ppermute | solution.py:393
  71.9 12.2 %collective-permute-start.24 = (bf16[96,1024]{1,0:T(8,128)(2,1)S(1)}, bf16[96,1024]{1,0:T(8,128)(2,1)S(1)}, u32[]{:S(2)}, u32[]{:S(2)}) collective-permute-start(bf16[96,1024]{1,0:T(8,128)(2,1)S(1)} %get-tuple-element.62), channel_id=1, source_target_pairs={{0,8},{1,9},{2,10},{3,11},{4,12},{5,13},{6,14},{7,15},{8,0},{9,1},... | collective-permute-start | bytes 589832 | tf_op jit(solution)/shard_map/ppermute | solution.py:397

commit v15 on v14

--- a/solution.py
+++ b/solution.py
@@ -16,6 +16,7 @@
 FAR_STEPS = 4
 CROSS_STEPS = 1
 CROSS_WEIGHT = 3_000_000_000
+FIRST_WEIGHT = 8_000_000_000
 SUM_WEIGHT = 1_000_000_000
 BACK_WEIGHT = 3_000_000_000
 VMEM_LIMIT = 32 * 1024 * 1024
@@ -407,7 +408,8 @@
     w_in_pair, w_out_pair = across(w_in, 1), across(w_out, 1)
     pipe = pipe.reshape(1)
     depth = width // pipes
-    in_y, in_late = (cut_part(pipe, w_in, depth, at, depth // 2) for at in (0, depth // 2))
+    in_y = lax.dynamic_slice_in_dim(w_in, pipe[0] * depth, depth // 2, 0)
+    in_late = cut_part(pipe, w_in, depth, depth // 2, depth // 2)
     kv = jnp.transpose(enc_kv[0], (1, 0, 2)).reshape(-1, width)
     (kv,) = after_all([kv], [in_y])
     kv_pieces = [kv]
@@ -437,7 +439,7 @@
     far = jnp.concatenate(far, axis=0) if len(far) > 1 else far[0]
 
     w_in_held, w_out_held, out_part, out_rest = hold(pipe, w_in, w_out, pipes, [near])
-    in_first = along(*after_all([in_y], [out_part]))
+    in_first = along(*after_all([in_y], [out_part], FIRST_WEIGHT))
     in_last = after_all([in_late], [in_first[0]])
     out_part, out_rest = after_all([out_part, out_rest], in_last)
     in_last = along(*in_last)

time: 87.3 us -> 90.5 us (1.037)
  local copies, waits for them, and re-layouts: 3.56 us -> 8.02 us
  waiting for transfers between devices: 41.3 us -> 43.8 us
  Pallas kernels: 14.7 us -> 12.8 us
  starting transfers between devices: 26.8 us -> 25.3 us
    ppermute x3, waiting for transfers between devices: 19.8 us -> 23.1 us  [groups_on(): lax.ppermute(value, 'expert', [(i, (i + shift) % devices) for i in range(...]
    ppermute x18, waiting for transfers between devices: 19.6 us -> 17.5 us  [across(): return lax.ppermute(value, 'expert', [(i, i ^ bit) for i in range(devices)])]
    dynamic_slice x0 -> x1, local copies, waits for them, and re-layouts: none -> 1.78 us  [body(): in_y = lax.dynamic_slice_in_dim(w_in, pipe[0] * depth, depth // 2, 0)]
    pallas_call x2 -> x1, Pallas kernels: 3.49 us -> 1.75 us  [cut_part(): call(functools.partial(part_kernel, stride, first), struct((size, whole.s...]
    unnamed x18 -> x20, local copies, waits for them, and re-layouts: 2.76 us -> 4.49 us
    ppermute x1, waiting for transfers between devices: 0.66 us -> 2.08 us  [body(): kv_pieces.append(lax.ppermute(kv, 'pipe', perm))]
    ppermute x1, starting transfers between devices: 2.93 us -> 1.55 us  [body(): kv_pieces.append(lax.ppermute(kv, 'pipe', perm))]
    ppermute x18, starting transfers between devices: 12.6 us -> 11.2 us  [across(): return lax.ppermute(value, 'expert', [(i, i ^ bit) for i in range(devices)])]
  transfers between devices with their start and end apart: 25 -> 25, of which waited for: 17 -> 16; matrix products, arithmetic and copies ran while one was open for 1% -> 4% of each run, Pallas kernels for 15% -> 12%
where the time goes in v15:
time: 90.5 us; the launch traced here: 90.1 us
  waiting for transfers between devices  43.8 us (48%)
  starting transfers between devices  25.3 us (28%)
  Pallas kernels  12.8 us (14%)
  local copies, waits for them, and re-layouts  8.02 us (9%)
    ppermute x3, waiting for transfers between devices, groups_on(): lax.ppermute(value, 'expert', [(i, (i + shift) % devices) for i in range(...  23.1 us
    ppermute x18, waiting for transfers between devices, across(): return lax.ppermute(value, 'expert', [(i, i ^ bit) for i in range(devices)])  17.5 us
    ppermute x18, starting transfers between devices, across(): return lax.ppermute(value, 'expert', [(i, i ^ bit) for i in range(devices)])  11.2 us
    ppermute x3, starting transfers between devices, groups_on(): lax.ppermute(value, 'expert', [(i, (i + shift) % devices) for i in range(...  8.01 us
    ppermute x3, starting transfers between devices, along(): return [value] + [lax.ppermute(value, 'pipe', perm) for perm in perms]  4.54 us
    unnamed x20, local copies, waits for them, and re-layouts  4.49 us
    pallas_call x3, Pallas kernels, down(): call(functools.partial(down_kernel, pipes, first), [struct((rows, width))...  3.07 us
    pallas_call x1, Pallas kernels, attend(): call(functools.partial(attend_kernel, pieces, groups, cap), outs, [VMEM]...  2.6 us
  transfers between devices with their start and end apart: 25, of which 16 were waited for; matrix products, arithmetic and copies ran while one was open for 4% of the time, Pallas kernels for 12%

profile of v15, /device:TPU:0, one launch (start us, length us, event | category | flops | bytes accessed | tf_op | source)
XLA Modules:
  0.0 90.1 jit_solution(15236562299813746773)
XLA Ops:
  0.0 0.5 collective-permute-start.2
  0.5 1.8 %constant_dynamic-slice_fusion.refs_1_ = bf16[512,384]{1,0:T(8,128)(2,1)} fusion(bf16[2048,384]{1,0:T(8,128)(2,1)} %whole.1, s32[]{:T(128)S(6)} %select_n.9), kind=kLoop, calls=%fused_computation | loop fusion | bytes 786436 | tf_op jit(solution)/shard_map/dynamic_slice | solution.py:411
  2.3 3.0 %collective-permute-start.4 = (bf16[512,384]{1,0:T(8,128)(2,1)}, bf16[512,384]{1,0:T(8,128)(2,1)S(1)}, u32[]{:S(2)}, u32[]{:S(2)}) collective-permute-start(bf16[512,384]{1,0:T(8,128)(2,1)} %constant_dynamic-slice_fusion.refs_1_), channel_id=1, source_target_pairs={{0,2},{1,3},{2,0},{3,1},{4,6},{5,7},{6,4},{7,5},{8,10},{9,11},{10,... | collective-permute-start | bytes 1179656 | tf_op jit(solution)/shard_map/ppermute | solution.py:394
  5.3 1.8 %copy.32 = bf16[2,32,2048]{2,1,0:T(8,128)(2,1)} copy(bf16[2,32,2048]{2,0,1:T(2,128)(2,1)} %bitcast.19) | data formatting | bytes 524288 | tf_op jit(solution)/shard_map/transpose | solution.py:413
  7.0 1.6 %collective-permute-start = (bf16[64,2048]{1,0:T(8,128)(2,1)}, bf16[64,2048]{1,0:T(8,128)(2,1)}, u32[]{:S(2)}, u32[]{:S(2)}) collective-permute-start(bf16[64,2048]{1,0:T(8,128)(2,1)} %hand_on.16.refs_4_), channel_id=1, source_target_pairs={{0,16},{16,0},{1,17},{17,1},{2,18},{18,2},{3,19},{19,3},{4,20},{20... | collective-permute-start | bytes 786440 | tf_op jit(solution)/shard_map/ppermute | solution.py:418
  8.6 1.7 %weight_part.1.refs_0_ = bf16[512,384]{1,0:T(8,128)(2,1)} custom-call(s32[1]{0:T(128)} %bitcast.10.pipe_ref.refs_0_, bf16[2048,384]{1,0:T(8,128)(2,1)} %whole.1), custom_call_target="tpu_custom_call" | custom-call | flops 1 | bytes 786432 | tf_op jit(solution)/shard_map/weight_part/pallas_call | solution.py:179
  10.4 1.0 %copy-done.4 = bf16[1,1,128,2048]{3,2,1,0:T(8,128)(2,1)S(1)} copy-done((bf16[1,1,128,2048]{3,2,1,0:T(8,128)(2,1)S(1)}, bf16[1,1,128,2048]{3,2,1,0:T(8,128)(2,1)}, u32[]{:S(2)}) %copy-start.4) | copy-done | bytes 524312
  11.4 1.0 %copy-done.5 = bf16[1,1,128,2048]{3,2,1,0:T(8,128)(2,1)S(1)} copy-done((bf16[1,1,128,2048]{3,2,1,0:T(8,128)(2,1)S(1)}, bf16[1,1,128,2048]{3,2,1,0:T(8,128)(2,1)}, u32[]{:S(2)}) %copy-start.5) | copy-done | bytes 524312
  12.5 0.7 copy-done.9
  13.2 2.1 %collective-permute-done.refs_5_.refs_1_ = bf16[64,2048]{1,0:T(8,128)(2,1)} collective-permute-done((bf16[64,2048]{1,0:T(8,128)(2,1)}, bf16[64,2048]{1,0:T(8,128)(2,1)}, u32[]{:S(2)}, u32[]{:S(2)}) %collective-permute-start) | collective-permute-done | bytes 262176 | tf_op jit(solution)/shard_map/ppermute | solution.py:418
  15.3 1.0 %copy-done.2 = bf16[512,384]{1,0:T(8,128)(2,1)S(1)} copy-done((bf16[512,384]{1,0:T(8,128)(2,1)S(1)}, bf16[512,384]{1,0:T(8,128)(2,1)}, u32[]{:S(2)}) %copy-start.2) | copy-done | bytes 393240
  16.3 0.7 copy-done.3
  17.4 2.6 %attend.1 = (f32[128,2048]{1,0:T(8,128)S(1)}, bf16[96,2048]{1,0:T(8,128)(2,1)S(1)}, bf16[96,2048]{1,0:T(8,128)(2,1)S(1)}) custom-call(bf16[128,2048]{1,0:T(8,128)(2,1)S(1)} %get-tuple-element.34.refs_0_, bf16[128,2048]{1,0:T(8,128)(2,1)S(1)} %get-tuple-element.35.refs_1_, f32[1,2048]{1,0:T(1,128)S(1)} %get-tuple-element.36.refs_2_, ...), custom_call_target="tpu_custom_call" | custom-call | flops 134217728 | bytes 3145728 | tf_op jit(solution)/shard_map/attend/pallas_call | solution.py:154
  20.0 1.9 %collective-permute-start.3 = (bf16[96,2048]{1,0:T(8,128)(2,1)S(1)}, bf16[96,2048]{1,0:T(8,128)(2,1)S(1)}, u32[]{:S(2)}, u32[]{:S(2)}) collective-permute-start(bf16[96,2048]{1,0:T(8,128)(2,1)S(1)} %get-tuple-element.41.refs_0_.own_in.refs_2_), channel_id=1, source_target_pairs={{0,4},{1,5},{2,6},{3,7},{4,0},{5,1},{6,2},{7,3},{8,12},{9,13},{10,... | collective-permute-start | bytes 1179656 | tf_op jit(solution)/shard_map/ppermute | solution.py:394
  21.9 0.7 hold_weights.1
  22.6 2.7 %collective-permute-start.8 = (bf16[96,2048]{1,0:T(8,128)(2,1)S(1)}, bf16[96,2048]{1,0:T(8,128)(2,1)S(1)}, u32[]{:S(2)}, u32[]{:S(2)}) collective-permute-start(bf16[96,2048]{1,0:T(8,128)(2,1)S(1)} %get-tuple-element.44), channel_id=1, source_target_pairs={{0,8},{1,9},{2,10},{3,11},{4,12},{5,13},{6,14},{7,15},{8,0},{9,1},... | collective-permute-start | bytes 1179656 | tf_op jit(solution)/shard_map/ppermute | solution.py:398
  25.2 1.5 %collective-permute-start.5 = (bf16[512,384]{1,0:T(8,128)(2,1)S(1)}, bf16[512,384]{1,0:T(8,128)(2,1)S(1)}, u32[]{:S(2)}, u32[]{:S(2)}) collective-permute-start(bf16[512,384]{1,0:T(8,128)(2,1)S(1)} %hand_on.17.refs_1_.refs_0_), channel_id=1, source_target_pairs={{0,16},{16,0},{1,17},{17,1},{2,18},{18,2},{3,19},{19,3},{4,20},{20... | collective-permute-start | bytes 1179656 | tf_op jit(solution)/shard_map/ppermute | solution.py:402
  26.7 0.4 collective-permute-done.6.refs_0_
  27.1 1.5 %collective-permute-start.7 = (bf16[512,384]{1,0:T(8,128)(2,1)S(1)}, bf16[512,384]{1,0:T(8,128)(2,1)S(1)}, u32[]{:S(2)}, u32[]{:S(2)}) collective-permute-start(bf16[512,384]{1,0:T(8,128)(2,1)S(1)} %hand_on.19.refs_2_), channel_id=1, source_target_pairs={{0,16},{16,0},{1,17},{17,1},{2,18},{18,2},{3,19},{19,3},{4,20},{20... | collective-permute-start | bytes 1179656 | tf_op jit(solution)/shard_map/ppermute | solution.py:402
  28.6 0.5 collective-permute-start.14
  29.1 12.3 %collective-permute-done.8.refs_0_ = bf16[96,2048]{1,0:T(8,128)(2,1)S(1)} collective-permute-done((bf16[96,2048]{1,0:T(8,128)(2,1)S(1)}, bf16[96,2048]{1,0:T(8,128)(2,1)S(1)}, u32[]{:S(2)}, u32[]{:S(2)}) %collective-permute-start.8) | collective-permute-done | bytes 393248 | tf_op jit(solution)/shard_map/ppermute | solution.py:398
  41.4 1.6 %collective-permute-start.16 = (bf16[160,2048]{1,0:T(8,128)(2,1)S(1)}, bf16[160,2048]{1,0:T(8,128)(2,1)S(1)}, u32[]{:S(2)}, u32[]{:S(2)}) collective-permute-start(bf16[160,2048]{1,0:T(8,128)(2,1)S(1)} %get-tuple-element.52), channel_id=1, source_target_pairs={{0,2},{1,3},{2,0},{3,1},{4,6},{5,7},{6,4},{7,5},{8,10},{9,11},{10,... | collective-permute-start | bytes 1966088 | tf_op jit(solution)/shard_map/ppermute | solution.py:394
  43.0 1.6 %collective-permute-start.15 = (bf16[112,2048]{1,0:T(8,128)(2,1)S(1)}, bf16[112,2048]{1,0:T(8,128)(2,1)S(1)}, u32[]{:S(2)}, u32[]{:S(2)}) collective-permute-start(bf16[112,2048]{1,0:T(8,128)(2,1)S(1)} %hand_on.27.refs_4_), channel_id=1, source_target_pairs={{0,16},{16,0},{1,17},{17,1},{2,18},{18,2},{3,19},{19,3},{4,20},{20... | collective-permute-start | bytes 1376264 | tf_op jit(solution)/shard_map/ppermute | solution.py:402
  44.6 4.6 %collective-permute-done.9.refs_4_.refs_0_ = bf16[96,2048]{1,0:T(8,128)(2,1)S(1)} collective-permute-done((bf16[96,2048]{1,0:T(8,128)(2,1)S(1)}, bf16[96,2048]{1,0:T(8,128)(2,1)S(1)}, u32[]{:S(2)}, u32[]{:S(2)}) %collective-permute-start.9) | collective-permute-done | bytes 393248 | tf_op jit(solution)/shard_map/ppermute | solution.py:394
  49.2 0.5 collective-permute-start.11
  49.7 1.2 %collective-permute-done.10.refs_8_ = bf16[512,384]{1,0:T(8,128)(2,1)S(1)} collective-permute-done((bf16[512,384]{1,0:T(8,128)(2,1)S(1)}, bf16[512,384]{1,0:T(8,128)(2,1)S(1)}, u32[]{:S(2)}, u32[]{:S(2)}) %collective-permute-start.10) | collective-permute-done | bytes 393248 | tf_op jit(solution)/shard_map/ppermute | solution.py:394
  51.1 0.4 collective-permute-done.11.refs_9_
  51.6 0.8 expert_up.3.refs_1_
  52.7 0.6 collective-permute-done.13.refs_11_
  53.2 0.8 expert_up_y.2.refs_2_.refs_1_
  54.1 0.8 collective-permute-done.16.refs_1_
  54.9 1.1 %collective-permute-done.15.refs_0_ = bf16[112,2048]{1,0:T(8,128)(2,1)S(1)} collective-permute-done((bf16[112,2048]{1,0:T(8,128)(2,1)S(1)}, bf16[112,2048]{1,0:T(8,128)(2,1)S(1)}, u32[]{:S(2)}, u32[]{:S(2)}) %collective-permute-start.15) | collective-permute-done | bytes 458784 | tf_op jit(solution)/shard_map/ppermute | solution.py:402
  56.0 0.5 collective-permute-start.18
  56.5 2.2 %collective-permute-done.18.refs_7_ = bf16[112,2048]{1,0:T(8,128)(2,1)S(1)} collective-permute-done((bf16[112,2048]{1,0:T(8,128)(2,1)S(1)}, bf16[112,2048]{1,0:T(8,128)(2,1)S(1)}, u32[]{:S(2)}, u32[]{:S(2)}) %collective-permute-start.18) | collective-permute-done | bytes 458784 | tf_op jit(solution)/shard_map/ppermute | solution.py:394
  58.7 0.8 expert_down.3
  59.5 2.0 %collective-permute-start.22 = (bf16[96,1024]{1,0:T(8,128)(2,1)S(1)}, bf16[96,1024]{1,0:T(8,128)(2,1)S(1)}, u32[]{:S(2)}, u32[]{:S(2)}) collective-permute-start(bf16[96,1024]{1,0:T(8,128)(2,1)S(1)} %get-tuple-element.61), channel_id=1, source_target_pairs={{0,4},{1,5},{2,6},{3,7},{4,0},{5,1},{6,2},{7,3},{8,12},{9,13},{10,... | collective-permute-start | bytes 589832 | tf_op jit(solution)/shard_map/ppermute | solution.py:394
  61.6 0.8 expert_up.2.refs_1_
  62.3 0.8 expert_down.4
  63.2 0.8 expert_up_y.3.refs_1_
  64.1 2.8 %collective-permute-done.22.z_ref = bf16[96,1024]{1,0:T(8,128)(2,1)S(1)} collective-permute-done((bf16[96,1024]{1,0:T(8,128)(2,1)S(1)}, bf16[96,1024]{1,0:T(8,128)(2,1)S(1)}, u32[]{:S(2)}, u32[]{:S(2)}) %collective-permute-start.22) | collective-permute-done | bytes 196640 | tf_op jit(solution)/shard_map/ppermute | solution.py:394
  67.0 3.5 %collective-permute-start.23 = (bf16[96,1024]{1,0:T(8,128)(2,1)S(1)}, bf16[96,1024]{1,0:T(8,128)(2,1)S(1)}, u32[]{:S(2)}, u32[]{:S(2)}) collective-permute-start(bf16[96,1024]{1,0:T(8,128)(2,1)S(1)} %far_total.3), channel_id=1, source_target_pairs={{0,8},{1,9},{2,10},{3,11},{4,12},{5,13},{6,14},{7,15},{8,0},{9,1},... | collective-permute-start | bytes 589832 | tf_op jit(solution)/shard_map/ppermute | solution.py:398
  70.4 1.5 %expert_down.5 = (bf16[96,2048]{1,0:T(8,128)(2,1)S(1)}, bf16[96,2048]{1,0:T(8,128)(2,1)S(1)}) custom-call(s32[1]{0:T(128)} %bitcast.10.pipe_ref.refs_0_, bf16[192,1536]{1,0:T(8,128)(2,1)S(1)} %expert_up_y.3.refs_1_, bf16[384,2048]{1,0:T(8,128)(2,1)S(1)} %get-tuple-element.49.refs_2_, bf16[384,2048]{1,0:T(8,128)(2,1)S(1)} %collective-permute-done.2.refs_7_.refs_3_, ...), custom_call_target="tpu_custom_call" | custom-call | flops 1207959552 | bytes 6291456 | tf_op jit(solution)/shard_map/expert_down/pallas_call | solution.py:321
  71.9 2.4 %collective-permute-done.20.z_ref = bf16[96,1024]{1,0:T(8,128)(2,1)S(1)} collective-permute-done((bf16[96,1024]{1,0:T(8,128)(2,1)S(1)}, bf16[96,1024]{1,0:T(8,128)(2,1)S(1)}, u32[]{:S(2)}, u32[]{:S(2)}) %collective-permute-start.20) | collective-permute-done | bytes 196640 | tf_op jit(solution)/shard_map/ppermute | solution.py:394
  74.4 1.9 %collective-permute-start.24 = (bf16[96,1024]{1,0:T(8,128)(2,1)S(1)}, bf16[96,1024]{1,0:T(8,128)(2,1)S(1)}, u32[]{:S(2)}, u32[]{:S(2)}) collective-permute-start(bf16[96,1024]{1,0:T(8,128)(2,1)S(1)} %get-tuple-element.62), channel_id=1, source_target_pairs={{0,8},{1,9},{2,10},{3,11},{4,12},{5,13},{6,14},{7,15},{8,0},{9,1},... | collective-permute-start | bytes 589832 | tf_op jit(solution)/shard_map/ppermute | solution.py:398
  76.3 3.0 %collective-permute-done.23.refs_0_ = bf16[96,1024]{1,0:T(8,128)(2,1)S(1)} collective-permute-done((bf16[96,1024]{1,0:T(8,128)(2,1)S(1)}, bf16[96,1024]{1,0:T(8,128)(2,1)S(1)}, u32[]{:S(2)}, u32[]{:S(2)}) %collective-permute-start.23) | collective-permute-done | bytes 196640 | tf_op jit(solution)/shard_map/ppermute | solution.py:398
  79.3 7.8 %collective-permute-done.24.refs_6_ = bf16[96,1024]{1,0:T(8,128)(2,1)S(1)} collective-permute-done((bf16[96,1024]{1,0:T(8,128)(2,1)S(1)}, bf16[96,1024]{1,0:T(8,128)(2,1)S(1)}, u32[]{:S(2)}, u32[]{:S(2)}) %collective-permute-start.24) | collective-permute-done | bytes 196640 | tf_op jit(solution)/shard_map/ppermute | solution.py:398
  87.1 1.8 %collective-permute-done.21.refs_4_ = bf16[96,2048]{1,0:T(8,128)(2,1)S(1)} collective-permute-done((bf16[96,2048]{1,0:T(8,128)(2,1)S(1)}, bf16[96,2048]{1,0:T(8,128)(2,1)S(1)}, u32[]{:S(2)}, u32[]{:S(2)}) %collective-permute-start.21) | collective-permute-done | bytes 393248 | tf_op jit(solution)/shard_map/ppermute | solution.py:394
  89.0 1.2 %finish.1 = bf16[128,2048]{1,0:T(8,128)(2,1)} custom-call(f32[128,2048]{1,0:T(8,128)S(1)} %get-tuple-element.38.refs_0_, f32[128,1]{1,0:T(8,128)S(1)} %get-tuple-element.39.refs_1_, s32[128,1]{1,0:T(8,128)S(1)} %get-tuple-element.40.refs_2_, bf16[96,2048]{1,0:T(8,128)(2,1)S(1)} %get-tuple-element.57.refs_3_, ...), custom_call_target="tpu_custom_call" | custom-call | flops 201326592 | bytes 4194304 | tf_op jit(solution)/shard_map/finish/pallas_call | solution.py:376
  (54 shorter events, 1.4 us)
Async XLA Ops:
  0.0 17.4 %collective-permute-start.2 = (bf16[384,2048]{1,0:T(8,128)(2,1)}, bf16[384,2048]{1,0:T(8,128)(2,1)S(1)}, u32[]{:S(2)}, u32[]{:S(2)}) collective-permute-start(bf16[384,2048]{1,0:T(8,128)(2,1)} %w_out.1), channel_id=1, source_target_pairs={{0,1},{1,0},{2,3},{3,2},{4,5},{5,4},{6,7},{7,6},{8,9},{9,8},{10,11... | collective-permute-start | bytes 4718600 | tf_op jit(solution)/shard_map/ppermute | solution.py:394
  0.5 16.9 %collective-permute-start.1 = (bf16[2048,384]{1,0:T(8,128)(2,1)}, bf16[2048,384]{1,0:T(8,128)(2,1)S(1)}, u32[]{:S(2)}, u32[]{:S(2)}) collective-permute-start(bf16[2048,384]{1,0:T(8,128)(2,1)} %whole.1), channel_id=1, source_target_pairs={{0,1},{1,0},{2,3},{3,2},{4,5},{5,4},{6,7},{7,6},{8,9},{9,8},{10,11... | collective-permute-start | bytes 4718600 | tf_op jit(solution)/shard_map/ppermute | solution.py:394
  2.3 22.9 %collective-permute-start.4 = (bf16[512,384]{1,0:T(8,128)(2,1)}, bf16[512,384]{1,0:T(8,128)(2,1)S(1)}, u32[]{:S(2)}, u32[]{:S(2)}) collective-permute-start(bf16[512,384]{1,0:T(8,128)(2,1)} %constant_dynamic-slice_fusion.refs_1_), channel_id=1, source_target_pairs={{0,2},{1,3},{2,0},{3,1},{4,6},{5,7},{6,4},{7,5},{8,10},{9,11},{10,... | collective-permute-start | bytes 1179656 | tf_op jit(solution)/shard_map/ppermute | solution.py:394
  7.0 3.3 %copy-start.6 = (f32[2048]{0:T(1024)S(1)}, f32[2048]{0:T(1024)}, u32[]{:S(2)}) copy-start(f32[2048]{0:T(1024)} %param.12) | copy-start | bytes 24580
  7.0 3.3 %copy-start.7 = (s32[1,1,128]{2,1,0:T(1,128)S(1)}, s32[1,1,128]{2,1,0:T(1,128)}, u32[]{:S(2)}) copy-start(s32[1,1,128]{2,1,0:T(1,128)} %param.15) | copy-start | bytes 1540
  7.0 3.3 %copy-start.8 = (s32[1,1,128]{2,1,0:T(1,128)S(1)}, s32[1,1,128]{2,1,0:T(1,128)}, u32[]{:S(2)}) copy-start(s32[1,1,128]{2,1,0:T(1,128)} %param.16) | copy-start | bytes 1540
  7.0 8.3 %collective-permute-start = (bf16[64,2048]{1,0:T(8,128)(2,1)}, bf16[64,2048]{1,0:T(8,128)(2,1)}, u32[]{:S(2)}, u32[]{:S(2)}) collective-permute-start(bf16[64,2048]{1,0:T(8,128)(2,1)} %hand_on.16.refs_4_), channel_id=1, source_target_pairs={{0,16},{16,0},{1,17},{17,1},{2,18},{18,2},{3,19},{19,3},{4,20},{20... | collective-permute-start | bytes 786440 | tf_op jit(solution)/shard_map/ppermute | solution.py:418
  10.4 1.0 %copy-start.4 = (bf16[1,1,128,2048]{3,2,1,0:T(8,128)(2,1)S(1)}, bf16[1,1,128,2048]{3,2,1,0:T(8,128)(2,1)}, u32[]{:S(2)}) copy-start(bf16[1,1,128,2048]{3,2,1,0:T(8,128)(2,1)} %param.9) | copy-start | bytes 1572868
  11.4 1.0 %copy-start.5 = (bf16[1,1,128,2048]{3,2,1,0:T(8,128)(2,1)S(1)}, bf16[1,1,128,2048]{3,2,1,0:T(8,128)(2,1)}, u32[]{:S(2)}) copy-start(bf16[1,1,128,2048]{3,2,1,0:T(8,128)(2,1)} %param.10) | copy-start | bytes 1572868
  12.5 0.7 copy-start.9
  15.3 1.0 %copy-start.2 = (bf16[512,384]{1,0:T(8,128)(2,1)S(1)}, bf16[512,384]{1,0:T(8,128)(2,1)}, u32[]{:S(2)}) copy-start(bf16[512,384]{1,0:T(8,128)(2,1)} %weight_part.1.refs_0_) | copy-start | bytes 1179652
  16.3 0.7 copy-start.3
  17.1 10.1 %collective-permute-start.6 = (bf16[512,384]{1,0:T(8,128)(2,1)}, bf16[512,384]{1,0:T(8,128)(2,1)S(1)}, u32[]{:S(2)}, u32[]{:S(2)}) collective-permute-start(bf16[512,384]{1,0:T(8,128)(2,1)} %copy-done.3), channel_id=1, source_target_pairs={{0,2},{1,3},{2,0},{3,1},{4,6},{5,7},{6,4},{7,5},{8,10},{9,11},{10,... | collective-permute-start | bytes 1179656 | tf_op jit(solution)/shard_map/ppermute | solution.py:394
  17.4 4.5 %copy-start = (bf16[2048,384]{1,0:T(8,128)(2,1)S(1)}, bf16[2048,384]{1,0:T(8,128)(2,1)}, u32[]{:S(2)}) copy-start(bf16[2048,384]{1,0:T(8,128)(2,1)} %whole.1) | copy-start | bytes 4718596
  17.4 4.5 %copy-start.1 = (bf16[384,2048]{1,0:T(8,128)(2,1)S(1)}, bf16[384,2048]{1,0:T(8,128)(2,1)}, u32[]{:S(2)}) copy-start(bf16[384,2048]{1,0:T(8,128)(2,1)} %w_out.1) | copy-start | bytes 4718596
  20.0 21.4 %collective-permute-start.3 = (bf16[96,2048]{1,0:T(8,128)(2,1)S(1)}, bf16[96,2048]{1,0:T(8,128)(2,1)S(1)}, u32[]{:S(2)}, u32[]{:S(2)}) collective-permute-start(bf16[96,2048]{1,0:T(8,128)(2,1)S(1)} %get-tuple-element.41.refs_0_.own_in.refs_2_), channel_id=1, source_target_pairs={{0,4},{1,5},{2,6},{3,7},{4,0},{5,1},{6,2},{7,3},{8,12},{9,13},{10,... | collective-permute-start | bytes 1179656 | tf_op jit(solution)/shard_map/ppermute | solution.py:394
  22.6 18.8 %collective-permute-start.8 = (bf16[96,2048]{1,0:T(8,128)(2,1)S(1)}, bf16[96,2048]{1,0:T(8,128)(2,1)S(1)}, u32[]{:S(2)}, u32[]{:S(2)}) collective-permute-start(bf16[96,2048]{1,0:T(8,128)(2,1)S(1)} %get-tuple-element.44), channel_id=1, source_target_pairs={{0,8},{1,9},{2,10},{3,11},{4,12},{5,13},{6,14},{7,15},{8,0},{9,1},... | collective-permute-start | bytes 1179656 | tf_op jit(solution)/shard_map/ppermute | solution.py:398
  25.2 19.3 %collective-permute-start.5 = (bf16[512,384]{1,0:T(8,128)(2,1)S(1)}, bf16[512,384]{1,0:T(8,128)(2,1)S(1)}, u32[]{:S(2)}, u32[]{:S(2)}) collective-permute-start(bf16[512,384]{1,0:T(8,128)(2,1)S(1)} %hand_on.17.refs_1_.refs_0_), channel_id=1, source_target_pairs={{0,16},{16,0},{1,17},{17,1},{2,18},{18,2},{3,19},{19,3},{4,20},{20... | collective-permute-start | bytes 1179656 | tf_op jit(solution)/shard_map/ppermute | solution.py:402
  27.1 15.9 %collective-permute-start.7 = (bf16[512,384]{1,0:T(8,128)(2,1)S(1)}, bf16[512,384]{1,0:T(8,128)(2,1)S(1)}, u32[]{:S(2)}, u32[]{:S(2)}) collective-permute-start(bf16[512,384]{1,0:T(8,128)(2,1)S(1)} %hand_on.19.refs_2_), channel_id=1, source_target_pairs={{0,16},{16,0},{1,17},{17,1},{2,18},{18,2},{3,19},{19,3},{4,20},{20... | collective-permute-start | bytes 1179656 | tf_op jit(solution)/shard_map/ppermute | solution.py:402
  28.6 14.4 %collective-permute-start.14 = (bf16[112,2048]{1,0:T(8,128)(2,1)S(1)}, bf16[112,2048]{1,0:T(8,128)(2,1)S(1)}, u32[]{:S(2)}, u32[]{:S(2)}) collective-permute-start(bf16[112,2048]{1,0:T(8,128)(2,1)S(1)} %get-tuple-element.51), channel_id=1, source_target_pairs={{0,2},{1,3},{2,0},{3,1},{4,6},{5,7},{6,4},{7,5},{8,10},{9,11},{10,... | collective-permute-start | bytes 1376264 | tf_op jit(solution)/shard_map/ppermute | solution.py:394
  41.4 7.8 %collective-permute-start.9 = (bf16[96,2048]{1,0:T(8,128)(2,1)S(1)}, bf16[96,2048]{1,0:T(8,128)(2,1)S(1)}, u32[]{:S(2)}, u32[]{:S(2)}) collective-permute-start(bf16[96,2048]{1,0:T(8,128)(2,1)S(1)} %hand_on.20.own_in.refs_2_), channel_id=1, source_target_pairs={{0,4},{1,5},{2,6},{3,7},{4,0},{5,1},{6,2},{7,3},{8,12},{9,13},{10,... | collective-permute-start | bytes 1179656 | tf_op jit(solution)/shard_map/ppermute | solution.py:394
  41.4 13.5 %collective-permute-start.16 = (bf16[160,2048]{1,0:T(8,128)(2,1)S(1)}, bf16[160,2048]{1,0:T(8,128)(2,1)S(1)}, u32[]{:S(2)}, u32[]{:S(2)}) collective-permute-start(bf16[160,2048]{1,0:T(8,128)(2,1)S(1)} %get-tuple-element.52), channel_id=1, source_target_pairs={{0,2},{1,3},{2,0},{3,1},{4,6},{5,7},{6,4},{7,5},{8,10},{9,11},{10,... | collective-permute-start | bytes 1966088 | tf_op jit(solution)/shard_map/ppermute | solution.py:394
  43.0 11.9 %collective-permute-start.17 = (bf16[112,2048]{1,0:T(8,128)(2,1)S(1)}, bf16[112,2048]{1,0:T(8,128)(2,1)S(1)}, u32[]{:S(2)}, u32[]{:S(2)}) collective-permute-start(bf16[112,2048]{1,0:T(8,128)(2,1)S(1)} %hand_on.27.refs_4_), channel_id=1, source_target_pairs={{0,1},{1,0},{2,3},{3,2},{4,5},{5,4},{6,7},{7,6},{8,9},{9,8},{10,11... | collective-permute-start | bytes 1376264 | tf_op jit(solution)/shard_map/ppermute | solution.py:394
  43.0 12.9 %collective-permute-start.15 = (bf16[112,2048]{1,0:T(8,128)(2,1)S(1)}, bf16[112,2048]{1,0:T(8,128)(2,1)S(1)}, u32[]{:S(2)}, u32[]{:S(2)}) collective-permute-start(bf16[112,2048]{1,0:T(8,128)(2,1)S(1)} %hand_on.27.refs_4_), channel_id=1, source_target_pairs={{0,16},{16,0},{1,17},{17,1},{2,18},{18,2},{3,19},{19,3},{4,20},{20... | collective-permute-start | bytes 1376264 | tf_op jit(solution)/shard_map/ppermute | solution.py:402
  49.2 1.7 %collective-permute-start.10 = (bf16[512,384]{1,0:T(8,128)(2,1)S(1)}, bf16[512,384]{1,0:T(8,128)(2,1)S(1)}, u32[]{:S(2)}, u32[]{:S(2)}) collective-permute-start(bf16[512,384]{1,0:T(8,128)(2,1)S(1)} %get-tuple-element.45.refs_4_), channel_id=1, source_target_pairs={{0,1},{1,0},{2,3},{3,2},{4,5},{5,4},{6,7},{7,6},{8,9},{9,8},{10,11... | collective-permute-start | bytes 1179656 | tf_op jit(solution)/shard_map/ppermute | solution.py:394
  49.2 2.3 %collective-permute-start.11 = (bf16[512,384]{1,0:T(8,128)(2,1)S(1)}, bf16[512,384]{1,0:T(8,128)(2,1)S(1)}, u32[]{:S(2)}, u32[]{:S(2)}) collective-permute-start(bf16[512,384]{1,0:T(8,128)(2,1)S(1)} %get-tuple-element.46.refs_5_), channel_id=1, source_target_pairs={{0,1},{1,0},{2,3},{3,2},{4,5},{5,4},{6,7},{7,6},{8,9},{9,8},{10,11... | collective-permute-start | bytes 1179656 | tf_op jit(solution)/shard_map/ppermute | solution.py:394
  50.9 1.7 %collective-permute-start.12 = (bf16[512,384]{1,0:T(8,128)(2,1)S(1)}, bf16[512,384]{1,0:T(8,128)(2,1)S(1)}, u32[]{:S(2)}, u32[]{:S(2)}) collective-permute-start(bf16[512,384]{1,0:T(8,128)(2,1)S(1)} %get-tuple-element.47.refs_6_), channel_id=1, source_target_pairs={{0,1},{1,0},{2,3},{3,2},{4,5},{5,4},{6,7},{7,6},{8,9},{9,8},{10,11... | collective-permute-start | bytes 1179656 | tf_op jit(solution)/shard_map/ppermute | solution.py:394
  51.5 1.7 %collective-permute-start.13 = (bf16[512,384]{1,0:T(8,128)(2,1)S(1)}, bf16[512,384]{1,0:T(8,128)(2,1)S(1)}, u32[]{:S(2)}, u32[]{:S(2)}) collective-permute-start(bf16[512,384]{1,0:T(8,128)(2,1)S(1)} %get-tuple-element.48.refs_7_), channel_id=1, source_target_pairs={{0,1},{1,0},{2,3},{3,2},{4,5},{5,4},{6,7},{7,6},{8,9},{9,8},{10,11... | collective-permute-start | bytes 1179656 | tf_op jit(solution)/shard_map/ppermute | solution.py:394
  56.0 2.8 %collective-permute-start.19 = (bf16[160,2048]{1,0:T(8,128)(2,1)S(1)}, bf16[160,2048]{1,0:T(8,128)(2,1)S(1)}, u32[]{:S(2)}, u32[]{:S(2)}) collective-permute-start(bf16[160,2048]{1,0:T(8,128)(2,1)S(1)} %get-tuple-element.54.refs_8_), channel_id=1, source_target_pairs={{0,1},{1,0},{2,3},{3,2},{4,5},{5,4},{6,7},{7,6},{8,9},{9,8},{10,11... | collective-permute-start | bytes 1966088 | tf_op jit(solution)/shard_map/ppermute | solution.py:394
  56.0 2.8 %collective-permute-start.18 = (bf16[112,2048]{1,0:T(8,128)(2,1)S(1)}, bf16[112,2048]{1,0:T(8,128)(2,1)S(1)}, u32[]{:S(2)}, u32[]{:S(2)}) collective-permute-start(bf16[112,2048]{1,0:T(8,128)(2,1)S(1)} %get-tuple-element.53.refs_5_), channel_id=1, source_target_pairs={{0,1},{1,0},{2,3},{3,2},{4,5},{5,4},{6,7},{7,6},{8,9},{9,8},{10,11... | collective-permute-start | bytes 1376264 | tf_op jit(solution)/shard_map/ppermute | solution.py:394
  59.5 7.4 %collective-permute-start.22 = (bf16[96,1024]{1,0:T(8,128)(2,1)S(1)}, bf16[96,1024]{1,0:T(8,128)(2,1)S(1)}, u32[]{:S(2)}, u32[]{:S(2)}) collective-permute-start(bf16[96,1024]{1,0:T(8,128)(2,1)S(1)} %get-tuple-element.61), channel_id=1, source_target_pairs={{0,4},{1,5},{2,6},{3,7},{4,0},{5,1},{6,2},{7,3},{8,12},{9,13},{10,... | collective-permute-start | bytes 589832 | tf_op jit(solution)/shard_map/ppermute | solution.py:394
  64.0 10.3 %collective-permute-start.20 = (bf16[96,1024]{1,0:T(8,128)(2,1)S(1)}, bf16[96,1024]{1,0:T(8,128)(2,1)S(1)}, u32[]{:S(2)}, u32[]{:S(2)}) collective-permute-start(bf16[96,1024]{1,0:T(8,128)(2,1)S(1)} %hand_on.29), channel_id=1, source_target_pairs={{0,4},{1,5},{2,6},{3,7},{4,0},{5,1},{6,2},{7,3},{8,12},{9,13},{10,... | collective-permute-start | bytes 589832 | tf_op jit(solution)/shard_map/ppermute | solution.py:394
  67.0 12.4 %collective-permute-start.23 = (bf16[96,1024]{1,0:T(8,128)(2,1)S(1)}, bf16[96,1024]{1,0:T(8,128)(2,1)S(1)}, u32[]{:S(2)}, u32[]{:S(2)}) collective-permute-start(bf16[96,1024]{1,0:T(8,128)(2,1)S(1)} %far_total.3), channel_id=1, source_target_pairs={{0,8},{1,9},{2,10},{3,11},{4,12},{5,13},{6,14},{7,15},{8,0},{9,1},... | collective-permute-start | bytes 589832 | tf_op jit(solution)/shard_map/ppermute | solution.py:398
  74.3 14.6 %collective-permute-start.21 = (bf16[96,2048]{1,0:T(8,128)(2,1)S(1)}, bf16[96,2048]{1,0:T(8,128)(2,1)S(1)}, u32[]{:S(2)}, u32[]{:S(2)}) collective-permute-start(bf16[96,2048]{1,0:T(8,128)(2,1)S(1)} %get-tuple-element.60), channel_id=1, source_target_pairs={{0,4},{1,5},{2,6},{3,7},{4,0},{5,1},{6,2},{7,3},{8,12},{9,13},{10,... | collective-permute-start | bytes 1179656 | tf_op jit(solution)/shard_map/ppermute | solution.py:394
  74.4 12.7 %collective-permute-start.24 = (bf16[96,1024]{1,0:T(8,128)(2,1)S(1)}, bf16[96,1024]{1,0:T(8,128)(2,1)S(1)}, u32[]{:S(2)}, u32[]{:S(2)}) collective-permute-start(bf16[96,1024]{1,0:T(8,128)(2,1)S(1)} %get-tuple-element.62), channel_id=1, source_target_pairs={{0,8},{1,9},{2,10},{3,11},{4,12},{5,13},{6,14},{7,15},{8,0},{9,1},... | collective-permute-start | bytes 589832 | tf_op jit(solution)/shard_map/ppermute | solution.py:398

commit v16 on v14

--- a/solution.py
+++ b/solution.py
@@ -16,6 +16,7 @@
 FAR_STEPS = 4
 CROSS_STEPS = 1
 CROSS_WEIGHT = 3_000_000_000
+FIRST_WEIGHT = 2_000_000_000
 SUM_WEIGHT = 1_000_000_000
 BACK_WEIGHT = 3_000_000_000
 VMEM_LIMIT = 32 * 1024 * 1024
@@ -362,7 +363,8 @@
         near = (own_ref[:, cols].astype(jnp.float32) + z_ref[:, cols].astype(jnp.float32)).astype(
             jnp.bfloat16
         )
-        side, inner = divmod(at, width // 2)
+        cut = back_refs[0].shape[1]
+        side, inner = (0, at) if at < cut else (1, at - cut)
         backs = [r[:, inner : inner + step] for r in back_refs[side::2]]
         found = jnp.concatenate([near, *backs], axis=0)
         picked = jnp.dot(picker, found, preferred_element_type=jnp.float32)
@@ -473,20 +475,20 @@
             pipe, act, [w_out_held, w_out_pair], out_parts, out_pair, rests, first, size, after
         )
 
-    half = width // 2
-    far_a, sent_a = experts_down(far_act, 0, half)
-    far_b, sent_b = experts_down(far_act, half, half, [far_a])
+    cut = width // 4
+    far_a, sent_a = experts_down(far_act, 0, cut)
+    far_b, sent_b = experts_down(far_act, cut, width - cut, [far_a])
     near_act = experts_up(near, near_z, [far_b])
     (sent_b,) = after_all([sent_b], [near_act])
     near_own, near_sent = experts_down(near_act, 0, width)
-    (sum_a,) = total(far_a, across(sent_a, 4), [])
+    (sum_a,) = total(far_a, *after_all([across(sent_a, 4)], [], FIRST_WEIGHT), [])
     sum_b, near_sent = total(far_b, across(sent_b, 4), [near_sent])
     backs = [
         groups_on(side[(count - 1) * cap : count * cap], groups - count)
         for count in range(1, groups)
         for side in (sum_a, sum_b)
     ]
-    backs[::2] = after_all(backs[::2], [], SUM_WEIGHT)
+    backs[::2] = after_all(backs[::2], [sum_b], SUM_WEIGHT)
     backs[::2] = after_all(backs[::2], [], BACK_WEIGHT)
     near_sums = [near_own, across(near_sent, 4)]
     output = finish(hidden, gates, flat, near_sums, backs, groups, cap)

time: 87.3 us -> 88.7 us (1.016)
  starting transfers between devices: 26.8 us -> 30.2 us
  waiting for transfers between devices: 41.3 us -> 39.3 us
    ppermute x3, starting transfers between devices: 7.77 us -> 10.5 us  [groups_on(): lax.ppermute(value, 'expert', [(i, (i + shift) % devices) for i in range(...]
    ppermute x3, waiting for transfers between devices: 19.8 us -> 18.3 us  [groups_on(): lax.ppermute(value, 'expert', [(i, (i + shift) % devices) for i in range(...]
  transfers between devices with their start and end apart: 25 -> 25, of which waited for: 17 -> 16; matrix products, arithmetic and copies ran while one was open for 1% -> 1% of each run, Pallas kernels for 15% -> 15%
where the time goes in v16:
time: 88.7 us; the launch traced here: 88 us
  waiting for transfers between devices  39.3 us (44%)
  starting transfers between devices  30.2 us (34%)
  Pallas kernels  14.8 us (17%)
  local copies, waits for them, and re-layouts  3.56 us (4%)
    ppermute x18, waiting for transfers between devices, across(): return lax.ppermute(value, 'expert', [(i, i ^ bit) for i in range(devices)])  19.1 us
    ppermute x3, waiting for transfers between devices, groups_on(): lax.ppermute(value, 'expert', [(i, (i + shift) % devices) for i in range(...  18.3 us
    ppermute x18, starting transfers between devices, across(): return lax.ppermute(value, 'expert', [(i, i ^ bit) for i in range(devices)])  13.2 us
    ppermute x3, starting transfers between devices, groups_on(): lax.ppermute(value, 'expert', [(i, (i + shift) % devices) for i in range(...  10.5 us
    pallas_call x2, Pallas kernels, cut_part(): call(functools.partial(part_kernel, stride, first), struct((size, whole.s...  3.49 us
    ppermute x3, starting transfers between devices, along(): return [value] + [lax.ppermute(value, 'pipe', perm) for perm in perms]  3.46 us
    pallas_call x3, Pallas kernels, down(): call(functools.partial(down_kernel, pipes, first), [struct((rows, width))...  3.16 us
    ppermute x1, starting transfers between devices, body(): kv_pieces.append(lax.ppermute(kv, 'pipe', perm))  2.93 us
  transfers between devices with their start and end apart: 25, of which 16 were waited for; matrix products, arithmetic and copies ran while one was open for 1% of the time, Pallas kernels for 15%

profile of v16, /device:TPU:0, one launch (start us, length us, event | category | flops | bytes accessed | tf_op | source)
XLA Modules:
  0.0 88.0 jit_solution(18383769145096921420)
XLA Ops:
  0.0 0.5 collective-permute-start.2
  0.5 1.7 %weight_part.2.refs_1_ = bf16[512,384]{1,0:T(8,128)(2,1)} custom-call(s32[1]{0:T(128)} %bitcast.10.pipe_ref.refs_0_, bf16[2048,384]{1,0:T(8,128)(2,1)} %whole.3), custom_call_target="tpu_custom_call" | custom-call | flops 1 | bytes 786432 | tf_op jit(solution)/shard_map/weight_part/pallas_call | solution.py:179
  2.3 0.8 copy.33
  3.1 2.9 %collective-permute-start = (bf16[64,2048]{1,0:T(8,128)(2,1)}, bf16[64,2048]{1,0:T(8,128)(2,1)}, u32[]{:S(2)}, u32[]{:S(2)}) collective-permute-start(bf16[64,2048]{1,0:T(8,128)(2,1)} %hand_on.17.refs_4_), channel_id=1, source_target_pairs={{0,16},{16,0},{1,17},{17,1},{2,18},{18,2},{3,19},{19,3},{4,20},{20... | collective-permute-start | bytes 786440 | tf_op jit(solution)/shard_map/ppermute | solution.py:418
  6.0 1.5 %collective-permute-start.4 = (bf16[512,384]{1,0:T(8,128)(2,1)}, bf16[512,384]{1,0:T(8,128)(2,1)S(1)}, u32[]{:S(2)}, u32[]{:S(2)}) collective-permute-start(bf16[512,384]{1,0:T(8,128)(2,1)} %weight_part.2.refs_1_), channel_id=1, source_target_pairs={{0,2},{1,3},{2,0},{3,1},{4,6},{5,7},{6,4},{7,5},{8,10},{9,11},{10,... | collective-permute-start | bytes 1179656 | tf_op jit(solution)/shard_map/ppermute | solution.py:395
  7.6 1.7 %weight_part.3.refs_0_ = bf16[512,384]{1,0:T(8,128)(2,1)} custom-call(s32[1]{0:T(128)} %bitcast.10.pipe_ref.refs_0_, bf16[2048,384]{1,0:T(8,128)(2,1)} %whole.3), custom_call_target="tpu_custom_call" | custom-call | flops 1 | bytes 786432 | tf_op jit(solution)/shard_map/weight_part/pallas_call | solution.py:179
  9.4 1.0 %copy-done.2 = bf16[1,1,128,2048]{3,2,1,0:T(8,128)(2,1)S(1)} copy-done((bf16[1,1,128,2048]{3,2,1,0:T(8,128)(2,1)S(1)}, bf16[1,1,128,2048]{3,2,1,0:T(8,128)(2,1)}, u32[]{:S(2)}) %copy-start.2) | copy-done | bytes 524312
  10.4 1.0 %copy-done.3 = bf16[1,1,128,2048]{3,2,1,0:T(8,128)(2,1)S(1)} copy-done((bf16[1,1,128,2048]{3,2,1,0:T(8,128)(2,1)S(1)}, bf16[1,1,128,2048]{3,2,1,0:T(8,128)(2,1)}, u32[]{:S(2)}) %copy-start.3) | copy-done | bytes 524312
  11.4 0.7 copy-done.7
  12.2 0.7 collective-permute-done.refs_5_.refs_1_
  12.9 1.8 %collective-permute-start.6 = (bf16[512,384]{1,0:T(8,128)(2,1)}, bf16[512,384]{1,0:T(8,128)(2,1)S(1)}, u32[]{:S(2)}, u32[]{:S(2)}) collective-permute-start(bf16[512,384]{1,0:T(8,128)(2,1)} %hand_on.19), channel_id=1, source_target_pairs={{0,2},{1,3},{2,0},{3,1},{4,6},{5,7},{6,4},{7,5},{8,10},{9,11},{10,... | collective-permute-start | bytes 1179656 | tf_op jit(solution)/shard_map/ppermute | solution.py:395
  14.7 2.6 %attend.1 = (f32[128,2048]{1,0:T(8,128)S(1)}, bf16[96,2048]{1,0:T(8,128)(2,1)S(1)}, bf16[96,2048]{1,0:T(8,128)(2,1)S(1)}) custom-call(bf16[128,2048]{1,0:T(8,128)(2,1)S(1)} %get-tuple-element.34.refs_0_, bf16[128,2048]{1,0:T(8,128)(2,1)S(1)} %get-tuple-element.35.refs_1_, f32[1,2048]{1,0:T(1,128)S(1)} %get-tuple-element.36.refs_2_, ...), custom_call_target="tpu_custom_call" | custom-call | flops 134217728 | bytes 3145728 | tf_op jit(solution)/shard_map/attend/pallas_call | solution.py:154
  17.3 2.7 %collective-permute-start.8 = (bf16[96,2048]{1,0:T(8,128)(2,1)S(1)}, bf16[96,2048]{1,0:T(8,128)(2,1)S(1)}, u32[]{:S(2)}, u32[]{:S(2)}) collective-permute-start(bf16[96,2048]{1,0:T(8,128)(2,1)S(1)} %get-tuple-element.44), channel_id=1, source_target_pairs={{0,8},{1,9},{2,10},{3,11},{4,12},{5,13},{6,14},{7,15},{8,0},{9,1},... | collective-permute-start | bytes 1179656 | tf_op jit(solution)/shard_map/ppermute | solution.py:399
  19.9 1.6 %collective-permute-start.3 = (bf16[96,2048]{1,0:T(8,128)(2,1)S(1)}, bf16[96,2048]{1,0:T(8,128)(2,1)S(1)}, u32[]{:S(2)}, u32[]{:S(2)}) collective-permute-start(bf16[96,2048]{1,0:T(8,128)(2,1)S(1)} %get-tuple-element.41.refs_0_.own_in.refs_2_), channel_id=1, source_target_pairs={{0,4},{1,5},{2,6},{3,7},{4,0},{5,1},{6,2},{7,3},{8,12},{9,13},{10,... | collective-permute-start | bytes 1179656 | tf_op jit(solution)/shard_map/ppermute | solution.py:395
  21.5 0.7 hold_weights.1
  22.3 1.6 %collective-permute-start.5 = (bf16[512,384]{1,0:T(8,128)(2,1)S(1)}, bf16[512,384]{1,0:T(8,128)(2,1)S(1)}, u32[]{:S(2)}, u32[]{:S(2)}) collective-permute-start(bf16[512,384]{1,0:T(8,128)(2,1)S(1)} %hand_on.18.refs_1_.refs_0_), channel_id=1, source_target_pairs={{0,16},{16,0},{1,17},{17,1},{2,18},{18,2},{3,19},{19,3},{4,20},{20... | collective-permute-start | bytes 1179656 | tf_op jit(solution)/shard_map/ppermute | solution.py:403
  23.8 1.6 %collective-permute-done.6.refs_0_ = bf16[512,384]{1,0:T(8,128)(2,1)S(1)} collective-permute-done((bf16[512,384]{1,0:T(8,128)(2,1)}, bf16[512,384]{1,0:T(8,128)(2,1)S(1)}, u32[]{:S(2)}, u32[]{:S(2)}) %collective-permute-start.6) | collective-permute-done | bytes 393248 | tf_op jit(solution)/shard_map/ppermute | solution.py:395
  25.8 1.7 %collective-permute-start.14 = (bf16[112,2048]{1,0:T(8,128)(2,1)S(1)}, bf16[112,2048]{1,0:T(8,128)(2,1)S(1)}, u32[]{:S(2)}, u32[]{:S(2)}) collective-permute-start(bf16[112,2048]{1,0:T(8,128)(2,1)S(1)} %get-tuple-element.51), channel_id=1, source_target_pairs={{0,2},{1,3},{2,0},{3,1},{4,6},{5,7},{6,4},{7,5},{8,10},{9,11},{10,... | collective-permute-start | bytes 1376264 | tf_op jit(solution)/shard_map/ppermute | solution.py:395
  27.5 9.2 %collective-permute-done.8.refs_0_ = bf16[96,2048]{1,0:T(8,128)(2,1)S(1)} collective-permute-done((bf16[96,2048]{1,0:T(8,128)(2,1)S(1)}, bf16[96,2048]{1,0:T(8,128)(2,1)S(1)}, u32[]{:S(2)}, u32[]{:S(2)}) %collective-permute-start.8) | collective-permute-done | bytes 393248 | tf_op jit(solution)/shard_map/ppermute | solution.py:399
  36.9 1.4 %collective-permute-start.9 = (bf16[96,2048]{1,0:T(8,128)(2,1)S(1)}, bf16[96,2048]{1,0:T(8,128)(2,1)S(1)}, u32[]{:S(2)}, u32[]{:S(2)}) collective-permute-start(bf16[96,2048]{1,0:T(8,128)(2,1)S(1)} %hand_on.21.own_in.refs_2_), channel_id=1, source_target_pairs={{0,4},{1,5},{2,6},{3,7},{4,0},{5,1},{6,2},{7,3},{8,12},{9,13},{10,... | collective-permute-start | bytes 1179656 | tf_op jit(solution)/shard_map/ppermute | solution.py:395
  38.4 0.5 collective-permute-start.16
  38.9 1.3 %collective-permute-done.7.refs_3_.refs_1_ = bf16[512,384]{1,0:T(8,128)(2,1)S(1)} collective-permute-done((bf16[512,384]{1,0:T(8,128)(2,1)S(1)}, bf16[512,384]{1,0:T(8,128)(2,1)S(1)}, u32[]{:S(2)}, u32[]{:S(2)}) %collective-permute-start.7) | collective-permute-done | bytes 393248 | tf_op jit(solution)/shard_map/ppermute | solution.py:403
  40.2 1.6 %collective-permute-start.15 = (bf16[112,2048]{1,0:T(8,128)(2,1)S(1)}, bf16[112,2048]{1,0:T(8,128)(2,1)S(1)}, u32[]{:S(2)}, u32[]{:S(2)}) collective-permute-start(bf16[112,2048]{1,0:T(8,128)(2,1)S(1)} %hand_on.28.refs_4_), channel_id=1, source_target_pairs={{0,16},{16,0},{1,17},{17,1},{2,18},{18,2},{3,19},{19,3},{4,20},{20... | collective-permute-start | bytes 1376264 | tf_op jit(solution)/shard_map/ppermute | solution.py:403
  41.7 4.9 %collective-permute-done.9.refs_4_.refs_0_ = bf16[96,2048]{1,0:T(8,128)(2,1)S(1)} collective-permute-done((bf16[96,2048]{1,0:T(8,128)(2,1)S(1)}, bf16[96,2048]{1,0:T(8,128)(2,1)S(1)}, u32[]{:S(2)}, u32[]{:S(2)}) %collective-permute-start.9) | collective-permute-done | bytes 393248 | tf_op jit(solution)/shard_map/ppermute | solution.py:395
  46.7 0.5 collective-permute-start.11
  47.2 1.2 %collective-permute-done.10.refs_8_ = bf16[512,384]{1,0:T(8,128)(2,1)S(1)} collective-permute-done((bf16[512,384]{1,0:T(8,128)(2,1)S(1)}, bf16[512,384]{1,0:T(8,128)(2,1)S(1)}, u32[]{:S(2)}, u32[]{:S(2)}) %collective-permute-start.10) | collective-permute-done | bytes 393248 | tf_op jit(solution)/shard_map/ppermute | solution.py:395
  48.5 0.4 collective-permute-done.11.refs_9_
  49.1 0.8 expert_up.3.refs_1_
  50.1 0.6 collective-permute-done.13.refs_11_
  50.7 0.9 expert_up_y.2.refs_2_.refs_1_
  51.5 2.2 %collective-permute-done.16.refs_1_ = bf16[160,2048]{1,0:T(8,128)(2,1)S(1)} collective-permute-done((bf16[160,2048]{1,0:T(8,128)(2,1)S(1)}, bf16[160,2048]{1,0:T(8,128)(2,1)S(1)}, u32[]{:S(2)}, u32[]{:S(2)}) %collective-permute-start.16) | collective-permute-done | bytes 655392 | tf_op jit(solution)/shard_map/ppermute | solution.py:395
  53.8 0.5 collective-permute-start.18
  54.3 0.8 expert_up.2.refs_1_
  55.1 1.4 %collective-permute-done.18.refs_7_ = bf16[112,2048]{1,0:T(8,128)(2,1)S(1)} collective-permute-done((bf16[112,2048]{1,0:T(8,128)(2,1)S(1)}, bf16[112,2048]{1,0:T(8,128)(2,1)S(1)}, u32[]{:S(2)}, u32[]{:S(2)}) %collective-permute-start.18) | collective-permute-done | bytes 458784 | tf_op jit(solution)/shard_map/ppermute | solution.py:395
  56.5 0.5 expert_down.3
  57.0 0.4 collective-permute-start.22
  57.4 1.2 %expert_down.4 = (bf16[96,1536]{1,0:T(8,128)(2,1)S(1)}, bf16[96,1536]{1,0:T(8,128)(2,1)S(1)}) custom-call(s32[1]{0:T(128)} %bitcast.10.pipe_ref.refs_0_, bf16[192,1536]{1,0:T(8,128)(2,1)S(1)} %expert_up_y.2.refs_2_.refs_1_, bf16[384,2048]{1,0:T(8,128)(2,1)S(1)} %get-tuple-element.49.refs_2_, bf16[384,2048]{1,0:T(8,128)(2,1)S(1)} %collective-permute-done.2.refs_7_.refs_3_, ...), custom_call_target="tpu_custom_call" | custom-call | flops 905969664 | bytes 4718592 | tf_op jit(solution)/shard_map/expert_down/pallas_call | solution.py:321
  58.6 0.9 expert_up_y.3.refs_1_
  59.5 1.8 %collective-permute-start.20 = (bf16[96,1536]{1,0:T(8,128)(2,1)S(1)}, bf16[96,1536]{1,0:T(8,128)(2,1)S(1)}, u32[]{:S(2)}, u32[]{:S(2)}) collective-permute-start(bf16[96,1536]{1,0:T(8,128)(2,1)S(1)} %hand_on.30), channel_id=1, source_target_pairs={{0,4},{1,5},{2,6},{3,7},{4,0},{5,1},{6,2},{7,3},{8,12},{9,13},{10,... | collective-permute-start | bytes 884744 | tf_op jit(solution)/shard_map/ppermute | solution.py:395
  61.2 0.7 collective-permute-done.22.refs_0_
  62.0 3.4 %collective-permute-start.23 = (bf16[96,512]{1,0:T(8,128)(2,1)S(1)}, bf16[96,512]{1,0:T(8,128)(2,1)S(1)}, u32[]{:S(2)}, u32[]{:S(2)}) collective-permute-start(bf16[96,512]{1,0:T(8,128)(2,1)S(1)} %far_total.3), channel_id=1, source_target_pairs={{0,8},{1,9},{2,10},{3,11},{4,12},{5,13},{6,14},{7,15},{8,0},{9,1},... | collective-permute-start | bytes 294920 | tf_op jit(solution)/shard_map/ppermute | solution.py:399
  65.4 1.5 %expert_down.5 = (bf16[96,2048]{1,0:T(8,128)(2,1)S(1)}, bf16[96,2048]{1,0:T(8,128)(2,1)S(1)}) custom-call(s32[1]{0:T(128)} %bitcast.10.pipe_ref.refs_0_, bf16[192,1536]{1,0:T(8,128)(2,1)S(1)} %expert_up_y.3.refs_1_, bf16[384,2048]{1,0:T(8,128)(2,1)S(1)} %get-tuple-element.49.refs_2_, bf16[384,2048]{1,0:T(8,128)(2,1)S(1)} %collective-permute-done.2.refs_7_.refs_3_, ...), custom_call_target="tpu_custom_call" | custom-call | flops 1207959552 | bytes 6291456 | tf_op jit(solution)/shard_map/expert_down/pallas_call | solution.py:321
  66.9 3.5 %collective-permute-done.20.z_ref = bf16[96,1536]{1,0:T(8,128)(2,1)S(1)} collective-permute-done((bf16[96,1536]{1,0:T(8,128)(2,1)S(1)}, bf16[96,1536]{1,0:T(8,128)(2,1)S(1)}, u32[]{:S(2)}, u32[]{:S(2)}) %collective-permute-start.20) | collective-permute-done | bytes 294944 | tf_op jit(solution)/shard_map/ppermute | solution.py:395
  70.5 0.7 collective-permute-start.21
  71.2 4.4 %collective-permute-start.24 = (bf16[96,1536]{1,0:T(8,128)(2,1)S(1)}, bf16[96,1536]{1,0:T(8,128)(2,1)S(1)}, u32[]{:S(2)}, u32[]{:S(2)}) collective-permute-start(bf16[96,1536]{1,0:T(8,128)(2,1)S(1)} %get-tuple-element.62.refs_1_), channel_id=1, source_target_pairs={{0,8},{1,9},{2,10},{3,11},{4,12},{5,13},{6,14},{7,15},{8,0},{9,1},... | collective-permute-start | bytes 884744 | tf_op jit(solution)/shard_map/ppermute | solution.py:399
  75.6 9.1 %collective-permute-done.24.refs_6_ = bf16[96,1536]{1,0:T(8,128)(2,1)S(1)} collective-permute-done((bf16[96,1536]{1,0:T(8,128)(2,1)S(1)}, bf16[96,1536]{1,0:T(8,128)(2,1)S(1)}, u32[]{:S(2)}, u32[]{:S(2)}) %collective-permute-start.24) | collective-permute-done | bytes 294944 | tf_op jit(solution)/shard_map/ppermute | solution.py:399
  84.7 2.1 %collective-permute-done.21.refs_4_ = bf16[96,2048]{1,0:T(8,128)(2,1)S(1)} collective-permute-done((bf16[96,2048]{1,0:T(8,128)(2,1)S(1)}, bf16[96,2048]{1,0:T(8,128)(2,1)S(1)}, u32[]{:S(2)}, u32[]{:S(2)}) %collective-permute-start.21) | collective-permute-done | bytes 393248 | tf_op jit(solution)/shard_map/ppermute | solution.py:395
  86.9 1.2 %finish.1 = bf16[128,2048]{1,0:T(8,128)(2,1)} custom-call(f32[128,2048]{1,0:T(8,128)S(1)} %get-tuple-element.38.refs_0_, f32[128,1]{1,0:T(8,128)S(1)} %get-tuple-element.39.refs_1_, s32[128,1]{1,0:T(8,128)S(1)} %get-tuple-element.40.refs_2_, bf16[96,2048]{1,0:T(8,128)(2,1)S(1)} %get-tuple-element.57.refs_3_, ...), custom_call_target="tpu_custom_call" | custom-call | flops 201326592 | bytes 4194304 | tf_op jit(solution)/shard_map/finish/pallas_call | solution.py:377
  (53 shorter events, 1.5 us)
Async XLA Ops:
  0.0 2.3 %copy-start.8 = (bf16[1,32,2,2048]{3,2,1,0:T(2,128)(2,1)S(1)}, bf16[1,32,2,2048]{3,2,1,0:T(2,128)(2,1)}, u32[]{:S(2)}) copy-start(bf16[1,32,2,2048]{3,2,1,0:T(2,128)(2,1)} %param.11) | copy-start | bytes 786436
  0.0 14.7 %collective-permute-start.2 = (bf16[384,2048]{1,0:T(8,128)(2,1)}, bf16[384,2048]{1,0:T(8,128)(2,1)S(1)}, u32[]{:S(2)}, u32[]{:S(2)}) collective-permute-start(bf16[384,2048]{1,0:T(8,128)(2,1)} %w_out.1), channel_id=1, source_target_pairs={{0,1},{1,0},{2,3},{3,2},{4,5},{5,4},{6,7},{7,6},{8,9},{9,8},{10,11... | collective-permute-start | bytes 4718600 | tf_op jit(solution)/shard_map/ppermute | solution.py:395
  0.5 14.2 %collective-permute-start.1 = (bf16[2048,384]{1,0:T(8,128)(2,1)}, bf16[2048,384]{1,0:T(8,128)(2,1)S(1)}, u32[]{:S(2)}, u32[]{:S(2)}) collective-permute-start(bf16[2048,384]{1,0:T(8,128)(2,1)} %whole.3), channel_id=1, source_target_pairs={{0,1},{1,0},{2,3},{3,2},{4,5},{5,4},{6,7},{7,6},{8,9},{9,8},{10,11... | collective-permute-start | bytes 4718600 | tf_op jit(solution)/shard_map/ppermute | solution.py:395
  3.1 6.2 %copy-start.4 = (f32[2048]{0:T(1024)S(1)}, f32[2048]{0:T(1024)}, u32[]{:S(2)}) copy-start(f32[2048]{0:T(1024)} %param.12) | copy-start | bytes 24580
  3.1 6.2 %copy-start.5 = (s32[1,1,128]{2,1,0:T(1,128)S(1)}, s32[1,1,128]{2,1,0:T(1,128)}, u32[]{:S(2)}) copy-start(s32[1,1,128]{2,1,0:T(1,128)} %param.15) | copy-start | bytes 1540
  3.1 6.2 %copy-start.6 = (s32[1,1,128]{2,1,0:T(1,128)S(1)}, s32[1,1,128]{2,1,0:T(1,128)}, u32[]{:S(2)}) copy-start(s32[1,1,128]{2,1,0:T(1,128)} %param.16) | copy-start | bytes 1540
  3.1 9.8 %collective-permute-start = (bf16[64,2048]{1,0:T(8,128)(2,1)}, bf16[64,2048]{1,0:T(8,128)(2,1)}, u32[]{:S(2)}, u32[]{:S(2)}) collective-permute-start(bf16[64,2048]{1,0:T(8,128)(2,1)} %hand_on.17.refs_4_), channel_id=1, source_target_pairs={{0,16},{16,0},{1,17},{17,1},{2,18},{18,2},{3,19},{19,3},{4,20},{20... | collective-permute-start | bytes 786440 | tf_op jit(solution)/shard_map/ppermute | solution.py:418
  6.0 16.2 %collective-permute-start.4 = (bf16[512,384]{1,0:T(8,128)(2,1)}, bf16[512,384]{1,0:T(8,128)(2,1)S(1)}, u32[]{:S(2)}, u32[]{:S(2)}) collective-permute-start(bf16[512,384]{1,0:T(8,128)(2,1)} %weight_part.2.refs_1_), channel_id=1, source_target_pairs={{0,2},{1,3},{2,0},{3,1},{4,6},{5,7},{6,4},{7,5},{8,10},{9,11},{10,... | collective-permute-start | bytes 1179656 | tf_op jit(solution)/shard_map/ppermute | solution.py:395
  9.3 1.0 %copy-start.2 = (bf16[1,1,128,2048]{3,2,1,0:T(8,128)(2,1)S(1)}, bf16[1,1,128,2048]{3,2,1,0:T(8,128)(2,1)}, u32[]{:S(2)}) copy-start(bf16[1,1,128,2048]{3,2,1,0:T(8,128)(2,1)} %param.9) | copy-start | bytes 1572868
  10.4 1.0 %copy-start.3 = (bf16[1,1,128,2048]{3,2,1,0:T(8,128)(2,1)S(1)}, bf16[1,1,128,2048]{3,2,1,0:T(8,128)(2,1)}, u32[]{:S(2)}) copy-start(bf16[1,1,128,2048]{3,2,1,0:T(8,128)(2,1)} %param.10) | copy-start | bytes 1572868
  11.4 0.7 copy-start.7
  12.9 12.6 %collective-permute-start.6 = (bf16[512,384]{1,0:T(8,128)(2,1)}, bf16[512,384]{1,0:T(8,128)(2,1)S(1)}, u32[]{:S(2)}, u32[]{:S(2)}) collective-permute-start(bf16[512,384]{1,0:T(8,128)(2,1)} %hand_on.19), channel_id=1, source_target_pairs={{0,2},{1,3},{2,0},{3,1},{4,6},{5,7},{6,4},{7,5},{8,10},{9,11},{10,... | collective-permute-start | bytes 1179656 | tf_op jit(solution)/shard_map/ppermute | solution.py:395
  14.7 6.9 %copy-start = (bf16[2048,384]{1,0:T(8,128)(2,1)S(1)}, bf16[2048,384]{1,0:T(8,128)(2,1)}, u32[]{:S(2)}) copy-start(bf16[2048,384]{1,0:T(8,128)(2,1)} %whole.3) | copy-start | bytes 4718596
  14.7 6.9 %copy-start.1 = (bf16[384,2048]{1,0:T(8,128)(2,1)S(1)}, bf16[384,2048]{1,0:T(8,128)(2,1)}, u32[]{:S(2)}) copy-start(bf16[384,2048]{1,0:T(8,128)(2,1)} %w_out.1) | copy-start | bytes 4718596
  17.3 19.5 %collective-permute-start.8 = (bf16[96,2048]{1,0:T(8,128)(2,1)S(1)}, bf16[96,2048]{1,0:T(8,128)(2,1)S(1)}, u32[]{:S(2)}, u32[]{:S(2)}) collective-permute-start(bf16[96,2048]{1,0:T(8,128)(2,1)S(1)} %get-tuple-element.44), channel_id=1, source_target_pairs={{0,8},{1,9},{2,10},{3,11},{4,12},{5,13},{6,14},{7,15},{8,0},{9,1},... | collective-permute-start | bytes 1179656 | tf_op jit(solution)/shard_map/ppermute | solution.py:399
  19.9 17.0 %collective-permute-start.3 = (bf16[96,2048]{1,0:T(8,128)(2,1)S(1)}, bf16[96,2048]{1,0:T(8,128)(2,1)S(1)}, u32[]{:S(2)}, u32[]{:S(2)}) collective-permute-start(bf16[96,2048]{1,0:T(8,128)(2,1)S(1)} %get-tuple-element.41.refs_0_.own_in.refs_2_), channel_id=1, source_target_pairs={{0,4},{1,5},{2,6},{3,7},{4,0},{5,1},{6,2},{7,3},{8,12},{9,13},{10,... | collective-permute-start | bytes 1179656 | tf_op jit(solution)/shard_map/ppermute | solution.py:395
  22.3 19.5 %collective-permute-start.5 = (bf16[512,384]{1,0:T(8,128)(2,1)S(1)}, bf16[512,384]{1,0:T(8,128)(2,1)S(1)}, u32[]{:S(2)}, u32[]{:S(2)}) collective-permute-start(bf16[512,384]{1,0:T(8,128)(2,1)S(1)} %hand_on.18.refs_1_.refs_0_), channel_id=1, source_target_pairs={{0,16},{16,0},{1,17},{17,1},{2,18},{18,2},{3,19},{19,3},{4,20},{20... | collective-permute-start | bytes 1179656 | tf_op jit(solution)/shard_map/ppermute | solution.py:403
  25.5 14.7 %collective-permute-start.7 = (bf16[512,384]{1,0:T(8,128)(2,1)S(1)}, bf16[512,384]{1,0:T(8,128)(2,1)S(1)}, u32[]{:S(2)}, u32[]{:S(2)}) collective-permute-start(bf16[512,384]{1,0:T(8,128)(2,1)S(1)} %hand_on.20.refs_2_), channel_id=1, source_target_pairs={{0,16},{16,0},{1,17},{17,1},{2,18},{18,2},{3,19},{19,3},{4,20},{20... | collective-permute-start | bytes 1179656 | tf_op jit(solution)/shard_map/ppermute | solution.py:403
  25.8 14.4 %collective-permute-start.14 = (bf16[112,2048]{1,0:T(8,128)(2,1)S(1)}, bf16[112,2048]{1,0:T(8,128)(2,1)S(1)}, u32[]{:S(2)}, u32[]{:S(2)}) collective-permute-start(bf16[112,2048]{1,0:T(8,128)(2,1)S(1)} %get-tuple-element.51), channel_id=1, source_target_pairs={{0,2},{1,3},{2,0},{3,1},{4,6},{5,7},{6,4},{7,5},{8,10},{9,11},{10,... | collective-permute-start | bytes 1376264 | tf_op jit(solution)/shard_map/ppermute | solution.py:395
  36.9 9.7 %collective-permute-start.9 = (bf16[96,2048]{1,0:T(8,128)(2,1)S(1)}, bf16[96,2048]{1,0:T(8,128)(2,1)S(1)}, u32[]{:S(2)}, u32[]{:S(2)}) collective-permute-start(bf16[96,2048]{1,0:T(8,128)(2,1)S(1)} %hand_on.21.own_in.refs_2_), channel_id=1, source_target_pairs={{0,4},{1,5},{2,6},{3,7},{4,0},{5,1},{6,2},{7,3},{8,12},{9,13},{10,... | collective-permute-start | bytes 1179656 | tf_op jit(solution)/shard_map/ppermute | solution.py:395
  38.4 15.3 %collective-permute-start.16 = (bf16[160,2048]{1,0:T(8,128)(2,1)S(1)}, bf16[160,2048]{1,0:T(8,128)(2,1)S(1)}, u32[]{:S(2)}, u32[]{:S(2)}) collective-permute-start(bf16[160,2048]{1,0:T(8,128)(2,1)S(1)} %get-tuple-element.52), channel_id=1, source_target_pairs={{0,2},{1,3},{2,0},{3,1},{4,6},{5,7},{6,4},{7,5},{8,10},{9,11},{10,... | collective-permute-start | bytes 1966088 | tf_op jit(solution)/shard_map/ppermute | solution.py:395
  40.2 13.5 %collective-permute-start.17 = (bf16[112,2048]{1,0:T(8,128)(2,1)S(1)}, bf16[112,2048]{1,0:T(8,128)(2,1)S(1)}, u32[]{:S(2)}, u32[]{:S(2)}) collective-permute-start(bf16[112,2048]{1,0:T(8,128)(2,1)S(1)} %hand_on.28.refs_4_), channel_id=1, source_target_pairs={{0,1},{1,0},{2,3},{3,2},{4,5},{5,4},{6,7},{7,6},{8,9},{9,8},{10,11... | collective-permute-start | bytes 1376264 | tf_op jit(solution)/shard_map/ppermute | solution.py:395
  40.2 13.5 %collective-permute-start.15 = (bf16[112,2048]{1,0:T(8,128)(2,1)S(1)}, bf16[112,2048]{1,0:T(8,128)(2,1)S(1)}, u32[]{:S(2)}, u32[]{:S(2)}) collective-permute-start(bf16[112,2048]{1,0:T(8,128)(2,1)S(1)} %hand_on.28.refs_4_), channel_id=1, source_target_pairs={{0,16},{16,0},{1,17},{17,1},{2,18},{18,2},{3,19},{19,3},{4,20},{20... | collective-permute-start | bytes 1376264 | tf_op jit(solution)/shard_map/ppermute | solution.py:403
  46.7 1.7 %collective-permute-start.10 = (bf16[512,384]{1,0:T(8,128)(2,1)S(1)}, bf16[512,384]{1,0:T(8,128)(2,1)S(1)}, u32[]{:S(2)}, u32[]{:S(2)}) collective-permute-start(bf16[512,384]{1,0:T(8,128)(2,1)S(1)} %get-tuple-element.45.refs_4_), channel_id=1, source_target_pairs={{0,1},{1,0},{2,3},{3,2},{4,5},{5,4},{6,7},{7,6},{8,9},{9,8},{10,11... | collective-permute-start | bytes 1179656 | tf_op jit(solution)/shard_map/ppermute | solution.py:395
  46.7 2.3 %collective-permute-start.11 = (bf16[512,384]{1,0:T(8,128)(2,1)S(1)}, bf16[512,384]{1,0:T(8,128)(2,1)S(1)}, u32[]{:S(2)}, u32[]{:S(2)}) collective-permute-start(bf16[512,384]{1,0:T(8,128)(2,1)S(1)} %get-tuple-element.46.refs_5_), channel_id=1, source_target_pairs={{0,1},{1,0},{2,3},{3,2},{4,5},{5,4},{6,7},{7,6},{8,9},{9,8},{10,11... | collective-permute-start | bytes 1179656 | tf_op jit(solution)/shard_map/ppermute | solution.py:395
  48.4 1.7 %collective-permute-start.12 = (bf16[512,384]{1,0:T(8,128)(2,1)S(1)}, bf16[512,384]{1,0:T(8,128)(2,1)S(1)}, u32[]{:S(2)}, u32[]{:S(2)}) collective-permute-start(bf16[512,384]{1,0:T(8,128)(2,1)S(1)} %get-tuple-element.47.refs_6_), channel_id=1, source_target_pairs={{0,1},{1,0},{2,3},{3,2},{4,5},{5,4},{6,7},{7,6},{8,9},{9,8},{10,11... | collective-permute-start | bytes 1179656 | tf_op jit(solution)/shard_map/ppermute | solution.py:395
  48.9 1.7 %collective-permute-start.13 = (bf16[512,384]{1,0:T(8,128)(2,1)S(1)}, bf16[512,384]{1,0:T(8,128)(2,1)S(1)}, u32[]{:S(2)}, u32[]{:S(2)}) collective-permute-start(bf16[512,384]{1,0:T(8,128)(2,1)S(1)} %get-tuple-element.48.refs_7_), channel_id=1, source_target_pairs={{0,1},{1,0},{2,3},{3,2},{4,5},{5,4},{6,7},{7,6},{8,9},{9,8},{10,11... | collective-permute-start | bytes 1179656 | tf_op jit(solution)/shard_map/ppermute | solution.py:395
  53.7 2.8 %collective-permute-start.19 = (bf16[160,2048]{1,0:T(8,128)(2,1)S(1)}, bf16[160,2048]{1,0:T(8,128)(2,1)S(1)}, u32[]{:S(2)}, u32[]{:S(2)}) collective-permute-start(bf16[160,2048]{1,0:T(8,128)(2,1)S(1)} %get-tuple-element.54.refs_8_), channel_id=1, source_target_pairs={{0,1},{1,0},{2,3},{3,2},{4,5},{5,4},{6,7},{7,6},{8,9},{9,8},{10,11... | collective-permute-start | bytes 1966088 | tf_op jit(solution)/shard_map/ppermute | solution.py:395
  53.8 2.7 %collective-permute-start.18 = (bf16[112,2048]{1,0:T(8,128)(2,1)S(1)}, bf16[112,2048]{1,0:T(8,128)(2,1)S(1)}, u32[]{:S(2)}, u32[]{:S(2)}) collective-permute-start(bf16[112,2048]{1,0:T(8,128)(2,1)S(1)} %get-tuple-element.53.refs_5_), channel_id=1, source_target_pairs={{0,1},{1,0},{2,3},{3,2},{4,5},{5,4},{6,7},{7,6},{8,9},{9,8},{10,11... | collective-permute-start | bytes 1376264 | tf_op jit(solution)/shard_map/ppermute | solution.py:395
  57.0 4.9 %collective-permute-start.22 = (bf16[96,512]{1,0:T(8,128)(2,1)S(1)}, bf16[96,512]{1,0:T(8,128)(2,1)S(1)}, u32[]{:S(2)}, u32[]{:S(2)}) collective-permute-start(bf16[96,512]{1,0:T(8,128)(2,1)S(1)} %get-tuple-element.61), channel_id=1, source_target_pairs={{0,4},{1,5},{2,6},{3,7},{4,0},{5,1},{6,2},{7,3},{8,12},{9,13},{10,... | collective-permute-start | bytes 294920 | tf_op jit(solution)/shard_map/ppermute | solution.py:395
  59.5 10.9 %collective-permute-start.20 = (bf16[96,1536]{1,0:T(8,128)(2,1)S(1)}, bf16[96,1536]{1,0:T(8,128)(2,1)S(1)}, u32[]{:S(2)}, u32[]{:S(2)}) collective-permute-start(bf16[96,1536]{1,0:T(8,128)(2,1)S(1)} %hand_on.30), channel_id=1, source_target_pairs={{0,4},{1,5},{2,6},{3,7},{4,0},{5,1},{6,2},{7,3},{8,12},{9,13},{10,... | collective-permute-start | bytes 884744 | tf_op jit(solution)/shard_map/ppermute | solution.py:395
  62.0 13.7 %collective-permute-start.23 = (bf16[96,512]{1,0:T(8,128)(2,1)S(1)}, bf16[96,512]{1,0:T(8,128)(2,1)S(1)}, u32[]{:S(2)}, u32[]{:S(2)}) collective-permute-start(bf16[96,512]{1,0:T(8,128)(2,1)S(1)} %far_total.3), channel_id=1, source_target_pairs={{0,8},{1,9},{2,10},{3,11},{4,12},{5,13},{6,14},{7,15},{8,0},{9,1},... | collective-permute-start | bytes 294920 | tf_op jit(solution)/shard_map/ppermute | solution.py:399
  70.5 16.4 %collective-permute-start.21 = (bf16[96,2048]{1,0:T(8,128)(2,1)S(1)}, bf16[96,2048]{1,0:T(8,128)(2,1)S(1)}, u32[]{:S(2)}, u32[]{:S(2)}) collective-permute-start(bf16[96,2048]{1,0:T(8,128)(2,1)S(1)} %get-tuple-element.60), channel_id=1, source_target_pairs={{0,4},{1,5},{2,6},{3,7},{4,0},{5,1},{6,2},{7,3},{8,12},{9,13},{10,... | collective-permute-start | bytes 1179656 | tf_op jit(solution)/shard_map/ppermute | solution.py:395
  71.2 13.5 %collective-permute-start.24 = (bf16[96,1536]{1,0:T(8,128)(2,1)S(1)}, bf16[96,1536]{1,0:T(8,128)(2,1)S(1)}, u32[]{:S(2)}, u32[]{:S(2)}) collective-permute-start(bf16[96,1536]{1,0:T(8,128)(2,1)S(1)} %get-tuple-element.62.refs_1_), channel_id=1, source_target_pairs={{0,8},{1,9},{2,10},{3,11},{4,12},{5,13},{6,14},{7,15},{8,0},{9,1},... | collective-permute-start | bytes 884744 | tf_op jit(solution)/shard_map/ppermute | solution.py:399

commit v17 on v14

--- a/solution.py
+++ b/solution.py
@@ -210,7 +210,7 @@
 
 def hold(pipe, w_in, w_out, pipes, after):
     units, width = w_out.shape
-    size = units * 7 // 12 // pipes // 16 * 16
+    size = units * 2 // 3 // pipes // 16 * 16
     return call(
         functools.partial(hold_kernel, pipes),
         [
@@ -436,9 +436,9 @@
     far = [groups_on(block, count) for count, block in enumerate(packed, 1)]
     far = jnp.concatenate(far, axis=0) if len(far) > 1 else far[0]
 
-    w_in_held, w_out_held, out_part, out_rest = hold(pipe, w_in, w_out, pipes, [near])
-    in_first = along(*after_all([in_y], [out_part]))
-    in_last = after_all([in_late], [in_first[0]])
+    in_first = along(*after_all([in_y], [near]))
+    w_in_held, w_out_held, out_part, out_rest = hold(pipe, w_in, w_out, pipes, in_first[:1])
+    in_last = after_all([in_late], [in_first[0], out_part])
     out_part, out_rest = after_all([out_part, out_rest], in_last)
     in_last = along(*in_last)
     out_y, rest_y = across(out_part, 2), across(out_rest, 2)

time: 87.3 us -> 88.7 us (1.016)
  waiting for transfers between devices: 41.3 us -> 44.5 us
  starting transfers between devices: 26.8 us -> 25.7 us
    ppermute x18, waiting for transfers between devices: 19.6 us -> 21.5 us  [across(): return lax.ppermute(value, 'expert', [(i, i ^ bit) for i in range(devices)])]
    ppermute x3, waiting for transfers between devices: 1.29 us -> 2.62 us  [along(): return [value] + [lax.ppermute(value, 'pipe', perm) for perm in perms]]
    ppermute x3, starting transfers between devices: 7.77 us -> 6.82 us  [groups_on(): lax.ppermute(value, 'expert', [(i, (i + shift) % devices) for i in range(...]
  transfers between devices with their start and end apart: 25 -> 25, of which waited for: 17 -> 18; matrix products, arithmetic and copies ran while one was open for 1% -> 1% of each run, Pallas kernels for 15% -> 14%
where the time goes in v17:
time: 88.7 us; the launch traced here: 88.4 us
  waiting for transfers between devices  44.5 us (50%)
  starting transfers between devices  25.7 us (29%)
  Pallas kernels  14.4 us (16%)
  local copies, waits for them, and re-layouts  3.56 us (4%)
    ppermute x18, waiting for transfers between devices, across(): return lax.ppermute(value, 'expert', [(i, i ^ bit) for i in range(devices)])  21.5 us
    ppermute x3, waiting for transfers between devices, groups_on(): lax.ppermute(value, 'expert', [(i, (i + shift) % devices) for i in range(...  19.8 us
    ppermute x18, starting transfers between devices, across(): return lax.ppermute(value, 'expert', [(i, i ^ bit) for i in range(devices)])  12.6 us
    ppermute x3, starting transfers between devices, groups_on(): lax.ppermute(value, 'expert', [(i, (i + shift) % devices) for i in range(...  6.82 us
    pallas_call x2, Pallas kernels, cut_part(): call(functools.partial(part_kernel, stride, first), struct((size, whole.s...  3.49 us
    ppermute x3, starting transfers between devices, along(): return [value] + [lax.ppermute(value, 'pipe', perm) for perm in perms]  3.39 us
    pallas_call x3, Pallas kernels, down(): call(functools.partial(down_kernel, pipes, first), [struct((rows, width))...  3.23 us
    ppermute x1, starting transfers between devices, body(): kv_pieces.append(lax.ppermute(kv, 'pipe', perm))  2.93 us
  transfers between devices with their start and end apart: 25, of which 18 were waited for; matrix products, arithmetic and copies ran while one was open for 1% of the time, Pallas kernels for 14%

profile of v17, /device:TPU:0, one launch (start us, length us, event | category | flops | bytes accessed | tf_op | source)
XLA Modules:
  0.0 88.4 jit_solution(15970599548050145298)
XLA Ops:
  0.0 0.5 collective-permute-start.2
  0.5 1.7 %weight_part.2.refs_1_ = bf16[512,384]{1,0:T(8,128)(2,1)} custom-call(s32[1]{0:T(128)} %bitcast.10.pipe_ref.refs_0_, bf16[2048,384]{1,0:T(8,128)(2,1)} %whole.3), custom_call_target="tpu_custom_call" | custom-call | flops 1 | bytes 786432 | tf_op jit(solution)/shard_map/weight_part/pallas_call | solution.py:178
  2.3 0.8 copy.32
  3.1 2.9 %collective-permute-start = (bf16[64,2048]{1,0:T(8,128)(2,1)}, bf16[64,2048]{1,0:T(8,128)(2,1)}, u32[]{:S(2)}, u32[]{:S(2)}) collective-permute-start(bf16[64,2048]{1,0:T(8,128)(2,1)} %hand_on.16.refs_4_), channel_id=1, source_target_pairs={{0,16},{16,0},{1,17},{17,1},{2,18},{18,2},{3,19},{19,3},{4,20},{20... | collective-permute-start | bytes 786440 | tf_op jit(solution)/shard_map/ppermute | solution.py:416
  6.0 1.5 %collective-permute-start.4 = (bf16[512,384]{1,0:T(8,128)(2,1)}, bf16[512,384]{1,0:T(8,128)(2,1)S(1)}, u32[]{:S(2)}, u32[]{:S(2)}) collective-permute-start(bf16[512,384]{1,0:T(8,128)(2,1)} %weight_part.2.refs_1_), channel_id=1, source_target_pairs={{0,2},{1,3},{2,0},{3,1},{4,6},{5,7},{6,4},{7,5},{8,10},{9,11},{10,... | collective-permute-start | bytes 1179656 | tf_op jit(solution)/shard_map/ppermute | solution.py:393
  7.6 1.7 %weight_part.3.refs_0_ = bf16[512,384]{1,0:T(8,128)(2,1)} custom-call(s32[1]{0:T(128)} %bitcast.10.pipe_ref.refs_0_, bf16[2048,384]{1,0:T(8,128)(2,1)} %whole.3), custom_call_target="tpu_custom_call" | custom-call | flops 1 | bytes 786432 | tf_op jit(solution)/shard_map/weight_part/pallas_call | solution.py:178
  9.4 1.0 %copy-done.2 = bf16[1,1,128,2048]{3,2,1,0:T(8,128)(2,1)S(1)} copy-done((bf16[1,1,128,2048]{3,2,1,0:T(8,128)(2,1)S(1)}, bf16[1,1,128,2048]{3,2,1,0:T(8,128)(2,1)}, u32[]{:S(2)}) %copy-start.2) | copy-done | bytes 524312
  10.4 1.0 %copy-done.3 = bf16[1,1,128,2048]{3,2,1,0:T(8,128)(2,1)S(1)} copy-done((bf16[1,1,128,2048]{3,2,1,0:T(8,128)(2,1)S(1)}, bf16[1,1,128,2048]{3,2,1,0:T(8,128)(2,1)}, u32[]{:S(2)}) %copy-start.3) | copy-done | bytes 524312
  11.4 0.7 copy-done.7
  12.2 0.7 collective-permute-done.refs_5_.refs_1_
  12.9 1.8 %collective-permute-start.6 = (bf16[512,384]{1,0:T(8,128)(2,1)}, bf16[512,384]{1,0:T(8,128)(2,1)S(1)}, u32[]{:S(2)}, u32[]{:S(2)}) collective-permute-start(bf16[512,384]{1,0:T(8,128)(2,1)} %hand_on.18), channel_id=1, source_target_pairs={{0,2},{1,3},{2,0},{3,1},{4,6},{5,7},{6,4},{7,5},{8,10},{9,11},{10,... | collective-permute-start | bytes 1179656 | tf_op jit(solution)/shard_map/ppermute | solution.py:393
  14.7 2.6 %attend.1 = (f32[128,2048]{1,0:T(8,128)S(1)}, bf16[96,2048]{1,0:T(8,128)(2,1)S(1)}, bf16[96,2048]{1,0:T(8,128)(2,1)S(1)}) custom-call(bf16[128,2048]{1,0:T(8,128)(2,1)S(1)} %get-tuple-element.34.refs_0_, bf16[128,2048]{1,0:T(8,128)(2,1)S(1)} %get-tuple-element.35.refs_1_, f32[1,2048]{1,0:T(1,128)S(1)} %get-tuple-element.36.refs_2_, ...), custom_call_target="tpu_custom_call" | custom-call | flops 134217728 | bytes 3145728 | tf_op jit(solution)/shard_map/attend/pallas_call | solution.py:153
  17.3 2.7 %collective-permute-start.8 = (bf16[96,2048]{1,0:T(8,128)(2,1)S(1)}, bf16[96,2048]{1,0:T(8,128)(2,1)S(1)}, u32[]{:S(2)}, u32[]{:S(2)}) collective-permute-start(bf16[96,2048]{1,0:T(8,128)(2,1)S(1)} %get-tuple-element.44), channel_id=1, source_target_pairs={{0,8},{1,9},{2,10},{3,11},{4,12},{5,13},{6,14},{7,15},{8,0},{9,1},... | collective-permute-start | bytes 1179656 | tf_op jit(solution)/shard_map/ppermute | solution.py:397
  19.9 1.6 %collective-permute-start.3 = (bf16[96,2048]{1,0:T(8,128)(2,1)S(1)}, bf16[96,2048]{1,0:T(8,128)(2,1)S(1)}, u32[]{:S(2)}, u32[]{:S(2)}) collective-permute-start(bf16[96,2048]{1,0:T(8,128)(2,1)S(1)} %get-tuple-element.41.refs_1_.own_in.refs_2_), channel_id=1, source_target_pairs={{0,4},{1,5},{2,6},{3,7},{4,0},{5,1},{6,2},{7,3},{8,12},{9,13},{10,... | collective-permute-start | bytes 1179656 | tf_op jit(solution)/shard_map/ppermute | solution.py:393
  21.5 1.5 %collective-permute-start.5 = (bf16[512,384]{1,0:T(8,128)(2,1)S(1)}, bf16[512,384]{1,0:T(8,128)(2,1)S(1)}, u32[]{:S(2)}, u32[]{:S(2)}) collective-permute-start(bf16[512,384]{1,0:T(8,128)(2,1)S(1)} %hand_on.17.refs_0_.refs_1_), channel_id=1, source_target_pairs={{0,16},{16,0},{1,17},{17,1},{2,18},{18,2},{3,19},{19,3},{4,20},{20... | collective-permute-start | bytes 1179656 | tf_op jit(solution)/shard_map/ppermute | solution.py:401
  23.4 2.1 %collective-permute-done.6.refs_0_ = bf16[512,384]{1,0:T(8,128)(2,1)S(1)} collective-permute-done((bf16[512,384]{1,0:T(8,128)(2,1)}, bf16[512,384]{1,0:T(8,128)(2,1)S(1)}, u32[]{:S(2)}, u32[]{:S(2)}) %collective-permute-start.6) | collective-permute-done | bytes 393248 | tf_op jit(solution)/shard_map/ppermute | solution.py:393
  25.8 1.7 %collective-permute-start.14 = (bf16[128,2048]{1,0:T(8,128)(2,1)S(1)}, bf16[128,2048]{1,0:T(8,128)(2,1)S(1)}, u32[]{:S(2)}, u32[]{:S(2)}) collective-permute-start(bf16[128,2048]{1,0:T(8,128)(2,1)S(1)} %get-tuple-element.51), channel_id=1, source_target_pairs={{0,2},{1,3},{2,0},{3,1},{4,6},{5,7},{6,4},{7,5},{8,10},{9,11},{10,... | collective-permute-start | bytes 1572872 | tf_op jit(solution)/shard_map/ppermute | solution.py:393
  27.5 9.2 %collective-permute-done.8.refs_0_ = bf16[96,2048]{1,0:T(8,128)(2,1)S(1)} collective-permute-done((bf16[96,2048]{1,0:T(8,128)(2,1)S(1)}, bf16[96,2048]{1,0:T(8,128)(2,1)S(1)}, u32[]{:S(2)}, u32[]{:S(2)}) %collective-permute-start.8) | collective-permute-done | bytes 393248 | tf_op jit(solution)/shard_map/ppermute | solution.py:397
  36.9 1.4 %collective-permute-start.9 = (bf16[96,2048]{1,0:T(8,128)(2,1)S(1)}, bf16[96,2048]{1,0:T(8,128)(2,1)S(1)}, u32[]{:S(2)}, u32[]{:S(2)}) collective-permute-start(bf16[96,2048]{1,0:T(8,128)(2,1)S(1)} %hand_on.20.own_in.refs_2_), channel_id=1, source_target_pairs={{0,4},{1,5},{2,6},{3,7},{4,0},{5,1},{6,2},{7,3},{8,12},{9,13},{10,... | collective-permute-start | bytes 1179656 | tf_op jit(solution)/shard_map/ppermute | solution.py:393
  38.4 0.5 collective-permute-start.16
  38.9 0.5 collective-permute-done.7.refs_3_.refs_1_
  39.4 1.5 %collective-permute-start.15 = (bf16[128,2048]{1,0:T(8,128)(2,1)S(1)}, bf16[128,2048]{1,0:T(8,128)(2,1)S(1)}, u32[]{:S(2)}, u32[]{:S(2)}) collective-permute-start(bf16[128,2048]{1,0:T(8,128)(2,1)S(1)} %hand_on.27.refs_4_), channel_id=1, source_target_pairs={{0,16},{16,0},{1,17},{17,1},{2,18},{18,2},{3,19},{19,3},{4,20},{20... | collective-permute-start | bytes 1572872 | tf_op jit(solution)/shard_map/ppermute | solution.py:401
  40.9 5.7 %collective-permute-done.9.refs_4_.refs_0_ = bf16[96,2048]{1,0:T(8,128)(2,1)S(1)} collective-permute-done((bf16[96,2048]{1,0:T(8,128)(2,1)S(1)}, bf16[96,2048]{1,0:T(8,128)(2,1)S(1)}, u32[]{:S(2)}, u32[]{:S(2)}) %collective-permute-start.9) | collective-permute-done | bytes 393248 | tf_op jit(solution)/shard_map/ppermute | solution.py:393
  46.7 0.5 collective-permute-start.11
  47.2 1.2 %collective-permute-done.10.refs_8_ = bf16[512,384]{1,0:T(8,128)(2,1)S(1)} collective-permute-done((bf16[512,384]{1,0:T(8,128)(2,1)S(1)}, bf16[512,384]{1,0:T(8,128)(2,1)S(1)}, u32[]{:S(2)}, u32[]{:S(2)}) %collective-permute-start.10) | collective-permute-done | bytes 393248 | tf_op jit(solution)/shard_map/ppermute | solution.py:393
  48.5 0.4 collective-permute-done.11.refs_9_
  49.1 0.8 expert_up.3.refs_1_
  50.1 0.6 collective-permute-done.13.refs_11_
  50.7 0.9 expert_up_y.2.refs_2_.refs_1_
  51.6 2.2 %collective-permute-done.15.refs_0_ = bf16[128,2048]{1,0:T(8,128)(2,1)S(1)} collective-permute-done((bf16[128,2048]{1,0:T(8,128)(2,1)S(1)}, bf16[128,2048]{1,0:T(8,128)(2,1)S(1)}, u32[]{:S(2)}, u32[]{:S(2)}) %collective-permute-start.15) | collective-permute-done | bytes 524320 | tf_op jit(solution)/shard_map/ppermute | solution.py:401
  53.7 0.5 collective-permute-start.19
  54.2 1.4 %collective-permute-done.18.refs_7_ = bf16[128,2048]{1,0:T(8,128)(2,1)S(1)} collective-permute-done((bf16[128,2048]{1,0:T(8,128)(2,1)S(1)}, bf16[128,2048]{1,0:T(8,128)(2,1)S(1)}, u32[]{:S(2)}, u32[]{:S(2)}) %collective-permute-start.18) | collective-permute-done | bytes 524320 | tf_op jit(solution)/shard_map/ppermute | solution.py:393
  55.6 0.7 collective-permute-done.19.refs_9_
  56.4 0.8 expert_down.3
  57.2 1.4 %collective-permute-start.22 = (bf16[96,1024]{1,0:T(8,128)(2,1)S(1)}, bf16[96,1024]{1,0:T(8,128)(2,1)S(1)}, u32[]{:S(2)}, u32[]{:S(2)}) collective-permute-start(bf16[96,1024]{1,0:T(8,128)(2,1)S(1)} %get-tuple-element.61), channel_id=1, source_target_pairs={{0,4},{1,5},{2,6},{3,7},{4,0},{5,1},{6,2},{7,3},{8,12},{9,13},{10,... | collective-permute-start | bytes 589832 | tf_op jit(solution)/shard_map/ppermute | solution.py:393
  58.6 0.8 expert_up.2.refs_1_
  59.4 0.8 expert_down.4
  60.3 0.9 expert_up_y.3.refs_1_
  61.2 0.7 collective-permute-start.20
  61.9 2.8 %collective-permute-done.22.z_ref = bf16[96,1024]{1,0:T(8,128)(2,1)S(1)} collective-permute-done((bf16[96,1024]{1,0:T(8,128)(2,1)S(1)}, bf16[96,1024]{1,0:T(8,128)(2,1)S(1)}, u32[]{:S(2)}, u32[]{:S(2)}) %collective-permute-start.22) | collective-permute-done | bytes 196640 | tf_op jit(solution)/shard_map/ppermute | solution.py:393
  64.7 1.9 %collective-permute-start.23 = (bf16[96,1024]{1,0:T(8,128)(2,1)S(1)}, bf16[96,1024]{1,0:T(8,128)(2,1)S(1)}, u32[]{:S(2)}, u32[]{:S(2)}) collective-permute-start(bf16[96,1024]{1,0:T(8,128)(2,1)S(1)} %far_total.3), channel_id=1, source_target_pairs={{0,8},{1,9},{2,10},{3,11},{4,12},{5,13},{6,14},{7,15},{8,0},{9,1},... | collective-permute-start | bytes 589832 | tf_op jit(solution)/shard_map/ppermute | solution.py:397
  66.6 1.5 %expert_down.5 = (bf16[96,2048]{1,0:T(8,128)(2,1)S(1)}, bf16[96,2048]{1,0:T(8,128)(2,1)S(1)}) custom-call(s32[1]{0:T(128)} %bitcast.10.pipe_ref.refs_0_, bf16[192,1536]{1,0:T(8,128)(2,1)S(1)} %expert_up_y.3.refs_1_, bf16[384,2048]{1,0:T(8,128)(2,1)S(1)} %get-tuple-element.49.refs_2_, bf16[384,2048]{1,0:T(8,128)(2,1)S(1)} %collective-permute-done.2.refs_7_.refs_3_, ...), custom_call_target="tpu_custom_call" | custom-call | flops 1207959552 | bytes 6291456 | tf_op jit(solution)/shard_map/expert_down/pallas_call | solution.py:320
  68.2 3.1 %collective-permute-done.20.z_ref = bf16[96,1024]{1,0:T(8,128)(2,1)S(1)} collective-permute-done((bf16[96,1024]{1,0:T(8,128)(2,1)S(1)}, bf16[96,1024]{1,0:T(8,128)(2,1)S(1)}, u32[]{:S(2)}, u32[]{:S(2)}) %collective-permute-start.20) | collective-permute-done | bytes 196640 | tf_op jit(solution)/shard_map/ppermute | solution.py:393
  71.4 2.3 %collective-permute-start.24 = (bf16[96,1024]{1,0:T(8,128)(2,1)S(1)}, bf16[96,1024]{1,0:T(8,128)(2,1)S(1)}, u32[]{:S(2)}, u32[]{:S(2)}) collective-permute-start(bf16[96,1024]{1,0:T(8,128)(2,1)S(1)} %get-tuple-element.62), channel_id=1, source_target_pairs={{0,8},{1,9},{2,10},{3,11},{4,12},{5,13},{6,14},{7,15},{8,0},{9,1},... | collective-permute-start | bytes 589832 | tf_op jit(solution)/shard_map/ppermute | solution.py:397
  73.7 3.0 %collective-permute-done.23.refs_0_ = bf16[96,1024]{1,0:T(8,128)(2,1)S(1)} collective-permute-done((bf16[96,1024]{1,0:T(8,128)(2,1)S(1)}, bf16[96,1024]{1,0:T(8,128)(2,1)S(1)}, u32[]{:S(2)}, u32[]{:S(2)}) %collective-permute-start.23) | collective-permute-done | bytes 196640 | tf_op jit(solution)/shard_map/ppermute | solution.py:397
  76.7 7.6 %collective-permute-done.24.refs_6_ = bf16[96,1024]{1,0:T(8,128)(2,1)S(1)} collective-permute-done((bf16[96,1024]{1,0:T(8,128)(2,1)S(1)}, bf16[96,1024]{1,0:T(8,128)(2,1)S(1)}, u32[]{:S(2)}, u32[]{:S(2)}) %collective-permute-start.24) | collective-permute-done | bytes 196640 | tf_op jit(solution)/shard_map/ppermute | solution.py:397
  84.2 3.0 %collective-permute-done.21.refs_4_ = bf16[96,2048]{1,0:T(8,128)(2,1)S(1)} collective-permute-done((bf16[96,2048]{1,0:T(8,128)(2,1)S(1)}, bf16[96,2048]{1,0:T(8,128)(2,1)S(1)}, u32[]{:S(2)}, u32[]{:S(2)}) %collective-permute-start.21) | collective-permute-done | bytes 393248 | tf_op jit(solution)/shard_map/ppermute | solution.py:393
  87.2 1.2 %finish.1 = bf16[128,2048]{1,0:T(8,128)(2,1)} custom-call(f32[128,2048]{1,0:T(8,128)S(1)} %get-tuple-element.38.refs_0_, f32[128,1]{1,0:T(8,128)S(1)} %get-tuple-element.39.refs_1_, s32[128,1]{1,0:T(8,128)S(1)} %get-tuple-element.40.refs_2_, bf16[96,2048]{1,0:T(8,128)(2,1)S(1)} %get-tuple-element.57.refs_3_, ...), custom_call_target="tpu_custom_call" | custom-call | flops 201326592 | bytes 4194304 | tf_op jit(solution)/shard_map/finish/pallas_call | solution.py:375
  (52 shorter events, 1.8 us)
Async XLA Ops:
  0.0 2.3 %copy-start.8 = (bf16[1,32,2,2048]{3,2,1,0:T(2,128)(2,1)S(1)}, bf16[1,32,2,2048]{3,2,1,0:T(2,128)(2,1)}, u32[]{:S(2)}) copy-start(bf16[1,32,2,2048]{3,2,1,0:T(2,128)(2,1)} %param.11) | copy-start | bytes 786436
  0.0 14.7 %collective-permute-start.2 = (bf16[384,2048]{1,0:T(8,128)(2,1)}, bf16[384,2048]{1,0:T(8,128)(2,1)S(1)}, u32[]{:S(2)}, u32[]{:S(2)}) collective-permute-start(bf16[384,2048]{1,0:T(8,128)(2,1)} %w_out.1), channel_id=1, source_target_pairs={{0,1},{1,0},{2,3},{3,2},{4,5},{5,4},{6,7},{7,6},{8,9},{9,8},{10,11... | collective-permute-start | bytes 4718600 | tf_op jit(solution)/shard_map/ppermute | solution.py:393
  0.5 14.2 %collective-permute-start.1 = (bf16[2048,384]{1,0:T(8,128)(2,1)}, bf16[2048,384]{1,0:T(8,128)(2,1)S(1)}, u32[]{:S(2)}, u32[]{:S(2)}) collective-permute-start(bf16[2048,384]{1,0:T(8,128)(2,1)} %whole.3), channel_id=1, source_target_pairs={{0,1},{1,0},{2,3},{3,2},{4,5},{5,4},{6,7},{7,6},{8,9},{9,8},{10,11... | collective-permute-start | bytes 4718600 | tf_op jit(solution)/shard_map/ppermute | solution.py:393
  3.1 6.2 %copy-start.4 = (f32[2048]{0:T(1024)S(1)}, f32[2048]{0:T(1024)}, u32[]{:S(2)}) copy-start(f32[2048]{0:T(1024)} %param.12) | copy-start | bytes 24580
  3.1 6.2 %copy-start.5 = (s32[1,1,128]{2,1,0:T(1,128)S(1)}, s32[1,1,128]{2,1,0:T(1,128)}, u32[]{:S(2)}) copy-start(s32[1,1,128]{2,1,0:T(1,128)} %param.15) | copy-start | bytes 1540
  3.1 6.2 %copy-start.6 = (s32[1,1,128]{2,1,0:T(1,128)S(1)}, s32[1,1,128]{2,1,0:T(1,128)}, u32[]{:S(2)}) copy-start(s32[1,1,128]{2,1,0:T(1,128)} %param.16) | copy-start | bytes 1540
  3.1 9.8 %collective-permute-start = (bf16[64,2048]{1,0:T(8,128)(2,1)}, bf16[64,2048]{1,0:T(8,128)(2,1)}, u32[]{:S(2)}, u32[]{:S(2)}) collective-permute-start(bf16[64,2048]{1,0:T(8,128)(2,1)} %hand_on.16.refs_4_), channel_id=1, source_target_pairs={{0,16},{16,0},{1,17},{17,1},{2,18},{18,2},{3,19},{19,3},{4,20},{20... | collective-permute-start | bytes 786440 | tf_op jit(solution)/shard_map/ppermute | solution.py:416
  6.0 15.5 %collective-permute-start.4 = (bf16[512,384]{1,0:T(8,128)(2,1)}, bf16[512,384]{1,0:T(8,128)(2,1)S(1)}, u32[]{:S(2)}, u32[]{:S(2)}) collective-permute-start(bf16[512,384]{1,0:T(8,128)(2,1)} %weight_part.2.refs_1_), channel_id=1, source_target_pairs={{0,2},{1,3},{2,0},{3,1},{4,6},{5,7},{6,4},{7,5},{8,10},{9,11},{10,... | collective-permute-start | bytes 1179656 | tf_op jit(solution)/shard_map/ppermute | solution.py:393
  9.3 1.0 %copy-start.2 = (bf16[1,1,128,2048]{3,2,1,0:T(8,128)(2,1)S(1)}, bf16[1,1,128,2048]{3,2,1,0:T(8,128)(2,1)}, u32[]{:S(2)}) copy-start(bf16[1,1,128,2048]{3,2,1,0:T(8,128)(2,1)} %param.9) | copy-start | bytes 1572868
  10.4 1.0 %copy-start.3 = (bf16[1,1,128,2048]{3,2,1,0:T(8,128)(2,1)S(1)}, bf16[1,1,128,2048]{3,2,1,0:T(8,128)(2,1)}, u32[]{:S(2)}) copy-start(bf16[1,1,128,2048]{3,2,1,0:T(8,128)(2,1)} %param.10) | copy-start | bytes 1572868
  11.4 0.7 copy-start.7
  12.9 12.6 %collective-permute-start.6 = (bf16[512,384]{1,0:T(8,128)(2,1)}, bf16[512,384]{1,0:T(8,128)(2,1)S(1)}, u32[]{:S(2)}, u32[]{:S(2)}) collective-permute-start(bf16[512,384]{1,0:T(8,128)(2,1)} %hand_on.18), channel_id=1, source_target_pairs={{0,2},{1,3},{2,0},{3,1},{4,6},{5,7},{6,4},{7,5},{8,10},{9,11},{10,... | collective-permute-start | bytes 1179656 | tf_op jit(solution)/shard_map/ppermute | solution.py:393
  14.7 8.4 %copy-start = (bf16[2048,384]{1,0:T(8,128)(2,1)S(1)}, bf16[2048,384]{1,0:T(8,128)(2,1)}, u32[]{:S(2)}) copy-start(bf16[2048,384]{1,0:T(8,128)(2,1)} %whole.3) | copy-start | bytes 4718596
  14.7 8.4 %copy-start.1 = (bf16[384,2048]{1,0:T(8,128)(2,1)S(1)}, bf16[384,2048]{1,0:T(8,128)(2,1)}, u32[]{:S(2)}) copy-start(bf16[384,2048]{1,0:T(8,128)(2,1)} %w_out.1) | copy-start | bytes 4718596
  17.3 19.5 %collective-permute-start.8 = (bf16[96,2048]{1,0:T(8,128)(2,1)S(1)}, bf16[96,2048]{1,0:T(8,128)(2,1)S(1)}, u32[]{:S(2)}, u32[]{:S(2)}) collective-permute-start(bf16[96,2048]{1,0:T(8,128)(2,1)S(1)} %get-tuple-element.44), channel_id=1, source_target_pairs={{0,8},{1,9},{2,10},{3,11},{4,12},{5,13},{6,14},{7,15},{8,0},{9,1},... | collective-permute-start | bytes 1179656 | tf_op jit(solution)/shard_map/ppermute | solution.py:397
  19.9 17.0 %collective-permute-start.3 = (bf16[96,2048]{1,0:T(8,128)(2,1)S(1)}, bf16[96,2048]{1,0:T(8,128)(2,1)S(1)}, u32[]{:S(2)}, u32[]{:S(2)}) collective-permute-start(bf16[96,2048]{1,0:T(8,128)(2,1)S(1)} %get-tuple-element.41.refs_1_.own_in.refs_2_), channel_id=1, source_target_pairs={{0,4},{1,5},{2,6},{3,7},{4,0},{5,1},{6,2},{7,3},{8,12},{9,13},{10,... | collective-permute-start | bytes 1179656 | tf_op jit(solution)/shard_map/ppermute | solution.py:393
  21.5 19.4 %collective-permute-start.5 = (bf16[512,384]{1,0:T(8,128)(2,1)S(1)}, bf16[512,384]{1,0:T(8,128)(2,1)S(1)}, u32[]{:S(2)}, u32[]{:S(2)}) collective-permute-start(bf16[512,384]{1,0:T(8,128)(2,1)S(1)} %hand_on.17.refs_0_.refs_1_), channel_id=1, source_target_pairs={{0,16},{16,0},{1,17},{17,1},{2,18},{18,2},{3,19},{19,3},{4,20},{20... | collective-permute-start | bytes 1179656 | tf_op jit(solution)/shard_map/ppermute | solution.py:401
  25.5 13.9 %collective-permute-start.7 = (bf16[512,384]{1,0:T(8,128)(2,1)S(1)}, bf16[512,384]{1,0:T(8,128)(2,1)S(1)}, u32[]{:S(2)}, u32[]{:S(2)}) collective-permute-start(bf16[512,384]{1,0:T(8,128)(2,1)S(1)} %hand_on.19.refs_2_), channel_id=1, source_target_pairs={{0,16},{16,0},{1,17},{17,1},{2,18},{18,2},{3,19},{19,3},{4,20},{20... | collective-permute-start | bytes 1179656 | tf_op jit(solution)/shard_map/ppermute | solution.py:401
  25.8 13.5 %collective-permute-start.14 = (bf16[128,2048]{1,0:T(8,128)(2,1)S(1)}, bf16[128,2048]{1,0:T(8,128)(2,1)S(1)}, u32[]{:S(2)}, u32[]{:S(2)}) collective-permute-start(bf16[128,2048]{1,0:T(8,128)(2,1)S(1)} %get-tuple-element.51), channel_id=1, source_target_pairs={{0,2},{1,3},{2,0},{3,1},{4,6},{5,7},{6,4},{7,5},{8,10},{9,11},{10,... | collective-permute-start | bytes 1572872 | tf_op jit(solution)/shard_map/ppermute | solution.py:393
  36.9 9.7 %collective-permute-start.9 = (bf16[96,2048]{1,0:T(8,128)(2,1)S(1)}, bf16[96,2048]{1,0:T(8,128)(2,1)S(1)}, u32[]{:S(2)}, u32[]{:S(2)}) collective-permute-start(bf16[96,2048]{1,0:T(8,128)(2,1)S(1)} %hand_on.20.own_in.refs_2_), channel_id=1, source_target_pairs={{0,4},{1,5},{2,6},{3,7},{4,0},{5,1},{6,2},{7,3},{8,12},{9,13},{10,... | collective-permute-start | bytes 1179656 | tf_op jit(solution)/shard_map/ppermute | solution.py:393
  38.4 13.2 %collective-permute-start.16 = (bf16[128,2048]{1,0:T(8,128)(2,1)S(1)}, bf16[128,2048]{1,0:T(8,128)(2,1)S(1)}, u32[]{:S(2)}, u32[]{:S(2)}) collective-permute-start(bf16[128,2048]{1,0:T(8,128)(2,1)S(1)} %get-tuple-element.52), channel_id=1, source_target_pairs={{0,2},{1,3},{2,0},{3,1},{4,6},{5,7},{6,4},{7,5},{8,10},{9,11},{10,... | collective-permute-start | bytes 1572872 | tf_op jit(solution)/shard_map/ppermute | solution.py:393
  39.4 12.2 %collective-permute-start.17 = (bf16[128,2048]{1,0:T(8,128)(2,1)S(1)}, bf16[128,2048]{1,0:T(8,128)(2,1)S(1)}, u32[]{:S(2)}, u32[]{:S(2)}) collective-permute-start(bf16[128,2048]{1,0:T(8,128)(2,1)S(1)} %hand_on.27.refs_4_), channel_id=1, source_target_pairs={{0,1},{1,0},{2,3},{3,2},{4,5},{5,4},{6,7},{7,6},{8,9},{9,8},{10,11... | collective-permute-start | bytes 1572872 | tf_op jit(solution)/shard_map/ppermute | solution.py:393
  39.4 14.3 %collective-permute-start.15 = (bf16[128,2048]{1,0:T(8,128)(2,1)S(1)}, bf16[128,2048]{1,0:T(8,128)(2,1)S(1)}, u32[]{:S(2)}, u32[]{:S(2)}) collective-permute-start(bf16[128,2048]{1,0:T(8,128)(2,1)S(1)} %hand_on.27.refs_4_), channel_id=1, source_target_pairs={{0,16},{16,0},{1,17},{17,1},{2,18},{18,2},{3,19},{19,3},{4,20},{20... | collective-permute-start | bytes 1572872 | tf_op jit(solution)/shard_map/ppermute | solution.py:401
  46.7 1.7 %collective-permute-start.10 = (bf16[512,384]{1,0:T(8,128)(2,1)S(1)}, bf16[512,384]{1,0:T(8,128)(2,1)S(1)}, u32[]{:S(2)}, u32[]{:S(2)}) collective-permute-start(bf16[512,384]{1,0:T(8,128)(2,1)S(1)} %get-tuple-element.45.refs_4_), channel_id=1, source_target_pairs={{0,1},{1,0},{2,3},{3,2},{4,5},{5,4},{6,7},{7,6},{8,9},{9,8},{10,11... | collective-permute-start | bytes 1179656 | tf_op jit(solution)/shard_map/ppermute | solution.py:393
  46.7 2.3 %collective-permute-start.11 = (bf16[512,384]{1,0:T(8,128)(2,1)S(1)}, bf16[512,384]{1,0:T(8,128)(2,1)S(1)}, u32[]{:S(2)}, u32[]{:S(2)}) collective-permute-start(bf16[512,384]{1,0:T(8,128)(2,1)S(1)} %get-tuple-element.46.refs_5_), channel_id=1, source_target_pairs={{0,1},{1,0},{2,3},{3,2},{4,5},{5,4},{6,7},{7,6},{8,9},{9,8},{10,11... | collective-permute-start | bytes 1179656 | tf_op jit(solution)/shard_map/ppermute | solution.py:393
  48.4 1.7 %collective-permute-start.12 = (bf16[512,384]{1,0:T(8,128)(2,1)S(1)}, bf16[512,384]{1,0:T(8,128)(2,1)S(1)}, u32[]{:S(2)}, u32[]{:S(2)}) collective-permute-start(bf16[512,384]{1,0:T(8,128)(2,1)S(1)} %get-tuple-element.47.refs_6_), channel_id=1, source_target_pairs={{0,1},{1,0},{2,3},{3,2},{4,5},{5,4},{6,7},{7,6},{8,9},{9,8},{10,11... | collective-permute-start | bytes 1179656 | tf_op jit(solution)/shard_map/ppermute | solution.py:393
  48.9 1.7 %collective-permute-start.13 = (bf16[512,384]{1,0:T(8,128)(2,1)S(1)}, bf16[512,384]{1,0:T(8,128)(2,1)S(1)}, u32[]{:S(2)}, u32[]{:S(2)}) collective-permute-start(bf16[512,384]{1,0:T(8,128)(2,1)S(1)} %get-tuple-element.48.refs_7_), channel_id=1, source_target_pairs={{0,1},{1,0},{2,3},{3,2},{4,5},{5,4},{6,7},{7,6},{8,9},{9,8},{10,11... | collective-permute-start | bytes 1179656 | tf_op jit(solution)/shard_map/ppermute | solution.py:393
  53.7 1.9 %collective-permute-start.18 = (bf16[128,2048]{1,0:T(8,128)(2,1)S(1)}, bf16[128,2048]{1,0:T(8,128)(2,1)S(1)}, u32[]{:S(2)}, u32[]{:S(2)}) collective-permute-start(bf16[128,2048]{1,0:T(8,128)(2,1)S(1)} %get-tuple-element.53.refs_5_), channel_id=1, source_target_pairs={{0,1},{1,0},{2,3},{3,2},{4,5},{5,4},{6,7},{7,6},{8,9},{9,8},{10,11... | collective-permute-start | bytes 1572872 | tf_op jit(solution)/shard_map/ppermute | solution.py:393
  53.7 2.7 %collective-permute-start.19 = (bf16[128,2048]{1,0:T(8,128)(2,1)S(1)}, bf16[128,2048]{1,0:T(8,128)(2,1)S(1)}, u32[]{:S(2)}, u32[]{:S(2)}) collective-permute-start(bf16[128,2048]{1,0:T(8,128)(2,1)S(1)} %get-tuple-element.54.refs_8_), channel_id=1, source_target_pairs={{0,1},{1,0},{2,3},{3,2},{4,5},{5,4},{6,7},{7,6},{8,9},{9,8},{10,11... | collective-permute-start | bytes 1572872 | tf_op jit(solution)/shard_map/ppermute | solution.py:393
  57.2 7.5 %collective-permute-start.22 = (bf16[96,1024]{1,0:T(8,128)(2,1)S(1)}, bf16[96,1024]{1,0:T(8,128)(2,1)S(1)}, u32[]{:S(2)}, u32[]{:S(2)}) collective-permute-start(bf16[96,1024]{1,0:T(8,128)(2,1)S(1)} %get-tuple-element.61), channel_id=1, source_target_pairs={{0,4},{1,5},{2,6},{3,7},{4,0},{5,1},{6,2},{7,3},{8,12},{9,13},{10,... | collective-permute-start | bytes 589832 | tf_op jit(solution)/shard_map/ppermute | solution.py:393
  61.2 10.1 %collective-permute-start.20 = (bf16[96,1024]{1,0:T(8,128)(2,1)S(1)}, bf16[96,1024]{1,0:T(8,128)(2,1)S(1)}, u32[]{:S(2)}, u32[]{:S(2)}) collective-permute-start(bf16[96,1024]{1,0:T(8,128)(2,1)S(1)} %hand_on.29), channel_id=1, source_target_pairs={{0,4},{1,5},{2,6},{3,7},{4,0},{5,1},{6,2},{7,3},{8,12},{9,13},{10,... | collective-permute-start | bytes 589832 | tf_op jit(solution)/shard_map/ppermute | solution.py:393
  64.7 11.9 %collective-permute-start.23 = (bf16[96,1024]{1,0:T(8,128)(2,1)S(1)}, bf16[96,1024]{1,0:T(8,128)(2,1)S(1)}, u32[]{:S(2)}, u32[]{:S(2)}) collective-permute-start(bf16[96,1024]{1,0:T(8,128)(2,1)S(1)} %far_total.3), channel_id=1, source_target_pairs={{0,8},{1,9},{2,10},{3,11},{4,12},{5,13},{6,14},{7,15},{8,0},{9,1},... | collective-permute-start | bytes 589832 | tf_op jit(solution)/shard_map/ppermute | solution.py:397
  71.3 15.9 %collective-permute-start.21 = (bf16[96,2048]{1,0:T(8,128)(2,1)S(1)}, bf16[96,2048]{1,0:T(8,128)(2,1)S(1)}, u32[]{:S(2)}, u32[]{:S(2)}) collective-permute-start(bf16[96,2048]{1,0:T(8,128)(2,1)S(1)} %get-tuple-element.60), channel_id=1, source_target_pairs={{0,4},{1,5},{2,6},{3,7},{4,0},{5,1},{6,2},{7,3},{8,12},{9,13},{10,... | collective-permute-start | bytes 1179656 | tf_op jit(solution)/shard_map/ppermute | solution.py:393
  71.4 12.8 %collective-permute-start.24 = (bf16[96,1024]{1,0:T(8,128)(2,1)S(1)}, bf16[96,1024]{1,0:T(8,128)(2,1)S(1)}, u32[]{:S(2)}, u32[]{:S(2)}) collective-permute-start(bf16[96,1024]{1,0:T(8,128)(2,1)S(1)} %get-tuple-element.62), channel_id=1, source_target_pairs={{0,8},{1,9},{2,10},{3,11},{4,12},{5,13},{6,14},{7,15},{8,0},{9,1},... | collective-permute-start | bytes 589832 | tf_op jit(solution)/shard_map/ppermute | solution.py:397

commit v18 on v14

--- a/solution.py
+++ b/solution.py
@@ -16,6 +16,7 @@
 FAR_STEPS = 4
 CROSS_STEPS = 1
 CROSS_WEIGHT = 3_000_000_000
+NEAR_WEIGHT = 1_000_000_000
 SUM_WEIGHT = 1_000_000_000
 BACK_WEIGHT = 3_000_000_000
 VMEM_LIMIT = 32 * 1024 * 1024
@@ -479,16 +480,16 @@
     near_act = experts_up(near, near_z, [far_b])
     (sent_b,) = after_all([sent_b], [near_act])
     near_own, near_sent = experts_down(near_act, 0, width)
-    (sum_a,) = total(far_a, across(sent_a, 4), [])
-    sum_b, near_sent = total(far_b, across(sent_b, 4), [near_sent])
+    sum_a, near_sent = total(far_a, across(sent_a, 4), [near_sent])
+    (sum_b,) = total(far_b, across(sent_b, 4), [])
     backs = [
         groups_on(side[(count - 1) * cap : count * cap], groups - count)
         for count in range(1, groups)
         for side in (sum_a, sum_b)
     ]
-    backs[::2] = after_all(backs[::2], [], SUM_WEIGHT)
+    backs[::2] = after_all(backs[::2], [sum_b], SUM_WEIGHT)
     backs[::2] = after_all(backs[::2], [], BACK_WEIGHT)
-    near_sums = [near_own, across(near_sent, 4)]
+    near_sums = [near_own, *after_all([across(near_sent, 4)], [], NEAR_WEIGHT)]
     output = finish(hidden, gates, flat, near_sums, backs, groups, cap)
     return output.reshape(1, 1, tokens, width)
 

time: 87.3 us -> 87.3 us (level)
  starting transfers between devices: 26.8 us -> 25.8 us
  waiting for transfers between devices: 41.3 us -> 42.3 us
    ppermute x18, waiting for transfers between devices: 19.6 us -> 26.5 us  [across(): return lax.ppermute(value, 'expert', [(i, i ^ bit) for i in range(devices)])]
    ppermute x3, waiting for transfers between devices: 19.8 us -> 13.8 us  [groups_on(): lax.ppermute(value, 'expert', [(i, (i + shift) % devices) for i in range(...]
    ppermute x3, starting transfers between devices: 7.77 us -> 6.56 us  [groups_on(): lax.ppermute(value, 'expert', [(i, (i + shift) % devices) for i in range(...]
  transfers between devices with their start and end apart: 25 -> 25, of which waited for: 17 -> 16; matrix products, arithmetic and copies ran while one was open for 1% -> 1% of each run, Pallas kernels for 15% -> 15%
where the time goes in v18:
time: 87.3 us; the launch traced here: 86.6 us
  waiting for transfers between devices  42.3 us (48%)
  starting transfers between devices  25.8 us (30%)
  Pallas kernels  14.7 us (17%)
  local copies, waits for them, and re-layouts  3.56 us (4%)
    ppermute x18, waiting for transfers between devices, across(): return lax.ppermute(value, 'expert', [(i, i ^ bit) for i in range(devices)])  26.5 us
    ppermute x3, waiting for transfers between devices, groups_on(): lax.ppermute(value, 'expert', [(i, (i + shift) % devices) for i in range(...  13.8 us
    ppermute x18, starting transfers between devices, across(): return lax.ppermute(value, 'expert', [(i, i ^ bit) for i in range(devices)])  12.9 us
    ppermute x3, starting transfers between devices, groups_on(): lax.ppermute(value, 'expert', [(i, (i + shift) % devices) for i in range(...  6.56 us
    pallas_call x2, Pallas kernels, cut_part(): call(functools.partial(part_kernel, stride, first), struct((size, whole.s...  3.49 us
    ppermute x3, starting transfers between devices, along(): return [value] + [lax.ppermute(value, 'pipe', perm) for perm in perms]  3.46 us
    pallas_call x3, Pallas kernels, down(): call(functools.partial(down_kernel, pipes, first), [struct((rows, width))...  3.19 us
    ppermute x1, starting transfers between devices, body(): kv_pieces.append(lax.ppermute(kv, 'pipe', perm))  2.93 us
  transfers between devices with their start and end apart: 25, of which 16 were waited for; matrix products, arithmetic and copies ran while one was open for 1% of the time, Pallas kernels for 15%

profile of v18, /device:TPU:0, one launch (start us, length us, event | category | flops | bytes accessed | tf_op | source)
XLA Modules:
  0.0 86.6 jit_solution(4414649246266102452)
XLA Ops:
  0.0 0.5 collective-permute-start.2
  0.5 1.7 %weight_part.2.refs_1_ = bf16[512,384]{1,0:T(8,128)(2,1)} custom-call(s32[1]{0:T(128)} %bitcast.10.pipe_ref.refs_0_, bf16[2048,384]{1,0:T(8,128)(2,1)} %whole.3), custom_call_target="tpu_custom_call" | custom-call | flops 1 | bytes 786432 | tf_op jit(solution)/shard_map/weight_part/pallas_call | solution.py:179
  2.3 0.8 copy.33
  3.1 2.9 %collective-permute-start = (bf16[64,2048]{1,0:T(8,128)(2,1)}, bf16[64,2048]{1,0:T(8,128)(2,1)}, u32[]{:S(2)}, u32[]{:S(2)}) collective-permute-start(bf16[64,2048]{1,0:T(8,128)(2,1)} %hand_on.17.refs_4_), channel_id=1, source_target_pairs={{0,16},{16,0},{1,17},{17,1},{2,18},{18,2},{3,19},{19,3},{4,20},{20... | collective-permute-start | bytes 786440 | tf_op jit(solution)/shard_map/ppermute | solution.py:417
  6.0 1.5 %collective-permute-start.4 = (bf16[512,384]{1,0:T(8,128)(2,1)}, bf16[512,384]{1,0:T(8,128)(2,1)S(1)}, u32[]{:S(2)}, u32[]{:S(2)}) collective-permute-start(bf16[512,384]{1,0:T(8,128)(2,1)} %weight_part.2.refs_1_), channel_id=1, source_target_pairs={{0,2},{1,3},{2,0},{3,1},{4,6},{5,7},{6,4},{7,5},{8,10},{9,11},{10,... | collective-permute-start | bytes 1179656 | tf_op jit(solution)/shard_map/ppermute | solution.py:394
  7.6 1.7 %weight_part.3.refs_0_ = bf16[512,384]{1,0:T(8,128)(2,1)} custom-call(s32[1]{0:T(128)} %bitcast.10.pipe_ref.refs_0_, bf16[2048,384]{1,0:T(8,128)(2,1)} %whole.3), custom_call_target="tpu_custom_call" | custom-call | flops 1 | bytes 786432 | tf_op jit(solution)/shard_map/weight_part/pallas_call | solution.py:179
  9.4 1.0 %copy-done.2 = bf16[1,1,128,2048]{3,2,1,0:T(8,128)(2,1)S(1)} copy-done((bf16[1,1,128,2048]{3,2,1,0:T(8,128)(2,1)S(1)}, bf16[1,1,128,2048]{3,2,1,0:T(8,128)(2,1)}, u32[]{:S(2)}) %copy-start.2) | copy-done | bytes 524312
  10.4 1.0 %copy-done.3 = bf16[1,1,128,2048]{3,2,1,0:T(8,128)(2,1)S(1)} copy-done((bf16[1,1,128,2048]{3,2,1,0:T(8,128)(2,1)S(1)}, bf16[1,1,128,2048]{3,2,1,0:T(8,128)(2,1)}, u32[]{:S(2)}) %copy-start.3) | copy-done | bytes 524312
  11.4 0.7 copy-done.7
  12.2 0.7 collective-permute-done.refs_5_.refs_1_
  12.9 1.8 %collective-permute-start.6 = (bf16[512,384]{1,0:T(8,128)(2,1)}, bf16[512,384]{1,0:T(8,128)(2,1)S(1)}, u32[]{:S(2)}, u32[]{:S(2)}) collective-permute-start(bf16[512,384]{1,0:T(8,128)(2,1)} %hand_on.19), channel_id=1, source_target_pairs={{0,2},{1,3},{2,0},{3,1},{4,6},{5,7},{6,4},{7,5},{8,10},{9,11},{10,... | collective-permute-start | bytes 1179656 | tf_op jit(solution)/shard_map/ppermute | solution.py:394
  14.7 2.6 %attend.1 = (f32[128,2048]{1,0:T(8,128)S(1)}, bf16[96,2048]{1,0:T(8,128)(2,1)S(1)}, bf16[96,2048]{1,0:T(8,128)(2,1)S(1)}) custom-call(bf16[128,2048]{1,0:T(8,128)(2,1)S(1)} %get-tuple-element.34.refs_0_, bf16[128,2048]{1,0:T(8,128)(2,1)S(1)} %get-tuple-element.35.refs_1_, f32[1,2048]{1,0:T(1,128)S(1)} %get-tuple-element.36.refs_2_, ...), custom_call_target="tpu_custom_call" | custom-call | flops 134217728 | bytes 3145728 | tf_op jit(solution)/shard_map/attend/pallas_call | solution.py:154
  17.3 2.7 %collective-permute-start.8 = (bf16[96,2048]{1,0:T(8,128)(2,1)S(1)}, bf16[96,2048]{1,0:T(8,128)(2,1)S(1)}, u32[]{:S(2)}, u32[]{:S(2)}) collective-permute-start(bf16[96,2048]{1,0:T(8,128)(2,1)S(1)} %get-tuple-element.44), channel_id=1, source_target_pairs={{0,8},{1,9},{2,10},{3,11},{4,12},{5,13},{6,14},{7,15},{8,0},{9,1},... | collective-permute-start | bytes 1179656 | tf_op jit(solution)/shard_map/ppermute | solution.py:398
  19.9 1.6 %collective-permute-start.3 = (bf16[96,2048]{1,0:T(8,128)(2,1)S(1)}, bf16[96,2048]{1,0:T(8,128)(2,1)S(1)}, u32[]{:S(2)}, u32[]{:S(2)}) collective-permute-start(bf16[96,2048]{1,0:T(8,128)(2,1)S(1)} %get-tuple-element.41.refs_0_.own_in.refs_2_), channel_id=1, source_target_pairs={{0,4},{1,5},{2,6},{3,7},{4,0},{5,1},{6,2},{7,3},{8,12},{9,13},{10,... | collective-permute-start | bytes 1179656 | tf_op jit(solution)/shard_map/ppermute | solution.py:394
  21.5 0.7 hold_weights.1
  22.3 1.6 %collective-permute-start.5 = (bf16[512,384]{1,0:T(8,128)(2,1)S(1)}, bf16[512,384]{1,0:T(8,128)(2,1)S(1)}, u32[]{:S(2)}, u32[]{:S(2)}) collective-permute-start(bf16[512,384]{1,0:T(8,128)(2,1)S(1)} %hand_on.18.refs_1_.refs_0_), channel_id=1, source_target_pairs={{0,16},{16,0},{1,17},{17,1},{2,18},{18,2},{3,19},{19,3},{4,20},{20... | collective-permute-start | bytes 1179656 | tf_op jit(solution)/shard_map/ppermute | solution.py:402
  23.8 1.6 %collective-permute-done.6.refs_0_ = bf16[512,384]{1,0:T(8,128)(2,1)S(1)} collective-permute-done((bf16[512,384]{1,0:T(8,128)(2,1)}, bf16[512,384]{1,0:T(8,128)(2,1)S(1)}, u32[]{:S(2)}, u32[]{:S(2)}) %collective-permute-start.6) | collective-permute-done | bytes 393248 | tf_op jit(solution)/shard_map/ppermute | solution.py:394
  25.5 0.4 collective-permute-start.7
  25.8 1.7 %collective-permute-start.14 = (bf16[112,2048]{1,0:T(8,128)(2,1)S(1)}, bf16[112,2048]{1,0:T(8,128)(2,1)S(1)}, u32[]{:S(2)}, u32[]{:S(2)}) collective-permute-start(bf16[112,2048]{1,0:T(8,128)(2,1)S(1)} %get-tuple-element.51), channel_id=1, source_target_pairs={{0,2},{1,3},{2,0},{3,1},{4,6},{5,7},{6,4},{7,5},{8,10},{9,11},{10,... | collective-permute-start | bytes 1376264 | tf_op jit(solution)/shard_map/ppermute | solution.py:394
  27.5 9.2 %collective-permute-done.8.refs_0_ = bf16[96,2048]{1,0:T(8,128)(2,1)S(1)} collective-permute-done((bf16[96,2048]{1,0:T(8,128)(2,1)S(1)}, bf16[96,2048]{1,0:T(8,128)(2,1)S(1)}, u32[]{:S(2)}, u32[]{:S(2)}) %collective-permute-start.8) | collective-permute-done | bytes 393248 | tf_op jit(solution)/shard_map/ppermute | solution.py:398
  36.9 1.4 %collective-permute-start.9 = (bf16[96,2048]{1,0:T(8,128)(2,1)S(1)}, bf16[96,2048]{1,0:T(8,128)(2,1)S(1)}, u32[]{:S(2)}, u32[]{:S(2)}) collective-permute-start(bf16[96,2048]{1,0:T(8,128)(2,1)S(1)} %hand_on.21.own_in.refs_2_), channel_id=1, source_target_pairs={{0,4},{1,5},{2,6},{3,7},{4,0},{5,1},{6,2},{7,3},{8,12},{9,13},{10,... | collective-permute-start | bytes 1179656 | tf_op jit(solution)/shard_map/ppermute | solution.py:394
  38.4 0.5 collective-permute-start.16
  38.9 1.3 %collective-permute-done.7.refs_3_.refs_1_ = bf16[512,384]{1,0:T(8,128)(2,1)S(1)} collective-permute-done((bf16[512,384]{1,0:T(8,128)(2,1)S(1)}, bf16[512,384]{1,0:T(8,128)(2,1)S(1)}, u32[]{:S(2)}, u32[]{:S(2)}) %collective-permute-start.7) | collective-permute-done | bytes 393248 | tf_op jit(solution)/shard_map/ppermute | solution.py:402
  40.2 1.6 %collective-permute-start.15 = (bf16[112,2048]{1,0:T(8,128)(2,1)S(1)}, bf16[112,2048]{1,0:T(8,128)(2,1)S(1)}, u32[]{:S(2)}, u32[]{:S(2)}) collective-permute-start(bf16[112,2048]{1,0:T(8,128)(2,1)S(1)} %hand_on.28.refs_4_), channel_id=1, source_target_pairs={{0,16},{16,0},{1,17},{17,1},{2,18},{18,2},{3,19},{19,3},{4,20},{20... | collective-permute-start | bytes 1376264 | tf_op jit(solution)/shard_map/ppermute | solution.py:402
  41.7 4.9 %collective-permute-done.9.refs_4_.refs_0_ = bf16[96,2048]{1,0:T(8,128)(2,1)S(1)} collective-permute-done((bf16[96,2048]{1,0:T(8,128)(2,1)S(1)}, bf16[96,2048]{1,0:T(8,128)(2,1)S(1)}, u32[]{:S(2)}, u32[]{:S(2)}) %collective-permute-start.9) | collective-permute-done | bytes 393248 | tf_op jit(solution)/shard_map/ppermute | solution.py:394
  46.7 0.5 collective-permute-start.11
  47.2 1.2 %collective-permute-done.10.refs_8_ = bf16[512,384]{1,0:T(8,128)(2,1)S(1)} collective-permute-done((bf16[512,384]{1,0:T(8,128)(2,1)S(1)}, bf16[512,384]{1,0:T(8,128)(2,1)S(1)}, u32[]{:S(2)}, u32[]{:S(2)}) %collective-permute-start.10) | collective-permute-done | bytes 393248 | tf_op jit(solution)/shard_map/ppermute | solution.py:394
  48.5 0.4 collective-permute-done.11.refs_9_
  49.1 0.8 expert_up.3.refs_1_
  50.1 0.6 collective-permute-done.13.refs_11_
  50.7 0.9 expert_up_y.2.refs_2_.refs_1_
  51.5 2.2 %collective-permute-done.16.refs_1_ = bf16[160,2048]{1,0:T(8,128)(2,1)S(1)} collective-permute-done((bf16[160,2048]{1,0:T(8,128)(2,1)S(1)}, bf16[160,2048]{1,0:T(8,128)(2,1)S(1)}, u32[]{:S(2)}, u32[]{:S(2)}) %collective-permute-start.16) | collective-permute-done | bytes 655392 | tf_op jit(solution)/shard_map/ppermute | solution.py:394
  53.8 0.5 collective-permute-start.18
  54.3 0.8 expert_up.2.refs_1_
  55.1 1.4 %collective-permute-done.18.refs_7_ = bf16[112,2048]{1,0:T(8,128)(2,1)S(1)} collective-permute-done((bf16[112,2048]{1,0:T(8,128)(2,1)S(1)}, bf16[112,2048]{1,0:T(8,128)(2,1)S(1)}, u32[]{:S(2)}, u32[]{:S(2)}) %collective-permute-start.18) | collective-permute-done | bytes 458784 | tf_op jit(solution)/shard_map/ppermute | solution.py:394
  56.5 0.8 expert_down.3
  57.4 0.4 collective-permute-start.20
  57.7 0.8 expert_down.4
  58.6 0.9 %expert_up_y.3.refs_1_ = bf16[192,1536]{1,0:T(8,128)(2,1)S(1)} custom-call(s32[1]{0:T(128)} %bitcast.10.pipe_ref.refs_0_, bf16[192,768]{1,0:T(8,128)(2,1)S(1)} %expert_up.2.refs_1_, bf16[96,2048]{1,0:T(8,128)(2,1)S(1)} %get-tuple-element.41.refs_0_.own_in.refs_2_, bf16[96,2048]{1,0:T(8,128)(2,1)S(1)} %collective-permute-done.3.z_in.refs_1_.refs_3_, ...), custom_call_target="tpu_custom_call" | custom-call | flops 603979776 | bytes 3145728 | tf_op jit(solution)/shard_map/expert_up_y/pallas_call | solution.py:278
  59.5 1.8 %collective-permute-start.23 = (bf16[96,1024]{1,0:T(8,128)(2,1)S(1)}, bf16[96,1024]{1,0:T(8,128)(2,1)S(1)}, u32[]{:S(2)}, u32[]{:S(2)}) collective-permute-start(bf16[96,1024]{1,0:T(8,128)(2,1)S(1)} %hand_on.31), channel_id=1, source_target_pairs={{0,4},{1,5},{2,6},{3,7},{4,0},{5,1},{6,2},{7,3},{8,12},{9,13},{10,... | collective-permute-start | bytes 589832 | tf_op jit(solution)/shard_map/ppermute | solution.py:394
  61.3 1.5 %expert_down.5 = (bf16[96,2048]{1,0:T(8,128)(2,1)S(1)}, bf16[96,2048]{1,0:T(8,128)(2,1)S(1)}) custom-call(s32[1]{0:T(128)} %bitcast.10.pipe_ref.refs_0_, bf16[192,1536]{1,0:T(8,128)(2,1)S(1)} %expert_up_y.3.refs_1_, bf16[384,2048]{1,0:T(8,128)(2,1)S(1)} %get-tuple-element.49.refs_2_, bf16[384,2048]{1,0:T(8,128)(2,1)S(1)} %collective-permute-done.2.refs_7_.refs_3_, ...), custom_call_target="tpu_custom_call" | custom-call | flops 1207959552 | bytes 6291456 | tf_op jit(solution)/shard_map/expert_down/pallas_call | solution.py:321
  62.8 2.4 %collective-permute-done.20.z_ref = bf16[96,1024]{1,0:T(8,128)(2,1)S(1)} collective-permute-done((bf16[96,1024]{1,0:T(8,128)(2,1)S(1)}, bf16[96,1024]{1,0:T(8,128)(2,1)S(1)}, u32[]{:S(2)}, u32[]{:S(2)}) %collective-permute-start.20) | collective-permute-done | bytes 196640 | tf_op jit(solution)/shard_map/ppermute | solution.py:394
  65.2 3.4 %collective-permute-start.22 = (bf16[96,1024]{1,0:T(8,128)(2,1)S(1)}, bf16[96,1024]{1,0:T(8,128)(2,1)S(1)}, u32[]{:S(2)}, u32[]{:S(2)}) collective-permute-start(bf16[96,1024]{1,0:T(8,128)(2,1)S(1)} %get-tuple-element.61), channel_id=1, source_target_pairs={{0,8},{1,9},{2,10},{3,11},{4,12},{5,13},{6,14},{7,15},{8,0},{9,1},... | collective-permute-start | bytes 589832 | tf_op jit(solution)/shard_map/ppermute | solution.py:398
  69.0 3.4 %collective-permute-done.23.z_ref = bf16[96,1024]{1,0:T(8,128)(2,1)S(1)} collective-permute-done((bf16[96,1024]{1,0:T(8,128)(2,1)S(1)}, bf16[96,1024]{1,0:T(8,128)(2,1)S(1)}, u32[]{:S(2)}, u32[]{:S(2)}) %collective-permute-start.23) | collective-permute-done | bytes 196640 | tf_op jit(solution)/shard_map/ppermute | solution.py:394
  72.4 0.5 collective-permute-start.24
  72.9 4.6 %collective-permute-done.22.refs_0_ = bf16[96,1024]{1,0:T(8,128)(2,1)S(1)} collective-permute-done((bf16[96,1024]{1,0:T(8,128)(2,1)S(1)}, bf16[96,1024]{1,0:T(8,128)(2,1)S(1)}, u32[]{:S(2)}, u32[]{:S(2)}) %collective-permute-start.22) | collective-permute-done | bytes 196640 | tf_op jit(solution)/shard_map/ppermute | solution.py:398
  77.5 8.0 %collective-permute-done.21.refs_0_ = bf16[96,2048]{1,0:T(8,128)(2,1)S(1)} collective-permute-done((bf16[96,2048]{1,0:T(8,128)(2,1)S(1)}, bf16[96,2048]{1,0:T(8,128)(2,1)S(1)}, u32[]{:S(2)}, u32[]{:S(2)}) %collective-permute-start.21) | collective-permute-done | bytes 393248 | tf_op jit(solution)/shard_map/ppermute | solution.py:394
  85.4 1.2 %finish.1 = bf16[128,2048]{1,0:T(8,128)(2,1)} custom-call(f32[128,2048]{1,0:T(8,128)S(1)} %get-tuple-element.38.refs_0_, f32[128,1]{1,0:T(8,128)S(1)} %get-tuple-element.39.refs_1_, s32[128,1]{1,0:T(8,128)S(1)} %get-tuple-element.40.refs_2_, bf16[96,2048]{1,0:T(8,128)(2,1)S(1)} %get-tuple-element.57.refs_3_, bf16[96,2048]{1,0:T(8,128)(2,1)S(1)} %hand_on.30.refs_4_, ...), custom_call_target="tpu_custom_call" | custom-call | flops 201326592 | bytes 4194304 | tf_op jit(solution)/shard_map/finish/pallas_call | solution.py:376
  (53 shorter events, 1.5 us)
Async XLA Ops:
  0.0 2.3 %copy-start.8 = (bf16[1,32,2,2048]{3,2,1,0:T(2,128)(2,1)S(1)}, bf16[1,32,2,2048]{3,2,1,0:T(2,128)(2,1)}, u32[]{:S(2)}) copy-start(bf16[1,32,2,2048]{3,2,1,0:T(2,128)(2,1)} %param.11) | copy-start | bytes 786436
  0.0 14.7 %collective-permute-start.2 = (bf16[384,2048]{1,0:T(8,128)(2,1)}, bf16[384,2048]{1,0:T(8,128)(2,1)S(1)}, u32[]{:S(2)}, u32[]{:S(2)}) collective-permute-start(bf16[384,2048]{1,0:T(8,128)(2,1)} %w_out.1), channel_id=1, source_target_pairs={{0,1},{1,0},{2,3},{3,2},{4,5},{5,4},{6,7},{7,6},{8,9},{9,8},{10,11... | collective-permute-start | bytes 4718600 | tf_op jit(solution)/shard_map/ppermute | solution.py:394
  0.5 14.2 %collective-permute-start.1 = (bf16[2048,384]{1,0:T(8,128)(2,1)}, bf16[2048,384]{1,0:T(8,128)(2,1)S(1)}, u32[]{:S(2)}, u32[]{:S(2)}) collective-permute-start(bf16[2048,384]{1,0:T(8,128)(2,1)} %whole.3), channel_id=1, source_target_pairs={{0,1},{1,0},{2,3},{3,2},{4,5},{5,4},{6,7},{7,6},{8,9},{9,8},{10,11... | collective-permute-start | bytes 4718600 | tf_op jit(solution)/shard_map/ppermute | solution.py:394
  3.1 6.2 %copy-start.4 = (f32[2048]{0:T(1024)S(1)}, f32[2048]{0:T(1024)}, u32[]{:S(2)}) copy-start(f32[2048]{0:T(1024)} %param.12) | copy-start | bytes 24580
  3.1 6.2 %copy-start.5 = (s32[1,1,128]{2,1,0:T(1,128)S(1)}, s32[1,1,128]{2,1,0:T(1,128)}, u32[]{:S(2)}) copy-start(s32[1,1,128]{2,1,0:T(1,128)} %param.15) | copy-start | bytes 1540
  3.1 6.2 %copy-start.6 = (s32[1,1,128]{2,1,0:T(1,128)S(1)}, s32[1,1,128]{2,1,0:T(1,128)}, u32[]{:S(2)}) copy-start(s32[1,1,128]{2,1,0:T(1,128)} %param.16) | copy-start | bytes 1540
  3.1 9.8 %collective-permute-start = (bf16[64,2048]{1,0:T(8,128)(2,1)}, bf16[64,2048]{1,0:T(8,128)(2,1)}, u32[]{:S(2)}, u32[]{:S(2)}) collective-permute-start(bf16[64,2048]{1,0:T(8,128)(2,1)} %hand_on.17.refs_4_), channel_id=1, source_target_pairs={{0,16},{16,0},{1,17},{17,1},{2,18},{18,2},{3,19},{19,3},{4,20},{20... | collective-permute-start | bytes 786440 | tf_op jit(solution)/shard_map/ppermute | solution.py:417
  6.0 16.2 %collective-permute-start.4 = (bf16[512,384]{1,0:T(8,128)(2,1)}, bf16[512,384]{1,0:T(8,128)(2,1)S(1)}, u32[]{:S(2)}, u32[]{:S(2)}) collective-permute-start(bf16[512,384]{1,0:T(8,128)(2,1)} %weight_part.2.refs_1_), channel_id=1, source_target_pairs={{0,2},{1,3},{2,0},{3,1},{4,6},{5,7},{6,4},{7,5},{8,10},{9,11},{10,... | collective-permute-start | bytes 1179656 | tf_op jit(solution)/shard_map/ppermute | solution.py:394
  9.3 1.0 %copy-start.2 = (bf16[1,1,128,2048]{3,2,1,0:T(8,128)(2,1)S(1)}, bf16[1,1,128,2048]{3,2,1,0:T(8,128)(2,1)}, u32[]{:S(2)}) copy-start(bf16[1,1,128,2048]{3,2,1,0:T(8,128)(2,1)} %param.9) | copy-start | bytes 1572868
  10.4 1.0 %copy-start.3 = (bf16[1,1,128,2048]{3,2,1,0:T(8,128)(2,1)S(1)}, bf16[1,1,128,2048]{3,2,1,0:T(8,128)(2,1)}, u32[]{:S(2)}) copy-start(bf16[1,1,128,2048]{3,2,1,0:T(8,128)(2,1)} %param.10) | copy-start | bytes 1572868
  11.4 0.7 copy-start.7
  12.9 12.6 %collective-permute-start.6 = (bf16[512,384]{1,0:T(8,128)(2,1)}, bf16[512,384]{1,0:T(8,128)(2,1)S(1)}, u32[]{:S(2)}, u32[]{:S(2)}) collective-permute-start(bf16[512,384]{1,0:T(8,128)(2,1)} %hand_on.19), channel_id=1, source_target_pairs={{0,2},{1,3},{2,0},{3,1},{4,6},{5,7},{6,4},{7,5},{8,10},{9,11},{10,... | collective-permute-start | bytes 1179656 | tf_op jit(solution)/shard_map/ppermute | solution.py:394
  14.7 6.9 %copy-start = (bf16[2048,384]{1,0:T(8,128)(2,1)S(1)}, bf16[2048,384]{1,0:T(8,128)(2,1)}, u32[]{:S(2)}) copy-start(bf16[2048,384]{1,0:T(8,128)(2,1)} %whole.3) | copy-start | bytes 4718596
  14.7 6.9 %copy-start.1 = (bf16[384,2048]{1,0:T(8,128)(2,1)S(1)}, bf16[384,2048]{1,0:T(8,128)(2,1)}, u32[]{:S(2)}) copy-start(bf16[384,2048]{1,0:T(8,128)(2,1)} %w_out.1) | copy-start | bytes 4718596
  17.3 19.5 %collective-permute-start.8 = (bf16[96,2048]{1,0:T(8,128)(2,1)S(1)}, bf16[96,2048]{1,0:T(8,128)(2,1)S(1)}, u32[]{:S(2)}, u32[]{:S(2)}) collective-permute-start(bf16[96,2048]{1,0:T(8,128)(2,1)S(1)} %get-tuple-element.44), channel_id=1, source_target_pairs={{0,8},{1,9},{2,10},{3,11},{4,12},{5,13},{6,14},{7,15},{8,0},{9,1},... | collective-permute-start | bytes 1179656 | tf_op jit(solution)/shard_map/ppermute | solution.py:398
  19.9 17.0 %collective-permute-start.3 = (bf16[96,2048]{1,0:T(8,128)(2,1)S(1)}, bf16[96,2048]{1,0:T(8,128)(2,1)S(1)}, u32[]{:S(2)}, u32[]{:S(2)}) collective-permute-start(bf16[96,2048]{1,0:T(8,128)(2,1)S(1)} %get-tuple-element.41.refs_0_.own_in.refs_2_), channel_id=1, source_target_pairs={{0,4},{1,5},{2,6},{3,7},{4,0},{5,1},{6,2},{7,3},{8,12},{9,13},{10,... | collective-permute-start | bytes 1179656 | tf_op jit(solution)/shard_map/ppermute | solution.py:394
  22.3 19.5 %collective-permute-start.5 = (bf16[512,384]{1,0:T(8,128)(2,1)S(1)}, bf16[512,384]{1,0:T(8,128)(2,1)S(1)}, u32[]{:S(2)}, u32[]{:S(2)}) collective-permute-start(bf16[512,384]{1,0:T(8,128)(2,1)S(1)} %hand_on.18.refs_1_.refs_0_), channel_id=1, source_target_pairs={{0,16},{16,0},{1,17},{17,1},{2,18},{18,2},{3,19},{19,3},{4,20},{20... | collective-permute-start | bytes 1179656 | tf_op jit(solution)/shard_map/ppermute | solution.py:402
  25.5 14.7 %collective-permute-start.7 = (bf16[512,384]{1,0:T(8,128)(2,1)S(1)}, bf16[512,384]{1,0:T(8,128)(2,1)S(1)}, u32[]{:S(2)}, u32[]{:S(2)}) collective-permute-start(bf16[512,384]{1,0:T(8,128)(2,1)S(1)} %hand_on.20.refs_2_), channel_id=1, source_target_pairs={{0,16},{16,0},{1,17},{17,1},{2,18},{18,2},{3,19},{19,3},{4,20},{20... | collective-permute-start | bytes 1179656 | tf_op jit(solution)/shard_map/ppermute | solution.py:402
  25.8 14.4 %collective-permute-start.14 = (bf16[112,2048]{1,0:T(8,128)(2,1)S(1)}, bf16[112,2048]{1,0:T(8,128)(2,1)S(1)}, u32[]{:S(2)}, u32[]{:S(2)}) collective-permute-start(bf16[112,2048]{1,0:T(8,128)(2,1)S(1)} %get-tuple-element.51), channel_id=1, source_target_pairs={{0,2},{1,3},{2,0},{3,1},{4,6},{5,7},{6,4},{7,5},{8,10},{9,11},{10,... | collective-permute-start | bytes 1376264 | tf_op jit(solution)/shard_map/ppermute | solution.py:394
  36.9 9.7 %collective-permute-start.9 = (bf16[96,2048]{1,0:T(8,128)(2,1)S(1)}, bf16[96,2048]{1,0:T(8,128)(2,1)S(1)}, u32[]{:S(2)}, u32[]{:S(2)}) collective-permute-start(bf16[96,2048]{1,0:T(8,128)(2,1)S(1)} %hand_on.21.own_in.refs_2_), channel_id=1, source_target_pairs={{0,4},{1,5},{2,6},{3,7},{4,0},{5,1},{6,2},{7,3},{8,12},{9,13},{10,... | collective-permute-start | bytes 1179656 | tf_op jit(solution)/shard_map/ppermute | solution.py:394
  38.4 15.3 %collective-permute-start.16 = (bf16[160,2048]{1,0:T(8,128)(2,1)S(1)}, bf16[160,2048]{1,0:T(8,128)(2,1)S(1)}, u32[]{:S(2)}, u32[]{:S(2)}) collective-permute-start(bf16[160,2048]{1,0:T(8,128)(2,1)S(1)} %get-tuple-element.52), channel_id=1, source_target_pairs={{0,2},{1,3},{2,0},{3,1},{4,6},{5,7},{6,4},{7,5},{8,10},{9,11},{10,... | collective-permute-start | bytes 1966088 | tf_op jit(solution)/shard_map/ppermute | solution.py:394
  40.2 13.5 %collective-permute-start.17 = (bf16[112,2048]{1,0:T(8,128)(2,1)S(1)}, bf16[112,2048]{1,0:T(8,128)(2,1)S(1)}, u32[]{:S(2)}, u32[]{:S(2)}) collective-permute-start(bf16[112,2048]{1,0:T(8,128)(2,1)S(1)} %hand_on.28.refs_4_), channel_id=1, source_target_pairs={{0,1},{1,0},{2,3},{3,2},{4,5},{5,4},{6,7},{7,6},{8,9},{9,8},{10,11... | collective-permute-start | bytes 1376264 | tf_op jit(solution)/shard_map/ppermute | solution.py:394
  40.2 13.5 %collective-permute-start.15 = (bf16[112,2048]{1,0:T(8,128)(2,1)S(1)}, bf16[112,2048]{1,0:T(8,128)(2,1)S(1)}, u32[]{:S(2)}, u32[]{:S(2)}) collective-permute-start(bf16[112,2048]{1,0:T(8,128)(2,1)S(1)} %hand_on.28.refs_4_), channel_id=1, source_target_pairs={{0,16},{16,0},{1,17},{17,1},{2,18},{18,2},{3,19},{19,3},{4,20},{20... | collective-permute-start | bytes 1376264 | tf_op jit(solution)/shard_map/ppermute | solution.py:402
  46.7 1.7 %collective-permute-start.10 = (bf16[512,384]{1,0:T(8,128)(2,1)S(1)}, bf16[512,384]{1,0:T(8,128)(2,1)S(1)}, u32[]{:S(2)}, u32[]{:S(2)}) collective-permute-start(bf16[512,384]{1,0:T(8,128)(2,1)S(1)} %get-tuple-element.45.refs_4_), channel_id=1, source_target_pairs={{0,1},{1,0},{2,3},{3,2},{4,5},{5,4},{6,7},{7,6},{8,9},{9,8},{10,11... | collective-permute-start | bytes 1179656 | tf_op jit(solution)/shard_map/ppermute | solution.py:394
  46.7 2.3 %collective-permute-start.11 = (bf16[512,384]{1,0:T(8,128)(2,1)S(1)}, bf16[512,384]{1,0:T(8,128)(2,1)S(1)}, u32[]{:S(2)}, u32[]{:S(2)}) collective-permute-start(bf16[512,384]{1,0:T(8,128)(2,1)S(1)} %get-tuple-element.46.refs_5_), channel_id=1, source_target_pairs={{0,1},{1,0},{2,3},{3,2},{4,5},{5,4},{6,7},{7,6},{8,9},{9,8},{10,11... | collective-permute-start | bytes 1179656 | tf_op jit(solution)/shard_map/ppermute | solution.py:394
  48.4 1.7 %collective-permute-start.12 = (bf16[512,384]{1,0:T(8,128)(2,1)S(1)}, bf16[512,384]{1,0:T(8,128)(2,1)S(1)}, u32[]{:S(2)}, u32[]{:S(2)}) collective-permute-start(bf16[512,384]{1,0:T(8,128)(2,1)S(1)} %get-tuple-element.47.refs_6_), channel_id=1, source_target_pairs={{0,1},{1,0},{2,3},{3,2},{4,5},{5,4},{6,7},{7,6},{8,9},{9,8},{10,11... | collective-permute-start | bytes 1179656 | tf_op jit(solution)/shard_map/ppermute | solution.py:394
  48.9 1.7 %collective-permute-start.13 = (bf16[512,384]{1,0:T(8,128)(2,1)S(1)}, bf16[512,384]{1,0:T(8,128)(2,1)S(1)}, u32[]{:S(2)}, u32[]{:S(2)}) collective-permute-start(bf16[512,384]{1,0:T(8,128)(2,1)S(1)} %get-tuple-element.48.refs_7_), channel_id=1, source_target_pairs={{0,1},{1,0},{2,3},{3,2},{4,5},{5,4},{6,7},{7,6},{8,9},{9,8},{10,11... | collective-permute-start | bytes 1179656 | tf_op jit(solution)/shard_map/ppermute | solution.py:394
  53.7 2.8 %collective-permute-start.19 = (bf16[160,2048]{1,0:T(8,128)(2,1)S(1)}, bf16[160,2048]{1,0:T(8,128)(2,1)S(1)}, u32[]{:S(2)}, u32[]{:S(2)}) collective-permute-start(bf16[160,2048]{1,0:T(8,128)(2,1)S(1)} %get-tuple-element.54.refs_8_), channel_id=1, source_target_pairs={{0,1},{1,0},{2,3},{3,2},{4,5},{5,4},{6,7},{7,6},{8,9},{9,8},{10,11... | collective-permute-start | bytes 1966088 | tf_op jit(solution)/shard_map/ppermute | solution.py:394
  53.8 2.7 %collective-permute-start.18 = (bf16[112,2048]{1,0:T(8,128)(2,1)S(1)}, bf16[112,2048]{1,0:T(8,128)(2,1)S(1)}, u32[]{:S(2)}, u32[]{:S(2)}) collective-permute-start(bf16[112,2048]{1,0:T(8,128)(2,1)S(1)} %get-tuple-element.53.refs_5_), channel_id=1, source_target_pairs={{0,1},{1,0},{2,3},{3,2},{4,5},{5,4},{6,7},{7,6},{8,9},{9,8},{10,11... | collective-permute-start | bytes 1376264 | tf_op jit(solution)/shard_map/ppermute | solution.py:394
  57.4 7.8 %collective-permute-start.20 = (bf16[96,1024]{1,0:T(8,128)(2,1)S(1)}, bf16[96,1024]{1,0:T(8,128)(2,1)S(1)}, u32[]{:S(2)}, u32[]{:S(2)}) collective-permute-start(bf16[96,1024]{1,0:T(8,128)(2,1)S(1)} %get-tuple-element.58), channel_id=1, source_target_pairs={{0,4},{1,5},{2,6},{3,7},{4,0},{5,1},{6,2},{7,3},{8,12},{9,13},{10,... | collective-permute-start | bytes 589832 | tf_op jit(solution)/shard_map/ppermute | solution.py:394
  59.5 12.9 %collective-permute-start.23 = (bf16[96,1024]{1,0:T(8,128)(2,1)S(1)}, bf16[96,1024]{1,0:T(8,128)(2,1)S(1)}, u32[]{:S(2)}, u32[]{:S(2)}) collective-permute-start(bf16[96,1024]{1,0:T(8,128)(2,1)S(1)} %hand_on.31), channel_id=1, source_target_pairs={{0,4},{1,5},{2,6},{3,7},{4,0},{5,1},{6,2},{7,3},{8,12},{9,13},{10,... | collective-permute-start | bytes 589832 | tf_op jit(solution)/shard_map/ppermute | solution.py:394
  65.2 12.2 %collective-permute-start.22 = (bf16[96,1024]{1,0:T(8,128)(2,1)S(1)}, bf16[96,1024]{1,0:T(8,128)(2,1)S(1)}, u32[]{:S(2)}, u32[]{:S(2)}) collective-permute-start(bf16[96,1024]{1,0:T(8,128)(2,1)S(1)} %get-tuple-element.61), channel_id=1, source_target_pairs={{0,8},{1,9},{2,10},{3,11},{4,12},{5,13},{6,14},{7,15},{8,0},{9,1},... | collective-permute-start | bytes 589832 | tf_op jit(solution)/shard_map/ppermute | solution.py:398
  68.7 16.8 %collective-permute-start.21 = (bf16[96,2048]{1,0:T(8,128)(2,1)S(1)}, bf16[96,2048]{1,0:T(8,128)(2,1)S(1)}, u32[]{:S(2)}, u32[]{:S(2)}) collective-permute-start(bf16[96,2048]{1,0:T(8,128)(2,1)S(1)} %get-tuple-element.60), channel_id=1, source_target_pairs={{0,4},{1,5},{2,6},{3,7},{4,0},{5,1},{6,2},{7,3},{8,12},{9,13},{10,... | collective-permute-start | bytes 1179656 | tf_op jit(solution)/shard_map/ppermute | solution.py:394
  72.4 13.0 %collective-permute-start.24 = (bf16[96,1024]{1,0:T(8,128)(2,1)S(1)}, bf16[96,1024]{1,0:T(8,128)(2,1)S(1)}, u32[]{:S(2)}, u32[]{:S(2)}) collective-permute-start(bf16[96,1024]{1,0:T(8,128)(2,1)S(1)} %far_total.3.refs_1_), channel_id=1, source_target_pairs={{0,8},{1,9},{2,10},{3,11},{4,12},{5,13},{6,14},{7,15},{8,0},{9,1},... | collective-permute-start | bytes 589832 | tf_op jit(solution)/shard_map/ppermute | solution.py:398

commit v19 on v12

--- a/solution.py
+++ b/solution.py
@@ -16,7 +16,13 @@
 FAR_STEPS = 4
 CROSS_STEPS = 1
 CROSS_WEIGHT = 3_000_000_000
-BACK_WEIGHT = 10_000_000_000
+PART_WEIGHT = 1
+FIRST_WEIGHT = 1
+REST_STEPS = 1
+REST_WEIGHT = 1
+SUM_WEIGHT = 1_000_000_000
+BACK_WEIGHT = 3_000_000_000
+BACK_STEPS = 1
 VMEM_LIMIT = 32 * 1024 * 1024
 PART_LIMIT = 60 * 1024 * 1024
 
@@ -188,7 +194,7 @@
 
 def hold_kernel(pipes, pipe_ref, w_in, w_out, *refs):
     in_held, out_held, out_part, out_rest, sems = refs[-5:]
-    size = out_part.shape[0]
+    size, half = out_part.shape
     at = pl.multiple_of(pipe_ref[0] * size, size)
     copies = [
         pltpu.make_async_copy(source, target, sems.at[i])
@@ -196,8 +202,8 @@
             (
                 (w_in, in_held),
                 (w_out, out_held),
-                (w_out.at[pl.ds(at, size)], out_part),
-                (w_out.at[pipes * size :], out_rest),
+                (w_out.at[pl.ds(at, size), pl.ds(0, half)], out_part),
+                (w_out.at[:, pl.ds(half, half)], out_rest),
             )
         )
     ]
@@ -209,14 +215,14 @@
 
 def hold(pipe, w_in, w_out, pipes, after):
     units, width = w_out.shape
-    size = units * 7 // 12 // pipes // 16 * 16
+    half = width // 2
     return call(
         functools.partial(hold_kernel, pipes),
         [
             struct(w_in.shape),
             struct(w_out.shape),
-            struct((size, width)),
-            struct((units - pipes * size, width)),
+            struct((units // pipes, half)),
+            struct((units, half)),
         ],
         [SMEM, ANY, ANY] + [ANY] * len(after),
         "hold_weights",
@@ -284,82 +290,104 @@
     )(pipe, act, own, z, *y_parts, *pair_parts, *after)
 
 
-def down_kernel(pipes, *refs):
+def multiply(act_ref, weights, first, own_ref, z_ref):
+    rows, width = own_ref.shape
+    step = 512
+    for at in range(0, width, step):
+        cols = slice(at, at + step)
+        there = slice(first + at, first + at + step)
+        block = [r[:, there] for r in weights[:2]] + [r[:, cols] for r in weights[2:]]
+        part = jnp.dot(
+            act_ref[...], jnp.concatenate(block, axis=0), preferred_element_type=jnp.float32
+        ).astype(jnp.bfloat16)
+        own_ref[:, cols] = part[:rows]
+        z_ref[:, cols] = part[rows:]
+
+
+def down_first_kernel(pipes, *refs):
     pipe = refs[0][0]
     act_ref, w_own, w_pair = refs[1:4]
-    y_parts, refs = refs[4 : 4 + pipes], refs[4 + pipes :]
-    pair_parts, refs = refs[:pipes], refs[pipes:]
-    y_rest, pair_rest = refs[:2]
+    y_parts = refs[4 : 4 + pipes]
+    pair_parts = refs[4 + pipes : 4 + 2 * pipes]
     own_ref, z_ref, held = refs[-3:]
-    rows, width = own_ref.shape
     units = w_own.shape[0]
     size = y_parts[0].shape[0]
     for shift in range(pipes):
         at = place(pipes, shift, pipe, size)
         held[pl.ds(at, size)] = y_parts[shift][...]
         held[pl.ds(pl.multiple_of(units + at, size), size)] = pair_parts[shift][...]
-    held[pipes * size : units] = y_rest[...]
-    held[units + pipes * size :] = pair_rest[...]
-    step = 512
-    for at in range(0, width, step):
-        cols = slice(at, at + step)
-        weights = jnp.concatenate([w_own[:, cols], w_pair[:, cols], held[:, cols]], axis=0)
-        part = jnp.dot(act_ref[...], weights, preferred_element_type=jnp.float32)
-        part = part.astype(jnp.bfloat16)
-        own_ref[:, cols] = part[:rows]
-        z_ref[:, cols] = part[rows:]
-
-
-def down(pipe, act, w_out, y_parts, pair_parts, rests, after=()):
+    multiply(act_ref, [w_own, w_pair, held], 0, own_ref, z_ref)
+
+
+def down_last_kernel(act_ref, w_own, w_pair, y_rest, pair_rest, *refs):
+    own_ref, z_ref = refs[-2:]
+    multiply(act_ref, [w_own, w_pair, y_rest, pair_rest], own_ref.shape[1], own_ref, z_ref)
+
+
+def down_first(pipe, act, w_out, y_parts, pair_parts):
     rows = act.shape[0] // 2
     units, width = w_out[0].shape
-    pipes = len(y_parts)
-    return call(
-        functools.partial(down_kernel, pipes),
-        [struct((rows, width))] * 2,
-        [SMEM] + [VMEM] * (5 + 2 * pipes) + [ANY] * len(after),
+    pipes, half = len(y_parts), width // 2
+    return call(
+        functools.partial(down_first_kernel, pipes),
+        [struct((rows, half))] * 2,
+        [SMEM] + [VMEM] * (3 + 2 * pipes),
         "expert_down",
-        16 * rows * width * units,
-        8 * units * width,
-        scratch=[pltpu.VMEM((2 * units, width), jnp.bfloat16)],
-    )(pipe, act, *w_out, *y_parts, *pair_parts, *rests, *after)
-
-
-def total_kernel(held, own_ref, z_ref, *refs):
-    refs[held][...] = (own_ref[...].astype(jnp.float32) + z_ref[...].astype(jnp.float32)).astype(
+        16 * rows * half * units,
+        8 * units * half,
+        scratch=[pltpu.VMEM((2 * units, half), jnp.bfloat16)],
+    )(pipe, act, *w_out, *y_parts, *pair_parts)
+
+
+def down_last(act, w_out, rests, after=()):
+    rows = act.shape[0] // 2
+    units, width = w_out[0].shape
+    half = width // 2
+    return call(
+        down_last_kernel,
+        [struct((rows, half))] * 2,
+        [VMEM] * 5 + [ANY] * len(after),
+        "expert_down_last",
+        16 * rows * half * units,
+        8 * units * half,
+    )(act, *w_out, *rests, *after)
+
+
+def total_kernel(own_ref, z_ref, out_ref):
+    out_ref[...] = (own_ref[...].astype(jnp.float32) + z_ref[...].astype(jnp.float32)).astype(
         jnp.bfloat16
     )
 
 
-def total(own, z, held):
-    outs = [struct(own.shape)] + [struct(value.shape) for value in held]
-    return call(
-        functools.partial(total_kernel, len(held)),
-        outs,
-        [VMEM] * 2 + [ANY] * len(held),
+def total(own, z):
+    return call(
+        total_kernel,
+        struct(own.shape),
+        [VMEM] * 2,
         "far_total",
         own.size,
         6 * own.size,
-        out_specs=[VMEM] + [ANY] * len(held),
-        aliases={2 + i: 1 + i for i in range(len(held))},
-    )(own, z, *held)
+    )(own, z)
 
 
 def finish_kernel(groups, cap, *refs):
     hidden_ref, gate_ref, flat_ref = refs[:3]
-    own_ref, z_ref = refs[3:5]
-    back_refs = refs[5:-1]
+    near_refs = refs[3:7]
+    back_refs = refs[7:-1]
     out_ref = refs[-1]
     tokens, width = hidden_ref.shape
+    half = width // 2
     slots = lax.broadcasted_iota(jnp.int32, (tokens, groups * cap), 1)
     picker = (slots == flat_ref[...]).astype(jnp.float32).astype(jnp.bfloat16)
     step = 512
     for at in range(0, width, step):
         cols = slice(at, at + step)
-        near = (own_ref[:, cols].astype(jnp.float32) + z_ref[:, cols].astype(jnp.float32)).astype(
-            jnp.bfloat16
-        )
-        found = jnp.concatenate([near] + [r[:, cols] for r in back_refs], axis=0)
+        side, inner = divmod(at, half)
+        part = slice(inner, inner + step)
+        own, z = near_refs[2 * side][:, part], near_refs[2 * side + 1][:, part]
+        near = (own.astype(jnp.float32) + z.astype(jnp.float32)).astype(jnp.bfloat16)
+        backs = [r[:, part] for r in back_refs[side::2]]
+        found = jnp.concatenate([near, *backs], axis=0)
         picked = jnp.dot(picker, found, preferred_element_type=jnp.float32)
         out_ref[:, cols] = (hidden_ref[:, cols] + gate_ref[...] * picked).astype(jnp.bfloat16)
 
@@ -391,11 +419,6 @@
         shift = count * WSPLIT
         return lax.ppermute(value, "expert", [(i, (i + shift) % devices) for i in range(devices)])
 
-    kv = jnp.transpose(enc_kv[0], (1, 0, 2)).reshape(-1, width)
-    kv_pieces = [kv]
-    for shift in range(1, pipes):
-        perm = [(i, (i + shift) % pipes) for i in range(pipes)]
-        kv_pieces.append(lax.ppermute(kv, "pipe", perm))
     def along(value):
         perms = [[(i, (i + shift) % pipes) for i in range(pipes)] for shift in range(1, pipes)]
         return [value] + [lax.ppermute(value, "pipe", perm) for perm in perms]
@@ -408,6 +431,12 @@
     pipe = pipe.reshape(1)
     depth = width // pipes
     in_y, in_late = (cut_part(pipe, w_in, depth, at, depth // 2) for at in (0, depth // 2))
+    kv = jnp.transpose(enc_kv[0], (1, 0, 2)).reshape(-1, width)
+    (kv,) = after_all([kv], [in_y])
+    kv_pieces = [kv]
+    for shift in range(1, pipes):
+        perm = [(i, (i + shift) % pipes) for i in range(pipes)]
+        kv_pieces.append(lax.ppermute(kv, "pipe", perm))
     in_y = across(in_y, 2)
     in_late = across(*after_all([in_late], kv_pieces[1:2]), 2)
 
@@ -449,7 +478,9 @@
         far_z = after_all(far_z, [], FAR_WEIGHT)
     (far_z,) = far_z
 
-    in_pair = paired(in_parts)
+    in_pair = paired(in_parts[:pipes])
+    in_parts = [*in_parts[:pipes], *after_all(in_parts[pipes:], in_pair)]
+    in_pair += paired(in_parts[pipes:])
 
     def experts_up(own, z, after=()):
         act = up(own, z, [w_in_held, w_in_pair])
@@ -457,22 +488,29 @@
 
     far_act = experts_up(far, far_z)
     out_parts = along(*after_all([out_y], [in_sent]))
-    *out_parts[1:], rest_y = after_all([*out_parts[1:], rest_y], [far_act])
-    out_pair = paired(out_parts)
+    out_pair = paired(out_parts[:1])
+    out_parts[1:] = after_all(out_parts[1:], [far_act, *out_pair], PART_WEIGHT)
+    out_pair += paired(out_parts[1:])
+    w_out_here = [w_out_held, w_out_pair]
+    far_a, sent_a = down_first(pipe, far_act, w_out_here, out_parts, out_pair)
+    near_act = experts_up(near, near_z, [far_a])
+    near_a, near_sent_a = down_first(pipe, near_act, w_out_here, out_parts, out_pair)
+    sum_a = total(far_a, *after_all([across(sent_a, 4)], [], FIRST_WEIGHT))
+    for step in range(REST_STEPS):
+        (rest_y,) = after_all([rest_y], [] if step else [near_a, sum_a], REST_WEIGHT)
     rests = [rest_y, across(rest_y, 1)]
-
-    def experts_down(act, after=()):
-        return down(pipe, act, [w_out_held, w_out_pair], out_parts, out_pair, rests, after)
-
-    far_own, far_sent = experts_down(far_act)
-    near_own, near_sent = experts_down(experts_up(near, near_z, [far_own]))
-    far_sum, near_sent = total(far_own, across(far_sent, 4), [near_sent])
+    far_b, sent_b = down_last(far_act, w_out_here, rests)
+    near_b, near_sent_b = down_last(near_act, w_out_here, rests, [far_b])
+    sum_b = total(far_b, across(sent_b, 4))
     backs = [
-        groups_on(far_sum[(count - 1) * cap : count * cap], groups - count)
+        groups_on(side[(count - 1) * cap : count * cap], groups - count)
         for count in range(1, groups)
+        for side in (sum_a, sum_b)
     ]
-    backs = after_all(backs, [], BACK_WEIGHT)
-    near_sums = [near_own, across(near_sent, 4)]
+    backs[::2] = after_all(backs[::2], [sum_b], SUM_WEIGHT)
+    for _ in range(BACK_STEPS):
+        backs[::2] = after_all(backs[::2], [], BACK_WEIGHT)
+    near_sums = [near_a, across(near_sent_a, 4), near_b, across(near_sent_b, 4)]
     output = finish(hidden, gates, flat, near_sums, backs, groups, cap)
     return output.reshape(1, 1, tokens, width)
 

time: 92.7 us -> 90.4 us (0.975)
  waiting for transfers between devices: 50.2 us -> 44.8 us
  starting transfers between devices: 22.9 us -> 27.1 us
  local copies, waits for them, and re-layouts: 4.5 us -> 3.56 us
    ppermute x2 -> x3, waiting for transfers between devices: 24.2 us -> 3.36 us  [groups_on(): lax.ppermute(value, 'expert', [(i, (i + shift) % devices) for i in range(...]
    ppermute x17 -> x19, waiting for transfers between devices: 25.6 us -> 39.9 us  [across(): return lax.ppermute(value, 'expert', [(i, i ^ bit) for i in range(devices)])]
    ppermute x17 -> x19, starting transfers between devices: 11 us -> 14.6 us  [across(): return lax.ppermute(value, 'expert', [(i, i ^ bit) for i in range(devices)])]
    transpose x1, local copies, waits for them, and re-layouts: 1.75 us -> 0.8 us  [body(): kv = jnp.transpose(enc_kv[0], (1, 0, 2)).reshape(-1, width)]
    pallas_call x3 -> x6, Pallas kernels: 3.13 us -> 3.4 us  [the longest x2 1.7 us: down_first(): call(functools.partial(down_first_kernel, pipes), [struct((rows, half))]...]
    ppermute x2 -> x3, starting transfers between devices: 6.12 us -> 6.1 us  [groups_on(): lax.ppermute(value, 'expert', [(i, (i + shift) % devices) for i in range(...]
    unnamed x16 -> x18, local copies, waits for them, and re-layouts: 2.75 us -> 2.76 us
  transfers between devices with their start and end apart: 23 -> 26, of which waited for: 14 -> 17; matrix products, arithmetic and copies ran while one was open for 2% -> 1% of each run, Pallas kernels for 13% -> 14%
where the time goes in v19:
time: 90.4 us; the launch traced here: 90.1 us
  waiting for transfers between devices  44.8 us (50%)
  starting transfers between devices  27.1 us (30%)
  Pallas kernels  14.4 us (16%)
  local copies, waits for them, and re-layouts  3.56 us (4%)
    ppermute x19, waiting for transfers between devices, across(): return lax.ppermute(value, 'expert', [(i, i ^ bit) for i in range(devices)])  39.9 us
    ppermute x19, starting transfers between devices, across(): return lax.ppermute(value, 'expert', [(i, i ^ bit) for i in range(devices)])  14.6 us
    ppermute x3, starting transfers between devices, groups_on(): lax.ppermute(value, 'expert', [(i, (i + shift) % devices) for i in range(...  6.1 us
    pallas_call x2, Pallas kernels, cut_part(): call(functools.partial(part_kernel, stride, first), struct((size, whole.s...  3.49 us
    ppermute x3, starting transfers between devices, along(): return [value] + [lax.ppermute(value, 'pipe', perm) for perm in perms]  3.4 us
    ppermute x3, waiting for transfers between devices, groups_on(): lax.ppermute(value, 'expert', [(i, (i + shift) % devices) for i in range(...  3.36 us
    ppermute x1, starting transfers between devices, body(): kv_pieces.append(lax.ppermute(kv, 'pipe', perm))  2.93 us
    unnamed x18, local copies, waits for them, and re-layouts  2.76 us
  transfers between devices with their start and end apart: 26, of which 17 were waited for; matrix products, arithmetic and copies ran while one was open for 1% of the time, Pallas kernels for 14%

profile of v19, /device:TPU:0, one launch (start us, length us, event | category | flops | bytes accessed | tf_op | source)
XLA Modules:
  0.0 90.1 jit_solution(10957824329252011482)
XLA Ops:
  0.0 0.5 collective-permute-start.1
  0.5 1.7 %weight_part.2.refs_1_ = bf16[512,384]{1,0:T(8,128)(2,1)} custom-call(s32[1]{0:T(128)} %bitcast.10.pipe_ref.refs_0_, bf16[2048,384]{1,0:T(8,128)(2,1)} %whole.3), custom_call_target="tpu_custom_call" | custom-call | flops 1 | bytes 786432 | tf_op jit(solution)/shard_map/weight_part/pallas_call | solution.py:183
  2.3 0.8 copy.33
  3.1 2.9 %collective-permute-start = (bf16[64,2048]{1,0:T(8,128)(2,1)}, bf16[64,2048]{1,0:T(8,128)(2,1)}, u32[]{:S(2)}, u32[]{:S(2)}) collective-permute-start(bf16[64,2048]{1,0:T(8,128)(2,1)} %hand_on.18.refs_4_), channel_id=1, source_target_pairs={{0,16},{16,0},{1,17},{17,1},{2,18},{18,2},{3,19},{19,3},{4,20},{20... | collective-permute-start | bytes 786440 | tf_op jit(solution)/shard_map/ppermute | solution.py:439
  6.0 1.5 %collective-permute-start.4 = (bf16[512,384]{1,0:T(8,128)(2,1)}, bf16[512,384]{1,0:T(8,128)(2,1)S(1)}, u32[]{:S(2)}, u32[]{:S(2)}) collective-permute-start(bf16[512,384]{1,0:T(8,128)(2,1)} %weight_part.2.refs_1_), channel_id=1, source_target_pairs={{0,2},{1,3},{2,0},{3,1},{4,6},{5,7},{6,4},{7,5},{8,10},{9,11},{10,... | collective-permute-start | bytes 1179656 | tf_op jit(solution)/shard_map/ppermute | solution.py:416
  7.5 1.7 %weight_part.3.refs_0_ = bf16[512,384]{1,0:T(8,128)(2,1)} custom-call(s32[1]{0:T(128)} %bitcast.10.pipe_ref.refs_0_, bf16[2048,384]{1,0:T(8,128)(2,1)} %whole.3), custom_call_target="tpu_custom_call" | custom-call | flops 1 | bytes 786432 | tf_op jit(solution)/shard_map/weight_part/pallas_call | solution.py:183
  9.4 1.0 %copy-done.2 = bf16[1,1,128,2048]{3,2,1,0:T(8,128)(2,1)S(1)} copy-done((bf16[1,1,128,2048]{3,2,1,0:T(8,128)(2,1)S(1)}, bf16[1,1,128,2048]{3,2,1,0:T(8,128)(2,1)}, u32[]{:S(2)}) %copy-start.2) | copy-done | bytes 524312
  10.4 1.0 %copy-done.3 = bf16[1,1,128,2048]{3,2,1,0:T(8,128)(2,1)S(1)} copy-done((bf16[1,1,128,2048]{3,2,1,0:T(8,128)(2,1)S(1)}, bf16[1,1,128,2048]{3,2,1,0:T(8,128)(2,1)}, u32[]{:S(2)}) %copy-start.3) | copy-done | bytes 524312
  11.4 0.7 copy-done.7
  12.2 0.7 collective-permute-done.refs_5_.refs_1_
  12.9 1.8 %collective-permute-start.6 = (bf16[512,384]{1,0:T(8,128)(2,1)}, bf16[512,384]{1,0:T(8,128)(2,1)S(1)}, u32[]{:S(2)}, u32[]{:S(2)}) collective-permute-start(bf16[512,384]{1,0:T(8,128)(2,1)} %hand_on.20), channel_id=1, source_target_pairs={{0,2},{1,3},{2,0},{3,1},{4,6},{5,7},{6,4},{7,5},{8,10},{9,11},{10,... | collective-permute-start | bytes 1179656 | tf_op jit(solution)/shard_map/ppermute | solution.py:416
  14.7 2.6 %attend.1 = (f32[128,2048]{1,0:T(8,128)S(1)}, bf16[96,2048]{1,0:T(8,128)(2,1)S(1)}, bf16[96,2048]{1,0:T(8,128)(2,1)S(1)}) custom-call(bf16[128,2048]{1,0:T(8,128)(2,1)S(1)} %get-tuple-element.34.refs_0_, bf16[128,2048]{1,0:T(8,128)(2,1)S(1)} %get-tuple-element.35.refs_1_, f32[1,2048]{1,0:T(1,128)S(1)} %get-tuple-element.36.refs_2_, ...), custom_call_target="tpu_custom_call" | custom-call | flops 134217728 | bytes 3145728 | tf_op jit(solution)/shard_map/attend/pallas_call | solution.py:158
  17.3 1.6 %collective-permute-start.3 = (bf16[96,2048]{1,0:T(8,128)(2,1)S(1)}, bf16[96,2048]{1,0:T(8,128)(2,1)S(1)}, u32[]{:S(2)}, u32[]{:S(2)}) collective-permute-start(bf16[96,2048]{1,0:T(8,128)(2,1)S(1)} %get-tuple-element.41.refs_0_.own_in.refs_2_), channel_id=1, source_target_pairs={{0,4},{1,5},{2,6},{3,7},{4,0},{5,1},{6,2},{7,3},{8,12},{9,13},{10,... | collective-permute-start | bytes 1179656 | tf_op jit(solution)/shard_map/ppermute | solution.py:416
  18.9 2.6 %collective-permute-start.8 = (bf16[96,2048]{1,0:T(8,128)(2,1)S(1)}, bf16[96,2048]{1,0:T(8,128)(2,1)S(1)}, u32[]{:S(2)}, u32[]{:S(2)}) collective-permute-start(bf16[96,2048]{1,0:T(8,128)(2,1)S(1)} %get-tuple-element.44), channel_id=1, source_target_pairs={{0,8},{1,9},{2,10},{3,11},{4,12},{5,13},{6,14},{7,15},{8,0},{9,1},... | collective-permute-start | bytes 1179656 | tf_op jit(solution)/shard_map/ppermute | solution.py:420
  21.9 1.6 %collective-permute-start.5 = (bf16[512,384]{1,0:T(8,128)(2,1)S(1)}, bf16[512,384]{1,0:T(8,128)(2,1)S(1)}, u32[]{:S(2)}, u32[]{:S(2)}) collective-permute-start(bf16[512,384]{1,0:T(8,128)(2,1)S(1)} %hand_on.19.refs_1_.refs_0_), channel_id=1, source_target_pairs={{0,16},{16,0},{1,17},{17,1},{2,18},{18,2},{3,19},{19,3},{4,20},{20... | collective-permute-start | bytes 1179656 | tf_op jit(solution)/shard_map/ppermute | solution.py:424
  23.5 2.0 %collective-permute-done.6.refs_0_ = bf16[512,384]{1,0:T(8,128)(2,1)S(1)} collective-permute-done((bf16[512,384]{1,0:T(8,128)(2,1)}, bf16[512,384]{1,0:T(8,128)(2,1)S(1)}, u32[]{:S(2)}, u32[]{:S(2)}) %collective-permute-start.6) | collective-permute-done | bytes 393248 | tf_op jit(solution)/shard_map/ppermute | solution.py:416
  25.8 1.7 %collective-permute-start.14 = (bf16[192,1024]{1,0:T(8,128)(2,1)S(1)}, bf16[192,1024]{1,0:T(8,128)(2,1)S(1)}, u32[]{:S(2)}, u32[]{:S(2)}) collective-permute-start(bf16[192,1024]{1,0:T(8,128)(2,1)S(1)} %get-tuple-element.53), channel_id=1, source_target_pairs={{0,2},{1,3},{2,0},{3,1},{4,6},{5,7},{6,4},{7,5},{8,10},{9,11},{10,... | collective-permute-start | bytes 1179656 | tf_op jit(solution)/shard_map/ppermute | solution.py:416
  27.5 8.1 %collective-permute-done.3.z_in.refs_1_.refs_3_ = bf16[96,2048]{1,0:T(8,128)(2,1)S(1)} collective-permute-done((bf16[96,2048]{1,0:T(8,128)(2,1)S(1)}, bf16[96,2048]{1,0:T(8,128)(2,1)S(1)}, u32[]{:S(2)}, u32[]{:S(2)}) %collective-permute-start.3) | collective-permute-done | bytes 393248 | tf_op jit(solution)/shard_map/ppermute | solution.py:416
  35.6 2.5 %collective-permute-done.8.refs_0_ = bf16[96,2048]{1,0:T(8,128)(2,1)S(1)} collective-permute-done((bf16[96,2048]{1,0:T(8,128)(2,1)S(1)}, bf16[96,2048]{1,0:T(8,128)(2,1)S(1)}, u32[]{:S(2)}, u32[]{:S(2)}) %collective-permute-start.8) | collective-permute-done | bytes 393248 | tf_op jit(solution)/shard_map/ppermute | solution.py:420
  38.4 0.5 collective-permute-start.19
  38.9 0.8 collective-permute-done.7.refs_3_.refs_1_
  39.8 1.5 %collective-permute-start.15 = (bf16[192,1024]{1,0:T(8,128)(2,1)S(1)}, bf16[192,1024]{1,0:T(8,128)(2,1)S(1)}, u32[]{:S(2)}, u32[]{:S(2)}) collective-permute-start(bf16[192,1024]{1,0:T(8,128)(2,1)S(1)} %hand_on.30.refs_4_), channel_id=1, source_target_pairs={{0,16},{16,0},{1,17},{17,1},{2,18},{18,2},{3,19},{19,3},{4,20},{20... | collective-permute-start | bytes 1179656 | tf_op jit(solution)/shard_map/ppermute | solution.py:424
  41.3 4.6 %collective-permute-done.9.refs_4_.refs_0_ = bf16[96,2048]{1,0:T(8,128)(2,1)S(1)} collective-permute-done((bf16[96,2048]{1,0:T(8,128)(2,1)S(1)}, bf16[96,2048]{1,0:T(8,128)(2,1)S(1)}, u32[]{:S(2)}, u32[]{:S(2)}) %collective-permute-start.9) | collective-permute-done | bytes 393248 | tf_op jit(solution)/shard_map/ppermute | solution.py:416
  45.9 0.5 collective-permute-start.11
  46.4 1.2 %collective-permute-done.10.refs_2_.refs_8_ = bf16[512,384]{1,0:T(8,128)(2,1)S(1)} collective-permute-done((bf16[512,384]{1,0:T(8,128)(2,1)S(1)}, bf16[512,384]{1,0:T(8,128)(2,1)S(1)}, u32[]{:S(2)}, u32[]{:S(2)}) %collective-permute-start.10) | collective-permute-done | bytes 393248 | tf_op jit(solution)/shard_map/ppermute | solution.py:416
  47.6 0.6 collective-permute-done.11.refs_3_.refs_9_
  48.7 0.8 expert_up.3.refs_1_
  49.9 0.6 collective-permute-done.13.refs_11_
  50.4 0.9 expert_up_y.2.refs_1_.act_ref
  51.5 1.6 %collective-permute-done.17.refs_7_ = bf16[192,1024]{1,0:T(8,128)(2,1)S(1)} collective-permute-done((bf16[192,1024]{1,0:T(8,128)(2,1)S(1)}, bf16[192,1024]{1,0:T(8,128)(2,1)S(1)}, u32[]{:S(2)}, u32[]{:S(2)}) %collective-permute-start.17) | collective-permute-done | bytes 393248 | tf_op jit(solution)/shard_map/ppermute | solution.py:416
  53.1 0.9 expert_down.2
  54.0 1.6 %collective-permute-start.20 = (bf16[96,1024]{1,0:T(8,128)(2,1)S(1)}, bf16[96,1024]{1,0:T(8,128)(2,1)S(1)}, u32[]{:S(2)}, u32[]{:S(2)}) collective-permute-start(bf16[96,1024]{1,0:T(8,128)(2,1)S(1)} %get-tuple-element.58), channel_id=1, source_target_pairs={{0,4},{1,5},{2,6},{3,7},{4,0},{5,1},{6,2},{7,3},{8,12},{9,13},{10,... | collective-permute-start | bytes 589832 | tf_op jit(solution)/shard_map/ppermute | solution.py:416
  55.6 0.8 expert_up.2.refs_1_
  56.4 0.9 expert_up_y.3.refs_1_.act_ref
  57.3 3.7 %collective-permute-done.20.refs_0_ = bf16[96,1024]{1,0:T(8,128)(2,1)S(1)} collective-permute-done((bf16[96,1024]{1,0:T(8,128)(2,1)S(1)}, bf16[96,1024]{1,0:T(8,128)(2,1)S(1)}, u32[]{:S(2)}, u32[]{:S(2)}) %collective-permute-start.20) | collective-permute-done | bytes 196640 | tf_op jit(solution)/shard_map/ppermute | solution.py:416
  61.0 0.8 expert_down.3
  62.0 2.3 %collective-permute-done.21.pair_rest = bf16[384,1024]{1,0:T(8,128)(2,1)S(1)} collective-permute-done((bf16[384,1024]{1,0:T(8,128)(2,1)S(1)}, bf16[384,1024]{1,0:T(8,128)(2,1)S(1)}, u32[]{:S(2)}, u32[]{:S(2)}) %collective-permute-start.21) | collective-permute-done | bytes 786464 | tf_op jit(solution)/shard_map/ppermute | solution.py:416
  64.3 0.8 expert_down_last.2
  65.1 1.6 %collective-permute-start.24 = (bf16[96,1024]{1,0:T(8,128)(2,1)S(1)}, bf16[96,1024]{1,0:T(8,128)(2,1)S(1)}, u32[]{:S(2)}, u32[]{:S(2)}) collective-permute-start(bf16[96,1024]{1,0:T(8,128)(2,1)S(1)} %get-tuple-element.62), channel_id=1, source_target_pairs={{0,4},{1,5},{2,6},{3,7},{4,0},{5,1},{6,2},{7,3},{8,12},{9,13},{10,... | collective-permute-start | bytes 589832 | tf_op jit(solution)/shard_map/ppermute | solution.py:416
  66.7 2.0 %collective-permute-start.23 = (bf16[96,1024]{1,0:T(8,128)(2,1)S(1)}, bf16[96,1024]{1,0:T(8,128)(2,1)S(1)}, u32[]{:S(2)}, u32[]{:S(2)}) collective-permute-start(bf16[96,1024]{1,0:T(8,128)(2,1)S(1)} %far_total.2.refs_2_), channel_id=1, source_target_pairs={{0,8},{1,9},{2,10},{3,11},{4,12},{5,13},{6,14},{7,15},{8,0},{9,1},... | collective-permute-start | bytes 589832 | tf_op jit(solution)/shard_map/ppermute | solution.py:420
  69.0 0.8 expert_down_last.3
  69.8 1.8 %collective-permute-start.22 = (bf16[96,1024]{1,0:T(8,128)(2,1)S(1)}, bf16[96,1024]{1,0:T(8,128)(2,1)S(1)}, u32[]{:S(2)}, u32[]{:S(2)}) collective-permute-start(bf16[96,1024]{1,0:T(8,128)(2,1)S(1)} %get-tuple-element.61), channel_id=1, source_target_pairs={{0,4},{1,5},{2,6},{3,7},{4,0},{5,1},{6,2},{7,3},{8,12},{9,13},{10,... | collective-permute-start | bytes 589832 | tf_op jit(solution)/shard_map/ppermute | solution.py:416
  71.6 4.6 %collective-permute-done.24.z_ref = bf16[96,1024]{1,0:T(8,128)(2,1)S(1)} collective-permute-done((bf16[96,1024]{1,0:T(8,128)(2,1)S(1)}, bf16[96,1024]{1,0:T(8,128)(2,1)S(1)}, u32[]{:S(2)}, u32[]{:S(2)}) %collective-permute-start.24) | collective-permute-done | bytes 196640 | tf_op jit(solution)/shard_map/ppermute | solution.py:416
  76.3 1.5 %collective-permute-start.25 = (bf16[96,1024]{1,0:T(8,128)(2,1)S(1)}, bf16[96,1024]{1,0:T(8,128)(2,1)S(1)}, u32[]{:S(2)}, u32[]{:S(2)}) collective-permute-start(bf16[96,1024]{1,0:T(8,128)(2,1)S(1)} %far_total.3.refs_1_), channel_id=1, source_target_pairs={{0,8},{1,9},{2,10},{3,11},{4,12},{5,13},{6,14},{7,15},{8,0},{9,1},... | collective-permute-start | bytes 589832 | tf_op jit(solution)/shard_map/ppermute | solution.py:420
  77.8 0.9 collective-permute-done.23.refs_0_
  78.7 6.8 %collective-permute-done.18.refs_4_ = bf16[96,1024]{1,0:T(8,128)(2,1)S(1)} collective-permute-done((bf16[96,1024]{1,0:T(8,128)(2,1)S(1)}, bf16[96,1024]{1,0:T(8,128)(2,1)S(1)}, u32[]{:S(2)}, u32[]{:S(2)}) %collective-permute-start.18) | collective-permute-done | bytes 196640 | tf_op jit(solution)/shard_map/ppermute | solution.py:416
  85.5 3.4 %collective-permute-done.22.refs_6_ = bf16[96,1024]{1,0:T(8,128)(2,1)S(1)} collective-permute-done((bf16[96,1024]{1,0:T(8,128)(2,1)S(1)}, bf16[96,1024]{1,0:T(8,128)(2,1)S(1)}, u32[]{:S(2)}, u32[]{:S(2)}) %collective-permute-start.22) | collective-permute-done | bytes 196640 | tf_op jit(solution)/shard_map/ppermute | solution.py:416
  89.0 1.2 %finish.1 = bf16[128,2048]{1,0:T(8,128)(2,1)} custom-call(f32[128,2048]{1,0:T(8,128)S(1)} %get-tuple-element.38.refs_0_, f32[128,1]{1,0:T(8,128)S(1)} %get-tuple-element.39.refs_1_, s32[128,1]{1,0:T(8,128)S(1)} %get-tuple-element.40.refs_2_, bf16[96,1024]{1,0:T(8,128)(2,1)S(1)} %get-tuple-element.55.refs_1_.refs_3_, ...), custom_call_target="tpu_custom_call" | custom-call | flops 201326592 | bytes 4194304 | tf_op jit(solution)/shard_map/finish/pallas_call | solution.py:398
  (57 shorter events, 2.9 us)
Async XLA Ops:
  0.0 2.3 %copy-start.8 = (bf16[1,32,2,2048]{3,2,1,0:T(2,128)(2,1)S(1)}, bf16[1,32,2,2048]{3,2,1,0:T(2,128)(2,1)}, u32[]{:S(2)}) copy-start(bf16[1,32,2,2048]{3,2,1,0:T(2,128)(2,1)} %param.11) | copy-start | bytes 786436
  0.0 14.6 %collective-permute-start.1 = (bf16[2048,384]{1,0:T(8,128)(2,1)}, bf16[2048,384]{1,0:T(8,128)(2,1)S(1)}, u32[]{:S(2)}, u32[]{:S(2)}) collective-permute-start(bf16[2048,384]{1,0:T(8,128)(2,1)} %whole.3), channel_id=1, source_target_pairs={{0,1},{1,0},{2,3},{3,2},{4,5},{5,4},{6,7},{7,6},{8,9},{9,8},{10,11... | collective-permute-start | bytes 4718600 | tf_op jit(solution)/shard_map/ppermute | solution.py:416
  0.5 14.2 %collective-permute-start.2 = (bf16[384,2048]{1,0:T(8,128)(2,1)}, bf16[384,2048]{1,0:T(8,128)(2,1)S(1)}, u32[]{:S(2)}, u32[]{:S(2)}) collective-permute-start(bf16[384,2048]{1,0:T(8,128)(2,1)} %w_out.1), channel_id=1, source_target_pairs={{0,1},{1,0},{2,3},{3,2},{4,5},{5,4},{6,7},{7,6},{8,9},{9,8},{10,11... | collective-permute-start | bytes 4718600 | tf_op jit(solution)/shard_map/ppermute | solution.py:416
  3.1 6.2 %copy-start.4 = (f32[2048]{0:T(1024)S(1)}, f32[2048]{0:T(1024)}, u32[]{:S(2)}) copy-start(f32[2048]{0:T(1024)} %param.12) | copy-start | bytes 24580
  3.1 6.2 %copy-start.5 = (s32[1,1,128]{2,1,0:T(1,128)S(1)}, s32[1,1,128]{2,1,0:T(1,128)}, u32[]{:S(2)}) copy-start(s32[1,1,128]{2,1,0:T(1,128)} %param.15) | copy-start | bytes 1540
  3.1 6.2 %copy-start.6 = (s32[1,1,128]{2,1,0:T(1,128)S(1)}, s32[1,1,128]{2,1,0:T(1,128)}, u32[]{:S(2)}) copy-start(s32[1,1,128]{2,1,0:T(1,128)} %param.16) | copy-start | bytes 1540
  3.1 9.8 %collective-permute-start = (bf16[64,2048]{1,0:T(8,128)(2,1)}, bf16[64,2048]{1,0:T(8,128)(2,1)}, u32[]{:S(2)}, u32[]{:S(2)}) collective-permute-start(bf16[64,2048]{1,0:T(8,128)(2,1)} %hand_on.18.refs_4_), channel_id=1, source_target_pairs={{0,16},{16,0},{1,17},{17,1},{2,18},{18,2},{3,19},{19,3},{4,20},{20... | collective-permute-start | bytes 786440 | tf_op jit(solution)/shard_map/ppermute | solution.py:439
  6.0 15.8 %collective-permute-start.4 = (bf16[512,384]{1,0:T(8,128)(2,1)}, bf16[512,384]{1,0:T(8,128)(2,1)S(1)}, u32[]{:S(2)}, u32[]{:S(2)}) collective-permute-start(bf16[512,384]{1,0:T(8,128)(2,1)} %weight_part.2.refs_1_), channel_id=1, source_target_pairs={{0,2},{1,3},{2,0},{3,1},{4,6},{5,7},{6,4},{7,5},{8,10},{9,11},{10,... | collective-permute-start | bytes 1179656 | tf_op jit(solution)/shard_map/ppermute | solution.py:416
  9.3 1.0 %copy-start.2 = (bf16[1,1,128,2048]{3,2,1,0:T(8,128)(2,1)S(1)}, bf16[1,1,128,2048]{3,2,1,0:T(8,128)(2,1)}, u32[]{:S(2)}) copy-start(bf16[1,1,128,2048]{3,2,1,0:T(8,128)(2,1)} %param.9) | copy-start | bytes 1572868
  10.4 1.0 %copy-start.3 = (bf16[1,1,128,2048]{3,2,1,0:T(8,128)(2,1)S(1)}, bf16[1,1,128,2048]{3,2,1,0:T(8,128)(2,1)}, u32[]{:S(2)}) copy-start(bf16[1,1,128,2048]{3,2,1,0:T(8,128)(2,1)} %param.10) | copy-start | bytes 1572868
  11.4 0.7 copy-start.7
  12.9 12.6 %collective-permute-start.6 = (bf16[512,384]{1,0:T(8,128)(2,1)}, bf16[512,384]{1,0:T(8,128)(2,1)S(1)}, u32[]{:S(2)}, u32[]{:S(2)}) collective-permute-start(bf16[512,384]{1,0:T(8,128)(2,1)} %hand_on.20), channel_id=1, source_target_pairs={{0,2},{1,3},{2,0},{3,1},{4,6},{5,7},{6,4},{7,5},{8,10},{9,11},{10,... | collective-permute-start | bytes 1179656 | tf_op jit(solution)/shard_map/ppermute | solution.py:416
  14.7 6.9 %copy-start = (bf16[2048,384]{1,0:T(8,128)(2,1)S(1)}, bf16[2048,384]{1,0:T(8,128)(2,1)}, u32[]{:S(2)}) copy-start(bf16[2048,384]{1,0:T(8,128)(2,1)} %whole.3) | copy-start | bytes 4718596
  14.7 6.9 %copy-start.1 = (bf16[384,2048]{1,0:T(8,128)(2,1)S(1)}, bf16[384,2048]{1,0:T(8,128)(2,1)}, u32[]{:S(2)}) copy-start(bf16[384,2048]{1,0:T(8,128)(2,1)} %w_out.1) | copy-start | bytes 4718596
  17.3 18.3 %collective-permute-start.3 = (bf16[96,2048]{1,0:T(8,128)(2,1)S(1)}, bf16[96,2048]{1,0:T(8,128)(2,1)S(1)}, u32[]{:S(2)}, u32[]{:S(2)}) collective-permute-start(bf16[96,2048]{1,0:T(8,128)(2,1)S(1)} %get-tuple-element.41.refs_0_.own_in.refs_2_), channel_id=1, source_target_pairs={{0,4},{1,5},{2,6},{3,7},{4,0},{5,1},{6,2},{7,3},{8,12},{9,13},{10,... | collective-permute-start | bytes 1179656 | tf_op jit(solution)/shard_map/ppermute | solution.py:416
  18.9 19.2 %collective-permute-start.8 = (bf16[96,2048]{1,0:T(8,128)(2,1)S(1)}, bf16[96,2048]{1,0:T(8,128)(2,1)S(1)}, u32[]{:S(2)}, u32[]{:S(2)}) collective-permute-start(bf16[96,2048]{1,0:T(8,128)(2,1)S(1)} %get-tuple-element.44), channel_id=1, source_target_pairs={{0,8},{1,9},{2,10},{3,11},{4,12},{5,13},{6,14},{7,15},{8,0},{9,1},... | collective-permute-start | bytes 1179656 | tf_op jit(solution)/shard_map/ppermute | solution.py:420
  21.9 19.4 %collective-permute-start.5 = (bf16[512,384]{1,0:T(8,128)(2,1)S(1)}, bf16[512,384]{1,0:T(8,128)(2,1)S(1)}, u32[]{:S(2)}, u32[]{:S(2)}) collective-permute-start(bf16[512,384]{1,0:T(8,128)(2,1)S(1)} %hand_on.19.refs_1_.refs_0_), channel_id=1, source_target_pairs={{0,16},{16,0},{1,17},{17,1},{2,18},{18,2},{3,19},{19,3},{4,20},{20... | collective-permute-start | bytes 1179656 | tf_op jit(solution)/shard_map/ppermute | solution.py:424
  25.5 14.3 %collective-permute-start.7 = (bf16[512,384]{1,0:T(8,128)(2,1)S(1)}, bf16[512,384]{1,0:T(8,128)(2,1)S(1)}, u32[]{:S(2)}, u32[]{:S(2)}) collective-permute-start(bf16[512,384]{1,0:T(8,128)(2,1)S(1)} %hand_on.21.refs_2_), channel_id=1, source_target_pairs={{0,16},{16,0},{1,17},{17,1},{2,18},{18,2},{3,19},{19,3},{4,20},{20... | collective-permute-start | bytes 1179656 | tf_op jit(solution)/shard_map/ppermute | solution.py:424
  25.8 13.1 %collective-permute-start.14 = (bf16[192,1024]{1,0:T(8,128)(2,1)S(1)}, bf16[192,1024]{1,0:T(8,128)(2,1)S(1)}, u32[]{:S(2)}, u32[]{:S(2)}) collective-permute-start(bf16[192,1024]{1,0:T(8,128)(2,1)S(1)} %get-tuple-element.53), channel_id=1, source_target_pairs={{0,2},{1,3},{2,0},{3,1},{4,6},{5,7},{6,4},{7,5},{8,10},{9,11},{10,... | collective-permute-start | bytes 1179656 | tf_op jit(solution)/shard_map/ppermute | solution.py:416
  38.1 7.8 %collective-permute-start.9 = (bf16[96,2048]{1,0:T(8,128)(2,1)S(1)}, bf16[96,2048]{1,0:T(8,128)(2,1)S(1)}, u32[]{:S(2)}, u32[]{:S(2)}) collective-permute-start(bf16[96,2048]{1,0:T(8,128)(2,1)S(1)} %hand_on.22.own_in.refs_2_), channel_id=1, source_target_pairs={{0,4},{1,5},{2,6},{3,7},{4,0},{5,1},{6,2},{7,3},{8,12},{9,13},{10,... | collective-permute-start | bytes 1179656 | tf_op jit(solution)/shard_map/ppermute | solution.py:416
  38.4 23.5 %collective-permute-start.19 = (bf16[384,1024]{1,0:T(8,128)(2,1)S(1)}, bf16[384,1024]{1,0:T(8,128)(2,1)S(1)}, u32[]{:S(2)}, u32[]{:S(2)}) collective-permute-start(bf16[384,1024]{1,0:T(8,128)(2,1)S(1)} %get-tuple-element.57), channel_id=1, source_target_pairs={{0,2},{1,3},{2,0},{3,1},{4,6},{5,7},{6,4},{7,5},{8,10},{9,11},{10,... | collective-permute-start | bytes 2359304 | tf_op jit(solution)/shard_map/ppermute | solution.py:416
  39.8 11.5 %collective-permute-start.15 = (bf16[192,1024]{1,0:T(8,128)(2,1)S(1)}, bf16[192,1024]{1,0:T(8,128)(2,1)S(1)}, u32[]{:S(2)}, u32[]{:S(2)}) collective-permute-start(bf16[192,1024]{1,0:T(8,128)(2,1)S(1)} %hand_on.30.refs_4_), channel_id=1, source_target_pairs={{0,16},{16,0},{1,17},{17,1},{2,18},{18,2},{3,19},{19,3},{4,20},{20... | collective-permute-start | bytes 1179656 | tf_op jit(solution)/shard_map/ppermute | solution.py:424
  41.3 10.0 %collective-permute-start.16 = (bf16[192,1024]{1,0:T(8,128)(2,1)S(1)}, bf16[192,1024]{1,0:T(8,128)(2,1)S(1)}, u32[]{:S(2)}, u32[]{:S(2)}) collective-permute-start(bf16[192,1024]{1,0:T(8,128)(2,1)S(1)} %hand_on.30.refs_4_), channel_id=1, source_target_pairs={{0,1},{1,0},{2,3},{3,2},{4,5},{5,4},{6,7},{7,6},{8,9},{9,8},{10,11... | collective-permute-start | bytes 1179656 | tf_op jit(solution)/shard_map/ppermute | solution.py:416
  45.9 1.7 %collective-permute-start.10 = (bf16[512,384]{1,0:T(8,128)(2,1)S(1)}, bf16[512,384]{1,0:T(8,128)(2,1)S(1)}, u32[]{:S(2)}, u32[]{:S(2)}) collective-permute-start(bf16[512,384]{1,0:T(8,128)(2,1)S(1)} %get-tuple-element.45.refs_4_), channel_id=1, source_target_pairs={{0,1},{1,0},{2,3},{3,2},{4,5},{5,4},{6,7},{7,6},{8,9},{9,8},{10,11... | collective-permute-start | bytes 1179656 | tf_op jit(solution)/shard_map/ppermute | solution.py:416
  45.9 2.3 %collective-permute-start.11 = (bf16[512,384]{1,0:T(8,128)(2,1)S(1)}, bf16[512,384]{1,0:T(8,128)(2,1)S(1)}, u32[]{:S(2)}, u32[]{:S(2)}) collective-permute-start(bf16[512,384]{1,0:T(8,128)(2,1)S(1)} %get-tuple-element.46.refs_5_), channel_id=1, source_target_pairs={{0,1},{1,0},{2,3},{3,2},{4,5},{5,4},{6,7},{7,6},{8,9},{9,8},{10,11... | collective-permute-start | bytes 1179656 | tf_op jit(solution)/shard_map/ppermute | solution.py:416
  48.2 1.7 %collective-permute-start.12 = (bf16[512,384]{1,0:T(8,128)(2,1)S(1)}, bf16[512,384]{1,0:T(8,128)(2,1)S(1)}, u32[]{:S(2)}, u32[]{:S(2)}) collective-permute-start(bf16[512,384]{1,0:T(8,128)(2,1)S(1)} %get-tuple-element.49.refs_6_), channel_id=1, source_target_pairs={{0,1},{1,0},{2,3},{3,2},{4,5},{5,4},{6,7},{7,6},{8,9},{9,8},{10,11... | collective-permute-start | bytes 1179656 | tf_op jit(solution)/shard_map/ppermute | solution.py:416
  48.3 2.1 %collective-permute-start.13 = (bf16[512,384]{1,0:T(8,128)(2,1)S(1)}, bf16[512,384]{1,0:T(8,128)(2,1)S(1)}, u32[]{:S(2)}, u32[]{:S(2)}) collective-permute-start(bf16[512,384]{1,0:T(8,128)(2,1)S(1)} %get-tuple-element.50.refs_7_), channel_id=1, source_target_pairs={{0,1},{1,0},{2,3},{3,2},{4,5},{5,4},{6,7},{7,6},{8,9},{9,8},{10,11... | collective-permute-start | bytes 1179656 | tf_op jit(solution)/shard_map/ppermute | solution.py:416
  51.3 1.8 %collective-permute-start.17 = (bf16[192,1024]{1,0:T(8,128)(2,1)S(1)}, bf16[192,1024]{1,0:T(8,128)(2,1)S(1)}, u32[]{:S(2)}, u32[]{:S(2)}) collective-permute-start(bf16[192,1024]{1,0:T(8,128)(2,1)S(1)} %hand_on.31.refs_5_), channel_id=1, source_target_pairs={{0,1},{1,0},{2,3},{3,2},{4,5},{5,4},{6,7},{7,6},{8,9},{9,8},{10,11... | collective-permute-start | bytes 1179656 | tf_op jit(solution)/shard_map/ppermute | solution.py:416
  54.0 7.0 %collective-permute-start.20 = (bf16[96,1024]{1,0:T(8,128)(2,1)S(1)}, bf16[96,1024]{1,0:T(8,128)(2,1)S(1)}, u32[]{:S(2)}, u32[]{:S(2)}) collective-permute-start(bf16[96,1024]{1,0:T(8,128)(2,1)S(1)} %get-tuple-element.58), channel_id=1, source_target_pairs={{0,4},{1,5},{2,6},{3,7},{4,0},{5,1},{6,2},{7,3},{8,12},{9,13},{10,... | collective-permute-start | bytes 589832 | tf_op jit(solution)/shard_map/ppermute | solution.py:416
  61.9 2.4 %collective-permute-start.21 = (bf16[384,1024]{1,0:T(8,128)(2,1)S(1)}, bf16[384,1024]{1,0:T(8,128)(2,1)S(1)}, u32[]{:S(2)}, u32[]{:S(2)}) collective-permute-start(bf16[384,1024]{1,0:T(8,128)(2,1)S(1)} %hand_on.33.y_rest), channel_id=1, source_target_pairs={{0,1},{1,0},{2,3},{3,2},{4,5},{5,4},{6,7},{7,6},{8,9},{9,8},{10,11... | collective-permute-start | bytes 2359304 | tf_op jit(solution)/shard_map/ppermute | solution.py:416
  65.1 11.2 %collective-permute-start.24 = (bf16[96,1024]{1,0:T(8,128)(2,1)S(1)}, bf16[96,1024]{1,0:T(8,128)(2,1)S(1)}, u32[]{:S(2)}, u32[]{:S(2)}) collective-permute-start(bf16[96,1024]{1,0:T(8,128)(2,1)S(1)} %get-tuple-element.62), channel_id=1, source_target_pairs={{0,4},{1,5},{2,6},{3,7},{4,0},{5,1},{6,2},{7,3},{8,12},{9,13},{10,... | collective-permute-start | bytes 589832 | tf_op jit(solution)/shard_map/ppermute | solution.py:416
  66.7 12.0 %collective-permute-start.23 = (bf16[96,1024]{1,0:T(8,128)(2,1)S(1)}, bf16[96,1024]{1,0:T(8,128)(2,1)S(1)}, u32[]{:S(2)}, u32[]{:S(2)}) collective-permute-start(bf16[96,1024]{1,0:T(8,128)(2,1)S(1)} %far_total.2.refs_2_), channel_id=1, source_target_pairs={{0,8},{1,9},{2,10},{3,11},{4,12},{5,13},{6,14},{7,15},{8,0},{9,1},... | collective-permute-start | bytes 589832 | tf_op jit(solution)/shard_map/ppermute | solution.py:420
  68.7 16.8 %collective-permute-start.18 = (bf16[96,1024]{1,0:T(8,128)(2,1)S(1)}, bf16[96,1024]{1,0:T(8,128)(2,1)S(1)}, u32[]{:S(2)}, u32[]{:S(2)}) collective-permute-start(bf16[96,1024]{1,0:T(8,128)(2,1)S(1)} %get-tuple-element.56), channel_id=1, source_target_pairs={{0,4},{1,5},{2,6},{3,7},{4,0},{5,1},{6,2},{7,3},{8,12},{9,13},{10,... | collective-permute-start | bytes 589832 | tf_op jit(solution)/shard_map/ppermute | solution.py:416
  69.8 19.1 %collective-permute-start.22 = (bf16[96,1024]{1,0:T(8,128)(2,1)S(1)}, bf16[96,1024]{1,0:T(8,128)(2,1)S(1)}, u32[]{:S(2)}, u32[]{:S(2)}) collective-permute-start(bf16[96,1024]{1,0:T(8,128)(2,1)S(1)} %get-tuple-element.61), channel_id=1, source_target_pairs={{0,4},{1,5},{2,6},{3,7},{4,0},{5,1},{6,2},{7,3},{8,12},{9,13},{10,... | collective-permute-start | bytes 589832 | tf_op jit(solution)/shard_map/ppermute | solution.py:416
  76.3 12.6 %collective-permute-start.25 = (bf16[96,1024]{1,0:T(8,128)(2,1)S(1)}, bf16[96,1024]{1,0:T(8,128)(2,1)S(1)}, u32[]{:S(2)}, u32[]{:S(2)}) collective-permute-start(bf16[96,1024]{1,0:T(8,128)(2,1)S(1)} %far_total.3.refs_1_), channel_id=1, source_target_pairs={{0,8},{1,9},{2,10},{3,11},{4,12},{5,13},{6,14},{7,15},{8,0},{9,1},... | collective-permute-start | bytes 589832 | tf_op jit(solution)/shard_map/ppermute | solution.py:420

commit v20 on v14

--- a/solution.py
+++ b/solution.py
@@ -299,7 +299,7 @@
     for shift in range(pipes):
         at = place(pipes, shift, pipe, size)
         held[pl.ds(at, size)] = y_parts[shift][:, whole]
-        held[pl.ds(pl.multiple_of(units + at, size), size)] = pair_parts[shift][:, whole]
+        held[pl.ds(pl.multiple_of(units + at, 16), size)] = pair_parts[shift][:, whole]
     held[pipes * size : units] = y_rest[:, whole]
     held[units + pipes * size :] = pair_rest[:, whole]
     step = 512

time: 87.3 us -> 87.3 us (level)
  no operation moved by 1% of the time
where the time goes in v20:
time: 87.3 us; the launch traced here: 86.6 us
  waiting for transfers between devices  41.3 us (47%)
  starting transfers between devices  26.8 us (31%)
  Pallas kernels  14.7 us (17%)
  local copies, waits for them, and re-layouts  3.56 us (4%)
    ppermute x3, waiting for transfers between devices, groups_on(): lax.ppermute(value, 'expert', [(i, (i + shift) % devices) for i in range(...  19.8 us
    ppermute x18, waiting for transfers between devices, across(): return lax.ppermute(value, 'expert', [(i, i ^ bit) for i in range(devices)])  19.6 us
    ppermute x18, starting transfers between devices, across(): return lax.ppermute(value, 'expert', [(i, i ^ bit) for i in range(devices)])  12.6 us
    ppermute x3, starting transfers between devices, groups_on(): lax.ppermute(value, 'expert', [(i, (i + shift) % devices) for i in range(...  7.77 us
    pallas_call x2, Pallas kernels, cut_part(): call(functools.partial(part_kernel, stride, first), struct((size, whole.s...  3.49 us
    ppermute x3, starting transfers between devices, along(): return [value] + [lax.ppermute(value, 'pipe', perm) for perm in perms]  3.46 us
    pallas_call x3, Pallas kernels, down(): call(functools.partial(down_kernel, pipes, first), [struct((rows, width))...  3.19 us
    ppermute x1, starting transfers between devices, body(): kv_pieces.append(lax.ppermute(kv, 'pipe', perm))  2.93 us
  transfers between devices with their start and end apart: 25, of which 17 were waited for; matrix products, arithmetic and copies ran while one was open for 1% of the time, Pallas kernels for 15%

profile of v20, /device:TPU:0, one launch (start us, length us, event | category | flops | bytes accessed | tf_op | source)
XLA Modules:
  0.0 86.6 jit_solution(12824094342543805301)
XLA Ops:
  0.0 0.5 collective-permute-start.2
  0.5 1.7 %weight_part.2.refs_1_ = bf16[512,384]{1,0:T(8,128)(2,1)} custom-call(s32[1]{0:T(128)} %bitcast.10.pipe_ref.refs_0_, bf16[2048,384]{1,0:T(8,128)(2,1)} %whole.3), custom_call_target="tpu_custom_call" | custom-call | flops 1 | bytes 786432 | tf_op jit(solution)/shard_map/weight_part/pallas_call | solution.py:178
  2.3 0.8 copy.32
  3.1 2.9 %collective-permute-start = (bf16[64,2048]{1,0:T(8,128)(2,1)}, bf16[64,2048]{1,0:T(8,128)(2,1)}, u32[]{:S(2)}, u32[]{:S(2)}) collective-permute-start(bf16[64,2048]{1,0:T(8,128)(2,1)} %hand_on.16.refs_4_), channel_id=1, source_target_pairs={{0,16},{16,0},{1,17},{17,1},{2,18},{18,2},{3,19},{19,3},{4,20},{20... | collective-permute-start | bytes 786440 | tf_op jit(solution)/shard_map/ppermute | solution.py:416
  6.0 1.5 %collective-permute-start.4 = (bf16[512,384]{1,0:T(8,128)(2,1)}, bf16[512,384]{1,0:T(8,128)(2,1)S(1)}, u32[]{:S(2)}, u32[]{:S(2)}) collective-permute-start(bf16[512,384]{1,0:T(8,128)(2,1)} %weight_part.2.refs_1_), channel_id=1, source_target_pairs={{0,2},{1,3},{2,0},{3,1},{4,6},{5,7},{6,4},{7,5},{8,10},{9,11},{10,... | collective-permute-start | bytes 1179656 | tf_op jit(solution)/shard_map/ppermute | solution.py:393
  7.6 1.7 %weight_part.3.refs_0_ = bf16[512,384]{1,0:T(8,128)(2,1)} custom-call(s32[1]{0:T(128)} %bitcast.10.pipe_ref.refs_0_, bf16[2048,384]{1,0:T(8,128)(2,1)} %whole.3), custom_call_target="tpu_custom_call" | custom-call | flops 1 | bytes 786432 | tf_op jit(solution)/shard_map/weight_part/pallas_call | solution.py:178
  9.4 1.0 %copy-done.2 = bf16[1,1,128,2048]{3,2,1,0:T(8,128)(2,1)S(1)} copy-done((bf16[1,1,128,2048]{3,2,1,0:T(8,128)(2,1)S(1)}, bf16[1,1,128,2048]{3,2,1,0:T(8,128)(2,1)}, u32[]{:S(2)}) %copy-start.2) | copy-done | bytes 524312
  10.4 1.0 %copy-done.3 = bf16[1,1,128,2048]{3,2,1,0:T(8,128)(2,1)S(1)} copy-done((bf16[1,1,128,2048]{3,2,1,0:T(8,128)(2,1)S(1)}, bf16[1,1,128,2048]{3,2,1,0:T(8,128)(2,1)}, u32[]{:S(2)}) %copy-start.3) | copy-done | bytes 524312
  11.4 0.7 copy-done.7
  12.2 0.7 collective-permute-done.refs_5_.refs_1_
  12.9 1.8 %collective-permute-start.6 = (bf16[512,384]{1,0:T(8,128)(2,1)}, bf16[512,384]{1,0:T(8,128)(2,1)S(1)}, u32[]{:S(2)}, u32[]{:S(2)}) collective-permute-start(bf16[512,384]{1,0:T(8,128)(2,1)} %hand_on.18), channel_id=1, source_target_pairs={{0,2},{1,3},{2,0},{3,1},{4,6},{5,7},{6,4},{7,5},{8,10},{9,11},{10,... | collective-permute-start | bytes 1179656 | tf_op jit(solution)/shard_map/ppermute | solution.py:393
  14.7 2.6 %attend.1 = (f32[128,2048]{1,0:T(8,128)S(1)}, bf16[96,2048]{1,0:T(8,128)(2,1)S(1)}, bf16[96,2048]{1,0:T(8,128)(2,1)S(1)}) custom-call(bf16[128,2048]{1,0:T(8,128)(2,1)S(1)} %get-tuple-element.34.refs_0_, bf16[128,2048]{1,0:T(8,128)(2,1)S(1)} %get-tuple-element.35.refs_1_, f32[1,2048]{1,0:T(1,128)S(1)} %get-tuple-element.36.refs_2_, ...), custom_call_target="tpu_custom_call" | custom-call | flops 134217728 | bytes 3145728 | tf_op jit(solution)/shard_map/attend/pallas_call | solution.py:153
  17.3 2.7 %collective-permute-start.8 = (bf16[96,2048]{1,0:T(8,128)(2,1)S(1)}, bf16[96,2048]{1,0:T(8,128)(2,1)S(1)}, u32[]{:S(2)}, u32[]{:S(2)}) collective-permute-start(bf16[96,2048]{1,0:T(8,128)(2,1)S(1)} %get-tuple-element.44), channel_id=1, source_target_pairs={{0,8},{1,9},{2,10},{3,11},{4,12},{5,13},{6,14},{7,15},{8,0},{9,1},... | collective-permute-start | bytes 1179656 | tf_op jit(solution)/shard_map/ppermute | solution.py:397
  19.9 1.6 %collective-permute-start.3 = (bf16[96,2048]{1,0:T(8,128)(2,1)S(1)}, bf16[96,2048]{1,0:T(8,128)(2,1)S(1)}, u32[]{:S(2)}, u32[]{:S(2)}) collective-permute-start(bf16[96,2048]{1,0:T(8,128)(2,1)S(1)} %get-tuple-element.41.refs_0_.own_in.refs_2_), channel_id=1, source_target_pairs={{0,4},{1,5},{2,6},{3,7},{4,0},{5,1},{6,2},{7,3},{8,12},{9,13},{10,... | collective-permute-start | bytes 1179656 | tf_op jit(solution)/shard_map/ppermute | solution.py:393
  21.5 0.7 hold_weights.1
  22.3 1.6 %collective-permute-start.5 = (bf16[512,384]{1,0:T(8,128)(2,1)S(1)}, bf16[512,384]{1,0:T(8,128)(2,1)S(1)}, u32[]{:S(2)}, u32[]{:S(2)}) collective-permute-start(bf16[512,384]{1,0:T(8,128)(2,1)S(1)} %hand_on.17.refs_1_.refs_0_), channel_id=1, source_target_pairs={{0,16},{16,0},{1,17},{17,1},{2,18},{18,2},{3,19},{19,3},{4,20},{20... | collective-permute-start | bytes 1179656 | tf_op jit(solution)/shard_map/ppermute | solution.py:401
  23.8 1.6 %collective-permute-done.6.refs_0_ = bf16[512,384]{1,0:T(8,128)(2,1)S(1)} collective-permute-done((bf16[512,384]{1,0:T(8,128)(2,1)}, bf16[512,384]{1,0:T(8,128)(2,1)S(1)}, u32[]{:S(2)}, u32[]{:S(2)}) %collective-permute-start.6) | collective-permute-done | bytes 393248 | tf_op jit(solution)/shard_map/ppermute | solution.py:393
  25.8 1.7 %collective-permute-start.14 = (bf16[112,2048]{1,0:T(8,128)(2,1)S(1)}, bf16[112,2048]{1,0:T(8,128)(2,1)S(1)}, u32[]{:S(2)}, u32[]{:S(2)}) collective-permute-start(bf16[112,2048]{1,0:T(8,128)(2,1)S(1)} %get-tuple-element.51), channel_id=1, source_target_pairs={{0,2},{1,3},{2,0},{3,1},{4,6},{5,7},{6,4},{7,5},{8,10},{9,11},{10,... | collective-permute-start | bytes 1376264 | tf_op jit(solution)/shard_map/ppermute | solution.py:393
  27.5 9.2 %collective-permute-done.8.refs_0_ = bf16[96,2048]{1,0:T(8,128)(2,1)S(1)} collective-permute-done((bf16[96,2048]{1,0:T(8,128)(2,1)S(1)}, bf16[96,2048]{1,0:T(8,128)(2,1)S(1)}, u32[]{:S(2)}, u32[]{:S(2)}) %collective-permute-start.8) | collective-permute-done | bytes 393248 | tf_op jit(solution)/shard_map/ppermute | solution.py:397
  36.9 1.4 %collective-permute-start.9 = (bf16[96,2048]{1,0:T(8,128)(2,1)S(1)}, bf16[96,2048]{1,0:T(8,128)(2,1)S(1)}, u32[]{:S(2)}, u32[]{:S(2)}) collective-permute-start(bf16[96,2048]{1,0:T(8,128)(2,1)S(1)} %hand_on.20.own_in.refs_2_), channel_id=1, source_target_pairs={{0,4},{1,5},{2,6},{3,7},{4,0},{5,1},{6,2},{7,3},{8,12},{9,13},{10,... | collective-permute-start | bytes 1179656 | tf_op jit(solution)/shard_map/ppermute | solution.py:393
  38.4 0.5 collective-permute-start.16
  38.9 1.3 %collective-permute-done.7.refs_3_.refs_1_ = bf16[512,384]{1,0:T(8,128)(2,1)S(1)} collective-permute-done((bf16[512,384]{1,0:T(8,128)(2,1)S(1)}, bf16[512,384]{1,0:T(8,128)(2,1)S(1)}, u32[]{:S(2)}, u32[]{:S(2)}) %collective-permute-start.7) | collective-permute-done | bytes 393248 | tf_op jit(solution)/shard_map/ppermute | solution.py:401
  40.2 1.6 %collective-permute-start.15 = (bf16[112,2048]{1,0:T(8,128)(2,1)S(1)}, bf16[112,2048]{1,0:T(8,128)(2,1)S(1)}, u32[]{:S(2)}, u32[]{:S(2)}) collective-permute-start(bf16[112,2048]{1,0:T(8,128)(2,1)S(1)} %hand_on.27.refs_4_), channel_id=1, source_target_pairs={{0,16},{16,0},{1,17},{17,1},{2,18},{18,2},{3,19},{19,3},{4,20},{20... | collective-permute-start | bytes 1376264 | tf_op jit(solution)/shard_map/ppermute | solution.py:401
  41.7 4.9 %collective-permute-done.9.refs_4_.refs_0_ = bf16[96,2048]{1,0:T(8,128)(2,1)S(1)} collective-permute-done((bf16[96,2048]{1,0:T(8,128)(2,1)S(1)}, bf16[96,2048]{1,0:T(8,128)(2,1)S(1)}, u32[]{:S(2)}, u32[]{:S(2)}) %collective-permute-start.9) | collective-permute-done | bytes 393248 | tf_op jit(solution)/shard_map/ppermute | solution.py:393
  46.7 0.5 collective-permute-start.11
  47.2 1.2 %collective-permute-done.10.refs_8_ = bf16[512,384]{1,0:T(8,128)(2,1)S(1)} collective-permute-done((bf16[512,384]{1,0:T(8,128)(2,1)S(1)}, bf16[512,384]{1,0:T(8,128)(2,1)S(1)}, u32[]{:S(2)}, u32[]{:S(2)}) %collective-permute-start.10) | collective-permute-done | bytes 393248 | tf_op jit(solution)/shard_map/ppermute | solution.py:393
  48.5 0.4 collective-permute-done.11.refs_9_
  49.1 0.8 expert_up.3.refs_1_
  50.1 0.6 collective-permute-done.13.refs_11_
  50.7 0.9 expert_up_y.2.refs_2_.refs_1_
  51.5 2.2 %collective-permute-done.16.refs_1_ = bf16[160,2048]{1,0:T(8,128)(2,1)S(1)} collective-permute-done((bf16[160,2048]{1,0:T(8,128)(2,1)S(1)}, bf16[160,2048]{1,0:T(8,128)(2,1)S(1)}, u32[]{:S(2)}, u32[]{:S(2)}) %collective-permute-start.16) | collective-permute-done | bytes 655392 | tf_op jit(solution)/shard_map/ppermute | solution.py:393
  53.8 0.5 collective-permute-start.18
  54.3 2.2 %collective-permute-done.18.refs_7_ = bf16[112,2048]{1,0:T(8,128)(2,1)S(1)} collective-permute-done((bf16[112,2048]{1,0:T(8,128)(2,1)S(1)}, bf16[112,2048]{1,0:T(8,128)(2,1)S(1)}, u32[]{:S(2)}, u32[]{:S(2)}) %collective-permute-start.18) | collective-permute-done | bytes 458784 | tf_op jit(solution)/shard_map/ppermute | solution.py:393
  56.5 0.8 expert_down.3
  57.4 0.4 collective-permute-start.22
  57.7 0.8 expert_up.2.refs_1_
  58.6 0.8 expert_down.4
  59.4 0.9 %expert_up_y.3.refs_1_ = bf16[192,1536]{1,0:T(8,128)(2,1)S(1)} custom-call(s32[1]{0:T(128)} %bitcast.10.pipe_ref.refs_0_, bf16[192,768]{1,0:T(8,128)(2,1)S(1)} %expert_up.2.refs_1_, bf16[96,2048]{1,0:T(8,128)(2,1)S(1)} %get-tuple-element.41.refs_0_.own_in.refs_2_, bf16[96,2048]{1,0:T(8,128)(2,1)S(1)} %collective-permute-done.3.z_in.refs_1_.refs_3_, ...), custom_call_target="tpu_custom_call" | custom-call | flops 603979776 | bytes 3145728 | tf_op jit(solution)/shard_map/expert_up_y/pallas_call | solution.py:277
  60.3 1.8 %collective-permute-start.20 = (bf16[96,1024]{1,0:T(8,128)(2,1)S(1)}, bf16[96,1024]{1,0:T(8,128)(2,1)S(1)}, u32[]{:S(2)}, u32[]{:S(2)}) collective-permute-start(bf16[96,1024]{1,0:T(8,128)(2,1)S(1)} %hand_on.29), channel_id=1, source_target_pairs={{0,4},{1,5},{2,6},{3,7},{4,0},{5,1},{6,2},{7,3},{8,12},{9,13},{10,... | collective-permute-start | bytes 589832 | tf_op jit(solution)/shard_map/ppermute | solution.py:393
  62.1 3.1 %collective-permute-done.22.z_ref = bf16[96,1024]{1,0:T(8,128)(2,1)S(1)} collective-permute-done((bf16[96,1024]{1,0:T(8,128)(2,1)S(1)}, bf16[96,1024]{1,0:T(8,128)(2,1)S(1)}, u32[]{:S(2)}, u32[]{:S(2)}) %collective-permute-start.22) | collective-permute-done | bytes 196640 | tf_op jit(solution)/shard_map/ppermute | solution.py:393
  65.2 3.4 %collective-permute-start.23 = (bf16[96,1024]{1,0:T(8,128)(2,1)S(1)}, bf16[96,1024]{1,0:T(8,128)(2,1)S(1)}, u32[]{:S(2)}, u32[]{:S(2)}) collective-permute-start(bf16[96,1024]{1,0:T(8,128)(2,1)S(1)} %far_total.3), channel_id=1, source_target_pairs={{0,8},{1,9},{2,10},{3,11},{4,12},{5,13},{6,14},{7,15},{8,0},{9,1},... | collective-permute-start | bytes 589832 | tf_op jit(solution)/shard_map/ppermute | solution.py:397
  68.7 1.5 %expert_down.5 = (bf16[96,2048]{1,0:T(8,128)(2,1)S(1)}, bf16[96,2048]{1,0:T(8,128)(2,1)S(1)}) custom-call(s32[1]{0:T(128)} %bitcast.10.pipe_ref.refs_0_, bf16[192,1536]{1,0:T(8,128)(2,1)S(1)} %expert_up_y.3.refs_1_, bf16[384,2048]{1,0:T(8,128)(2,1)S(1)} %get-tuple-element.49.refs_2_, bf16[384,2048]{1,0:T(8,128)(2,1)S(1)} %collective-permute-done.2.refs_7_.refs_3_, ...), custom_call_target="tpu_custom_call" | custom-call | flops 1207959552 | bytes 6291456 | tf_op jit(solution)/shard_map/expert_down/pallas_call | solution.py:320
  70.2 1.6 %collective-permute-done.20.z_ref = bf16[96,1024]{1,0:T(8,128)(2,1)S(1)} collective-permute-done((bf16[96,1024]{1,0:T(8,128)(2,1)S(1)}, bf16[96,1024]{1,0:T(8,128)(2,1)S(1)}, u32[]{:S(2)}, u32[]{:S(2)}) %collective-permute-start.20) | collective-permute-done | bytes 196640 | tf_op jit(solution)/shard_map/ppermute | solution.py:393
  71.9 1.7 %collective-permute-start.24 = (bf16[96,1024]{1,0:T(8,128)(2,1)S(1)}, bf16[96,1024]{1,0:T(8,128)(2,1)S(1)}, u32[]{:S(2)}, u32[]{:S(2)}) collective-permute-start(bf16[96,1024]{1,0:T(8,128)(2,1)S(1)} %get-tuple-element.62), channel_id=1, source_target_pairs={{0,8},{1,9},{2,10},{3,11},{4,12},{5,13},{6,14},{7,15},{8,0},{9,1},... | collective-permute-start | bytes 589832 | tf_op jit(solution)/shard_map/ppermute | solution.py:397
  73.6 3.8 %collective-permute-done.23.refs_0_ = bf16[96,1024]{1,0:T(8,128)(2,1)S(1)} collective-permute-done((bf16[96,1024]{1,0:T(8,128)(2,1)S(1)}, bf16[96,1024]{1,0:T(8,128)(2,1)S(1)}, u32[]{:S(2)}, u32[]{:S(2)}) %collective-permute-start.23) | collective-permute-done | bytes 196640 | tf_op jit(solution)/shard_map/ppermute | solution.py:397
  77.4 6.8 %collective-permute-done.24.refs_6_ = bf16[96,1024]{1,0:T(8,128)(2,1)S(1)} collective-permute-done((bf16[96,1024]{1,0:T(8,128)(2,1)S(1)}, bf16[96,1024]{1,0:T(8,128)(2,1)S(1)}, u32[]{:S(2)}, u32[]{:S(2)}) %collective-permute-start.24) | collective-permute-done | bytes 196640 | tf_op jit(solution)/shard_map/ppermute | solution.py:397
  84.2 1.3 %collective-permute-done.21.refs_4_ = bf16[96,2048]{1,0:T(8,128)(2,1)S(1)} collective-permute-done((bf16[96,2048]{1,0:T(8,128)(2,1)S(1)}, bf16[96,2048]{1,0:T(8,128)(2,1)S(1)}, u32[]{:S(2)}, u32[]{:S(2)}) %collective-permute-start.21) | collective-permute-done | bytes 393248 | tf_op jit(solution)/shard_map/ppermute | solution.py:393
  85.4 1.2 %finish.1 = bf16[128,2048]{1,0:T(8,128)(2,1)} custom-call(f32[128,2048]{1,0:T(8,128)S(1)} %get-tuple-element.38.refs_0_, f32[128,1]{1,0:T(8,128)S(1)} %get-tuple-element.39.refs_1_, s32[128,1]{1,0:T(8,128)S(1)} %get-tuple-element.40.refs_2_, bf16[96,2048]{1,0:T(8,128)(2,1)S(1)} %get-tuple-element.57.refs_3_, ...), custom_call_target="tpu_custom_call" | custom-call | flops 201326592 | bytes 4194304 | tf_op jit(solution)/shard_map/finish/pallas_call | solution.py:375
  (52 shorter events, 1.5 us)
Async XLA Ops:
  0.0 2.3 %copy-start.8 = (bf16[1,32,2,2048]{3,2,1,0:T(2,128)(2,1)S(1)}, bf16[1,32,2,2048]{3,2,1,0:T(2,128)(2,1)}, u32[]{:S(2)}) copy-start(bf16[1,32,2,2048]{3,2,1,0:T(2,128)(2,1)} %param.11) | copy-start | bytes 786436
  0.0 14.7 %collective-permute-start.2 = (bf16[384,2048]{1,0:T(8,128)(2,1)}, bf16[384,2048]{1,0:T(8,128)(2,1)S(1)}, u32[]{:S(2)}, u32[]{:S(2)}) collective-permute-start(bf16[384,2048]{1,0:T(8,128)(2,1)} %w_out.1), channel_id=1, source_target_pairs={{0,1},{1,0},{2,3},{3,2},{4,5},{5,4},{6,7},{7,6},{8,9},{9,8},{10,11... | collective-permute-start | bytes 4718600 | tf_op jit(solution)/shard_map/ppermute | solution.py:393
  0.5 14.2 %collective-permute-start.1 = (bf16[2048,384]{1,0:T(8,128)(2,1)}, bf16[2048,384]{1,0:T(8,128)(2,1)S(1)}, u32[]{:S(2)}, u32[]{:S(2)}) collective-permute-start(bf16[2048,384]{1,0:T(8,128)(2,1)} %whole.3), channel_id=1, source_target_pairs={{0,1},{1,0},{2,3},{3,2},{4,5},{5,4},{6,7},{7,6},{8,9},{9,8},{10,11... | collective-permute-start | bytes 4718600 | tf_op jit(solution)/shard_map/ppermute | solution.py:393
  3.1 6.2 %copy-start.4 = (f32[2048]{0:T(1024)S(1)}, f32[2048]{0:T(1024)}, u32[]{:S(2)}) copy-start(f32[2048]{0:T(1024)} %param.12) | copy-start | bytes 24580
  3.1 6.2 %copy-start.5 = (s32[1,1,128]{2,1,0:T(1,128)S(1)}, s32[1,1,128]{2,1,0:T(1,128)}, u32[]{:S(2)}) copy-start(s32[1,1,128]{2,1,0:T(1,128)} %param.15) | copy-start | bytes 1540
  3.1 6.2 %copy-start.6 = (s32[1,1,128]{2,1,0:T(1,128)S(1)}, s32[1,1,128]{2,1,0:T(1,128)}, u32[]{:S(2)}) copy-start(s32[1,1,128]{2,1,0:T(1,128)} %param.16) | copy-start | bytes 1540
  3.1 9.8 %collective-permute-start = (bf16[64,2048]{1,0:T(8,128)(2,1)}, bf16[64,2048]{1,0:T(8,128)(2,1)}, u32[]{:S(2)}, u32[]{:S(2)}) collective-permute-start(bf16[64,2048]{1,0:T(8,128)(2,1)} %hand_on.16.refs_4_), channel_id=1, source_target_pairs={{0,16},{16,0},{1,17},{17,1},{2,18},{18,2},{3,19},{19,3},{4,20},{20... | collective-permute-start | bytes 786440 | tf_op jit(solution)/shard_map/ppermute | solution.py:416
  6.0 16.2 %collective-permute-start.4 = (bf16[512,384]{1,0:T(8,128)(2,1)}, bf16[512,384]{1,0:T(8,128)(2,1)S(1)}, u32[]{:S(2)}, u32[]{:S(2)}) collective-permute-start(bf16[512,384]{1,0:T(8,128)(2,1)} %weight_part.2.refs_1_), channel_id=1, source_target_pairs={{0,2},{1,3},{2,0},{3,1},{4,6},{5,7},{6,4},{7,5},{8,10},{9,11},{10,... | collective-permute-start | bytes 1179656 | tf_op jit(solution)/shard_map/ppermute | solution.py:393
  9.3 1.0 %copy-start.2 = (bf16[1,1,128,2048]{3,2,1,0:T(8,128)(2,1)S(1)}, bf16[1,1,128,2048]{3,2,1,0:T(8,128)(2,1)}, u32[]{:S(2)}) copy-start(bf16[1,1,128,2048]{3,2,1,0:T(8,128)(2,1)} %param.9) | copy-start | bytes 1572868
  10.4 1.0 %copy-start.3 = (bf16[1,1,128,2048]{3,2,1,0:T(8,128)(2,1)S(1)}, bf16[1,1,128,2048]{3,2,1,0:T(8,128)(2,1)}, u32[]{:S(2)}) copy-start(bf16[1,1,128,2048]{3,2,1,0:T(8,128)(2,1)} %param.10) | copy-start | bytes 1572868
  11.4 0.7 copy-start.7
  12.9 12.6 %collective-permute-start.6 = (bf16[512,384]{1,0:T(8,128)(2,1)}, bf16[512,384]{1,0:T(8,128)(2,1)S(1)}, u32[]{:S(2)}, u32[]{:S(2)}) collective-permute-start(bf16[512,384]{1,0:T(8,128)(2,1)} %hand_on.18), channel_id=1, source_target_pairs={{0,2},{1,3},{2,0},{3,1},{4,6},{5,7},{6,4},{7,5},{8,10},{9,11},{10,... | collective-permute-start | bytes 1179656 | tf_op jit(solution)/shard_map/ppermute | solution.py:393
  14.7 6.9 %copy-start = (bf16[2048,384]{1,0:T(8,128)(2,1)S(1)}, bf16[2048,384]{1,0:T(8,128)(2,1)}, u32[]{:S(2)}) copy-start(bf16[2048,384]{1,0:T(8,128)(2,1)} %whole.3) | copy-start | bytes 4718596
  14.7 6.9 %copy-start.1 = (bf16[384,2048]{1,0:T(8,128)(2,1)S(1)}, bf16[384,2048]{1,0:T(8,128)(2,1)}, u32[]{:S(2)}) copy-start(bf16[384,2048]{1,0:T(8,128)(2,1)} %w_out.1) | copy-start | bytes 4718596
  17.3 19.5 %collective-permute-start.8 = (bf16[96,2048]{1,0:T(8,128)(2,1)S(1)}, bf16[96,2048]{1,0:T(8,128)(2,1)S(1)}, u32[]{:S(2)}, u32[]{:S(2)}) collective-permute-start(bf16[96,2048]{1,0:T(8,128)(2,1)S(1)} %get-tuple-element.44), channel_id=1, source_target_pairs={{0,8},{1,9},{2,10},{3,11},{4,12},{5,13},{6,14},{7,15},{8,0},{9,1},... | collective-permute-start | bytes 1179656 | tf_op jit(solution)/shard_map/ppermute | solution.py:397
  19.9 17.0 %collective-permute-start.3 = (bf16[96,2048]{1,0:T(8,128)(2,1)S(1)}, bf16[96,2048]{1,0:T(8,128)(2,1)S(1)}, u32[]{:S(2)}, u32[]{:S(2)}) collective-permute-start(bf16[96,2048]{1,0:T(8,128)(2,1)S(1)} %get-tuple-element.41.refs_0_.own_in.refs_2_), channel_id=1, source_target_pairs={{0,4},{1,5},{2,6},{3,7},{4,0},{5,1},{6,2},{7,3},{8,12},{9,13},{10,... | collective-permute-start | bytes 1179656 | tf_op jit(solution)/shard_map/ppermute | solution.py:393
  22.3 19.5 %collective-permute-start.5 = (bf16[512,384]{1,0:T(8,128)(2,1)S(1)}, bf16[512,384]{1,0:T(8,128)(2,1)S(1)}, u32[]{:S(2)}, u32[]{:S(2)}) collective-permute-start(bf16[512,384]{1,0:T(8,128)(2,1)S(1)} %hand_on.17.refs_1_.refs_0_), channel_id=1, source_target_pairs={{0,16},{16,0},{1,17},{17,1},{2,18},{18,2},{3,19},{19,3},{4,20},{20... | collective-permute-start | bytes 1179656 | tf_op jit(solution)/shard_map/ppermute | solution.py:401
  25.5 14.7 %collective-permute-start.7 = (bf16[512,384]{1,0:T(8,128)(2,1)S(1)}, bf16[512,384]{1,0:T(8,128)(2,1)S(1)}, u32[]{:S(2)}, u32[]{:S(2)}) collective-permute-start(bf16[512,384]{1,0:T(8,128)(2,1)S(1)} %hand_on.19.refs_2_), channel_id=1, source_target_pairs={{0,16},{16,0},{1,17},{17,1},{2,18},{18,2},{3,19},{19,3},{4,20},{20... | collective-permute-start | bytes 1179656 | tf_op jit(solution)/shard_map/ppermute | solution.py:401
  25.8 14.4 %collective-permute-start.14 = (bf16[112,2048]{1,0:T(8,128)(2,1)S(1)}, bf16[112,2048]{1,0:T(8,128)(2,1)S(1)}, u32[]{:S(2)}, u32[]{:S(2)}) collective-permute-start(bf16[112,2048]{1,0:T(8,128)(2,1)S(1)} %get-tuple-element.51), channel_id=1, source_target_pairs={{0,2},{1,3},{2,0},{3,1},{4,6},{5,7},{6,4},{7,5},{8,10},{9,11},{10,... | collective-permute-start | bytes 1376264 | tf_op jit(solution)/shard_map/ppermute | solution.py:393
  36.9 9.7 %collective-permute-start.9 = (bf16[96,2048]{1,0:T(8,128)(2,1)S(1)}, bf16[96,2048]{1,0:T(8,128)(2,1)S(1)}, u32[]{:S(2)}, u32[]{:S(2)}) collective-permute-start(bf16[96,2048]{1,0:T(8,128)(2,1)S(1)} %hand_on.20.own_in.refs_2_), channel_id=1, source_target_pairs={{0,4},{1,5},{2,6},{3,7},{4,0},{5,1},{6,2},{7,3},{8,12},{9,13},{10,... | collective-permute-start | bytes 1179656 | tf_op jit(solution)/shard_map/ppermute | solution.py:393
  38.4 15.3 %collective-permute-start.16 = (bf16[160,2048]{1,0:T(8,128)(2,1)S(1)}, bf16[160,2048]{1,0:T(8,128)(2,1)S(1)}, u32[]{:S(2)}, u32[]{:S(2)}) collective-permute-start(bf16[160,2048]{1,0:T(8,128)(2,1)S(1)} %get-tuple-element.52), channel_id=1, source_target_pairs={{0,2},{1,3},{2,0},{3,1},{4,6},{5,7},{6,4},{7,5},{8,10},{9,11},{10,... | collective-permute-start | bytes 1966088 | tf_op jit(solution)/shard_map/ppermute | solution.py:393
  40.2 13.5 %collective-permute-start.17 = (bf16[112,2048]{1,0:T(8,128)(2,1)S(1)}, bf16[112,2048]{1,0:T(8,128)(2,1)S(1)}, u32[]{:S(2)}, u32[]{:S(2)}) collective-permute-start(bf16[112,2048]{1,0:T(8,128)(2,1)S(1)} %hand_on.27.refs_4_), channel_id=1, source_target_pairs={{0,1},{1,0},{2,3},{3,2},{4,5},{5,4},{6,7},{7,6},{8,9},{9,8},{10,11... | collective-permute-start | bytes 1376264 | tf_op jit(solution)/shard_map/ppermute | solution.py:393
  40.2 13.5 %collective-permute-start.15 = (bf16[112,2048]{1,0:T(8,128)(2,1)S(1)}, bf16[112,2048]{1,0:T(8,128)(2,1)S(1)}, u32[]{:S(2)}, u32[]{:S(2)}) collective-permute-start(bf16[112,2048]{1,0:T(8,128)(2,1)S(1)} %hand_on.27.refs_4_), channel_id=1, source_target_pairs={{0,16},{16,0},{1,17},{17,1},{2,18},{18,2},{3,19},{19,3},{4,20},{20... | collective-permute-start | bytes 1376264 | tf_op jit(solution)/shard_map/ppermute | solution.py:401
  46.7 1.7 %collective-permute-start.10 = (bf16[512,384]{1,0:T(8,128)(2,1)S(1)}, bf16[512,384]{1,0:T(8,128)(2,1)S(1)}, u32[]{:S(2)}, u32[]{:S(2)}) collective-permute-start(bf16[512,384]{1,0:T(8,128)(2,1)S(1)} %get-tuple-element.45.refs_4_), channel_id=1, source_target_pairs={{0,1},{1,0},{2,3},{3,2},{4,5},{5,4},{6,7},{7,6},{8,9},{9,8},{10,11... | collective-permute-start | bytes 1179656 | tf_op jit(solution)/shard_map/ppermute | solution.py:393
  46.7 2.3 %collective-permute-start.11 = (bf16[512,384]{1,0:T(8,128)(2,1)S(1)}, bf16[512,384]{1,0:T(8,128)(2,1)S(1)}, u32[]{:S(2)}, u32[]{:S(2)}) collective-permute-start(bf16[512,384]{1,0:T(8,128)(2,1)S(1)} %get-tuple-element.46.refs_5_), channel_id=1, source_target_pairs={{0,1},{1,0},{2,3},{3,2},{4,5},{5,4},{6,7},{7,6},{8,9},{9,8},{10,11... | collective-permute-start | bytes 1179656 | tf_op jit(solution)/shard_map/ppermute | solution.py:393
  48.4 1.7 %collective-permute-start.12 = (bf16[512,384]{1,0:T(8,128)(2,1)S(1)}, bf16[512,384]{1,0:T(8,128)(2,1)S(1)}, u32[]{:S(2)}, u32[]{:S(2)}) collective-permute-start(bf16[512,384]{1,0:T(8,128)(2,1)S(1)} %get-tuple-element.47.refs_6_), channel_id=1, source_target_pairs={{0,1},{1,0},{2,3},{3,2},{4,5},{5,4},{6,7},{7,6},{8,9},{9,8},{10,11... | collective-permute-start | bytes 1179656 | tf_op jit(solution)/shard_map/ppermute | solution.py:393
  48.9 1.7 %collective-permute-start.13 = (bf16[512,384]{1,0:T(8,128)(2,1)S(1)}, bf16[512,384]{1,0:T(8,128)(2,1)S(1)}, u32[]{:S(2)}, u32[]{:S(2)}) collective-permute-start(bf16[512,384]{1,0:T(8,128)(2,1)S(1)} %get-tuple-element.48.refs_7_), channel_id=1, source_target_pairs={{0,1},{1,0},{2,3},{3,2},{4,5},{5,4},{6,7},{7,6},{8,9},{9,8},{10,11... | collective-permute-start | bytes 1179656 | tf_op jit(solution)/shard_map/ppermute | solution.py:393
  53.7 2.8 %collective-permute-start.19 = (bf16[160,2048]{1,0:T(8,128)(2,1)S(1)}, bf16[160,2048]{1,0:T(8,128)(2,1)S(1)}, u32[]{:S(2)}, u32[]{:S(2)}) collective-permute-start(bf16[160,2048]{1,0:T(8,128)(2,1)S(1)} %get-tuple-element.54.refs_8_), channel_id=1, source_target_pairs={{0,1},{1,0},{2,3},{3,2},{4,5},{5,4},{6,7},{7,6},{8,9},{9,8},{10,11... | collective-permute-start | bytes 1966088 | tf_op jit(solution)/shard_map/ppermute | solution.py:393
  53.8 2.7 %collective-permute-start.18 = (bf16[112,2048]{1,0:T(8,128)(2,1)S(1)}, bf16[112,2048]{1,0:T(8,128)(2,1)S(1)}, u32[]{:S(2)}, u32[]{:S(2)}) collective-permute-start(bf16[112,2048]{1,0:T(8,128)(2,1)S(1)} %get-tuple-element.53.refs_5_), channel_id=1, source_target_pairs={{0,1},{1,0},{2,3},{3,2},{4,5},{5,4},{6,7},{7,6},{8,9},{9,8},{10,11... | collective-permute-start | bytes 1376264 | tf_op jit(solution)/shard_map/ppermute | solution.py:393
  57.4 7.8 %collective-permute-start.22 = (bf16[96,1024]{1,0:T(8,128)(2,1)S(1)}, bf16[96,1024]{1,0:T(8,128)(2,1)S(1)}, u32[]{:S(2)}, u32[]{:S(2)}) collective-permute-start(bf16[96,1024]{1,0:T(8,128)(2,1)S(1)} %get-tuple-element.61), channel_id=1, source_target_pairs={{0,4},{1,5},{2,6},{3,7},{4,0},{5,1},{6,2},{7,3},{8,12},{9,13},{10,... | collective-permute-start | bytes 589832 | tf_op jit(solution)/shard_map/ppermute | solution.py:393
  60.3 11.5 %collective-permute-start.20 = (bf16[96,1024]{1,0:T(8,128)(2,1)S(1)}, bf16[96,1024]{1,0:T(8,128)(2,1)S(1)}, u32[]{:S(2)}, u32[]{:S(2)}) collective-permute-start(bf16[96,1024]{1,0:T(8,128)(2,1)S(1)} %hand_on.29), channel_id=1, source_target_pairs={{0,4},{1,5},{2,6},{3,7},{4,0},{5,1},{6,2},{7,3},{8,12},{9,13},{10,... | collective-permute-start | bytes 589832 | tf_op jit(solution)/shard_map/ppermute | solution.py:393
  65.2 12.2 %collective-permute-start.23 = (bf16[96,1024]{1,0:T(8,128)(2,1)S(1)}, bf16[96,1024]{1,0:T(8,128)(2,1)S(1)}, u32[]{:S(2)}, u32[]{:S(2)}) collective-permute-start(bf16[96,1024]{1,0:T(8,128)(2,1)S(1)} %far_total.3), channel_id=1, source_target_pairs={{0,8},{1,9},{2,10},{3,11},{4,12},{5,13},{6,14},{7,15},{8,0},{9,1},... | collective-permute-start | bytes 589832 | tf_op jit(solution)/shard_map/ppermute | solution.py:397
  71.9 13.6 %collective-permute-start.21 = (bf16[96,2048]{1,0:T(8,128)(2,1)S(1)}, bf16[96,2048]{1,0:T(8,128)(2,1)S(1)}, u32[]{:S(2)}, u32[]{:S(2)}) collective-permute-start(bf16[96,2048]{1,0:T(8,128)(2,1)S(1)} %get-tuple-element.60), channel_id=1, source_target_pairs={{0,4},{1,5},{2,6},{3,7},{4,0},{5,1},{6,2},{7,3},{8,12},{9,13},{10,... | collective-permute-start | bytes 1179656 | tf_op jit(solution)/shard_map/ppermute | solution.py:393
  71.9 12.2 %collective-permute-start.24 = (bf16[96,1024]{1,0:T(8,128)(2,1)S(1)}, bf16[96,1024]{1,0:T(8,128)(2,1)S(1)}, u32[]{:S(2)}, u32[]{:S(2)}) collective-permute-start(bf16[96,1024]{1,0:T(8,128)(2,1)S(1)} %get-tuple-element.62), channel_id=1, source_target_pairs={{0,8},{1,9},{2,10},{3,11},{4,12},{5,13},{6,14},{7,15},{8,0},{9,1},... | collective-permute-start | bytes 589832 | tf_op jit(solution)/shard_map/ppermute | solution.py:397

commit v21 on v17

--- a/solution.py
+++ b/solution.py
@@ -210,7 +210,7 @@
 
 def hold(pipe, w_in, w_out, pipes, after):
     units, width = w_out.shape
-    size = units * 2 // 3 // pipes // 16 * 16
+    size = units * 7 // 12 // pipes // 16 * 16
     return call(
         functools.partial(hold_kernel, pipes),
         [
@@ -299,7 +299,7 @@
     for shift in range(pipes):
         at = place(pipes, shift, pipe, size)
         held[pl.ds(at, size)] = y_parts[shift][:, whole]
-        held[pl.ds(pl.multiple_of(units + at, size), size)] = pair_parts[shift][:, whole]
+        held[pl.ds(pl.multiple_of(units + at, 16), size)] = pair_parts[shift][:, whole]
     held[pipes * size : units] = y_rest[:, whole]
     held[units + pipes * size :] = pair_rest[:, whole]
     step = 512

time: 88.7 us -> 87.3 us (0.984)
  waiting for transfers between devices: 44.5 us -> 41.4 us
  starting transfers between devices: 25.7 us -> 26.7 us
    ppermute x3, waiting for transfers between devices: 2.62 us -> 0.48 us  [along(): return [value] + [lax.ppermute(value, 'pipe', perm) for perm in perms]]
    ppermute x18, waiting for transfers between devices: 21.5 us -> 20.4 us  [across(): return lax.ppermute(value, 'expert', [(i, i ^ bit) for i in range(devices)])]
    ppermute x3, starting transfers between devices: 6.82 us -> 7.77 us  [groups_on(): lax.ppermute(value, 'expert', [(i, (i + shift) % devices) for i in range(...]
  transfers between devices with their start and end apart: 25 -> 25, of which waited for: 18 -> 17; matrix products, arithmetic and copies ran while one was open for 1% -> 1% of each run, Pallas kernels for 14% -> 15%
where the time goes in v21:
time: 87.3 us; the launch traced here: 86.6 us
  waiting for transfers between devices  41.4 us (47%)
  starting transfers between devices  26.7 us (31%)
  Pallas kernels  14.8 us (17%)
  local copies, waits for them, and re-layouts  3.56 us (4%)
    ppermute x18, waiting for transfers between devices, across(): return lax.ppermute(value, 'expert', [(i, i ^ bit) for i in range(devices)])  20.4 us
    ppermute x3, waiting for transfers between devices, groups_on(): lax.ppermute(value, 'expert', [(i, (i + shift) % devices) for i in range(...  19.8 us
    ppermute x18, starting transfers between devices, across(): return lax.ppermute(value, 'expert', [(i, i ^ bit) for i in range(devices)])  12.6 us
    ppermute x3, starting transfers between devices, groups_on(): lax.ppermute(value, 'expert', [(i, (i + shift) % devices) for i in range(...  7.77 us
    pallas_call x2, Pallas kernels, cut_part(): call(functools.partial(part_kernel, stride, first), struct((size, whole.s...  3.49 us
    ppermute x3, starting transfers between devices, along(): return [value] + [lax.ppermute(value, 'pipe', perm) for perm in perms]  3.4 us
    pallas_call x3, Pallas kernels, down(): call(functools.partial(down_kernel, pipes, first), [struct((rows, width))...  3.21 us
    ppermute x1, starting transfers between devices, body(): kv_pieces.append(lax.ppermute(kv, 'pipe', perm))  2.93 us
  transfers between devices with their start and end apart: 25, of which 17 were waited for; matrix products, arithmetic and copies ran while one was open for 1% of the time, Pallas kernels for 15%

profile of v21, /device:TPU:0, one launch (start us, length us, event | category | flops | bytes accessed | tf_op | source)
XLA Modules:
  0.0 86.6 jit_solution(4497502853258469233)
XLA Ops:
  0.0 0.5 collective-permute-start.2
  0.5 1.7 %weight_part.2.refs_1_ = bf16[512,384]{1,0:T(8,128)(2,1)} custom-call(s32[1]{0:T(128)} %bitcast.10.pipe_ref.refs_0_, bf16[2048,384]{1,0:T(8,128)(2,1)} %whole.3), custom_call_target="tpu_custom_call" | custom-call | flops 1 | bytes 786432 | tf_op jit(solution)/shard_map/weight_part/pallas_call | solution.py:178
  2.3 0.8 copy.32
  3.1 2.9 %collective-permute-start = (bf16[64,2048]{1,0:T(8,128)(2,1)}, bf16[64,2048]{1,0:T(8,128)(2,1)}, u32[]{:S(2)}, u32[]{:S(2)}) collective-permute-start(bf16[64,2048]{1,0:T(8,128)(2,1)} %hand_on.16.refs_4_), channel_id=1, source_target_pairs={{0,16},{16,0},{1,17},{17,1},{2,18},{18,2},{3,19},{19,3},{4,20},{20... | collective-permute-start | bytes 786440 | tf_op jit(solution)/shard_map/ppermute | solution.py:416
  6.0 1.5 %collective-permute-start.4 = (bf16[512,384]{1,0:T(8,128)(2,1)}, bf16[512,384]{1,0:T(8,128)(2,1)S(1)}, u32[]{:S(2)}, u32[]{:S(2)}) collective-permute-start(bf16[512,384]{1,0:T(8,128)(2,1)} %weight_part.2.refs_1_), channel_id=1, source_target_pairs={{0,2},{1,3},{2,0},{3,1},{4,6},{5,7},{6,4},{7,5},{8,10},{9,11},{10,... | collective-permute-start | bytes 1179656 | tf_op jit(solution)/shard_map/ppermute | solution.py:393
  7.6 1.7 %weight_part.3.refs_0_ = bf16[512,384]{1,0:T(8,128)(2,1)} custom-call(s32[1]{0:T(128)} %bitcast.10.pipe_ref.refs_0_, bf16[2048,384]{1,0:T(8,128)(2,1)} %whole.3), custom_call_target="tpu_custom_call" | custom-call | flops 1 | bytes 786432 | tf_op jit(solution)/shard_map/weight_part/pallas_call | solution.py:178
  9.4 1.0 %copy-done.2 = bf16[1,1,128,2048]{3,2,1,0:T(8,128)(2,1)S(1)} copy-done((bf16[1,1,128,2048]{3,2,1,0:T(8,128)(2,1)S(1)}, bf16[1,1,128,2048]{3,2,1,0:T(8,128)(2,1)}, u32[]{:S(2)}) %copy-start.2) | copy-done | bytes 524312
  10.4 1.0 %copy-done.3 = bf16[1,1,128,2048]{3,2,1,0:T(8,128)(2,1)S(1)} copy-done((bf16[1,1,128,2048]{3,2,1,0:T(8,128)(2,1)S(1)}, bf16[1,1,128,2048]{3,2,1,0:T(8,128)(2,1)}, u32[]{:S(2)}) %copy-start.3) | copy-done | bytes 524312
  11.4 0.7 copy-done.7
  12.2 0.7 collective-permute-done.refs_5_.refs_1_
  12.9 1.8 %collective-permute-start.6 = (bf16[512,384]{1,0:T(8,128)(2,1)}, bf16[512,384]{1,0:T(8,128)(2,1)S(1)}, u32[]{:S(2)}, u32[]{:S(2)}) collective-permute-start(bf16[512,384]{1,0:T(8,128)(2,1)} %hand_on.18), channel_id=1, source_target_pairs={{0,2},{1,3},{2,0},{3,1},{4,6},{5,7},{6,4},{7,5},{8,10},{9,11},{10,... | collective-permute-start | bytes 1179656 | tf_op jit(solution)/shard_map/ppermute | solution.py:393
  14.7 2.6 %attend.1 = (f32[128,2048]{1,0:T(8,128)S(1)}, bf16[96,2048]{1,0:T(8,128)(2,1)S(1)}, bf16[96,2048]{1,0:T(8,128)(2,1)S(1)}) custom-call(bf16[128,2048]{1,0:T(8,128)(2,1)S(1)} %get-tuple-element.34.refs_0_, bf16[128,2048]{1,0:T(8,128)(2,1)S(1)} %get-tuple-element.35.refs_1_, f32[1,2048]{1,0:T(1,128)S(1)} %get-tuple-element.36.refs_2_, ...), custom_call_target="tpu_custom_call" | custom-call | flops 134217728 | bytes 3145728 | tf_op jit(solution)/shard_map/attend/pallas_call | solution.py:153
  17.3 2.7 %collective-permute-start.8 = (bf16[96,2048]{1,0:T(8,128)(2,1)S(1)}, bf16[96,2048]{1,0:T(8,128)(2,1)S(1)}, u32[]{:S(2)}, u32[]{:S(2)}) collective-permute-start(bf16[96,2048]{1,0:T(8,128)(2,1)S(1)} %get-tuple-element.44), channel_id=1, source_target_pairs={{0,8},{1,9},{2,10},{3,11},{4,12},{5,13},{6,14},{7,15},{8,0},{9,1},... | collective-permute-start | bytes 1179656 | tf_op jit(solution)/shard_map/ppermute | solution.py:397
  19.9 1.6 %collective-permute-start.3 = (bf16[96,2048]{1,0:T(8,128)(2,1)S(1)}, bf16[96,2048]{1,0:T(8,128)(2,1)S(1)}, u32[]{:S(2)}, u32[]{:S(2)}) collective-permute-start(bf16[96,2048]{1,0:T(8,128)(2,1)S(1)} %get-tuple-element.41.refs_1_.own_in.refs_2_), channel_id=1, source_target_pairs={{0,4},{1,5},{2,6},{3,7},{4,0},{5,1},{6,2},{7,3},{8,12},{9,13},{10,... | collective-permute-start | bytes 1179656 | tf_op jit(solution)/shard_map/ppermute | solution.py:393
  21.5 1.5 %collective-permute-start.5 = (bf16[512,384]{1,0:T(8,128)(2,1)S(1)}, bf16[512,384]{1,0:T(8,128)(2,1)S(1)}, u32[]{:S(2)}, u32[]{:S(2)}) collective-permute-start(bf16[512,384]{1,0:T(8,128)(2,1)S(1)} %hand_on.17.refs_0_.refs_1_), channel_id=1, source_target_pairs={{0,16},{16,0},{1,17},{17,1},{2,18},{18,2},{3,19},{19,3},{4,20},{20... | collective-permute-start | bytes 1179656 | tf_op jit(solution)/shard_map/ppermute | solution.py:401
  23.0 0.7 hold_weights.1
  23.8 1.7 %collective-permute-done.6.refs_0_ = bf16[512,384]{1,0:T(8,128)(2,1)S(1)} collective-permute-done((bf16[512,384]{1,0:T(8,128)(2,1)}, bf16[512,384]{1,0:T(8,128)(2,1)S(1)}, u32[]{:S(2)}, u32[]{:S(2)}) %collective-permute-start.6) | collective-permute-done | bytes 393248 | tf_op jit(solution)/shard_map/ppermute | solution.py:393
  25.8 1.7 %collective-permute-start.14 = (bf16[112,2048]{1,0:T(8,128)(2,1)S(1)}, bf16[112,2048]{1,0:T(8,128)(2,1)S(1)}, u32[]{:S(2)}, u32[]{:S(2)}) collective-permute-start(bf16[112,2048]{1,0:T(8,128)(2,1)S(1)} %get-tuple-element.51), channel_id=1, source_target_pairs={{0,2},{1,3},{2,0},{3,1},{4,6},{5,7},{6,4},{7,5},{8,10},{9,11},{10,... | collective-permute-start | bytes 1376264 | tf_op jit(solution)/shard_map/ppermute | solution.py:393
  27.5 9.2 %collective-permute-done.8.refs_0_ = bf16[96,2048]{1,0:T(8,128)(2,1)S(1)} collective-permute-done((bf16[96,2048]{1,0:T(8,128)(2,1)S(1)}, bf16[96,2048]{1,0:T(8,128)(2,1)S(1)}, u32[]{:S(2)}, u32[]{:S(2)}) %collective-permute-start.8) | collective-permute-done | bytes 393248 | tf_op jit(solution)/shard_map/ppermute | solution.py:397
  36.9 1.4 %collective-permute-start.9 = (bf16[96,2048]{1,0:T(8,128)(2,1)S(1)}, bf16[96,2048]{1,0:T(8,128)(2,1)S(1)}, u32[]{:S(2)}, u32[]{:S(2)}) collective-permute-start(bf16[96,2048]{1,0:T(8,128)(2,1)S(1)} %hand_on.20.own_in.refs_2_), channel_id=1, source_target_pairs={{0,4},{1,5},{2,6},{3,7},{4,0},{5,1},{6,2},{7,3},{8,12},{9,13},{10,... | collective-permute-start | bytes 1179656 | tf_op jit(solution)/shard_map/ppermute | solution.py:393
  38.4 0.5 collective-permute-start.16
  38.9 0.5 collective-permute-done.7.refs_3_.refs_1_
  39.4 1.6 %collective-permute-start.15 = (bf16[112,2048]{1,0:T(8,128)(2,1)S(1)}, bf16[112,2048]{1,0:T(8,128)(2,1)S(1)}, u32[]{:S(2)}, u32[]{:S(2)}) collective-permute-start(bf16[112,2048]{1,0:T(8,128)(2,1)S(1)} %hand_on.27.refs_4_), channel_id=1, source_target_pairs={{0,16},{16,0},{1,17},{17,1},{2,18},{18,2},{3,19},{19,3},{4,20},{20... | collective-permute-start | bytes 1376264 | tf_op jit(solution)/shard_map/ppermute | solution.py:401
  40.9 5.7 %collective-permute-done.9.refs_4_.refs_0_ = bf16[96,2048]{1,0:T(8,128)(2,1)S(1)} collective-permute-done((bf16[96,2048]{1,0:T(8,128)(2,1)S(1)}, bf16[96,2048]{1,0:T(8,128)(2,1)S(1)}, u32[]{:S(2)}, u32[]{:S(2)}) %collective-permute-start.9) | collective-permute-done | bytes 393248 | tf_op jit(solution)/shard_map/ppermute | solution.py:393
  46.7 0.5 collective-permute-start.11
  47.2 1.2 %collective-permute-done.10.refs_8_ = bf16[512,384]{1,0:T(8,128)(2,1)S(1)} collective-permute-done((bf16[512,384]{1,0:T(8,128)(2,1)S(1)}, bf16[512,384]{1,0:T(8,128)(2,1)S(1)}, u32[]{:S(2)}, u32[]{:S(2)}) %collective-permute-start.10) | collective-permute-done | bytes 393248 | tf_op jit(solution)/shard_map/ppermute | solution.py:393
  48.5 0.4 collective-permute-done.11.refs_9_
  49.1 0.8 expert_up.3.refs_1_
  50.1 0.6 collective-permute-done.13.refs_11_
  50.7 0.9 expert_up_y.2.refs_2_.refs_1_
  51.5 2.2 %collective-permute-done.16.refs_1_ = bf16[160,2048]{1,0:T(8,128)(2,1)S(1)} collective-permute-done((bf16[160,2048]{1,0:T(8,128)(2,1)S(1)}, bf16[160,2048]{1,0:T(8,128)(2,1)S(1)}, u32[]{:S(2)}, u32[]{:S(2)}) %collective-permute-start.16) | collective-permute-done | bytes 655392 | tf_op jit(solution)/shard_map/ppermute | solution.py:393
  53.8 0.5 collective-permute-start.18
  54.3 2.2 %collective-permute-done.18.refs_7_ = bf16[112,2048]{1,0:T(8,128)(2,1)S(1)} collective-permute-done((bf16[112,2048]{1,0:T(8,128)(2,1)S(1)}, bf16[112,2048]{1,0:T(8,128)(2,1)S(1)}, u32[]{:S(2)}, u32[]{:S(2)}) %collective-permute-start.18) | collective-permute-done | bytes 458784 | tf_op jit(solution)/shard_map/ppermute | solution.py:393
  56.5 0.8 expert_down.3
  57.4 0.4 collective-permute-start.22
  57.7 0.8 expert_up.2.refs_1_
  58.6 0.8 expert_down.4
  59.4 0.9 %expert_up_y.3.refs_1_ = bf16[192,1536]{1,0:T(8,128)(2,1)S(1)} custom-call(s32[1]{0:T(128)} %bitcast.10.pipe_ref.refs_0_, bf16[192,768]{1,0:T(8,128)(2,1)S(1)} %expert_up.2.refs_1_, bf16[96,2048]{1,0:T(8,128)(2,1)S(1)} %get-tuple-element.41.refs_1_.own_in.refs_2_, bf16[96,2048]{1,0:T(8,128)(2,1)S(1)} %collective-permute-done.3.z_in.refs_1_.refs_3_, ...), custom_call_target="tpu_custom_call" | custom-call | flops 603979776 | bytes 3145728 | tf_op jit(solution)/shard_map/expert_up_y/pallas_call | solution.py:277
  60.3 1.8 %collective-permute-start.20 = (bf16[96,1024]{1,0:T(8,128)(2,1)S(1)}, bf16[96,1024]{1,0:T(8,128)(2,1)S(1)}, u32[]{:S(2)}, u32[]{:S(2)}) collective-permute-start(bf16[96,1024]{1,0:T(8,128)(2,1)S(1)} %hand_on.29), channel_id=1, source_target_pairs={{0,4},{1,5},{2,6},{3,7},{4,0},{5,1},{6,2},{7,3},{8,12},{9,13},{10,... | collective-permute-start | bytes 589832 | tf_op jit(solution)/shard_map/ppermute | solution.py:393
  62.1 3.1 %collective-permute-done.22.z_ref = bf16[96,1024]{1,0:T(8,128)(2,1)S(1)} collective-permute-done((bf16[96,1024]{1,0:T(8,128)(2,1)S(1)}, bf16[96,1024]{1,0:T(8,128)(2,1)S(1)}, u32[]{:S(2)}, u32[]{:S(2)}) %collective-permute-start.22) | collective-permute-done | bytes 196640 | tf_op jit(solution)/shard_map/ppermute | solution.py:393
  65.2 3.4 %collective-permute-start.23 = (bf16[96,1024]{1,0:T(8,128)(2,1)S(1)}, bf16[96,1024]{1,0:T(8,128)(2,1)S(1)}, u32[]{:S(2)}, u32[]{:S(2)}) collective-permute-start(bf16[96,1024]{1,0:T(8,128)(2,1)S(1)} %far_total.3), channel_id=1, source_target_pairs={{0,8},{1,9},{2,10},{3,11},{4,12},{5,13},{6,14},{7,15},{8,0},{9,1},... | collective-permute-start | bytes 589832 | tf_op jit(solution)/shard_map/ppermute | solution.py:397
  68.7 1.5 %expert_down.5 = (bf16[96,2048]{1,0:T(8,128)(2,1)S(1)}, bf16[96,2048]{1,0:T(8,128)(2,1)S(1)}) custom-call(s32[1]{0:T(128)} %bitcast.10.pipe_ref.refs_0_, bf16[192,1536]{1,0:T(8,128)(2,1)S(1)} %expert_up_y.3.refs_1_, bf16[384,2048]{1,0:T(8,128)(2,1)S(1)} %get-tuple-element.49.refs_2_, bf16[384,2048]{1,0:T(8,128)(2,1)S(1)} %collective-permute-done.2.refs_7_.refs_3_, ...), custom_call_target="tpu_custom_call" | custom-call | flops 1207959552 | bytes 6291456 | tf_op jit(solution)/shard_map/expert_down/pallas_call | solution.py:320
  70.2 1.6 %collective-permute-done.20.z_ref = bf16[96,1024]{1,0:T(8,128)(2,1)S(1)} collective-permute-done((bf16[96,1024]{1,0:T(8,128)(2,1)S(1)}, bf16[96,1024]{1,0:T(8,128)(2,1)S(1)}, u32[]{:S(2)}, u32[]{:S(2)}) %collective-permute-start.20) | collective-permute-done | bytes 196640 | tf_op jit(solution)/shard_map/ppermute | solution.py:393
  71.9 1.7 %collective-permute-start.24 = (bf16[96,1024]{1,0:T(8,128)(2,1)S(1)}, bf16[96,1024]{1,0:T(8,128)(2,1)S(1)}, u32[]{:S(2)}, u32[]{:S(2)}) collective-permute-start(bf16[96,1024]{1,0:T(8,128)(2,1)S(1)} %get-tuple-element.62), channel_id=1, source_target_pairs={{0,8},{1,9},{2,10},{3,11},{4,12},{5,13},{6,14},{7,15},{8,0},{9,1},... | collective-permute-start | bytes 589832 | tf_op jit(solution)/shard_map/ppermute | solution.py:397
  73.6 3.8 %collective-permute-done.23.refs_0_ = bf16[96,1024]{1,0:T(8,128)(2,1)S(1)} collective-permute-done((bf16[96,1024]{1,0:T(8,128)(2,1)S(1)}, bf16[96,1024]{1,0:T(8,128)(2,1)S(1)}, u32[]{:S(2)}, u32[]{:S(2)}) %collective-permute-start.23) | collective-permute-done | bytes 196640 | tf_op jit(solution)/shard_map/ppermute | solution.py:397
  77.4 6.8 %collective-permute-done.24.refs_6_ = bf16[96,1024]{1,0:T(8,128)(2,1)S(1)} collective-permute-done((bf16[96,1024]{1,0:T(8,128)(2,1)S(1)}, bf16[96,1024]{1,0:T(8,128)(2,1)S(1)}, u32[]{:S(2)}, u32[]{:S(2)}) %collective-permute-start.24) | collective-permute-done | bytes 196640 | tf_op jit(solution)/shard_map/ppermute | solution.py:397
  84.2 1.3 %collective-permute-done.21.refs_4_ = bf16[96,2048]{1,0:T(8,128)(2,1)S(1)} collective-permute-done((bf16[96,2048]{1,0:T(8,128)(2,1)S(1)}, bf16[96,2048]{1,0:T(8,128)(2,1)S(1)}, u32[]{:S(2)}, u32[]{:S(2)}) %collective-permute-start.21) | collective-permute-done | bytes 393248 | tf_op jit(solution)/shard_map/ppermute | solution.py:393
  85.4 1.2 %finish.1 = bf16[128,2048]{1,0:T(8,128)(2,1)} custom-call(f32[128,2048]{1,0:T(8,128)S(1)} %get-tuple-element.38.refs_0_, f32[128,1]{1,0:T(8,128)S(1)} %get-tuple-element.39.refs_1_, s32[128,1]{1,0:T(8,128)S(1)} %get-tuple-element.40.refs_2_, bf16[96,2048]{1,0:T(8,128)(2,1)S(1)} %get-tuple-element.57.refs_3_, ...), custom_call_target="tpu_custom_call" | custom-call | flops 201326592 | bytes 4194304 | tf_op jit(solution)/shard_map/finish/pallas_call | solution.py:375
  (52 shorter events, 1.5 us)
Async XLA Ops:
  0.0 2.3 %copy-start.8 = (bf16[1,32,2,2048]{3,2,1,0:T(2,128)(2,1)S(1)}, bf16[1,32,2,2048]{3,2,1,0:T(2,128)(2,1)}, u32[]{:S(2)}) copy-start(bf16[1,32,2,2048]{3,2,1,0:T(2,128)(2,1)} %param.11) | copy-start | bytes 786436
  0.0 14.7 %collective-permute-start.2 = (bf16[384,2048]{1,0:T(8,128)(2,1)}, bf16[384,2048]{1,0:T(8,128)(2,1)S(1)}, u32[]{:S(2)}, u32[]{:S(2)}) collective-permute-start(bf16[384,2048]{1,0:T(8,128)(2,1)} %w_out.1), channel_id=1, source_target_pairs={{0,1},{1,0},{2,3},{3,2},{4,5},{5,4},{6,7},{7,6},{8,9},{9,8},{10,11... | collective-permute-start | bytes 4718600 | tf_op jit(solution)/shard_map/ppermute | solution.py:393
  0.5 14.2 %collective-permute-start.1 = (bf16[2048,384]{1,0:T(8,128)(2,1)}, bf16[2048,384]{1,0:T(8,128)(2,1)S(1)}, u32[]{:S(2)}, u32[]{:S(2)}) collective-permute-start(bf16[2048,384]{1,0:T(8,128)(2,1)} %whole.3), channel_id=1, source_target_pairs={{0,1},{1,0},{2,3},{3,2},{4,5},{5,4},{6,7},{7,6},{8,9},{9,8},{10,11... | collective-permute-start | bytes 4718600 | tf_op jit(solution)/shard_map/ppermute | solution.py:393
  3.1 6.2 %copy-start.4 = (f32[2048]{0:T(1024)S(1)}, f32[2048]{0:T(1024)}, u32[]{:S(2)}) copy-start(f32[2048]{0:T(1024)} %param.12) | copy-start | bytes 24580
  3.1 6.2 %copy-start.5 = (s32[1,1,128]{2,1,0:T(1,128)S(1)}, s32[1,1,128]{2,1,0:T(1,128)}, u32[]{:S(2)}) copy-start(s32[1,1,128]{2,1,0:T(1,128)} %param.15) | copy-start | bytes 1540
  3.1 6.2 %copy-start.6 = (s32[1,1,128]{2,1,0:T(1,128)S(1)}, s32[1,1,128]{2,1,0:T(1,128)}, u32[]{:S(2)}) copy-start(s32[1,1,128]{2,1,0:T(1,128)} %param.16) | copy-start | bytes 1540
  3.1 9.8 %collective-permute-start = (bf16[64,2048]{1,0:T(8,128)(2,1)}, bf16[64,2048]{1,0:T(8,128)(2,1)}, u32[]{:S(2)}, u32[]{:S(2)}) collective-permute-start(bf16[64,2048]{1,0:T(8,128)(2,1)} %hand_on.16.refs_4_), channel_id=1, source_target_pairs={{0,16},{16,0},{1,17},{17,1},{2,18},{18,2},{3,19},{19,3},{4,20},{20... | collective-permute-start | bytes 786440 | tf_op jit(solution)/shard_map/ppermute | solution.py:416
  6.0 15.5 %collective-permute-start.4 = (bf16[512,384]{1,0:T(8,128)(2,1)}, bf16[512,384]{1,0:T(8,128)(2,1)S(1)}, u32[]{:S(2)}, u32[]{:S(2)}) collective-permute-start(bf16[512,384]{1,0:T(8,128)(2,1)} %weight_part.2.refs_1_), channel_id=1, source_target_pairs={{0,2},{1,3},{2,0},{3,1},{4,6},{5,7},{6,4},{7,5},{8,10},{9,11},{10,... | collective-permute-start | bytes 1179656 | tf_op jit(solution)/shard_map/ppermute | solution.py:393
  9.3 1.0 %copy-start.2 = (bf16[1,1,128,2048]{3,2,1,0:T(8,128)(2,1)S(1)}, bf16[1,1,128,2048]{3,2,1,0:T(8,128)(2,1)}, u32[]{:S(2)}) copy-start(bf16[1,1,128,2048]{3,2,1,0:T(8,128)(2,1)} %param.9) | copy-start | bytes 1572868
  10.4 1.0 %copy-start.3 = (bf16[1,1,128,2048]{3,2,1,0:T(8,128)(2,1)S(1)}, bf16[1,1,128,2048]{3,2,1,0:T(8,128)(2,1)}, u32[]{:S(2)}) copy-start(bf16[1,1,128,2048]{3,2,1,0:T(8,128)(2,1)} %param.10) | copy-start | bytes 1572868
  11.4 0.7 copy-start.7
  12.9 12.6 %collective-permute-start.6 = (bf16[512,384]{1,0:T(8,128)(2,1)}, bf16[512,384]{1,0:T(8,128)(2,1)S(1)}, u32[]{:S(2)}, u32[]{:S(2)}) collective-permute-start(bf16[512,384]{1,0:T(8,128)(2,1)} %hand_on.18), channel_id=1, source_target_pairs={{0,2},{1,3},{2,0},{3,1},{4,6},{5,7},{6,4},{7,5},{8,10},{9,11},{10,... | collective-permute-start | bytes 1179656 | tf_op jit(solution)/shard_map/ppermute | solution.py:393
  14.7 8.4 %copy-start = (bf16[2048,384]{1,0:T(8,128)(2,1)S(1)}, bf16[2048,384]{1,0:T(8,128)(2,1)}, u32[]{:S(2)}) copy-start(bf16[2048,384]{1,0:T(8,128)(2,1)} %whole.3) | copy-start | bytes 4718596
  14.7 8.4 %copy-start.1 = (bf16[384,2048]{1,0:T(8,128)(2,1)S(1)}, bf16[384,2048]{1,0:T(8,128)(2,1)}, u32[]{:S(2)}) copy-start(bf16[384,2048]{1,0:T(8,128)(2,1)} %w_out.1) | copy-start | bytes 4718596
  17.3 19.5 %collective-permute-start.8 = (bf16[96,2048]{1,0:T(8,128)(2,1)S(1)}, bf16[96,2048]{1,0:T(8,128)(2,1)S(1)}, u32[]{:S(2)}, u32[]{:S(2)}) collective-permute-start(bf16[96,2048]{1,0:T(8,128)(2,1)S(1)} %get-tuple-element.44), channel_id=1, source_target_pairs={{0,8},{1,9},{2,10},{3,11},{4,12},{5,13},{6,14},{7,15},{8,0},{9,1},... | collective-permute-start | bytes 1179656 | tf_op jit(solution)/shard_map/ppermute | solution.py:397
  19.9 17.0 %collective-permute-start.3 = (bf16[96,2048]{1,0:T(8,128)(2,1)S(1)}, bf16[96,2048]{1,0:T(8,128)(2,1)S(1)}, u32[]{:S(2)}, u32[]{:S(2)}) collective-permute-start(bf16[96,2048]{1,0:T(8,128)(2,1)S(1)} %get-tuple-element.41.refs_1_.own_in.refs_2_), channel_id=1, source_target_pairs={{0,4},{1,5},{2,6},{3,7},{4,0},{5,1},{6,2},{7,3},{8,12},{9,13},{10,... | collective-permute-start | bytes 1179656 | tf_op jit(solution)/shard_map/ppermute | solution.py:393
  21.5 19.4 %collective-permute-start.5 = (bf16[512,384]{1,0:T(8,128)(2,1)S(1)}, bf16[512,384]{1,0:T(8,128)(2,1)S(1)}, u32[]{:S(2)}, u32[]{:S(2)}) collective-permute-start(bf16[512,384]{1,0:T(8,128)(2,1)S(1)} %hand_on.17.refs_0_.refs_1_), channel_id=1, source_target_pairs={{0,16},{16,0},{1,17},{17,1},{2,18},{18,2},{3,19},{19,3},{4,20},{20... | collective-permute-start | bytes 1179656 | tf_op jit(solution)/shard_map/ppermute | solution.py:401
  25.5 13.9 %collective-permute-start.7 = (bf16[512,384]{1,0:T(8,128)(2,1)S(1)}, bf16[512,384]{1,0:T(8,128)(2,1)S(1)}, u32[]{:S(2)}, u32[]{:S(2)}) collective-permute-start(bf16[512,384]{1,0:T(8,128)(2,1)S(1)} %hand_on.19.refs_2_), channel_id=1, source_target_pairs={{0,16},{16,0},{1,17},{17,1},{2,18},{18,2},{3,19},{19,3},{4,20},{20... | collective-permute-start | bytes 1179656 | tf_op jit(solution)/shard_map/ppermute | solution.py:401
  25.8 13.5 %collective-permute-start.14 = (bf16[112,2048]{1,0:T(8,128)(2,1)S(1)}, bf16[112,2048]{1,0:T(8,128)(2,1)S(1)}, u32[]{:S(2)}, u32[]{:S(2)}) collective-permute-start(bf16[112,2048]{1,0:T(8,128)(2,1)S(1)} %get-tuple-element.51), channel_id=1, source_target_pairs={{0,2},{1,3},{2,0},{3,1},{4,6},{5,7},{6,4},{7,5},{8,10},{9,11},{10,... | collective-permute-start | bytes 1376264 | tf_op jit(solution)/shard_map/ppermute | solution.py:393
  36.9 9.7 %collective-permute-start.9 = (bf16[96,2048]{1,0:T(8,128)(2,1)S(1)}, bf16[96,2048]{1,0:T(8,128)(2,1)S(1)}, u32[]{:S(2)}, u32[]{:S(2)}) collective-permute-start(bf16[96,2048]{1,0:T(8,128)(2,1)S(1)} %hand_on.20.own_in.refs_2_), channel_id=1, source_target_pairs={{0,4},{1,5},{2,6},{3,7},{4,0},{5,1},{6,2},{7,3},{8,12},{9,13},{10,... | collective-permute-start | bytes 1179656 | tf_op jit(solution)/shard_map/ppermute | solution.py:393
  38.4 15.3 %collective-permute-start.16 = (bf16[160,2048]{1,0:T(8,128)(2,1)S(1)}, bf16[160,2048]{1,0:T(8,128)(2,1)S(1)}, u32[]{:S(2)}, u32[]{:S(2)}) collective-permute-start(bf16[160,2048]{1,0:T(8,128)(2,1)S(1)} %get-tuple-element.52), channel_id=1, source_target_pairs={{0,2},{1,3},{2,0},{3,1},{4,6},{5,7},{6,4},{7,5},{8,10},{9,11},{10,... | collective-permute-start | bytes 1966088 | tf_op jit(solution)/shard_map/ppermute | solution.py:393
  39.4 14.3 %collective-permute-start.17 = (bf16[112,2048]{1,0:T(8,128)(2,1)S(1)}, bf16[112,2048]{1,0:T(8,128)(2,1)S(1)}, u32[]{:S(2)}, u32[]{:S(2)}) collective-permute-start(bf16[112,2048]{1,0:T(8,128)(2,1)S(1)} %hand_on.27.refs_4_), channel_id=1, source_target_pairs={{0,1},{1,0},{2,3},{3,2},{4,5},{5,4},{6,7},{7,6},{8,9},{9,8},{10,11... | collective-permute-start | bytes 1376264 | tf_op jit(solution)/shard_map/ppermute | solution.py:393
  39.4 14.3 %collective-permute-start.15 = (bf16[112,2048]{1,0:T(8,128)(2,1)S(1)}, bf16[112,2048]{1,0:T(8,128)(2,1)S(1)}, u32[]{:S(2)}, u32[]{:S(2)}) collective-permute-start(bf16[112,2048]{1,0:T(8,128)(2,1)S(1)} %hand_on.27.refs_4_), channel_id=1, source_target_pairs={{0,16},{16,0},{1,17},{17,1},{2,18},{18,2},{3,19},{19,3},{4,20},{20... | collective-permute-start | bytes 1376264 | tf_op jit(solution)/shard_map/ppermute | solution.py:401
  46.7 1.7 %collective-permute-start.10 = (bf16[512,384]{1,0:T(8,128)(2,1)S(1)}, bf16[512,384]{1,0:T(8,128)(2,1)S(1)}, u32[]{:S(2)}, u32[]{:S(2)}) collective-permute-start(bf16[512,384]{1,0:T(8,128)(2,1)S(1)} %get-tuple-element.45.refs_4_), channel_id=1, source_target_pairs={{0,1},{1,0},{2,3},{3,2},{4,5},{5,4},{6,7},{7,6},{8,9},{9,8},{10,11... | collective-permute-start | bytes 1179656 | tf_op jit(solution)/shard_map/ppermute | solution.py:393
  46.7 2.3 %collective-permute-start.11 = (bf16[512,384]{1,0:T(8,128)(2,1)S(1)}, bf16[512,384]{1,0:T(8,128)(2,1)S(1)}, u32[]{:S(2)}, u32[]{:S(2)}) collective-permute-start(bf16[512,384]{1,0:T(8,128)(2,1)S(1)} %get-tuple-element.46.refs_5_), channel_id=1, source_target_pairs={{0,1},{1,0},{2,3},{3,2},{4,5},{5,4},{6,7},{7,6},{8,9},{9,8},{10,11... | collective-permute-start | bytes 1179656 | tf_op jit(solution)/shard_map/ppermute | solution.py:393
  48.4 1.7 %collective-permute-start.12 = (bf16[512,384]{1,0:T(8,128)(2,1)S(1)}, bf16[512,384]{1,0:T(8,128)(2,1)S(1)}, u32[]{:S(2)}, u32[]{:S(2)}) collective-permute-start(bf16[512,384]{1,0:T(8,128)(2,1)S(1)} %get-tuple-element.47.refs_6_), channel_id=1, source_target_pairs={{0,1},{1,0},{2,3},{3,2},{4,5},{5,4},{6,7},{7,6},{8,9},{9,8},{10,11... | collective-permute-start | bytes 1179656 | tf_op jit(solution)/shard_map/ppermute | solution.py:393
  48.9 1.7 %collective-permute-start.13 = (bf16[512,384]{1,0:T(8,128)(2,1)S(1)}, bf16[512,384]{1,0:T(8,128)(2,1)S(1)}, u32[]{:S(2)}, u32[]{:S(2)}) collective-permute-start(bf16[512,384]{1,0:T(8,128)(2,1)S(1)} %get-tuple-element.48.refs_7_), channel_id=1, source_target_pairs={{0,1},{1,0},{2,3},{3,2},{4,5},{5,4},{6,7},{7,6},{8,9},{9,8},{10,11... | collective-permute-start | bytes 1179656 | tf_op jit(solution)/shard_map/ppermute | solution.py:393
  53.7 2.8 %collective-permute-start.19 = (bf16[160,2048]{1,0:T(8,128)(2,1)S(1)}, bf16[160,2048]{1,0:T(8,128)(2,1)S(1)}, u32[]{:S(2)}, u32[]{:S(2)}) collective-permute-start(bf16[160,2048]{1,0:T(8,128)(2,1)S(1)} %get-tuple-element.54.refs_8_), channel_id=1, source_target_pairs={{0,1},{1,0},{2,3},{3,2},{4,5},{5,4},{6,7},{7,6},{8,9},{9,8},{10,11... | collective-permute-start | bytes 1966088 | tf_op jit(solution)/shard_map/ppermute | solution.py:393
  53.8 2.7 %collective-permute-start.18 = (bf16[112,2048]{1,0:T(8,128)(2,1)S(1)}, bf16[112,2048]{1,0:T(8,128)(2,1)S(1)}, u32[]{:S(2)}, u32[]{:S(2)}) collective-permute-start(bf16[112,2048]{1,0:T(8,128)(2,1)S(1)} %get-tuple-element.53.refs_5_), channel_id=1, source_target_pairs={{0,1},{1,0},{2,3},{3,2},{4,5},{5,4},{6,7},{7,6},{8,9},{9,8},{10,11... | collective-permute-start | bytes 1376264 | tf_op jit(solution)/shard_map/ppermute | solution.py:393
  57.4 7.8 %collective-permute-start.22 = (bf16[96,1024]{1,0:T(8,128)(2,1)S(1)}, bf16[96,1024]{1,0:T(8,128)(2,1)S(1)}, u32[]{:S(2)}, u32[]{:S(2)}) collective-permute-start(bf16[96,1024]{1,0:T(8,128)(2,1)S(1)} %get-tuple-element.61), channel_id=1, source_target_pairs={{0,4},{1,5},{2,6},{3,7},{4,0},{5,1},{6,2},{7,3},{8,12},{9,13},{10,... | collective-permute-start | bytes 589832 | tf_op jit(solution)/shard_map/ppermute | solution.py:393
  60.3 11.5 %collective-permute-start.20 = (bf16[96,1024]{1,0:T(8,128)(2,1)S(1)}, bf16[96,1024]{1,0:T(8,128)(2,1)S(1)}, u32[]{:S(2)}, u32[]{:S(2)}) collective-permute-start(bf16[96,1024]{1,0:T(8,128)(2,1)S(1)} %hand_on.29), channel_id=1, source_target_pairs={{0,4},{1,5},{2,6},{3,7},{4,0},{5,1},{6,2},{7,3},{8,12},{9,13},{10,... | collective-permute-start | bytes 589832 | tf_op jit(solution)/shard_map/ppermute | solution.py:393
  65.2 12.2 %collective-permute-start.23 = (bf16[96,1024]{1,0:T(8,128)(2,1)S(1)}, bf16[96,1024]{1,0:T(8,128)(2,1)S(1)}, u32[]{:S(2)}, u32[]{:S(2)}) collective-permute-start(bf16[96,1024]{1,0:T(8,128)(2,1)S(1)} %far_total.3), channel_id=1, source_target_pairs={{0,8},{1,9},{2,10},{3,11},{4,12},{5,13},{6,14},{7,15},{8,0},{9,1},... | collective-permute-start | bytes 589832 | tf_op jit(solution)/shard_map/ppermute | solution.py:397
  71.9 13.6 %collective-permute-start.21 = (bf16[96,2048]{1,0:T(8,128)(2,1)S(1)}, bf16[96,2048]{1,0:T(8,128)(2,1)S(1)}, u32[]{:S(2)}, u32[]{:S(2)}) collective-permute-start(bf16[96,2048]{1,0:T(8,128)(2,1)S(1)} %get-tuple-element.60), channel_id=1, source_target_pairs={{0,4},{1,5},{2,6},{3,7},{4,0},{5,1},{6,2},{7,3},{8,12},{9,13},{10,... | collective-permute-start | bytes 1179656 | tf_op jit(solution)/shard_map/ppermute | solution.py:393
  71.9 12.3 %collective-permute-start.24 = (bf16[96,1024]{1,0:T(8,128)(2,1)S(1)}, bf16[96,1024]{1,0:T(8,128)(2,1)S(1)}, u32[]{:S(2)}, u32[]{:S(2)}) collective-permute-start(bf16[96,1024]{1,0:T(8,128)(2,1)S(1)} %get-tuple-element.62), channel_id=1, source_target_pairs={{0,8},{1,9},{2,10},{3,11},{4,12},{5,13},{6,14},{7,15},{8,0},{9,1},... | collective-permute-start | bytes 589832 | tf_op jit(solution)/shard_map/ppermute | solution.py:397
